TPU v7x, 32 devices: a whole 2x2x4 slice. The times are simulated.
32 devices in a mesh: dp: 2 (over x), seq: 16 (over z, y, core).
Axes of the slice: x: 2, y: 2, z: 4, core: 2. Of those that a mesh axis runs over, the one named last changes fastest.
Arguments:
- queries: bfloat16 [2, 2048, 1024], P('dp', 'seq'), may hold values from -6 to 6
- keys: bfloat16 [2, 2048, 1024], P('dp', 'seq'), may hold values from -6 to 6
- values: bfloat16 [2, 2048, 1024], P('dp', 'seq'), may hold values from -6 to 6
- cotangent: bfloat16 [2, 2048, 1024], P('dp', 'seq'), may hold values from -6 to 6
- out_weight: bfloat16 [1024, 1024], P('dp'), may hold values from -0.1875 to 0.1875
Outputs:
- output: bfloat16 [2, 2048, 1024], P('dp', 'seq')
- grad_queries: bfloat16 [2, 2048, 1024], P('dp', 'seq')
- grad_keys: bfloat16 [2, 2048, 1024], P('dp', 'seq')
- grad_values: bfloat16 [2, 2048, 1024], P('dp', 'seq')
- grad_weight: float32 [1024, 1024], P(('dp', 'seq'))
All inputs are finite; a program needn't handle non-finite values.
Results may differ from a plain program's by a relative error of at most 0.015.
Values may be sent and summed in bfloat16 or wider, within the bound.
No kernel may reach another device: no remote copies, remote signals or barrier semaphores. Data moves between devices by JAX's collectives and lax.ppermute only.
A program may use at most 128 MiB of HBM per device.

v0:
```python
import math

import jax
import jax.numpy as jnp
from jax import lax
from jax.sharding import PartitionSpec as P

DH = 128


epsilon = 1e-05


def entering(x, axis, join, neutral, backward):
    count = lax.axis_size(axis)
    place = lax.axis_index(axis)
    ahead = count - 1 - place if backward else place
    gathered = lax.all_gather(x.astype(jnp.bfloat16), axis)
    state = jnp.zeros_like(x) + jnp.asarray(neutral, x.dtype)

    def one(turn, state):
        source = count - 1 - turn if backward else turn
        return join(state, lax.dynamic_index_in_dim(gathered, source, 0, False).astype(x.dtype))

    return lax.fori_loop(0, ahead, one, state)


def adding(earlier, latter):
    return earlier + latter


def contract_rows(left, right):
    return lax.dot_general(
        left, right, (((0,), (0,)), ((), ())), preferred_element_type=jnp.float32
    )


def apply_state(form, rows, state):
    upper = state.astype(jnp.bfloat16)
    lower = (state - upper.astype(jnp.float32)).astype(jnp.bfloat16)
    first = jnp.einsum(form, rows, upper, preferred_element_type=jnp.float32)
    return first + jnp.einsum(form, rows, lower, preferred_element_type=jnp.float32)


def local(queries, keys, values, cotangent, out_weight):
    local_seqs, block, features = queries.shape
    heads = features // DH
    shape = (local_seqs, block, heads, DH)
    query_heads = queries.reshape(shape)
    key_heads = keys.reshape(shape)
    value_heads = values.reshape(shape)
    causal = jnp.tril(jnp.ones((block, block), dtype=jnp.bool_))
    scores = jnp.einsum(
        "bthd,bshd->bhts", query_heads, key_heads, preferred_element_type=jnp.float32
    )
    attend = jnp.where(causal, scores, jnp.float32(0.0)).astype(jnp.bfloat16)
    local_kv = jnp.einsum(
        "bshd,bshe->bhde", key_heads, value_heads, preferred_element_type=jnp.float32
    )
    prior = entering(local_kv, "seq", adding, jnp.zeros_like(local_kv), False)
    mixed = jnp.einsum("bhts,bshd->bthd", attend, value_heads, preferred_element_type=jnp.float32)
    mixed = mixed + apply_state("bthd,bhde->bthe", query_heads, prior)
    root_mean = jnp.sqrt(jnp.mean(mixed * mixed, axis=-1, keepdims=True) + epsilon)
    normed = mixed / root_mean
    total_rows = local_seqs * block
    normed_rows = normed.astype(jnp.bfloat16).reshape(total_rows, features)
    out_rows = cotangent.reshape(total_rows, cotangent.shape[2])
    projected = lax.dot_general(
        normed_rows,
        lax.all_gather(out_weight, "dp", axis=0, tiled=True),
        (((1,), (1,)), ((), ())),
        preferred_element_type=jnp.float32,
    )
    columns = out_rows
    dnormed = jnp.dot(
        columns,
        lax.all_gather(out_weight, "dp", axis=0, tiled=True),
        preferred_element_type=jnp.float32,
    )
    output = projected.astype(jnp.bfloat16).reshape(local_seqs, block, cotangent.shape[2])
    dnormed = dnormed.reshape(shape)
    dmixed = (dnormed - normed * jnp.mean(dnormed * normed, axis=-1, keepdims=True)) / root_mean
    dmixed_b = dmixed.astype(jnp.bfloat16)
    local_u = jnp.einsum(
        "bthd,bthe->bhde", query_heads, dmixed_b, preferred_element_type=jnp.float32
    )
    later = entering(local_u, "seq", adding, jnp.zeros_like(local_u), True)
    back = jnp.where(
        causal,
        jnp.einsum("bthe,bshe->bhts", dmixed_b, value_heads, preferred_element_type=jnp.float32),
        jnp.float32(0.0),
    ).astype(jnp.bfloat16)
    grad_q = jnp.einsum("bhts,bshd->bthd", back, key_heads, preferred_element_type=jnp.float32)
    grad_q = grad_q + apply_state("bthe,bhde->bthd", dmixed_b, prior)
    grad_k = jnp.einsum("bhts,bthd->bshd", back, query_heads, preferred_element_type=jnp.float32)
    grad_k = grad_k + apply_state("bshe,bhde->bshd", value_heads, later)
    grad_v = jnp.einsum("bhts,bthe->bshe", attend, dmixed_b, preferred_element_type=jnp.float32)
    grad_v = grad_v + apply_state("bshd,bhde->bshe", key_heads, later)
    data_size = lax.axis_size("dp")
    seq_size = lax.axis_size("seq")
    factor = 1.0 / math.sqrt(local_seqs * data_size * block * seq_size)
    columns = out_rows
    grad_weight = lax.psum_scatter(
        contract_rows(columns, normed_rows) * factor, ("dp", "seq"), scatter_dimension=0, tiled=True
    )
    return (
        output,
        grad_q.reshape(local_seqs, block, features).astype(jnp.bfloat16),
        grad_k.reshape(local_seqs, block, features).astype(jnp.bfloat16),
        grad_v.reshape(local_seqs, block, features).astype(jnp.bfloat16),
        grad_weight,
    )


def solution(mesh):
    return jax.shard_map(
        local,
        mesh=mesh,
        in_specs=(
            P("dp", "seq", None),
            P("dp", "seq", None),
            P("dp", "seq", None),
            P("dp", "seq", None),
            P("dp", None),
        ),
        out_specs=(
            P("dp", "seq", None),
            P("dp", "seq", None),
            P("dp", "seq", None),
            P("dp", "seq", None),
            P(("dp", "seq"), None),
        ),
        check_vma=False,
    )
```

profile of v0, /device:TPU:0, one launch (start us, length us, event | category | flops | bytes accessed | tf_op | source)
XLA Modules:
  0.0 318.0 jit_solution(5663738919505653896)
XLA Ops:
  9.2 1.1 copy.80
  12.4 1.0 fusion.6
  13.4 32.0 %all-gather.6.cloned.1.call-done = bf16[1024,1024]{1,0:T(8,128)(2,1)} async-done(((bf16[512,1024]{1,0:T(8,128)(2,1)}), bf16[1024,1024]{1,0:T(8,128)(2,1)}) %all-gather.6.cloned.1.call-update) | async-done | bytes 2097168 | tf_op jit(solution)/shard_map/all_gather | solution.py:70
  45.4 2.9 copy.49
  48.3 50.5 %all-gather.8.cloned.1.call-done = bf16[128,128,128]{2,1,0:T(8,128)(2,1)} async-done(((bf16[8,128,128]{2,1,0:T(8,128)(2,1)}), bf16[128,128,128]{2,1,0:T(8,128)(2,1)}) %all-gather.8.cloned.1.call-update) | async-done | bytes 4194320 | tf_op jit(solution)/shard_map/all_gather | solution.py:18
  99.5 1.3 multiply_reduce_fusion.1
  103.5 2.7 multiply_bitcast_fusion
  106.2 5.4 %copy.76 = f32[1024,1024]{1,0:T(8,128)} copy(f32[1024,1024]{0,1:T(8,128)} %multiply_bitcast_fusion) | data formatting | bytes 8388608
  111.6 1.4 fusion.7
  113.0 1.3 fusion.22
  114.3 1.2 convolution_add_fusion.2
  115.5 1.3 fusion.9
  117.6 2.5 fusion.10
  120.1 1.2 fusion.18
  121.3 47.6 %all-gather.10.cloned.1.call-done = bf16[128,128,128]{2,1,0:T(8,128)(2,1)} async-done(((bf16[8,128,128]{2,1,0:T(8,128)(2,1)}), bf16[128,128,128]{2,1,0:T(8,128)(2,1)}) %all-gather.10.cloned.1.call-update) | async-done | bytes 4194320 | tf_op jit(solution)/shard_map/all_gather | solution.py:18
  169.0 16.4 %while.23 = (s32[]{:T(128)}, f32[1,8,128,128]{3,2,1,0:T(8,128)S(1)}, s32[]{:T(128)}, bf16[16,1,8,128,128]{4,3,2,1,0:T(8,128)(2,1)}, s32[]{:T(128)}, /*index=5*/s32[]{:T(128)}, s32[]{:T(128)}, s32[]{:T(128)}) while((s32[]{:T(128)}, f32[1,8,128,128]{3,2,1,0:T(8,128)S(1)}, s32[]{:T(128)}, bf16[16,1,8,128,128]{4,3,2,1,0:T(8,128)(2,1)}, s32[]{:T(128)}, ...), condition=%wide.region_5.6_spmd, body=%wide.region_4.5_spmd.sunk | while | flops 262150 | bytes 1310863 | solution.py:25
  169.0 1.1 convert_add_fusion.5
  170.1 1.1 convert_add_fusion.5
  171.2 1.1 convert_add_fusion.5
  172.3 1.1 convert_add_fusion.5
  173.4 1.1 convert_add_fusion.5
  174.5 1.1 convert_add_fusion.5
  175.6 1.1 convert_add_fusion.5
  176.7 1.1 convert_add_fusion.5
  177.7 1.1 convert_add_fusion.5
  178.8 1.1 convert_add_fusion.5
  179.9 1.1 convert_add_fusion.5
  181.0 1.1 convert_add_fusion.5
  182.1 1.1 convert_add_fusion.5
  183.2 1.1 convert_add_fusion.5
  184.3 1.1 convert_add_fusion.5
  188.7 122.8 %reduce-scatter.4.cloned.1.call-done = f32[32,1024]{1,0:T(8,128)} async-done(((f32[1024,1024]{1,0:T(8,128)}), f32[32,1024]{1,0:T(8,128)}) %reduce-scatter.4.cloned.1.call-update) | async-done | bytes 131088
  (52 shorter events, 11.5 us)
Async XLA Ops:
  7.2 93.6 %copy-start = (bf16[1,128,1024]{2,1,0:T(8,128)(2,1)S(1)}, bf16[1,128,1024]{2,1,0:T(8,128)(2,1)}, u32[]{:S(2)}) copy-start(bf16[1,128,1024]{2,1,0:T(8,128)(2,1)} %param.12) | copy-start | bytes 786436
  7.2 38.2 %all-gather.6.cloned.1.call-start = ((), (), s32[]{:S(2)}) async-start(), calls=%async_computation.1 | async-start | bytes 3145728 | tf_op jit(solution)/shard_map/all_gather | solution.py:70
  7.9 90.8 %all-gather.8.cloned.1.call-start = ((), (), s32[]{:S(2)}) async-start(), calls=%async_computation.2 | async-start | bytes 4456448 | tf_op jit(solution)/shard_map/all_gather | solution.py:18
  9.0 89.8 %copy-start.4 = (bf16[16,8,8,128]{3,2,1,0:T(8,128)(2,1)}, bf16[16,8,8,128]{3,2,1,0:T(8,128)(2,1)S(1)}, u32[]{:S(2)}) copy-start(bf16[16,8,8,128]{3,2,1,0:T(8,128)(2,1)S(1)} %copy.79) | copy-start | bytes 786436
  9.2 2.1 copy-start.6
  11.3 157.7 %all-gather.10.cloned.1.call-start = ((), (), s32[]{:S(2)}) async-start(), calls=%async_computation.3 | async-start | bytes 4456448 | tf_op jit(solution)/shard_map/all_gather | solution.py:18
  101.6 0.7 copy-start.2
  101.7 9.9 %copy-start.7 = (bf16[1,128,8,128]{1,3,2,0:T(8,128)(2,1)}, bf16[1,128,8,128]{1,3,2,0:T(8,128)(2,1)S(1)}, u32[]{:S(2)}) copy-start(bf16[1,128,8,128]{1,3,2,0:T(8,128)(2,1)S(1)} %get-tuple-element.129) | copy-start | bytes 786436
  103.5 208.0 %reduce-scatter.4.cloned.1.call-start = ((), (), s32[]{:S(2)}) async-start(), calls=%async_computation.4 | async-start | bytes 4325376
  111.5 6.1 %copy-start.1 = (bf16[1024,1024]{1,0:T(8,128)(2,1)S(1)}, bf16[1024,1024]{1,0:T(8,128)(2,1)}, u32[]{:S(2)}) copy-start(bf16[1024,1024]{1,0:T(8,128)(2,1)} %all-gather.6.cloned.1.call-done) | copy-start | bytes 6291460
  113.0 3.8 %copy-start.8 = (bf16[8,128,128]{2,1,0:T(8,128)(2,1)}, bf16[8,128,128]{2,1,0:T(8,128)(2,1)S(1)}, u32[]{:S(2)}) copy-start(bf16[8,128,128]{2,1,0:T(8,128)(2,1)S(1)} %fusion.7) | copy-start | bytes 786436
  115.4 4.7 %copy-start.3 = (bf16[1,128,8,128]{1,3,2,0:T(8,128)(2,1)S(1)}, bf16[1,128,8,128]{1,3,2,0:T(8,128)(2,1)}, u32[]{:S(2)}) copy-start(bf16[1,128,8,128]{1,3,2,0:T(8,128)(2,1)} %copy-done.2) | copy-start | bytes 786436
  120.1 65.3 %copy-start.5 = (bf16[16,8,8,128]{3,2,1,0:T(8,128)(2,1)S(1)}, bf16[16,8,8,128]{3,2,1,0:T(8,128)(2,1)}, u32[]{:S(2)}) copy-start(bf16[16,8,8,128]{3,2,1,0:T(8,128)(2,1)} %copy-done.4) | copy-start | bytes 786436
  185.4 2.1 copy-start.9
Sparse Core Ops, SparseCore 0:
  9.6 35.7 all-gather.5
  48.1 50.5 all-gather.7
  103.6 65.3 all-gather.9
  171.6 139.7 reduce-scatter.3
where the time goes:
time: 319 us; the launch traced here: 318 us
  waiting for transfers between devices  254 us (80%)
  matrix products  17.8 us (6%)
  other arithmetic  16.2 us (5%)
  local copies, waits for them, and re-layouts  15.7 us (5%)
  between operations  14 us (4%)
    unnamed x5, waiting for transfers between devices  124 us
    all_gather x2, waiting for transfers between devices, entering(): gathered = lax.all_gather(x.astype(jnp.bfloat16), axis)  98.1 us
    all_gather x1, waiting for transfers between devices, local(): lax.all_gather(out_weight, 'dp', axis=0, tiled=True)  32 us
    add x15, other arithmetic, adding(): return earlier + latter  16.1 us
    unnamed x27, local copies, waits for them, and re-layouts  11.7 us
  transfers between devices with their start and end apart: 4, of which 4 were waited for; matrix products, arithmetic and copies ran while one was open for 14% of the time, Pallas kernels for 0%

commit v1 on v0

v1 whole, which is shorter than its diff:
```python
import functools
import math

import jax
import jax.numpy as jnp
from jax import lax
from jax.experimental import pallas as pl
from jax.experimental.pallas import tpu as pltpu
from jax.sharding import PartitionSpec as P

DH = 128
EPSILON = 1e-05
BF16 = jnp.bfloat16
F32 = jnp.float32


def dot(left, right, left_dim, right_dim):
    return lax.dot_general(
        left, right, (((left_dim,), (right_dim,)), ((), ())), preferred_element_type=F32
    )


def call(body, outs, *args, flops=10**8, scratch=()):
    nbytes = sum(a.size * a.dtype.itemsize for a in args)
    nbytes += sum(math.prod(s) * jnp.dtype(d).itemsize for s, d in outs)
    return pl.pallas_call(
        body,
        out_shape=[jax.ShapeDtypeStruct(s, d) for s, d in outs],
        in_specs=[pl.BlockSpec(memory_space=pltpu.VMEM)] * len(args),
        out_specs=[pl.BlockSpec(memory_space=pltpu.VMEM)] * len(outs),
        scratch_shapes=list(scratch),
        cost_estimate=pl.CostEstimate(flops=flops, bytes_accessed=nbytes, transcendentals=0),
        compiler_params=pltpu.CompilerParams(vmem_limit_bytes=40 * 2**20),
    )(*args)


def head(h):
    return slice(h * DH, (h + 1) * DH)


def causal(block):
    rows = lax.broadcasted_iota(jnp.int32, (block, block), 0)
    return lax.broadcasted_iota(jnp.int32, (block, block), 1) <= rows


def local_kv_kernel(k_ref, v_ref, kv_ref):
    for h in range(k_ref.shape[1] // DH):
        kv_ref[head(h), :] = dot(k_ref[:, head(h)], v_ref[:, head(h)], 0, 0).astype(BF16)


def prefix_kernel(backward, parts_ref, sums_ref):
    count = parts_ref.shape[0]
    total = jnp.zeros(parts_ref.shape[1:], F32)
    for turn in range(count):
        at = count - 1 - turn if backward else turn
        sums_ref[at] = total.astype(BF16)
        total = total + parts_ref[at].astype(F32)


def early_kernel(q_ref, k_ref, v_ref, c_ref, w_ref, attend_ref, within_ref, dnormed_ref):
    mask = causal(q_ref.shape[0])
    for h in range(q_ref.shape[1] // DH):
        scores = dot(q_ref[:, head(h)], k_ref[:, head(h)], 1, 1)
        attend = jnp.where(mask, scores, 0.0).astype(BF16)
        attend_ref[h] = attend
        within_ref[:, head(h)] = dot(attend, v_ref[:, head(h)], 1, 0)
    dnormed_ref[...] = dot(c_ref[...], w_ref[...], 1, 0)


def middle_kernel(q_ref, prior_ref, within_ref, dnormed_ref, normed_ref, dmixed_ref, u_ref):
    for h in range(q_ref.shape[1] // DH):
        q = q_ref[:, head(h)]
        mixed = within_ref[:, head(h)] + dot(q, prior_ref[head(h), :], 1, 0)
        scale = lax.rsqrt(jnp.mean(mixed * mixed, axis=-1, keepdims=True) + EPSILON)
        normed = mixed * scale
        normed_ref[:, head(h)] = normed.astype(BF16)
        dnormed = dnormed_ref[:, head(h)]
        along = jnp.mean(dnormed * normed, axis=-1, keepdims=True)
        dmixed = ((dnormed - normed * along) * scale).astype(BF16)
        dmixed_ref[:, head(h)] = dmixed
        u_ref[head(h), :] = dot(q, dmixed, 0, 0).astype(BF16)


def late_kernel(
    q_ref, k_ref, v_ref, w_ref, attend_ref, prior_ref, normed_ref, dmixed_ref,
    output_ref, gq_ref, gk_ref, gv_ref,
):
    mask = causal(q_ref.shape[0])
    output_ref[...] = dot(normed_ref[...], w_ref[...], 1, 1).astype(BF16)
    for h in range(q_ref.shape[1] // DH):
        dmixed = dmixed_ref[:, head(h)]
        back = jnp.where(mask, dot(dmixed, v_ref[:, head(h)], 1, 1), 0.0).astype(BF16)
        gq = dot(back, k_ref[:, head(h)], 1, 0) + dot(dmixed, prior_ref[head(h), :], 1, 1)
        gq_ref[:, head(h)] = gq.astype(BF16)
        gk_ref[:, head(h)] = dot(back, q_ref[:, head(h)], 0, 0)
        gv_ref[:, head(h)] = dot(attend_ref[h], dmixed, 0, 0)


def last_kernel(k_ref, v_ref, later_ref, gk_part_ref, gv_part_ref, gk_ref, gv_ref):
    for h in range(k_ref.shape[1] // DH):
        later = later_ref[head(h), :]
        gk = gk_part_ref[:, head(h)] + dot(v_ref[:, head(h)], later, 1, 1)
        gk_ref[:, head(h)] = gk.astype(BF16)
        gv = gv_part_ref[:, head(h)] + dot(k_ref[:, head(h)], later, 1, 0)
        gv_ref[:, head(h)] = gv.astype(BF16)


def scan(state, count, backward):
    parts = state.reshape(count, state.shape[0] // count, state.shape[1])
    parts = lax.all_to_all(parts, "seq", 0, 0, tiled=True)
    (sums,) = call(functools.partial(prefix_kernel, backward), [(parts.shape, BF16)], parts)
    sums = lax.all_to_all(sums, "seq", 0, 0, tiled=True)
    return sums.reshape(state.shape)


def flip(x, axis, count, bits):
    return lax.ppermute(x, axis, [(i, i ^ bits) for i in range(count)])


def gather_weight(weight, dp, seq):
    if dp != 2 or seq % 2:
        return lax.all_gather(weight, "dp", axis=0, tiled=True)
    half = weight.shape[0] // 2
    core = lax.axis_index("seq") % 2
    group = lax.axis_index("dp")
    mine = lax.dynamic_slice_in_dim(weight, core * half, half, 0)
    got = flip(mine, "dp", dp, 1)
    other = flip(got, "seq", seq, 1)
    low = jnp.where(core == 0, got, other)
    high = jnp.where(core == 0, other, got)
    far = jnp.concatenate([low, high], axis=0)
    return jnp.where(
        group == 0, jnp.concatenate([weight, far], 0), jnp.concatenate([far, weight], 0)
    )


def pick_kernel(piece, pieces, c_ref, d_ref, out_ref, turned):
    tokens = c_ref.shape[0]
    columns = c_ref.shape[1]
    place = lax.axis_index("dp") * lax.axis_size("seq") + lax.axis_index("seq")
    for at, ref in enumerate((c_ref, d_ref)):
        rows = ref[...].astype(F32).T
        turned[:, :, at * tokens : (at + 1) * tokens] = rows.reshape(columns // piece, piece, tokens)
    for r, bits in enumerate(pieces):
        out_ref[r * piece : (r + 1) * piece, :] = turned[jnp.bitwise_xor(place, bits)].astype(BF16)


def product_kernel(split, cot_ref, n_ref, m_ref, *outs):
    tokens = n_ref.shape[0]
    rows = cot_ref.shape[0] // split
    for i, out in enumerate(outs):
        at = slice(i * rows, (i + 1) * rows)
        total = dot(cot_ref[at, :tokens], n_ref[...], 1, 0)
        total = total + dot(cot_ref[at, tokens:], m_ref[...], 1, 0)
        out[...] = total.astype(out.dtype)


def spread_kernel(own_ref, a_ref, b_ref, c_ref, keep_ref, *sends):
    rows = keep_ref.shape[0]
    for i, out in enumerate((keep_ref, *sends)):
        at = slice(i * rows, (i + 1) * rows)
        total = own_ref[at, :] + a_ref[at, :].astype(F32)
        total = total + b_ref[at, :].astype(F32) + c_ref[at, :].astype(F32)
        out[...] = total.astype(out.dtype)


def finish_kernel(factor, own_ref, a_ref, b_ref, c_ref, out_ref):
    total = own_ref[...] + a_ref[...].astype(F32)
    total = total + b_ref[...].astype(F32) + c_ref[...].astype(F32)
    out_ref[...] = total * factor


def local(queries, keys, values, cotangent, out_weight, *, dp, seq):
    local_seqs, block, features = queries.shape
    outputs = cotangent.shape[2]
    rows = local_seqs * block
    heads = features // DH
    q, k, v = (x.reshape(rows, features) for x in (queries, keys, values))
    cot = cotangent.reshape(rows, outputs)
    factor = 1.0 / math.sqrt(rows * dp * seq)
    tuned = dp == 2 and seq == 16

    weight = gather_weight(out_weight, dp, seq)
    (kv,) = call(local_kv_kernel, [((features, DH), BF16)], k, v)
    prior = scan(kv, seq, False)
    if tuned:
        cot_other = flip(cot, "seq", seq, 1)
        piece = outputs // (dp * seq)
        groups = [(x << 4) | (y << 1) for x in (0, 1) for y in (0, 1)]
        pieces = [g | (z << 2) for g in groups for z in range(4)]
        (turned,) = call(
            functools.partial(pick_kernel, piece, pieces),
            [((outputs // 2, 2 * rows), BF16)], cot, cot_other,
            scratch=[pltpu.VMEM((dp * seq, piece, 2 * rows), F32)],
        )
    attend, within, dnormed = call(
        early_kernel,
        [((heads, block, block), BF16), ((rows, features), F32), ((rows, features), F32)],
        q, k, v, cot, weight,
    )
    normed, dmixed, u = call(
        middle_kernel,
        [((rows, features), BF16), ((rows, features), BF16), ((features, DH), BF16)],
        q, prior, within, dnormed,
    )
    if tuned:
        normed_other = flip(normed, "seq", seq, 1)
    later = scan(u, seq, True)
    output, gq, gk_part, gv_part = call(
        late_kernel,
        [((rows, outputs), BF16), ((rows, features), BF16), ((rows, features), F32), ((rows, features), F32)],
        q, k, v, weight, attend, prior, normed, dmixed,
    )
    if tuned:
        size = outputs // 2 // 4
        own, s1, s2, s3 = call(
            functools.partial(product_kernel, 4),
            [((size, features), F32)] + [((size, features), BF16)] * 3,
            turned, normed, normed_other,
        )
        axes = ("dp", "seq")
        got = [flip(s, axes, dp * seq, bits) for s, bits in zip((s1, s2, s3), groups[1:])]
        keep, *sends = call(
            spread_kernel,
            [((piece, features), F32)] + [((piece, features), BF16)] * 3,
            own, *got,
        )
        got = [flip(s, "seq", seq, z << 2) for z, s in enumerate(sends, 1)]
        (grad_weight,) = call(
            functools.partial(finish_kernel, factor), [((piece, features), F32)], keep, *got
        )
    else:
        partial = dot(cot, normed, 0, 0) * factor
        grad_weight = lax.psum_scatter(partial, ("dp", "seq"), scatter_dimension=0, tiled=True)
    gk, gv = call(
        last_kernel, [((rows, features), BF16)] * 2, k, v, later, gk_part, gv_part
    )
    shape = queries.shape
    return (
        output.reshape(cotangent.shape), gq.reshape(shape), gk.reshape(shape), gv.reshape(shape),
        grad_weight,
    )


def solution(mesh):
    dp, seq = mesh.shape["dp"], mesh.shape["seq"]
    return jax.shard_map(
        functools.partial(local, dp=dp, seq=seq),
        mesh=mesh,
        in_specs=(P("dp", "seq", None),) * 4 + (P("dp", None),),
        out_specs=(P("dp", "seq", None),) * 4 + (P(("dp", "seq"), None),),
        check_vma=False,
    )
```

time: 319 us -> 111 us (0.35)
  waiting for transfers between devices: 254 us -> 48.2 us
  starting transfers between devices: 0.16 us -> 29.8 us
  matrix products: 17.8 us -> 0 us
  other arithmetic: 16.2 us -> 2.24 us
  Pallas kernels: 0 us -> 13.6 us
  between operations: 14 us -> 0.91 us
    all_gather x3 -> x0, waiting for transfers between devices: 130 us -> none  [the longest x2 98.1 us: entering(): gathered = lax.all_gather(x.astype(jnp.bfloat16), axis)]
    unnamed x5 -> x0, waiting for transfers between devices: 124 us -> none
    ppermute x0 -> x10, waiting for transfers between devices: none -> 25.1 us  [flip(): return lax.ppermute(x, axis, [(i, i ^ bits) for i in range(count)])]
    all_to_all x0 -> x4, waiting for transfers between devices: none -> 23.2 us  [the longest x2 19.5 us: scan(): parts = lax.all_to_all(parts, 'seq', 0, 0, tiled=True)]
    all_to_all x0 -> x4, starting transfers between devices: none -> 18.2 us  [the longest x2 10.5 us: scan(): parts = lax.all_to_all(parts, 'seq', 0, 0, tiled=True)]
    dot_general x19 -> x0, matrix products: 17.8 us -> none  [the longest x1 2.66 us: contract_rows(): lax.dot_general(left, right, (((0,), (0,)), ((), ())), preferred_element_...]
    add x15 -> x0, other arithmetic: 16.1 us -> none  [adding(): return earlier + latter]
    pallas_call x0 -> x11, Pallas kernels: none -> 13.6 us  [call(): pl.pallas_call(body, out_shape=[jax.ShapeDtypeStruct(s, d) for s, d in ou...]
  transfers between devices with their start and end apart: 4 -> 14, of which waited for: 4 -> 8; matrix products, arithmetic and copies ran while one was open for 14% -> 2% of each run, Pallas kernels for 0% -> 10%
where the time goes in v1:
time: 111 us; the launch traced here: 110 us
  waiting for transfers between devices  48.2 us (43%)
  starting transfers between devices  29.8 us (27%)
  local copies, waits for them, and re-layouts  14.9 us (13%)
  Pallas kernels  13.6 us (12%)
  other arithmetic  2.24 us (2%)
    ppermute x10, waiting for transfers between devices, flip(): return lax.ppermute(x, axis, [(i, i ^ bits) for i in range(count)])  25.1 us
    all_to_all x2, waiting for transfers between devices, scan(): parts = lax.all_to_all(parts, 'seq', 0, 0, tiled=True)  19.5 us
    unnamed x44, local copies, waits for them, and re-layouts  13.8 us
    pallas_call x11, Pallas kernels, call(): pl.pallas_call(body, out_shape=[jax.ShapeDtypeStruct(s, d) for s, d in ou...  13.6 us
    ppermute x10, starting transfers between devices, flip(): return lax.ppermute(x, axis, [(i, i ^ bits) for i in range(count)])  11.6 us
    all_to_all x2, starting transfers between devices, scan(): parts = lax.all_to_all(parts, 'seq', 0, 0, tiled=True)  10.5 us
    all_to_all x2, starting transfers between devices, scan(): sums = lax.all_to_all(sums, 'seq', 0, 0, tiled=True)  7.73 us
    all_to_all x2, waiting for transfers between devices, scan(): sums = lax.all_to_all(sums, 'seq', 0, 0, tiled=True)  3.66 us
  transfers between devices with their start and end apart: 14, of which 8 were waited for; matrix products, arithmetic and copies ran while one was open for 2% of the time, Pallas kernels for 10%

profile of v1, /device:TPU:0, one launch (start us, length us, event | category | flops | bytes accessed | tf_op | source)
XLA Modules:
  0.0 109.7 jit_solution(6138521206231918009)
XLA Ops:
  0.6 1.1 constant_dynamic-slice_fusion
  1.7 3.0 %collective-permute-start = (bf16[256,1024]{1,0:T(8,128)(2,1)S(1)}, bf16[256,1024]{1,0:T(8,128)(2,1)S(1)}, u32[]{:S(2)}, u32[]{:S(2)}) collective-permute-start(bf16[256,1024]{1,0:T(8,128)(2,1)S(1)} %constant_dynamic-slice_fusion), channel_id=1, source_target_pairs={{0,16},{16,0},{1,17},{17,1},{2,18},{18,2},{3,19},{19,3},{4,20},{20... | collective-permute-start | bytes 1572872 | tf_op jit(solution)/shard_map/ppermute | solution.py:117
  4.7 11.9 %collective-permute-done = bf16[256,1024]{1,0:T(8,128)(2,1)S(1)} collective-permute-done((bf16[256,1024]{1,0:T(8,128)(2,1)S(1)}, bf16[256,1024]{1,0:T(8,128)(2,1)S(1)}, u32[]{:S(2)}, u32[]{:S(2)}) %collective-permute-start) | collective-permute-done | bytes 524320 | tf_op jit(solution)/shard_map/ppermute | solution.py:117
  16.7 0.9 copy-done
  17.6 0.9 copy-done.2
  18.6 1.0 shard_map.93
  19.5 6.3 %all-to-all-start = ((bf16[16,64,128]{2,1,0:T(8,128)(2,1)}), bf16[16,64,128]{2,1,0:T(8,128)(2,1)S(1)}, u32[]{:S(2)}, u32[]{:S(2)}) async-start(bf16[16,64,128]{2,1,0:T(8,128)(2,1)} %bitcast.4), calls=%async_computation | async-start | bytes 524288 | tf_op jit(solution)/shard_map/all_to_all | solution.py:110
  25.8 10.0 %all-to-all-done.parts_ref = bf16[16,64,128]{2,1,0:T(8,128)(2,1)S(1)} async-done(((bf16[16,64,128]{2,1,0:T(8,128)(2,1)}), bf16[16,64,128]{2,1,0:T(8,128)(2,1)S(1)}, u32[]{:S(2)}, u32[]{:S(2)}) %all-to-all-start) | async-done | bytes 262176 | tf_op jit(solution)/shard_map/all_to_all | solution.py:110
  36.6 3.5 %all-to-all-start.1 = ((bf16[16,64,128]{2,1,0:T(8,128)(2,1)}), bf16[16,64,128]{2,1,0:T(8,128)(2,1)S(1)}, u32[]{:S(2)}, u32[]{:S(2)}) async-start(bf16[16,64,128]{2,1,0:T(8,128)(2,1)} %shard_map.94), calls=%async_computation.1 | async-start | bytes 524288 | tf_op jit(solution)/shard_map/all_to_all | solution.py:112
  40.3 2.2 %maximum_select_fusion.w_ref = bf16[1024,1024]{1,0:T(8,128)(2,1)S(1)} fusion(bf16[256,1024]{1,0:T(8,128)(2,1)S(1)} %get-tuple-element.46, bf16[256,1024]{1,0:T(8,128)(2,1)S(1)} %get-tuple-element.45, bf16[512,1024]{1,0:T(8,128)(2,1)} %param.9, pred[]{:T(512)S(6)} %eq.9), kind=kLoop, calls=%fused_computation | loop fusion | flops 13631488 | bytes 4194305 | tf_op jit(solution)/shard_map/jit(_where)/select_n | solution.py:132
  42.5 1.6 %shard_map.92 = (bf16[8,128,128]{2,1,0:T(8,128)(2,1)S(1)}, f32[128,1024]{1,0:T(8,128)S(1)}, f32[128,1024]{1,0:T(8,128)S(1)}) custom-call(bf16[128,1024]{1,0:T(8,128)(2,1)S(1)} %bitcast.20, bf16[128,1024]{1,0:T(8,128)(2,1)S(1)} %bitcast.13, bf16[128,1024]{1,0:T(8,128)(2,1)S(1)} %bitcast.17, bf16[128,1024]{1,0:T(8,128)(2,1)S(1)} %bitcast.25, ...), custom_call_target="tpu_custom_call" | custom-call | flops 100000000 | bytes 4456448 | tf_op jit(solution)/shard_map/pallas_call | solution.py:26
  46.5 3.7 %all-to-all-done.1 = bf16[16,64,128]{2,1,0:T(8,128)(2,1)S(1)} async-done(((bf16[16,64,128]{2,1,0:T(8,128)(2,1)}), bf16[16,64,128]{2,1,0:T(8,128)(2,1)S(1)}, u32[]{:S(2)}, u32[]{:S(2)}) %all-to-all-start.1) | async-done | bytes 262176 | tf_op jit(solution)/shard_map/all_to_all | solution.py:112
  50.2 1.0 copy-done.14
  51.2 1.0 copy-done.16
  55.1 4.2 %all-to-all-start.2 = ((bf16[16,64,128]{2,1,0:T(8,128)(2,1)}), bf16[16,64,128]{2,1,0:T(8,128)(2,1)}, u32[]{:S(2)}, u32[]{:S(2)}) async-start(bf16[16,64,128]{2,1,0:T(8,128)(2,1)} %bitcast.28), calls=%async_computation.2 | async-start | bytes 524288 | tf_op jit(solution)/shard_map/all_to_all | solution.py:110
  59.9 9.5 %all-to-all-done.2.parts_ref = bf16[16,64,128]{2,1,0:T(8,128)(2,1)} async-done(((bf16[16,64,128]{2,1,0:T(8,128)(2,1)}), bf16[16,64,128]{2,1,0:T(8,128)(2,1)}, u32[]{:S(2)}, u32[]{:S(2)}) %all-to-all-start.2) | async-done | bytes 262176 | tf_op jit(solution)/shard_map/all_to_all | solution.py:110
  69.4 1.0 shard_map.97
  71.1 4.2 %all-to-all-start.3 = ((bf16[16,64,128]{2,1,0:T(8,128)(2,1)}), bf16[16,64,128]{2,1,0:T(8,128)(2,1)}, u32[]{:S(2)}, u32[]{:S(2)}) async-start(bf16[16,64,128]{2,1,0:T(8,128)(2,1)} %copy-done.6), calls=%async_computation.3 | async-start | bytes 524288 | tf_op jit(solution)/shard_map/all_to_all | solution.py:112
  75.3 1.2 %shard_map.99.cot_ref = bf16[512,256]{1,0:T(8,128)(2,1)S(1)} custom-call(bf16[128,1024]{1,0:T(8,128)(2,1)S(1)} %bitcast.27, bf16[128,1024]{1,0:T(8,128)(2,1)} %collective-permute-done.2.d_ref), custom_call_target="tpu_custom_call" | custom-call | flops 100000000 | bytes 786432 | tf_op jit(solution)/shard_map/pallas_call | solution.py:26
  76.6 0.9 copy-done.8
  77.5 1.6 %shard_map.100 = (f32[128,1024]{1,0:T(8,128)S(1)}, bf16[128,1024]{1,0:T(8,128)(2,1)S(1)}, bf16[128,1024]{1,0:T(8,128)(2,1)S(1)}, bf16[128,1024]{1,0:T(8,128)(2,1)S(1)}) custom-call(bf16[512,256]{1,0:T(8,128)(2,1)S(1)} %shard_map.99.cot_ref, bf16[128,1024]{1,0:T(8,128)(2,1)S(1)} %copy-done.8, bf16[128,1024]{1,0:T(8,128)(2,1)} %collective-permute-done.3.m_ref), custom_call_target="tpu_custom_call" | custom-call | flops 100000000 | bytes 2097152 | tf_op jit(solution)/shard_map/pallas_call | solution.py:26
  79.2 1.8 %collective-permute-start.4 = (bf16[128,1024]{1,0:T(8,128)(2,1)S(1)}, bf16[128,1024]{1,0:T(8,128)(2,1)S(1)}, u32[]{:S(2)}, u32[]{:S(2)}) collective-permute-start(bf16[128,1024]{1,0:T(8,128)(2,1)S(1)} %get-tuple-element.38), channel_id=1, source_target_pairs={{0,2},{1,3},{2,0},{3,1},{4,6},{5,7},{6,4},{7,5},{8,10},{9,11},{10,... | collective-permute-start | bytes 786440 | tf_op jit(solution)/shard_map/ppermute | solution.py:117
  81.0 1.5 %collective-permute-start.5 = (bf16[128,1024]{1,0:T(8,128)(2,1)S(1)}, bf16[128,1024]{1,0:T(8,128)(2,1)S(1)}, u32[]{:S(2)}, u32[]{:S(2)}) collective-permute-start(bf16[128,1024]{1,0:T(8,128)(2,1)S(1)} %get-tuple-element.39), channel_id=1, source_target_pairs={{0,16},{1,17},{2,18},{3,19},{4,20},{5,21},{6,22},{7,23},{8,24},{9,... | collective-permute-start | bytes 786440 | tf_op jit(solution)/shard_map/ppermute | solution.py:117
  82.7 6.7 %collective-permute-done.4.a_ref = bf16[128,1024]{1,0:T(8,128)(2,1)S(1)} collective-permute-done((bf16[128,1024]{1,0:T(8,128)(2,1)S(1)}, bf16[128,1024]{1,0:T(8,128)(2,1)S(1)}, u32[]{:S(2)}, u32[]{:S(2)}) %collective-permute-start.4) | collective-permute-done | bytes 262176 | tf_op jit(solution)/shard_map/ppermute | solution.py:117
  90.2 4.3 %collective-permute-done.6.c_ref = bf16[128,1024]{1,0:T(8,128)(2,1)S(1)} collective-permute-done((bf16[128,1024]{1,0:T(8,128)(2,1)S(1)}, bf16[128,1024]{1,0:T(8,128)(2,1)S(1)}, u32[]{:S(2)}, u32[]{:S(2)}) %collective-permute-start.6) | collective-permute-done | bytes 262176 | tf_op jit(solution)/shard_map/ppermute | solution.py:117
  94.6 1.7 %collective-permute-start.7 = (bf16[32,1024]{1,0:T(8,128)(2,1)S(1)}, bf16[32,1024]{1,0:T(8,128)(2,1)S(1)}, u32[]{:S(2)}, u32[]{:S(2)}) collective-permute-start(bf16[32,1024]{1,0:T(8,128)(2,1)S(1)} %get-tuple-element.42), channel_id=1, source_target_pairs={{0,4},{1,5},{2,6},{3,7},{4,0},{5,1},{6,2},{7,3},{8,12},{9,13},{10,... | collective-permute-start | bytes 196616 | tf_op jit(solution)/shard_map/ppermute | solution.py:117
  96.3 2.4 %collective-permute-start.8 = (bf16[32,1024]{1,0:T(8,128)(2,1)S(1)}, bf16[32,1024]{1,0:T(8,128)(2,1)S(1)}, u32[]{:S(2)}, u32[]{:S(2)}) collective-permute-start(bf16[32,1024]{1,0:T(8,128)(2,1)S(1)} %get-tuple-element.43), channel_id=1, source_target_pairs={{0,8},{1,9},{2,10},{3,11},{4,12},{5,13},{6,14},{7,15},{8,0},{9,1},... | collective-permute-start | bytes 196616 | tf_op jit(solution)/shard_map/ppermute | solution.py:117
  99.1 2.7 %shard_map.96 = (bf16[128,1024]{1,0:T(8,128)(2,1)}, bf16[128,1024]{1,0:T(8,128)(2,1)}, f32[128,1024]{1,0:T(8,128)S(1)}, f32[128,1024]{1,0:T(8,128)S(1)}) custom-call(bf16[128,1024]{1,0:T(8,128)(2,1)S(1)} %bitcast.22, bf16[128,1024]{1,0:T(8,128)(2,1)S(1)} %bitcast.14, bf16[128,1024]{1,0:T(8,128)(2,1)S(1)} %bitcast.18, ...), custom_call_target="tpu_custom_call" | custom-call | flops 100000000 | bytes 5505024 | tf_op jit(solution)/shard_map/pallas_call | solution.py:26
  103.4 1.4 %collective-permute-done.9.c_ref = bf16[32,1024]{1,0:T(8,128)(2,1)S(1)} collective-permute-done((bf16[32,1024]{1,0:T(8,128)(2,1)S(1)}, bf16[32,1024]{1,0:T(8,128)(2,1)S(1)}, u32[]{:S(2)}, u32[]{:S(2)}) %collective-permute-start.9) | collective-permute-done | bytes 65568 | tf_op jit(solution)/shard_map/ppermute | solution.py:117
  105.5 1.0 copy-done.10
  106.6 1.0 copy-done.12
  107.6 2.1 %shard_map.98 = (bf16[128,1024]{1,0:T(8,128)(2,1)}, bf16[128,1024]{1,0:T(8,128)(2,1)}) custom-call(bf16[128,1024]{1,0:T(8,128)(2,1)S(1)} %bitcast.15, bf16[128,1024]{1,0:T(8,128)(2,1)S(1)} %bitcast.19, bf16[1024,128]{1,0:T(8,128)(2,1)} %bitcast.9.later_ref, f32[128,1024]{1,0:T(8,128)S(1)} %copy-done.10, f32[128,1024]{1,0:T(8,128)S(1)} %copy-done.12), custom_call_target="tpu_custom_call" | custom-call | flops 100000000 | bytes 2359296 | tf_op jit(solution)/shard_map/pallas_call | solution.py:26
  (54 shorter events, 11.1 us)
Async XLA Ops:
  1.7 14.9 %collective-permute-start = (bf16[256,1024]{1,0:T(8,128)(2,1)S(1)}, bf16[256,1024]{1,0:T(8,128)(2,1)S(1)}, u32[]{:S(2)}, u32[]{:S(2)}) collective-permute-start(bf16[256,1024]{1,0:T(8,128)(2,1)S(1)} %constant_dynamic-slice_fusion), channel_id=1, source_target_pairs={{0,16},{16,0},{1,17},{17,1},{2,18},{18,2},{3,19},{19,3},{4,20},{20... | collective-permute-start | bytes 1572872 | tf_op jit(solution)/shard_map/ppermute | solution.py:117
  16.7 23.5 %collective-permute-start.1 = (bf16[256,1024]{1,0:T(8,128)(2,1)S(1)}, bf16[256,1024]{1,0:T(8,128)(2,1)S(1)}, u32[]{:S(2)}, u32[]{:S(2)}) collective-permute-start(bf16[256,1024]{1,0:T(8,128)(2,1)S(1)} %collective-permute-done), channel_id=1, source_target_pairs={{0,1},{1,0},{2,3},{3,2},{4,5},{5,4},{6,7},{7,6},{8,9},{9,8},{10,11... | collective-permute-start | bytes 1572872 | tf_op jit(solution)/shard_map/ppermute | solution.py:117
  16.7 1.0 copy-start
  17.6 0.9 copy-start.2
  19.5 16.4 %all-to-all-start = ((bf16[16,64,128]{2,1,0:T(8,128)(2,1)}), bf16[16,64,128]{2,1,0:T(8,128)(2,1)S(1)}, u32[]{:S(2)}, u32[]{:S(2)}) async-start(bf16[16,64,128]{2,1,0:T(8,128)(2,1)} %bitcast.4), calls=%async_computation | async-start | bytes 524288 | tf_op jit(solution)/shard_map/all_to_all | solution.py:110
  36.6 13.5 %all-to-all-start.1 = ((bf16[16,64,128]{2,1,0:T(8,128)(2,1)}), bf16[16,64,128]{2,1,0:T(8,128)(2,1)S(1)}, u32[]{:S(2)}, u32[]{:S(2)}) async-start(bf16[16,64,128]{2,1,0:T(8,128)(2,1)} %shard_map.94), calls=%async_computation.1 | async-start | bytes 524288 | tf_op jit(solution)/shard_map/all_to_all | solution.py:112
  40.3 2.2 %copy-start.1 = (bf16[1,128,1024]{2,1,0:T(8,128)(2,1)S(1)}, bf16[1,128,1024]{2,1,0:T(8,128)(2,1)}, u32[]{:S(2)}) copy-start(bf16[1,128,1024]{2,1,0:T(8,128)(2,1)} %param.6) | copy-start | bytes 786436
  40.3 2.2 %copy-start.3 = (bf16[1,128,1024]{2,1,0:T(8,128)(2,1)S(1)}, bf16[1,128,1024]{2,1,0:T(8,128)(2,1)}, u32[]{:S(2)}) copy-start(bf16[1,128,1024]{2,1,0:T(8,128)(2,1)} %param.7) | copy-start | bytes 786436
  40.3 2.2 %copy-start.4 = (bf16[1,128,1024]{2,1,0:T(8,128)(2,1)S(1)}, bf16[1,128,1024]{2,1,0:T(8,128)(2,1)}, u32[]{:S(2)}) copy-start(bf16[1,128,1024]{2,1,0:T(8,128)(2,1)} %param.5) | copy-start | bytes 786436
  40.3 2.2 %copy-start.5 = (bf16[1,128,1024]{2,1,0:T(8,128)(2,1)S(1)}, bf16[1,128,1024]{2,1,0:T(8,128)(2,1)}, u32[]{:S(2)}) copy-start(bf16[1,128,1024]{2,1,0:T(8,128)(2,1)} %param.8) | copy-start | bytes 786436
  44.2 0.8 copy-start.13
  45.0 0.8 copy-start.15
  50.2 1.0 copy-start.14
  51.2 1.0 copy-start.16
  55.1 14.2 %all-to-all-start.2 = ((bf16[16,64,128]{2,1,0:T(8,128)(2,1)}), bf16[16,64,128]{2,1,0:T(8,128)(2,1)}, u32[]{:S(2)}, u32[]{:S(2)}) async-start(bf16[16,64,128]{2,1,0:T(8,128)(2,1)} %bitcast.28), calls=%async_computation.2 | async-start | bytes 524288 | tf_op jit(solution)/shard_map/all_to_all | solution.py:110
  59.3 16.0 %collective-permute-start.2 = (bf16[128,1024]{1,0:T(8,128)(2,1)S(1)}, bf16[128,1024]{1,0:T(8,128)(2,1)}, u32[]{:S(2)}, u32[]{:S(2)}) collective-permute-start(bf16[128,1024]{1,0:T(8,128)(2,1)S(1)} %bitcast.26), channel_id=1, source_target_pairs={{0,1},{1,0},{2,3},{3,2},{4,5},{5,4},{6,7},{7,6},{8,9},{9,8},{10,11... | collective-permute-start | bytes 786440 | tf_op jit(solution)/shard_map/ppermute | solution.py:117
  59.5 17.0 %collective-permute-start.3 = (bf16[128,1024]{1,0:T(8,128)(2,1)}, bf16[128,1024]{1,0:T(8,128)(2,1)}, u32[]{:S(2)}, u32[]{:S(2)}) collective-permute-start(bf16[128,1024]{1,0:T(8,128)(2,1)} %copy-done.7), channel_id=1, source_target_pairs={{0,1},{1,0},{2,3},{3,2},{4,5},{5,4},{6,7},{7,6},{8,9},{9,8},{10,11... | collective-permute-start | bytes 786440 | tf_op jit(solution)/shard_map/ppermute | solution.py:117
  70.4 0.7 copy-start.6
  71.1 34.4 %all-to-all-start.3 = ((bf16[16,64,128]{2,1,0:T(8,128)(2,1)}), bf16[16,64,128]{2,1,0:T(8,128)(2,1)}, u32[]{:S(2)}, u32[]{:S(2)}) async-start(bf16[16,64,128]{2,1,0:T(8,128)(2,1)} %copy-done.6), calls=%async_computation.3 | async-start | bytes 524288 | tf_op jit(solution)/shard_map/all_to_all | solution.py:112
  75.3 23.8 %copy-start.19 = (bf16[8,128,128]{2,1,0:T(8,128)(2,1)S(1)}, bf16[8,128,128]{2,1,0:T(8,128)(2,1)}, u32[]{:S(2)}) copy-start(bf16[8,128,128]{2,1,0:T(8,128)(2,1)} %copy-done.18) | copy-start | bytes 786436
  75.3 23.8 %copy-start.21 = (bf16[128,1024]{1,0:T(8,128)(2,1)S(1)}, bf16[128,1024]{1,0:T(8,128)(2,1)}, u32[]{:S(2)}) copy-start(bf16[128,1024]{1,0:T(8,128)(2,1)} %copy-done.20) | copy-start | bytes 786436
  76.6 1.0 copy-start.8
  79.2 10.2 %collective-permute-start.4 = (bf16[128,1024]{1,0:T(8,128)(2,1)S(1)}, bf16[128,1024]{1,0:T(8,128)(2,1)S(1)}, u32[]{:S(2)}, u32[]{:S(2)}) collective-permute-start(bf16[128,1024]{1,0:T(8,128)(2,1)S(1)} %get-tuple-element.38), channel_id=1, source_target_pairs={{0,2},{1,3},{2,0},{3,1},{4,6},{5,7},{6,4},{7,5},{8,10},{9,11},{10,... | collective-permute-start | bytes 786440 | tf_op jit(solution)/shard_map/ppermute | solution.py:117
  81.0 9.2 %collective-permute-start.5 = (bf16[128,1024]{1,0:T(8,128)(2,1)S(1)}, bf16[128,1024]{1,0:T(8,128)(2,1)S(1)}, u32[]{:S(2)}, u32[]{:S(2)}) collective-permute-start(bf16[128,1024]{1,0:T(8,128)(2,1)S(1)} %get-tuple-element.39), channel_id=1, source_target_pairs={{0,16},{1,17},{2,18},{3,19},{4,20},{5,21},{6,22},{7,23},{8,24},{9,... | collective-permute-start | bytes 786440 | tf_op jit(solution)/shard_map/ppermute | solution.py:117
  82.5 12.0 %collective-permute-start.6 = (bf16[128,1024]{1,0:T(8,128)(2,1)S(1)}, bf16[128,1024]{1,0:T(8,128)(2,1)S(1)}, u32[]{:S(2)}, u32[]{:S(2)}) collective-permute-start(bf16[128,1024]{1,0:T(8,128)(2,1)S(1)} %get-tuple-element.40), channel_id=1, source_target_pairs={{0,18},{1,19},{2,16},{3,17},{4,22},{5,23},{6,20},{7,21},{8,26},{9,... | collective-permute-start | bytes 786440 | tf_op jit(solution)/shard_map/ppermute | solution.py:117
  94.6 8.8 %collective-permute-start.7 = (bf16[32,1024]{1,0:T(8,128)(2,1)S(1)}, bf16[32,1024]{1,0:T(8,128)(2,1)S(1)}, u32[]{:S(2)}, u32[]{:S(2)}) collective-permute-start(bf16[32,1024]{1,0:T(8,128)(2,1)S(1)} %get-tuple-element.42), channel_id=1, source_target_pairs={{0,4},{1,5},{2,6},{3,7},{4,0},{5,1},{6,2},{7,3},{8,12},{9,13},{10,... | collective-permute-start | bytes 196616 | tf_op jit(solution)/shard_map/ppermute | solution.py:117
  96.3 7.1 %collective-permute-start.8 = (bf16[32,1024]{1,0:T(8,128)(2,1)S(1)}, bf16[32,1024]{1,0:T(8,128)(2,1)S(1)}, u32[]{:S(2)}, u32[]{:S(2)}) collective-permute-start(bf16[32,1024]{1,0:T(8,128)(2,1)S(1)} %get-tuple-element.43), channel_id=1, source_target_pairs={{0,8},{1,9},{2,10},{3,11},{4,12},{5,13},{6,14},{7,15},{8,0},{9,1},... | collective-permute-start | bytes 196616 | tf_op jit(solution)/shard_map/ppermute | solution.py:117
  98.8 6.1 %collective-permute-start.9 = (bf16[32,1024]{1,0:T(8,128)(2,1)S(1)}, bf16[32,1024]{1,0:T(8,128)(2,1)S(1)}, u32[]{:S(2)}, u32[]{:S(2)}) collective-permute-start(bf16[32,1024]{1,0:T(8,128)(2,1)S(1)} %get-tuple-element.44), channel_id=1, source_target_pairs={{0,12},{1,13},{2,14},{3,15},{4,8},{5,9},{6,10},{7,11},{8,4},{9,5},... | collective-permute-start | bytes 196616 | tf_op jit(solution)/shard_map/ppermute | solution.py:117
  101.8 0.8 copy-start.9
  102.6 0.8 copy-start.11
  105.5 1.0 copy-start.10
  106.6 1.0 copy-start.12
  (4 other events, 2.8 us)

commit v2 on v0

v2 whole, which is shorter than its diff:
```python
import functools
import math

import jax
import jax.numpy as jnp
from jax import lax
from jax.experimental import pallas as pl
from jax.experimental.pallas import tpu as pltpu
from jax.sharding import PartitionSpec as P

DH = 128
SLAB = 4
EPSILON = 1e-05
BF16 = jnp.bfloat16
F32 = jnp.float32


def dot(left, right, left_dim, right_dim):
    return lax.dot_general(
        left, right, (((left_dim,), (right_dim,)), ((), ())), preferred_element_type=F32
    )


def call(body, outs, *args, flops=10**8, scratch=(), far=()):
    nbytes = sum(a.size * a.dtype.itemsize for a in args)
    nbytes += sum(math.prod(s) * jnp.dtype(d).itemsize for s, d in outs)
    return pl.pallas_call(
        body,
        out_shape=[jax.ShapeDtypeStruct(s, d) for s, d in outs],
        in_specs=[
            pl.BlockSpec(memory_space=pltpu.HBM) if i in far else pl.BlockSpec()
            for i in range(len(args))
        ],
        scratch_shapes=list(scratch),
        cost_estimate=pl.CostEstimate(flops=flops, bytes_accessed=nbytes, transcendentals=0),
        compiler_params=pltpu.CompilerParams(vmem_limit_bytes=32 * 2**20),
    )(*args)


def after(x, *others):
    return lax.optimization_barrier((x, *others))[0]


def flip(x, axis, count, bits):
    return lax.ppermute(x, axis, [(i, i ^ bits) for i in range(count)])


def head(h):
    return slice(h * DH, (h + 1) * DH)


def cut(start, size):
    return pl.ds(pl.multiple_of(start * size, size), size)


def member(r):
    return jnp.bitwise_xor(lax.rem(lax.axis_index("seq"), SLAB), r)


def causal(block):
    rows = lax.broadcasted_iota(jnp.int32, (block, block), 0)
    return lax.broadcasted_iota(jnp.int32, (block, block), 1) <= rows


def fetch(pairs, sems):
    copies = [pltpu.make_async_copy(a, b, sems.at[i]) for i, (a, b) in enumerate(pairs)]
    for copy in copies:
        copy.start()
    for copy in copies:
        copy.wait()


def start_kernel(k_hbm, v_hbm, *refs):
    states, (k_ref, v_ref, sems) = refs[:SLAB], refs[SLAB:]
    fetch([(k_hbm, k_ref), (v_hbm, v_ref)], sems)
    width = k_ref.shape[1] // SLAB
    for r, out in enumerate(states):
        k = k_ref[:, cut(member(r), width)]
        v = v_ref[:, cut(member(r), width)]
        for h in range(width // DH):
            out[head(h), :] = dot(k[:, head(h)], v[:, head(h)], 0, 0).astype(BF16)


def pack_kernel(q_hbm, k_hbm, v_hbm, w_hbm, *refs):
    outs, (q_ref, k_ref, v_ref, w_ref, sems) = refs[: SLAB + 2], refs[SLAB + 2 :]
    fetch([(q_hbm, q_ref), (k_hbm, k_ref), (v_hbm, v_ref), (w_hbm, w_ref)], sems)
    width = q_ref.shape[1] // SLAB
    block = q_ref.shape[0]
    for r, out in enumerate(outs[:SLAB]):
        for i, ref in enumerate((q_ref, k_ref, v_ref)):
            out[i * block : (i + 1) * block, :] = ref[:, cut(member(r), width)]
    for r, out in zip((0, 2), outs[SLAB:]):
        out[...] = w_ref[:, cut(member(r), width)]


def total_kernel(*refs):
    *parts, out = refs
    total = parts[0][...].astype(F32)
    for part in parts[1:]:
        total = total + part[...].astype(F32)
    out[...] = total.astype(BF16)


def early_kernel(groups, *refs):
    tokens, cots = refs[:SLAB], refs[SLAB : 2 * SLAB]
    weights = refs[2 * SLAB : 2 * SLAB + groups]
    attend_ref, within_ref, dnormed_ref = refs[2 * SLAB + groups :]
    block = cots[0].shape[0]
    width = within_ref.shape[1]
    heads = width // DH
    mask = causal(block)
    rows = weights[0].shape[0]
    me = lax.axis_index("dp")
    for r in range(SLAB):
        at = slice(r * block, (r + 1) * block)
        total = dot(cots[r][:, cut(me, rows)], weights[0][...], 1, 0)
        for j in range(1, groups):
            total = total + dot(cots[r][:, cut(jnp.bitwise_xor(me, j), rows)], weights[j][...], 1, 0)
        dnormed_ref[at, :] = total
        for h in range(heads):
            q, k, v = (tokens[r][i * block : (i + 1) * block, head(h)] for i in range(3))
            attend = jnp.where(mask, dot(q, k, 1, 1), 0.0).astype(BF16)
            attend_ref[r * heads + h] = attend
            within_ref[at, head(h)] = dot(attend, v, 1, 0)


def middle_kernel(*refs):
    tokens, states = refs[:SLAB], refs[SLAB : 2 * SLAB]
    *before, within_ref, dnormed_ref = refs[2 * SLAB : -(SLAB + 5)]
    normeds = refs[-(SLAB + 5) : -5]
    dmixed_ref, prior_ref, u_ref, all_u_ref, running = refs[-5:]
    block = tokens[0].shape[0] // 3
    width = within_ref.shape[1]
    heads = width // DH
    for r in range(SLAB):
        running[member(r)] = states[r][...].astype(F32)
    total = before[0][...].astype(F32)
    for ref in before[1:]:
        total = total + ref[...].astype(F32)
    for i in range(SLAB):
        total, running[i] = total + running[i], total
    sums = [jnp.zeros((DH, DH), F32)] * heads
    for r in range(SLAB):
        at = slice(r * block, (r + 1) * block)
        prior = running[member(r)].astype(BF16)
        prior_ref[r] = prior
        for h in range(heads):
            q = tokens[r][:block, head(h)]
            mixed = within_ref[at, head(h)] + dot(q, prior[head(h), :], 1, 0)
            scale = lax.rsqrt(jnp.mean(mixed * mixed, axis=-1, keepdims=True) + EPSILON)
            normed = mixed * scale
            normeds[r][:, head(h)] = normed.astype(BF16)
            dnormed = dnormed_ref[at, head(h)]
            along = jnp.mean(dnormed * normed, axis=-1, keepdims=True)
            dmixed = ((dnormed - normed * along) * scale).astype(BF16)
            dmixed_ref[at, head(h)] = dmixed
            u = dot(q, dmixed, 0, 0)
            u_ref[r, head(h), :] = u
            sums[h] = sums[h] + u
    for h in range(heads):
        all_u_ref[head(h), :] = sums[h].astype(BF16)


def late_kernel(*refs):
    tokens = refs[:SLAB]
    attend_ref, dmixed_ref, prior_ref = refs[SLAB : SLAB + 3]
    gqs, part_ref = refs[SLAB + 3 : -1], refs[-1]
    block, width = gqs[0].shape
    heads = width // DH
    mask = causal(block)
    for r in range(SLAB):
        at = slice(r * block, (r + 1) * block)
        for h in range(heads):
            q, k, v = (tokens[r][i * block : (i + 1) * block, head(h)] for i in range(3))
            dmixed = dmixed_ref[at, head(h)]
            back = jnp.where(mask, dot(dmixed, v, 1, 1), 0.0).astype(BF16)
            gq = dot(back, k, 1, 0) + dot(dmixed, prior_ref[r, head(h), :], 1, 1)
            gqs[r][:, head(h)] = gq.astype(BF16)
            part_ref[r, :block, head(h)] = dot(back, q, 0, 0)
            part_ref[r, block:, head(h)] = dot(attend_ref[r * heads + h], dmixed, 0, 0)


def last_kernel(*refs):
    tokens = refs[:SLAB]
    *behind, u_ref, part_ref = refs[SLAB : -(SLAB + 1)]
    outs, running = refs[-(SLAB + 1) : -1], refs[-1]
    block = tokens[0].shape[0] // 3
    heads = outs[0].shape[1] // DH
    for r in range(SLAB):
        running[member(r)] = u_ref[r]
    total = behind[0][...].astype(F32)
    for ref in behind[1:]:
        total = total + ref[...].astype(F32)
    for i in reversed(range(SLAB)):
        total, running[i] = total + running[i], total
    for r in range(SLAB):
        later = running[member(r)].astype(BF16)
        for h in range(heads):
            k, v = (tokens[r][i * block : (i + 1) * block, head(h)] for i in (1, 2))
            gk = part_ref[r, :block, head(h)] + dot(v, later[head(h), :], 1, 1)
            gv = part_ref[r, block:, head(h)] + dot(k, later[head(h), :], 1, 0)
            outs[r][:block, head(h)] = gk.astype(BF16)
            outs[r][block:, head(h)] = gv.astype(BF16)


def output_kernel(groups, *refs):
    normeds, gqs = refs[:SLAB], refs[SLAB : 2 * SLAB]
    own_ref, *far = refs[2 * SLAB : 2 * SLAB + 1 + (groups - 1) * SLAB]
    out_ref, gq_ref, normed_ref = refs[2 * SLAB + 1 + (groups - 1) * SLAB :]
    width = normeds[0].shape[1]
    rows = own_ref.shape[0]
    me = lax.axis_index("dp")
    for r in range(SLAB):
        gq_ref[:, cut(member(r), width)] = gqs[r][...]
        normed_ref[:, cut(member(r), width)] = normeds[r][...]
    out_ref[:, cut(me, rows)] = dot(normed_ref[...], own_ref[...], 1, 1).astype(BF16)
    for j in range(1, groups):
        total = dot(normeds[0][...], far[(j - 1) * SLAB][...], 1, 1)
        for r in range(1, SLAB):
            total = total + dot(normeds[r][...], far[(j - 1) * SLAB + r][...], 1, 1)
        out_ref[:, cut(jnp.bitwise_xor(me, j), rows)] = total.astype(BF16)


def join_kernel(*refs):
    parts, (gk_ref, gv_ref) = refs[:SLAB], refs[SLAB:]
    block = gk_ref.shape[0]
    width = parts[0].shape[1]
    for r in range(SLAB):
        gk_ref[:, cut(member(r), width)] = parts[r][:block, :]
        gv_ref[:, cut(member(r), width)] = parts[r][block:, :]


def product_kernel(slabs, *refs):
    cots, normeds, (keep_ref, send_ref) = refs[:SLAB], refs[SLAB : 2 * SLAB], refs[2 * SLAB :]
    me = lax.axis_index("dp")
    slab = lax.div(lax.axis_index("seq"), SLAB)
    rows = keep_ref.shape[0] // slabs
    for j, out in enumerate((keep_ref, send_ref)):
        for d in range(slabs):
            at = jnp.bitwise_xor(me, j) * slabs + jnp.bitwise_xor(slab, d)
            total = dot(cots[0][:, cut(at, rows)], normeds[0][...], 0, 0)
            for r in range(1, SLAB):
                total = total + dot(cots[r][:, cut(at, rows)], normeds[r][...], 0, 0)
            out[d * rows : (d + 1) * rows, :] = total.astype(out.dtype)


def spread_kernel(own_ref, got_ref, keep_ref, *sends):
    rows = keep_ref.shape[0]
    for d, out in enumerate((keep_ref, *sends)):
        at = slice(d * rows, (d + 1) * rows)
        out[...] = (own_ref[at, :] + got_ref[at, :].astype(F32)).astype(out.dtype)


def share_kernel(slabs, *refs):
    own_ref, *got = refs[:slabs]
    outs, total_ref = refs[slabs:-1], refs[-1]
    total = own_ref[...]
    for ref in got:
        total = total + ref[...].astype(F32)
    total_ref[...] = total
    rows = outs[0].shape[0]
    for r, out in enumerate(outs):
        out[...] = total_ref[cut(member(r), rows), :]


def finish_kernel(factor, *refs):
    parts, out_ref = refs[:-1], refs[-1]
    width = parts[0].shape[1]
    for r in range(SLAB):
        out_ref[:, cut(member(r), width)] = parts[r][...] * factor


def local(queries, keys, values, cotangent, out_weight, *, dp, seq):
    local_seqs, block, features = queries.shape
    outputs = cotangent.shape[2]
    rows = local_seqs * block
    slabs = seq // SLAB
    width = features // SLAB
    heads = width // DH
    q, k, v = (x.reshape(rows, features) for x in (queries, keys, values))
    cot = cotangent.reshape(rows, outputs)
    factor = 1.0 / math.sqrt(rows * dp * seq)

    def spread(parts):
        return [parts[0]] + [flip(parts[r], "seq", seq, r) for r in range(1, SLAB)]

    def along(x, sign):
        found = []
        for d in range(1, slabs):
            step = sign * d * SLAB
            pairs = [(i, i + step) for i in range(seq) if 0 <= i + step < seq]
            found.append(lax.ppermute(x, "seq", pairs))
        return found

    states = call(
        start_kernel, [((width, DH), BF16)] * SLAB, k, v, far=(0, 1),
        scratch=[pltpu.VMEM(k.shape, BF16), pltpu.VMEM(v.shape, BF16), pltpu.SemaphoreType.DMA((2,))],
    )
    got_states = spread(states)
    q2, k2, v2, w2, cot2 = lax.optimization_barrier((q, k, v, out_weight, cot, states[0]))[:5]
    *tokens, w_own, w_next = call(
        pack_kernel,
        [((3 * rows, width), BF16)] * SLAB + [((out_weight.shape[0], width), BF16)] * 2,
        q2, k2, v2, w2, far=(0, 1, 2, 3),
        scratch=[pltpu.VMEM(x.shape, BF16) for x in (q, k, v, out_weight)]
        + [pltpu.SemaphoreType.DMA((4,))],
    )
    cot_y = flip(cot2, "seq", seq, 2)
    cots = [cot, flip(cot2, "seq", seq, 1), cot_y, flip(cot_y, "seq", seq, 1)]
    tokens = spread(tokens)
    w_far = []
    for j in range(1, dp):
        w0, w1 = flip(w_own, "dp", dp, j), flip(w_next, "dp", dp, j)
        w_far.append([w0, flip(w0, "seq", seq, 1), w1, flip(w1, "seq", seq, 1)])

    (slab_kv,) = call(total_kernel, [((width, DH), BF16)], *got_states)
    before = along(slab_kv, 1)
    attend, within, dnormed = call(
        functools.partial(early_kernel, dp),
        [((SLAB * heads, rows, rows), BF16), ((SLAB * rows, width), F32), ((SLAB * rows, width), F32)],
        *tokens, *cots, w_own, *(w[0] for w in w_far),
    )
    *normeds, dmixed, prior, u, slab_u = call(
        middle_kernel,
        [((rows, width), BF16)] * SLAB
        + [((SLAB * rows, width), BF16), ((SLAB, width, DH), BF16), ((SLAB, width, DH), F32),
           ((width, DH), BF16)],
        *tokens, *got_states, *before, within, dnormed,
        scratch=[pltpu.VMEM((SLAB, width, DH), F32)],
    )
    behind = along(slab_u, -1)
    tuned = dp == 2 and outputs // (dp * slabs) % 128 == 0
    if tuned:
        piece = outputs // (dp * slabs)
        keep, send = call(
            functools.partial(product_kernel, slabs),
            [((outputs // dp, width), F32), ((outputs // dp, width), BF16)],
            *cots, *normeds,
        )
        got = flip(send, "dp", dp, 1)
    *gqs, parts = call(
        late_kernel,
        [((rows, width), BF16)] * SLAB + [((SLAB, 2 * rows, width), F32)],
        *tokens, attend, dmixed, prior,
    )
    got_normeds = spread(normeds)
    got_gqs = spread(gqs)
    grads = call(
        last_kernel, [((2 * rows, width), BF16)] * SLAB, *tokens, *behind, u, parts,
        scratch=[pltpu.VMEM((SLAB, width, DH), F32)],
    )
    got_grads = spread(grads)
    output, gq, normed = call(
        functools.partial(output_kernel, dp),
        [((rows, outputs), BF16), ((rows, features), BF16), ((rows, features), BF16)],
        *got_normeds, *got_gqs, out_weight, *(x for w in w_far for x in w),
    )
    if tuned:
        keep, *sends = call(
            spread_kernel, [((piece, width), F32)] + [((piece, width), BF16)] * (slabs - 1), keep, got
        )
        got = [flip(s, "seq", seq, d * SLAB) for d, s in enumerate(sends, 1)]
        shares = call(
            functools.partial(share_kernel, slabs), [((piece // SLAB, width), F32)] * SLAB, keep, *got,
            scratch=[pltpu.VMEM((piece, width), F32)],
        )
        (grad_weight,) = call(
            functools.partial(finish_kernel, factor),
            [((piece // SLAB, features), F32)], *spread(shares),
        )
    else:
        partial = dot(cot, normed, 0, 0) * factor
        grad_weight = lax.psum_scatter(partial, ("dp", "seq"), scatter_dimension=0, tiled=True)
    gk, gv = call(join_kernel, [((rows, features), BF16)] * 2, *got_grads)
    shape = queries.shape
    return (
        output.reshape(cotangent.shape), gq.reshape(shape), gk.reshape(shape), gv.reshape(shape),
        grad_weight,
    )


def solution(mesh):
    dp, seq = mesh.shape["dp"], mesh.shape["seq"]
    return jax.shard_map(
        functools.partial(local, dp=dp, seq=seq),
        mesh=mesh,
        in_specs=(P("dp", "seq", None),) * 4 + (P("dp", None),),
        out_specs=(P("dp", "seq", None),) * 4 + (P(("dp", "seq"), None),),
        check_vma=False,
    )
```

time: 319 us -> 76.5 us (0.24)
  waiting for transfers between devices: 254 us -> 25.3 us
  starting transfers between devices: 0.16 us -> 36.9 us
  matrix products: 17.8 us -> 0 us
  other arithmetic: 16.2 us -> 0 us
  between operations: 14 us -> 0.88 us
  local copies, waits for them, and re-layouts: 15.7 us -> 4.69 us
  Pallas kernels: 0 us -> 8.37 us
    all_gather x3 -> x0, waiting for transfers between devices: 130 us -> none  [the longest x2 98.1 us: entering(): gathered = lax.all_gather(x.astype(jnp.bfloat16), axis)]
    unnamed x5 -> x0, waiting for transfers between devices: 124 us -> none
    ppermute x0 -> x35, starting transfers between devices: none -> 36.9 us  [the longest x29 23.5 us: flip(): return lax.ppermute(x, axis, [(i, i ^ bits) for i in range(count)])]
    ppermute x0 -> x35, waiting for transfers between devices: none -> 25.3 us  [the longest x29 20.3 us: flip(): return lax.ppermute(x, axis, [(i, i ^ bits) for i in range(count)])]
    dot_general x19 -> x0, matrix products: 17.8 us -> none  [the longest x1 2.66 us: contract_rows(): lax.dot_general(left, right, (((0,), (0,)), ((), ())), preferred_element_...]
    add x15 -> x0, other arithmetic: 16.1 us -> none  [adding(): return earlier + latter]
    pallas_call x0 -> x13, Pallas kernels: none -> 8.37 us  [call(): pl.pallas_call(body, out_shape=[jax.ShapeDtypeStruct(s, d) for s, d in ou...]
    unnamed x27 -> x14, local copies, waits for them, and re-layouts: 11.7 us -> 4.69 us
  transfers between devices with their start and end apart: 4 -> 35, of which waited for: 4 -> 10; matrix products, arithmetic and copies ran while one was open for 14% -> 0% of each run, Pallas kernels for 0% -> 10%
where the time goes in v2:
time: 76.5 us; the launch traced here: 76.1 us
  starting transfers between devices  36.9 us (48%)
  waiting for transfers between devices  25.3 us (33%)
  Pallas kernels  8.37 us (11%)
  local copies, waits for them, and re-layouts  4.69 us (6%)
  between operations  0.88 us (1%)
    ppermute x29, starting transfers between devices, flip(): return lax.ppermute(x, axis, [(i, i ^ bits) for i in range(count)])  23.5 us
    ppermute x29, waiting for transfers between devices, flip(): return lax.ppermute(x, axis, [(i, i ^ bits) for i in range(count)])  20.3 us
    ppermute x6, starting transfers between devices, along(): found.append(lax.ppermute(x, 'seq', pairs))  13.4 us
    pallas_call x13, Pallas kernels, call(): pl.pallas_call(body, out_shape=[jax.ShapeDtypeStruct(s, d) for s, d in ou...  8.37 us
    ppermute x6, waiting for transfers between devices, along(): found.append(lax.ppermute(x, 'seq', pairs))  4.94 us
    unnamed x14, local copies, waits for them, and re-layouts  4.69 us
  transfers between devices with their start and end apart: 35, of which 10 were waited for; matrix products, arithmetic and copies ran while one was open for 0% of the time, Pallas kernels for 10%

profile of v2, /device:TPU:0, one launch (start us, length us, event | category | flops | bytes accessed | tf_op | source)
XLA Modules:
  0.0 76.1 jit_solution(9603400257531724876)
XLA Ops:
  0.6 0.9 %copy-done.3 = bf16[1,128,1024]{2,1,0:T(8,128)(2,1)S(1)} copy-done((bf16[1,128,1024]{2,1,0:T(8,128)(2,1)S(1)}, bf16[1,128,1024]{2,1,0:T(8,128)(2,1)}, u32[]{:S(2)}) %copy-start.3) | copy-done | bytes 262168
  1.6 0.9 %copy-done.5 = bf16[1,128,1024]{2,1,0:T(8,128)(2,1)S(1)} copy-done((bf16[1,128,1024]{2,1,0:T(8,128)(2,1)S(1)}, bf16[1,128,1024]{2,1,0:T(8,128)(2,1)}, u32[]{:S(2)}) %copy-start.5) | copy-done | bytes 262168
  3.5 3.0 %collective-permute-start.10 = (bf16[128,1024]{1,0:T(8,128)(2,1)S(1)}, bf16[128,1024]{1,0:T(8,128)(2,1)S(1)}, u32[]{:S(2)}, u32[]{:S(2)}) collective-permute-start(bf16[128,1024]{1,0:T(8,128)(2,1)S(1)} %bitcast.8), channel_id=1, source_target_pairs={{0,2},{1,3},{2,0},{3,1},{4,6},{5,7},{6,4},{7,5},{8,10},{9,11},{10,... | collective-permute-start | bytes 786440 | tf_op jit(solution)/shard_map/ppermute | solution.py:45
  6.5 1.2 %copy-done = bf16[512,1024]{1,0:T(8,128)(2,1)S(1)} copy-done((bf16[512,1024]{1,0:T(8,128)(2,1)S(1)}, bf16[512,1024]{1,0:T(8,128)(2,1)}, u32[]{:S(2)}) %copy-start) | copy-done | bytes 1048600
  7.7 0.9 %copy-done.6 = bf16[1,128,1024]{2,1,0:T(8,128)(2,1)S(1)} copy-done((bf16[1,128,1024]{2,1,0:T(8,128)(2,1)S(1)}, bf16[1,128,1024]{2,1,0:T(8,128)(2,1)}, u32[]{:S(2)}) %copy-start.6) | copy-done | bytes 262168
  9.6 1.8 %collective-permute-start.4 = (bf16[256,128]{1,0:T(8,128)(2,1)S(1)}, bf16[256,128]{1,0:T(8,128)(2,1)S(1)}, u32[]{:S(2)}, u32[]{:S(2)}) collective-permute-start(bf16[256,128]{1,0:T(8,128)(2,1)S(1)} %get-tuple-element.64), channel_id=1, source_target_pairs={{0,2},{1,3},{2,0},{3,1},{4,6},{5,7},{6,4},{7,5},{8,10},{9,11},{10,... | collective-permute-start | bytes 196616 | tf_op jit(solution)/shard_map/ppermute | solution.py:45
  11.3 0.9 %collective-permute-start.5 = (bf16[256,128]{1,0:T(8,128)(2,1)S(1)}, bf16[256,128]{1,0:T(8,128)(2,1)S(1)}, u32[]{:S(2)}, u32[]{:S(2)}) collective-permute-start(bf16[256,128]{1,0:T(8,128)(2,1)S(1)} %get-tuple-element.65), channel_id=1, source_target_pairs={{0,3},{1,2},{2,1},{3,0},{4,7},{5,6},{6,5},{7,4},{8,11},{9,10},{10,... | collective-permute-start | bytes 196616 | tf_op jit(solution)/shard_map/ppermute | solution.py:45
  12.2 6.7 %collective-permute-done.4.refs_2_.refs_6_ = bf16[256,128]{1,0:T(8,128)(2,1)S(1)} collective-permute-done((bf16[256,128]{1,0:T(8,128)(2,1)S(1)}, bf16[256,128]{1,0:T(8,128)(2,1)S(1)}, u32[]{:S(2)}, u32[]{:S(2)}) %collective-permute-start.4) | collective-permute-done | bytes 65568 | tf_op jit(solution)/shard_map/ppermute | solution.py:45
  18.9 1.9 %collective-permute-start.12 = (bf16[512,256]{1,0:T(8,128)(2,1)S(1)}, bf16[512,256]{1,0:T(8,128)(2,1)S(1)}, u32[]{:S(2)}, u32[]{:S(2)}) collective-permute-start(bf16[512,256]{1,0:T(8,128)(2,1)S(1)} %get-tuple-element.67.refs_8_), channel_id=1, source_target_pairs={{0,16},{16,0},{1,17},{17,1},{2,18},{18,2},{3,19},{19,3},{4,20},{20... | collective-permute-start | bytes 786440 | tf_op jit(solution)/shard_map/ppermute | solution.py:45
  21.4 1.7 %collective-permute-start.2 = (bf16[384,256]{1,0:T(8,128)(2,1)S(1)}, bf16[384,256]{1,0:T(8,128)(2,1)S(1)}, u32[]{:S(2)}, u32[]{:S(2)}) collective-permute-start(bf16[384,256]{1,0:T(8,128)(2,1)S(1)} %get-tuple-element.62), channel_id=1, source_target_pairs={{0,3},{1,2},{2,1},{3,0},{4,7},{5,6},{6,5},{7,4},{8,11},{9,10},{10,... | collective-permute-start | bytes 589832 | tf_op jit(solution)/shard_map/ppermute | solution.py:45
  23.1 4.9 %collective-permute-done.2.refs_3_ = bf16[384,256]{1,0:T(8,128)(2,1)S(1)} collective-permute-done((bf16[384,256]{1,0:T(8,128)(2,1)S(1)}, bf16[384,256]{1,0:T(8,128)(2,1)S(1)}, u32[]{:S(2)}, u32[]{:S(2)}) %collective-permute-start.2) | collective-permute-done | bytes 196640 | tf_op jit(solution)/shard_map/ppermute | solution.py:45
  28.0 3.8 %collective-permute-start.6 = (bf16[256,128]{1,0:T(8,128)(2,1)S(1)}, bf16[256,128]{1,0:T(8,128)(2,1)S(1)}, u32[]{:S(2)}, u32[]{:S(2)}) collective-permute-start(bf16[256,128]{1,0:T(8,128)(2,1)S(1)} %shard_map.94), channel_id=1, source_target_pairs={{0,4},{1,5},{2,6},{3,7},{4,8},{5,9},{6,10},{7,11},{8,12},{9,13},{1... | collective-permute-start | bytes 196616 | tf_op jit(solution)/shard_map/ppermute | solution.py:292
  31.8 4.5 %collective-permute-start.7 = (bf16[256,128]{1,0:T(8,128)(2,1)S(1)}, bf16[256,128]{1,0:T(8,128)(2,1)S(1)}, u32[]{:S(2)}, u32[]{:S(2)}) collective-permute-start(bf16[256,128]{1,0:T(8,128)(2,1)S(1)} %shard_map.94), channel_id=1, source_target_pairs={{0,8},{1,9},{2,10},{3,11},{4,12},{5,13},{6,14},{7,15},{16,24},{17,... | collective-permute-start | bytes 196616 | tf_op jit(solution)/shard_map/ppermute | solution.py:292
  36.3 1.3 %collective-permute-start.8 = (bf16[256,128]{1,0:T(8,128)(2,1)S(1)}, bf16[256,128]{1,0:T(8,128)(2,1)S(1)}, u32[]{:S(2)}, u32[]{:S(2)}) collective-permute-start(bf16[256,128]{1,0:T(8,128)(2,1)S(1)} %shard_map.94), channel_id=1, source_target_pairs={{0,12},{1,13},{2,14},{3,15},{16,28},{17,29},{18,30},{19,31}} | collective-permute-start | bytes 196616 | tf_op jit(solution)/shard_map/ppermute | solution.py:292
  38.2 1.1 %shard_map.95 = (bf16[8,128,128]{2,1,0:T(8,128)(2,1)S(1)}, f32[512,256]{1,0:T(8,128)S(1)}, f32[512,256]{1,0:T(8,128)S(1)}) custom-call(bf16[384,256]{1,0:T(8,128)(2,1)S(1)} %get-tuple-element.59.refs_0_, bf16[384,256]{1,0:T(8,128)(2,1)S(1)} %collective-permute-done.refs_1_, bf16[384,256]{1,0:T(8,128)(2,1)S(1)} %collective-permute-done.1.refs_2_, ...), custom_call_target="tpu_custom_call" | custom-call | flops 100000000 | bytes 3670016 | tf_op jit(solution)/shard_map/pallas_call | solution.py:27
  41.1 1.6 %collective-permute-start.28 = (bf16[512,256]{1,0:T(8,128)(2,1)S(1)}, bf16[512,256]{1,0:T(8,128)(2,1)S(1)}, u32[]{:S(2)}, u32[]{:S(2)}) collective-permute-start(bf16[512,256]{1,0:T(8,128)(2,1)S(1)} %get-tuple-element.94), channel_id=1, source_target_pairs={{0,16},{16,0},{1,17},{17,1},{2,18},{18,2},{3,19},{19,3},{4,20},{20... | collective-permute-start | bytes 786440 | tf_op jit(solution)/shard_map/ppermute | solution.py:45
  42.7 1.3 %collective-permute-start.22 = (bf16[256,128]{1,0:T(8,128)(2,1)S(1)}, bf16[256,128]{1,0:T(8,128)(2,1)S(1)}, u32[]{:S(2)}, u32[]{:S(2)}) collective-permute-start(bf16[256,128]{1,0:T(8,128)(2,1)S(1)} %get-tuple-element.84), channel_id=1, source_target_pairs={{4,0},{5,1},{6,2},{7,3},{8,4},{9,5},{10,6},{11,7},{12,8},{13,9},{1... | collective-permute-start | bytes 196616 | tf_op jit(solution)/shard_map/ppermute | solution.py:292
  43.9 1.3 %collective-permute-start.23 = (bf16[256,128]{1,0:T(8,128)(2,1)S(1)}, bf16[256,128]{1,0:T(8,128)(2,1)S(1)}, u32[]{:S(2)}, u32[]{:S(2)}) collective-permute-start(bf16[256,128]{1,0:T(8,128)(2,1)S(1)} %get-tuple-element.84), channel_id=1, source_target_pairs={{8,0},{9,1},{10,2},{11,3},{12,4},{13,5},{14,6},{15,7},{24,16},{25,... | collective-permute-start | bytes 196616 | tf_op jit(solution)/shard_map/ppermute | solution.py:292
  45.2 1.3 %collective-permute-start.24 = (bf16[256,128]{1,0:T(8,128)(2,1)S(1)}, bf16[256,128]{1,0:T(8,128)(2,1)S(1)}, u32[]{:S(2)}, u32[]{:S(2)}) collective-permute-start(bf16[256,128]{1,0:T(8,128)(2,1)S(1)} %get-tuple-element.84), channel_id=1, source_target_pairs={{12,0},{13,1},{14,2},{15,3},{28,16},{29,17},{30,18},{31,19}} | collective-permute-start | bytes 196616 | tf_op jit(solution)/shard_map/ppermute | solution.py:292
  46.5 1.4 %shard_map.97 = (bf16[128,256]{1,0:T(8,128)(2,1)S(1)}, bf16[128,256]{1,0:T(8,128)(2,1)S(1)}, bf16[128,256]{1,0:T(8,128)(2,1)S(1)}, bf16[128,256]{1,0:T(8,128)(2,1)S(1)}, f32[4,256,256]{2,1,0:T(8,128)S(1)}) custom-call(bf16[384,256]{1,0:T(8,128)(2,1)S(1)} %get-tuple-element.59.refs_0_, bf16[384,256]{1,0:T(8,128)(2,1)S(1)} %collective-permute-done.refs_1_, ...), custom_call_target="tpu_custom_call" | custom-call | flops 100000000 | bytes 2883584 | tf_op jit(solution)/shard_map/pallas_call | solution.py:27
  48.8 1.5 %collective-permute-start.17 = (bf16[128,256]{1,0:T(8,128)(2,1)S(1)}, bf16[128,256]{1,0:T(8,128)(2,1)S(1)}, u32[]{:S(2)}, u32[]{:S(2)}) collective-permute-start(bf16[128,256]{1,0:T(8,128)(2,1)S(1)} %get-tuple-element.79), channel_id=1, source_target_pairs={{0,2},{1,3},{2,0},{3,1},{4,6},{5,7},{6,4},{7,5},{8,10},{9,11},{10,... | collective-permute-start | bytes 196616 | tf_op jit(solution)/shard_map/ppermute | solution.py:45
  50.4 1.3 %collective-permute-done.23.refs_5_ = bf16[256,128]{1,0:T(8,128)(2,1)S(1)} collective-permute-done((bf16[256,128]{1,0:T(8,128)(2,1)S(1)}, bf16[256,128]{1,0:T(8,128)(2,1)S(1)}, u32[]{:S(2)}, u32[]{:S(2)}) %collective-permute-start.23) | collective-permute-done | bytes 65568 | tf_op jit(solution)/shard_map/ppermute | solution.py:292
  51.7 2.7 %collective-permute-done.24.refs_6_ = bf16[256,128]{1,0:T(8,128)(2,1)S(1)} collective-permute-done((bf16[256,128]{1,0:T(8,128)(2,1)S(1)}, bf16[256,128]{1,0:T(8,128)(2,1)S(1)}, u32[]{:S(2)}, u32[]{:S(2)}) %collective-permute-start.24) | collective-permute-done | bytes 65568 | tf_op jit(solution)/shard_map/ppermute | solution.py:292
  54.4 2.2 %collective-permute-start.30 = (bf16[128,256]{1,0:T(8,128)(2,1)S(1)}, bf16[128,256]{1,0:T(8,128)(2,1)S(1)}, u32[]{:S(2)}, u32[]{:S(2)}) collective-permute-start(bf16[128,256]{1,0:T(8,128)(2,1)S(1)} %get-tuple-element.97), channel_id=1, source_target_pairs={{0,8},{1,9},{2,10},{3,11},{4,12},{5,13},{6,14},{7,15},{8,0},{9,1},... | collective-permute-start | bytes 196616 | tf_op jit(solution)/shard_map/ppermute | solution.py:45
  56.6 2.2 %collective-permute-start.31 = (bf16[128,256]{1,0:T(8,128)(2,1)S(1)}, bf16[128,256]{1,0:T(8,128)(2,1)S(1)}, u32[]{:S(2)}, u32[]{:S(2)}) collective-permute-start(bf16[128,256]{1,0:T(8,128)(2,1)S(1)} %get-tuple-element.98), channel_id=1, source_target_pairs={{0,12},{1,13},{2,14},{3,15},{4,8},{5,9},{6,10},{7,11},{8,4},{9,5},... | collective-permute-start | bytes 196616 | tf_op jit(solution)/shard_map/ppermute | solution.py:45
  59.3 1.6 %collective-permute-start.26 = (bf16[256,256]{1,0:T(8,128)(2,1)S(1)}, bf16[256,256]{1,0:T(8,128)(2,1)S(1)}, u32[]{:S(2)}, u32[]{:S(2)}) collective-permute-start(bf16[256,256]{1,0:T(8,128)(2,1)S(1)} %get-tuple-element.89), channel_id=1, source_target_pairs={{0,2},{1,3},{2,0},{3,1},{4,6},{5,7},{6,4},{7,5},{8,10},{9,11},{10,... | collective-permute-start | bytes 393224 | tf_op jit(solution)/shard_map/ppermute | solution.py:45
  61.9 1.5 %collective-permute-start.14 = (bf16[128,256]{1,0:T(8,128)(2,1)S(1)}, bf16[128,256]{1,0:T(8,128)(2,1)S(1)}, u32[]{:S(2)}, u32[]{:S(2)}) collective-permute-start(bf16[128,256]{1,0:T(8,128)(2,1)S(1)} %get-tuple-element.72.refs_6_), channel_id=1, source_target_pairs={{0,2},{1,3},{2,0},{3,1},{4,6},{5,7},{6,4},{7,5},{8,10},{9,11},{10,... | collective-permute-start | bytes 196616 | tf_op jit(solution)/shard_map/ppermute | solution.py:45
  63.5 6.4 %collective-permute-done.14.refs_2_ = bf16[128,256]{1,0:T(8,128)(2,1)S(1)} collective-permute-done((bf16[128,256]{1,0:T(8,128)(2,1)S(1)}, bf16[128,256]{1,0:T(8,128)(2,1)S(1)}, u32[]{:S(2)}, u32[]{:S(2)}) %collective-permute-start.14) | collective-permute-done | bytes 65568 | tf_op jit(solution)/shard_map/ppermute | solution.py:45
  70.4 1.5 %collective-permute-start.33 = (f32[32,256]{1,0:T(8,128)S(1)}, f32[32,256]{1,0:T(8,128)S(1)}, u32[]{:S(2)}, u32[]{:S(2)}) collective-permute-start(f32[32,256]{1,0:T(8,128)S(1)} %get-tuple-element.101), channel_id=1, source_target_pairs={{0,2},{1,3},{2,0},{3,1},{4,6},{5,7},{6,4},{7,5},{8,10},{9,11},{10,... | collective-permute-start | bytes 98312 | tf_op jit(solution)/shard_map/ppermute | solution.py:45
  72.0 1.5 %shard_map.98 = (bf16[128,1024]{1,0:T(8,128)(2,1)}, bf16[128,1024]{1,0:T(8,128)(2,1)}, bf16[128,1024]{1,0:T(8,128)(2,1)}) custom-call(bf16[128,256]{1,0:T(8,128)(2,1)S(1)} %get-tuple-element.70.refs_0_.refs_4_, bf16[128,256]{1,0:T(8,128)(2,1)S(1)} %collective-permute-done.13.refs_1_, bf16[128,256]{1,0:T(8,128)(2,1)S(1)} %collective-permute-done.14.refs_2_, ...), custom_call_target="tpu_custom_call" | custom-call | flops 100000000 | bytes 3407872 | tf_op jit(solution)/shard_map/pallas_call | solution.py:27
  73.6 0.8 %shard_map.100 = (bf16[128,1024]{1,0:T(8,128)(2,1)}, bf16[128,1024]{1,0:T(8,128)(2,1)}) custom-call(bf16[256,256]{1,0:T(8,128)(2,1)S(1)} %get-tuple-element.87.refs_0_, bf16[256,256]{1,0:T(8,128)(2,1)S(1)} %collective-permute-done.25.refs_1_, bf16[256,256]{1,0:T(8,128)(2,1)S(1)} %collective-permute-done.26.refs_2_, ...), custom_call_target="tpu_custom_call" | custom-call | flops 100000000 | bytes 1048576 | tf_op jit(solution)/shard_map/pallas_call | solution.py:27
  74.4 1.0 %collective-permute-done.34.refs_3_ = f32[32,256]{1,0:T(8,128)S(1)} collective-permute-done((f32[32,256]{1,0:T(8,128)S(1)}, f32[32,256]{1,0:T(8,128)S(1)}, u32[]{:S(2)}, u32[]{:S(2)}) %collective-permute-start.34) | collective-permute-done | bytes 32800 | tf_op jit(solution)/shard_map/ppermute | solution.py:45
  (65 shorter events, 8.6 us)
Async XLA Ops:
  3.5 17.8 %collective-permute-start.10 = (bf16[128,1024]{1,0:T(8,128)(2,1)S(1)}, bf16[128,1024]{1,0:T(8,128)(2,1)S(1)}, u32[]{:S(2)}, u32[]{:S(2)}) collective-permute-start(bf16[128,1024]{1,0:T(8,128)(2,1)S(1)} %bitcast.8), channel_id=1, source_target_pairs={{0,2},{1,3},{2,0},{3,1},{4,6},{5,7},{6,4},{7,5},{8,10},{9,11},{10,... | collective-permute-start | bytes 786440 | tf_op jit(solution)/shard_map/ppermute | solution.py:45
  9.0 11.8 %collective-permute-start = (bf16[384,256]{1,0:T(8,128)(2,1)S(1)}, bf16[384,256]{1,0:T(8,128)(2,1)S(1)}, u32[]{:S(2)}, u32[]{:S(2)}) collective-permute-start(bf16[384,256]{1,0:T(8,128)(2,1)S(1)} %get-tuple-element.60), channel_id=1, source_target_pairs={{0,1},{1,0},{2,3},{3,2},{4,5},{5,4},{6,7},{7,6},{8,9},{9,8},{10,11... | collective-permute-start | bytes 589832 | tf_op jit(solution)/shard_map/ppermute | solution.py:45
  9.1 12.3 %collective-permute-start.1 = (bf16[384,256]{1,0:T(8,128)(2,1)S(1)}, bf16[384,256]{1,0:T(8,128)(2,1)S(1)}, u32[]{:S(2)}, u32[]{:S(2)}) collective-permute-start(bf16[384,256]{1,0:T(8,128)(2,1)S(1)} %get-tuple-element.61), channel_id=1, source_target_pairs={{0,2},{1,3},{2,0},{3,1},{4,6},{5,7},{6,4},{7,5},{8,10},{9,11},{10,... | collective-permute-start | bytes 589832 | tf_op jit(solution)/shard_map/ppermute | solution.py:45
  9.6 9.3 %collective-permute-start.4 = (bf16[256,128]{1,0:T(8,128)(2,1)S(1)}, bf16[256,128]{1,0:T(8,128)(2,1)S(1)}, u32[]{:S(2)}, u32[]{:S(2)}) collective-permute-start(bf16[256,128]{1,0:T(8,128)(2,1)S(1)} %get-tuple-element.64), channel_id=1, source_target_pairs={{0,2},{1,3},{2,0},{3,1},{4,6},{5,7},{6,4},{7,5},{8,10},{9,11},{10,... | collective-permute-start | bytes 196616 | tf_op jit(solution)/shard_map/ppermute | solution.py:45
  11.3 9.5 %collective-permute-start.5 = (bf16[256,128]{1,0:T(8,128)(2,1)S(1)}, bf16[256,128]{1,0:T(8,128)(2,1)S(1)}, u32[]{:S(2)}, u32[]{:S(2)}) collective-permute-start(bf16[256,128]{1,0:T(8,128)(2,1)S(1)} %get-tuple-element.65), channel_id=1, source_target_pairs={{0,3},{1,2},{2,1},{3,0},{4,7},{5,6},{6,5},{7,4},{8,11},{9,10},{10,... | collective-permute-start | bytes 196616 | tf_op jit(solution)/shard_map/ppermute | solution.py:45
  18.9 12.9 %collective-permute-start.12 = (bf16[512,256]{1,0:T(8,128)(2,1)S(1)}, bf16[512,256]{1,0:T(8,128)(2,1)S(1)}, u32[]{:S(2)}, u32[]{:S(2)}) collective-permute-start(bf16[512,256]{1,0:T(8,128)(2,1)S(1)} %get-tuple-element.67.refs_8_), channel_id=1, source_target_pairs={{0,16},{16,0},{1,17},{17,1},{2,18},{18,2},{3,19},{19,3},{4,20},{20... | collective-permute-start | bytes 786440 | tf_op jit(solution)/shard_map/ppermute | solution.py:45
  20.8 15.5 %collective-permute-start.9 = (bf16[128,1024]{1,0:T(8,128)(2,1)S(1)}, bf16[128,1024]{1,0:T(8,128)(2,1)S(1)}, u32[]{:S(2)}, u32[]{:S(2)}) collective-permute-start(bf16[128,1024]{1,0:T(8,128)(2,1)S(1)} %bitcast.9), channel_id=1, source_target_pairs={{0,1},{1,0},{2,3},{3,2},{4,5},{5,4},{6,7},{7,6},{8,9},{9,8},{10,11... | collective-permute-start | bytes 786440 | tf_op jit(solution)/shard_map/ppermute | solution.py:45
  20.8 16.8 %collective-permute-start.20 = (bf16[512,256]{1,0:T(8,128)(2,1)S(1)}, bf16[512,256]{1,0:T(8,128)(2,1)S(1)}, u32[]{:S(2)}, u32[]{:S(2)}) collective-permute-start(bf16[512,256]{1,0:T(8,128)(2,1)S(1)} %get-tuple-element.81), channel_id=1, source_target_pairs={{0,16},{16,0},{1,17},{17,1},{2,18},{18,2},{3,19},{19,3},{4,20},{20... | collective-permute-start | bytes 786440 | tf_op jit(solution)/shard_map/ppermute | solution.py:45
  21.3 16.4 %collective-permute-start.11 = (bf16[128,1024]{1,0:T(8,128)(2,1)S(1)}, bf16[128,1024]{1,0:T(8,128)(2,1)S(1)}, u32[]{:S(2)}, u32[]{:S(2)}) collective-permute-start(bf16[128,1024]{1,0:T(8,128)(2,1)S(1)} %collective-permute-done.10.refs_6_.refs_2_), channel_id=1, source_target_pairs={{0,1},{1,0},{2,3},{3,2},{4,5},{5,4},{6,7},{7,6},{8,9},{9,8},{10,11... | collective-permute-start | bytes 786440 | tf_op jit(solution)/shard_map/ppermute | solution.py:45
  21.4 6.6 %collective-permute-start.2 = (bf16[384,256]{1,0:T(8,128)(2,1)S(1)}, bf16[384,256]{1,0:T(8,128)(2,1)S(1)}, u32[]{:S(2)}, u32[]{:S(2)}) collective-permute-start(bf16[384,256]{1,0:T(8,128)(2,1)S(1)} %get-tuple-element.62), channel_id=1, source_target_pairs={{0,3},{1,2},{2,1},{3,0},{4,7},{5,6},{6,5},{7,4},{8,11},{9,10},{10,... | collective-permute-start | bytes 589832 | tf_op jit(solution)/shard_map/ppermute | solution.py:45
  28.0 11.3 %collective-permute-start.6 = (bf16[256,128]{1,0:T(8,128)(2,1)S(1)}, bf16[256,128]{1,0:T(8,128)(2,1)S(1)}, u32[]{:S(2)}, u32[]{:S(2)}) collective-permute-start(bf16[256,128]{1,0:T(8,128)(2,1)S(1)} %shard_map.94), channel_id=1, source_target_pairs={{0,4},{1,5},{2,6},{3,7},{4,8},{5,9},{6,10},{7,11},{8,12},{9,13},{1... | collective-permute-start | bytes 196616 | tf_op jit(solution)/shard_map/ppermute | solution.py:292
  31.8 7.5 %collective-permute-start.7 = (bf16[256,128]{1,0:T(8,128)(2,1)S(1)}, bf16[256,128]{1,0:T(8,128)(2,1)S(1)}, u32[]{:S(2)}, u32[]{:S(2)}) collective-permute-start(bf16[256,128]{1,0:T(8,128)(2,1)S(1)} %shard_map.94), channel_id=1, source_target_pairs={{0,8},{1,9},{2,10},{3,11},{4,12},{5,13},{6,14},{7,15},{16,24},{17,... | collective-permute-start | bytes 196616 | tf_op jit(solution)/shard_map/ppermute | solution.py:292
  37.6 7.6 %collective-permute-start.19 = (bf16[512,256]{1,0:T(8,128)(2,1)S(1)}, bf16[512,256]{1,0:T(8,128)(2,1)S(1)}, u32[]{:S(2)}, u32[]{:S(2)}) collective-permute-start(bf16[512,256]{1,0:T(8,128)(2,1)S(1)} %collective-permute-done.12.refs_9_), channel_id=1, source_target_pairs={{0,1},{1,0},{2,3},{3,2},{4,5},{5,4},{6,7},{7,6},{8,9},{9,8},{10,11... | collective-permute-start | bytes 786440 | tf_op jit(solution)/shard_map/ppermute | solution.py:45
  37.7 10.3 %collective-permute-start.21 = (bf16[512,256]{1,0:T(8,128)(2,1)S(1)}, bf16[512,256]{1,0:T(8,128)(2,1)S(1)}, u32[]{:S(2)}, u32[]{:S(2)}) collective-permute-start(bf16[512,256]{1,0:T(8,128)(2,1)S(1)} %collective-permute-done.20.refs_11_), channel_id=1, source_target_pairs={{0,1},{1,0},{2,3},{3,2},{4,5},{5,4},{6,7},{7,6},{8,9},{9,8},{10,11... | collective-permute-start | bytes 786440 | tf_op jit(solution)/shard_map/ppermute | solution.py:45
  41.1 9.2 %collective-permute-start.28 = (bf16[512,256]{1,0:T(8,128)(2,1)S(1)}, bf16[512,256]{1,0:T(8,128)(2,1)S(1)}, u32[]{:S(2)}, u32[]{:S(2)}) collective-permute-start(bf16[512,256]{1,0:T(8,128)(2,1)S(1)} %get-tuple-element.94), channel_id=1, source_target_pairs={{0,16},{16,0},{1,17},{17,1},{2,18},{18,2},{3,19},{19,3},{4,20},{20... | collective-permute-start | bytes 786440 | tf_op jit(solution)/shard_map/ppermute | solution.py:45
  42.7 6.1 %collective-permute-start.22 = (bf16[256,128]{1,0:T(8,128)(2,1)S(1)}, bf16[256,128]{1,0:T(8,128)(2,1)S(1)}, u32[]{:S(2)}, u32[]{:S(2)}) collective-permute-start(bf16[256,128]{1,0:T(8,128)(2,1)S(1)} %get-tuple-element.84), channel_id=1, source_target_pairs={{4,0},{5,1},{6,2},{7,3},{8,4},{9,5},{10,6},{11,7},{12,8},{13,9},{1... | collective-permute-start | bytes 196616 | tf_op jit(solution)/shard_map/ppermute | solution.py:292
  43.9 7.8 %collective-permute-start.23 = (bf16[256,128]{1,0:T(8,128)(2,1)S(1)}, bf16[256,128]{1,0:T(8,128)(2,1)S(1)}, u32[]{:S(2)}, u32[]{:S(2)}) collective-permute-start(bf16[256,128]{1,0:T(8,128)(2,1)S(1)} %get-tuple-element.84), channel_id=1, source_target_pairs={{8,0},{9,1},{10,2},{11,3},{12,4},{13,5},{14,6},{15,7},{24,16},{25,... | collective-permute-start | bytes 196616 | tf_op jit(solution)/shard_map/ppermute | solution.py:292
  45.2 9.1 %collective-permute-start.24 = (bf16[256,128]{1,0:T(8,128)(2,1)S(1)}, bf16[256,128]{1,0:T(8,128)(2,1)S(1)}, u32[]{:S(2)}, u32[]{:S(2)}) collective-permute-start(bf16[256,128]{1,0:T(8,128)(2,1)S(1)} %get-tuple-element.84), channel_id=1, source_target_pairs={{12,0},{13,1},{14,2},{15,3},{28,16},{29,17},{30,18},{31,19}} | collective-permute-start | bytes 196616 | tf_op jit(solution)/shard_map/ppermute | solution.py:292
  48.0 6.4 %collective-permute-start.16 = (bf16[128,256]{1,0:T(8,128)(2,1)S(1)}, bf16[128,256]{1,0:T(8,128)(2,1)S(1)}, u32[]{:S(2)}, u32[]{:S(2)}) collective-permute-start(bf16[128,256]{1,0:T(8,128)(2,1)S(1)} %get-tuple-element.78), channel_id=1, source_target_pairs={{0,1},{1,0},{2,3},{3,2},{4,5},{5,4},{6,7},{7,6},{8,9},{9,8},{10,11... | collective-permute-start | bytes 196616 | tf_op jit(solution)/shard_map/ppermute | solution.py:45
  48.8 7.8 %collective-permute-start.17 = (bf16[128,256]{1,0:T(8,128)(2,1)S(1)}, bf16[128,256]{1,0:T(8,128)(2,1)S(1)}, u32[]{:S(2)}, u32[]{:S(2)}) collective-permute-start(bf16[128,256]{1,0:T(8,128)(2,1)S(1)} %get-tuple-element.79), channel_id=1, source_target_pairs={{0,2},{1,3},{2,0},{3,1},{4,6},{5,7},{6,4},{7,5},{8,10},{9,11},{10,... | collective-permute-start | bytes 196616 | tf_op jit(solution)/shard_map/ppermute | solution.py:45
  50.3 8.9 %collective-permute-start.18 = (bf16[128,256]{1,0:T(8,128)(2,1)S(1)}, bf16[128,256]{1,0:T(8,128)(2,1)S(1)}, u32[]{:S(2)}, u32[]{:S(2)}) collective-permute-start(bf16[128,256]{1,0:T(8,128)(2,1)S(1)} %get-tuple-element.80), channel_id=1, source_target_pairs={{0,3},{1,2},{2,1},{3,0},{4,7},{5,6},{6,5},{7,4},{8,11},{9,10},{10,... | collective-permute-start | bytes 196616 | tf_op jit(solution)/shard_map/ppermute | solution.py:45
  51.7 7.6 %collective-permute-start.13 = (bf16[128,256]{1,0:T(8,128)(2,1)S(1)}, bf16[128,256]{1,0:T(8,128)(2,1)S(1)}, u32[]{:S(2)}, u32[]{:S(2)}) collective-permute-start(bf16[128,256]{1,0:T(8,128)(2,1)S(1)} %get-tuple-element.71.refs_5_), channel_id=1, source_target_pairs={{0,1},{1,0},{2,3},{3,2},{4,5},{5,4},{6,7},{7,6},{8,9},{9,8},{10,11... | collective-permute-start | bytes 196616 | tf_op jit(solution)/shard_map/ppermute | solution.py:45
  54.4 6.5 %collective-permute-start.29 = (bf16[128,256]{1,0:T(8,128)(2,1)S(1)}, bf16[128,256]{1,0:T(8,128)(2,1)S(1)}, u32[]{:S(2)}, u32[]{:S(2)}) collective-permute-start(bf16[128,256]{1,0:T(8,128)(2,1)S(1)} %get-tuple-element.96), channel_id=1, source_target_pairs={{0,4},{1,5},{2,6},{3,7},{4,0},{5,1},{6,2},{7,3},{8,12},{9,13},{10,... | collective-permute-start | bytes 196616 | tf_op jit(solution)/shard_map/ppermute | solution.py:45
  54.4 7.6 %collective-permute-start.30 = (bf16[128,256]{1,0:T(8,128)(2,1)S(1)}, bf16[128,256]{1,0:T(8,128)(2,1)S(1)}, u32[]{:S(2)}, u32[]{:S(2)}) collective-permute-start(bf16[128,256]{1,0:T(8,128)(2,1)S(1)} %get-tuple-element.97), channel_id=1, source_target_pairs={{0,8},{1,9},{2,10},{3,11},{4,12},{5,13},{6,14},{7,15},{8,0},{9,1},... | collective-permute-start | bytes 196616 | tf_op jit(solution)/shard_map/ppermute | solution.py:45
  56.6 6.9 %collective-permute-start.31 = (bf16[128,256]{1,0:T(8,128)(2,1)S(1)}, bf16[128,256]{1,0:T(8,128)(2,1)S(1)}, u32[]{:S(2)}, u32[]{:S(2)}) collective-permute-start(bf16[128,256]{1,0:T(8,128)(2,1)S(1)} %get-tuple-element.98), channel_id=1, source_target_pairs={{0,12},{1,13},{2,14},{3,15},{4,8},{5,9},{6,10},{7,11},{8,4},{9,5},... | collective-permute-start | bytes 196616 | tf_op jit(solution)/shard_map/ppermute | solution.py:45
  59.2 12.7 %collective-permute-start.25 = (bf16[256,256]{1,0:T(8,128)(2,1)S(1)}, bf16[256,256]{1,0:T(8,128)(2,1)S(1)}, u32[]{:S(2)}, u32[]{:S(2)}) collective-permute-start(bf16[256,256]{1,0:T(8,128)(2,1)S(1)} %get-tuple-element.88), channel_id=1, source_target_pairs={{0,1},{1,0},{2,3},{3,2},{4,5},{5,4},{6,7},{7,6},{8,9},{9,8},{10,11... | collective-permute-start | bytes 393224 | tf_op jit(solution)/shard_map/ppermute | solution.py:45
  59.3 14.3 %collective-permute-start.26 = (bf16[256,256]{1,0:T(8,128)(2,1)S(1)}, bf16[256,256]{1,0:T(8,128)(2,1)S(1)}, u32[]{:S(2)}, u32[]{:S(2)}) collective-permute-start(bf16[256,256]{1,0:T(8,128)(2,1)S(1)} %get-tuple-element.89), channel_id=1, source_target_pairs={{0,2},{1,3},{2,0},{3,1},{4,6},{5,7},{6,4},{7,5},{8,10},{9,11},{10,... | collective-permute-start | bytes 393224 | tf_op jit(solution)/shard_map/ppermute | solution.py:45
  60.9 12.7 %collective-permute-start.27 = (bf16[256,256]{1,0:T(8,128)(2,1)S(1)}, bf16[256,256]{1,0:T(8,128)(2,1)S(1)}, u32[]{:S(2)}, u32[]{:S(2)}) collective-permute-start(bf16[256,256]{1,0:T(8,128)(2,1)S(1)} %get-tuple-element.90), channel_id=1, source_target_pairs={{0,3},{1,2},{2,1},{3,0},{4,7},{5,6},{6,5},{7,4},{8,11},{9,10},{10,... | collective-permute-start | bytes 393224 | tf_op jit(solution)/shard_map/ppermute | solution.py:45
  61.9 8.0 %collective-permute-start.14 = (bf16[128,256]{1,0:T(8,128)(2,1)S(1)}, bf16[128,256]{1,0:T(8,128)(2,1)S(1)}, u32[]{:S(2)}, u32[]{:S(2)}) collective-permute-start(bf16[128,256]{1,0:T(8,128)(2,1)S(1)} %get-tuple-element.72.refs_6_), channel_id=1, source_target_pairs={{0,2},{1,3},{2,0},{3,1},{4,6},{5,7},{6,4},{7,5},{8,10},{9,11},{10,... | collective-permute-start | bytes 196616 | tf_op jit(solution)/shard_map/ppermute | solution.py:45
  63.5 6.9 %collective-permute-start.15 = (bf16[128,256]{1,0:T(8,128)(2,1)S(1)}, bf16[128,256]{1,0:T(8,128)(2,1)S(1)}, u32[]{:S(2)}, u32[]{:S(2)}) collective-permute-start(bf16[128,256]{1,0:T(8,128)(2,1)S(1)} %get-tuple-element.73.refs_7_), channel_id=1, source_target_pairs={{0,3},{1,2},{2,1},{3,0},{4,7},{5,6},{6,5},{7,4},{8,11},{9,10},{10,... | collective-permute-start | bytes 196616 | tf_op jit(solution)/shard_map/ppermute | solution.py:45
  69.9 4.5 %collective-permute-start.32 = (f32[32,256]{1,0:T(8,128)S(1)}, f32[32,256]{1,0:T(8,128)S(1)}, u32[]{:S(2)}, u32[]{:S(2)}) collective-permute-start(f32[32,256]{1,0:T(8,128)S(1)} %get-tuple-element.100), channel_id=1, source_target_pairs={{0,1},{1,0},{2,3},{3,2},{4,5},{5,4},{6,7},{7,6},{8,9},{9,8},{10,11... | collective-permute-start | bytes 98312 | tf_op jit(solution)/shard_map/ppermute | solution.py:45
  70.4 4.0 %collective-permute-start.33 = (f32[32,256]{1,0:T(8,128)S(1)}, f32[32,256]{1,0:T(8,128)S(1)}, u32[]{:S(2)}, u32[]{:S(2)}) collective-permute-start(f32[32,256]{1,0:T(8,128)S(1)} %get-tuple-element.101), channel_id=1, source_target_pairs={{0,2},{1,3},{2,0},{3,1},{4,6},{5,7},{6,4},{7,5},{8,10},{9,11},{10,... | collective-permute-start | bytes 98312 | tf_op jit(solution)/shard_map/ppermute | solution.py:45
  (10 other events, 31.0 us)

commit v3 on v0

v3 whole, which is shorter than its diff:
```python
import functools
import math

import jax
import jax.numpy as jnp
from jax import lax
from jax.experimental import pallas as pl
from jax.experimental.pallas import tpu as pltpu
from jax.sharding import PartitionSpec as P

DH = 128
SLAB = 4
EPSILON = 1e-05
BF16 = jnp.bfloat16
F32 = jnp.float32


def dot(left, right, left_dim, right_dim):
    return lax.dot_general(
        left, right, (((left_dim,), (right_dim,)), ((), ())), preferred_element_type=F32
    )


def call(body, outs, *args, flops=10**8, scratch=(), far=(), vmem=32):
    nbytes = sum(a.size * a.dtype.itemsize for a in args)
    nbytes += sum(math.prod(s) * jnp.dtype(d).itemsize for s, d in outs)
    return pl.pallas_call(
        body,
        out_shape=[jax.ShapeDtypeStruct(s, d) for s, d in outs],
        in_specs=[
            pl.BlockSpec(memory_space=pltpu.HBM) if i in far else pl.BlockSpec()
            for i in range(len(args))
        ],
        scratch_shapes=list(scratch),
        cost_estimate=pl.CostEstimate(flops=flops, bytes_accessed=nbytes, transcendentals=0),
        compiler_params=pltpu.CompilerParams(vmem_limit_bytes=vmem * 2**20),
    )(*args)


def after(x, *others):
    return lax.optimization_barrier((x, *others))[0]


def flip(x, axis, count, bits):
    return lax.ppermute(x, axis, [(i, i ^ bits) for i in range(count)])


def head(h):
    return slice(h * DH, (h + 1) * DH)


def cut(start, size):
    return pl.ds(pl.multiple_of(start * size, size), size)


def member(r):
    return jnp.bitwise_xor(lax.rem(lax.axis_index("seq"), SLAB), r)


def causal(block):
    rows = lax.broadcasted_iota(jnp.int32, (block, block), 0)
    return lax.broadcasted_iota(jnp.int32, (block, block), 1) <= rows


def fetch(pairs, sems):
    copies = [pltpu.make_async_copy(a, b, sems.at[i]) for i, (a, b) in enumerate(pairs)]
    for copy in copies:
        copy.start()
    for copy in copies:
        copy.wait()


def start_kernel(k_hbm, v_hbm, states_ref, k_ref, v_ref, sems):
    fetch([(k_hbm, k_ref), (v_hbm, v_ref)], sems)
    for h in range(k_ref.shape[1] // DH):
        states_ref[head(h), :] = dot(k_ref[:, head(h)], v_ref[:, head(h)], 0, 0).astype(BF16)


def pack_kernel(q_hbm, k_hbm, v_hbm, w_hbm, tokens_ref, columns_ref, q_ref, k_ref, v_ref, w_ref, sems):
    fetch([(q_hbm, q_ref), (k_hbm, k_ref), (v_hbm, v_ref), (w_hbm, w_ref)], sems)
    block, width = q_ref.shape[0], q_ref.shape[1] // SLAB
    for i, ref in enumerate((q_ref, k_ref, v_ref)):
        for p in range(SLAB):
            tokens_ref[p, i * block : (i + 1) * block, :] = ref[:, p * width : (p + 1) * width]
    for i in range(2):
        columns_ref[i] = w_ref[:, cut(member(2 * i), width)]


def slab_sum_kernel(backward, parts_ref, out_ref):
    total = parts_ref[0].astype(F32)
    for p in range(1, SLAB):
        total = total + parts_ref[p].astype(F32)
    scatter_slab(backward, total, out_ref)


def scatter_slab(backward, total, out_ref):
    slab = lax.div(lax.axis_index("seq"), SLAB)
    for d in range(out_ref.shape[0]):
        wanted = d < slab if backward else d > slab
        out_ref[d] = jnp.where(wanted, total, 0.0).astype(BF16)


def gather_slab(ref):
    total = ref[0].astype(F32)
    for d in range(1, ref.shape[0]):
        total = total + ref[d].astype(F32)
    return total


def early_kernel(groups, tokens_ref, *refs):
    cots, weights = refs[:SLAB], refs[SLAB : SLAB + groups]
    attend_ref, within_ref, dnormed_ref = refs[SLAB + groups :]
    block = cots[0].shape[0]
    width = within_ref.shape[2]
    heads = width // DH
    mask = causal(block)
    rows = weights[0].shape[1]
    me = lax.axis_index("dp")
    for r in range(SLAB):
        total = dot(cots[r][:, cut(me, rows)], weights[0][0], 1, 0)
        for j in range(1, groups):
            total = total + dot(cots[r][:, cut(jnp.bitwise_xor(me, j), rows)], weights[j][0], 1, 0)
        dnormed_ref[member(r)] = total
    for p in range(SLAB):
        for h in range(heads):
            q, k, v = (tokens_ref[p, i * block : (i + 1) * block, head(h)] for i in range(3))
            attend = jnp.where(mask, dot(q, k, 1, 1), 0.0).astype(BF16)
            attend_ref[p * heads + h] = attend
            within_ref[p, :, head(h)] = dot(attend, v, 1, 0)


def middle_kernel(
    tokens_ref, states_ref, before_ref, within_ref, dnormed_ref,
    normed_ref, dmixed_ref, prior_ref, u_ref, slab_ref,
):
    block = within_ref.shape[1]
    heads = within_ref.shape[2] // DH
    running = gather_slab(before_ref)
    slab_u = jnp.zeros(running.shape, F32)
    for p in range(SLAB):
        prior = running.astype(BF16)
        prior_ref[p] = prior
        running = running + states_ref[p].astype(F32)
        us = []
        for h in range(heads):
            q = tokens_ref[p, :block, head(h)]
            mixed = within_ref[p, :, head(h)] + dot(q, prior[head(h), :], 1, 0)
            scale = lax.rsqrt(jnp.mean(mixed * mixed, axis=-1, keepdims=True) + EPSILON)
            normed = mixed * scale
            normed_ref[p, :, head(h)] = normed.astype(BF16)
            dnormed = dnormed_ref[p, :, head(h)]
            along = jnp.mean(dnormed * normed, axis=-1, keepdims=True)
            dmixed = ((dnormed - normed * along) * scale).astype(BF16)
            dmixed_ref[p, :, head(h)] = dmixed
            us.append(dot(q, dmixed, 0, 0))
        u = jnp.concatenate(us, axis=0)
        u_ref[p] = u
        slab_u = slab_u + u
    scatter_slab(True, slab_u, slab_ref)


def late_kernel(
    tokens_ref, attend_ref, dmixed_ref, prior_ref, normed_ref, back_ref, part_ref
):
    block = dmixed_ref.shape[1]
    heads = dmixed_ref.shape[2] // DH
    mask = causal(block)
    for p in range(SLAB):
        back_ref[p, :block, :] = normed_ref[p]
        for h in range(heads):
            q, k, v = (tokens_ref[p, i * block : (i + 1) * block, head(h)] for i in range(3))
            dmixed = dmixed_ref[p, :, head(h)]
            back = jnp.where(mask, dot(dmixed, v, 1, 1), 0.0).astype(BF16)
            gq = dot(back, k, 1, 0) + dot(dmixed, prior_ref[p, head(h), :], 1, 1)
            back_ref[p, block:, head(h)] = gq.astype(BF16)
            part_ref[p, :block, head(h)] = dot(back, q, 0, 0)
            part_ref[p, block:, head(h)] = dot(attend_ref[p * heads + h], dmixed, 0, 0)


def last_kernel(tokens_ref, behind_ref, u_ref, part_ref, out_ref):
    block = part_ref.shape[1] // 2
    heads = part_ref.shape[2] // DH
    running = gather_slab(behind_ref)
    for p in reversed(range(SLAB)):
        later = running.astype(BF16)
        running = running + u_ref[p]
        for h in range(heads):
            k, v = (tokens_ref[p, i * block : (i + 1) * block, head(h)] for i in (1, 2))
            gk = part_ref[p, :block, head(h)] + dot(v, later[head(h), :], 1, 1)
            gv = part_ref[p, block:, head(h)] + dot(k, later[head(h), :], 1, 0)
            out_ref[p, :block, head(h)] = gk.astype(BF16)
            out_ref[p, block:, head(h)] = gv.astype(BF16)


def output_kernel(groups, got_ref, own_ref, *refs):
    far, (out_ref, gq_ref, normed_ref) = refs[: 2 * (groups - 1)], refs[2 * (groups - 1) :]
    block, width = got_ref.shape[1] // 2, got_ref.shape[2]
    rows = own_ref.shape[0]
    me = lax.axis_index("dp")
    for p in range(SLAB):
        normed_ref[:, p * width : (p + 1) * width] = got_ref[p, :block, :]
        gq_ref[:, p * width : (p + 1) * width] = got_ref[p, block:, :]
    out_ref[:, cut(me, rows)] = dot(normed_ref[...], own_ref[...], 1, 1).astype(BF16)
    for j in range(1, groups):
        total = jnp.zeros((block, rows), F32)
        for r in range(SLAB):
            weight = far[2 * (j - 1) + r % 2][r // 2]
            total = total + dot(got_ref[member(r), :block, :], weight, 1, 1)
        out_ref[:, cut(jnp.bitwise_xor(me, j), rows)] = total.astype(BF16)


def join_kernel(got_ref, gk_ref, gv_ref):
    block, width = gk_ref.shape[0], got_ref.shape[2]
    for p in range(SLAB):
        gk_ref[:, p * width : (p + 1) * width] = got_ref[p, :block, :]
        gv_ref[:, p * width : (p + 1) * width] = got_ref[p, block:, :]


def product_kernel(normed_ref, *refs):
    cots, (keep_ref, send_ref) = refs[:SLAB], refs[SLAB:]
    me = lax.axis_index("dp")
    rows = keep_ref.shape[0]
    for j, out in enumerate((keep_ref, send_ref)):
        total = jnp.zeros(out.shape, F32)
        for r in range(SLAB):
            cot = cots[r][:, cut(jnp.bitwise_xor(me, j), rows)]
            total = total + dot(cot, normed_ref[member(r)], 0, 0)
        out[...] = total.astype(out.dtype)


def spread_kernel(own_ref, got_ref, out_ref):
    out_ref[...] = (own_ref[...] + got_ref[...].astype(F32)).astype(BF16)


def share_kernel(got_ref, out_ref):
    out_ref[...] = gather_slab(got_ref)


def finish_kernel(factor, got_ref, out_ref):
    width = got_ref.shape[2]
    for p in range(SLAB):
        out_ref[:, p * width : (p + 1) * width] = got_ref[p] * factor


def local(queries, keys, values, cotangent, out_weight, *, dp, seq):
    local_seqs, block, features = queries.shape
    outputs = cotangent.shape[2]
    rows = local_seqs * block
    slabs = seq // SLAB
    width = features // SLAB
    heads = width // DH
    q, k, v = (x.reshape(rows, features) for x in (queries, keys, values))
    cot = cotangent.reshape(rows, outputs)
    factor = 1.0 / math.sqrt(rows * dp * seq)
    near = [[s * SLAB + p for p in range(SLAB)] for s in range(slabs)]
    across = [[s * SLAB + p for s in range(slabs)] for p in range(SLAB)]

    def trade(x, groups):
        return lax.all_to_all(x, "seq", 0, 0, axis_index_groups=groups, tiled=True)

    (states,) = call(
        start_kernel, [((features, DH), BF16)], k, v, far=(0, 1), vmem=60,
        scratch=[pltpu.VMEM(k.shape, BF16), pltpu.VMEM(v.shape, BF16), pltpu.SemaphoreType.DMA((2,))],
    )
    got_states = trade(states.reshape(SLAB, width, DH), near)
    q2, k2, v2, w2, cot2 = lax.optimization_barrier((q, k, v, out_weight, cot, states))[:5]
    tokens, columns = call(
        pack_kernel,
        [((SLAB, 3 * rows, width), BF16), ((2, out_weight.shape[0], width), BF16)],
        q2, k2, v2, w2, far=(0, 1, 2, 3), vmem=60,
        scratch=[pltpu.VMEM(x.shape, BF16) for x in (q, k, v, out_weight)]
        + [pltpu.SemaphoreType.DMA((4,))],
    )
    w_far = []
    for j in range(1, dp):
        found = flip(columns, "dp", dp, j)
        w_far.append((found, flip(found, "seq", seq, 1)))
    cot_y = flip(cot2, "seq", seq, 2)
    cots = [cot, flip(cot2, "seq", seq, 1), cot_y, flip(cot_y, "seq", seq, 1)]
    (slab_kv,) = call(
        functools.partial(slab_sum_kernel, False), [((slabs, width, DH), BF16)], got_states
    )
    before = trade(slab_kv, across)
    tokens = trade(after(tokens, slab_kv), near)
    attend, within, dnormed = call(
        functools.partial(early_kernel, dp),
        [((SLAB * heads, rows, rows), BF16), ((SLAB, rows, width), F32), ((SLAB, rows, width), F32)],
        tokens, *cots, columns, *(w[0] for w in w_far),
    )
    normed, dmixed, prior, u, slab_u = call(
        middle_kernel,
        [((SLAB, rows, width), BF16), ((SLAB, rows, width), BF16), ((SLAB, width, DH), BF16),
         ((SLAB, width, DH), F32), ((slabs, width, DH), BF16)],
        tokens, got_states, before, within, dnormed,
    )
    behind = trade(slab_u, across)
    tuned = dp == 2 and outputs // (dp * seq) % 8 == 0
    if tuned:
        keep, send = call(
            product_kernel, [((outputs // dp, width), F32), ((outputs // dp, width), BF16)],
            normed, *cots,
        )
        got = flip(send, "dp", dp, 1)
    back, parts = call(
        late_kernel,
        [((SLAB, 2 * rows, width), BF16), ((SLAB, 2 * rows, width), F32)],
        tokens, attend, dmixed, prior, normed,
    )
    got_back = trade(back, near)
    (grads,) = call(last_kernel, [((SLAB, 2 * rows, width), BF16)], tokens, behind, u, parts)
    got_grads = trade(grads, near)
    output, gq, own_normed = call(
        functools.partial(output_kernel, dp),
        [((rows, outputs), BF16), ((rows, features), BF16), ((rows, features), BF16)],
        got_back, out_weight, *(x for w in w_far for x in w),
    )
    if tuned:
        piece = outputs // (dp * slabs)
        (total,) = call(spread_kernel, [((outputs // dp, width), BF16)], keep, got)
        got = trade(total.reshape(slabs, piece, width), across)
        (share,) = call(share_kernel, [((piece, width), F32)], got)
        got = trade(share.reshape(SLAB, piece // SLAB, width), near)
        (grad_weight,) = call(
            functools.partial(finish_kernel, factor), [((piece // SLAB, features), F32)], got
        )
    else:
        partial = dot(cot, own_normed, 0, 0) * factor
        grad_weight = lax.psum_scatter(partial, ("dp", "seq"), scatter_dimension=0, tiled=True)
    gk, gv = call(join_kernel, [((rows, features), BF16)] * 2, got_grads)
    shape = queries.shape
    return (
        output.reshape(cotangent.shape), gq.reshape(shape), gk.reshape(shape), gv.reshape(shape),
        grad_weight,
    )


def solution(mesh):
    dp, seq = mesh.shape["dp"], mesh.shape["seq"]
    return jax.shard_map(
        functools.partial(local, dp=dp, seq=seq),
        mesh=mesh,
        in_specs=(P("dp", "seq", None),) * 4 + (P("dp", None),),
        out_specs=(P("dp", "seq", None),) * 4 + (P(("dp", "seq"), None),),
        check_vma=False,
    )
```

time: 319 us -> 109 us (0.34)
  waiting for transfers between devices: 254 us -> 40.1 us
  starting transfers between devices: 0.16 us -> 38.8 us
  Pallas kernels: 0 us -> 18.4 us
  matrix products: 17.8 us -> 0 us
  other arithmetic: 16.2 us -> 0 us
  between operations: 14 us -> 0.76 us
  local copies, waits for them, and re-layouts: 15.7 us -> 10.3 us
    all_gather x3 -> x0, waiting for transfers between devices: 130 us -> none  [the longest x2 98.1 us: entering(): gathered = lax.all_gather(x.astype(jnp.bfloat16), axis)]
    unnamed x5 -> x0, waiting for transfers between devices: 124 us -> none
    all_to_all x0 -> x8, starting transfers between devices: none -> 32.2 us  [trade(): return lax.all_to_all(x, 'seq', 0, 0, axis_index_groups=groups, tiled=True)]
    all_to_all x0 -> x8, waiting for transfers between devices: none -> 32.1 us  [trade(): return lax.all_to_all(x, 'seq', 0, 0, axis_index_groups=groups, tiled=True)]
    pallas_call x0 -> x13, Pallas kernels: none -> 18.4 us  [call(): pl.pallas_call(body, out_shape=[jax.ShapeDtypeStruct(s, d) for s, d in ou...]
    dot_general x19 -> x0, matrix products: 17.8 us -> none  [the longest x1 2.66 us: contract_rows(): lax.dot_general(left, right, (((0,), (0,)), ((), ())), preferred_element_...]
    add x15 -> x0, other arithmetic: 16.1 us -> none  [adding(): return earlier + latter]
    ppermute x0 -> x6, waiting for transfers between devices: none -> 7.97 us  [flip(): return lax.ppermute(x, axis, [(i, i ^ bits) for i in range(count)])]
  transfers between devices with their start and end apart: 4 -> 14, of which waited for: 4 -> 10; matrix products, arithmetic and copies ran while one was open for 14% -> 0% of each run, Pallas kernels for 0% -> 12%
where the time goes in v3:
time: 109 us; the launch traced here: 108 us
  waiting for transfers between devices  40.1 us (37%)
  starting transfers between devices  38.8 us (36%)
  Pallas kernels  18.4 us (17%)
  local copies, waits for them, and re-layouts  10.3 us (9%)
    all_to_all x8, starting transfers between devices, trade(): return lax.all_to_all(x, 'seq', 0, 0, axis_index_groups=groups, tiled=True)  32.2 us
    all_to_all x8, waiting for transfers between devices, trade(): return lax.all_to_all(x, 'seq', 0, 0, axis_index_groups=groups, tiled=True)  32.1 us
    pallas_call x13, Pallas kernels, call(): pl.pallas_call(body, out_shape=[jax.ShapeDtypeStruct(s, d) for s, d in ou...  18.4 us
    unnamed x30, local copies, waits for them, and re-layouts  10.3 us
    ppermute x6, waiting for transfers between devices, flip(): return lax.ppermute(x, axis, [(i, i ^ bits) for i in range(count)])  7.97 us
    ppermute x6, starting transfers between devices, flip(): return lax.ppermute(x, axis, [(i, i ^ bits) for i in range(count)])  6.6 us
  transfers between devices with their start and end apart: 14, of which 10 were waited for; matrix products, arithmetic and copies ran while one was open for 0% of the time, Pallas kernels for 12%

profile of v3, /device:TPU:0, one launch (start us, length us, event | category | flops | bytes accessed | tf_op | source)
XLA Modules:
  0.0 108.4 jit_solution(16189946114734921239)
XLA Ops:
  0.6 2.0 %shard_map.92 = bf16[1024,128]{1,0:T(8,128)(2,1)} custom-call(bf16[128,1024]{1,0:T(8,128)(2,1)} %bitcast.15, bf16[128,1024]{1,0:T(8,128)(2,1)} %bitcast.17), custom_call_target="tpu_custom_call" | custom-call | flops 100000000 | bytes 786432 | tf_op jit(solution)/shard_map/pallas_call | solution.py:27
  2.7 4.2 %all-to-all-start = ((bf16[4,256,128]{2,1,0:T(8,128)(2,1)}), bf16[4,256,128]{2,1,0:T(8,128)(2,1)S(1)}, u32[]{:S(2)}, u32[]{:S(2)}) async-start(bf16[4,256,128]{2,1,0:T(8,128)(2,1)} %bitcast.19), calls=%async_computation | async-start | bytes 524288 | tf_op jit(solution)/shard_map/all_to_all | solution.py:259
  6.9 2.7 %shard_map.93 = (bf16[4,384,256]{2,1,0:T(8,128)(2,1)}, bf16[2,512,256]{2,1,0:T(8,128)(2,1)}) custom-call(bf16[128,1024]{1,0:T(8,128)(2,1)} %bitcast.20, bf16[128,1024]{1,0:T(8,128)(2,1)} %bitcast.16, bf16[128,1024]{1,0:T(8,128)(2,1)} %bitcast.18, bf16[512,1024]{1,0:T(8,128)(2,1)} %own_ref.1), custom_call_target="tpu_custom_call" | custom-call | flops 100000000 | bytes 3145728 | tf_op jit(solution)/shard_map/pallas_call | solution.py:27
  9.6 3.3 %all-to-all-done.parts_ref.states_ref = bf16[4,256,128]{2,1,0:T(8,128)(2,1)S(1)} async-done(((bf16[4,256,128]{2,1,0:T(8,128)(2,1)}), bf16[4,256,128]{2,1,0:T(8,128)(2,1)S(1)}, u32[]{:S(2)}, u32[]{:S(2)}) %all-to-all-start) | async-done | bytes 262176 | tf_op jit(solution)/shard_map/all_to_all | solution.py:259
  13.7 3.6 %all-to-all-start.1 = ((bf16[4,384,256]{2,1,0:T(8,128)(2,1)}), bf16[4,384,256]{2,1,0:T(8,128)(2,1)S(1)}, u32[]{:S(2)}, u32[]{:S(2)}) async-start(bf16[4,384,256]{2,1,0:T(8,128)(2,1)} %get-tuple-element.34), calls=%async_computation.1 | async-start | bytes 1572864 | tf_op jit(solution)/shard_map/all_to_all | solution.py:259
  17.3 2.1 %collective-permute-start.3 = (bf16[2,512,256]{2,1,0:T(8,128)(2,1)}, bf16[2,512,256]{2,1,0:T(8,128)(2,1)S(1)}, u32[]{:S(2)}, u32[]{:S(2)}) collective-permute-start(bf16[2,512,256]{2,1,0:T(8,128)(2,1)} %get-tuple-element.36.refs_4_), channel_id=1, source_target_pairs={{0,16},{16,0},{1,17},{17,1},{2,18},{18,2},{3,19},{19,3},{4,20},{20... | collective-permute-start | bytes 1572872 | tf_op jit(solution)/shard_map/ppermute | solution.py:45
  19.5 1.9 %collective-permute-start.1 = (bf16[128,1024]{1,0:T(8,128)(2,1)S(1)}, bf16[128,1024]{1,0:T(8,128)(2,1)S(1)}, u32[]{:S(2)}, u32[]{:S(2)}) collective-permute-start(bf16[128,1024]{1,0:T(8,128)(2,1)S(1)} %bitcast.11), channel_id=1, source_target_pairs={{0,2},{1,3},{2,0},{3,1},{4,6},{5,7},{6,4},{7,5},{8,10},{9,11},{10,... | collective-permute-start | bytes 786440 | tf_op jit(solution)/shard_map/ppermute | solution.py:45
  21.4 8.0 %all-to-all-done.1.tokens_ref = bf16[4,384,256]{2,1,0:T(8,128)(2,1)S(1)} async-done(((bf16[4,384,256]{2,1,0:T(8,128)(2,1)}), bf16[4,384,256]{2,1,0:T(8,128)(2,1)S(1)}, u32[]{:S(2)}, u32[]{:S(2)}) %all-to-all-start.1) | async-done | bytes 786464 | tf_op jit(solution)/shard_map/all_to_all | solution.py:259
  29.4 5.5 %all-to-all-start.2 = ((bf16[4,256,128]{2,1,0:T(8,128)(2,1)}), bf16[4,256,128]{2,1,0:T(8,128)(2,1)S(1)}, u32[]{:S(2)}, u32[]{:S(2)}) async-start(bf16[4,256,128]{2,1,0:T(8,128)(2,1)} %shard_map.94), calls=%async_computation.2 | async-start | bytes 524288 | tf_op jit(solution)/shard_map/all_to_all | solution.py:259
  35.4 1.0 collective-permute-done.refs_1_
  36.8 2.6 %shard_map.95 = (bf16[8,128,128]{2,1,0:T(8,128)(2,1)S(1)}, f32[4,128,256]{2,1,0:T(8,128)S(1)}, f32[4,128,256]{2,1,0:T(8,128)S(1)}) custom-call(bf16[4,384,256]{2,1,0:T(8,128)(2,1)S(1)} %all-to-all-done.1.tokens_ref, bf16[128,1024]{1,0:T(8,128)(2,1)S(1)} %bitcast.13, bf16[128,1024]{1,0:T(8,128)(2,1)S(1)} %collective-permute-done.refs_1_, ...), custom_call_target="tpu_custom_call" | custom-call | flops 100000000 | bytes 4194304 | tf_op jit(solution)/shard_map/pallas_call | solution.py:27
  41.7 1.4 %all-to-all-done.2.before_ref = bf16[4,256,128]{2,1,0:T(8,128)(2,1)S(1)} async-done(((bf16[4,256,128]{2,1,0:T(8,128)(2,1)}), bf16[4,256,128]{2,1,0:T(8,128)(2,1)S(1)}, u32[]{:S(2)}, u32[]{:S(2)}) %all-to-all-start.2) | async-done | bytes 262176 | tf_op jit(solution)/shard_map/all_to_all | solution.py:259
  43.1 1.0 copy-done.6
  44.1 1.0 copy-done.8
  45.2 1.5 %shard_map.96 = (bf16[4,128,256]{2,1,0:T(8,128)(2,1)S(1)}, bf16[4,128,256]{2,1,0:T(8,128)(2,1)S(1)}, bf16[4,256,128]{2,1,0:T(8,128)(2,1)S(1)}, f32[4,256,128]{2,1,0:T(8,128)S(1)}, bf16[4,256,128]{2,1,0:T(8,128)(2,1)}) custom-call(bf16[4,384,256]{2,1,0:T(8,128)(2,1)S(1)} %all-to-all-done.1.tokens_ref, ...), custom_call_target="tpu_custom_call" | custom-call | flops 100000000 | bytes 3932160 | tf_op jit(solution)/shard_map/pallas_call | solution.py:27
  48.8 3.7 %all-to-all-start.4 = ((bf16[4,256,128]{2,1,0:T(8,128)(2,1)}), bf16[4,256,128]{2,1,0:T(8,128)(2,1)S(1)}, u32[]{:S(2)}, u32[]{:S(2)}) async-start(bf16[4,256,128]{2,1,0:T(8,128)(2,1)} %get-tuple-element.46), calls=%async_computation.4 | async-start | bytes 524288 | tf_op jit(solution)/shard_map/all_to_all | solution.py:259
  53.3 1.6 %collective-permute-start.5 = (bf16[512,256]{1,0:T(8,128)(2,1)S(1)}, bf16[512,256]{1,0:T(8,128)(2,1)S(1)}, u32[]{:S(2)}, u32[]{:S(2)}) collective-permute-start(bf16[512,256]{1,0:T(8,128)(2,1)S(1)} %get-tuple-element.52), channel_id=1, source_target_pairs={{0,16},{16,0},{1,17},{17,1},{2,18},{18,2},{3,19},{19,3},{4,20},{20... | collective-permute-start | bytes 786440 | tf_op jit(solution)/shard_map/ppermute | solution.py:45
  54.8 6.6 %collective-permute-done.5.got_ref = bf16[512,256]{1,0:T(8,128)(2,1)S(1)} collective-permute-done((bf16[512,256]{1,0:T(8,128)(2,1)S(1)}, bf16[512,256]{1,0:T(8,128)(2,1)S(1)}, u32[]{:S(2)}, u32[]{:S(2)}) %collective-permute-start.5) | collective-permute-done | bytes 262176 | tf_op jit(solution)/shard_map/ppermute | solution.py:45
  62.1 5.0 %all-to-all-start.6 = ((bf16[4,128,256]{2,1,0:T(8,128)(2,1)}), bf16[4,128,256]{2,1,0:T(8,128)(2,1)S(1)}, u32[]{:S(2)}, u32[]{:S(2)}) async-start(bf16[4,128,256]{2,1,0:T(8,128)(2,1)} %bitcast.9), calls=%async_computation.6 | async-start | bytes 524288 | tf_op jit(solution)/shard_map/all_to_all | solution.py:259
  67.1 0.9 copy-done.12
  68.0 0.9 copy-done.14
  69.0 1.4 %shard_map.97 = (bf16[4,256,256]{2,1,0:T(8,128)(2,1)S(1)}, f32[4,256,256]{2,1,0:T(8,128)S(1)}) custom-call(bf16[4,384,256]{2,1,0:T(8,128)(2,1)S(1)} %all-to-all-done.1.tokens_ref, bf16[8,128,128]{2,1,0:T(8,128)(2,1)S(1)} %copy-done.10, bf16[4,128,256]{2,1,0:T(8,128)(2,1)S(1)} %copy-done.12, bf16[4,256,128]{2,1,0:T(8,128)(2,1)S(1)} %copy-done.14, ...), custom_call_target="tpu_custom_call" | custom-call | flops 100000000 | bytes 3407872 | tf_op jit(solution)/shard_map/pallas_call | solution.py:27
  71.2 3.8 %all-to-all-done.6.got_ref = bf16[4,128,256]{2,1,0:T(8,128)(2,1)S(1)} async-done(((bf16[4,128,256]{2,1,0:T(8,128)(2,1)}), bf16[4,128,256]{2,1,0:T(8,128)(2,1)S(1)}, u32[]{:S(2)}, u32[]{:S(2)}) %all-to-all-start.6) | async-done | bytes 262176 | tf_op jit(solution)/shard_map/all_to_all | solution.py:259
  75.0 3.5 %all-to-all-start.3 = ((bf16[4,256,256]{2,1,0:T(8,128)(2,1)}), bf16[4,256,256]{2,1,0:T(8,128)(2,1)S(1)}, u32[]{:S(2)}, u32[]{:S(2)}) async-start(bf16[4,256,256]{2,1,0:T(8,128)(2,1)} %copy-done.2), calls=%async_computation.3 | async-start | bytes 1048576 | tf_op jit(solution)/shard_map/all_to_all | solution.py:259
  79.6 7.7 %all-to-all-done.3.got_ref = bf16[4,256,256]{2,1,0:T(8,128)(2,1)S(1)} async-done(((bf16[4,256,256]{2,1,0:T(8,128)(2,1)}), bf16[4,256,256]{2,1,0:T(8,128)(2,1)S(1)}, u32[]{:S(2)}, u32[]{:S(2)}) %all-to-all-start.3) | async-done | bytes 524320 | tf_op jit(solution)/shard_map/all_to_all | solution.py:259
  87.3 3.3 %all-to-all-start.7 = ((f32[4,32,256]{2,1,0:T(8,128)}), f32[4,32,256]{2,1,0:T(8,128)S(1)}, u32[]{:S(2)}, u32[]{:S(2)}) async-start(f32[4,32,256]{2,1,0:T(8,128)} %bitcast.10), calls=%async_computation.7 | async-start | bytes 262144 | tf_op jit(solution)/shard_map/all_to_all | solution.py:259
  90.6 1.0 copy-done.4
  91.7 1.1 %shard_map.99 = bf16[4,256,256]{2,1,0:T(8,128)(2,1)} custom-call(bf16[4,384,256]{2,1,0:T(8,128)(2,1)S(1)} %all-to-all-done.1.tokens_ref, bf16[4,256,128]{2,1,0:T(8,128)(2,1)S(1)} %all-to-all-done.4.behind_ref, f32[4,256,128]{2,1,0:T(8,128)S(1)} %copy-done.4, f32[4,256,256]{2,1,0:T(8,128)S(1)} %get-tuple-element.48.part_ref), custom_call_target="tpu_custom_call" | custom-call | flops 100000000 | bytes 3145728 | tf_op jit(solution)/shard_map/pallas_call | solution.py:27
  92.8 2.4 %all-to-all-done.7.got_ref = f32[4,32,256]{2,1,0:T(8,128)S(1)} async-done(((f32[4,32,256]{2,1,0:T(8,128)}), f32[4,32,256]{2,1,0:T(8,128)S(1)}, u32[]{:S(2)}, u32[]{:S(2)}) %all-to-all-start.7) | async-done | bytes 131104 | tf_op jit(solution)/shard_map/all_to_all | solution.py:259
  95.2 3.5 %all-to-all-start.5 = ((bf16[4,256,256]{2,1,0:T(8,128)(2,1)}), bf16[4,256,256]{2,1,0:T(8,128)(2,1)S(1)}, u32[]{:S(2)}, u32[]{:S(2)}) async-start(bf16[4,256,256]{2,1,0:T(8,128)(2,1)} %shard_map.99), calls=%async_computation.5 | async-start | bytes 1048576 | tf_op jit(solution)/shard_map/all_to_all | solution.py:259
  98.7 2.6 %shard_map.98 = (bf16[128,1024]{1,0:T(8,128)(2,1)}, bf16[128,1024]{1,0:T(8,128)(2,1)}, bf16[128,1024]{1,0:T(8,128)(2,1)}) custom-call(bf16[4,256,256]{2,1,0:T(8,128)(2,1)S(1)} %all-to-all-done.3.got_ref, bf16[512,1024]{1,0:T(8,128)(2,1)S(1)} %copy-done, bf16[2,512,256]{2,1,0:T(8,128)(2,1)S(1)} %collective-permute-done.3.refs_5_.refs_0_, ...), custom_call_target="tpu_custom_call" | custom-call | flops 100000000 | bytes 3407872 | tf_op jit(solution)/shard_map/pallas_call | solution.py:27
  102.0 5.5 %all-to-all-done.5.got_ref = bf16[4,256,256]{2,1,0:T(8,128)(2,1)S(1)} async-done(((bf16[4,256,256]{2,1,0:T(8,128)(2,1)}), bf16[4,256,256]{2,1,0:T(8,128)(2,1)S(1)}, u32[]{:S(2)}, u32[]{:S(2)}) %all-to-all-start.5) | async-done | bytes 524320 | tf_op jit(solution)/shard_map/all_to_all | solution.py:259
  (39 shorter events, 11.1 us)
Async XLA Ops:
  2.7 10.3 %all-to-all-start = ((bf16[4,256,128]{2,1,0:T(8,128)(2,1)}), bf16[4,256,128]{2,1,0:T(8,128)(2,1)S(1)}, u32[]{:S(2)}, u32[]{:S(2)}) async-start(bf16[4,256,128]{2,1,0:T(8,128)(2,1)} %bitcast.19), calls=%async_computation | async-start | bytes 524288 | tf_op jit(solution)/shard_map/all_to_all | solution.py:259
  13.7 5.8 %copy-start.1 = (bf16[1,128,1024]{2,1,0:T(8,128)(2,1)S(1)}, bf16[1,128,1024]{2,1,0:T(8,128)(2,1)}, u32[]{:S(2)}) copy-start(bf16[1,128,1024]{2,1,0:T(8,128)(2,1)} %param.8) | copy-start | bytes 786436
  13.7 15.7 %all-to-all-start.1 = ((bf16[4,384,256]{2,1,0:T(8,128)(2,1)}), bf16[4,384,256]{2,1,0:T(8,128)(2,1)S(1)}, u32[]{:S(2)}, u32[]{:S(2)}) async-start(bf16[4,384,256]{2,1,0:T(8,128)(2,1)} %get-tuple-element.34), calls=%async_computation.1 | async-start | bytes 1572864 | tf_op jit(solution)/shard_map/all_to_all | solution.py:259
  17.3 19.1 %collective-permute-start.3 = (bf16[2,512,256]{2,1,0:T(8,128)(2,1)}, bf16[2,512,256]{2,1,0:T(8,128)(2,1)S(1)}, u32[]{:S(2)}, u32[]{:S(2)}) collective-permute-start(bf16[2,512,256]{2,1,0:T(8,128)(2,1)} %get-tuple-element.36.refs_4_), channel_id=1, source_target_pairs={{0,16},{16,0},{1,17},{17,1},{2,18},{18,2},{3,19},{19,3},{4,20},{20... | collective-permute-start | bytes 1572872 | tf_op jit(solution)/shard_map/ppermute | solution.py:45
  19.5 15.4 %collective-permute-start.1 = (bf16[128,1024]{1,0:T(8,128)(2,1)S(1)}, bf16[128,1024]{1,0:T(8,128)(2,1)S(1)}, u32[]{:S(2)}, u32[]{:S(2)}) collective-permute-start(bf16[128,1024]{1,0:T(8,128)(2,1)S(1)} %bitcast.11), channel_id=1, source_target_pairs={{0,2},{1,3},{2,0},{3,1},{4,6},{5,7},{6,4},{7,5},{8,10},{9,11},{10,... | collective-permute-start | bytes 786440 | tf_op jit(solution)/shard_map/ppermute | solution.py:45
  29.4 13.7 %all-to-all-start.2 = ((bf16[4,256,128]{2,1,0:T(8,128)(2,1)}), bf16[4,256,128]{2,1,0:T(8,128)(2,1)S(1)}, u32[]{:S(2)}, u32[]{:S(2)}) async-start(bf16[4,256,128]{2,1,0:T(8,128)(2,1)} %shard_map.94), calls=%async_computation.2 | async-start | bytes 524288 | tf_op jit(solution)/shard_map/all_to_all | solution.py:259
  34.9 1.5 %collective-permute-start = (bf16[128,1024]{1,0:T(8,128)(2,1)S(1)}, bf16[128,1024]{1,0:T(8,128)(2,1)S(1)}, u32[]{:S(2)}, u32[]{:S(2)}) collective-permute-start(bf16[128,1024]{1,0:T(8,128)(2,1)S(1)} %bitcast.12), channel_id=1, source_target_pairs={{0,1},{1,0},{2,3},{3,2},{4,5},{5,4},{6,7},{7,6},{8,9},{9,8},{10,11... | collective-permute-start | bytes 786440 | tf_op jit(solution)/shard_map/ppermute | solution.py:45
  34.9 1.9 %collective-permute-start.2 = (bf16[128,1024]{1,0:T(8,128)(2,1)S(1)}, bf16[128,1024]{1,0:T(8,128)(2,1)S(1)}, u32[]{:S(2)}, u32[]{:S(2)}) collective-permute-start(bf16[128,1024]{1,0:T(8,128)(2,1)S(1)} %collective-permute-done.1.refs_2_), channel_id=1, source_target_pairs={{0,1},{1,0},{2,3},{3,2},{4,5},{5,4},{6,7},{7,6},{8,9},{9,8},{10,11... | collective-permute-start | bytes 786440 | tf_op jit(solution)/shard_map/ppermute | solution.py:45
  39.4 0.8 copy-start.5
  40.2 0.8 copy-start.7
  41.0 0.7 copy-start.9
  43.1 1.0 copy-start.6
  44.1 1.0 copy-start.8
  46.6 0.8 copy-start.3
  47.4 0.7 copy-start.11
  48.1 0.7 copy-start.13
  48.8 13.3 %all-to-all-start.4 = ((bf16[4,256,128]{2,1,0:T(8,128)(2,1)}), bf16[4,256,128]{2,1,0:T(8,128)(2,1)S(1)}, u32[]{:S(2)}, u32[]{:S(2)}) async-start(bf16[4,256,128]{2,1,0:T(8,128)(2,1)} %get-tuple-element.46), calls=%async_computation.4 | async-start | bytes 524288 | tf_op jit(solution)/shard_map/all_to_all | solution.py:259
  53.3 8.1 %collective-permute-start.5 = (bf16[512,256]{1,0:T(8,128)(2,1)S(1)}, bf16[512,256]{1,0:T(8,128)(2,1)S(1)}, u32[]{:S(2)}, u32[]{:S(2)}) collective-permute-start(bf16[512,256]{1,0:T(8,128)(2,1)S(1)} %get-tuple-element.52), channel_id=1, source_target_pairs={{0,16},{16,0},{1,17},{17,1},{2,18},{18,2},{3,19},{19,3},{4,20},{20... | collective-permute-start | bytes 786440 | tf_op jit(solution)/shard_map/ppermute | solution.py:45
  62.1 5.0 %copy-start.10 = (bf16[8,128,128]{2,1,0:T(8,128)(2,1)S(1)}, bf16[8,128,128]{2,1,0:T(8,128)(2,1)}, u32[]{:S(2)}) copy-start(bf16[8,128,128]{2,1,0:T(8,128)(2,1)} %copy-done.9) | copy-start | bytes 786436
  62.1 12.9 %all-to-all-start.6 = ((bf16[4,128,256]{2,1,0:T(8,128)(2,1)}), bf16[4,128,256]{2,1,0:T(8,128)(2,1)S(1)}, u32[]{:S(2)}, u32[]{:S(2)}) async-start(bf16[4,128,256]{2,1,0:T(8,128)(2,1)} %bitcast.9), calls=%async_computation.6 | async-start | bytes 524288 | tf_op jit(solution)/shard_map/all_to_all | solution.py:259
  67.1 1.0 copy-start.12
  68.0 0.9 copy-start.14
  70.4 0.8 copy-start.2
  75.0 12.3 %all-to-all-start.3 = ((bf16[4,256,256]{2,1,0:T(8,128)(2,1)}), bf16[4,256,256]{2,1,0:T(8,128)(2,1)S(1)}, u32[]{:S(2)}, u32[]{:S(2)}) async-start(bf16[4,256,256]{2,1,0:T(8,128)(2,1)} %copy-done.2), calls=%async_computation.3 | async-start | bytes 1048576 | tf_op jit(solution)/shard_map/all_to_all | solution.py:259
  78.5 20.2 %collective-permute-start.4 = (bf16[2,512,256]{2,1,0:T(8,128)(2,1)S(1)}, bf16[2,512,256]{2,1,0:T(8,128)(2,1)}, u32[]{:S(2)}, u32[]{:S(2)}) collective-permute-start(bf16[2,512,256]{2,1,0:T(8,128)(2,1)S(1)} %collective-permute-done.3.refs_5_.refs_0_), channel_id=1, source_target_pairs={{0,1},{1,0},{2,3},{3,2},{4,5},{5,4},{6,7},{7,6},{8,9},{9,8},{10,11... | collective-permute-start | bytes 1572872 | tf_op jit(solution)/shard_map/ppermute | solution.py:45
  87.3 7.9 %all-to-all-start.7 = ((f32[4,32,256]{2,1,0:T(8,128)}), f32[4,32,256]{2,1,0:T(8,128)S(1)}, u32[]{:S(2)}, u32[]{:S(2)}) async-start(f32[4,32,256]{2,1,0:T(8,128)} %bitcast.10), calls=%async_computation.7 | async-start | bytes 262144 | tf_op jit(solution)/shard_map/all_to_all | solution.py:259
  90.6 1.0 copy-start.4
  92.8 5.9 %copy-start = (bf16[512,1024]{1,0:T(8,128)(2,1)S(1)}, bf16[512,1024]{1,0:T(8,128)(2,1)}, u32[]{:S(2)}) copy-start(bf16[512,1024]{1,0:T(8,128)(2,1)} %own_ref.1) | copy-start | bytes 3145732
  95.2 12.3 %all-to-all-start.5 = ((bf16[4,256,256]{2,1,0:T(8,128)(2,1)}), bf16[4,256,256]{2,1,0:T(8,128)(2,1)S(1)}, u32[]{:S(2)}, u32[]{:S(2)}) async-start(bf16[4,256,256]{2,1,0:T(8,128)(2,1)} %shard_map.99), calls=%async_computation.5 | async-start | bytes 1048576 | tf_op jit(solution)/shard_map/all_to_all | solution.py:259

commit v4 on v2

v4 whole, which is shorter than its diff:
```python
import functools
import math

import jax
import jax.numpy as jnp
from jax import lax
from jax.experimental import pallas as pl
from jax.experimental.pallas import tpu as pltpu
from jax.sharding import PartitionSpec as P

DH = 128
SLAB = 4
EPSILON = 1e-05
BF16 = jnp.bfloat16
F32 = jnp.float32


def dot(left, right, left_dim, right_dim):
    return lax.dot_general(
        left, right, (((left_dim,), (right_dim,)), ((), ())), preferred_element_type=F32
    )


class Chain:
    def __init__(self):
        self.last = None

    def __call__(self, body, outs, *args, scratch=()):
        count = len(args)
        specs = [pl.BlockSpec()] * count
        inner = body
        if self.last is not None:
            args = (*args, self.last)
            specs = [*specs, pl.BlockSpec(memory_space=pl.ANY)]

            def inner(*refs):
                body(*refs[:count], *refs[count + 1 :])

        found = pl.pallas_call(
            inner,
            out_shape=[jax.ShapeDtypeStruct(s, d) for s, d in outs],
            in_specs=specs,
            scratch_shapes=list(scratch),
            cost_estimate=pl.CostEstimate(flops=1, bytes_accessed=1, transcendentals=0),
            compiler_params=pltpu.CompilerParams(vmem_limit_bytes=32 * 2**20),
        )(*args)
        self.last = found[-1]
        return found


def after(x, *others):
    return lax.optimization_barrier((x, *others))[0]


def flip(x, axis, count, bits):
    return lax.ppermute(x, axis, [(i, i ^ bits) for i in range(count)])


def head(h):
    return slice(h * DH, (h + 1) * DH)


def part(i, size):
    return slice(i * size, (i + 1) * size)


def cut(start, size):
    return pl.ds(pl.multiple_of(start * size, size), size)


def member(r):
    return jnp.bitwise_xor(lax.rem(lax.axis_index("seq"), SLAB), r)


def causal(block):
    rows = lax.broadcasted_iota(jnp.int32, (block, block), 0)
    return lax.broadcasted_iota(jnp.int32, (block, block), 1) <= rows


def start_kernel(k_ref, v_ref, keep_ref, send_ref):
    width = k_ref.shape[1] // SLAB
    for r in range(SLAB):
        k = k_ref[:, cut(member(r), width)]
        v = v_ref[:, cut(member(r), width)]
        out = (keep_ref, send_ref)[r % 2]
        for h in range(width // DH):
            out[r // 2, head(h), :] = dot(k[:, head(h)], v[:, head(h)], 0, 0).astype(out.dtype)


def halve_kernel(keep_ref, got_ref, own_ref, send_ref):
    own_ref[...] = keep_ref[0] + got_ref[0].astype(F32)
    send_ref[...] = (keep_ref[1] + got_ref[1].astype(F32)).astype(BF16)


def add_kernel(own_ref, got_ref, out_ref):
    out_ref[...] = (own_ref[...].astype(F32) + got_ref[...].astype(F32)).astype(out_ref.dtype)


def columns_kernel(w_ref, out_ref):
    width = out_ref.shape[2]
    for i in range(2):
        out_ref[i] = w_ref[:, cut(member(2 * i), width)]


def pack_kernel(q_ref, k_ref, v_ref, c_ref, *outs):
    block = q_ref.shape[0]
    width = q_ref.shape[1] // SLAB
    for r, out in enumerate(outs):
        for i, ref in enumerate((q_ref, k_ref, v_ref)):
            out[part(i, block), :] = ref[:, cut(member(r), width)]
    for i in range(c_ref.shape[1] // width):
        outs[1][part(3 + i, block), :] = c_ref[:, part(i, width)]


def attend_kernel(*refs):
    tokens, (attend_ref, within_ref, states_ref) = refs[:-3], refs[-3:]
    _, block, width = within_ref.shape
    mask = causal(block)
    for r, ref in enumerate(tokens):
        for h in range(width // DH):
            q, k, v = (ref[part(i, block), head(h)] for i in range(3))
            attend = jnp.where(mask, dot(q, k, 1, 1), 0.0).astype(BF16)
            attend_ref[r, h] = attend
            within_ref[r, :, head(h)] = dot(attend, v, 1, 0)
            states_ref[r, head(h), :] = dot(k, v, 0, 0)


def dnormed_kernel(groups, token_ref, *refs):
    cots, weights = refs[: SLAB - 1], refs[SLAB - 1 : SLAB - 1 + groups]
    dnormed_ref, cot_ref = refs[SLAB - 1 + groups :]
    block, outputs = cots[0].shape
    width = dnormed_ref.shape[2]
    rows = weights[0].shape[1]
    me = lax.axis_index("dp")
    for i in range(outputs // width):
        cot_ref[1, :, part(i, width)] = token_ref[part(3 + i, block), :]
    for r, ref in zip((0, 2, 3), cots):
        cot_ref[r] = ref[...]
    for r in range(SLAB):
        total = dot(cot_ref[r, :, cut(me, rows)], weights[0][0], 1, 0)
        for j in range(1, groups):
            total = total + dot(cot_ref[r, :, cut(jnp.bitwise_xor(me, j), rows)], weights[j][0], 1, 0)
        dnormed_ref[r] = total


def from_slabs(backward, refs):
    slab = lax.div(lax.axis_index("seq"), SLAB)
    total = jnp.zeros(refs[0].shape, F32)
    for i, ref in enumerate(refs):
        bit = lax.rem(lax.div(slab, 1 << i), 2)
        total = total + jnp.where(bit == (0 if backward else 1), ref[...].astype(F32), 0.0)
    return total


def middle_kernel(*refs):
    tokens = refs[:SLAB]
    *before, within0, states0, within1, states1, dnormed_ref = refs[SLAB : -(SLAB + 5)]
    withins, states = (within0, within1), (states0, states1)
    normeds = refs[-(SLAB + 5) : -5]
    dmixed_ref, prior_ref, u_ref, slab_ref, running = refs[-5:]
    block, width = normeds[0].shape
    heads = width // DH
    for r in range(SLAB):
        running[member(r)] = states[r // 2][r % 2]
    total = from_slabs(False, before)
    for p in range(SLAB):
        total, running[p] = total + running[p], total
    sums = [jnp.zeros((DH, DH), F32)] * heads
    for r in range(SLAB):
        prior = running[member(r)].astype(BF16)
        prior_ref[r] = prior
        for h in range(heads):
            q = tokens[r][:block, head(h)]
            mixed = withins[r // 2][r % 2, :, head(h)] + dot(q, prior[head(h), :], 1, 0)
            scale = lax.rsqrt(jnp.mean(mixed * mixed, axis=-1, keepdims=True) + EPSILON)
            normed = mixed * scale
            normeds[r][:, head(h)] = normed.astype(BF16)
            dnormed = dnormed_ref[r, :, head(h)]
            along = jnp.mean(dnormed * normed, axis=-1, keepdims=True)
            dmixed = ((dnormed - normed * along) * scale).astype(BF16)
            dmixed_ref[part(r, block), head(h)] = dmixed
            u = dot(q, dmixed, 0, 0)
            u_ref[r, head(h), :] = u
            sums[h] = sums[h] + u
    for h in range(heads):
        slab_ref[head(h), :] = sums[h].astype(BF16)


def late_kernel(*refs):
    tokens, normeds = refs[:SLAB], refs[SLAB : 2 * SLAB]
    attends, dmixed_ref, prior_ref = refs[2 * SLAB : 2 * SLAB + 2], *refs[2 * SLAB + 2 : 2 * SLAB + 4]
    outs, part_ref = refs[2 * SLAB + 4 : -1], refs[-1]
    block, width = normeds[0].shape
    heads = width // DH
    mask = causal(block)
    for r in range(SLAB):
        outs[r][:block, :] = normeds[r][...]
        for h in range(heads):
            q, k, v = (tokens[r][part(i, block), head(h)] for i in range(3))
            dmixed = dmixed_ref[part(r, block), head(h)]
            back = jnp.where(mask, dot(dmixed, v, 1, 1), 0.0).astype(BF16)
            gq = dot(back, k, 1, 0) + dot(dmixed, prior_ref[r, head(h), :], 1, 1)
            outs[r][block:, head(h)] = gq.astype(BF16)
            part_ref[r, :block, head(h)] = dot(back, q, 0, 0)
            part_ref[r, block:, head(h)] = dot(attends[r // 2][r % 2, h], dmixed, 0, 0)


def last_kernel(*refs):
    tokens = refs[:SLAB]
    *behind, u_ref, part_ref = refs[SLAB : -(SLAB + 1)]
    outs, running = refs[-(SLAB + 1) : -1], refs[-1]
    block = tokens[0].shape[0] // 3
    heads = outs[0].shape[1] // DH
    for r in range(SLAB):
        running[member(r)] = u_ref[r]
    total = from_slabs(True, behind)
    for p in reversed(range(SLAB)):
        total, running[p] = total + running[p], total
    for r in range(SLAB):
        later = running[member(r)].astype(BF16)
        for h in range(heads):
            k, v = (tokens[r][part(i, block), head(h)] for i in (1, 2))
            gk = part_ref[r, :block, head(h)] + dot(v, later[head(h), :], 1, 1)
            gv = part_ref[r, block:, head(h)] + dot(k, later[head(h), :], 1, 0)
            outs[r][:block, head(h)] = gk.astype(BF16)
            outs[r][block:, head(h)] = gv.astype(BF16)


def output_kernel(groups, *refs):
    backs, own_ref = refs[:SLAB], refs[SLAB]
    far, (out_ref, gq_ref, normed_ref) = refs[SLAB + 1 : -3], refs[-3:]
    block, width = backs[0].shape[0] // 2, backs[0].shape[1]
    rows = own_ref.shape[0]
    me = lax.axis_index("dp")
    for r in range(SLAB):
        normed_ref[:, cut(member(r), width)] = backs[r][:block, :]
        gq_ref[:, cut(member(r), width)] = backs[r][block:, :]
    out_ref[:, cut(me, rows)] = dot(normed_ref[...], own_ref[...], 1, 1).astype(BF16)
    for j in range(1, groups):
        total = jnp.zeros((block, rows), F32)
        for r in range(SLAB):
            total = total + dot(backs[r][:block, :], far[2 * (j - 1) + r % 2][r // 2], 1, 1)
        out_ref[:, cut(jnp.bitwise_xor(me, j), rows)] = total.astype(BF16)


def join_kernel(*refs):
    parts, (gk_ref, gv_ref) = refs[:SLAB], refs[SLAB:]
    block = gk_ref.shape[0]
    width = parts[0].shape[1]
    for r in range(SLAB):
        gk_ref[:, cut(member(r), width)] = parts[r][:block, :]
        gv_ref[:, cut(member(r), width)] = parts[r][block:, :]


def product_kernel(slabs, cot_ref, *refs):
    normeds, (keep_ref, send_ref) = refs[:SLAB], refs[SLAB:]
    me = lax.axis_index("dp")
    slab = lax.div(lax.axis_index("seq"), SLAB)
    rows = keep_ref.shape[0] // slabs
    for j, out in enumerate((send_ref, keep_ref)):
        for d in range(slabs):
            at = jnp.bitwise_xor(me, 1 - j) * slabs + jnp.bitwise_xor(slab, d)
            total = dot(cot_ref[0, :, cut(at, rows)], normeds[0][...], 0, 0)
            for r in range(1, SLAB):
                total = total + dot(cot_ref[r, :, cut(at, rows)], normeds[r][...], 0, 0)
            out[part(d, rows), :] = total.astype(out.dtype)


def split_kernel(own_ref, got_ref, keep_ref, send_ref):
    rows = keep_ref.shape[0] // 2
    for i in range(4):
        total = own_ref[part(i, rows), :] + got_ref[part(i, rows), :].astype(F32)
        out = (keep_ref, send_ref)[i % 2]
        out[part(i // 2, rows), :] = total.astype(out.dtype)


def split_again_kernel(own_ref, got_ref, keep_ref, send_ref):
    rows = keep_ref.shape[0]
    for i, out in enumerate((keep_ref, send_ref)):
        total = own_ref[part(i, rows), :] + got_ref[part(i, rows), :].astype(F32)
        out[...] = total.astype(out.dtype)


def share_kernel(own_ref, got_ref, keep_ref, send_ref, total_ref):
    total_ref[...] = own_ref[...] + got_ref[...].astype(F32)
    rows = keep_ref.shape[0] // 2
    for i, r in enumerate((0, 1)):
        keep_ref[part(i, rows), :] = total_ref[cut(member(r), rows), :]
    for i, r in enumerate((2, 3)):
        send_ref[part(i, rows), :] = total_ref[cut(member(r), rows), :]


def pass_kernel(own_ref, got_ref, keep_ref, send_ref):
    rows = own_ref.shape[0] // 2
    for i, ref in enumerate((own_ref, got_ref)):
        keep_ref[part(i, rows), :] = ref[:rows, :]
        send_ref[part(i, rows), :] = ref[rows:, :]


def finish_kernel(factor, keep_ref, got_ref, out_ref):
    rows, width = out_ref.shape[0], keep_ref.shape[1]
    for i, ref in enumerate((keep_ref, got_ref)):
        for j in range(2):
            out_ref[:, cut(member(i + 2 * j), width)] = ref[part(j, rows), :] * factor


def local(queries, keys, values, cotangent, out_weight, *, dp, seq):
    call = Chain()
    local_seqs, block, features = queries.shape
    outputs = cotangent.shape[2]
    rows = local_seqs * block
    slabs = seq // SLAB
    width = features // SLAB
    heads = width // DH
    q, k, v = (x.reshape(rows, features) for x in (queries, keys, values))
    cot = cotangent.reshape(rows, outputs)
    factor = 1.0 / math.sqrt(rows * dp * seq)
    near = functools.partial(flip, axis="seq", count=seq)

    def spread(parts):
        found = {r: near(parts[r], bits=r) for r in (2, 3, 1)}
        return [parts[0], found[1], found[2], found[3]]

    def doubling(total):
        found = []
        bits = SLAB
        while bits < seq:
            if found:
                (total,) = call(add_kernel, [(total.shape, BF16)], total, found[-1])
            found.append(near(total, bits=bits))
            bits *= 2
        return found, total

    cot_y = near(cot, bits=2)
    keep, send = call(
        start_kernel, [((2, width, DH), F32), ((2, width, DH), BF16)], k, v
    )
    got = near(send, bits=1)
    (columns,) = call(columns_kernel, [((2, out_weight.shape[0], width), BF16)], out_weight)
    tokens = call(
        pack_kernel,
        [((3 * rows + r % 2 * (r < 2) * rows * (outputs // width), width), BF16) for r in range(SLAB)],
        q, k, v, cot,
    )
    w_far = [flip(columns, "dp", dp, j) for j in range(1, dp)]
    own, send = call(halve_kernel, [((width, DH), F32), ((width, DH), BF16)], keep, got)
    got = near(send, bits=2)
    (slab_kv,) = call(add_kernel, [((width, DH), BF16)], own, got)
    attended = [((2, heads, rows, rows), BF16), ((2, rows, width), F32), ((2, width, DH), F32)]
    token1 = near(tokens[1], bits=1)
    send2, send3 = lax.optimization_barrier((tokens[2], tokens[3], slab_kv))[:2]
    attend0, within0, states0 = call(attend_kernel, attended, tokens[0], token1)
    before, last_kv = doubling(slab_kv)
    tokens = [tokens[0], token1, near(send2, bits=2), near(send3, bits=3)]
    cots = [cot, cot_y, near(cot_y, bits=1)]
    attend1, within1, states1 = call(attend_kernel, attended, tokens[2], tokens[3])
    dnormed, cots = call(
        functools.partial(dnormed_kernel, dp),
        [((SLAB, rows, width), F32), ((SLAB, rows, outputs), BF16)],
        token1, *cots, columns, *w_far,
    )
    *normeds, dmixed, prior, u, slab_u = call(
        middle_kernel,
        [((rows, width), BF16)] * SLAB
        + [((SLAB * rows, width), BF16), ((SLAB, width, DH), BF16), ((SLAB, width, DH), F32),
           ((width, DH), BF16)],
        *tokens, *before, within0, states0, within1, states1, dnormed,
        scratch=[pltpu.VMEM((SLAB, width, DH), F32)],
    )
    tuned = dp == 2 and slabs == 4 and outputs // (dp * seq) % 8 == 0
    if tuned:
        keep, send = call(
            functools.partial(product_kernel, slabs),
            [((outputs // dp, width), F32), ((outputs // dp, width), BF16)], cots, *normeds,
        )
        got = flip(send, "dp", dp, 1)
    behind, last_u = doubling(slab_u)
    *backs, parts = call(
        late_kernel,
        [((2 * rows, width), BF16)] * SLAB + [((SLAB, 2 * rows, width), F32)],
        *tokens, *normeds, attend0, attend1, dmixed, prior,
    )
    backs = spread(backs)
    w_all = [x for w in w_far for x in (w, near(w, bits=1))]
    if tuned:
        piece = outputs // (dp * slabs)
        keep, send = call(
            split_kernel, [((2 * piece, width), F32), ((2 * piece, width), BF16)], keep, got
        )
        got = near(send, bits=SLAB)
    grads = call(
        last_kernel, [((2 * rows, width), BF16)] * SLAB, *tokens, *behind, u, parts,
        scratch=[pltpu.VMEM((SLAB, width, DH), F32)],
    )
    got_grads = spread(grads)
    if tuned:
        keep, send = call(
            split_again_kernel, [((piece, width), F32), ((piece, width), BF16)], keep, got
        )
        got = near(send, bits=2 * SLAB)
        keep, send = call(
            share_kernel, [((piece // 2, width), F32)] * 2, keep, got,
            scratch=[pltpu.VMEM((piece, width), F32)],
        )
        got = near(send, bits=2)
    gk, gv = call(join_kernel, [((rows, features), BF16)] * 2, *got_grads)
    output, gq, own_normed = call(
        functools.partial(output_kernel, dp),
        [((rows, outputs), BF16), ((rows, features), BF16), ((rows, features), BF16)],
        *backs, out_weight, *w_all,
    )
    if tuned:
        keep, send = call(pass_kernel, [((piece // 2, width), F32)] * 2, keep, got)
        got = near(send, bits=1)
        (grad_weight,) = call(
            functools.partial(finish_kernel, factor),
            [((piece // SLAB, features), F32)], keep, got,
        )
    else:
        partial = dot(cot, own_normed, 0, 0) * factor
        grad_weight = lax.psum_scatter(partial, ("dp", "seq"), scatter_dimension=0, tiled=True)
    shape = queries.shape
    return (
        output.reshape(cotangent.shape), gq.reshape(shape), gk.reshape(shape), gv.reshape(shape),
        grad_weight,
    )


def solution(mesh):
    dp, seq = mesh.shape["dp"], mesh.shape["seq"]
    return jax.shard_map(
        functools.partial(local, dp=dp, seq=seq),
        mesh=mesh,
        in_specs=(P("dp", "seq", None),) * 4 + (P("dp", None),),
        out_specs=(P("dp", "seq", None),) * 4 + (P(("dp", "seq"), None),),
        check_vma=False,
    )
```

time: 76.5 us -> 63.4 us (0.83)
  starting transfers between devices: 36.9 us -> 24.9 us
  waiting for transfers between devices: 25.3 us -> 23.8 us
    ppermute x6 -> x0, starting transfers between devices: 13.4 us -> none  [along(): found.append(lax.ppermute(x, 'seq', pairs))]
    ppermute x6 -> x0, waiting for transfers between devices: 4.94 us -> none  [along(): found.append(lax.ppermute(x, 'seq', pairs))]
    ppermute x29 -> x24, waiting for transfers between devices: 20.3 us -> 23.8 us  [flip(): return lax.ppermute(x, axis, [(i, i ^ bits) for i in range(count)])]
    ppermute x29 -> x24, starting transfers between devices: 23.5 us -> 24.9 us  [flip(): return lax.ppermute(x, axis, [(i, i ^ bits) for i in range(count)])]
    unnamed x14 -> x18, local copies, waits for them, and re-layouts: 4.69 us -> 5.16 us
    pallas_call x13 -> x21, Pallas kernels: 8.37 us -> 8.44 us  [__call__(): pl.pallas_call(inner, out_shape=[jax.ShapeDtypeStruct(s, d) for s, d in o...]
  transfers between devices with their start and end apart: 35 -> 24, of which waited for: 10 -> 15; matrix products, arithmetic and copies ran while one was open for 0% -> 0% of each run, Pallas kernels for 10% -> 9%
where the time goes in v4:
time: 63.4 us; the launch traced here: 63.1 us
  starting transfers between devices  24.9 us (39%)
  waiting for transfers between devices  23.8 us (38%)
  Pallas kernels  8.44 us (13%)
  local copies, waits for them, and re-layouts  5.16 us (8%)
  between operations  0.81 us (1%)
    ppermute x24, starting transfers between devices, flip(): return lax.ppermute(x, axis, [(i, i ^ bits) for i in range(count)])  24.9 us
    ppermute x24, waiting for transfers between devices, flip(): return lax.ppermute(x, axis, [(i, i ^ bits) for i in range(count)])  23.8 us
    pallas_call x21, Pallas kernels, __call__(): pl.pallas_call(inner, out_shape=[jax.ShapeDtypeStruct(s, d) for s, d in o...  8.44 us
    unnamed x18, local copies, waits for them, and re-layouts  5.16 us
  transfers between devices with their start and end apart: 24, of which 15 were waited for; matrix products, arithmetic and copies ran while one was open for 0% of the time, Pallas kernels for 9%

profile of v4, /device:TPU:0, one launch (start us, length us, event | category | flops | bytes accessed | tf_op | source)
XLA Modules:
  0.0 63.1 jit_solution(17279761768199404297)
XLA Ops:
  0.6 0.9 %copy-done.3 = bf16[1,128,1024]{2,1,0:T(8,128)(2,1)S(1)} copy-done((bf16[1,128,1024]{2,1,0:T(8,128)(2,1)S(1)}, bf16[1,128,1024]{2,1,0:T(8,128)(2,1)}, u32[]{:S(2)}) %copy-start.3) | copy-done | bytes 262168
  1.6 0.9 %copy-done.5 = bf16[1,128,1024]{2,1,0:T(8,128)(2,1)S(1)} copy-done((bf16[1,128,1024]{2,1,0:T(8,128)(2,1)S(1)}, bf16[1,128,1024]{2,1,0:T(8,128)(2,1)}, u32[]{:S(2)}) %copy-start.5) | copy-done | bytes 262168
  2.8 1.2 %copy-done = bf16[512,1024]{1,0:T(8,128)(2,1)S(1)} copy-done((bf16[512,1024]{1,0:T(8,128)(2,1)S(1)}, bf16[512,1024]{1,0:T(8,128)(2,1)}, u32[]{:S(2)}) %copy-start) | copy-done | bytes 1048600
  4.1 0.8 %copy-done.2 = bf16[1,128,1024]{2,1,0:T(8,128)(2,1)S(1)} copy-done((bf16[1,128,1024]{2,1,0:T(8,128)(2,1)S(1)}, bf16[1,128,1024]{2,1,0:T(8,128)(2,1)}, u32[]{:S(2)}) %copy-start.2) | copy-done | bytes 262168
  5.9 2.6 %collective-permute-start.7 = (bf16[128,1024]{1,0:T(8,128)(2,1)S(1)}, bf16[128,1024]{1,0:T(8,128)(2,1)S(1)}, u32[]{:S(2)}, u32[]{:S(2)}) collective-permute-start(bf16[128,1024]{1,0:T(8,128)(2,1)S(1)} %bitcast.9), channel_id=1, source_target_pairs={{0,2},{1,3},{2,0},{3,1},{4,6},{5,7},{6,4},{7,5},{8,10},{9,11},{10,... | collective-permute-start | bytes 786440 | tf_op jit(solution)/shard_map/ppermute | solution.py:56
  8.4 1.5 %collective-permute-start.9 = (bf16[2,512,256]{2,1,0:T(8,128)(2,1)S(1)}, bf16[2,512,256]{2,1,0:T(8,128)(2,1)S(1)}, u32[]{:S(2)}, u32[]{:S(2)}) collective-permute-start(bf16[2,512,256]{2,1,0:T(8,128)(2,1)S(1)} %shard_map.93.refs_4_), channel_id=1, source_target_pairs={{0,16},{16,0},{1,17},{17,1},{2,18},{18,2},{3,19},{19,3},{4,20},{20... | collective-permute-start | bytes 1572872 | tf_op jit(solution)/shard_map/ppermute | solution.py:56
  9.9 1.3 %collective-permute-done.1.refs_1_ = bf16[2,256,128]{2,1,0:T(8,128)(2,1)S(1)} collective-permute-done((bf16[2,256,128]{2,1,0:T(8,128)(2,1)S(1)}, bf16[2,256,128]{2,1,0:T(8,128)(2,1)S(1)}, u32[]{:S(2)}, u32[]{:S(2)}) %collective-permute-start.1) | collective-permute-done | bytes 131104 | tf_op jit(solution)/shard_map/ppermute | solution.py:56
  11.9 3.7 %collective-permute-done.7.refs_2_ = bf16[128,1024]{1,0:T(8,128)(2,1)S(1)} collective-permute-done((bf16[128,1024]{1,0:T(8,128)(2,1)S(1)}, bf16[128,1024]{1,0:T(8,128)(2,1)S(1)}, u32[]{:S(2)}, u32[]{:S(2)}) %collective-permute-start.7) | collective-permute-done | bytes 262176 | tf_op jit(solution)/shard_map/ppermute | solution.py:56
  15.6 1.1 %collective-permute-done.2.refs_1_ = bf16[256,128]{1,0:T(8,128)(2,1)S(1)} collective-permute-done((bf16[256,128]{1,0:T(8,128)(2,1)S(1)}, bf16[256,128]{1,0:T(8,128)(2,1)S(1)}, u32[]{:S(2)}, u32[]{:S(2)}) %collective-permute-start.2) | collective-permute-done | bytes 65568 | tf_op jit(solution)/shard_map/ppermute | solution.py:56
  16.8 1.8 %collective-permute-start.3 = (bf16[384,256]{1,0:T(8,128)(2,1)S(1)}, bf16[384,256]{1,0:T(8,128)(2,1)S(1)}, u32[]{:S(2)}, u32[]{:S(2)}) collective-permute-start(bf16[384,256]{1,0:T(8,128)(2,1)S(1)} %get-tuple-element.63), channel_id=1, source_target_pairs={{0,2},{1,3},{2,0},{3,1},{4,6},{5,7},{6,4},{7,5},{8,10},{9,11},{10,... | collective-permute-start | bytes 589832 | tf_op jit(solution)/shard_map/ppermute | solution.py:56
  18.6 1.6 %collective-permute-start.5 = (bf16[256,128]{1,0:T(8,128)(2,1)S(1)}, bf16[256,128]{1,0:T(8,128)(2,1)S(1)}, u32[]{:S(2)}, u32[]{:S(2)}) collective-permute-start(bf16[256,128]{1,0:T(8,128)(2,1)S(1)} %shard_map.96.refs_2_.refs_0_), channel_id=1, source_target_pairs={{0,4},{1,5},{2,6},{3,7},{4,0},{5,1},{6,2},{7,3},{8,12},{9,13},{10,... | collective-permute-start | bytes 196616 | tf_op jit(solution)/shard_map/ppermute | solution.py:56
  20.6 2.5 %collective-permute-done.5.refs_1_.refs_4_ = bf16[256,128]{1,0:T(8,128)(2,1)S(1)} collective-permute-done((bf16[256,128]{1,0:T(8,128)(2,1)S(1)}, bf16[256,128]{1,0:T(8,128)(2,1)S(1)}, u32[]{:S(2)}, u32[]{:S(2)}) %collective-permute-start.5) | collective-permute-done | bytes 65568 | tf_op jit(solution)/shard_map/ppermute | solution.py:56
  23.1 2.8 %collective-permute-start.6 = (bf16[256,128]{1,0:T(8,128)(2,1)S(1)}, bf16[256,128]{1,0:T(8,128)(2,1)S(1)}, u32[]{:S(2)}, u32[]{:S(2)}) collective-permute-start(bf16[256,128]{1,0:T(8,128)(2,1)S(1)} %shard_map.98.refs_2_), channel_id=1, source_target_pairs={{0,8},{1,9},{2,10},{3,11},{4,12},{5,13},{6,14},{7,15},{8,0},{9,1},... | collective-permute-start | bytes 196616 | tf_op jit(solution)/shard_map/ppermute | solution.py:56
  25.9 0.9 %collective-permute-done.4.refs_1_.refs_3_ = bf16[384,256]{1,0:T(8,128)(2,1)S(1)} collective-permute-done((bf16[384,256]{1,0:T(8,128)(2,1)S(1)}, bf16[384,256]{1,0:T(8,128)(2,1)S(1)}, u32[]{:S(2)}, u32[]{:S(2)}) %collective-permute-start.4) | collective-permute-done | bytes 196640 | tf_op jit(solution)/shard_map/ppermute | solution.py:56
  27.7 2.0 %collective-permute-done.6.refs_5_ = bf16[256,128]{1,0:T(8,128)(2,1)S(1)} collective-permute-done((bf16[256,128]{1,0:T(8,128)(2,1)S(1)}, bf16[256,128]{1,0:T(8,128)(2,1)S(1)}, u32[]{:S(2)}, u32[]{:S(2)}) %collective-permute-start.6) | collective-permute-done | bytes 65568 | tf_op jit(solution)/shard_map/ppermute | solution.py:56
  31.3 1.6 %collective-permute-start.16 = (bf16[512,256]{1,0:T(8,128)(2,1)S(1)}, bf16[512,256]{1,0:T(8,128)(2,1)S(1)}, u32[]{:S(2)}, u32[]{:S(2)}) collective-permute-start(bf16[512,256]{1,0:T(8,128)(2,1)S(1)} %get-tuple-element.80.refs_2_), channel_id=1, source_target_pairs={{0,16},{16,0},{1,17},{17,1},{2,18},{18,2},{3,19},{19,3},{4,20},{20... | collective-permute-start | bytes 786440 | tf_op jit(solution)/shard_map/ppermute | solution.py:56
  33.3 4.1 %collective-permute-done.10.refs_1_.refs_4_ = bf16[256,128]{1,0:T(8,128)(2,1)S(1)} collective-permute-done((bf16[256,128]{1,0:T(8,128)(2,1)S(1)}, bf16[256,128]{1,0:T(8,128)(2,1)S(1)}, u32[]{:S(2)}, u32[]{:S(2)}) %collective-permute-start.10) | collective-permute-done | bytes 65568 | tf_op jit(solution)/shard_map/ppermute | solution.py:56
  37.4 2.1 %collective-permute-start.15 = (bf16[256,128]{1,0:T(8,128)(2,1)S(1)}, bf16[256,128]{1,0:T(8,128)(2,1)S(1)}, u32[]{:S(2)}, u32[]{:S(2)}) collective-permute-start(bf16[256,128]{1,0:T(8,128)(2,1)S(1)} %shard_map.103.refs_12_), channel_id=1, source_target_pairs={{0,8},{1,9},{2,10},{3,11},{4,12},{5,13},{6,14},{7,15},{8,0},{9,1},... | collective-permute-start | bytes 196616 | tf_op jit(solution)/shard_map/ppermute | solution.py:56
  39.5 1.4 %shard_map.104 = (bf16[256,256]{1,0:T(8,128)(2,1)S(1)}, bf16[256,256]{1,0:T(8,128)(2,1)S(1)}, bf16[256,256]{1,0:T(8,128)(2,1)S(1)}, bf16[256,256]{1,0:T(8,128)(2,1)S(1)}, f32[4,256,256]{2,1,0:T(8,128)S(1)}) custom-call(bf16[384,256]{1,0:T(8,128)(2,1)S(1)} %get-tuple-element.56.refs_0_, bf16[896,256]{1,0:T(8,128)(2,1)S(1)} %collective-permute-done.refs_1_.refs_0_, ...), custom_call_target="tpu_custom_call" | custom-call | flops 1 | bytes 1 | tf_op jit(solution)/shard_map/pallas_call | solution.py:39
  41.0 1.8 %collective-permute-start.20 = (bf16[256,256]{1,0:T(8,128)(2,1)S(1)}, bf16[256,256]{1,0:T(8,128)(2,1)S(1)}, u32[]{:S(2)}, u32[]{:S(2)}) collective-permute-start(bf16[256,256]{1,0:T(8,128)(2,1)S(1)} %get-tuple-element.88.refs_8_), channel_id=1, source_target_pairs={{0,4},{1,5},{2,6},{3,7},{4,0},{5,1},{6,2},{7,3},{8,12},{9,13},{10,... | collective-permute-start | bytes 393224 | tf_op jit(solution)/shard_map/ppermute | solution.py:56
  44.1 1.5 %collective-permute-start.18 = (bf16[256,256]{1,0:T(8,128)(2,1)S(1)}, bf16[256,256]{1,0:T(8,128)(2,1)S(1)}, u32[]{:S(2)}, u32[]{:S(2)}) collective-permute-start(bf16[256,256]{1,0:T(8,128)(2,1)S(1)} %get-tuple-element.91), channel_id=1, source_target_pairs={{0,2},{1,3},{2,0},{3,1},{4,6},{5,7},{6,4},{7,5},{8,10},{9,11},{10,... | collective-permute-start | bytes 393224 | tf_op jit(solution)/shard_map/ppermute | solution.py:56
  47.1 1.5 %collective-permute-start.11 = (bf16[256,256]{1,0:T(8,128)(2,1)S(1)}, bf16[256,256]{1,0:T(8,128)(2,1)S(1)}, u32[]{:S(2)}, u32[]{:S(2)}) collective-permute-start(bf16[256,256]{1,0:T(8,128)(2,1)S(1)} %get-tuple-element.82), channel_id=1, source_target_pairs={{0,1},{1,0},{2,3},{3,2},{4,5},{5,4},{6,7},{7,6},{8,9},{9,8},{10,11... | collective-permute-start | bytes 393224 | tf_op jit(solution)/shard_map/ppermute | solution.py:56
  48.6 1.4 %collective-permute-done.18.refs_2_ = bf16[256,256]{1,0:T(8,128)(2,1)S(1)} collective-permute-done((bf16[256,256]{1,0:T(8,128)(2,1)S(1)}, bf16[256,256]{1,0:T(8,128)(2,1)S(1)}, u32[]{:S(2)}, u32[]{:S(2)}) %collective-permute-start.18) | collective-permute-done | bytes 131104 | tf_op jit(solution)/shard_map/ppermute | solution.py:56
  50.0 1.4 %collective-permute-start.12 = (bf16[256,256]{1,0:T(8,128)(2,1)S(1)}, bf16[256,256]{1,0:T(8,128)(2,1)S(1)}, u32[]{:S(2)}, u32[]{:S(2)}) collective-permute-start(bf16[256,256]{1,0:T(8,128)(2,1)S(1)} %get-tuple-element.83), channel_id=1, source_target_pairs={{0,2},{1,3},{2,0},{3,1},{4,6},{5,7},{6,4},{7,5},{8,10},{9,11},{10,... | collective-permute-start | bytes 393224 | tf_op jit(solution)/shard_map/ppermute | solution.py:56
  51.6 1.2 %collective-permute-done.19.refs_3_ = bf16[256,256]{1,0:T(8,128)(2,1)S(1)} collective-permute-done((bf16[256,256]{1,0:T(8,128)(2,1)S(1)}, bf16[256,256]{1,0:T(8,128)(2,1)S(1)}, u32[]{:S(2)}, u32[]{:S(2)}) %collective-permute-start.19) | collective-permute-done | bytes 131104 | tf_op jit(solution)/shard_map/ppermute | solution.py:56
  52.8 1.4 %collective-permute-start.22 = (f32[64,256]{1,0:T(8,128)S(1)}, f32[64,256]{1,0:T(8,128)S(1)}, u32[]{:S(2)}, u32[]{:S(2)}) collective-permute-start(f32[64,256]{1,0:T(8,128)S(1)} %get-tuple-element.96.refs_4_), channel_id=1, source_target_pairs={{0,2},{1,3},{2,0},{3,1},{4,6},{5,7},{6,4},{7,5},{8,10},{9,11},{10,... | collective-permute-start | bytes 196616 | tf_op jit(solution)/shard_map/ppermute | solution.py:56
  55.1 1.4 %collective-permute-done.12.refs_2_ = bf16[256,256]{1,0:T(8,128)(2,1)S(1)} collective-permute-done((bf16[256,256]{1,0:T(8,128)(2,1)S(1)}, bf16[256,256]{1,0:T(8,128)(2,1)S(1)}, u32[]{:S(2)}, u32[]{:S(2)}) %collective-permute-start.12) | collective-permute-done | bytes 131104 | tf_op jit(solution)/shard_map/ppermute | solution.py:56
  56.4 1.6 %collective-permute-done.13.refs_3_ = bf16[256,256]{1,0:T(8,128)(2,1)S(1)} collective-permute-done((bf16[256,256]{1,0:T(8,128)(2,1)S(1)}, bf16[256,256]{1,0:T(8,128)(2,1)S(1)}, u32[]{:S(2)}, u32[]{:S(2)}) %collective-permute-start.13) | collective-permute-done | bytes 131104 | tf_op jit(solution)/shard_map/ppermute | solution.py:56
  58.1 0.9 %copy-done.8 = bf16[128,1024]{1,0:T(8,128)(2,1)S(1)} copy-done((bf16[128,1024]{1,0:T(8,128)(2,1)S(1)}, bf16[128,1024]{1,0:T(8,128)(2,1)}, u32[]{:S(2)}) %copy-start.8) | copy-done | bytes 262168
  59.0 1.5 %shard_map.110 = (bf16[128,1024]{1,0:T(8,128)(2,1)}, bf16[128,1024]{1,0:T(8,128)(2,1)}, bf16[128,1024]{1,0:T(8,128)(2,1)S(1)}) custom-call(bf16[256,256]{1,0:T(8,128)(2,1)S(1)} %get-tuple-element.81.refs_0_, bf16[256,256]{1,0:T(8,128)(2,1)S(1)} %collective-permute-done.11.refs_1_, bf16[256,256]{1,0:T(8,128)(2,1)S(1)} %collective-permute-done.12.refs_2_, ...), custom_call_target="tpu_custom_call" | custom-call | flops 1 | bytes 1 | tf_op jit(solution)/shard_map/pallas_call | solution.py:39
  60.6 1.0 %collective-permute-start.23 = (f32[64,256]{1,0:T(8,128)S(1)}, f32[64,256]{1,0:T(8,128)S(1)}, u32[]{:S(2)}, u32[]{:S(2)}) collective-permute-start(f32[64,256]{1,0:T(8,128)S(1)} %get-tuple-element.104.refs_2_), channel_id=1, source_target_pairs={{0,1},{1,0},{2,3},{3,2},{4,5},{5,4},{6,7},{7,6},{8,9},{9,8},{10,11... | collective-permute-start | bytes 196616 | tf_op jit(solution)/shard_map/ppermute | solution.py:56
  61.6 0.9 %collective-permute-done.23.refs_1_ = f32[64,256]{1,0:T(8,128)S(1)} collective-permute-done((f32[64,256]{1,0:T(8,128)S(1)}, f32[64,256]{1,0:T(8,128)S(1)}, u32[]{:S(2)}, u32[]{:S(2)}) %collective-permute-start.23) | collective-permute-done | bytes 65568 | tf_op jit(solution)/shard_map/ppermute | solution.py:56
  (55 shorter events, 9.7 us)
Async XLA Ops:
  0.6 1.0 %copy-start.3 = (bf16[1,128,1024]{2,1,0:T(8,128)(2,1)S(1)}, bf16[1,128,1024]{2,1,0:T(8,128)(2,1)}, u32[]{:S(2)}) copy-start(bf16[1,128,1024]{2,1,0:T(8,128)(2,1)} %param.6) | copy-start | bytes 786436
  1.6 0.9 %copy-start.5 = (bf16[1,128,1024]{2,1,0:T(8,128)(2,1)S(1)}, bf16[1,128,1024]{2,1,0:T(8,128)(2,1)}, u32[]{:S(2)}) copy-start(bf16[1,128,1024]{2,1,0:T(8,128)(2,1)} %param.7) | copy-start | bytes 786436
  2.8 1.2 %copy-start = (bf16[512,1024]{1,0:T(8,128)(2,1)S(1)}, bf16[512,1024]{1,0:T(8,128)(2,1)}, u32[]{:S(2)}) copy-start(bf16[512,1024]{1,0:T(8,128)(2,1)} %refs_4_.1) | copy-start | bytes 3145732
  4.0 1.0 %copy-start.4 = (bf16[1,128,1024]{2,1,0:T(8,128)(2,1)S(1)}, bf16[1,128,1024]{2,1,0:T(8,128)(2,1)}, u32[]{:S(2)}) copy-start(bf16[1,128,1024]{2,1,0:T(8,128)(2,1)} %param.6) | copy-start | bytes 786436
  4.0 1.1 %copy-start.6 = (bf16[1,128,1024]{2,1,0:T(8,128)(2,1)S(1)}, bf16[1,128,1024]{2,1,0:T(8,128)(2,1)}, u32[]{:S(2)}) copy-start(bf16[1,128,1024]{2,1,0:T(8,128)(2,1)} %param.7) | copy-start | bytes 786436
  4.0 1.2 %copy-start.7 = (bf16[1,128,1024]{2,1,0:T(8,128)(2,1)S(1)}, bf16[1,128,1024]{2,1,0:T(8,128)(2,1)}, u32[]{:S(2)}) copy-start(bf16[1,128,1024]{2,1,0:T(8,128)(2,1)} %param.5) | copy-start | bytes 786436
  5.3 13.3 %collective-permute-start = (bf16[896,256]{1,0:T(8,128)(2,1)S(1)}, bf16[896,256]{1,0:T(8,128)(2,1)S(1)}, u32[]{:S(2)}, u32[]{:S(2)}) collective-permute-start(bf16[896,256]{1,0:T(8,128)(2,1)S(1)} %get-tuple-element.57), channel_id=1, source_target_pairs={{0,1},{1,0},{2,3},{3,2},{4,5},{5,4},{6,7},{7,6},{8,9},{9,8},{10,11... | collective-permute-start | bytes 1376264 | tf_op jit(solution)/shard_map/ppermute | solution.py:56
  5.9 9.7 %collective-permute-start.7 = (bf16[128,1024]{1,0:T(8,128)(2,1)S(1)}, bf16[128,1024]{1,0:T(8,128)(2,1)S(1)}, u32[]{:S(2)}, u32[]{:S(2)}) collective-permute-start(bf16[128,1024]{1,0:T(8,128)(2,1)S(1)} %bitcast.9), channel_id=1, source_target_pairs={{0,2},{1,3},{2,0},{3,1},{4,6},{5,7},{6,4},{7,5},{8,10},{9,11},{10,... | collective-permute-start | bytes 786440 | tf_op jit(solution)/shard_map/ppermute | solution.py:56
  8.4 18.8 %collective-permute-start.9 = (bf16[2,512,256]{2,1,0:T(8,128)(2,1)S(1)}, bf16[2,512,256]{2,1,0:T(8,128)(2,1)S(1)}, u32[]{:S(2)}, u32[]{:S(2)}) collective-permute-start(bf16[2,512,256]{2,1,0:T(8,128)(2,1)S(1)} %shard_map.93.refs_4_), channel_id=1, source_target_pairs={{0,16},{16,0},{1,17},{17,1},{2,18},{18,2},{3,19},{19,3},{4,20},{20... | collective-permute-start | bytes 1572872 | tf_op jit(solution)/shard_map/ppermute | solution.py:56
  9.9 1.3 %collective-permute-start.1 = (bf16[2,256,128]{2,1,0:T(8,128)(2,1)S(1)}, bf16[2,256,128]{2,1,0:T(8,128)(2,1)S(1)}, u32[]{:S(2)}, u32[]{:S(2)}) collective-permute-start(bf16[2,256,128]{2,1,0:T(8,128)(2,1)S(1)} %get-tuple-element.55.refs_1_), channel_id=1, source_target_pairs={{0,1},{1,0},{2,3},{3,2},{4,5},{5,4},{6,7},{7,6},{8,9},{9,8},{10,11... | collective-permute-start | bytes 393224 | tf_op jit(solution)/shard_map/ppermute | solution.py:56
  11.3 5.4 %collective-permute-start.2 = (bf16[256,128]{1,0:T(8,128)(2,1)S(1)}, bf16[256,128]{1,0:T(8,128)(2,1)S(1)}, u32[]{:S(2)}, u32[]{:S(2)}) collective-permute-start(bf16[256,128]{1,0:T(8,128)(2,1)S(1)} %get-tuple-element.62.refs_2_), channel_id=1, source_target_pairs={{0,2},{1,3},{2,0},{3,1},{4,6},{5,7},{6,4},{7,5},{8,10},{9,11},{10,... | collective-permute-start | bytes 196616 | tf_op jit(solution)/shard_map/ppermute | solution.py:56
  15.6 11.6 %collective-permute-start.8 = (bf16[128,1024]{1,0:T(8,128)(2,1)S(1)}, bf16[128,1024]{1,0:T(8,128)(2,1)S(1)}, u32[]{:S(2)}, u32[]{:S(2)}) collective-permute-start(bf16[128,1024]{1,0:T(8,128)(2,1)S(1)} %collective-permute-done.7.refs_2_), channel_id=1, source_target_pairs={{0,1},{1,0},{2,3},{3,2},{4,5},{5,4},{6,7},{7,6},{8,9},{9,8},{10,11... | collective-permute-start | bytes 786440 | tf_op jit(solution)/shard_map/ppermute | solution.py:56
  16.8 9.1 %collective-permute-start.3 = (bf16[384,256]{1,0:T(8,128)(2,1)S(1)}, bf16[384,256]{1,0:T(8,128)(2,1)S(1)}, u32[]{:S(2)}, u32[]{:S(2)}) collective-permute-start(bf16[384,256]{1,0:T(8,128)(2,1)S(1)} %get-tuple-element.63), channel_id=1, source_target_pairs={{0,2},{1,3},{2,0},{3,1},{4,6},{5,7},{6,4},{7,5},{8,10},{9,11},{10,... | collective-permute-start | bytes 589832 | tf_op jit(solution)/shard_map/ppermute | solution.py:56
  18.6 8.2 %collective-permute-start.4 = (bf16[384,256]{1,0:T(8,128)(2,1)S(1)}, bf16[384,256]{1,0:T(8,128)(2,1)S(1)}, u32[]{:S(2)}, u32[]{:S(2)}) collective-permute-start(bf16[384,256]{1,0:T(8,128)(2,1)S(1)} %get-tuple-element.64.refs_2_), channel_id=1, source_target_pairs={{0,3},{1,2},{2,1},{3,0},{4,7},{5,6},{6,5},{7,4},{8,11},{9,10},{10,... | collective-permute-start | bytes 589832 | tf_op jit(solution)/shard_map/ppermute | solution.py:56
  18.6 4.5 %collective-permute-start.5 = (bf16[256,128]{1,0:T(8,128)(2,1)S(1)}, bf16[256,128]{1,0:T(8,128)(2,1)S(1)}, u32[]{:S(2)}, u32[]{:S(2)}) collective-permute-start(bf16[256,128]{1,0:T(8,128)(2,1)S(1)} %shard_map.96.refs_2_.refs_0_), channel_id=1, source_target_pairs={{0,4},{1,5},{2,6},{3,7},{4,0},{5,1},{6,2},{7,3},{8,12},{9,13},{10,... | collective-permute-start | bytes 196616 | tf_op jit(solution)/shard_map/ppermute | solution.py:56
  23.1 6.6 %collective-permute-start.6 = (bf16[256,128]{1,0:T(8,128)(2,1)S(1)}, bf16[256,128]{1,0:T(8,128)(2,1)S(1)}, u32[]{:S(2)}, u32[]{:S(2)}) collective-permute-start(bf16[256,128]{1,0:T(8,128)(2,1)S(1)} %shard_map.98.refs_2_), channel_id=1, source_target_pairs={{0,8},{1,9},{2,10},{3,11},{4,12},{5,13},{6,14},{7,15},{8,0},{9,1},... | collective-permute-start | bytes 196616 | tf_op jit(solution)/shard_map/ppermute | solution.py:56
  31.3 9.7 %collective-permute-start.16 = (bf16[512,256]{1,0:T(8,128)(2,1)S(1)}, bf16[512,256]{1,0:T(8,128)(2,1)S(1)}, u32[]{:S(2)}, u32[]{:S(2)}) collective-permute-start(bf16[512,256]{1,0:T(8,128)(2,1)S(1)} %get-tuple-element.80.refs_2_), channel_id=1, source_target_pairs={{0,16},{16,0},{1,17},{17,1},{2,18},{18,2},{3,19},{19,3},{4,20},{20... | collective-permute-start | bytes 786440 | tf_op jit(solution)/shard_map/ppermute | solution.py:56
  32.9 25.2 %collective-permute-start.14 = (bf16[2,512,256]{2,1,0:T(8,128)(2,1)S(1)}, bf16[2,512,256]{2,1,0:T(8,128)(2,1)S(1)}, u32[]{:S(2)}, u32[]{:S(2)}) collective-permute-start(bf16[2,512,256]{2,1,0:T(8,128)(2,1)S(1)} %collective-permute-done.9.refs_5_), channel_id=1, source_target_pairs={{0,1},{1,0},{2,3},{3,2},{4,5},{5,4},{6,7},{7,6},{8,9},{9,8},{10,11... | collective-permute-start | bytes 1572872 | tf_op jit(solution)/shard_map/ppermute | solution.py:56
  32.9 4.5 %collective-permute-start.10 = (bf16[256,128]{1,0:T(8,128)(2,1)S(1)}, bf16[256,128]{1,0:T(8,128)(2,1)S(1)}, u32[]{:S(2)}, u32[]{:S(2)}) collective-permute-start(bf16[256,128]{1,0:T(8,128)(2,1)S(1)} %get-tuple-element.79.refs_5_.refs_0_), channel_id=1, source_target_pairs={{0,4},{1,5},{2,6},{3,7},{4,0},{5,1},{6,2},{7,3},{8,12},{9,13},{10,... | collective-permute-start | bytes 196616 | tf_op jit(solution)/shard_map/ppermute | solution.py:56
  37.4 6.1 %collective-permute-start.15 = (bf16[256,128]{1,0:T(8,128)(2,1)S(1)}, bf16[256,128]{1,0:T(8,128)(2,1)S(1)}, u32[]{:S(2)}, u32[]{:S(2)}) collective-permute-start(bf16[256,128]{1,0:T(8,128)(2,1)S(1)} %shard_map.103.refs_12_), channel_id=1, source_target_pairs={{0,8},{1,9},{2,10},{3,11},{4,12},{5,13},{6,14},{7,15},{8,0},{9,1},... | collective-permute-start | bytes 196616 | tf_op jit(solution)/shard_map/ppermute | solution.py:56
  41.0 5.3 %collective-permute-start.20 = (bf16[256,256]{1,0:T(8,128)(2,1)S(1)}, bf16[256,256]{1,0:T(8,128)(2,1)S(1)}, u32[]{:S(2)}, u32[]{:S(2)}) collective-permute-start(bf16[256,256]{1,0:T(8,128)(2,1)S(1)} %get-tuple-element.88.refs_8_), channel_id=1, source_target_pairs={{0,4},{1,5},{2,6},{3,7},{4,0},{5,1},{6,2},{7,3},{8,12},{9,13},{10,... | collective-permute-start | bytes 393224 | tf_op jit(solution)/shard_map/ppermute | solution.py:56
  44.0 14.1 %copy-start.1 = (bf16[512,1024]{1,0:T(8,128)(2,1)S(1)}, bf16[512,1024]{1,0:T(8,128)(2,1)}, u32[]{:S(2)}) copy-start(bf16[512,1024]{1,0:T(8,128)(2,1)} %refs_4_.1) | copy-start | bytes 3145732
  44.0 3.1 %collective-permute-start.17 = (bf16[256,256]{1,0:T(8,128)(2,1)S(1)}, bf16[256,256]{1,0:T(8,128)(2,1)S(1)}, u32[]{:S(2)}, u32[]{:S(2)}) collective-permute-start(bf16[256,256]{1,0:T(8,128)(2,1)S(1)} %get-tuple-element.90), channel_id=1, source_target_pairs={{0,1},{1,0},{2,3},{3,2},{4,5},{5,4},{6,7},{7,6},{8,9},{9,8},{10,11... | collective-permute-start | bytes 393224 | tf_op jit(solution)/shard_map/ppermute | solution.py:56
  44.1 5.9 %collective-permute-start.18 = (bf16[256,256]{1,0:T(8,128)(2,1)S(1)}, bf16[256,256]{1,0:T(8,128)(2,1)S(1)}, u32[]{:S(2)}, u32[]{:S(2)}) collective-permute-start(bf16[256,256]{1,0:T(8,128)(2,1)S(1)} %get-tuple-element.91), channel_id=1, source_target_pairs={{0,2},{1,3},{2,0},{3,1},{4,6},{5,7},{6,4},{7,5},{8,10},{9,11},{10,... | collective-permute-start | bytes 393224 | tf_op jit(solution)/shard_map/ppermute | solution.py:56
  46.4 5.2 %collective-permute-start.21 = (bf16[128,256]{1,0:T(8,128)(2,1)S(1)}, bf16[128,256]{1,0:T(8,128)(2,1)S(1)}, u32[]{:S(2)}, u32[]{:S(2)}) collective-permute-start(bf16[128,256]{1,0:T(8,128)(2,1)S(1)} %get-tuple-element.95.refs_2_), channel_id=1, source_target_pairs={{0,8},{1,9},{2,10},{3,11},{4,12},{5,13},{6,14},{7,15},{8,0},{9,1},... | collective-permute-start | bytes 196616 | tf_op jit(solution)/shard_map/ppermute | solution.py:56
  47.0 5.8 %collective-permute-start.19 = (bf16[256,256]{1,0:T(8,128)(2,1)S(1)}, bf16[256,256]{1,0:T(8,128)(2,1)S(1)}, u32[]{:S(2)}, u32[]{:S(2)}) collective-permute-start(bf16[256,256]{1,0:T(8,128)(2,1)S(1)} %get-tuple-element.92.refs_2_), channel_id=1, source_target_pairs={{0,3},{1,2},{2,1},{3,0},{4,7},{5,6},{6,5},{7,4},{8,11},{9,10},{10,... | collective-permute-start | bytes 393224 | tf_op jit(solution)/shard_map/ppermute | solution.py:56
  47.1 8.0 %collective-permute-start.11 = (bf16[256,256]{1,0:T(8,128)(2,1)S(1)}, bf16[256,256]{1,0:T(8,128)(2,1)S(1)}, u32[]{:S(2)}, u32[]{:S(2)}) collective-permute-start(bf16[256,256]{1,0:T(8,128)(2,1)S(1)} %get-tuple-element.82), channel_id=1, source_target_pairs={{0,1},{1,0},{2,3},{3,2},{4,5},{5,4},{6,7},{7,6},{8,9},{9,8},{10,11... | collective-permute-start | bytes 393224 | tf_op jit(solution)/shard_map/ppermute | solution.py:56
  50.0 6.4 %collective-permute-start.12 = (bf16[256,256]{1,0:T(8,128)(2,1)S(1)}, bf16[256,256]{1,0:T(8,128)(2,1)S(1)}, u32[]{:S(2)}, u32[]{:S(2)}) collective-permute-start(bf16[256,256]{1,0:T(8,128)(2,1)S(1)} %get-tuple-element.83), channel_id=1, source_target_pairs={{0,2},{1,3},{2,0},{3,1},{4,6},{5,7},{6,4},{7,5},{8,10},{9,11},{10,... | collective-permute-start | bytes 393224 | tf_op jit(solution)/shard_map/ppermute | solution.py:56
  51.6 6.5 %collective-permute-start.13 = (bf16[256,256]{1,0:T(8,128)(2,1)S(1)}, bf16[256,256]{1,0:T(8,128)(2,1)S(1)}, u32[]{:S(2)}, u32[]{:S(2)}) collective-permute-start(bf16[256,256]{1,0:T(8,128)(2,1)S(1)} %get-tuple-element.84), channel_id=1, source_target_pairs={{0,3},{1,2},{2,1},{3,0},{4,7},{5,6},{6,5},{7,4},{8,11},{9,10},{10,... | collective-permute-start | bytes 393224 | tf_op jit(solution)/shard_map/ppermute | solution.py:56
  52.8 7.8 %collective-permute-start.22 = (f32[64,256]{1,0:T(8,128)S(1)}, f32[64,256]{1,0:T(8,128)S(1)}, u32[]{:S(2)}, u32[]{:S(2)}) collective-permute-start(f32[64,256]{1,0:T(8,128)S(1)} %get-tuple-element.96.refs_4_), channel_id=1, source_target_pairs={{0,2},{1,3},{2,0},{3,1},{4,6},{5,7},{6,4},{7,5},{8,10},{9,11},{10,... | collective-permute-start | bytes 196616 | tf_op jit(solution)/shard_map/ppermute | solution.py:56
  58.1 1.0 %copy-start.8 = (bf16[128,1024]{1,0:T(8,128)(2,1)S(1)}, bf16[128,1024]{1,0:T(8,128)(2,1)}, u32[]{:S(2)}) copy-start(bf16[128,1024]{1,0:T(8,128)(2,1)} %get-tuple-element.97.refs_7_) | copy-start | bytes 786436
  60.6 1.9 %collective-permute-start.23 = (f32[64,256]{1,0:T(8,128)S(1)}, f32[64,256]{1,0:T(8,128)S(1)}, u32[]{:S(2)}, u32[]{:S(2)}) collective-permute-start(f32[64,256]{1,0:T(8,128)S(1)} %get-tuple-element.104.refs_2_), channel_id=1, source_target_pairs={{0,1},{1,0},{2,3},{3,2},{4,5},{5,4},{6,7},{7,6},{8,9},{9,8},{10,11... | collective-permute-start | bytes 196616 | tf_op jit(solution)/shard_map/ppermute | solution.py:56
  (1 other events, 0.9 us)

commit v5 on v4

v5 whole, which is shorter than its diff:
```python
import functools
import math

import jax
import jax.numpy as jnp
from jax import lax
from jax.experimental import pallas as pl
from jax.experimental.pallas import tpu as pltpu
from jax.sharding import PartitionSpec as P

DH = 128
SLAB = 4
EPSILON = 1e-05
BF16 = jnp.bfloat16
F32 = jnp.float32


def dot(left, right, left_dim, right_dim):
    return lax.dot_general(
        left, right, (((left_dim,), (right_dim,)), ((), ())), preferred_element_type=F32
    )


class Chain:
    def __init__(self):
        self.last = None

    def __call__(self, body, outs, *args, scratch=(), far=False, wait=()):
        count = len(args)
        if far:
            args = [pltpu.with_memory_space_constraint(x, pltpu.HBM) for x in args]
        specs = [pl.BlockSpec(memory_space=pl.ANY) if far else pl.BlockSpec()] * count
        inner = body
        if self.last is not None:
            extra = (self.last, *wait)
            args = (*args, *extra)
            specs = [*specs, *[pl.BlockSpec(memory_space=pl.ANY)] * len(extra)]

            def inner(*refs):
                body(*refs[:count], *refs[count + len(extra) :])

        found = pl.pallas_call(
            inner,
            out_shape=[jax.ShapeDtypeStruct(s, d) for s, d in outs],
            in_specs=specs,
            scratch_shapes=list(scratch),
            cost_estimate=pl.CostEstimate(flops=1, bytes_accessed=1, transcendentals=0),
            compiler_params=pltpu.CompilerParams(vmem_limit_bytes=32 * 2**20),
        )(*args)
        self.last = found[-1]
        return found


def after(x, *others):
    return lax.optimization_barrier((x, *others))[0]


def flip(x, axis, count, bits):
    return lax.ppermute(x, axis, [(i, i ^ bits) for i in range(count)])


def head(h):
    return slice(h * DH, (h + 1) * DH)


def part(i, size):
    return slice(i * size, (i + 1) * size)


def cut(start, size):
    return pl.ds(pl.multiple_of(start * size, size), size)


def member(r):
    return jnp.bitwise_xor(lax.rem(lax.axis_index("seq"), SLAB), r)


def causal(block):
    rows = lax.broadcasted_iota(jnp.int32, (block, block), 0)
    return lax.broadcasted_iota(jnp.int32, (block, block), 1) <= rows


def fetch(pairs, sems):
    copies = [pltpu.make_async_copy(a, b, sems.at[i]) for i, (a, b) in enumerate(pairs)]
    for copy in copies:
        copy.start()
    return copies


def front_kernel(k_hbm, v_hbm, q_hbm, c_hbm, w_hbm, *refs):
    keep_ref, message_ref, own_ref, far_ref, columns_ref = refs[:5]
    k_ref, v_ref, q_ref, c_ref, w_ref, sems = refs[5:]
    copies = fetch(
        [(k_hbm, k_ref), (v_hbm, v_ref), (q_hbm, q_ref), (c_hbm, c_ref), (w_hbm, w_ref)], sems
    )
    block = k_ref.shape[0]
    width = k_ref.shape[1] // SLAB
    copies[0].wait()
    copies[1].wait()
    for r in range(SLAB):
        k, v = k_ref[:, cut(member(r), width)], v_ref[:, cut(member(r), width)]
        for h in range(width // DH):
            state = dot(k[:, head(h)], v[:, head(h)], 0, 0)
            if r % 2:
                message_ref[part(r // 2, DH), head(h)] = state.astype(BF16)
            else:
                keep_ref[r // 2, :, head(h)] = state
    copies[2].wait()
    places = ((own_ref, 0), (message_ref, 2 * DH), (far_ref, 0), (message_ref, 2 * DH + 3 * block))
    for r, (out, at) in enumerate(places):
        for i, ref in enumerate((q_ref, k_ref, v_ref)):
            out[at + i * block : at + (i + 1) * block, :] = ref[:, cut(member(r), width)]
    copies[3].wait()
    for i in range(c_ref.shape[1] // width):
        message_ref[2 * DH + (6 + i) * block : 2 * DH + (7 + i) * block, :] = c_ref[:, part(i, width)]
    copies[4].wait()
    for i in range(2):
        columns_ref[i] = w_ref[:, cut(member(2 * i), width)]


def halve_kernel(keep_ref, got_ref, own_ref, send_ref):
    own_ref[...] = keep_ref[0] + got_ref[part(0, DH), :].astype(F32)
    send_ref[...] = (keep_ref[1] + got_ref[part(1, DH), :].astype(F32)).astype(BF16)


def pair_kernel(message_ref, far_ref, out_ref):
    size = far_ref.shape[0]
    out_ref[:size, :] = far_ref[...]
    out_ref[size:, :] = message_ref[2 * DH + size : 2 * DH + 2 * size, :]


def add_kernel(own_ref, got_ref, out_ref):
    out_ref[...] = (own_ref[...].astype(F32) + got_ref[...].astype(F32)).astype(out_ref.dtype)


def tokens_of(r, own_ref, message_ref, far_ref):
    size = own_ref.shape[0]
    if r == 0:
        return own_ref
    if r == 1:
        return message_ref.at[2 * DH : 2 * DH + size]
    return far_ref.at[(r - 2) * size : (r - 1) * size]


def attend_kernel(halves, *refs):
    tokens, (attend_ref, within_ref, states_ref) = refs[:-3], refs[-3:]
    _, block, width = within_ref.shape
    mask = causal(block)
    if halves:
        tokens = [tokens_of(r, tokens[0], tokens[1], None) for r in (0, 1)]
    else:
        tokens = [tokens[0].at[part(r, 3 * block)] for r in (0, 1)]
    for r, ref in enumerate(tokens):
        for h in range(width // DH):
            q, k, v = (ref[part(i, block), head(h)] for i in range(3))
            attend = jnp.where(mask, dot(q, k, 1, 1), 0.0).astype(BF16)
            attend_ref[r, h] = attend
            within_ref[r, :, head(h)] = dot(attend, v, 1, 0)
            states_ref[r, :, head(h)] = dot(k, v, 0, 0)


def dnormed_kernel(groups, message_ref, *refs):
    cots, weights = refs[: SLAB - 1], refs[SLAB - 1 : SLAB - 1 + groups]
    dnormed_ref, cot_ref = refs[SLAB - 1 + groups :]
    block, outputs = cots[0].shape
    width = dnormed_ref.shape[2]
    rows = weights[0].shape[1]
    me = lax.axis_index("dp")
    at = 2 * DH + 6 * block
    for i in range(outputs // width):
        cot_ref[1, :, part(i, width)] = message_ref[at + i * block : at + (i + 1) * block, :]
    for r, ref in zip((0, 2, 3), cots):
        cot_ref[r] = ref[...]
    for r in range(SLAB):
        total = dot(cot_ref[r, :, cut(me, rows)], weights[0][0], 1, 0)
        for j in range(1, groups):
            total = total + dot(cot_ref[r, :, cut(jnp.bitwise_xor(me, j), rows)], weights[j][0], 1, 0)
        dnormed_ref[r] = total


def from_slabs(backward, refs):
    slab = lax.div(lax.axis_index("seq"), SLAB)
    total = jnp.zeros(refs[0].shape, F32)
    for i, ref in enumerate(refs):
        bit = lax.rem(lax.div(slab, 1 << i), 2)
        total = total + jnp.where(bit == (0 if backward else 1), ref[...].astype(F32), 0.0)
    return total


def middle_kernel(*refs):
    tokens = refs[:3]
    *before, within0, states0, within1, states1, dnormed_ref = refs[3:-6]
    withins, states = (within0, within1), (states0, states1)
    normed_ref, dmixed_ref, prior_ref, u_ref, slab_ref, running = refs[-6:]
    _, block, width = normed_ref.shape
    heads = width // DH
    for r in range(SLAB):
        running[member(r)] = states[r // 2][r % 2]
    total = from_slabs(False, before)
    for p in range(SLAB):
        total, running[p] = total + running[p], total
    sums = [jnp.zeros((DH, DH), F32)] * heads
    for r in range(SLAB):
        prior = running[member(r)].astype(BF16)
        prior_ref[r] = prior
        for h in range(heads):
            q = tokens_of(r, *tokens)[:block, head(h)]
            mixed = withins[r // 2][r % 2, :, head(h)] + dot(q, prior[:, head(h)], 1, 0)
            scale = lax.rsqrt(jnp.mean(mixed * mixed, axis=-1, keepdims=True) + EPSILON)
            normed = mixed * scale
            normed_ref[r, :, head(h)] = normed.astype(BF16)
            dnormed = dnormed_ref[r, :, head(h)]
            along = jnp.mean(dnormed * normed, axis=-1, keepdims=True)
            dmixed = ((dnormed - normed * along) * scale).astype(BF16)
            dmixed_ref[r, :, head(h)] = dmixed
            u = dot(q, dmixed, 0, 0)
            u_ref[r, :, head(h)] = u
            sums[h] = sums[h] + u
    for h in range(heads):
        slab_ref[:, head(h)] = sums[h].astype(BF16)


def late_kernel(*refs):
    tokens, (normed_ref, attend0, attend1, dmixed_ref, prior_ref, near_ref, far_ref, part_ref) = (
        refs[:3], refs[3:]
    )
    _, block, width = normed_ref.shape
    mask = causal(block)
    for r in range(SLAB):
        out = (near_ref, far_ref)[r // 2].at[part(r % 2, 2 * block)]
        token = tokens_of(r, *tokens)
        out[:block, :] = normed_ref[r]
        for h in range(width // DH):
            q, k, v = (token[part(i, block), head(h)] for i in range(3))
            dmixed = dmixed_ref[r, :, head(h)]
            back = jnp.where(mask, dot(dmixed, v, 1, 1), 0.0).astype(BF16)
            gq = dot(back, k, 1, 0) + dot(dmixed, prior_ref[r, :, head(h)], 1, 1)
            out[block:, head(h)] = gq.astype(BF16)
            part_ref[r, :block, head(h)] = dot(back, q, 0, 0)
            part_ref[r, block:, head(h)] = dot((attend0, attend1)[r // 2][r % 2, h], dmixed, 0, 0)


def last_kernel(*refs):
    tokens = refs[:3]
    *behind, u_ref, part_ref, near_ref, far_ref, running = refs[3:]
    block = part_ref.shape[1] // 2
    for r in range(SLAB):
        running[member(r)] = u_ref[r]
    total = from_slabs(True, behind)
    for p in reversed(range(SLAB)):
        total, running[p] = total + running[p], total
    for r in range(SLAB):
        out = (near_ref, far_ref)[r // 2].at[part(r % 2, 2 * block)]
        token = tokens_of(r, *tokens)
        later = running[member(r)].astype(BF16)
        for h in range(part_ref.shape[2] // DH):
            k, v = (token[part(i, block), head(h)] for i in (1, 2))
            gk = part_ref[r, :block, head(h)] + dot(v, later[:, head(h)], 1, 1)
            gv = part_ref[r, block:, head(h)] + dot(k, later[:, head(h)], 1, 0)
            out[:block, head(h)] = gk.astype(BF16)
            out[block:, head(h)] = gv.astype(BF16)


def relay_kernel(near_ref, far_ref, out_ref):
    size = near_ref.shape[0] // 2
    out_ref[:size, :] = near_ref[size:, :]
    out_ref[size:, :] = far_ref[size:, :]


def arrived(near_ref, far_ref, core_ref):
    size = near_ref.shape[0] // 2
    first, second = slice(0, size), slice(size, 2 * size)
    return near_ref.at[first], core_ref.at[first], far_ref.at[first], core_ref.at[second]


def output_kernel(groups, *refs):
    backs, own_ref = arrived(*refs[:3]), refs[3]
    far, (out_ref, gq_ref, normed_ref) = refs[4:-3], refs[-3:]
    block, width = backs[0].shape[0] // 2, backs[0].shape[1]
    rows = own_ref.shape[0]
    me = lax.axis_index("dp")
    for r in range(SLAB):
        normed_ref[:, cut(member(r), width)] = backs[r][:block, :]
        gq_ref[:, cut(member(r), width)] = backs[r][block:, :]
    out_ref[:, cut(me, rows)] = dot(normed_ref[...], own_ref[...], 1, 1).astype(BF16)
    for j in range(1, groups):
        total = jnp.zeros((block, rows), F32)
        for r in range(SLAB):
            total = total + dot(backs[r][:block, :], far[2 * (j - 1) + r % 2][r // 2], 1, 1)
        out_ref[:, cut(jnp.bitwise_xor(me, j), rows)] = total.astype(BF16)


def join_kernel(*refs):
    parts, (gk_ref, gv_ref) = arrived(*refs[:3]), refs[3:]
    block = gk_ref.shape[0]
    width = parts[0].shape[1]
    for r in range(SLAB):
        gk_ref[:, cut(member(r), width)] = parts[r][:block, :]
        gv_ref[:, cut(member(r), width)] = parts[r][block:, :]


def product_kernel(slabs, cot_ref, normed_ref, keep_ref, send_ref):
    me = lax.axis_index("dp")
    slab = lax.div(lax.axis_index("seq"), SLAB)
    rows = keep_ref.shape[0] // slabs
    for j, out in enumerate((send_ref, keep_ref)):
        for d in range(slabs):
            at = jnp.bitwise_xor(me, 1 - j) * slabs + jnp.bitwise_xor(slab, d)
            total = dot(cot_ref[0, :, cut(at, rows)], normed_ref[0], 0, 0)
            for r in range(1, SLAB):
                total = total + dot(cot_ref[r, :, cut(at, rows)], normed_ref[r], 0, 0)
            out[part(d, rows), :] = total.astype(out.dtype)


def split_kernel(own_ref, got_ref, keep_ref, send_ref):
    rows = keep_ref.shape[0] // 2
    for i in range(4):
        total = own_ref[part(i, rows), :] + got_ref[part(i, rows), :].astype(F32)
        out = (keep_ref, send_ref)[i % 2]
        out[part(i // 2, rows), :] = total.astype(out.dtype)


def split_again_kernel(own_ref, got_ref, keep_ref, send_ref):
    rows = keep_ref.shape[0]
    for i, out in enumerate((keep_ref, send_ref)):
        total = own_ref[part(i, rows), :] + got_ref[part(i, rows), :].astype(F32)
        out[...] = total.astype(out.dtype)


def share_kernel(own_ref, got_ref, keep_ref, send_ref, total_ref):
    total_ref[...] = own_ref[...] + got_ref[...].astype(F32)
    rows = keep_ref.shape[0] // 2
    for i, r in enumerate((0, 1)):
        keep_ref[part(i, rows), :] = total_ref[cut(member(r), rows), :]
    for i, r in enumerate((2, 3)):
        send_ref[part(i, rows), :] = total_ref[cut(member(r), rows), :]


def pass_kernel(own_ref, got_ref, keep_ref, send_ref):
    rows = own_ref.shape[0] // 2
    for i, ref in enumerate((own_ref, got_ref)):
        keep_ref[part(i, rows), :] = ref[:rows, :]
        send_ref[part(i, rows), :] = ref[rows:, :]


def finish_kernel(factor, keep_ref, got_ref, out_ref):
    rows, width = out_ref.shape[0], keep_ref.shape[1]
    for i, ref in enumerate((keep_ref, got_ref)):
        for j in range(2):
            out_ref[:, cut(member(i + 2 * j), width)] = ref[part(j, rows), :] * factor


def local(queries, keys, values, cotangent, out_weight, *, dp, seq):
    call = Chain()
    local_seqs, block, features = queries.shape
    outputs = cotangent.shape[2]
    rows = local_seqs * block
    slabs = seq // SLAB
    width = features // SLAB
    heads = width // DH
    q, k, v = (x.reshape(rows, features) for x in (queries, keys, values))
    cot = cotangent.reshape(rows, outputs)
    factor = 1.0 / math.sqrt(rows * dp * seq)
    near = functools.partial(flip, axis="seq", count=seq)

    def doubling(total):
        found = []
        bits = SLAB
        while bits < seq:
            if found:
                (total,) = call(add_kernel, [(total.shape, BF16)], total, found[-1])
            found.append(near(total, bits=bits))
            bits *= 2
        return found, total

    cot_y = near(cot, bits=2)
    keep, message, own_tokens, far_tokens, columns = call(
        front_kernel,
        [((2, DH, width), F32), ((2 * DH + (6 + outputs // width) * rows, width), BF16),
         ((3 * rows, width), BF16), ((3 * rows, width), BF16), ((2, out_weight.shape[0], width), BF16)],
        k, v, q, cot, out_weight, far=True,
        scratch=[pltpu.VMEM(x.shape, BF16) for x in (k, v, q, cot, out_weight)]
        + [pltpu.SemaphoreType.DMA((5,))],
    )
    message = near(message, bits=1)
    w_far = [flip(columns, "dp", dp, j) for j in range(1, dp)]
    own, send = call(halve_kernel, [((DH, width), F32), ((DH, width), BF16)], keep, message)
    got = near(send, bits=2)
    (slab_kv,) = call(add_kernel, [((DH, width), BF16)], own, got, wait=[cot_y])
    (far_tokens,) = call(pair_kernel, [((6 * rows, width), BF16)], message, far_tokens)
    far_tokens = near(far_tokens, bits=2)
    attended = [((2, heads, rows, rows), BF16), ((2, rows, width), F32), ((2, DH, width), F32)]
    attend0, within0, states0 = call(
        functools.partial(attend_kernel, True), attended, own_tokens, message
    )
    before, last_kv = doubling(slab_kv)
    cot_yc = near(after(cot_y, last_kv), bits=1)
    attend1, within1, states1 = call(functools.partial(attend_kernel, False), attended, far_tokens)
    dnormed, cots = call(
        functools.partial(dnormed_kernel, dp),
        [((SLAB, rows, width), F32), ((SLAB, rows, outputs), BF16)],
        message, cot, cot_y, cot_yc, columns, *w_far,
    )
    w_all = [x for w in w_far for x in (w, near(w, bits=1))]
    tokens = (own_tokens, message, far_tokens)
    normed, dmixed, prior, u, slab_u = call(
        middle_kernel,
        [((SLAB, rows, width), BF16), ((SLAB, rows, width), BF16), ((SLAB, DH, width), BF16),
         ((SLAB, DH, width), F32), ((DH, width), BF16)],
        *tokens, *before, within0, states0, within1, states1, dnormed,
        scratch=[pltpu.VMEM((SLAB, DH, width), F32)],
    )
    tuned = dp == 2 and slabs == 4 and outputs // (dp * seq) % 8 == 0
    if tuned:
        keep, send = call(
            functools.partial(product_kernel, slabs),
            [((outputs // dp, width), F32), ((outputs // dp, width), BF16)], cots, normed,
        )
        got = flip(send, "dp", dp, 1)
    behind, _ = doubling(slab_u)
    back, back_far, parts = call(
        late_kernel,
        [((4 * rows, width), BF16)] * 2 + [((SLAB, 2 * rows, width), F32)],
        *tokens, normed, attend0, attend1, dmixed, prior,
    )
    back_far = near(back_far, bits=2)
    if tuned:
        piece = outputs // (dp * slabs)
        keep, send = call(
            split_kernel, [((2 * piece, width), F32), ((2 * piece, width), BF16)], keep, got
        )
        got = near(send, bits=SLAB)
    grads, grads_far = call(
        last_kernel, [((4 * rows, width), BF16)] * 2, *tokens, *behind, u, parts,
        scratch=[pltpu.VMEM((SLAB, DH, width), F32)],
    )
    grads_far = near(grads_far, bits=2)
    if tuned:
        keep, send = call(
            split_again_kernel, [((piece, width), F32), ((piece, width), BF16)], keep, got
        )
        got = near(send, bits=2 * SLAB)
    if tuned:
        keep, share = call(
            share_kernel, [((piece // 2, width), F32)] * 2, keep, got,
            scratch=[pltpu.VMEM((piece, width), F32)],
        )
        got = near(share, bits=2)
    (send,) = call(relay_kernel, [((4 * rows, width), BF16)], back, back_far)
    backs = (back, back_far, near(send, bits=1))
    if tuned:
        keep, share = call(pass_kernel, [((piece // 2, width), F32)] * 2, keep, got)
        got = near(share, bits=1)
    (send,) = call(relay_kernel, [((4 * rows, width), BF16)], grads, grads_far)
    grads = (grads, grads_far, near(send, bits=1))
    output, gq, own_normed = call(
        functools.partial(output_kernel, dp),
        [((rows, outputs), BF16), ((rows, features), BF16), ((rows, features), BF16)],
        *backs, out_weight, *w_all,
    )
    gk, gv = call(join_kernel, [((rows, features), BF16)] * 2, *grads)
    if tuned:
        (grad_weight,) = call(
            functools.partial(finish_kernel, factor),
            [((piece // SLAB, features), F32)], keep, got,
        )
    else:
        partial = dot(cot, own_normed, 0, 0) * factor
        grad_weight = lax.psum_scatter(partial, ("dp", "seq"), scatter_dimension=0, tiled=True)
    shape = queries.shape
    return (
        output.reshape(cotangent.shape), gq.reshape(shape), gk.reshape(shape), gv.reshape(shape),
        grad_weight,
    )


def solution(mesh):
    dp, seq = mesh.shape["dp"], mesh.shape["seq"]
    return jax.shard_map(
        functools.partial(local, dp=dp, seq=seq),
        mesh=mesh,
        in_specs=(P("dp", "seq", None),) * 4 + (P("dp", None),),
        out_specs=(P("dp", "seq", None),) * 4 + (P(("dp", "seq"), None),),
        check_vma=False,
    )
```

time: 63.4 us -> 58.3 us (0.920)
  local copies, waits for them, and re-layouts: 5.16 us -> 0.96 us
  starting transfers between devices: 24.9 us -> 22.7 us
  Pallas kernels: 8.44 us -> 9.76 us
    unnamed x18 -> x6, local copies, waits for them, and re-layouts: 5.16 us -> 0.96 us
    ppermute x24 -> x20, starting transfers between devices: 24.9 us -> 22.7 us  [flip(): return lax.ppermute(x, axis, [(i, i ^ bits) for i in range(count)])]
    pallas_call x21 -> x22, Pallas kernels: 8.44 us -> 9.76 us  [__call__(): pl.pallas_call(inner, out_shape=[jax.ShapeDtypeStruct(s, d) for s, d in o...]
    ppermute x24 -> x20, waiting for transfers between devices: 23.8 us -> 23.9 us  [flip(): return lax.ppermute(x, axis, [(i, i ^ bits) for i in range(count)])]
  transfers between devices with their start and end apart: 24 -> 20, of which waited for: 15 -> 9; matrix products, arithmetic and copies ran while one was open for 0% -> 0% of each run, Pallas kernels for 9% -> 10%
where the time goes in v5:
time: 58.3 us; the launch traced here: 58.2 us
  waiting for transfers between devices  23.9 us (41%)
  starting transfers between devices  22.7 us (39%)
  Pallas kernels  9.76 us (17%)
  local copies, waits for them, and re-layouts  0.96 us (2%)
  between operations  0.81 us (1%)
    ppermute x20, waiting for transfers between devices, flip(): return lax.ppermute(x, axis, [(i, i ^ bits) for i in range(count)])  23.9 us
    ppermute x20, starting transfers between devices, flip(): return lax.ppermute(x, axis, [(i, i ^ bits) for i in range(count)])  22.7 us
    pallas_call x22, Pallas kernels, __call__(): pl.pallas_call(inner, out_shape=[jax.ShapeDtypeStruct(s, d) for s, d in o...  9.76 us
  transfers between devices with their start and end apart: 20, of which 9 were waited for; matrix products, arithmetic and copies ran while one was open for 0% of the time, Pallas kernels for 10%

profile of v5, /device:TPU:0, one launch (start us, length us, event | category | flops | bytes accessed | tf_op | source)
XLA Modules:
  0.0 58.2 jit_solution(11771217034303532040)
XLA Ops:
  0.6 1.7 %shard_map.92 = (f32[2,128,256]{2,1,0:T(8,128)S(1)}, bf16[1536,256]{1,0:T(8,128)(2,1)S(1)}, bf16[384,256]{1,0:T(8,128)(2,1)S(1)}, bf16[384,256]{1,0:T(8,128)(2,1)S(1)}, bf16[2,512,256]{2,1,0:T(8,128)(2,1)S(1)}) custom-call(bf16[128,1024]{1,0:T(8,128)(2,1)} %bitcast.12, bf16[128,1024]{1,0:T(8,128)(2,1)} %bitcast.13, bf16[128,1024]{1,0:T(8,128)(2,1)} %bitcast.14, ...), custom_call_target="tpu_custom_call" | custom-call | flops 1 | bytes 1 | tf_op jit(solution)/shard_map/pallas_call | solution.py:42
  2.3 0.5 collective-permute-start
  2.9 2.6 %collective-permute-start.2 = (bf16[128,1024]{1,0:T(8,128)(2,1)S(1)}, bf16[128,1024]{1,0:T(8,128)(2,1)S(1)}, u32[]{:S(2)}, u32[]{:S(2)}) collective-permute-start(bf16[128,1024]{1,0:T(8,128)(2,1)S(1)} %bitcast.9), channel_id=1, source_target_pairs={{0,2},{1,3},{2,0},{3,1},{4,6},{5,7},{6,4},{7,5},{8,10},{9,11},{10,... | collective-permute-start | bytes 786440 | tf_op jit(solution)/shard_map/ppermute | solution.py:59
  5.5 1.5 %collective-permute-start.7 = (bf16[2,512,256]{2,1,0:T(8,128)(2,1)S(1)}, bf16[2,512,256]{2,1,0:T(8,128)(2,1)S(1)}, u32[]{:S(2)}, u32[]{:S(2)}) collective-permute-start(bf16[2,512,256]{2,1,0:T(8,128)(2,1)S(1)} %get-tuple-element.50.refs_2_.refs_4_), channel_id=1, source_target_pairs={{0,16},{16,0},{1,17},{17,1},{2,18},{18,2},{3,19},{19,3},{4,20},{20... | collective-permute-start | bytes 1572872 | tf_op jit(solution)/shard_map/ppermute | solution.py:59
  7.0 0.8 %collective-permute-start.1 = (bf16[128,256]{1,0:T(8,128)(2,1)S(1)}, bf16[128,256]{1,0:T(8,128)(2,1)S(1)}, u32[]{:S(2)}, u32[]{:S(2)}) collective-permute-start(bf16[128,256]{1,0:T(8,128)(2,1)S(1)} %get-tuple-element.52.refs_2_), channel_id=1, source_target_pairs={{0,2},{1,3},{2,0},{3,1},{4,6},{5,7},{6,4},{7,5},{8,10},{9,11},{10,... | collective-permute-start | bytes 196616 | tf_op jit(solution)/shard_map/ppermute | solution.py:59
  7.8 4.9 %collective-permute-done.2.refs_3_.refs_2_ = bf16[128,1024]{1,0:T(8,128)(2,1)S(1)} collective-permute-done((bf16[128,1024]{1,0:T(8,128)(2,1)S(1)}, bf16[128,1024]{1,0:T(8,128)(2,1)S(1)}, u32[]{:S(2)}, u32[]{:S(2)}) %collective-permute-start.2) | collective-permute-done | bytes 262176 | tf_op jit(solution)/shard_map/ppermute | solution.py:59
  12.6 1.1 %collective-permute-done.1.refs_1_ = bf16[128,256]{1,0:T(8,128)(2,1)S(1)} collective-permute-done((bf16[128,256]{1,0:T(8,128)(2,1)S(1)}, bf16[128,256]{1,0:T(8,128)(2,1)S(1)}, u32[]{:S(2)}, u32[]{:S(2)}) %collective-permute-start.1) | collective-permute-done | bytes 65568 | tf_op jit(solution)/shard_map/ppermute | solution.py:59
  13.8 1.8 %collective-permute-start.3 = (bf16[768,256]{1,0:T(8,128)(2,1)S(1)}, bf16[768,256]{1,0:T(8,128)(2,1)S(1)}, u32[]{:S(2)}, u32[]{:S(2)}) collective-permute-start(bf16[768,256]{1,0:T(8,128)(2,1)S(1)} %shard_map.95.refs_2_), channel_id=1, source_target_pairs={{0,2},{1,3},{2,0},{3,1},{4,6},{5,7},{6,4},{7,5},{8,10},{9,11},{10,... | collective-permute-start | bytes 1179656 | tf_op jit(solution)/shard_map/ppermute | solution.py:59
  15.6 1.6 %collective-permute-start.4 = (bf16[128,256]{1,0:T(8,128)(2,1)S(1)}, bf16[128,256]{1,0:T(8,128)(2,1)S(1)}, u32[]{:S(2)}, u32[]{:S(2)}) collective-permute-start(bf16[128,256]{1,0:T(8,128)(2,1)S(1)} %shard_map.94.refs_2_.refs_0_), channel_id=1, source_target_pairs={{0,4},{1,5},{2,6},{3,7},{4,0},{5,1},{6,2},{7,3},{8,12},{9,13},{10,... | collective-permute-start | bytes 196616 | tf_op jit(solution)/shard_map/ppermute | solution.py:59
  17.6 2.3 %collective-permute-done.4.refs_1_.refs_3_ = bf16[128,256]{1,0:T(8,128)(2,1)S(1)} collective-permute-done((bf16[128,256]{1,0:T(8,128)(2,1)S(1)}, bf16[128,256]{1,0:T(8,128)(2,1)S(1)}, u32[]{:S(2)}, u32[]{:S(2)}) %collective-permute-start.4) | collective-permute-done | bytes 65568 | tf_op jit(solution)/shard_map/ppermute | solution.py:59
  20.0 2.7 %collective-permute-start.5 = (bf16[128,256]{1,0:T(8,128)(2,1)S(1)}, bf16[128,256]{1,0:T(8,128)(2,1)S(1)}, u32[]{:S(2)}, u32[]{:S(2)}) collective-permute-start(bf16[128,256]{1,0:T(8,128)(2,1)S(1)} %shard_map.97.refs_1_), channel_id=1, source_target_pairs={{0,8},{1,9},{2,10},{3,11},{4,12},{5,13},{6,14},{7,15},{8,0},{9,1},... | collective-permute-start | bytes 196616 | tf_op jit(solution)/shard_map/ppermute | solution.py:59
  22.7 2.1 %collective-permute-done.3.refs_0_.refs_2_ = bf16[768,256]{1,0:T(8,128)(2,1)S(1)} collective-permute-done((bf16[768,256]{1,0:T(8,128)(2,1)S(1)}, bf16[768,256]{1,0:T(8,128)(2,1)S(1)}, u32[]{:S(2)}, u32[]{:S(2)}) %collective-permute-start.3) | collective-permute-done | bytes 393248 | tf_op jit(solution)/shard_map/ppermute | solution.py:59
  25.2 0.5 shard_map.99
  25.7 1.1 %collective-permute-done.5.refs_4_ = bf16[128,256]{1,0:T(8,128)(2,1)S(1)} collective-permute-done((bf16[128,256]{1,0:T(8,128)(2,1)S(1)}, bf16[128,256]{1,0:T(8,128)(2,1)S(1)}, u32[]{:S(2)}, u32[]{:S(2)}) %collective-permute-start.5) | collective-permute-done | bytes 65568 | tf_op jit(solution)/shard_map/ppermute | solution.py:59
  26.8 0.8 %shard_map.100 = (bf16[4,128,256]{2,1,0:T(8,128)(2,1)S(1)}, bf16[4,128,256]{2,1,0:T(8,128)(2,1)S(1)}, bf16[4,128,256]{2,1,0:T(8,128)(2,1)S(1)}, f32[4,128,256]{2,1,0:T(8,128)S(1)}, bf16[128,256]{1,0:T(8,128)(2,1)S(1)}) custom-call(bf16[384,256]{1,0:T(8,128)(2,1)S(1)} %get-tuple-element.46.refs_0_, ...), custom_call_target="tpu_custom_call" | custom-call | flops 1 | bytes 1 | tf_op jit(solution)/shard_map/pallas_call | solution.py:42
  27.6 0.8 %shard_map.101 = (f32[512,256]{1,0:T(8,128)S(1)}, bf16[512,256]{1,0:T(8,128)(2,1)S(1)}) custom-call(bf16[4,128,1024]{2,1,0:T(8,128)(2,1)S(1)} %get-tuple-element.59.refs_10_.refs_0_, bf16[4,128,256]{2,1,0:T(8,128)(2,1)S(1)} %get-tuple-element.60.refs_1_.refs_3_, bf16[128,256]{1,0:T(8,128)(2,1)S(1)} %get-tuple-element.65.refs_2_.refs_0_), custom_call_target="tpu_custom_call" | custom-call | flops 1 | bytes 1 | tf_op jit(solution)/shard_map/pallas_call | solution.py:42
  28.4 1.6 %collective-permute-start.10 = (bf16[512,256]{1,0:T(8,128)(2,1)S(1)}, bf16[512,256]{1,0:T(8,128)(2,1)S(1)}, u32[]{:S(2)}, u32[]{:S(2)}) collective-permute-start(bf16[512,256]{1,0:T(8,128)(2,1)S(1)} %get-tuple-element.66.refs_2_), channel_id=1, source_target_pairs={{0,16},{16,0},{1,17},{17,1},{2,18},{18,2},{3,19},{19,3},{4,20},{20... | collective-permute-start | bytes 786440 | tf_op jit(solution)/shard_map/ppermute | solution.py:59
  29.9 0.7 %collective-permute-start.8 = (bf16[128,256]{1,0:T(8,128)(2,1)S(1)}, bf16[128,256]{1,0:T(8,128)(2,1)S(1)}, u32[]{:S(2)}, u32[]{:S(2)}) collective-permute-start(bf16[128,256]{1,0:T(8,128)(2,1)S(1)} %get-tuple-element.65.refs_2_.refs_0_), channel_id=1, source_target_pairs={{0,4},{1,5},{2,6},{3,7},{4,0},{5,1},{6,2},{7,3},{8,12},{9,13},{10,... | collective-permute-start | bytes 196616 | tf_op jit(solution)/shard_map/ppermute | solution.py:59
  30.6 3.6 %collective-permute-done.8.refs_1_.refs_3_ = bf16[128,256]{1,0:T(8,128)(2,1)S(1)} collective-permute-done((bf16[128,256]{1,0:T(8,128)(2,1)S(1)}, bf16[128,256]{1,0:T(8,128)(2,1)S(1)}, u32[]{:S(2)}, u32[]{:S(2)}) %collective-permute-start.8) | collective-permute-done | bytes 65568 | tf_op jit(solution)/shard_map/ppermute | solution.py:59
  34.2 2.1 %collective-permute-start.12 = (bf16[128,256]{1,0:T(8,128)(2,1)S(1)}, bf16[128,256]{1,0:T(8,128)(2,1)S(1)}, u32[]{:S(2)}, u32[]{:S(2)}) collective-permute-start(bf16[128,256]{1,0:T(8,128)(2,1)S(1)} %shard_map.102.refs_8_), channel_id=1, source_target_pairs={{0,8},{1,9},{2,10},{3,11},{4,12},{5,13},{6,14},{7,15},{8,0},{9,1},... | collective-permute-start | bytes 196616 | tf_op jit(solution)/shard_map/ppermute | solution.py:59
  36.3 1.4 %shard_map.103 = (bf16[512,256]{1,0:T(8,128)(2,1)S(1)}, bf16[512,256]{1,0:T(8,128)(2,1)S(1)}, f32[4,256,256]{2,1,0:T(8,128)S(1)}) custom-call(bf16[384,256]{1,0:T(8,128)(2,1)S(1)} %get-tuple-element.46.refs_0_, bf16[1536,256]{1,0:T(8,128)(2,1)S(1)} %collective-permute-done.refs_1_.refs_0_, bf16[768,256]{1,0:T(8,128)(2,1)S(1)} %collective-permute-done.3.refs_0_.refs_2_, ...), custom_call_target="tpu_custom_call" | custom-call | flops 1 | bytes 1 | tf_op jit(solution)/shard_map/pallas_call | solution.py:42
  37.8 2.1 %collective-permute-start.11 = (bf16[256,256]{1,0:T(8,128)(2,1)S(1)}, bf16[256,256]{1,0:T(8,128)(2,1)S(1)}, u32[]{:S(2)}, u32[]{:S(2)}) collective-permute-start(bf16[256,256]{1,0:T(8,128)(2,1)S(1)} %get-tuple-element.72.refs_7_), channel_id=1, source_target_pairs={{0,4},{1,5},{2,6},{3,7},{4,0},{5,1},{6,2},{7,3},{8,12},{9,13},{10,... | collective-permute-start | bytes 393224 | tf_op jit(solution)/shard_map/ppermute | solution.py:59
  39.9 0.6 collective-permute-start.9
  40.9 1.5 %collective-permute-start.16 = (bf16[512,256]{1,0:T(8,128)(2,1)S(1)}, bf16[512,256]{1,0:T(8,128)(2,1)S(1)}, u32[]{:S(2)}, u32[]{:S(2)}) collective-permute-start(bf16[512,256]{1,0:T(8,128)(2,1)S(1)} %get-tuple-element.74.refs_2_), channel_id=1, source_target_pairs={{0,2},{1,3},{2,0},{3,1},{4,6},{5,7},{6,4},{7,5},{8,10},{9,11},{10,... | collective-permute-start | bytes 786440 | tf_op jit(solution)/shard_map/ppermute | solution.py:59
  42.9 1.1 %collective-permute-start.13 = (bf16[128,256]{1,0:T(8,128)(2,1)S(1)}, bf16[128,256]{1,0:T(8,128)(2,1)S(1)}, u32[]{:S(2)}, u32[]{:S(2)}) collective-permute-start(bf16[128,256]{1,0:T(8,128)(2,1)S(1)} %get-tuple-element.76.refs_2_), channel_id=1, source_target_pairs={{0,8},{1,9},{2,10},{3,11},{4,12},{5,13},{6,14},{7,15},{8,0},{9,1},... | collective-permute-start | bytes 196616 | tf_op jit(solution)/shard_map/ppermute | solution.py:59
  43.9 4.4 %collective-permute-done.13.refs_1_ = bf16[128,256]{1,0:T(8,128)(2,1)S(1)} collective-permute-done((bf16[128,256]{1,0:T(8,128)(2,1)S(1)}, bf16[128,256]{1,0:T(8,128)(2,1)S(1)}, u32[]{:S(2)}, u32[]{:S(2)}) %collective-permute-start.13) | collective-permute-done | bytes 65568 | tf_op jit(solution)/shard_map/ppermute | solution.py:59
  48.3 1.0 %collective-permute-start.17 = (f32[64,256]{1,0:T(8,128)S(1)}, f32[64,256]{1,0:T(8,128)S(1)}, u32[]{:S(2)}, u32[]{:S(2)}) collective-permute-start(f32[64,256]{1,0:T(8,128)S(1)} %get-tuple-element.77.refs_2_), channel_id=1, source_target_pairs={{0,2},{1,3},{2,0},{3,1},{4,6},{5,7},{6,4},{7,5},{8,10},{9,11},{10,... | collective-permute-start | bytes 196616 | tf_op jit(solution)/shard_map/ppermute | solution.py:59
  49.4 4.1 %collective-permute-done.17.refs_1_ = f32[64,256]{1,0:T(8,128)S(1)} collective-permute-done((f32[64,256]{1,0:T(8,128)S(1)}, f32[64,256]{1,0:T(8,128)S(1)}, u32[]{:S(2)}, u32[]{:S(2)}) %collective-permute-start.17) | collective-permute-done | bytes 65568 | tf_op jit(solution)/shard_map/ppermute | solution.py:59
  54.1 1.6 %shard_map.111 = (bf16[128,1024]{1,0:T(8,128)(2,1)}, bf16[128,1024]{1,0:T(8,128)(2,1)}, bf16[128,1024]{1,0:T(8,128)(2,1)S(1)}) custom-call(bf16[512,256]{1,0:T(8,128)(2,1)S(1)} %get-tuple-element.67.refs_0_, bf16[512,256]{1,0:T(8,128)(2,1)S(1)} %collective-permute-done.9.refs_1_, bf16[512,256]{1,0:T(8,128)(2,1)S(1)} %collective-permute-done.14.refs_2_, ...), custom_call_target="tpu_custom_call" | custom-call | flops 1 | bytes 1 | tf_op jit(solution)/shard_map/pallas_call | solution.py:42
  55.7 0.8 %shard_map.112 = (bf16[128,1024]{1,0:T(8,128)(2,1)}, bf16[128,1024]{1,0:T(8,128)(2,1)}) custom-call(bf16[512,256]{1,0:T(8,128)(2,1)S(1)} %get-tuple-element.78.refs_0_, bf16[512,256]{1,0:T(8,128)(2,1)S(1)} %collective-permute-done.16.refs_1_, bf16[512,256]{1,0:T(8,128)(2,1)S(1)} %collective-permute-done.18.refs_2_, ...), custom_call_target="tpu_custom_call" | custom-call | flops 1 | bytes 1 | tf_op jit(solution)/shard_map/pallas_call | solution.py:42
  56.5 0.9 %copy-done.2 = bf16[128,1024]{1,0:T(8,128)(2,1)S(1)} copy-done((bf16[128,1024]{1,0:T(8,128)(2,1)S(1)}, bf16[128,1024]{1,0:T(8,128)(2,1)}, u32[]{:S(2)}) %copy-start.2) | copy-done | bytes 262168
  57.5 0.7 %shard_map.113 = f32[32,1024]{1,0:T(8,128)} custom-call(f32[64,256]{1,0:T(8,128)S(1)} %get-tuple-element.86.refs_0_, f32[64,256]{1,0:T(8,128)S(1)} %collective-permute-done.19.refs_1_, bf16[128,1024]{1,0:T(8,128)(2,1)S(1)} %copy-done.2), custom_call_target="tpu_custom_call" | custom-call | flops 1 | bytes 1 | tf_op jit(solution)/shard_map/pallas_call | solution.py:42
  (36 shorter events, 2.7 us)
Async XLA Ops:
  0.6 2.2 %copy-start.1 = (bf16[1,128,1024]{2,1,0:T(8,128)(2,1)S(1)}, bf16[1,128,1024]{2,1,0:T(8,128)(2,1)}, u32[]{:S(2)}) copy-start(bf16[1,128,1024]{2,1,0:T(8,128)(2,1)} %param.8) | copy-start | bytes 786436
  2.3 4.6 %collective-permute-start = (bf16[1536,256]{1,0:T(8,128)(2,1)S(1)}, bf16[1536,256]{1,0:T(8,128)(2,1)S(1)}, u32[]{:S(2)}, u32[]{:S(2)}) collective-permute-start(bf16[1536,256]{1,0:T(8,128)(2,1)S(1)} %get-tuple-element.47), channel_id=1, source_target_pairs={{0,1},{1,0},{2,3},{3,2},{4,5},{5,4},{6,7},{7,6},{8,9},{9,8},{10,11... | collective-permute-start | bytes 2359304 | tf_op jit(solution)/shard_map/ppermute | solution.py:59
  2.9 9.8 %collective-permute-start.2 = (bf16[128,1024]{1,0:T(8,128)(2,1)S(1)}, bf16[128,1024]{1,0:T(8,128)(2,1)S(1)}, u32[]{:S(2)}, u32[]{:S(2)}) collective-permute-start(bf16[128,1024]{1,0:T(8,128)(2,1)S(1)} %bitcast.9), channel_id=1, source_target_pairs={{0,2},{1,3},{2,0},{3,1},{4,6},{5,7},{6,4},{7,5},{8,10},{9,11},{10,... | collective-permute-start | bytes 786440 | tf_op jit(solution)/shard_map/ppermute | solution.py:59
  5.5 19.7 %collective-permute-start.7 = (bf16[2,512,256]{2,1,0:T(8,128)(2,1)S(1)}, bf16[2,512,256]{2,1,0:T(8,128)(2,1)S(1)}, u32[]{:S(2)}, u32[]{:S(2)}) collective-permute-start(bf16[2,512,256]{2,1,0:T(8,128)(2,1)S(1)} %get-tuple-element.50.refs_2_.refs_4_), channel_id=1, source_target_pairs={{0,16},{16,0},{1,17},{17,1},{2,18},{18,2},{3,19},{19,3},{4,20},{20... | collective-permute-start | bytes 1572872 | tf_op jit(solution)/shard_map/ppermute | solution.py:59
  7.0 6.8 %collective-permute-start.1 = (bf16[128,256]{1,0:T(8,128)(2,1)S(1)}, bf16[128,256]{1,0:T(8,128)(2,1)S(1)}, u32[]{:S(2)}, u32[]{:S(2)}) collective-permute-start(bf16[128,256]{1,0:T(8,128)(2,1)S(1)} %get-tuple-element.52.refs_2_), channel_id=1, source_target_pairs={{0,2},{1,3},{2,0},{3,1},{4,6},{5,7},{6,4},{7,5},{8,10},{9,11},{10,... | collective-permute-start | bytes 196616 | tf_op jit(solution)/shard_map/ppermute | solution.py:59
  13.8 10.9 %collective-permute-start.3 = (bf16[768,256]{1,0:T(8,128)(2,1)S(1)}, bf16[768,256]{1,0:T(8,128)(2,1)S(1)}, u32[]{:S(2)}, u32[]{:S(2)}) collective-permute-start(bf16[768,256]{1,0:T(8,128)(2,1)S(1)} %shard_map.95.refs_2_), channel_id=1, source_target_pairs={{0,2},{1,3},{2,0},{3,1},{4,6},{5,7},{6,4},{7,5},{8,10},{9,11},{10,... | collective-permute-start | bytes 1179656 | tf_op jit(solution)/shard_map/ppermute | solution.py:59
  15.6 4.3 %collective-permute-start.4 = (bf16[128,256]{1,0:T(8,128)(2,1)S(1)}, bf16[128,256]{1,0:T(8,128)(2,1)S(1)}, u32[]{:S(2)}, u32[]{:S(2)}) collective-permute-start(bf16[128,256]{1,0:T(8,128)(2,1)S(1)} %shard_map.94.refs_2_.refs_0_), channel_id=1, source_target_pairs={{0,4},{1,5},{2,6},{3,7},{4,0},{5,1},{6,2},{7,3},{8,12},{9,13},{10,... | collective-permute-start | bytes 196616 | tf_op jit(solution)/shard_map/ppermute | solution.py:59
  19.9 5.2 %collective-permute-start.6 = (bf16[128,1024]{1,0:T(8,128)(2,1)S(1)}, bf16[128,1024]{1,0:T(8,128)(2,1)S(1)}, u32[]{:S(2)}, u32[]{:S(2)}) collective-permute-start(bf16[128,1024]{1,0:T(8,128)(2,1)S(1)} %collective-permute-done.2.refs_3_.refs_2_), channel_id=1, source_target_pairs={{0,1},{1,0},{2,3},{3,2},{4,5},{5,4},{6,7},{7,6},{8,9},{9,8},{10,11... | collective-permute-start | bytes 786440 | tf_op jit(solution)/shard_map/ppermute | solution.py:59
  20.0 6.8 %collective-permute-start.5 = (bf16[128,256]{1,0:T(8,128)(2,1)S(1)}, bf16[128,256]{1,0:T(8,128)(2,1)S(1)}, u32[]{:S(2)}, u32[]{:S(2)}) collective-permute-start(bf16[128,256]{1,0:T(8,128)(2,1)S(1)} %shard_map.97.refs_1_), channel_id=1, source_target_pairs={{0,8},{1,9},{2,10},{3,11},{4,12},{5,13},{6,14},{7,15},{8,0},{9,1},... | collective-permute-start | bytes 196616 | tf_op jit(solution)/shard_map/ppermute | solution.py:59
  28.4 9.4 %collective-permute-start.10 = (bf16[512,256]{1,0:T(8,128)(2,1)S(1)}, bf16[512,256]{1,0:T(8,128)(2,1)S(1)}, u32[]{:S(2)}, u32[]{:S(2)}) collective-permute-start(bf16[512,256]{1,0:T(8,128)(2,1)S(1)} %get-tuple-element.66.refs_2_), channel_id=1, source_target_pairs={{0,16},{16,0},{1,17},{17,1},{2,18},{18,2},{3,19},{19,3},{4,20},{20... | collective-permute-start | bytes 786440 | tf_op jit(solution)/shard_map/ppermute | solution.py:59
  29.9 4.3 %collective-permute-start.8 = (bf16[128,256]{1,0:T(8,128)(2,1)S(1)}, bf16[128,256]{1,0:T(8,128)(2,1)S(1)}, u32[]{:S(2)}, u32[]{:S(2)}) collective-permute-start(bf16[128,256]{1,0:T(8,128)(2,1)S(1)} %get-tuple-element.65.refs_2_.refs_0_), channel_id=1, source_target_pairs={{0,4},{1,5},{2,6},{3,7},{4,0},{5,1},{6,2},{7,3},{8,12},{9,13},{10,... | collective-permute-start | bytes 196616 | tf_op jit(solution)/shard_map/ppermute | solution.py:59
  34.2 6.2 %collective-permute-start.12 = (bf16[128,256]{1,0:T(8,128)(2,1)S(1)}, bf16[128,256]{1,0:T(8,128)(2,1)S(1)}, u32[]{:S(2)}, u32[]{:S(2)}) collective-permute-start(bf16[128,256]{1,0:T(8,128)(2,1)S(1)} %shard_map.102.refs_8_), channel_id=1, source_target_pairs={{0,8},{1,9},{2,10},{3,11},{4,12},{5,13},{6,14},{7,15},{8,0},{9,1},... | collective-permute-start | bytes 196616 | tf_op jit(solution)/shard_map/ppermute | solution.py:59
  37.8 5.0 %collective-permute-start.11 = (bf16[256,256]{1,0:T(8,128)(2,1)S(1)}, bf16[256,256]{1,0:T(8,128)(2,1)S(1)}, u32[]{:S(2)}, u32[]{:S(2)}) collective-permute-start(bf16[256,256]{1,0:T(8,128)(2,1)S(1)} %get-tuple-element.72.refs_7_), channel_id=1, source_target_pairs={{0,4},{1,5},{2,6},{3,7},{4,0},{5,1},{6,2},{7,3},{8,12},{9,13},{10,... | collective-permute-start | bytes 393224 | tf_op jit(solution)/shard_map/ppermute | solution.py:59
  39.9 9.4 %collective-permute-start.9 = (bf16[512,256]{1,0:T(8,128)(2,1)S(1)}, bf16[512,256]{1,0:T(8,128)(2,1)S(1)}, u32[]{:S(2)}, u32[]{:S(2)}) collective-permute-start(bf16[512,256]{1,0:T(8,128)(2,1)S(1)} %get-tuple-element.68), channel_id=1, source_target_pairs={{0,2},{1,3},{2,0},{3,1},{4,6},{5,7},{6,4},{7,5},{8,10},{9,11},{10,... | collective-permute-start | bytes 786440 | tf_op jit(solution)/shard_map/ppermute | solution.py:59
  40.9 12.6 %collective-permute-start.16 = (bf16[512,256]{1,0:T(8,128)(2,1)S(1)}, bf16[512,256]{1,0:T(8,128)(2,1)S(1)}, u32[]{:S(2)}, u32[]{:S(2)}) collective-permute-start(bf16[512,256]{1,0:T(8,128)(2,1)S(1)} %get-tuple-element.74.refs_2_), channel_id=1, source_target_pairs={{0,2},{1,3},{2,0},{3,1},{4,6},{5,7},{6,4},{7,5},{8,10},{9,11},{10,... | collective-permute-start | bytes 786440 | tf_op jit(solution)/shard_map/ppermute | solution.py:59
  42.5 11.7 %collective-permute-start.15 = (bf16[2,512,256]{2,1,0:T(8,128)(2,1)S(1)}, bf16[2,512,256]{2,1,0:T(8,128)(2,1)S(1)}, u32[]{:S(2)}, u32[]{:S(2)}) collective-permute-start(bf16[2,512,256]{2,1,0:T(8,128)(2,1)S(1)} %collective-permute-done.7.refs_5_.refs_4_), channel_id=1, source_target_pairs={{0,1},{1,0},{2,3},{3,2},{4,5},{5,4},{6,7},{7,6},{8,9},{9,8},{10,11... | collective-permute-start | bytes 1572872 | tf_op jit(solution)/shard_map/ppermute | solution.py:59
  42.9 5.4 %collective-permute-start.13 = (bf16[128,256]{1,0:T(8,128)(2,1)S(1)}, bf16[128,256]{1,0:T(8,128)(2,1)S(1)}, u32[]{:S(2)}, u32[]{:S(2)}) collective-permute-start(bf16[128,256]{1,0:T(8,128)(2,1)S(1)} %get-tuple-element.76.refs_2_), channel_id=1, source_target_pairs={{0,8},{1,9},{2,10},{3,11},{4,12},{5,13},{6,14},{7,15},{8,0},{9,1},... | collective-permute-start | bytes 196616 | tf_op jit(solution)/shard_map/ppermute | solution.py:59
  48.3 5.2 %collective-permute-start.17 = (f32[64,256]{1,0:T(8,128)S(1)}, f32[64,256]{1,0:T(8,128)S(1)}, u32[]{:S(2)}, u32[]{:S(2)}) collective-permute-start(f32[64,256]{1,0:T(8,128)S(1)} %get-tuple-element.77.refs_2_), channel_id=1, source_target_pairs={{0,2},{1,3},{2,0},{3,1},{4,6},{5,7},{6,4},{7,5},{8,10},{9,11},{10,... | collective-permute-start | bytes 196616 | tf_op jit(solution)/shard_map/ppermute | solution.py:59
  49.3 4.8 %copy-start = (bf16[512,1024]{1,0:T(8,128)(2,1)S(1)}, bf16[512,1024]{1,0:T(8,128)(2,1)}, u32[]{:S(2)}) copy-start(bf16[512,1024]{1,0:T(8,128)(2,1)} %refs_3_.1) | copy-start | bytes 3145732
  49.4 4.8 %collective-permute-start.14 = (bf16[512,256]{1,0:T(8,128)(2,1)S(1)}, bf16[512,256]{1,0:T(8,128)(2,1)S(1)}, u32[]{:S(2)}, u32[]{:S(2)}) collective-permute-start(bf16[512,256]{1,0:T(8,128)(2,1)S(1)} %shard_map.108.refs_2_), channel_id=1, source_target_pairs={{0,1},{1,0},{2,3},{3,2},{4,5},{5,4},{6,7},{7,6},{8,9},{9,8},{10,11... | collective-permute-start | bytes 786440 | tf_op jit(solution)/shard_map/ppermute | solution.py:59
  53.6 2.1 %collective-permute-start.18 = (bf16[512,256]{1,0:T(8,128)(2,1)S(1)}, bf16[512,256]{1,0:T(8,128)(2,1)S(1)}, u32[]{:S(2)}, u32[]{:S(2)}) collective-permute-start(bf16[512,256]{1,0:T(8,128)(2,1)S(1)} %shard_map.110.refs_6_), channel_id=1, source_target_pairs={{0,1},{1,0},{2,3},{3,2},{4,5},{5,4},{6,7},{7,6},{8,9},{9,8},{10,11... | collective-permute-start | bytes 786440 | tf_op jit(solution)/shard_map/ppermute | solution.py:59
  53.6 2.9 %collective-permute-start.19 = (f32[64,256]{1,0:T(8,128)S(1)}, f32[64,256]{1,0:T(8,128)S(1)}, u32[]{:S(2)}, u32[]{:S(2)}) collective-permute-start(f32[64,256]{1,0:T(8,128)S(1)} %get-tuple-element.80.refs_2_), channel_id=1, source_target_pairs={{0,1},{1,0},{2,3},{3,2},{4,5},{5,4},{6,7},{7,6},{8,9},{9,8},{10,11... | collective-permute-start | bytes 196616 | tf_op jit(solution)/shard_map/ppermute | solution.py:59
  56.5 1.0 %copy-start.2 = (bf16[128,1024]{1,0:T(8,128)(2,1)S(1)}, bf16[128,1024]{1,0:T(8,128)(2,1)}, u32[]{:S(2)}) copy-start(bf16[128,1024]{1,0:T(8,128)(2,1)} %get-tuple-element.85.refs_2_) | copy-start | bytes 786436

commit v6 on v5

--- a/solution.py
+++ b/solution.py
@@ -25,7 +25,7 @@
     def __init__(self):
         self.last = None
 
-    def __call__(self, body, outs, *args, scratch=(), far=False, wait=()):
+    def __call__(self, body, outs, *args, scratch=(), far=False, wait=(), cost=1, end=False):
         count = len(args)
         if far:
             args = [pltpu.with_memory_space_constraint(x, pltpu.HBM) for x in args]
@@ -44,10 +44,11 @@
             out_shape=[jax.ShapeDtypeStruct(s, d) for s, d in outs],
             in_specs=specs,
             scratch_shapes=list(scratch),
-            cost_estimate=pl.CostEstimate(flops=1, bytes_accessed=1, transcendentals=0),
+            cost_estimate=pl.CostEstimate(flops=cost, bytes_accessed=1, transcendentals=0),
             compiler_params=pltpu.CompilerParams(vmem_limit_bytes=32 * 2**20),
         )(*args)
-        self.last = found[-1]
+        if not end:
+            self.last = min(reversed(found), key=lambda x: x.size)
         return found
 
 
@@ -88,8 +89,8 @@
 
 
 def front_kernel(k_hbm, v_hbm, q_hbm, c_hbm, w_hbm, *refs):
-    keep_ref, message_ref, own_ref, far_ref, columns_ref = refs[:5]
-    k_ref, v_ref, q_ref, c_ref, w_ref, sems = refs[5:]
+    keep_ref, states_ref, message_ref, own_ref, far_ref, columns_ref = refs[:6]
+    k_ref, v_ref, q_ref, c_ref, w_ref, sems = refs[6:]
     copies = fetch(
         [(k_hbm, k_ref), (v_hbm, v_ref), (q_hbm, q_ref), (c_hbm, c_ref), (w_hbm, w_ref)], sems
     )
@@ -101,18 +102,18 @@
         k, v = k_ref[:, cut(member(r), width)], v_ref[:, cut(member(r), width)]
         for h in range(width // DH):
             state = dot(k[:, head(h)], v[:, head(h)], 0, 0)
-            if r % 2:
-                message_ref[part(r // 2, DH), head(h)] = state.astype(BF16)
+            if r < 2:
+                keep_ref[r, :, head(h)] = state
             else:
-                keep_ref[r // 2, :, head(h)] = state
+                states_ref[part(r - 2, DH), head(h)] = state.astype(BF16)
     copies[2].wait()
-    places = ((own_ref, 0), (message_ref, 2 * DH), (far_ref, 0), (message_ref, 2 * DH + 3 * block))
+    places = ((own_ref, 0), (message_ref, 0), (far_ref, 0), (message_ref, 3 * block))
     for r, (out, at) in enumerate(places):
         for i, ref in enumerate((q_ref, k_ref, v_ref)):
             out[at + i * block : at + (i + 1) * block, :] = ref[:, cut(member(r), width)]
     copies[3].wait()
     for i in range(c_ref.shape[1] // width):
-        message_ref[2 * DH + (6 + i) * block : 2 * DH + (7 + i) * block, :] = c_ref[:, part(i, width)]
+        message_ref[part(6 + i, block), :] = c_ref[:, part(i, width)]
     copies[4].wait()
     for i in range(2):
         columns_ref[i] = w_ref[:, cut(member(2 * i), width)]
@@ -126,7 +127,7 @@
 def pair_kernel(message_ref, far_ref, out_ref):
     size = far_ref.shape[0]
     out_ref[:size, :] = far_ref[...]
-    out_ref[size:, :] = message_ref[2 * DH + size : 2 * DH + 2 * size, :]
+    out_ref[size:, :] = message_ref[part(1, size), :]
 
 
 def add_kernel(own_ref, got_ref, out_ref):
@@ -138,7 +139,7 @@
     if r == 0:
         return own_ref
     if r == 1:
-        return message_ref.at[2 * DH : 2 * DH + size]
+        return message_ref.at[:size]
     return far_ref.at[(r - 2) * size : (r - 1) * size]
 
 
@@ -166,9 +167,8 @@
     width = dnormed_ref.shape[2]
     rows = weights[0].shape[1]
     me = lax.axis_index("dp")
-    at = 2 * DH + 6 * block
     for i in range(outputs // width):
-        cot_ref[1, :, part(i, width)] = message_ref[at + i * block : at + (i + 1) * block, :]
+        cot_ref[1, :, part(i, width)] = message_ref[part(6 + i, block), :]
     for r, ref in zip((0, 2, 3), cots):
         cot_ref[r] = ref[...]
     for r in range(SLAB):
@@ -221,13 +221,11 @@
 
 
 def late_kernel(*refs):
-    tokens, (normed_ref, attend0, attend1, dmixed_ref, prior_ref, near_ref, far_ref, part_ref) = (
-        refs[:3], refs[3:]
-    )
+    tokens, (normed_ref, attend0, attend1, dmixed_ref, prior_ref, *outs, part_ref) = refs[:3], refs[3:]
     _, block, width = normed_ref.shape
     mask = causal(block)
     for r in range(SLAB):
-        out = (near_ref, far_ref)[r // 2].at[part(r % 2, 2 * block)]
+        out = outs[r]
         token = tokens_of(r, *tokens)
         out[:block, :] = normed_ref[r]
         for h in range(width // DH):
@@ -242,7 +240,8 @@
 
 def last_kernel(*refs):
     tokens = refs[:3]
-    *behind, u_ref, part_ref, near_ref, far_ref, running = refs[3:]
+    *behind, u_ref, part_ref = refs[3 : -(SLAB + 1)]
+    outs, running = refs[-(SLAB + 1) : -1], refs[-1]
     block = part_ref.shape[1] // 2
     for r in range(SLAB):
         running[member(r)] = u_ref[r]
@@ -250,7 +249,7 @@
     for p in reversed(range(SLAB)):
         total, running[p] = total + running[p], total
     for r in range(SLAB):
-        out = (near_ref, far_ref)[r // 2].at[part(r % 2, 2 * block)]
+        out = outs[r]
         token = tokens_of(r, *tokens)
         later = running[member(r)].astype(BF16)
         for h in range(part_ref.shape[2] // DH):
@@ -261,21 +260,9 @@
             out[block:, head(h)] = gv.astype(BF16)
 
 
-def relay_kernel(near_ref, far_ref, out_ref):
-    size = near_ref.shape[0] // 2
-    out_ref[:size, :] = near_ref[size:, :]
-    out_ref[size:, :] = far_ref[size:, :]
-
-
-def arrived(near_ref, far_ref, core_ref):
-    size = near_ref.shape[0] // 2
-    first, second = slice(0, size), slice(size, 2 * size)
-    return near_ref.at[first], core_ref.at[first], far_ref.at[first], core_ref.at[second]
-
-
 def output_kernel(groups, *refs):
-    backs, own_ref = arrived(*refs[:3]), refs[3]
-    far, (out_ref, gq_ref, normed_ref) = refs[4:-3], refs[-3:]
+    backs, own_ref = refs[:SLAB], refs[SLAB]
+    far, (out_ref, gq_ref, normed_ref) = refs[SLAB + 1 : -3], refs[-3:]
     block, width = backs[0].shape[0] // 2, backs[0].shape[1]
     rows = own_ref.shape[0]
     me = lax.axis_index("dp")
@@ -291,7 +278,7 @@
 
 
 def join_kernel(*refs):
-    parts, (gk_ref, gv_ref) = arrived(*refs[:3]), refs[3:]
+    parts, (gk_ref, gv_ref) = refs[:SLAB], refs[SLAB:]
     block = gk_ref.shape[0]
     width = parts[0].shape[1]
     for r in range(SLAB):
@@ -363,102 +350,105 @@
     factor = 1.0 / math.sqrt(rows * dp * seq)
     near = functools.partial(flip, axis="seq", count=seq)
 
-    def doubling(total):
+    def spread(parts, *first):
+        found = {r: near(after(parts[r], *first), bits=r) for r in (2, 3, 1)}
+        return [parts[0], found[1], found[2], found[3]]
+
+    def doubling(total, cost=1):
         found = []
         bits = SLAB
         while bits < seq:
             if found:
-                (total,) = call(add_kernel, [(total.shape, BF16)], total, found[-1])
+                (total,) = call(add_kernel, [(total.shape, BF16)], total, found[-1], cost=cost)
             found.append(near(total, bits=bits))
             bits *= 2
         return found, total
 
     cot_y = near(cot, bits=2)
-    keep, message, own_tokens, far_tokens, columns = call(
+    keep, send, message, own_tokens, far_tokens, columns = call(
         front_kernel,
-        [((2, DH, width), F32), ((2 * DH + (6 + outputs // width) * rows, width), BF16),
+        [((2, DH, width), F32), ((2 * DH, width), BF16), (((6 + outputs // width) * rows, width), BF16),
          ((3 * rows, width), BF16), ((3 * rows, width), BF16), ((2, out_weight.shape[0], width), BF16)],
         k, v, q, cot, out_weight, far=True,
         scratch=[pltpu.VMEM(x.shape, BF16) for x in (k, v, q, cot, out_weight)]
         + [pltpu.SemaphoreType.DMA((5,))],
     )
+    got = near(send, bits=2)
     message = near(message, bits=1)
     w_far = [flip(columns, "dp", dp, j) for j in range(1, dp)]
-    own, send = call(halve_kernel, [((DH, width), F32), ((DH, width), BF16)], keep, message)
-    got = near(send, bits=2)
-    (slab_kv,) = call(add_kernel, [((DH, width), BF16)], own, got, wait=[cot_y])
+    own, send = call(
+        halve_kernel, [((DH, width), F32), ((DH, width), BF16)], keep, got, cost=10**10
+    )
+    got = near(send, bits=1)
+    (slab_kv,) = call(add_kernel, [((DH, width), BF16)], own, got)
     (far_tokens,) = call(pair_kernel, [((6 * rows, width), BF16)], message, far_tokens)
     far_tokens = near(far_tokens, bits=2)
     attended = [((2, heads, rows, rows), BF16), ((2, rows, width), F32), ((2, DH, width), F32)]
     attend0, within0, states0 = call(
         functools.partial(attend_kernel, True), attended, own_tokens, message
     )
-    before, last_kv = doubling(slab_kv)
-    cot_yc = near(after(cot_y, last_kv), bits=1)
+    cot_yc = near(after(cot_y, within0), bits=1)
+    before, _ = doubling(slab_kv, 3 * 10**9)
     attend1, within1, states1 = call(functools.partial(attend_kernel, False), attended, far_tokens)
     dnormed, cots = call(
         functools.partial(dnormed_kernel, dp),
         [((SLAB, rows, width), F32), ((SLAB, rows, outputs), BF16)],
         message, cot, cot_y, cot_yc, columns, *w_far,
     )
-    w_all = [x for w in w_far for x in (w, near(w, bits=1))]
+    w_all = [x for w in w_far for x in (w, near(after(w, within1), bits=1))]
     tokens = (own_tokens, message, far_tokens)
     normed, dmixed, prior, u, slab_u = call(
         middle_kernel,
         [((SLAB, rows, width), BF16), ((SLAB, rows, width), BF16), ((SLAB, DH, width), BF16),
          ((SLAB, DH, width), F32), ((DH, width), BF16)],
-        *tokens, *before, within0, states0, within1, states1, dnormed,
+        *tokens, *before, within0, states0, within1, states1, dnormed, cost=10**10,
         scratch=[pltpu.VMEM((SLAB, DH, width), F32)],
     )
     tuned = dp == 2 and slabs == 4 and outputs // (dp * seq) % 8 == 0
     if tuned:
         keep, send = call(
             functools.partial(product_kernel, slabs),
-            [((outputs // dp, width), F32), ((outputs // dp, width), BF16)], cots, normed,
+            [((outputs // dp, width), F32), ((outputs // dp, width), BF16)], cots, normed, wait=w_all[1::2],
         )
         got = flip(send, "dp", dp, 1)
-    behind, _ = doubling(slab_u)
-    back, back_far, parts = call(
+    *backs, parts = call(
         late_kernel,
-        [((4 * rows, width), BF16)] * 2 + [((SLAB, 2 * rows, width), F32)],
+        [((2 * rows, width), BF16)] * SLAB + [((SLAB, 2 * rows, width), F32)],
         *tokens, normed, attend0, attend1, dmixed, prior,
     )
-    back_far = near(back_far, bits=2)
+    behind, last_u = doubling(slab_u)
+    backs = spread(backs, last_u)
     if tuned:
         piece = outputs // (dp * slabs)
         keep, send = call(
-            split_kernel, [((2 * piece, width), F32), ((2 * piece, width), BF16)], keep, got
+            split_kernel, [((2 * piece, width), F32), ((2 * piece, width), BF16)], keep, got, cost=1
         )
         got = near(send, bits=SLAB)
-    grads, grads_far = call(
-        last_kernel, [((4 * rows, width), BF16)] * 2, *tokens, *behind, u, parts,
+    grads = call(
+        last_kernel, [((2 * rows, width), BF16)] * SLAB, *tokens, *behind, u, parts, cost=3 * 10**9,
         scratch=[pltpu.VMEM((SLAB, DH, width), F32)],
     )
-    grads_far = near(grads_far, bits=2)
     if tuned:
         keep, send = call(
-            split_again_kernel, [((piece, width), F32), ((piece, width), BF16)], keep, got
+            split_again_kernel, [((piece, width), F32), ((piece, width), BF16)], keep, got, cost=1
         )
         got = near(send, bits=2 * SLAB)
+    grads = spread(grads, keep)
+    output, gq, own_normed = call(
+        functools.partial(output_kernel, dp),
+        [((rows, outputs), BF16), ((rows, features), BF16), ((rows, features), BF16)],
+        *backs, out_weight, *w_all,
+    )
     if tuned:
         keep, share = call(
             share_kernel, [((piece // 2, width), F32)] * 2, keep, got,
             scratch=[pltpu.VMEM((piece, width), F32)],
         )
         got = near(share, bits=2)
-    (send,) = call(relay_kernel, [((4 * rows, width), BF16)], back, back_far)
-    backs = (back, back_far, near(send, bits=1))
     if tuned:
         keep, share = call(pass_kernel, [((piece // 2, width), F32)] * 2, keep, got)
         got = near(share, bits=1)
-    (send,) = call(relay_kernel, [((4 * rows, width), BF16)], grads, grads_far)
-    grads = (grads, grads_far, near(send, bits=1))
-    output, gq, own_normed = call(
-        functools.partial(output_kernel, dp),
-        [((rows, outputs), BF16), ((rows, features), BF16), ((rows, features), BF16)],
-        *backs, out_weight, *w_all,
-    )
-    gk, gv = call(join_kernel, [((rows, features), BF16)] * 2, *grads)
+    gk, gv = call(join_kernel, [((rows, features), BF16)] * 2, *grads, end=True)
     if tuned:
         (grad_weight,) = call(
             functools.partial(finish_kernel, factor),

time: 58.3 us -> 56 us (0.961)
  local copies, waits for them, and re-layouts: 0.96 us -> 0.01 us
  waiting for transfers between devices: 23.9 us -> 23 us
    unnamed x6 -> x4, local copies, waits for them, and re-layouts: 0.96 us -> 0.01 us
    ppermute x20 -> x23, waiting for transfers between devices: 23.9 us -> 23 us  [flip(): return lax.ppermute(x, axis, [(i, i ^ bits) for i in range(count)])]
    ppermute x20 -> x23, starting transfers between devices: 22.7 us -> 22.2 us  [flip(): return lax.ppermute(x, axis, [(i, i ^ bits) for i in range(count)])]
    pallas_call x22 -> x20, Pallas kernels: 9.76 us -> 9.72 us  [__call__(): pl.pallas_call(inner, out_shape=[jax.ShapeDtypeStruct(s, d) for s, d in o...]
  transfers between devices with their start and end apart: 20 -> 23, of which waited for: 9 -> 11; matrix products, arithmetic and copies ran while one was open for 0% -> 0% of each run, Pallas kernels for 10% -> 12%
where the time goes in v6:
time: 56 us; the launch traced here: 55.8 us
  waiting for transfers between devices  23 us (41%)
  starting transfers between devices  22.2 us (40%)
  Pallas kernels  9.72 us (17%)
  between operations  0.83 us (1%)
    ppermute x23, waiting for transfers between devices, flip(): return lax.ppermute(x, axis, [(i, i ^ bits) for i in range(count)])  23 us
    ppermute x23, starting transfers between devices, flip(): return lax.ppermute(x, axis, [(i, i ^ bits) for i in range(count)])  22.2 us
    pallas_call x20, Pallas kernels, __call__(): pl.pallas_call(inner, out_shape=[jax.ShapeDtypeStruct(s, d) for s, d in o...  9.72 us
  transfers between devices with their start and end apart: 23, of which 11 were waited for; matrix products, arithmetic and copies ran while one was open for 0% of the time, Pallas kernels for 12%

profile of v6, /device:TPU:0, one launch (start us, length us, event | category | flops | bytes accessed | tf_op | source)
XLA Modules:
  0.0 55.8 jit_solution(8552194930146862942)
XLA Ops:
  0.6 1.7 %shard_map.92 = (f32[2,128,256]{2,1,0:T(8,128)S(1)}, bf16[256,256]{1,0:T(8,128)(2,1)S(1)}, bf16[1280,256]{1,0:T(8,128)(2,1)S(1)}, bf16[384,256]{1,0:T(8,128)(2,1...) custom-call(bf16[128,1024]{1,0:T(8,128)(2,1)} %bitcast.11, bf16[128,1024]{1,0:T(8,128)(2,1)} %bitcast.12, ...), custom_call_target="tpu_custom_call" | custom-call | flops 1 | bytes 1 | tf_op jit(solution)/shard_map/pallas_call | solution.py:42
  2.3 3.0 %collective-permute-start.1 = (bf16[256,256]{1,0:T(8,128)(2,1)S(1)}, bf16[256,256]{1,0:T(8,128)(2,1)S(1)}, u32[]{:S(2)}, u32[]{:S(2)}) collective-permute-start(bf16[256,256]{1,0:T(8,128)(2,1)S(1)} %get-tuple-element.62.refs_2_), channel_id=1, source_target_pairs={{0,2},{1,3},{2,0},{3,1},{4,6},{5,7},{6,4},{7,5},{8,10},{9,11},{10,... | collective-permute-start | bytes 393224 | tf_op jit(solution)/shard_map/ppermute | solution.py:60
  5.5 1.9 %collective-permute-start.8 = (bf16[2,512,256]{2,1,0:T(8,128)(2,1)S(1)}, bf16[2,512,256]{2,1,0:T(8,128)(2,1)S(1)}, u32[]{:S(2)}, u32[]{:S(2)}) collective-permute-start(bf16[2,512,256]{2,1,0:T(8,128)(2,1)S(1)} %get-tuple-element.70.refs_4_), channel_id=1, source_target_pairs={{0,16},{16,0},{1,17},{17,1},{2,18},{18,2},{3,19},{19,3},{4,20},{20... | collective-permute-start | bytes 1572872 | tf_op jit(solution)/shard_map/ppermute | solution.py:60
  7.4 2.3 %collective-permute-done.1.refs_1_ = bf16[256,256]{1,0:T(8,128)(2,1)S(1)} collective-permute-done((bf16[256,256]{1,0:T(8,128)(2,1)S(1)}, bf16[256,256]{1,0:T(8,128)(2,1)S(1)}, u32[]{:S(2)}, u32[]{:S(2)}) %collective-permute-start.1) | collective-permute-done | bytes 131104 | tf_op jit(solution)/shard_map/ppermute | solution.py:60
  9.8 1.2 %collective-permute-done.2.refs_1_ = bf16[128,256]{1,0:T(8,128)(2,1)S(1)} collective-permute-done((bf16[128,256]{1,0:T(8,128)(2,1)S(1)}, bf16[128,256]{1,0:T(8,128)(2,1)S(1)}, u32[]{:S(2)}, u32[]{:S(2)}) %collective-permute-start.2) | collective-permute-done | bytes 65568 | tf_op jit(solution)/shard_map/ppermute | solution.py:60
  11.1 2.2 %collective-permute-start.4 = (bf16[128,256]{1,0:T(8,128)(2,1)S(1)}, bf16[128,256]{1,0:T(8,128)(2,1)S(1)}, u32[]{:S(2)}, u32[]{:S(2)}) collective-permute-start(bf16[128,256]{1,0:T(8,128)(2,1)S(1)} %shard_map.94.refs_2_.refs_0_), channel_id=1, source_target_pairs={{0,4},{1,5},{2,6},{3,7},{4,0},{5,1},{6,2},{7,3},{8,12},{9,13},{10,... | collective-permute-start | bytes 196616 | tf_op jit(solution)/shard_map/ppermute | solution.py:60
  13.3 1.6 %collective-permute-start.3 = (bf16[768,256]{1,0:T(8,128)(2,1)S(1)}, bf16[768,256]{1,0:T(8,128)(2,1)S(1)}, u32[]{:S(2)}, u32[]{:S(2)}) collective-permute-start(bf16[768,256]{1,0:T(8,128)(2,1)S(1)} %shard_map.95.refs_2_), channel_id=1, source_target_pairs={{0,2},{1,3},{2,0},{3,1},{4,6},{5,7},{6,4},{7,5},{8,10},{9,11},{10,... | collective-permute-start | bytes 1179656 | tf_op jit(solution)/shard_map/ppermute | solution.py:60
  15.7 2.9 %collective-permute-start.5 = (bf16[128,256]{1,0:T(8,128)(2,1)S(1)}, bf16[128,256]{1,0:T(8,128)(2,1)S(1)}, u32[]{:S(2)}, u32[]{:S(2)}) collective-permute-start(bf16[128,256]{1,0:T(8,128)(2,1)S(1)} %shard_map.97.refs_1_), channel_id=1, source_target_pairs={{0,8},{1,9},{2,10},{3,11},{4,12},{5,13},{6,14},{7,15},{8,0},{9,1},... | collective-permute-start | bytes 196616 | tf_op jit(solution)/shard_map/ppermute | solution.py:60
  18.6 5.6 %collective-permute-done.3.refs_0_.refs_2_ = bf16[768,256]{1,0:T(8,128)(2,1)S(1)} collective-permute-done((bf16[768,256]{1,0:T(8,128)(2,1)S(1)}, bf16[768,256]{1,0:T(8,128)(2,1)S(1)}, u32[]{:S(2)}, u32[]{:S(2)}) %collective-permute-start.3) | collective-permute-done | bytes 393248 | tf_op jit(solution)/shard_map/ppermute | solution.py:60
  24.2 0.4 shard_map.98
  24.8 0.5 shard_map.99
  25.3 0.8 %shard_map.100 = (bf16[4,128,256]{2,1,0:T(8,128)(2,1)S(1)}, bf16[4,128,256]{2,1,0:T(8,128)(2,1)S(1)}, bf16[4,128,256]{2,1,0:T(8,128)(2,1)S(1)}, f32[4,128,256]{2,1,0:T(8,128)S(1)}, bf16[128,256]{1,0:T(8,128)(2,1)S(1)}) custom-call(bf16[384,256]{1,0:T(8,128)(2,1)S(1)} %get-tuple-element.58.refs_0_, ...), custom_call_target="tpu_custom_call" | custom-call | flops 10000000000 | bytes 1 | tf_op jit(solution)/shard_map/pallas_call | solution.py:42
  26.1 0.6 %collective-permute-done.9.refs_3_.refs_6_ = bf16[2,512,256]{2,1,0:T(8,128)(2,1)S(1)} collective-permute-done((bf16[2,512,256]{2,1,0:T(8,128)(2,1)S(1)}, bf16[2,512,256]{2,1,0:T(8,128)(2,1)S(1)}, u32[]{:S(2)}, u32[]{:S(2)}) %collective-permute-start.9) | collective-permute-done | bytes 524320 | tf_op jit(solution)/shard_map/ppermute | solution.py:60
  26.6 0.8 %shard_map.101 = (f32[512,256]{1,0:T(8,128)S(1)}, bf16[512,256]{1,0:T(8,128)(2,1)S(1)}) custom-call(bf16[4,128,1024]{2,1,0:T(8,128)(2,1)S(1)} %get-tuple-element.77.refs_0_, bf16[4,128,256]{2,1,0:T(8,128)(2,1)S(1)} %get-tuple-element.72.refs_1_.refs_3_, bf16[128,256]{1,0:T(8,128)(2,1)S(1)} %get-tuple-element.78.refs_2_.refs_0_, ...), custom_call_target="tpu_custom_call" | custom-call | flops 1 | bytes 1 | tf_op jit(solution)/shard_map/pallas_call | solution.py:42
  27.4 1.6 %collective-permute-start.14 = (bf16[512,256]{1,0:T(8,128)(2,1)S(1)}, bf16[512,256]{1,0:T(8,128)(2,1)S(1)}, u32[]{:S(2)}, u32[]{:S(2)}) collective-permute-start(bf16[512,256]{1,0:T(8,128)(2,1)S(1)} %get-tuple-element.80.refs_8_), channel_id=1, source_target_pairs={{0,16},{16,0},{1,17},{17,1},{2,18},{18,2},{3,19},{19,3},{4,20},{20... | collective-permute-start | bytes 786440 | tf_op jit(solution)/shard_map/ppermute | solution.py:60
  29.0 0.5 collective-permute-start.10
  29.4 1.4 %shard_map.102 = (bf16[256,256]{1,0:T(8,128)(2,1)S(1)}, bf16[256,256]{1,0:T(8,128)(2,1)S(1)}, bf16[256,256]{1,0:T(8,128)(2,1)S(1)}, bf16[256,256]{1,0:T(8,128)(2,1)S(1)}, f32[4,256,256]{2,1,0:T(8,128)S(1)}) custom-call(bf16[384,256]{1,0:T(8,128)(2,1)S(1)} %get-tuple-element.58.refs_0_, bf16[1280,256]{1,0:T(8,128)(2,1)S(1)} %collective-permute-done.refs_0_.refs_1_, ...), custom_call_target="tpu_custom_call" | custom-call | flops 1 | bytes 1 | tf_op jit(solution)/shard_map/pallas_call | solution.py:42
  30.9 2.4 %collective-permute-done.10.refs_1_.refs_3_ = bf16[128,256]{1,0:T(8,128)(2,1)S(1)} collective-permute-done((bf16[128,256]{1,0:T(8,128)(2,1)S(1)}, bf16[128,256]{1,0:T(8,128)(2,1)S(1)}, u32[]{:S(2)}, u32[]{:S(2)}) %collective-permute-start.10) | collective-permute-done | bytes 65568 | tf_op jit(solution)/shard_map/ppermute | solution.py:60
  33.3 2.7 %collective-permute-start.16 = (bf16[128,256]{1,0:T(8,128)(2,1)S(1)}, bf16[128,256]{1,0:T(8,128)(2,1)S(1)}, u32[]{:S(2)}, u32[]{:S(2)}) collective-permute-start(bf16[128,256]{1,0:T(8,128)(2,1)S(1)} %shard_map.103.refs_2_), channel_id=1, source_target_pairs={{0,8},{1,9},{2,10},{3,11},{4,12},{5,13},{6,14},{7,15},{8,0},{9,1},... | collective-permute-start | bytes 196616 | tf_op jit(solution)/shard_map/ppermute | solution.py:60
  35.9 1.6 %collective-permute-start.12 = (bf16[256,256]{1,0:T(8,128)(2,1)S(1)}, bf16[256,256]{1,0:T(8,128)(2,1)S(1)}, u32[]{:S(2)}, u32[]{:S(2)}) collective-permute-start(bf16[256,256]{1,0:T(8,128)(2,1)S(1)} %get-tuple-element.86), channel_id=1, source_target_pairs={{0,2},{1,3},{2,0},{3,1},{4,6},{5,7},{6,4},{7,5},{8,10},{9,11},{10,... | collective-permute-start | bytes 393224 | tf_op jit(solution)/shard_map/ppermute | solution.py:60
  37.8 0.5 collective-permute-start.15
  38.4 0.7 %collective-permute-done.16.refs_4_ = bf16[128,256]{1,0:T(8,128)(2,1)S(1)} collective-permute-done((bf16[128,256]{1,0:T(8,128)(2,1)S(1)}, bf16[128,256]{1,0:T(8,128)(2,1)S(1)}, u32[]{:S(2)}, u32[]{:S(2)}) %collective-permute-start.16) | collective-permute-done | bytes 65568 | tf_op jit(solution)/shard_map/ppermute | solution.py:60
  39.1 0.5 shard_map.105
  39.6 3.9 %collective-permute-done.15.refs_1_ = bf16[256,256]{1,0:T(8,128)(2,1)S(1)} collective-permute-done((bf16[256,256]{1,0:T(8,128)(2,1)S(1)}, bf16[256,256]{1,0:T(8,128)(2,1)S(1)}, u32[]{:S(2)}, u32[]{:S(2)}) %collective-permute-start.15) | collective-permute-done | bytes 131104 | tf_op jit(solution)/shard_map/ppermute | solution.py:60
  43.5 0.4 collective-permute-start.20
  43.9 1.3 %collective-permute-start.18 = (bf16[256,256]{1,0:T(8,128)(2,1)S(1)}, bf16[256,256]{1,0:T(8,128)(2,1)S(1)}, u32[]{:S(2)}, u32[]{:S(2)}) collective-permute-start(bf16[256,256]{1,0:T(8,128)(2,1)S(1)} %get-tuple-element.102), channel_id=1, source_target_pairs={{0,2},{1,3},{2,0},{3,1},{4,6},{5,7},{6,4},{7,5},{8,10},{9,11},{10,... | collective-permute-start | bytes 393224 | tf_op jit(solution)/shard_map/ppermute | solution.py:60
  45.3 1.6 %shard_map.107 = (bf16[128,1024]{1,0:T(8,128)(2,1)}, bf16[128,1024]{1,0:T(8,128)(2,1)}, bf16[128,1024]{1,0:T(8,128)(2,1)S(1)}) custom-call(bf16[256,256]{1,0:T(8,128)(2,1)S(1)} %get-tuple-element.81.refs_0_, bf16[256,256]{1,0:T(8,128)(2,1)S(1)} %collective-permute-done.11.refs_1_, bf16[256,256]{1,0:T(8,128)(2,1)S(1)} %collective-permute-done.12.refs_2_, ...), custom_call_target="tpu_custom_call" | custom-call | flops 1 | bytes 1 | tf_op jit(solution)/shard_map/pallas_call | solution.py:42
  46.9 2.5 %collective-permute-done.20.refs_1_ = bf16[128,256]{1,0:T(8,128)(2,1)S(1)} collective-permute-done((bf16[128,256]{1,0:T(8,128)(2,1)S(1)}, bf16[128,256]{1,0:T(8,128)(2,1)S(1)}, u32[]{:S(2)}, u32[]{:S(2)}) %collective-permute-start.20) | collective-permute-done | bytes 65568 | tf_op jit(solution)/shard_map/ppermute | solution.py:60
  49.4 1.4 %collective-permute-start.21 = (f32[64,256]{1,0:T(8,128)S(1)}, f32[64,256]{1,0:T(8,128)S(1)}, u32[]{:S(2)}, u32[]{:S(2)}) collective-permute-start(f32[64,256]{1,0:T(8,128)S(1)} %get-tuple-element.106.refs_2_), channel_id=1, source_target_pairs={{0,2},{1,3},{2,0},{3,1},{4,6},{5,7},{6,4},{7,5},{8,10},{9,11},{10,... | collective-permute-start | bytes 196616 | tf_op jit(solution)/shard_map/ppermute | solution.py:60
  50.8 3.0 %collective-permute-done.21.refs_1_ = f32[64,256]{1,0:T(8,128)S(1)} collective-permute-done((f32[64,256]{1,0:T(8,128)S(1)}, f32[64,256]{1,0:T(8,128)S(1)}, u32[]{:S(2)}, u32[]{:S(2)}) %collective-permute-start.21) | collective-permute-done | bytes 65568 | tf_op jit(solution)/shard_map/ppermute | solution.py:60
  53.9 0.8 %shard_map.110 = (bf16[128,1024]{1,0:T(8,128)(2,1)}, bf16[128,1024]{1,0:T(8,128)(2,1)}) custom-call(bf16[256,256]{1,0:T(8,128)(2,1)S(1)} %get-tuple-element.97.refs_0_, bf16[256,256]{1,0:T(8,128)(2,1)S(1)} %collective-permute-done.17.refs_1_, bf16[256,256]{1,0:T(8,128)(2,1)S(1)} %collective-permute-done.18.refs_2_, ...), custom_call_target="tpu_custom_call" | custom-call | flops 1 | bytes 1 | tf_op jit(solution)/shard_map/pallas_call | solution.py:42
  55.1 0.7 %shard_map.111 = f32[32,1024]{1,0:T(8,128)} custom-call(f32[64,256]{1,0:T(8,128)S(1)} %get-tuple-element.110.refs_0_, f32[64,256]{1,0:T(8,128)S(1)} %collective-permute-done.22.refs_1_, f32[64,256]{1,0:T(8,128)S(1)} %get-tuple-element.107.refs_4_.refs_2_), custom_call_target="tpu_custom_call" | custom-call | flops 1 | bytes 1 | tf_op jit(solution)/shard_map/pallas_call | solution.py:42
  (38 shorter events, 2.0 us)
Async XLA Ops:
  0.6 4.7 %copy-start.1 = (bf16[1,128,1024]{2,1,0:T(8,128)(2,1)S(1)}, bf16[1,128,1024]{2,1,0:T(8,128)(2,1)}, u32[]{:S(2)}) copy-start(bf16[1,128,1024]{2,1,0:T(8,128)(2,1)} %param.8) | copy-start | bytes 786436
  2.3 7.4 %collective-permute-start.1 = (bf16[256,256]{1,0:T(8,128)(2,1)S(1)}, bf16[256,256]{1,0:T(8,128)(2,1)S(1)}, u32[]{:S(2)}, u32[]{:S(2)}) collective-permute-start(bf16[256,256]{1,0:T(8,128)(2,1)S(1)} %get-tuple-element.62.refs_2_), channel_id=1, source_target_pairs={{0,2},{1,3},{2,0},{3,1},{4,6},{5,7},{6,4},{7,5},{8,10},{9,11},{10,... | collective-permute-start | bytes 393224 | tf_op jit(solution)/shard_map/ppermute | solution.py:60
  5.4 9.9 %collective-permute-start.6 = (bf16[128,1024]{1,0:T(8,128)(2,1)S(1)}, bf16[128,1024]{1,0:T(8,128)(2,1)S(1)}, u32[]{:S(2)}, u32[]{:S(2)}) collective-permute-start(bf16[128,1024]{1,0:T(8,128)(2,1)S(1)} %bitcast.9), channel_id=1, source_target_pairs={{0,2},{1,3},{2,0},{3,1},{4,6},{5,7},{6,4},{7,5},{8,10},{9,11},{10,... | collective-permute-start | bytes 786440 | tf_op jit(solution)/shard_map/ppermute | solution.py:60
  5.5 7.8 %collective-permute-start = (bf16[1280,256]{1,0:T(8,128)(2,1)S(1)}, bf16[1280,256]{1,0:T(8,128)(2,1)S(1)}, u32[]{:S(2)}, u32[]{:S(2)}) collective-permute-start(bf16[1280,256]{1,0:T(8,128)(2,1)S(1)} %get-tuple-element.59), channel_id=1, source_target_pairs={{0,1},{1,0},{2,3},{3,2},{4,5},{5,4},{6,7},{7,6},{8,9},{9,8},{10,11... | collective-permute-start | bytes 1966088 | tf_op jit(solution)/shard_map/ppermute | solution.py:60
  5.5 19.2 %collective-permute-start.8 = (bf16[2,512,256]{2,1,0:T(8,128)(2,1)S(1)}, bf16[2,512,256]{2,1,0:T(8,128)(2,1)S(1)}, u32[]{:S(2)}, u32[]{:S(2)}) collective-permute-start(bf16[2,512,256]{2,1,0:T(8,128)(2,1)S(1)} %get-tuple-element.70.refs_4_), channel_id=1, source_target_pairs={{0,16},{16,0},{1,17},{17,1},{2,18},{18,2},{3,19},{19,3},{4,20},{20... | collective-permute-start | bytes 1572872 | tf_op jit(solution)/shard_map/ppermute | solution.py:60
  9.7 1.3 %collective-permute-start.2 = (bf16[128,256]{1,0:T(8,128)(2,1)S(1)}, bf16[128,256]{1,0:T(8,128)(2,1)S(1)}, u32[]{:S(2)}, u32[]{:S(2)}) collective-permute-start(bf16[128,256]{1,0:T(8,128)(2,1)S(1)} %get-tuple-element.64.refs_2_), channel_id=1, source_target_pairs={{0,1},{1,0},{2,3},{3,2},{4,5},{5,4},{6,7},{7,6},{8,9},{9,8},{10,11... | collective-permute-start | bytes 196616 | tf_op jit(solution)/shard_map/ppermute | solution.py:60
  11.1 4.6 %collective-permute-start.4 = (bf16[128,256]{1,0:T(8,128)(2,1)S(1)}, bf16[128,256]{1,0:T(8,128)(2,1)S(1)}, u32[]{:S(2)}, u32[]{:S(2)}) collective-permute-start(bf16[128,256]{1,0:T(8,128)(2,1)S(1)} %shard_map.94.refs_2_.refs_0_), channel_id=1, source_target_pairs={{0,4},{1,5},{2,6},{3,7},{4,0},{5,1},{6,2},{7,3},{8,12},{9,13},{10,... | collective-permute-start | bytes 196616 | tf_op jit(solution)/shard_map/ppermute | solution.py:60
  13.3 11.0 %collective-permute-start.3 = (bf16[768,256]{1,0:T(8,128)(2,1)S(1)}, bf16[768,256]{1,0:T(8,128)(2,1)S(1)}, u32[]{:S(2)}, u32[]{:S(2)}) collective-permute-start(bf16[768,256]{1,0:T(8,128)(2,1)S(1)} %shard_map.95.refs_2_), channel_id=1, source_target_pairs={{0,2},{1,3},{2,0},{3,1},{4,6},{5,7},{6,4},{7,5},{8,10},{9,11},{10,... | collective-permute-start | bytes 1179656 | tf_op jit(solution)/shard_map/ppermute | solution.py:60
  15.3 9.5 %collective-permute-start.7 = (bf16[128,1024]{1,0:T(8,128)(2,1)S(1)}, bf16[128,1024]{1,0:T(8,128)(2,1)S(1)}, u32[]{:S(2)}, u32[]{:S(2)}) collective-permute-start(bf16[128,1024]{1,0:T(8,128)(2,1)S(1)} %collective-permute-done.6.refs_2_), channel_id=1, source_target_pairs={{0,1},{1,0},{2,3},{3,2},{4,5},{5,4},{6,7},{7,6},{8,9},{9,8},{10,11... | collective-permute-start | bytes 786440 | tf_op jit(solution)/shard_map/ppermute | solution.py:60
  15.7 9.6 %collective-permute-start.5 = (bf16[128,256]{1,0:T(8,128)(2,1)S(1)}, bf16[128,256]{1,0:T(8,128)(2,1)S(1)}, u32[]{:S(2)}, u32[]{:S(2)}) collective-permute-start(bf16[128,256]{1,0:T(8,128)(2,1)S(1)} %shard_map.97.refs_1_), channel_id=1, source_target_pairs={{0,8},{1,9},{2,10},{3,11},{4,12},{5,13},{6,14},{7,15},{8,0},{9,1},... | collective-permute-start | bytes 196616 | tf_op jit(solution)/shard_map/ppermute | solution.py:60
  24.7 2.0 %collective-permute-start.9 = (bf16[2,512,256]{2,1,0:T(8,128)(2,1)S(1)}, bf16[2,512,256]{2,1,0:T(8,128)(2,1)S(1)}, u32[]{:S(2)}, u32[]{:S(2)}) collective-permute-start(bf16[2,512,256]{2,1,0:T(8,128)(2,1)S(1)} %collective-permute-done.8.refs_5_), channel_id=1, source_target_pairs={{0,1},{1,0},{2,3},{3,2},{4,5},{5,4},{6,7},{7,6},{8,9},{9,8},{10,11... | collective-permute-start | bytes 1572872 | tf_op jit(solution)/shard_map/ppermute | solution.py:60
  27.4 10.4 %collective-permute-start.14 = (bf16[512,256]{1,0:T(8,128)(2,1)S(1)}, bf16[512,256]{1,0:T(8,128)(2,1)S(1)}, u32[]{:S(2)}, u32[]{:S(2)}) collective-permute-start(bf16[512,256]{1,0:T(8,128)(2,1)S(1)} %get-tuple-element.80.refs_8_), channel_id=1, source_target_pairs={{0,16},{16,0},{1,17},{17,1},{2,18},{18,2},{3,19},{19,3},{4,20},{20... | collective-permute-start | bytes 786440 | tf_op jit(solution)/shard_map/ppermute | solution.py:60
  29.0 4.3 %collective-permute-start.10 = (bf16[128,256]{1,0:T(8,128)(2,1)S(1)}, bf16[128,256]{1,0:T(8,128)(2,1)S(1)}, u32[]{:S(2)}, u32[]{:S(2)}) collective-permute-start(bf16[128,256]{1,0:T(8,128)(2,1)S(1)} %get-tuple-element.78.refs_2_.refs_0_), channel_id=1, source_target_pairs={{0,4},{1,5},{2,6},{3,7},{4,0},{5,1},{6,2},{7,3},{8,12},{9,13},{10,... | collective-permute-start | bytes 196616 | tf_op jit(solution)/shard_map/ppermute | solution.py:60
  33.3 5.8 %collective-permute-start.16 = (bf16[128,256]{1,0:T(8,128)(2,1)S(1)}, bf16[128,256]{1,0:T(8,128)(2,1)S(1)}, u32[]{:S(2)}, u32[]{:S(2)}) collective-permute-start(bf16[128,256]{1,0:T(8,128)(2,1)S(1)} %shard_map.103.refs_2_), channel_id=1, source_target_pairs={{0,8},{1,9},{2,10},{3,11},{4,12},{5,13},{6,14},{7,15},{8,0},{9,1},... | collective-permute-start | bytes 196616 | tf_op jit(solution)/shard_map/ppermute | solution.py:60
  35.9 8.0 %collective-permute-start.13 = (bf16[256,256]{1,0:T(8,128)(2,1)S(1)}, bf16[256,256]{1,0:T(8,128)(2,1)S(1)}, u32[]{:S(2)}, u32[]{:S(2)}) collective-permute-start(bf16[256,256]{1,0:T(8,128)(2,1)S(1)} %get-tuple-element.87.refs_2_), channel_id=1, source_target_pairs={{0,3},{1,2},{2,1},{3,0},{4,7},{5,6},{6,5},{7,4},{8,11},{9,10},{10,... | collective-permute-start | bytes 393224 | tf_op jit(solution)/shard_map/ppermute | solution.py:60
  35.9 9.4 %collective-permute-start.12 = (bf16[256,256]{1,0:T(8,128)(2,1)S(1)}, bf16[256,256]{1,0:T(8,128)(2,1)S(1)}, u32[]{:S(2)}, u32[]{:S(2)}) collective-permute-start(bf16[256,256]{1,0:T(8,128)(2,1)S(1)} %get-tuple-element.86), channel_id=1, source_target_pairs={{0,2},{1,3},{2,0},{3,1},{4,6},{5,7},{6,4},{7,5},{8,10},{9,11},{10,... | collective-permute-start | bytes 393224 | tf_op jit(solution)/shard_map/ppermute | solution.py:60
  37.5 7.8 %collective-permute-start.11 = (bf16[256,256]{1,0:T(8,128)(2,1)S(1)}, bf16[256,256]{1,0:T(8,128)(2,1)S(1)}, u32[]{:S(2)}, u32[]{:S(2)}) collective-permute-start(bf16[256,256]{1,0:T(8,128)(2,1)S(1)} %get-tuple-element.84), channel_id=1, source_target_pairs={{0,1},{1,0},{2,3},{3,2},{4,5},{5,4},{6,7},{7,6},{8,9},{9,8},{10,11... | collective-permute-start | bytes 393224 | tf_op jit(solution)/shard_map/ppermute | solution.py:60
  37.8 5.7 %collective-permute-start.15 = (bf16[256,256]{1,0:T(8,128)(2,1)S(1)}, bf16[256,256]{1,0:T(8,128)(2,1)S(1)}, u32[]{:S(2)}, u32[]{:S(2)}) collective-permute-start(bf16[256,256]{1,0:T(8,128)(2,1)S(1)} %get-tuple-element.90.refs_7_), channel_id=1, source_target_pairs={{0,4},{1,5},{2,6},{3,7},{4,0},{5,1},{6,2},{7,3},{8,12},{9,13},{10,... | collective-permute-start | bytes 393224 | tf_op jit(solution)/shard_map/ppermute | solution.py:60
  39.1 6.2 %copy-start = (bf16[512,1024]{1,0:T(8,128)(2,1)S(1)}, bf16[512,1024]{1,0:T(8,128)(2,1)}, u32[]{:S(2)}) copy-start(bf16[512,1024]{1,0:T(8,128)(2,1)} %refs_4_.1) | copy-start | bytes 3145732
  43.5 5.8 %collective-permute-start.20 = (bf16[128,256]{1,0:T(8,128)(2,1)S(1)}, bf16[128,256]{1,0:T(8,128)(2,1)S(1)}, u32[]{:S(2)}, u32[]{:S(2)}) collective-permute-start(bf16[128,256]{1,0:T(8,128)(2,1)S(1)} %get-tuple-element.94.refs_7_), channel_id=1, source_target_pairs={{0,8},{1,9},{2,10},{3,11},{4,12},{5,13},{6,14},{7,15},{8,0},{9,1},... | collective-permute-start | bytes 196616 | tf_op jit(solution)/shard_map/ppermute | solution.py:60
  43.9 10.0 %collective-permute-start.19 = (bf16[256,256]{1,0:T(8,128)(2,1)S(1)}, bf16[256,256]{1,0:T(8,128)(2,1)S(1)}, u32[]{:S(2)}, u32[]{:S(2)}) collective-permute-start(bf16[256,256]{1,0:T(8,128)(2,1)S(1)} %get-tuple-element.103.refs_2_), channel_id=1, source_target_pairs={{0,3},{1,2},{2,1},{3,0},{4,7},{5,6},{6,5},{7,4},{8,11},{9,10},{10,... | collective-permute-start | bytes 393224 | tf_op jit(solution)/shard_map/ppermute | solution.py:60
  43.9 10.0 %collective-permute-start.18 = (bf16[256,256]{1,0:T(8,128)(2,1)S(1)}, bf16[256,256]{1,0:T(8,128)(2,1)S(1)}, u32[]{:S(2)}, u32[]{:S(2)}) collective-permute-start(bf16[256,256]{1,0:T(8,128)(2,1)S(1)} %get-tuple-element.102), channel_id=1, source_target_pairs={{0,2},{1,3},{2,0},{3,1},{4,6},{5,7},{6,4},{7,5},{8,10},{9,11},{10,... | collective-permute-start | bytes 393224 | tf_op jit(solution)/shard_map/ppermute | solution.py:60
  49.4 4.4 %collective-permute-start.21 = (f32[64,256]{1,0:T(8,128)S(1)}, f32[64,256]{1,0:T(8,128)S(1)}, u32[]{:S(2)}, u32[]{:S(2)}) collective-permute-start(f32[64,256]{1,0:T(8,128)S(1)} %get-tuple-element.106.refs_2_), channel_id=1, source_target_pairs={{0,2},{1,3},{2,0},{3,1},{4,6},{5,7},{6,4},{7,5},{8,10},{9,11},{10,... | collective-permute-start | bytes 196616 | tf_op jit(solution)/shard_map/ppermute | solution.py:60
  50.8 3.2 %collective-permute-start.17 = (bf16[256,256]{1,0:T(8,128)(2,1)S(1)}, bf16[256,256]{1,0:T(8,128)(2,1)S(1)}, u32[]{:S(2)}, u32[]{:S(2)}) collective-permute-start(bf16[256,256]{1,0:T(8,128)(2,1)S(1)} %get-tuple-element.100), channel_id=1, source_target_pairs={{0,1},{1,0},{2,3},{3,2},{4,5},{5,4},{6,7},{7,6},{8,9},{9,8},{10,11... | collective-permute-start | bytes 393224 | tf_op jit(solution)/shard_map/ppermute | solution.py:60
  53.8 1.3 %collective-permute-start.22 = (f32[64,256]{1,0:T(8,128)S(1)}, f32[64,256]{1,0:T(8,128)S(1)}, u32[]{:S(2)}, u32[]{:S(2)}) collective-permute-start(f32[64,256]{1,0:T(8,128)S(1)} %get-tuple-element.107.refs_4_.refs_2_), channel_id=1, source_target_pairs={{0,1},{1,0},{2,3},{3,2},{4,5},{5,4},{6,7},{7,6},{8,9},{9,8},{10,11... | collective-permute-start | bytes 196616 | tf_op jit(solution)/shard_map/ppermute | solution.py:60

commit v7 on v6

v7 whole, which is shorter than its diff:
```python
import functools
import math

import jax
import jax.numpy as jnp
from jax import lax
from jax.experimental import pallas as pl
from jax.experimental.pallas import tpu as pltpu
from jax.sharding import PartitionSpec as P

DH = 128
SLAB = 4
EPSILON = 1e-05
BF16 = jnp.bfloat16
F32 = jnp.float32


def dot(left, right, left_dim, right_dim):
    return lax.dot_general(
        left, right, (((left_dim,), (right_dim,)), ((), ())), preferred_element_type=F32
    )


class Chain:
    def __init__(self):
        self.last = None

    def __call__(self, body, outs, *args, scratch=(), far=False, wait=(), cost=1, end=False):
        count = len(args)
        if far:
            args = [pltpu.with_memory_space_constraint(x, pltpu.HBM) for x in args]
        specs = [pl.BlockSpec(memory_space=pl.ANY) if far else pl.BlockSpec()] * count
        inner = body
        if self.last is not None:
            extra = (self.last, *wait)
            args = (*args, *extra)
            specs = [*specs, *[pl.BlockSpec(memory_space=pl.ANY)] * len(extra)]

            def inner(*refs):
                body(*refs[:count], *refs[count + len(extra) :])

        found = pl.pallas_call(
            inner,
            out_shape=[jax.ShapeDtypeStruct(s, d) for s, d in outs],
            in_specs=specs,
            scratch_shapes=list(scratch),
            cost_estimate=pl.CostEstimate(flops=cost, bytes_accessed=1, transcendentals=0),
            compiler_params=pltpu.CompilerParams(vmem_limit_bytes=32 * 2**20),
        )(*args)
        if not end:
            self.last = min(reversed(found), key=lambda x: x.size)
        return found


def after(x, *others):
    return lax.optimization_barrier((x, *others))[0]


def flip(x, axis, count, bits):
    return lax.ppermute(x, axis, [(i, i ^ bits) for i in range(count)])


def head(h):
    return slice(h * DH, (h + 1) * DH)


def part(i, size):
    return slice(i * size, (i + 1) * size)


def cut(start, size):
    return pl.ds(pl.multiple_of(start * size, size), size)


def member(r):
    return jnp.bitwise_xor(lax.rem(lax.axis_index("seq"), SLAB), r)


def causal(block):
    rows = lax.broadcasted_iota(jnp.int32, (block, block), 0)
    return lax.broadcasted_iota(jnp.int32, (block, block), 1) <= rows


def fetch(pairs, sems):
    copies = [pltpu.make_async_copy(a, b, sems.at[i]) for i, (a, b) in enumerate(pairs)]
    for copy in copies:
        copy.start()
    return copies


def front_kernel(k_hbm, v_hbm, w_hbm, own_ref, near_ref, far_ref, columns_ref, k_ref, v_ref, w_ref, sems):
    copies = fetch([(k_hbm, k_ref), (v_hbm, v_ref), (w_hbm, w_ref)], sems)
    width = k_ref.shape[1] // SLAB
    copies[0].wait()
    copies[1].wait()
    places = (own_ref, near_ref, far_ref.at[part(0, DH)], far_ref.at[part(1, DH)])
    for r, out in enumerate(places):
        k, v = k_ref[:, cut(member(r), width)], v_ref[:, cut(member(r), width)]
        for h in range(width // DH):
            out[:, head(h)] = dot(k[:, head(h)], v[:, head(h)], 0, 0).astype(out.dtype)
    copies[2].wait()
    for i in range(2):
        columns_ref[i] = w_ref[:, cut(member(2 * i), width)]


def pack_kernel(q_hbm, k_hbm, v_hbm, c_hbm, *refs):
    attend_ref, own_ref, message_ref, far_ref, q_ref, k_ref, v_ref, c_ref, sems = refs
    copies = fetch([(q_hbm, q_ref), (k_hbm, k_ref), (v_hbm, v_ref), (c_hbm, c_ref)], sems)
    block = q_ref.shape[0]
    width = q_ref.shape[1] // SLAB
    for copy in copies[:3]:
        copy.wait()
    mask = causal(block)
    places = (own_ref, message_ref.at[: 2 * block], far_ref, message_ref.at[2 * block : 4 * block])
    for r, out in enumerate(places):
        q, k, v = (ref[:, cut(member(r), width)] for ref in (q_ref, k_ref, v_ref))
        out[:block, :] = q
        for h in range(width // DH):
            attend = jnp.where(mask, dot(q[:, head(h)], k[:, head(h)], 1, 1), 0.0).astype(BF16)
            attend_ref[r, h] = attend
            out[block:, head(h)] = dot(attend, v[:, head(h)], 1, 0).astype(BF16)
    copies[3].wait()
    for i in range(c_ref.shape[1] // width):
        message_ref[part(4 + i, block), :] = c_ref[:, part(i, width)]


def cross_kernel(near_ref, got_ref, out_ref):
    out_ref[part(0, DH), :] = near_ref[...]
    out_ref[part(1, DH), :] = got_ref[part(1, DH), :]


def total_kernel(own_ref, far_ref, near_ref, out_ref):
    total = own_ref[...] + far_ref[part(0, DH), :].astype(F32)
    total = total + near_ref[part(0, DH), :].astype(F32) + near_ref[part(1, DH), :].astype(F32)
    out_ref[...] = total.astype(BF16)


def pair_kernel(message_ref, far_ref, out_ref):
    size = far_ref.shape[0]
    out_ref[:size, :] = far_ref[...]
    out_ref[size:, :] = message_ref[part(1, size), :]


def add_kernel(own_ref, got_ref, out_ref):
    out_ref[...] = (own_ref[...].astype(F32) + got_ref[...].astype(F32)).astype(out_ref.dtype)


def dnormed_kernel(groups, message_ref, *refs):
    cots, weights = refs[: SLAB - 1], refs[SLAB - 1 : SLAB - 1 + groups]
    dnormed_ref, cot_ref = refs[SLAB - 1 + groups :]
    block, outputs = cots[0].shape
    width = dnormed_ref.shape[2]
    rows = weights[0].shape[1]
    me = lax.axis_index("dp")
    for i in range(outputs // width):
        cot_ref[1, :, part(i, width)] = message_ref[part(4 + i, block), :]
    for r, ref in zip((0, 2, 3), cots):
        cot_ref[r] = ref[...]
    for r in range(SLAB):
        total = dot(cot_ref[r, :, cut(me, rows)], weights[0][0], 1, 0)
        for j in range(1, groups):
            total = total + dot(cot_ref[r, :, cut(jnp.bitwise_xor(me, j), rows)], weights[j][0], 1, 0)
        dnormed_ref[r] = total


def from_slabs(backward, refs):
    slab = lax.div(lax.axis_index("seq"), SLAB)
    total = jnp.zeros(refs[0].shape, F32)
    for i, ref in enumerate(refs):
        bit = lax.rem(lax.div(slab, 1 << i), 2)
        total = total + jnp.where(bit == (0 if backward else 1), ref[...].astype(F32), 0.0)
    return total


def middle_kernel(*refs):
    own_ref, message_ref, token_far, own_state, far_state, near_state, dnormed_ref = refs[:7]
    *before, normed_ref, back0, back1, back2, back3, u_ref, slab_ref, running = refs[7:]
    _, block, width = normed_ref.shape
    heads = width // DH
    size = 2 * block
    tokens = (own_ref, message_ref.at[:size], token_far.at[:size], token_far.at[size:])
    running[member(0)] = own_state[...]
    running[member(1)] = near_state[part(0, DH), :].astype(F32)
    running[member(2)] = far_state[part(0, DH), :].astype(F32)
    running[member(3)] = near_state[part(1, DH), :].astype(F32)
    total = from_slabs(False, before)
    for p in range(SLAB):
        total, running[p] = total + running[p], total
    sums = [jnp.zeros((DH, DH), F32)] * heads
    for r in range(SLAB):
        out = (back0, back1, back2, back3)[r]
        prior = running[member(r)].astype(BF16)
        out[size:, :] = prior
        for h in range(heads):
            q = tokens[r][:block, head(h)]
            mixed = tokens[r][block:, head(h)].astype(F32) + dot(q, prior[:, head(h)], 1, 0)
            scale = lax.rsqrt(jnp.mean(mixed * mixed, axis=-1, keepdims=True) + EPSILON)
            normed = mixed * scale
            normed_ref[r, :, head(h)] = normed.astype(BF16)
            out[:block, head(h)] = normed.astype(BF16)
            dnormed = dnormed_ref[r, :, head(h)]
            along = jnp.mean(dnormed * normed, axis=-1, keepdims=True)
            dmixed = ((dnormed - normed * along) * scale).astype(BF16)
            out[block:size, head(h)] = dmixed
            u = dot(q, dmixed, 0, 0)
            u_ref[r, :, head(h)] = u
            sums[h] = sums[h] + u
    for h in range(heads):
        slab_ref[:, head(h)] = sums[h].astype(BF16)


def later_kernel(*refs):
    *behind, u_ref, near_ref, far_ref, running = refs
    for r in range(SLAB):
        running[member(r)] = u_ref[r]
    total = from_slabs(True, behind)
    for p in reversed(range(SLAB)):
        total, running[p] = total + running[p], total
    for r in range(SLAB):
        (near_ref, far_ref)[r // 2][part(r % 2, DH), :] = running[member(r)].astype(BF16)


def relay_kernel(near_ref, far_ref, out_ref):
    size = near_ref.shape[0] // 2
    out_ref[:size, :] = near_ref[size:, :]
    out_ref[size:, :] = far_ref[size:, :]


def arrived(near_ref, far_ref, core_ref):
    size = near_ref.shape[0] // 2
    first, second = slice(0, size), slice(size, 2 * size)
    return near_ref.at[first], core_ref.at[first], far_ref.at[first], core_ref.at[second]


def late_kernel(groups, *refs):
    backs, (q_ref, k_ref, v_ref, attend_ref, own_ref) = refs[:SLAB], refs[SLAB : SLAB + 5]
    far, (out_ref, gq_ref, gk_ref, gv_ref, normed_ref) = refs[SLAB + 5 : -5], refs[-5:]
    block, width = q_ref.shape[0], backs[0].shape[1]
    size = 2 * block
    rows = own_ref.shape[0]
    me = lax.axis_index("dp")
    mask = causal(block)
    for r in range(SLAB):
        at = cut(member(r), width)
        normed_ref[:, at] = backs[r][:block, :]
        q, k, v = q_ref[:, at], k_ref[:, at], v_ref[:, at]
        gqs, gks, gvs = [], [], []
        for h in range(width // DH):
            dmixed = backs[r][block:size, head(h)]
            back = jnp.where(mask, dot(dmixed, v[:, head(h)], 1, 1), 0.0).astype(BF16)
            gqs.append(dot(back, k[:, head(h)], 1, 0) + dot(dmixed, backs[r][size:, head(h)], 1, 1))
            gks.append(dot(back, q[:, head(h)], 0, 0))
            gvs.append(dot(attend_ref[r, h], dmixed, 0, 0))
        gq_ref[:, at] = jnp.concatenate(gqs, axis=1).astype(BF16)
        gk_ref[r] = jnp.concatenate(gks, axis=1)
        gv_ref[r] = jnp.concatenate(gvs, axis=1)
    out_ref[:, cut(me, rows)] = dot(normed_ref[...], own_ref[...], 1, 1).astype(BF16)
    for j in range(1, groups):
        total = jnp.zeros((block, rows), F32)
        for r in range(SLAB):
            total = total + dot(backs[r][:block, :], far[2 * (j - 1) + r % 2][r // 2], 1, 1)
        out_ref[:, cut(jnp.bitwise_xor(me, j), rows)] = total.astype(BF16)


def last_kernel(near_ref, far_ref, core_ref, k_ref, v_ref, gk_part, gv_part, gk_ref, gv_ref):
    laters = arrived(near_ref, far_ref, core_ref)
    width = near_ref.shape[1]
    for r in range(SLAB):
        at = cut(member(r), width)
        k, v = k_ref[:, at], v_ref[:, at]
        gks, gvs = [], []
        for h in range(width // DH):
            later = laters[r][:, head(h)]
            gks.append(gk_part[r, :, head(h)] + dot(v[:, head(h)], later, 1, 1))
            gvs.append(gv_part[r, :, head(h)] + dot(k[:, head(h)], later, 1, 0))
        gk_ref[:, at] = jnp.concatenate(gks, axis=1).astype(BF16)
        gv_ref[:, at] = jnp.concatenate(gvs, axis=1).astype(BF16)


def product_kernel(slabs, cot_ref, normed_ref, keep_ref, send_ref):
    me = lax.axis_index("dp")
    slab = lax.div(lax.axis_index("seq"), SLAB)
    rows = keep_ref.shape[0] // slabs
    for j, out in enumerate((send_ref, keep_ref)):
        for d in range(slabs):
            at = jnp.bitwise_xor(me, 1 - j) * slabs + jnp.bitwise_xor(slab, d)
            total = dot(cot_ref[0, :, cut(at, rows)], normed_ref[0], 0, 0)
            for r in range(1, SLAB):
                total = total + dot(cot_ref[r, :, cut(at, rows)], normed_ref[r], 0, 0)
            out[part(d, rows), :] = total.astype(out.dtype)


def split_kernel(own_ref, got_ref, keep_ref, send_ref):
    rows = keep_ref.shape[0] // 2
    for i in range(4):
        total = own_ref[part(i, rows), :] + got_ref[part(i, rows), :].astype(F32)
        out = (keep_ref, send_ref)[i % 2]
        out[part(i // 2, rows), :] = total.astype(out.dtype)


def split_again_kernel(own_ref, got_ref, keep_ref, send_ref):
    rows = keep_ref.shape[0]
    for i, out in enumerate((keep_ref, send_ref)):
        total = own_ref[part(i, rows), :] + got_ref[part(i, rows), :].astype(F32)
        out[...] = total.astype(out.dtype)


def share_kernel(own_ref, got_ref, keep_ref, send_ref, total_ref):
    total_ref[...] = own_ref[...] + got_ref[...].astype(F32)
    rows = keep_ref.shape[0] // 2
    for i, r in enumerate((0, 1)):
        keep_ref[part(i, rows), :] = total_ref[cut(member(r), rows), :]
    for i, r in enumerate((2, 3)):
        send_ref[part(i, rows), :] = total_ref[cut(member(r), rows), :]


def pass_kernel(own_ref, got_ref, keep_ref, send_ref):
    rows = own_ref.shape[0] // 2
    for i, ref in enumerate((own_ref, got_ref)):
        keep_ref[part(i, rows), :] = ref[:rows, :]
        send_ref[part(i, rows), :] = ref[rows:, :]


def finish_kernel(factor, keep_ref, got_ref, out_ref):
    rows, width = out_ref.shape[0], keep_ref.shape[1]
    for i, ref in enumerate((keep_ref, got_ref)):
        for j in range(2):
            out_ref[:, cut(member(i + 2 * j), width)] = ref[part(j, rows), :] * factor


def local(queries, keys, values, cotangent, out_weight, *, dp, seq):
    call = Chain()
    local_seqs, block, features = queries.shape
    outputs = cotangent.shape[2]
    rows = local_seqs * block
    slabs = seq // SLAB
    width = features // SLAB
    heads = width // DH
    q, k, v = (x.reshape(rows, features) for x in (queries, keys, values))
    cot = cotangent.reshape(rows, outputs)
    factor = 1.0 / math.sqrt(rows * dp * seq)
    near = functools.partial(flip, axis="seq", count=seq)

    def doubling(total, cost=1):
        found = []
        bits = SLAB
        while bits < seq:
            if found:
                (total,) = call(add_kernel, [(total.shape, BF16)], total, found[-1], cost=cost)
            found.append(near(total, bits=bits))
            bits *= 2
        return found, total

    def scratch(*arrays):
        return [pltpu.VMEM(x.shape, BF16) for x in arrays] + [pltpu.SemaphoreType.DMA((len(arrays),))]

    cot_y = near(cot, bits=2)
    own_state, near_state, far_state, columns = call(
        front_kernel,
        [((DH, width), F32), ((DH, width), BF16), ((2 * DH, width), BF16),
         ((2, out_weight.shape[0], width), BF16)],
        k, v, out_weight, far=True, scratch=scratch(k, v, out_weight),
    )
    far_state = near(far_state, bits=2)
    w_far = [flip(columns, "dp", dp, j) for j in range(1, dp)]
    attend, own_tokens, message, far_tokens = call(
        pack_kernel,
        [((SLAB, heads, rows, rows), BF16), ((2 * rows, width), BF16),
         (((4 + outputs // width) * rows, width), BF16), ((2 * rows, width), BF16)],
        q, k, v, cot, far=True, scratch=scratch(q, k, v, cot),
    )
    message = near(message, bits=1)
    (near_state,) = call(
        cross_kernel, [((2 * DH, width), BF16)], near_state, far_state, cost=5 * 10**9
    )
    near_state = near(near_state, bits=1)
    (slab_kv,) = call(total_kernel, [((DH, width), BF16)], own_state, far_state, near_state)
    (far_tokens,) = call(pair_kernel, [((4 * rows, width), BF16)], message, far_tokens)
    cot_yc = near(after(cot_y, far_tokens), bits=1)
    far_tokens = near(far_tokens, bits=2)
    before, _ = doubling(slab_kv, 2 * 10**9)
    dnormed, cots = call(
        functools.partial(dnormed_kernel, dp),
        [((SLAB, rows, width), F32), ((SLAB, rows, outputs), BF16)],
        message, cot, cot_y, cot_yc, columns, *w_far,
    )
    w_all = [x for w in w_far for x in (w, near(after(w, dnormed), bits=1))]
    normed, *backs, u, slab_u = call(
        middle_kernel,
        [((SLAB, rows, width), BF16)] + [((2 * rows + DH, width), BF16)] * SLAB
        + [((SLAB, DH, width), F32), ((DH, width), BF16)],
        own_tokens, message, far_tokens, own_state, far_state, near_state, dnormed, *before,
        cost=10**10, scratch=[pltpu.VMEM((SLAB, DH, width), F32)],
    )
    tuned = dp == 2 and slabs == 4 and outputs // (dp * seq) % 8 == 0
    piece = outputs // (dp * slabs)
    if tuned:
        keep, send = call(
            functools.partial(product_kernel, slabs),
            [((outputs // dp, width), F32), ((outputs // dp, width), BF16)], cots, normed, wait=w_all[1::2],
        )
        got = flip(send, "dp", dp, 1)
    backs = [backs[0], *(near(backs[r], bits=r) for r in range(1, SLAB))]
    behind, last_u = doubling(slab_u)
    if tuned:
        keep, send = call(
            split_kernel, [((2 * piece, width), F32), ((2 * piece, width), BF16)], keep, got, cost=1
        )
        got = near(send, bits=SLAB)
    later, later_far = call(
        later_kernel, [((2 * DH, width), BF16)] * 2, *behind, u, cost=3 * 10**9,
        scratch=[pltpu.VMEM((SLAB, DH, width), F32)],
    )
    later_far = near(later_far, bits=2)
    if tuned:
        keep, send = call(
            split_again_kernel, [((piece, width), F32), ((piece, width), BF16)], keep, got, cost=1
        )
        got = near(send, bits=2 * SLAB)
    output, gq, gk_part, gv_part, own_normed = call(
        functools.partial(late_kernel, dp),
        [((rows, outputs), BF16), ((rows, features), BF16), ((SLAB, rows, width), F32),
         ((SLAB, rows, width), F32), ((rows, features), BF16)],
        *backs, q, k, v, attend, out_weight, *w_all,
    )
    if tuned:
        keep, share = call(
            share_kernel, [((piece // 2, width), F32)] * 2, keep, got,
            scratch=[pltpu.VMEM((piece, width), F32)],
        )
        got = near(share, bits=2)
    (send,) = call(relay_kernel, [((2 * DH, width), BF16)], later, later_far)
    later_core = near(send, bits=1)
    if tuned:
        keep, share = call(pass_kernel, [((piece // 2, width), F32)] * 2, keep, got)
        got = near(share, bits=1)
    gk, gv = call(
        last_kernel, [((rows, features), BF16)] * 2,
        later, later_far, later_core, k, v, gk_part, gv_part, end=True,
    )
    if tuned:
        (grad_weight,) = call(
            functools.partial(finish_kernel, factor),
            [((piece // SLAB, features), F32)], keep, got, end=True,
        )
    else:
        partial = dot(cot, own_normed, 0, 0) * factor
        grad_weight = lax.psum_scatter(partial, ("dp", "seq"), scatter_dimension=0, tiled=True)
    shape = queries.shape
    return (
        output.reshape(cotangent.shape), gq.reshape(shape), gk.reshape(shape), gv.reshape(shape),
        grad_weight,
    )


def solution(mesh):
    dp, seq = mesh.shape["dp"], mesh.shape["seq"]
    return jax.shard_map(
        functools.partial(local, dp=dp, seq=seq),
        mesh=mesh,
        in_specs=(P("dp", "seq", None),) * 4 + (P("dp", None),),
        out_specs=(P("dp", "seq", None),) * 4 + (P(("dp", "seq"), None),),
        check_vma=False,
    )
```

time: 56 us -> 55.3 us (0.987)
  waiting for transfers between devices: 23 us -> 17 us
  starting transfers between devices: 22.2 us -> 25.3 us
  Pallas kernels: 9.72 us -> 12 us
    ppermute x23 -> x22, waiting for transfers between devices: 23 us -> 17 us  [flip(): return lax.ppermute(x, axis, [(i, i ^ bits) for i in range(count)])]
    ppermute x23 -> x22, starting transfers between devices: 22.2 us -> 25.3 us  [flip(): return lax.ppermute(x, axis, [(i, i ^ bits) for i in range(count)])]
    pallas_call x20 -> x19, Pallas kernels: 9.72 us -> 12 us  [__call__(): pl.pallas_call(inner, out_shape=[jax.ShapeDtypeStruct(s, d) for s, d in o...]
  transfers between devices with their start and end apart: 23 -> 22, of which waited for: 11 -> 10; matrix products, arithmetic and copies ran while one was open for 0% -> 0% of each run, Pallas kernels for 12% -> 16%
where the time goes in v7:
time: 55.3 us; the launch traced here: 55.1 us
  starting transfers between devices  25.3 us (46%)
  waiting for transfers between devices  17 us (31%)
  Pallas kernels  12 us (22%)
  between operations  0.79 us (1%)
    ppermute x22, starting transfers between devices, flip(): return lax.ppermute(x, axis, [(i, i ^ bits) for i in range(count)])  25.3 us
    ppermute x22, waiting for transfers between devices, flip(): return lax.ppermute(x, axis, [(i, i ^ bits) for i in range(count)])  17 us
    pallas_call x19, Pallas kernels, __call__(): pl.pallas_call(inner, out_shape=[jax.ShapeDtypeStruct(s, d) for s, d in o...  12 us
  transfers between devices with their start and end apart: 22, of which 10 were waited for; matrix products, arithmetic and copies ran while one was open for 0% of the time, Pallas kernels for 16%

profile of v7, /device:TPU:0, one launch (start us, length us, event | category | flops | bytes accessed | tf_op | source)
XLA Modules:
  0.0 55.1 jit_solution(5445936005204591098)
XLA Ops:
  0.6 1.5 %shard_map.92 = (f32[128,256]{1,0:T(8,128)S(1)}, bf16[128,256]{1,0:T(8,128)(2,1)S(1)}, bf16[256,256]{1,0:T(8,128)(2,1)S(1)}, bf16[2,512,256]{2,1,0:T(8,128)(2,1)S(1)}) custom-call(bf16[128,1024]{1,0:T(8,128)(2,1)} %bitcast.8, bf16[128,1024]{1,0:T(8,128)(2,1)} %bitcast.12, bf16[512,1024]{1,0:T(8,128)(2,1)} %refs_8_.1), custom_call_target="tpu_custom_call" | custom-call | flops 1 | bytes 1 | tf_op jit(solution)/shard_map/pallas_call | solution.py:42
  2.1 3.0 %collective-permute-start.1 = (bf16[256,256]{1,0:T(8,128)(2,1)S(1)}, bf16[256,256]{1,0:T(8,128)(2,1)S(1)}, u32[]{:S(2)}, u32[]{:S(2)}) collective-permute-start(bf16[256,256]{1,0:T(8,128)(2,1)S(1)} %get-tuple-element.48), channel_id=1, source_target_pairs={{0,2},{1,3},{2,0},{3,1},{4,6},{5,7},{6,4},{7,5},{8,10},{9,11},{10,... | collective-permute-start | bytes 393224 | tf_op jit(solution)/shard_map/ppermute | solution.py:60
  5.2 1.9 %collective-permute-start.6 = (bf16[2,512,256]{2,1,0:T(8,128)(2,1)S(1)}, bf16[2,512,256]{2,1,0:T(8,128)(2,1)S(1)}, u32[]{:S(2)}, u32[]{:S(2)}) collective-permute-start(bf16[2,512,256]{2,1,0:T(8,128)(2,1)S(1)} %get-tuple-element.50.refs_4_), channel_id=1, source_target_pairs={{0,16},{16,0},{1,17},{17,1},{2,18},{18,2},{3,19},{19,3},{4,20},{20... | collective-permute-start | bytes 1572872 | tf_op jit(solution)/shard_map/ppermute | solution.py:60
  7.2 2.5 %shard_map.93 = (bf16[4,2,128,128]{3,2,1,0:T(8,128)(2,1)S(1)}, bf16[256,256]{1,0:T(8,128)(2,1)S(1)}, bf16[1024,256]{1,0:T(8,128)(2,1)S(1)}, bf16[256,256]{1,0:T(8,128)(2,1)S(1)}) custom-call(bf16[128,1024]{1,0:T(8,128)(2,1)} %bitcast.16, bf16[128,1024]{1,0:T(8,128)(2,1)} %bitcast.9, bf16[128,1024]{1,0:T(8,128)(2,1)} %bitcast.13, ...), custom_call_target="tpu_custom_call" | custom-call | flops 1 | bytes 1 | tf_op jit(solution)/shard_map/pallas_call | solution.py:42
  9.8 0.5 collective-permute-start.2
  10.3 1.5 %collective-permute-done.2.refs_2_.refs_5_ = bf16[256,256]{1,0:T(8,128)(2,1)S(1)} collective-permute-done((bf16[256,256]{1,0:T(8,128)(2,1)S(1)}, bf16[256,256]{1,0:T(8,128)(2,1)S(1)}, u32[]{:S(2)}, u32[]{:S(2)}) %collective-permute-start.2) | collective-permute-done | bytes 131104 | tf_op jit(solution)/shard_map/ppermute | solution.py:60
  11.9 1.6 %collective-permute-start.7 = (bf16[128,256]{1,0:T(8,128)(2,1)S(1)}, bf16[128,256]{1,0:T(8,128)(2,1)S(1)}, u32[]{:S(2)}, u32[]{:S(2)}) collective-permute-start(bf16[128,256]{1,0:T(8,128)(2,1)S(1)} %shard_map.95.refs_2_.refs_0_), channel_id=1, source_target_pairs={{0,4},{1,5},{2,6},{3,7},{4,0},{5,1},{6,2},{7,3},{8,12},{9,13},{10,... | collective-permute-start | bytes 196616 | tf_op jit(solution)/shard_map/ppermute | solution.py:60
  13.5 0.7 %collective-permute-done.4.refs_2_ = bf16[128,1024]{1,0:T(8,128)(2,1)S(1)} collective-permute-done((bf16[128,1024]{1,0:T(8,128)(2,1)}, bf16[128,1024]{1,0:T(8,128)(2,1)S(1)}, u32[]{:S(2)}, u32[]{:S(2)}) %collective-permute-start.4) | collective-permute-done | bytes 262176 | tf_op jit(solution)/shard_map/ppermute | solution.py:60
  14.3 1.7 %collective-permute-start.3 = (bf16[512,256]{1,0:T(8,128)(2,1)S(1)}, bf16[512,256]{1,0:T(8,128)(2,1)S(1)}, u32[]{:S(2)}, u32[]{:S(2)}) collective-permute-start(bf16[512,256]{1,0:T(8,128)(2,1)S(1)} %shard_map.96.refs_2_), channel_id=1, source_target_pairs={{0,2},{1,3},{2,0},{3,1},{4,6},{5,7},{6,4},{7,5},{8,10},{9,11},{10,... | collective-permute-start | bytes 786440 | tf_op jit(solution)/shard_map/ppermute | solution.py:60
  16.2 2.6 %collective-permute-start.8 = (bf16[128,256]{1,0:T(8,128)(2,1)S(1)}, bf16[128,256]{1,0:T(8,128)(2,1)S(1)}, u32[]{:S(2)}, u32[]{:S(2)}) collective-permute-start(bf16[128,256]{1,0:T(8,128)(2,1)S(1)} %shard_map.97.refs_6_), channel_id=1, source_target_pairs={{0,8},{1,9},{2,10},{3,11},{4,12},{5,13},{6,14},{7,15},{8,0},{9,1},... | collective-permute-start | bytes 196616 | tf_op jit(solution)/shard_map/ppermute | solution.py:60
  18.9 1.5 %shard_map.98 = (f32[4,128,256]{2,1,0:T(8,128)S(1)}, bf16[4,128,1024]{2,1,0:T(8,128)(2,1)S(1)}) custom-call(bf16[1024,256]{1,0:T(8,128)(2,1)S(1)} %collective-permute-done.refs_0_.refs_1_, bf16[128,1024]{1,0:T(8,128)(2,1)} %bitcast.3.refs_3_.refs_1_, bf16[128,1024]{1,0:T(8,128)(2,1)S(1)} %collective-permute-done.4.refs_2_, ...), custom_call_target="tpu_custom_call" | custom-call | flops 1 | bytes 1 | tf_op jit(solution)/shard_map/pallas_call | solution.py:42
  20.4 2.4 %collective-permute-done.8.refs_8_ = bf16[128,256]{1,0:T(8,128)(2,1)S(1)} collective-permute-done((bf16[128,256]{1,0:T(8,128)(2,1)S(1)}, bf16[128,256]{1,0:T(8,128)(2,1)S(1)}, u32[]{:S(2)}, u32[]{:S(2)}) %collective-permute-start.8) | collective-permute-done | bytes 65568 | tf_op jit(solution)/shard_map/ppermute | solution.py:60
  23.0 0.8 %shard_map.99 = (bf16[4,128,256]{2,1,0:T(8,128)(2,1)S(1)}, bf16[384,256]{1,0:T(8,128)(2,1)S(1)}, bf16[384,256]{1,0:T(8,128)(2,1)S(1)}, bf16[384,256]{1,0:T(8,128...) custom-call(bf16[256,256]{1,0:T(8,128)(2,1)S(1)} %get-tuple-element.44.refs_0_, ...), custom_call_target="tpu_custom_call" | custom-call | flops 10000000000 | bytes 1 | tf_op jit(solution)/shard_map/pallas_call | solution.py:42
  23.8 0.8 %shard_map.100 = (f32[512,256]{1,0:T(8,128)S(1)}, bf16[512,256]{1,0:T(8,128)(2,1)S(1)}) custom-call(bf16[4,128,1024]{2,1,0:T(8,128)(2,1)S(1)} %get-tuple-element.58.refs_0_, bf16[4,128,256]{2,1,0:T(8,128)(2,1)S(1)} %get-tuple-element.59.refs_1_, bf16[128,256]{1,0:T(8,128)(2,1)S(1)} %get-tuple-element.60.refs_2_.refs_0_, ...), custom_call_target="tpu_custom_call" | custom-call | flops 1 | bytes 1 | tf_op jit(solution)/shard_map/pallas_call | solution.py:42
  24.6 1.8 %collective-permute-start.13 = (bf16[512,256]{1,0:T(8,128)(2,1)S(1)}, bf16[512,256]{1,0:T(8,128)(2,1)S(1)}, u32[]{:S(2)}, u32[]{:S(2)}) collective-permute-start(bf16[512,256]{1,0:T(8,128)(2,1)S(1)} %get-tuple-element.62.refs_2_), channel_id=1, source_target_pairs={{0,16},{16,0},{1,17},{17,1},{2,18},{18,2},{3,19},{19,3},{4,20},{20... | collective-permute-start | bytes 786440 | tf_op jit(solution)/shard_map/ppermute | solution.py:60
  26.3 1.6 %collective-permute-start.14 = (bf16[128,256]{1,0:T(8,128)(2,1)S(1)}, bf16[128,256]{1,0:T(8,128)(2,1)S(1)}, u32[]{:S(2)}, u32[]{:S(2)}) collective-permute-start(bf16[128,256]{1,0:T(8,128)(2,1)S(1)} %get-tuple-element.60.refs_2_.refs_0_), channel_id=1, source_target_pairs={{0,4},{1,5},{2,6},{3,7},{4,0},{5,1},{6,2},{7,3},{8,12},{9,13},{10,... | collective-permute-start | bytes 196616 | tf_op jit(solution)/shard_map/ppermute | solution.py:60
  27.9 2.7 %collective-permute-done.14.refs_1_.refs_0_ = bf16[128,256]{1,0:T(8,128)(2,1)S(1)} collective-permute-done((bf16[128,256]{1,0:T(8,128)(2,1)S(1)}, bf16[128,256]{1,0:T(8,128)(2,1)S(1)}, u32[]{:S(2)}, u32[]{:S(2)}) %collective-permute-start.14) | collective-permute-done | bytes 65568 | tf_op jit(solution)/shard_map/ppermute | solution.py:60
  30.6 2.7 %collective-permute-start.16 = (bf16[128,256]{1,0:T(8,128)(2,1)S(1)}, bf16[128,256]{1,0:T(8,128)(2,1)S(1)}, u32[]{:S(2)}, u32[]{:S(2)}) collective-permute-start(bf16[128,256]{1,0:T(8,128)(2,1)S(1)} %shard_map.101.refs_2_), channel_id=1, source_target_pairs={{0,8},{1,9},{2,10},{3,11},{4,12},{5,13},{6,14},{7,15},{8,0},{9,1},... | collective-permute-start | bytes 196616 | tf_op jit(solution)/shard_map/ppermute | solution.py:60
  33.3 1.5 %collective-permute-start.10 = (bf16[384,256]{1,0:T(8,128)(2,1)S(1)}, bf16[384,256]{1,0:T(8,128)(2,1)S(1)}, u32[]{:S(2)}, u32[]{:S(2)}) collective-permute-start(bf16[384,256]{1,0:T(8,128)(2,1)S(1)} %get-tuple-element.54), channel_id=1, source_target_pairs={{0,2},{1,3},{2,0},{3,1},{4,6},{5,7},{6,4},{7,5},{8,10},{9,11},{10,... | collective-permute-start | bytes 589832 | tf_op jit(solution)/shard_map/ppermute | solution.py:60
  34.8 0.3 collective-permute-start.11
  35.2 1.6 %collective-permute-start.15 = (bf16[256,256]{1,0:T(8,128)(2,1)S(1)}, bf16[256,256]{1,0:T(8,128)(2,1)S(1)}, u32[]{:S(2)}, u32[]{:S(2)}) collective-permute-start(bf16[256,256]{1,0:T(8,128)(2,1)S(1)} %get-tuple-element.64.refs_3_), channel_id=1, source_target_pairs={{0,4},{1,5},{2,6},{3,7},{4,0},{5,1},{6,2},{7,3},{8,12},{9,13},{10,... | collective-permute-start | bytes 393224 | tf_op jit(solution)/shard_map/ppermute | solution.py:60
  37.0 1.6 %collective-permute-start.17 = (bf16[256,256]{1,0:T(8,128)(2,1)S(1)}, bf16[256,256]{1,0:T(8,128)(2,1)S(1)}, u32[]{:S(2)}, u32[]{:S(2)}) collective-permute-start(bf16[256,256]{1,0:T(8,128)(2,1)S(1)} %get-tuple-element.66.refs_2_), channel_id=1, source_target_pairs={{0,2},{1,3},{2,0},{3,1},{4,6},{5,7},{6,4},{7,5},{8,10},{9,11},{10,... | collective-permute-start | bytes 393224 | tf_op jit(solution)/shard_map/ppermute | solution.py:60
  38.6 2.4 %collective-permute-done.15.refs_1_ = bf16[256,256]{1,0:T(8,128)(2,1)S(1)} collective-permute-done((bf16[256,256]{1,0:T(8,128)(2,1)S(1)}, bf16[256,256]{1,0:T(8,128)(2,1)S(1)}, u32[]{:S(2)}, u32[]{:S(2)}) %collective-permute-start.15) | collective-permute-done | bytes 131104 | tf_op jit(solution)/shard_map/ppermute | solution.py:60
  41.0 0.4 collective-permute-start.18
  41.4 3.0 %collective-permute-done.11.refs_3_ = bf16[384,256]{1,0:T(8,128)(2,1)S(1)} collective-permute-done((bf16[384,256]{1,0:T(8,128)(2,1)S(1)}, bf16[384,256]{1,0:T(8,128)(2,1)S(1)}, u32[]{:S(2)}, u32[]{:S(2)}) %collective-permute-start.11) | collective-permute-done | bytes 196640 | tf_op jit(solution)/shard_map/ppermute | solution.py:60
  44.5 2.8 %shard_map.105 = (bf16[128,1024]{1,0:T(8,128)(2,1)}, bf16[128,1024]{1,0:T(8,128)(2,1)}, f32[4,128,256]{2,1,0:T(8,128)S(1)}, f32[4,128,256]{2,1,0:T(8,128)S(1)}, bf16[128,1024]{1,0:T(8,128)(2,1)S(1)}) custom-call(bf16[384,256]{1,0:T(8,128)(2,1)S(1)} %get-tuple-element.52.refs_0_, bf16[384,256]{1,0:T(8,128)(2,1)S(1)} %collective-permute-done.9.refs_1_, ...), custom_call_target="tpu_custom_call" | custom-call | flops 1 | bytes 1 | tf_op jit(solution)/shard_map/pallas_call | solution.py:42
  47.3 1.6 %collective-permute-start.20 = (f32[64,256]{1,0:T(8,128)S(1)}, f32[64,256]{1,0:T(8,128)S(1)}, u32[]{:S(2)}, u32[]{:S(2)}) collective-permute-start(f32[64,256]{1,0:T(8,128)S(1)} %get-tuple-element.73.refs_2_), channel_id=1, source_target_pairs={{0,2},{1,3},{2,0},{3,1},{4,6},{5,7},{6,4},{7,5},{8,10},{9,11},{10,... | collective-permute-start | bytes 196616 | tf_op jit(solution)/shard_map/ppermute | solution.py:60
  48.9 0.4 collective-permute-start.19
  49.3 2.7 %collective-permute-done.20.refs_1_ = f32[64,256]{1,0:T(8,128)S(1)} collective-permute-done((f32[64,256]{1,0:T(8,128)S(1)}, f32[64,256]{1,0:T(8,128)S(1)}, u32[]{:S(2)}, u32[]{:S(2)}) %collective-permute-start.20) | collective-permute-done | bytes 65568 | tf_op jit(solution)/shard_map/ppermute | solution.py:60
  52.1 1.2 %collective-permute-done.21.refs_1_ = f32[64,256]{1,0:T(8,128)S(1)} collective-permute-done((f32[64,256]{1,0:T(8,128)S(1)}, f32[64,256]{1,0:T(8,128)S(1)}, u32[]{:S(2)}, u32[]{:S(2)}) %collective-permute-start.21) | collective-permute-done | bytes 65568 | tf_op jit(solution)/shard_map/ppermute | solution.py:60
  53.3 0.7 %shard_map.110 = f32[32,1024]{1,0:T(8,128)} custom-call(f32[64,256]{1,0:T(8,128)S(1)} %get-tuple-element.80.refs_0_, f32[64,256]{1,0:T(8,128)S(1)} %collective-permute-done.21.refs_1_, f32[64,256]{1,0:T(8,128)S(1)} %get-tuple-element.77.refs_7_.refs_2_), custom_call_target="tpu_custom_call" | custom-call | flops 1 | bytes 1 | tf_op jit(solution)/shard_map/pallas_call | solution.py:42
  54.0 1.1 %shard_map.109 = (bf16[128,1024]{1,0:T(8,128)(2,1)}, bf16[128,1024]{1,0:T(8,128)(2,1)}) custom-call(bf16[256,256]{1,0:T(8,128)(2,1)S(1)} %get-tuple-element.70.refs_0_, bf16[256,256]{1,0:T(8,128)(2,1)S(1)} %collective-permute-done.17.refs_1_, bf16[256,256]{1,0:T(8,128)(2,1)S(1)} %collective-permute-done.19.refs_2_, bf16[128,1024]{1,0:T(8,128)(2,1)S(1)} %bitcast.11, ...), custom_call_target="tpu_custom_call" | custom-call | flops 1 | bytes 1 | tf_op jit(solution)/shard_map/pallas_call | solution.py:42
  (39 shorter events, 1.0 us)
Async XLA Ops:
  2.1 7.6 %collective-permute-start.1 = (bf16[256,256]{1,0:T(8,128)(2,1)S(1)}, bf16[256,256]{1,0:T(8,128)(2,1)S(1)}, u32[]{:S(2)}, u32[]{:S(2)}) collective-permute-start(bf16[256,256]{1,0:T(8,128)(2,1)S(1)} %get-tuple-element.48), channel_id=1, source_target_pairs={{0,2},{1,3},{2,0},{3,1},{4,6},{5,7},{6,4},{7,5},{8,10},{9,11},{10,... | collective-permute-start | bytes 393224 | tf_op jit(solution)/shard_map/ppermute | solution.py:60
  5.2 9.1 %collective-permute-start.4 = (bf16[128,1024]{1,0:T(8,128)(2,1)}, bf16[128,1024]{1,0:T(8,128)(2,1)S(1)}, u32[]{:S(2)}, u32[]{:S(2)}) collective-permute-start(bf16[128,1024]{1,0:T(8,128)(2,1)} %bitcast.3.refs_3_.refs_1_), channel_id=1, source_target_pairs={{0,2},{1,3},{2,0},{3,1},{4,6},{5,7},{6,4},{7,5},{8,10},{9,11},{10,... | collective-permute-start | bytes 786440 | tf_op jit(solution)/shard_map/ppermute | solution.py:60
  5.2 13.6 %collective-permute-start.6 = (bf16[2,512,256]{2,1,0:T(8,128)(2,1)S(1)}, bf16[2,512,256]{2,1,0:T(8,128)(2,1)S(1)}, u32[]{:S(2)}, u32[]{:S(2)}) collective-permute-start(bf16[2,512,256]{2,1,0:T(8,128)(2,1)S(1)} %get-tuple-element.50.refs_4_), channel_id=1, source_target_pairs={{0,16},{16,0},{1,17},{17,1},{2,18},{18,2},{3,19},{19,3},{4,20},{20... | collective-permute-start | bytes 1572872 | tf_op jit(solution)/shard_map/ppermute | solution.py:60
  9.7 3.8 %collective-permute-start = (bf16[1024,256]{1,0:T(8,128)(2,1)S(1)}, bf16[1024,256]{1,0:T(8,128)(2,1)S(1)}, u32[]{:S(2)}, u32[]{:S(2)}) collective-permute-start(bf16[1024,256]{1,0:T(8,128)(2,1)S(1)} %get-tuple-element.45), channel_id=1, source_target_pairs={{0,1},{1,0},{2,3},{3,2},{4,5},{5,4},{6,7},{7,6},{8,9},{9,8},{10,11... | collective-permute-start | bytes 1572872 | tf_op jit(solution)/shard_map/ppermute | solution.py:60
  9.8 2.1 %collective-permute-start.2 = (bf16[256,256]{1,0:T(8,128)(2,1)S(1)}, bf16[256,256]{1,0:T(8,128)(2,1)S(1)}, u32[]{:S(2)}, u32[]{:S(2)}) collective-permute-start(bf16[256,256]{1,0:T(8,128)(2,1)S(1)} %shard_map.94.refs_3_), channel_id=1, source_target_pairs={{0,1},{1,0},{2,3},{3,2},{4,5},{5,4},{6,7},{7,6},{8,9},{9,8},{10,11... | collective-permute-start | bytes 393224 | tf_op jit(solution)/shard_map/ppermute | solution.py:60
  11.9 4.3 %collective-permute-start.7 = (bf16[128,256]{1,0:T(8,128)(2,1)S(1)}, bf16[128,256]{1,0:T(8,128)(2,1)S(1)}, u32[]{:S(2)}, u32[]{:S(2)}) collective-permute-start(bf16[128,256]{1,0:T(8,128)(2,1)S(1)} %shard_map.95.refs_2_.refs_0_), channel_id=1, source_target_pairs={{0,4},{1,5},{2,6},{3,7},{4,0},{5,1},{6,2},{7,3},{8,12},{9,13},{10,... | collective-permute-start | bytes 196616 | tf_op jit(solution)/shard_map/ppermute | solution.py:60
  14.3 4.6 %collective-permute-start.5 = (bf16[128,1024]{1,0:T(8,128)(2,1)S(1)}, bf16[128,1024]{1,0:T(8,128)(2,1)S(1)}, u32[]{:S(2)}, u32[]{:S(2)}) collective-permute-start(bf16[128,1024]{1,0:T(8,128)(2,1)S(1)} %collective-permute-done.4.refs_2_), channel_id=1, source_target_pairs={{0,1},{1,0},{2,3},{3,2},{4,5},{5,4},{6,7},{7,6},{8,9},{9,8},{10,11... | collective-permute-start | bytes 786440 | tf_op jit(solution)/shard_map/ppermute | solution.py:60
  14.3 8.7 %collective-permute-start.3 = (bf16[512,256]{1,0:T(8,128)(2,1)S(1)}, bf16[512,256]{1,0:T(8,128)(2,1)S(1)}, u32[]{:S(2)}, u32[]{:S(2)}) collective-permute-start(bf16[512,256]{1,0:T(8,128)(2,1)S(1)} %shard_map.96.refs_2_), channel_id=1, source_target_pairs={{0,2},{1,3},{2,0},{3,1},{4,6},{5,7},{6,4},{7,5},{8,10},{9,11},{10,... | collective-permute-start | bytes 786440 | tf_op jit(solution)/shard_map/ppermute | solution.py:60
  16.2 6.6 %collective-permute-start.8 = (bf16[128,256]{1,0:T(8,128)(2,1)S(1)}, bf16[128,256]{1,0:T(8,128)(2,1)S(1)}, u32[]{:S(2)}, u32[]{:S(2)}) collective-permute-start(bf16[128,256]{1,0:T(8,128)(2,1)S(1)} %shard_map.97.refs_6_), channel_id=1, source_target_pairs={{0,8},{1,9},{2,10},{3,11},{4,12},{5,13},{6,14},{7,15},{8,0},{9,1},... | collective-permute-start | bytes 196616 | tf_op jit(solution)/shard_map/ppermute | solution.py:60
  20.4 3.4 %collective-permute-start.12 = (bf16[2,512,256]{2,1,0:T(8,128)(2,1)S(1)}, bf16[2,512,256]{2,1,0:T(8,128)(2,1)S(1)}, u32[]{:S(2)}, u32[]{:S(2)}) collective-permute-start(bf16[2,512,256]{2,1,0:T(8,128)(2,1)S(1)} %collective-permute-done.6.refs_5_.refs_9_), channel_id=1, source_target_pairs={{0,1},{1,0},{2,3},{3,2},{4,5},{5,4},{6,7},{7,6},{8,9},{9,8},{10,11... | collective-permute-start | bytes 1572872 | tf_op jit(solution)/shard_map/ppermute | solution.py:60
  24.6 10.6 %collective-permute-start.13 = (bf16[512,256]{1,0:T(8,128)(2,1)S(1)}, bf16[512,256]{1,0:T(8,128)(2,1)S(1)}, u32[]{:S(2)}, u32[]{:S(2)}) collective-permute-start(bf16[512,256]{1,0:T(8,128)(2,1)S(1)} %get-tuple-element.62.refs_2_), channel_id=1, source_target_pairs={{0,16},{16,0},{1,17},{17,1},{2,18},{18,2},{3,19},{19,3},{4,20},{20... | collective-permute-start | bytes 786440 | tf_op jit(solution)/shard_map/ppermute | solution.py:60
  26.3 4.3 %collective-permute-start.14 = (bf16[128,256]{1,0:T(8,128)(2,1)S(1)}, bf16[128,256]{1,0:T(8,128)(2,1)S(1)}, u32[]{:S(2)}, u32[]{:S(2)}) collective-permute-start(bf16[128,256]{1,0:T(8,128)(2,1)S(1)} %get-tuple-element.60.refs_2_.refs_0_), channel_id=1, source_target_pairs={{0,4},{1,5},{2,6},{3,7},{4,0},{5,1},{6,2},{7,3},{8,12},{9,13},{10,... | collective-permute-start | bytes 196616 | tf_op jit(solution)/shard_map/ppermute | solution.py:60
  30.6 6.2 %collective-permute-start.16 = (bf16[128,256]{1,0:T(8,128)(2,1)S(1)}, bf16[128,256]{1,0:T(8,128)(2,1)S(1)}, u32[]{:S(2)}, u32[]{:S(2)}) collective-permute-start(bf16[128,256]{1,0:T(8,128)(2,1)S(1)} %shard_map.101.refs_2_), channel_id=1, source_target_pairs={{0,8},{1,9},{2,10},{3,11},{4,12},{5,13},{6,14},{7,15},{8,0},{9,1},... | collective-permute-start | bytes 196616 | tf_op jit(solution)/shard_map/ppermute | solution.py:60
  33.3 8.1 %collective-permute-start.9 = (bf16[384,256]{1,0:T(8,128)(2,1)S(1)}, bf16[384,256]{1,0:T(8,128)(2,1)S(1)}, u32[]{:S(2)}, u32[]{:S(2)}) collective-permute-start(bf16[384,256]{1,0:T(8,128)(2,1)S(1)} %get-tuple-element.53), channel_id=1, source_target_pairs={{0,1},{1,0},{2,3},{3,2},{4,5},{5,4},{6,7},{7,6},{8,9},{9,8},{10,11... | collective-permute-start | bytes 589832 | tf_op jit(solution)/shard_map/ppermute | solution.py:60
  33.3 8.1 %collective-permute-start.10 = (bf16[384,256]{1,0:T(8,128)(2,1)S(1)}, bf16[384,256]{1,0:T(8,128)(2,1)S(1)}, u32[]{:S(2)}, u32[]{:S(2)}) collective-permute-start(bf16[384,256]{1,0:T(8,128)(2,1)S(1)} %get-tuple-element.54), channel_id=1, source_target_pairs={{0,2},{1,3},{2,0},{3,1},{4,6},{5,7},{6,4},{7,5},{8,10},{9,11},{10,... | collective-permute-start | bytes 589832 | tf_op jit(solution)/shard_map/ppermute | solution.py:60
  34.8 9.6 %collective-permute-start.11 = (bf16[384,256]{1,0:T(8,128)(2,1)S(1)}, bf16[384,256]{1,0:T(8,128)(2,1)S(1)}, u32[]{:S(2)}, u32[]{:S(2)}) collective-permute-start(bf16[384,256]{1,0:T(8,128)(2,1)S(1)} %get-tuple-element.55), channel_id=1, source_target_pairs={{0,3},{1,2},{2,1},{3,0},{4,7},{5,6},{6,5},{7,4},{8,11},{9,10},{10,... | collective-permute-start | bytes 589832 | tf_op jit(solution)/shard_map/ppermute | solution.py:60
  35.2 5.8 %collective-permute-start.15 = (bf16[256,256]{1,0:T(8,128)(2,1)S(1)}, bf16[256,256]{1,0:T(8,128)(2,1)S(1)}, u32[]{:S(2)}, u32[]{:S(2)}) collective-permute-start(bf16[256,256]{1,0:T(8,128)(2,1)S(1)} %get-tuple-element.64.refs_3_), channel_id=1, source_target_pairs={{0,4},{1,5},{2,6},{3,7},{4,0},{5,1},{6,2},{7,3},{8,12},{9,13},{10,... | collective-permute-start | bytes 393224 | tf_op jit(solution)/shard_map/ppermute | solution.py:60
  36.8 7.6 %copy-start = (bf16[512,1024]{1,0:T(8,128)(2,1)S(1)}, bf16[512,1024]{1,0:T(8,128)(2,1)}, u32[]{:S(2)}) copy-start(bf16[512,1024]{1,0:T(8,128)(2,1)} %refs_8_.1) | copy-start | bytes 3145732
  36.8 7.6 %copy-start.3 = (bf16[1,128,1024]{2,1,0:T(8,128)(2,1)S(1)}, bf16[1,128,1024]{2,1,0:T(8,128)(2,1)}, u32[]{:S(2)}) copy-start(bf16[1,128,1024]{2,1,0:T(8,128)(2,1)} %param.5) | copy-start | bytes 786436
  37.0 11.9 %collective-permute-start.17 = (bf16[256,256]{1,0:T(8,128)(2,1)S(1)}, bf16[256,256]{1,0:T(8,128)(2,1)S(1)}, u32[]{:S(2)}, u32[]{:S(2)}) collective-permute-start(bf16[256,256]{1,0:T(8,128)(2,1)S(1)} %get-tuple-element.66.refs_2_), channel_id=1, source_target_pairs={{0,2},{1,3},{2,0},{3,1},{4,6},{5,7},{6,4},{7,5},{8,10},{9,11},{10,... | collective-permute-start | bytes 393224 | tf_op jit(solution)/shard_map/ppermute | solution.py:60
  41.0 3.5 %copy-start.1 = (bf16[1,128,1024]{2,1,0:T(8,128)(2,1)S(1)}, bf16[1,128,1024]{2,1,0:T(8,128)(2,1)}, u32[]{:S(2)}) copy-start(bf16[1,128,1024]{2,1,0:T(8,128)(2,1)} %param.6) | copy-start | bytes 786436
  41.0 3.5 %copy-start.2 = (bf16[1,128,1024]{2,1,0:T(8,128)(2,1)S(1)}, bf16[1,128,1024]{2,1,0:T(8,128)(2,1)}, u32[]{:S(2)}) copy-start(bf16[1,128,1024]{2,1,0:T(8,128)(2,1)} %param.7) | copy-start | bytes 786436
  41.0 6.3 %collective-permute-start.18 = (bf16[128,256]{1,0:T(8,128)(2,1)S(1)}, bf16[128,256]{1,0:T(8,128)(2,1)S(1)}, u32[]{:S(2)}, u32[]{:S(2)}) collective-permute-start(bf16[128,256]{1,0:T(8,128)(2,1)S(1)} %get-tuple-element.67.refs_11_), channel_id=1, source_target_pairs={{0,8},{1,9},{2,10},{3,11},{4,12},{5,13},{6,14},{7,15},{8,0},{9,1},... | collective-permute-start | bytes 196616 | tf_op jit(solution)/shard_map/ppermute | solution.py:60
  47.3 4.7 %collective-permute-start.20 = (f32[64,256]{1,0:T(8,128)S(1)}, f32[64,256]{1,0:T(8,128)S(1)}, u32[]{:S(2)}, u32[]{:S(2)}) collective-permute-start(f32[64,256]{1,0:T(8,128)S(1)} %get-tuple-element.73.refs_2_), channel_id=1, source_target_pairs={{0,2},{1,3},{2,0},{3,1},{4,6},{5,7},{6,4},{7,5},{8,10},{9,11},{10,... | collective-permute-start | bytes 196616 | tf_op jit(solution)/shard_map/ppermute | solution.py:60
  48.9 5.1 %collective-permute-start.19 = (bf16[256,256]{1,0:T(8,128)(2,1)S(1)}, bf16[256,256]{1,0:T(8,128)(2,1)S(1)}, u32[]{:S(2)}, u32[]{:S(2)}) collective-permute-start(bf16[256,256]{1,0:T(8,128)(2,1)S(1)} %shard_map.107.refs_2_), channel_id=1, source_target_pairs={{0,1},{1,0},{2,3},{3,2},{4,5},{5,4},{6,7},{7,6},{8,9},{9,8},{10,11... | collective-permute-start | bytes 393224 | tf_op jit(solution)/shard_map/ppermute | solution.py:60
  52.0 1.3 %collective-permute-start.21 = (f32[64,256]{1,0:T(8,128)S(1)}, f32[64,256]{1,0:T(8,128)S(1)}, u32[]{:S(2)}, u32[]{:S(2)}) collective-permute-start(f32[64,256]{1,0:T(8,128)S(1)} %get-tuple-element.77.refs_7_.refs_2_), channel_id=1, source_target_pairs={{0,1},{1,0},{2,3},{3,2},{4,5},{5,4},{6,7},{7,6},{8,9},{9,8},{10,11... | collective-permute-start | bytes 196616 | tf_op jit(solution)/shard_map/ppermute | solution.py:60

commit v8 on v7

--- a/solution.py
+++ b/solution.py
@@ -378,7 +378,7 @@
     (far_tokens,) = call(pair_kernel, [((4 * rows, width), BF16)], message, far_tokens)
     cot_yc = near(after(cot_y, far_tokens), bits=1)
     far_tokens = near(far_tokens, bits=2)
-    before, _ = doubling(slab_kv, 2 * 10**9)
+    before, _ = doubling(slab_kv, 22 * 10**8)
     dnormed, cots = call(
         functools.partial(dnormed_kernel, dp),
         [((SLAB, rows, width), F32), ((SLAB, rows, outputs), BF16)],
@@ -401,14 +401,14 @@
         )
         got = flip(send, "dp", dp, 1)
     backs = [backs[0], *(near(backs[r], bits=r) for r in range(1, SLAB))]
-    behind, last_u = doubling(slab_u)
+    behind, last_u = doubling(slab_u, 10**9)
     if tuned:
         keep, send = call(
             split_kernel, [((2 * piece, width), F32), ((2 * piece, width), BF16)], keep, got, cost=1
         )
         got = near(send, bits=SLAB)
     later, later_far = call(
-        later_kernel, [((2 * DH, width), BF16)] * 2, *behind, u, cost=3 * 10**9,
+        later_kernel, [((2 * DH, width), BF16)] * 2, *behind, u, cost=10**9, wait=backs[1:],
         scratch=[pltpu.VMEM((SLAB, DH, width), F32)],
     )
     later_far = near(later_far, bits=2)
@@ -417,6 +417,8 @@
             split_again_kernel, [((piece, width), F32), ((piece, width), BF16)], keep, got, cost=1
         )
         got = near(send, bits=2 * SLAB)
+    (send,) = call(relay_kernel, [((2 * DH, width), BF16)], later, later_far)
+    later_core = near(send, bits=1)
     output, gq, gk_part, gv_part, own_normed = call(
         functools.partial(late_kernel, dp),
         [((rows, outputs), BF16), ((rows, features), BF16), ((SLAB, rows, width), F32),
@@ -429,15 +431,13 @@
             scratch=[pltpu.VMEM((piece, width), F32)],
         )
         got = near(share, bits=2)
-    (send,) = call(relay_kernel, [((2 * DH, width), BF16)], later, later_far)
-    later_core = near(send, bits=1)
-    if tuned:
-        keep, share = call(pass_kernel, [((piece // 2, width), F32)] * 2, keep, got)
-        got = near(share, bits=1)
     gk, gv = call(
         last_kernel, [((rows, features), BF16)] * 2,
         later, later_far, later_core, k, v, gk_part, gv_part, end=True,
     )
+    if tuned:
+        keep, share = call(pass_kernel, [((piece // 2, width), F32)] * 2, keep, got)
+        got = near(share, bits=1)
     if tuned:
         (grad_weight,) = call(
             functools.partial(finish_kernel, factor),

time: 55.3 us -> 52.8 us (0.955)
  waiting for transfers between devices: 17 us -> 12.7 us
  starting transfers between devices: 25.3 us -> 27.1 us
    ppermute x22, waiting for transfers between devices: 17 us -> 12.7 us  [flip(): return lax.ppermute(x, axis, [(i, i ^ bits) for i in range(count)])]
    ppermute x22, starting transfers between devices: 25.3 us -> 27.1 us  [flip(): return lax.ppermute(x, axis, [(i, i ^ bits) for i in range(count)])]
  transfers between devices with their start and end apart: 22 -> 22, of which waited for: 10 -> 10; matrix products, arithmetic and copies ran while one was open for 0% -> 0% of each run, Pallas kernels for 16% -> 17%
where the time goes in v8:
time: 52.8 us; the launch traced here: 52.6 us
  starting transfers between devices  27.1 us (51%)
  waiting for transfers between devices  12.7 us (24%)
  Pallas kernels  12 us (23%)
  between operations  0.83 us (2%)
    ppermute x22, starting transfers between devices, flip(): return lax.ppermute(x, axis, [(i, i ^ bits) for i in range(count)])  27.1 us
    ppermute x22, waiting for transfers between devices, flip(): return lax.ppermute(x, axis, [(i, i ^ bits) for i in range(count)])  12.7 us
    pallas_call x19, Pallas kernels, __call__(): pl.pallas_call(inner, out_shape=[jax.ShapeDtypeStruct(s, d) for s, d in o...  12 us
  transfers between devices with their start and end apart: 22, of which 10 were waited for; matrix products, arithmetic and copies ran while one was open for 0% of the time, Pallas kernels for 17%

profile of v8, /device:TPU:0, one launch (start us, length us, event | category | flops | bytes accessed | tf_op | source)
XLA Modules:
  0.0 52.6 jit_solution(14343653040971956676)
XLA Ops:
  0.6 1.5 %shard_map.92 = (f32[128,256]{1,0:T(8,128)S(1)}, bf16[128,256]{1,0:T(8,128)(2,1)S(1)}, bf16[256,256]{1,0:T(8,128)(2,1)S(1)}, bf16[2,512,256]{2,1,0:T(8,128)(2,1)S(1)}) custom-call(bf16[128,1024]{1,0:T(8,128)(2,1)} %bitcast.8, bf16[128,1024]{1,0:T(8,128)(2,1)} %bitcast.12, bf16[512,1024]{1,0:T(8,128)(2,1)} %refs_8_.1), custom_call_target="tpu_custom_call" | custom-call | flops 1 | bytes 1 | tf_op jit(solution)/shard_map/pallas_call | solution.py:42
  2.1 3.0 %collective-permute-start.1 = (bf16[256,256]{1,0:T(8,128)(2,1)S(1)}, bf16[256,256]{1,0:T(8,128)(2,1)S(1)}, u32[]{:S(2)}, u32[]{:S(2)}) collective-permute-start(bf16[256,256]{1,0:T(8,128)(2,1)S(1)} %get-tuple-element.48), channel_id=1, source_target_pairs={{0,2},{1,3},{2,0},{3,1},{4,6},{5,7},{6,4},{7,5},{8,10},{9,11},{10,... | collective-permute-start | bytes 393224 | tf_op jit(solution)/shard_map/ppermute | solution.py:60
  5.2 1.9 %collective-permute-start.6 = (bf16[2,512,256]{2,1,0:T(8,128)(2,1)S(1)}, bf16[2,512,256]{2,1,0:T(8,128)(2,1)S(1)}, u32[]{:S(2)}, u32[]{:S(2)}) collective-permute-start(bf16[2,512,256]{2,1,0:T(8,128)(2,1)S(1)} %get-tuple-element.50.refs_4_), channel_id=1, source_target_pairs={{0,16},{16,0},{1,17},{17,1},{2,18},{18,2},{3,19},{19,3},{4,20},{20... | collective-permute-start | bytes 1572872 | tf_op jit(solution)/shard_map/ppermute | solution.py:60
  7.2 2.5 %shard_map.93 = (bf16[4,2,128,128]{3,2,1,0:T(8,128)(2,1)S(1)}, bf16[256,256]{1,0:T(8,128)(2,1)S(1)}, bf16[1024,256]{1,0:T(8,128)(2,1)S(1)}, bf16[256,256]{1,0:T(8,128)(2,1)S(1)}) custom-call(bf16[128,1024]{1,0:T(8,128)(2,1)} %bitcast.16, bf16[128,1024]{1,0:T(8,128)(2,1)} %bitcast.9, bf16[128,1024]{1,0:T(8,128)(2,1)} %bitcast.13, ...), custom_call_target="tpu_custom_call" | custom-call | flops 1 | bytes 1 | tf_op jit(solution)/shard_map/pallas_call | solution.py:42
  9.8 0.5 %collective-permute-start.2 = (bf16[256,256]{1,0:T(8,128)(2,1)S(1)}, bf16[256,256]{1,0:T(8,128)(2,1)S(1)}, u32[]{:S(2)}, u32[]{:S(2)}) collective-permute-start(bf16[256,256]{1,0:T(8,128)(2,1)S(1)} %shard_map.94.refs_3_), channel_id=1, source_target_pairs={{0,1},{1,0},{2,3},{3,2},{4,5},{5,4},{6,7},{7,6},{8,9},{9,8},{10,11... | collective-permute-start | bytes 393224 | tf_op jit(solution)/shard_map/ppermute | solution.py:60
  10.3 1.5 %collective-permute-done.2.refs_2_.refs_5_ = bf16[256,256]{1,0:T(8,128)(2,1)S(1)} collective-permute-done((bf16[256,256]{1,0:T(8,128)(2,1)S(1)}, bf16[256,256]{1,0:T(8,128)(2,1)S(1)}, u32[]{:S(2)}, u32[]{:S(2)}) %collective-permute-start.2) | collective-permute-done | bytes 131104 | tf_op jit(solution)/shard_map/ppermute | solution.py:60
  11.9 1.6 %collective-permute-start.7 = (bf16[128,256]{1,0:T(8,128)(2,1)S(1)}, bf16[128,256]{1,0:T(8,128)(2,1)S(1)}, u32[]{:S(2)}, u32[]{:S(2)}) collective-permute-start(bf16[128,256]{1,0:T(8,128)(2,1)S(1)} %shard_map.95.refs_2_.refs_0_), channel_id=1, source_target_pairs={{0,4},{1,5},{2,6},{3,7},{4,0},{5,1},{6,2},{7,3},{8,12},{9,13},{10,... | collective-permute-start | bytes 196616 | tf_op jit(solution)/shard_map/ppermute | solution.py:60
  13.5 1.6 %collective-permute-start.3 = (bf16[512,256]{1,0:T(8,128)(2,1)S(1)}, bf16[512,256]{1,0:T(8,128)(2,1)S(1)}, u32[]{:S(2)}, u32[]{:S(2)}) collective-permute-start(bf16[512,256]{1,0:T(8,128)(2,1)S(1)} %shard_map.96.refs_2_), channel_id=1, source_target_pairs={{0,2},{1,3},{2,0},{3,1},{4,6},{5,7},{6,4},{7,5},{8,10},{9,11},{10,... | collective-permute-start | bytes 786440 | tf_op jit(solution)/shard_map/ppermute | solution.py:60
  15.1 1.1 %collective-permute-done.7.refs_1_.refs_7_ = bf16[128,256]{1,0:T(8,128)(2,1)S(1)} collective-permute-done((bf16[128,256]{1,0:T(8,128)(2,1)S(1)}, bf16[128,256]{1,0:T(8,128)(2,1)S(1)}, u32[]{:S(2)}, u32[]{:S(2)}) %collective-permute-start.7) | collective-permute-done | bytes 65568 | tf_op jit(solution)/shard_map/ppermute | solution.py:60
  16.2 2.6 %collective-permute-start.8 = (bf16[128,256]{1,0:T(8,128)(2,1)S(1)}, bf16[128,256]{1,0:T(8,128)(2,1)S(1)}, u32[]{:S(2)}, u32[]{:S(2)}) collective-permute-start(bf16[128,256]{1,0:T(8,128)(2,1)S(1)} %shard_map.97.refs_6_), channel_id=1, source_target_pairs={{0,8},{1,9},{2,10},{3,11},{4,12},{5,13},{6,14},{7,15},{8,0},{9,1},... | collective-permute-start | bytes 196616 | tf_op jit(solution)/shard_map/ppermute | solution.py:60
  18.9 1.5 %shard_map.98 = (f32[4,128,256]{2,1,0:T(8,128)S(1)}, bf16[4,128,1024]{2,1,0:T(8,128)(2,1)S(1)}) custom-call(bf16[1024,256]{1,0:T(8,128)(2,1)S(1)} %collective-permute-done.refs_0_.refs_1_, bf16[128,1024]{1,0:T(8,128)(2,1)} %bitcast.3.refs_3_.refs_1_, bf16[128,1024]{1,0:T(8,128)(2,1)S(1)} %collective-permute-done.4.refs_2_, ...), custom_call_target="tpu_custom_call" | custom-call | flops 1 | bytes 1 | tf_op jit(solution)/shard_map/pallas_call | solution.py:42
  20.4 1.0 %collective-permute-done.8.refs_8_ = bf16[128,256]{1,0:T(8,128)(2,1)S(1)} collective-permute-done((bf16[128,256]{1,0:T(8,128)(2,1)S(1)}, bf16[128,256]{1,0:T(8,128)(2,1)S(1)}, u32[]{:S(2)}, u32[]{:S(2)}) %collective-permute-start.8) | collective-permute-done | bytes 65568 | tf_op jit(solution)/shard_map/ppermute | solution.py:60
  21.5 0.2 collective-permute-done.3.refs_2_
  21.7 0.8 %shard_map.99 = (bf16[4,128,256]{2,1,0:T(8,128)(2,1)S(1)}, bf16[384,256]{1,0:T(8,128)(2,1)S(1)}, bf16[384,256]{1,0:T(8,128)(2,1)S(1)}, bf16[384,256]{1,0:T(8,128...) custom-call(bf16[256,256]{1,0:T(8,128)(2,1)S(1)} %get-tuple-element.44.refs_0_, ...), custom_call_target="tpu_custom_call" | custom-call | flops 10000000000 | bytes 1 | tf_op jit(solution)/shard_map/pallas_call | solution.py:42
  22.5 0.8 %shard_map.100 = (f32[512,256]{1,0:T(8,128)S(1)}, bf16[512,256]{1,0:T(8,128)(2,1)S(1)}) custom-call(bf16[4,128,1024]{2,1,0:T(8,128)(2,1)S(1)} %get-tuple-element.59.refs_0_, bf16[4,128,256]{2,1,0:T(8,128)(2,1)S(1)} %get-tuple-element.60.refs_1_, bf16[128,256]{1,0:T(8,128)(2,1)S(1)} %get-tuple-element.58.refs_2_.refs_0_, ...), custom_call_target="tpu_custom_call" | custom-call | flops 1 | bytes 1 | tf_op jit(solution)/shard_map/pallas_call | solution.py:42
  23.2 1.3 %collective-permute-start.15 = (bf16[512,256]{1,0:T(8,128)(2,1)S(1)}, bf16[512,256]{1,0:T(8,128)(2,1)S(1)}, u32[]{:S(2)}, u32[]{:S(2)}) collective-permute-start(bf16[512,256]{1,0:T(8,128)(2,1)S(1)} %get-tuple-element.61.refs_2_), channel_id=1, source_target_pairs={{0,16},{16,0},{1,17},{17,1},{2,18},{18,2},{3,19},{19,3},{4,20},{20... | collective-permute-start | bytes 786440 | tf_op jit(solution)/shard_map/ppermute | solution.py:60
  24.5 1.6 %collective-permute-start.13 = (bf16[128,256]{1,0:T(8,128)(2,1)S(1)}, bf16[128,256]{1,0:T(8,128)(2,1)S(1)}, u32[]{:S(2)}, u32[]{:S(2)}) collective-permute-start(bf16[128,256]{1,0:T(8,128)(2,1)S(1)} %get-tuple-element.58.refs_2_.refs_0_), channel_id=1, source_target_pairs={{0,4},{1,5},{2,6},{3,7},{4,0},{5,1},{6,2},{7,3},{8,12},{9,13},{10,... | collective-permute-start | bytes 196616 | tf_op jit(solution)/shard_map/ppermute | solution.py:60
  26.1 1.5 %collective-permute-start.10 = (bf16[384,256]{1,0:T(8,128)(2,1)S(1)}, bf16[384,256]{1,0:T(8,128)(2,1)S(1)}, u32[]{:S(2)}, u32[]{:S(2)}) collective-permute-start(bf16[384,256]{1,0:T(8,128)(2,1)S(1)} %get-tuple-element.54), channel_id=1, source_target_pairs={{0,2},{1,3},{2,0},{3,1},{4,6},{5,7},{6,4},{7,5},{8,10},{9,11},{10,... | collective-permute-start | bytes 589832 | tf_op jit(solution)/shard_map/ppermute | solution.py:60
  27.6 0.3 collective-permute-start.11
  28.0 0.8 %collective-permute-done.13.refs_1_.refs_0_ = bf16[128,256]{1,0:T(8,128)(2,1)S(1)} collective-permute-done((bf16[128,256]{1,0:T(8,128)(2,1)S(1)}, bf16[128,256]{1,0:T(8,128)(2,1)S(1)}, u32[]{:S(2)}, u32[]{:S(2)}) %collective-permute-start.13) | collective-permute-done | bytes 65568 | tf_op jit(solution)/shard_map/ppermute | solution.py:60
  28.8 2.7 %collective-permute-start.14 = (bf16[128,256]{1,0:T(8,128)(2,1)S(1)}, bf16[128,256]{1,0:T(8,128)(2,1)S(1)}, u32[]{:S(2)}, u32[]{:S(2)}) collective-permute-start(bf16[128,256]{1,0:T(8,128)(2,1)S(1)} %shard_map.101.refs_2_), channel_id=1, source_target_pairs={{0,8},{1,9},{2,10},{3,11},{4,12},{5,13},{6,14},{7,15},{8,0},{9,1},... | collective-permute-start | bytes 196616 | tf_op jit(solution)/shard_map/ppermute | solution.py:60
  31.6 1.9 %collective-permute-start.17 = (bf16[256,256]{1,0:T(8,128)(2,1)S(1)}, bf16[256,256]{1,0:T(8,128)(2,1)S(1)}, u32[]{:S(2)}, u32[]{:S(2)}) collective-permute-start(bf16[256,256]{1,0:T(8,128)(2,1)S(1)} %get-tuple-element.64.refs_3_), channel_id=1, source_target_pairs={{0,4},{1,5},{2,6},{3,7},{4,0},{5,1},{6,2},{7,3},{8,12},{9,13},{10,... | collective-permute-start | bytes 393224 | tf_op jit(solution)/shard_map/ppermute | solution.py:60
  33.4 0.4 collective-permute-done.10.refs_5_.refs_2_
  33.8 3.4 %collective-permute-done.11.refs_6_.refs_3_ = bf16[384,256]{1,0:T(8,128)(2,1)S(1)} collective-permute-done((bf16[384,256]{1,0:T(8,128)(2,1)S(1)}, bf16[384,256]{1,0:T(8,128)(2,1)S(1)}, u32[]{:S(2)}, u32[]{:S(2)}) %collective-permute-start.11) | collective-permute-done | bytes 196640 | tf_op jit(solution)/shard_map/ppermute | solution.py:60
  37.4 1.6 %collective-permute-start.16 = (bf16[256,256]{1,0:T(8,128)(2,1)S(1)}, bf16[256,256]{1,0:T(8,128)(2,1)S(1)}, u32[]{:S(2)}, u32[]{:S(2)}) collective-permute-start(bf16[256,256]{1,0:T(8,128)(2,1)S(1)} %get-tuple-element.66.refs_2_), channel_id=1, source_target_pairs={{0,2},{1,3},{2,0},{3,1},{4,6},{5,7},{6,4},{7,5},{8,10},{9,11},{10,... | collective-permute-start | bytes 393224 | tf_op jit(solution)/shard_map/ppermute | solution.py:60
  39.0 2.9 %collective-permute-start.19 = (bf16[128,256]{1,0:T(8,128)(2,1)S(1)}, bf16[128,256]{1,0:T(8,128)(2,1)S(1)}, u32[]{:S(2)}, u32[]{:S(2)}) collective-permute-start(bf16[128,256]{1,0:T(8,128)(2,1)S(1)} %get-tuple-element.68.refs_2_), channel_id=1, source_target_pairs={{0,8},{1,9},{2,10},{3,11},{4,12},{5,13},{6,14},{7,15},{8,0},{9,1},... | collective-permute-start | bytes 196616 | tf_op jit(solution)/shard_map/ppermute | solution.py:60
  41.9 1.1 %collective-permute-done.16.refs_1_ = bf16[256,256]{1,0:T(8,128)(2,1)S(1)} collective-permute-done((bf16[256,256]{1,0:T(8,128)(2,1)S(1)}, bf16[256,256]{1,0:T(8,128)(2,1)S(1)}, u32[]{:S(2)}, u32[]{:S(2)}) %collective-permute-start.16) | collective-permute-done | bytes 131104 | tf_op jit(solution)/shard_map/ppermute | solution.py:60
  43.2 2.8 %shard_map.106 = (bf16[128,1024]{1,0:T(8,128)(2,1)}, bf16[128,1024]{1,0:T(8,128)(2,1)}, f32[4,128,256]{2,1,0:T(8,128)S(1)}, f32[4,128,256]{2,1,0:T(8,128)S(1)}, bf16[128,1024]{1,0:T(8,128)(2,1)S(1)}) custom-call(bf16[384,256]{1,0:T(8,128)(2,1)S(1)} %get-tuple-element.52.refs_0_, bf16[384,256]{1,0:T(8,128)(2,1)S(1)} %collective-permute-done.9.refs_4_.refs_1_, ...), custom_call_target="tpu_custom_call" | custom-call | flops 1 | bytes 1 | tf_op jit(solution)/shard_map/pallas_call | solution.py:42
  46.1 1.6 %collective-permute-start.20 = (f32[64,256]{1,0:T(8,128)S(1)}, f32[64,256]{1,0:T(8,128)S(1)}, u32[]{:S(2)}, u32[]{:S(2)}) collective-permute-start(f32[64,256]{1,0:T(8,128)S(1)} %get-tuple-element.75.refs_7_.refs_2_), channel_id=1, source_target_pairs={{0,2},{1,3},{2,0},{3,1},{4,6},{5,7},{6,4},{7,5},{8,10},{9,11},{10,... | collective-permute-start | bytes 196616 | tf_op jit(solution)/shard_map/ppermute | solution.py:60
  47.7 3.0 %collective-permute-done.20.refs_1_ = f32[64,256]{1,0:T(8,128)S(1)} collective-permute-done((f32[64,256]{1,0:T(8,128)S(1)}, f32[64,256]{1,0:T(8,128)S(1)}, u32[]{:S(2)}, u32[]{:S(2)}) %collective-permute-start.20) | collective-permute-done | bytes 65568 | tf_op jit(solution)/shard_map/ppermute | solution.py:60
  50.7 1.2 %shard_map.108 = (bf16[128,1024]{1,0:T(8,128)(2,1)}, bf16[128,1024]{1,0:T(8,128)(2,1)}) custom-call(bf16[256,256]{1,0:T(8,128)(2,1)S(1)} %get-tuple-element.65.refs_0_, bf16[256,256]{1,0:T(8,128)(2,1)S(1)} %collective-permute-done.16.refs_1_, bf16[256,256]{1,0:T(8,128)(2,1)S(1)} %collective-permute-done.18.refs_2_, bf16[128,1024]{1,0:T(8,128)(2,1)S(1)} %bitcast.11, ...), custom_call_target="tpu_custom_call" | custom-call | flops 1 | bytes 1 | tf_op jit(solution)/shard_map/pallas_call | solution.py:42
  51.9 0.7 %shard_map.110 = f32[32,1024]{1,0:T(8,128)} custom-call(f32[64,256]{1,0:T(8,128)S(1)} %get-tuple-element.79.refs_0_, f32[64,256]{1,0:T(8,128)S(1)} %collective-permute-done.21.refs_1_, f32[64,256]{1,0:T(8,128)S(1)} %get-tuple-element.80.refs_2_), custom_call_target="tpu_custom_call" | custom-call | flops 1 | bytes 1 | tf_op jit(solution)/shard_map/pallas_call | solution.py:42
  (39 shorter events, 0.9 us)
Async XLA Ops:
  2.1 7.6 %collective-permute-start.1 = (bf16[256,256]{1,0:T(8,128)(2,1)S(1)}, bf16[256,256]{1,0:T(8,128)(2,1)S(1)}, u32[]{:S(2)}, u32[]{:S(2)}) collective-permute-start(bf16[256,256]{1,0:T(8,128)(2,1)S(1)} %get-tuple-element.48), channel_id=1, source_target_pairs={{0,2},{1,3},{2,0},{3,1},{4,6},{5,7},{6,4},{7,5},{8,10},{9,11},{10,... | collective-permute-start | bytes 393224 | tf_op jit(solution)/shard_map/ppermute | solution.py:60
  5.2 10.0 %collective-permute-start.4 = (bf16[128,1024]{1,0:T(8,128)(2,1)}, bf16[128,1024]{1,0:T(8,128)(2,1)S(1)}, u32[]{:S(2)}, u32[]{:S(2)}) collective-permute-start(bf16[128,1024]{1,0:T(8,128)(2,1)} %bitcast.3.refs_3_.refs_1_), channel_id=1, source_target_pairs={{0,2},{1,3},{2,0},{3,1},{4,6},{5,7},{6,4},{7,5},{8,10},{9,11},{10,... | collective-permute-start | bytes 786440 | tf_op jit(solution)/shard_map/ppermute | solution.py:60
  5.2 13.6 %collective-permute-start.6 = (bf16[2,512,256]{2,1,0:T(8,128)(2,1)S(1)}, bf16[2,512,256]{2,1,0:T(8,128)(2,1)S(1)}, u32[]{:S(2)}, u32[]{:S(2)}) collective-permute-start(bf16[2,512,256]{2,1,0:T(8,128)(2,1)S(1)} %get-tuple-element.50.refs_4_), channel_id=1, source_target_pairs={{0,16},{16,0},{1,17},{17,1},{2,18},{18,2},{3,19},{19,3},{4,20},{20... | collective-permute-start | bytes 1572872 | tf_op jit(solution)/shard_map/ppermute | solution.py:60
  9.7 3.8 %collective-permute-start = (bf16[1024,256]{1,0:T(8,128)(2,1)S(1)}, bf16[1024,256]{1,0:T(8,128)(2,1)S(1)}, u32[]{:S(2)}, u32[]{:S(2)}) collective-permute-start(bf16[1024,256]{1,0:T(8,128)(2,1)S(1)} %get-tuple-element.45), channel_id=1, source_target_pairs={{0,1},{1,0},{2,3},{3,2},{4,5},{5,4},{6,7},{7,6},{8,9},{9,8},{10,11... | collective-permute-start | bytes 1572872 | tf_op jit(solution)/shard_map/ppermute | solution.py:60
  9.8 2.1 %collective-permute-start.2 = (bf16[256,256]{1,0:T(8,128)(2,1)S(1)}, bf16[256,256]{1,0:T(8,128)(2,1)S(1)}, u32[]{:S(2)}, u32[]{:S(2)}) collective-permute-start(bf16[256,256]{1,0:T(8,128)(2,1)S(1)} %shard_map.94.refs_3_), channel_id=1, source_target_pairs={{0,1},{1,0},{2,3},{3,2},{4,5},{5,4},{6,7},{7,6},{8,9},{9,8},{10,11... | collective-permute-start | bytes 393224 | tf_op jit(solution)/shard_map/ppermute | solution.py:60
  11.9 4.3 %collective-permute-start.7 = (bf16[128,256]{1,0:T(8,128)(2,1)S(1)}, bf16[128,256]{1,0:T(8,128)(2,1)S(1)}, u32[]{:S(2)}, u32[]{:S(2)}) collective-permute-start(bf16[128,256]{1,0:T(8,128)(2,1)S(1)} %shard_map.95.refs_2_.refs_0_), channel_id=1, source_target_pairs={{0,4},{1,5},{2,6},{3,7},{4,0},{5,1},{6,2},{7,3},{8,12},{9,13},{10,... | collective-permute-start | bytes 196616 | tf_op jit(solution)/shard_map/ppermute | solution.py:60
  13.5 8.1 %collective-permute-start.3 = (bf16[512,256]{1,0:T(8,128)(2,1)S(1)}, bf16[512,256]{1,0:T(8,128)(2,1)S(1)}, u32[]{:S(2)}, u32[]{:S(2)}) collective-permute-start(bf16[512,256]{1,0:T(8,128)(2,1)S(1)} %shard_map.96.refs_2_), channel_id=1, source_target_pairs={{0,2},{1,3},{2,0},{3,1},{4,6},{5,7},{6,4},{7,5},{8,10},{9,11},{10,... | collective-permute-start | bytes 786440 | tf_op jit(solution)/shard_map/ppermute | solution.py:60
  15.1 3.8 %collective-permute-start.5 = (bf16[128,1024]{1,0:T(8,128)(2,1)S(1)}, bf16[128,1024]{1,0:T(8,128)(2,1)S(1)}, u32[]{:S(2)}, u32[]{:S(2)}) collective-permute-start(bf16[128,1024]{1,0:T(8,128)(2,1)S(1)} %collective-permute-done.4.refs_2_), channel_id=1, source_target_pairs={{0,1},{1,0},{2,3},{3,2},{4,5},{5,4},{6,7},{7,6},{8,9},{9,8},{10,11... | collective-permute-start | bytes 786440 | tf_op jit(solution)/shard_map/ppermute | solution.py:60
  16.2 5.3 %collective-permute-start.8 = (bf16[128,256]{1,0:T(8,128)(2,1)S(1)}, bf16[128,256]{1,0:T(8,128)(2,1)S(1)}, u32[]{:S(2)}, u32[]{:S(2)}) collective-permute-start(bf16[128,256]{1,0:T(8,128)(2,1)S(1)} %shard_map.97.refs_6_), channel_id=1, source_target_pairs={{0,8},{1,9},{2,10},{3,11},{4,12},{5,13},{6,14},{7,15},{8,0},{9,1},... | collective-permute-start | bytes 196616 | tf_op jit(solution)/shard_map/ppermute | solution.py:60
  20.4 2.1 %collective-permute-start.12 = (bf16[2,512,256]{2,1,0:T(8,128)(2,1)S(1)}, bf16[2,512,256]{2,1,0:T(8,128)(2,1)S(1)}, u32[]{:S(2)}, u32[]{:S(2)}) collective-permute-start(bf16[2,512,256]{2,1,0:T(8,128)(2,1)S(1)} %collective-permute-done.6.refs_5_.refs_9_), channel_id=1, source_target_pairs={{0,1},{1,0},{2,3},{3,2},{4,5},{5,4},{6,7},{7,6},{8,9},{9,8},{10,11... | collective-permute-start | bytes 1572872 | tf_op jit(solution)/shard_map/ppermute | solution.py:60
  23.2 8.3 %collective-permute-start.15 = (bf16[512,256]{1,0:T(8,128)(2,1)S(1)}, bf16[512,256]{1,0:T(8,128)(2,1)S(1)}, u32[]{:S(2)}, u32[]{:S(2)}) collective-permute-start(bf16[512,256]{1,0:T(8,128)(2,1)S(1)} %get-tuple-element.61.refs_2_), channel_id=1, source_target_pairs={{0,16},{16,0},{1,17},{17,1},{2,18},{18,2},{3,19},{19,3},{4,20},{20... | collective-permute-start | bytes 786440 | tf_op jit(solution)/shard_map/ppermute | solution.py:60
  24.5 4.3 %collective-permute-start.13 = (bf16[128,256]{1,0:T(8,128)(2,1)S(1)}, bf16[128,256]{1,0:T(8,128)(2,1)S(1)}, u32[]{:S(2)}, u32[]{:S(2)}) collective-permute-start(bf16[128,256]{1,0:T(8,128)(2,1)S(1)} %get-tuple-element.58.refs_2_.refs_0_), channel_id=1, source_target_pairs={{0,4},{1,5},{2,6},{3,7},{4,0},{5,1},{6,2},{7,3},{8,12},{9,13},{10,... | collective-permute-start | bytes 196616 | tf_op jit(solution)/shard_map/ppermute | solution.py:60
  26.1 7.3 %collective-permute-start.9 = (bf16[384,256]{1,0:T(8,128)(2,1)S(1)}, bf16[384,256]{1,0:T(8,128)(2,1)S(1)}, u32[]{:S(2)}, u32[]{:S(2)}) collective-permute-start(bf16[384,256]{1,0:T(8,128)(2,1)S(1)} %get-tuple-element.53), channel_id=1, source_target_pairs={{0,1},{1,0},{2,3},{3,2},{4,5},{5,4},{6,7},{7,6},{8,9},{9,8},{10,11... | collective-permute-start | bytes 589832 | tf_op jit(solution)/shard_map/ppermute | solution.py:60
  26.1 7.7 %collective-permute-start.10 = (bf16[384,256]{1,0:T(8,128)(2,1)S(1)}, bf16[384,256]{1,0:T(8,128)(2,1)S(1)}, u32[]{:S(2)}, u32[]{:S(2)}) collective-permute-start(bf16[384,256]{1,0:T(8,128)(2,1)S(1)} %get-tuple-element.54), channel_id=1, source_target_pairs={{0,2},{1,3},{2,0},{3,1},{4,6},{5,7},{6,4},{7,5},{8,10},{9,11},{10,... | collective-permute-start | bytes 589832 | tf_op jit(solution)/shard_map/ppermute | solution.py:60
  27.6 9.6 %collective-permute-start.11 = (bf16[384,256]{1,0:T(8,128)(2,1)S(1)}, bf16[384,256]{1,0:T(8,128)(2,1)S(1)}, u32[]{:S(2)}, u32[]{:S(2)}) collective-permute-start(bf16[384,256]{1,0:T(8,128)(2,1)S(1)} %get-tuple-element.55), channel_id=1, source_target_pairs={{0,3},{1,2},{2,1},{3,0},{4,7},{5,6},{6,5},{7,4},{8,11},{9,10},{10,... | collective-permute-start | bytes 589832 | tf_op jit(solution)/shard_map/ppermute | solution.py:60
  28.8 8.4 %collective-permute-start.14 = (bf16[128,256]{1,0:T(8,128)(2,1)S(1)}, bf16[128,256]{1,0:T(8,128)(2,1)S(1)}, u32[]{:S(2)}, u32[]{:S(2)}) collective-permute-start(bf16[128,256]{1,0:T(8,128)(2,1)S(1)} %shard_map.101.refs_2_), channel_id=1, source_target_pairs={{0,8},{1,9},{2,10},{3,11},{4,12},{5,13},{6,14},{7,15},{8,0},{9,1},... | collective-permute-start | bytes 196616 | tf_op jit(solution)/shard_map/ppermute | solution.py:60
  31.6 7.4 %collective-permute-start.17 = (bf16[256,256]{1,0:T(8,128)(2,1)S(1)}, bf16[256,256]{1,0:T(8,128)(2,1)S(1)}, u32[]{:S(2)}, u32[]{:S(2)}) collective-permute-start(bf16[256,256]{1,0:T(8,128)(2,1)S(1)} %get-tuple-element.64.refs_3_), channel_id=1, source_target_pairs={{0,4},{1,5},{2,6},{3,7},{4,0},{5,1},{6,2},{7,3},{8,12},{9,13},{10,... | collective-permute-start | bytes 393224 | tf_op jit(solution)/shard_map/ppermute | solution.py:60
  37.3 5.9 %copy-start = (bf16[512,1024]{1,0:T(8,128)(2,1)S(1)}, bf16[512,1024]{1,0:T(8,128)(2,1)}, u32[]{:S(2)}) copy-start(bf16[512,1024]{1,0:T(8,128)(2,1)} %refs_8_.1) | copy-start | bytes 3145732
  37.4 5.7 %collective-permute-start.16 = (bf16[256,256]{1,0:T(8,128)(2,1)S(1)}, bf16[256,256]{1,0:T(8,128)(2,1)S(1)}, u32[]{:S(2)}, u32[]{:S(2)}) collective-permute-start(bf16[256,256]{1,0:T(8,128)(2,1)S(1)} %get-tuple-element.66.refs_2_), channel_id=1, source_target_pairs={{0,2},{1,3},{2,0},{3,1},{4,6},{5,7},{6,4},{7,5},{8,10},{9,11},{10,... | collective-permute-start | bytes 393224 | tf_op jit(solution)/shard_map/ppermute | solution.py:60
  39.0 4.2 %copy-start.2 = (bf16[1,128,1024]{2,1,0:T(8,128)(2,1)S(1)}, bf16[1,128,1024]{2,1,0:T(8,128)(2,1)}, u32[]{:S(2)}) copy-start(bf16[1,128,1024]{2,1,0:T(8,128)(2,1)} %param.7) | copy-start | bytes 786436
  39.0 4.2 %copy-start.3 = (bf16[1,128,1024]{2,1,0:T(8,128)(2,1)S(1)}, bf16[1,128,1024]{2,1,0:T(8,128)(2,1)}, u32[]{:S(2)}) copy-start(bf16[1,128,1024]{2,1,0:T(8,128)(2,1)} %param.5) | copy-start | bytes 786436
  39.0 4.2 %copy-start.1 = (bf16[1,128,1024]{2,1,0:T(8,128)(2,1)S(1)}, bf16[1,128,1024]{2,1,0:T(8,128)(2,1)}, u32[]{:S(2)}) copy-start(bf16[1,128,1024]{2,1,0:T(8,128)(2,1)} %param.6) | copy-start | bytes 786436
  39.0 7.0 %collective-permute-start.19 = (bf16[128,256]{1,0:T(8,128)(2,1)S(1)}, bf16[128,256]{1,0:T(8,128)(2,1)S(1)}, u32[]{:S(2)}, u32[]{:S(2)}) collective-permute-start(bf16[128,256]{1,0:T(8,128)(2,1)S(1)} %get-tuple-element.68.refs_2_), channel_id=1, source_target_pairs={{0,8},{1,9},{2,10},{3,11},{4,12},{5,13},{6,14},{7,15},{8,0},{9,1},... | collective-permute-start | bytes 196616 | tf_op jit(solution)/shard_map/ppermute | solution.py:60
  43.1 7.6 %collective-permute-start.18 = (bf16[256,256]{1,0:T(8,128)(2,1)S(1)}, bf16[256,256]{1,0:T(8,128)(2,1)S(1)}, u32[]{:S(2)}, u32[]{:S(2)}) collective-permute-start(bf16[256,256]{1,0:T(8,128)(2,1)S(1)} %shard_map.105.refs_11_), channel_id=1, source_target_pairs={{0,1},{1,0},{2,3},{3,2},{4,5},{5,4},{6,7},{7,6},{8,9},{9,8},{10,11... | collective-permute-start | bytes 393224 | tf_op jit(solution)/shard_map/ppermute | solution.py:60
  46.1 4.5 %collective-permute-start.20 = (f32[64,256]{1,0:T(8,128)S(1)}, f32[64,256]{1,0:T(8,128)S(1)}, u32[]{:S(2)}, u32[]{:S(2)}) collective-permute-start(f32[64,256]{1,0:T(8,128)S(1)} %get-tuple-element.75.refs_7_.refs_2_), channel_id=1, source_target_pairs={{0,2},{1,3},{2,0},{3,1},{4,6},{5,7},{6,4},{7,5},{8,10},{9,11},{10,... | collective-permute-start | bytes 196616 | tf_op jit(solution)/shard_map/ppermute | solution.py:60
  50.6 1.3 %collective-permute-start.21 = (f32[64,256]{1,0:T(8,128)S(1)}, f32[64,256]{1,0:T(8,128)S(1)}, u32[]{:S(2)}, u32[]{:S(2)}) collective-permute-start(f32[64,256]{1,0:T(8,128)S(1)} %get-tuple-element.80.refs_2_), channel_id=1, source_target_pairs={{0,1},{1,0},{2,3},{3,2},{4,5},{5,4},{6,7},{7,6},{8,9},{9,8},{10,11... | collective-permute-start | bytes 196616 | tf_op jit(solution)/shard_map/ppermute | solution.py:60

commit v9 on v7

--- a/solution.py
+++ b/solution.py
@@ -103,13 +103,9 @@
         columns_ref[i] = w_ref[:, cut(member(2 * i), width)]
 
 
-def pack_kernel(q_hbm, k_hbm, v_hbm, c_hbm, *refs):
-    attend_ref, own_ref, message_ref, far_ref, q_ref, k_ref, v_ref, c_ref, sems = refs
-    copies = fetch([(q_hbm, q_ref), (k_hbm, k_ref), (v_hbm, v_ref), (c_hbm, c_ref)], sems)
+def pack_kernel(q_ref, k_ref, v_ref, c_ref, attend_ref, own_ref, message_ref, far_ref):
     block = q_ref.shape[0]
     width = q_ref.shape[1] // SLAB
-    for copy in copies[:3]:
-        copy.wait()
     mask = causal(block)
     places = (own_ref, message_ref.at[: 2 * block], far_ref, message_ref.at[2 * block : 4 * block])
     for r, out in enumerate(places):
@@ -119,7 +115,6 @@
             attend = jnp.where(mask, dot(q[:, head(h)], k[:, head(h)], 1, 1), 0.0).astype(BF16)
             attend_ref[r, h] = attend
             out[block:, head(h)] = dot(attend, v[:, head(h)], 1, 0).astype(BF16)
-    copies[3].wait()
     for i in range(c_ref.shape[1] // width):
         message_ref[part(4 + i, block), :] = c_ref[:, part(i, width)]
 
@@ -309,9 +304,9 @@
     total_ref[...] = own_ref[...] + got_ref[...].astype(F32)
     rows = keep_ref.shape[0] // 2
     for i, r in enumerate((0, 1)):
-        keep_ref[part(i, rows), :] = total_ref[cut(member(r), rows), :]
+        keep_ref[part(i, rows), :] = total_ref[cut(member(r), rows), :].astype(BF16)
     for i, r in enumerate((2, 3)):
-        send_ref[part(i, rows), :] = total_ref[cut(member(r), rows), :]
+        send_ref[part(i, rows), :] = total_ref[cut(member(r), rows), :].astype(BF16)
 
 
 def pass_kernel(own_ref, got_ref, keep_ref, send_ref):
@@ -325,7 +320,7 @@
     rows, width = out_ref.shape[0], keep_ref.shape[1]
     for i, ref in enumerate((keep_ref, got_ref)):
         for j in range(2):
-            out_ref[:, cut(member(i + 2 * j), width)] = ref[part(j, rows), :] * factor
+            out_ref[:, cut(member(i + 2 * j), width)] = ref[part(j, rows), :].astype(F32) * factor
 
 
 def local(queries, keys, values, cotangent, out_weight, *, dp, seq):
@@ -367,7 +362,7 @@
         pack_kernel,
         [((SLAB, heads, rows, rows), BF16), ((2 * rows, width), BF16),
          (((4 + outputs // width) * rows, width), BF16), ((2 * rows, width), BF16)],
-        q, k, v, cot, far=True, scratch=scratch(q, k, v, cot),
+        q, k, v, cot,
     )
     message = near(message, bits=1)
     (near_state,) = call(
@@ -378,7 +373,7 @@
     (far_tokens,) = call(pair_kernel, [((4 * rows, width), BF16)], message, far_tokens)
     cot_yc = near(after(cot_y, far_tokens), bits=1)
     far_tokens = near(far_tokens, bits=2)
-    before, _ = doubling(slab_kv, 2 * 10**9)
+    before, _ = doubling(slab_kv, 22 * 10**8)
     dnormed, cots = call(
         functools.partial(dnormed_kernel, dp),
         [((SLAB, rows, width), F32), ((SLAB, rows, outputs), BF16)],
@@ -397,24 +392,24 @@
     if tuned:
         keep, send = call(
             functools.partial(product_kernel, slabs),
-            [((outputs // dp, width), F32), ((outputs // dp, width), BF16)], cots, normed, wait=w_all[1::2],
+            [((outputs // dp, width), F32), ((outputs // dp, width), BF16)], cots, normed,
         )
         got = flip(send, "dp", dp, 1)
     backs = [backs[0], *(near(backs[r], bits=r) for r in range(1, SLAB))]
-    behind, last_u = doubling(slab_u)
+    behind, last_u = doubling(slab_u, 10**9)
     if tuned:
         keep, send = call(
-            split_kernel, [((2 * piece, width), F32), ((2 * piece, width), BF16)], keep, got, cost=1
+            split_kernel, [((2 * piece, width), F32), ((2 * piece, width), BF16)], keep, got, wait=w_all[1::2]
         )
         got = near(send, bits=SLAB)
     later, later_far = call(
-        later_kernel, [((2 * DH, width), BF16)] * 2, *behind, u, cost=3 * 10**9,
+        later_kernel, [((2 * DH, width), BF16)] * 2, *behind, u, cost=10**9, wait=backs[1:3],
         scratch=[pltpu.VMEM((SLAB, DH, width), F32)],
     )
     later_far = near(later_far, bits=2)
     if tuned:
         keep, send = call(
-            split_again_kernel, [((piece, width), F32), ((piece, width), BF16)], keep, got, cost=1
+            split_again_kernel, [((piece, width), F32), ((piece, width), BF16)], keep, got, cost=3 * 10**8
         )
         got = near(send, bits=2 * SLAB)
     output, gq, gk_part, gv_part, own_normed = call(
@@ -425,14 +420,14 @@
     )
     if tuned:
         keep, share = call(
-            share_kernel, [((piece // 2, width), F32)] * 2, keep, got,
+            share_kernel, [((piece // 2, width), BF16)] * 2, keep, got,
             scratch=[pltpu.VMEM((piece, width), F32)],
         )
         got = near(share, bits=2)
     (send,) = call(relay_kernel, [((2 * DH, width), BF16)], later, later_far)
     later_core = near(send, bits=1)
     if tuned:
-        keep, share = call(pass_kernel, [((piece // 2, width), F32)] * 2, keep, got)
+        keep, share = call(pass_kernel, [((piece // 2, width), BF16)] * 2, keep, got, cost=3 * 10**9)
         got = near(share, bits=1)
     gk, gv = call(
         last_kernel, [((rows, features), BF16)] * 2,
@@ -442,6 +437,7 @@
         (grad_weight,) = call(
             functools.partial(finish_kernel, factor),
             [((piece // SLAB, features), F32)], keep, got, end=True,
+            wait=[pltpu.with_memory_space_constraint(gk, pltpu.HBM)],
         )
     else:
         partial = dot(cot, own_normed, 0, 0) * factor

time: 55.3 us -> 49.5 us (0.90)
  waiting for transfers between devices: 17 us -> 12.2 us
  Pallas kernels: 12 us -> 9.94 us
  starting transfers between devices: 25.3 us -> 26.4 us
    ppermute x22, waiting for transfers between devices: 17 us -> 12.2 us  [flip(): return lax.ppermute(x, axis, [(i, i ^ bits) for i in range(count)])]
    pallas_call x19, Pallas kernels: 12 us -> 9.94 us  [__call__(): pl.pallas_call(inner, out_shape=[jax.ShapeDtypeStruct(s, d) for s, d in o...]
    ppermute x22, starting transfers between devices: 25.3 us -> 26.4 us  [flip(): return lax.ppermute(x, axis, [(i, i ^ bits) for i in range(count)])]
  transfers between devices with their start and end apart: 22 -> 22, of which waited for: 10 -> 11; matrix products, arithmetic and copies ran while one was open for 0% -> 0% of each run, Pallas kernels for 16% -> 16%
where the time goes in v9:
time: 49.5 us; the launch traced here: 49.4 us
  starting transfers between devices  26.4 us (53%)
  waiting for transfers between devices  12.2 us (25%)
  Pallas kernels  9.94 us (20%)
  between operations  0.82 us (2%)
    ppermute x22, starting transfers between devices, flip(): return lax.ppermute(x, axis, [(i, i ^ bits) for i in range(count)])  26.4 us
    ppermute x22, waiting for transfers between devices, flip(): return lax.ppermute(x, axis, [(i, i ^ bits) for i in range(count)])  12.2 us
    pallas_call x19, Pallas kernels, __call__(): pl.pallas_call(inner, out_shape=[jax.ShapeDtypeStruct(s, d) for s, d in o...  9.94 us
  transfers between devices with their start and end apart: 22, of which 11 were waited for; matrix products, arithmetic and copies ran while one was open for 0% of the time, Pallas kernels for 16%

profile of v9, /device:TPU:0, one launch (start us, length us, event | category | flops | bytes accessed | tf_op | source)
XLA Modules:
  0.0 49.4 jit_solution(14088500149251736579)
XLA Ops:
  0.7 1.6 %shard_map.92 = (f32[128,256]{1,0:T(8,128)S(1)}, bf16[128,256]{1,0:T(8,128)(2,1)S(1)}, bf16[256,256]{1,0:T(8,128)(2,1)S(1)}, bf16[2,512,256]{2,1,0:T(8,128)(2,1)S(1)}) custom-call(bf16[128,1024]{1,0:T(8,128)(2,1)} %bitcast.8, bf16[128,1024]{1,0:T(8,128)(2,1)} %bitcast.12, bf16[512,1024]{1,0:T(8,128)(2,1)} %refs_8_.1), custom_call_target="tpu_custom_call" | custom-call | flops 1 | bytes 1 | tf_op jit(solution)/shard_map/pallas_call | solution.py:42
  2.2 3.0 %collective-permute-start.1 = (bf16[256,256]{1,0:T(8,128)(2,1)S(1)}, bf16[256,256]{1,0:T(8,128)(2,1)S(1)}, u32[]{:S(2)}, u32[]{:S(2)}) collective-permute-start(bf16[256,256]{1,0:T(8,128)(2,1)S(1)} %get-tuple-element.48), channel_id=1, source_target_pairs={{0,2},{1,3},{2,0},{3,1},{4,6},{5,7},{6,4},{7,5},{8,10},{9,11},{10,... | collective-permute-start | bytes 393224 | tf_op jit(solution)/shard_map/ppermute | solution.py:60
  5.4 1.9 %collective-permute-start.6 = (bf16[2,512,256]{2,1,0:T(8,128)(2,1)S(1)}, bf16[2,512,256]{2,1,0:T(8,128)(2,1)S(1)}, u32[]{:S(2)}, u32[]{:S(2)}) collective-permute-start(bf16[2,512,256]{2,1,0:T(8,128)(2,1)S(1)} %get-tuple-element.50.refs_4_), channel_id=1, source_target_pairs={{0,16},{16,0},{1,17},{17,1},{2,18},{18,2},{3,19},{19,3},{4,20},{20... | collective-permute-start | bytes 1572872 | tf_op jit(solution)/shard_map/ppermute | solution.py:60
  7.3 1.4 %shard_map.93 = (bf16[4,2,128,128]{3,2,1,0:T(8,128)(2,1)S(1)}, bf16[256,256]{1,0:T(8,128)(2,1)S(1)}, bf16[1024,256]{1,0:T(8,128)(2,1)S(1)}, bf16[256,256]{1,0:T(8,128)(2,1)S(1)}) custom-call(bf16[128,1024]{1,0:T(8,128)(2,1)S(1)} %bitcast.19, bf16[128,1024]{1,0:T(8,128)(2,1)S(1)} %bitcast.9, bf16[128,1024]{1,0:T(8,128)(2,1)S(1)} %bitcast.13, ...), custom_call_target="tpu_custom_call" | custom-call | flops 1 | bytes 1 | tf_op jit(solution)/shard_map/pallas_call | solution.py:42
  8.7 0.9 %collective-permute-done.1.refs_1_.refs_4_ = bf16[256,256]{1,0:T(8,128)(2,1)S(1)} collective-permute-done((bf16[256,256]{1,0:T(8,128)(2,1)S(1)}, bf16[256,256]{1,0:T(8,128)(2,1)S(1)}, u32[]{:S(2)}, u32[]{:S(2)}) %collective-permute-start.1) | collective-permute-done | bytes 131104 | tf_op jit(solution)/shard_map/ppermute | solution.py:60
  9.7 1.3 %collective-permute-done.2.refs_2_.refs_5_ = bf16[256,256]{1,0:T(8,128)(2,1)S(1)} collective-permute-done((bf16[256,256]{1,0:T(8,128)(2,1)S(1)}, bf16[256,256]{1,0:T(8,128)(2,1)S(1)}, u32[]{:S(2)}, u32[]{:S(2)}) %collective-permute-start.2) | collective-permute-done | bytes 131104 | tf_op jit(solution)/shard_map/ppermute | solution.py:60
  11.1 2.2 %collective-permute-start.7 = (bf16[128,256]{1,0:T(8,128)(2,1)S(1)}, bf16[128,256]{1,0:T(8,128)(2,1)S(1)}, u32[]{:S(2)}, u32[]{:S(2)}) collective-permute-start(bf16[128,256]{1,0:T(8,128)(2,1)S(1)} %shard_map.95.refs_2_.refs_0_), channel_id=1, source_target_pairs={{0,4},{1,5},{2,6},{3,7},{4,0},{5,1},{6,2},{7,3},{8,12},{9,13},{10,... | collective-permute-start | bytes 196616 | tf_op jit(solution)/shard_map/ppermute | solution.py:60
  13.3 1.6 %collective-permute-start.3 = (bf16[512,256]{1,0:T(8,128)(2,1)S(1)}, bf16[512,256]{1,0:T(8,128)(2,1)S(1)}, u32[]{:S(2)}, u32[]{:S(2)}) collective-permute-start(bf16[512,256]{1,0:T(8,128)(2,1)S(1)} %shard_map.96.refs_2_), channel_id=1, source_target_pairs={{0,2},{1,3},{2,0},{3,1},{4,6},{5,7},{6,4},{7,5},{8,10},{9,11},{10,... | collective-permute-start | bytes 786440 | tf_op jit(solution)/shard_map/ppermute | solution.py:60
  14.9 0.8 %collective-permute-done.7.refs_1_.refs_7_ = bf16[128,256]{1,0:T(8,128)(2,1)S(1)} collective-permute-done((bf16[128,256]{1,0:T(8,128)(2,1)S(1)}, bf16[128,256]{1,0:T(8,128)(2,1)S(1)}, u32[]{:S(2)}, u32[]{:S(2)}) %collective-permute-start.7) | collective-permute-done | bytes 65568 | tf_op jit(solution)/shard_map/ppermute | solution.py:60
  15.7 2.9 %collective-permute-start.8 = (bf16[128,256]{1,0:T(8,128)(2,1)S(1)}, bf16[128,256]{1,0:T(8,128)(2,1)S(1)}, u32[]{:S(2)}, u32[]{:S(2)}) collective-permute-start(bf16[128,256]{1,0:T(8,128)(2,1)S(1)} %shard_map.97.refs_6_), channel_id=1, source_target_pairs={{0,8},{1,9},{2,10},{3,11},{4,12},{5,13},{6,14},{7,15},{8,0},{9,1},... | collective-permute-start | bytes 196616 | tf_op jit(solution)/shard_map/ppermute | solution.py:60
  18.6 0.1 collective-permute-done.6.refs_5_.refs_9_
  18.7 0.5 %shard_map.98 = (f32[4,128,256]{2,1,0:T(8,128)S(1)}, bf16[4,128,1024]{2,1,0:T(8,128)(2,1)S(1)}) custom-call(bf16[1024,256]{1,0:T(8,128)(2,1)S(1)} %collective-permute-done.refs_0_.refs_1_, bf16[128,1024]{1,0:T(8,128)(2,1)S(1)} %bitcast.18, bf16[128,1024]{1,0:T(8,128)(2,1)S(1)} %collective-permute-done.4.refs_2_, ...), custom_call_target="tpu_custom_call" | custom-call | flops 1 | bytes 1 | tf_op jit(solution)/shard_map/pallas_call | solution.py:42
  19.3 1.9 %collective-permute-done.8.refs_8_ = bf16[128,256]{1,0:T(8,128)(2,1)S(1)} collective-permute-done((bf16[128,256]{1,0:T(8,128)(2,1)S(1)}, bf16[128,256]{1,0:T(8,128)(2,1)S(1)}, u32[]{:S(2)}, u32[]{:S(2)}) %collective-permute-start.8) | collective-permute-done | bytes 65568 | tf_op jit(solution)/shard_map/ppermute | solution.py:60
  21.2 0.2 collective-permute-done.3.refs_2_
  21.4 0.8 %shard_map.99 = (bf16[4,128,256]{2,1,0:T(8,128)(2,1)S(1)}, bf16[384,256]{1,0:T(8,128)(2,1)S(1)}, bf16[384,256]{1,0:T(8,128)(2,1)S(1)}, bf16[384,256]{1,0:T(8,128...) custom-call(bf16[256,256]{1,0:T(8,128)(2,1)S(1)} %get-tuple-element.44.refs_0_, ...), custom_call_target="tpu_custom_call" | custom-call | flops 10000000000 | bytes 1 | tf_op jit(solution)/shard_map/pallas_call | solution.py:42
  22.2 0.8 %shard_map.100 = (f32[512,256]{1,0:T(8,128)S(1)}, bf16[512,256]{1,0:T(8,128)(2,1)S(1)}) custom-call(bf16[4,128,1024]{2,1,0:T(8,128)(2,1)S(1)} %get-tuple-element.58.refs_0_, bf16[4,128,256]{2,1,0:T(8,128)(2,1)S(1)} %get-tuple-element.59.refs_1_, bf16[128,256]{1,0:T(8,128)(2,1)S(1)} %get-tuple-element.60.refs_2_.refs_0_), custom_call_target="tpu_custom_call" | custom-call | flops 1 | bytes 1 | tf_op jit(solution)/shard_map/pallas_call | solution.py:42
  23.0 1.6 %collective-permute-start.13 = (bf16[512,256]{1,0:T(8,128)(2,1)S(1)}, bf16[512,256]{1,0:T(8,128)(2,1)S(1)}, u32[]{:S(2)}, u32[]{:S(2)}) collective-permute-start(bf16[512,256]{1,0:T(8,128)(2,1)S(1)} %get-tuple-element.62.refs_2_), channel_id=1, source_target_pairs={{0,16},{16,0},{1,17},{17,1},{2,18},{18,2},{3,19},{19,3},{4,20},{20... | collective-permute-start | bytes 786440 | tf_op jit(solution)/shard_map/ppermute | solution.py:60
  24.5 1.4 %collective-permute-start.14 = (bf16[128,256]{1,0:T(8,128)(2,1)S(1)}, bf16[128,256]{1,0:T(8,128)(2,1)S(1)}, u32[]{:S(2)}, u32[]{:S(2)}) collective-permute-start(bf16[128,256]{1,0:T(8,128)(2,1)S(1)} %get-tuple-element.60.refs_2_.refs_0_), channel_id=1, source_target_pairs={{0,4},{1,5},{2,6},{3,7},{4,0},{5,1},{6,2},{7,3},{8,12},{9,13},{10,... | collective-permute-start | bytes 196616 | tf_op jit(solution)/shard_map/ppermute | solution.py:60
  25.9 1.5 %collective-permute-start.10 = (bf16[384,256]{1,0:T(8,128)(2,1)S(1)}, bf16[384,256]{1,0:T(8,128)(2,1)S(1)}, u32[]{:S(2)}, u32[]{:S(2)}) collective-permute-start(bf16[384,256]{1,0:T(8,128)(2,1)S(1)} %get-tuple-element.54), channel_id=1, source_target_pairs={{0,2},{1,3},{2,0},{3,1},{4,6},{5,7},{6,4},{7,5},{8,10},{9,11},{10,... | collective-permute-start | bytes 589832 | tf_op jit(solution)/shard_map/ppermute | solution.py:60
  27.4 1.4 %collective-permute-done.14.refs_1_.refs_0_ = bf16[128,256]{1,0:T(8,128)(2,1)S(1)} collective-permute-done((bf16[128,256]{1,0:T(8,128)(2,1)S(1)}, bf16[128,256]{1,0:T(8,128)(2,1)S(1)}, u32[]{:S(2)}, u32[]{:S(2)}) %collective-permute-start.14) | collective-permute-done | bytes 65568 | tf_op jit(solution)/shard_map/ppermute | solution.py:60
  28.8 2.7 %collective-permute-start.16 = (bf16[128,256]{1,0:T(8,128)(2,1)S(1)}, bf16[128,256]{1,0:T(8,128)(2,1)S(1)}, u32[]{:S(2)}, u32[]{:S(2)}) collective-permute-start(bf16[128,256]{1,0:T(8,128)(2,1)S(1)} %shard_map.101.refs_2_), channel_id=1, source_target_pairs={{0,8},{1,9},{2,10},{3,11},{4,12},{5,13},{6,14},{7,15},{8,0},{9,1},... | collective-permute-start | bytes 196616 | tf_op jit(solution)/shard_map/ppermute | solution.py:60
  31.5 2.0 %collective-permute-start.15 = (bf16[256,256]{1,0:T(8,128)(2,1)S(1)}, bf16[256,256]{1,0:T(8,128)(2,1)S(1)}, u32[]{:S(2)}, u32[]{:S(2)}) collective-permute-start(bf16[256,256]{1,0:T(8,128)(2,1)S(1)} %get-tuple-element.64.refs_3_), channel_id=1, source_target_pairs={{0,4},{1,5},{2,6},{3,7},{4,0},{5,1},{6,2},{7,3},{8,12},{9,13},{10,... | collective-permute-start | bytes 393224 | tf_op jit(solution)/shard_map/ppermute | solution.py:60
  33.5 0.6 %collective-permute-done.16.refs_1_ = bf16[128,256]{1,0:T(8,128)(2,1)S(1)} collective-permute-done((bf16[128,256]{1,0:T(8,128)(2,1)S(1)}, bf16[128,256]{1,0:T(8,128)(2,1)S(1)}, u32[]{:S(2)}, u32[]{:S(2)}) %collective-permute-start.16) | collective-permute-done | bytes 65568 | tf_op jit(solution)/shard_map/ppermute | solution.py:60
  34.3 1.6 %collective-permute-start.17 = (bf16[256,256]{1,0:T(8,128)(2,1)S(1)}, bf16[256,256]{1,0:T(8,128)(2,1)S(1)}, u32[]{:S(2)}, u32[]{:S(2)}) collective-permute-start(bf16[256,256]{1,0:T(8,128)(2,1)S(1)} %get-tuple-element.66.refs_2_), channel_id=1, source_target_pairs={{0,2},{1,3},{2,0},{3,1},{4,6},{5,7},{6,4},{7,5},{8,10},{9,11},{10,... | collective-permute-start | bytes 393224 | tf_op jit(solution)/shard_map/ppermute | solution.py:60
  35.9 0.9 %collective-permute-done.15.refs_1_ = bf16[256,256]{1,0:T(8,128)(2,1)S(1)} collective-permute-done((bf16[256,256]{1,0:T(8,128)(2,1)S(1)}, bf16[256,256]{1,0:T(8,128)(2,1)S(1)}, u32[]{:S(2)}, u32[]{:S(2)}) %collective-permute-start.15) | collective-permute-done | bytes 131104 | tf_op jit(solution)/shard_map/ppermute | solution.py:60
  36.9 2.0 %collective-permute-start.18 = (bf16[128,256]{1,0:T(8,128)(2,1)S(1)}, bf16[128,256]{1,0:T(8,128)(2,1)S(1)}, u32[]{:S(2)}, u32[]{:S(2)}) collective-permute-start(bf16[128,256]{1,0:T(8,128)(2,1)S(1)} %get-tuple-element.67.refs_11_), channel_id=1, source_target_pairs={{0,8},{1,9},{2,10},{3,11},{4,12},{5,13},{6,14},{7,15},{8,0},{9,1},... | collective-permute-start | bytes 196616 | tf_op jit(solution)/shard_map/ppermute | solution.py:60
  38.9 1.8 %collective-permute-done.11.refs_3_ = bf16[384,256]{1,0:T(8,128)(2,1)S(1)} collective-permute-done((bf16[384,256]{1,0:T(8,128)(2,1)S(1)}, bf16[384,256]{1,0:T(8,128)(2,1)S(1)}, u32[]{:S(2)}, u32[]{:S(2)}) %collective-permute-start.11) | collective-permute-done | bytes 196640 | tf_op jit(solution)/shard_map/ppermute | solution.py:60
  40.7 2.8 %shard_map.105 = (bf16[128,1024]{1,0:T(8,128)(2,1)}, bf16[128,1024]{1,0:T(8,128)(2,1)}, f32[4,128,256]{2,1,0:T(8,128)S(1)}, f32[4,128,256]{2,1,0:T(8,128)S(1)}, bf16[128,1024]{1,0:T(8,128)(2,1)S(1)}) custom-call(bf16[384,256]{1,0:T(8,128)(2,1)S(1)} %get-tuple-element.52.refs_0_, bf16[384,256]{1,0:T(8,128)(2,1)S(1)} %collective-permute-done.9.refs_4_.refs_1_, ...), custom_call_target="tpu_custom_call" | custom-call | flops 1 | bytes 1 | tf_op jit(solution)/shard_map/pallas_call | solution.py:42
  43.5 1.7 %collective-permute-start.20 = (bf16[64,256]{1,0:T(8,128)(2,1)S(1)}, bf16[64,256]{1,0:T(8,128)(2,1)S(1)}, u32[]{:S(2)}, u32[]{:S(2)}) collective-permute-start(bf16[64,256]{1,0:T(8,128)(2,1)S(1)} %get-tuple-element.73.refs_2_), channel_id=1, source_target_pairs={{0,2},{1,3},{2,0},{3,1},{4,6},{5,7},{6,4},{7,5},{8,10},{9,11},{10,... | collective-permute-start | bytes 98312 | tf_op jit(solution)/shard_map/ppermute | solution.py:60
  45.3 2.2 %collective-permute-done.20.refs_1_ = bf16[64,256]{1,0:T(8,128)(2,1)S(1)} collective-permute-done((bf16[64,256]{1,0:T(8,128)(2,1)S(1)}, bf16[64,256]{1,0:T(8,128)(2,1)S(1)}, u32[]{:S(2)}, u32[]{:S(2)}) %collective-permute-start.20) | collective-permute-done | bytes 32800 | tf_op jit(solution)/shard_map/ppermute | solution.py:60
  47.5 1.2 %shard_map.109 = (bf16[128,1024]{1,0:T(8,128)(2,1)}, bf16[128,1024]{1,0:T(8,128)(2,1)}) custom-call(bf16[256,256]{1,0:T(8,128)(2,1)S(1)} %get-tuple-element.70.refs_0_, bf16[256,256]{1,0:T(8,128)(2,1)S(1)} %collective-permute-done.17.refs_1_, bf16[256,256]{1,0:T(8,128)(2,1)S(1)} %collective-permute-done.19.refs_2_, bf16[128,1024]{1,0:T(8,128)(2,1)S(1)} %bitcast.11, ...), custom_call_target="tpu_custom_call" | custom-call | flops 1 | bytes 1 | tf_op jit(solution)/shard_map/pallas_call | solution.py:42
  48.7 0.7 %shard_map.110 = f32[32,1024]{1,0:T(8,128)} custom-call(bf16[64,256]{1,0:T(8,128)(2,1)S(1)} %get-tuple-element.80.refs_0_, bf16[64,256]{1,0:T(8,128)(2,1)S(1)} %collective-permute-done.21.refs_1_, bf16[64,256]{1,0:T(8,128)(2,1)S(1)} %get-tuple-element.77.refs_7_.refs_2_, bf16[128,1024]{1,0:T(8,128)(2,1)} %get-tuple-element.78.refs_3_), custom_call_target="tpu_custom_call" | custom-call | flops 1 | bytes 1 | tf_op jit(solution)/shard_map/pallas_call | solution.py:42
  (41 shorter events, 0.8 us)
Async XLA Ops:
  0.6 4.6 %copy-start.3 = (bf16[1,128,1024]{2,1,0:T(8,128)(2,1)S(1)}, bf16[1,128,1024]{2,1,0:T(8,128)(2,1)}, u32[]{:S(2)}) copy-start(bf16[1,128,1024]{2,1,0:T(8,128)(2,1)} %param.8) | copy-start | bytes 786436
  0.6 6.6 %copy-start.1 = (bf16[1,128,1024]{2,1,0:T(8,128)(2,1)S(1)}, bf16[1,128,1024]{2,1,0:T(8,128)(2,1)}, u32[]{:S(2)}) copy-start(bf16[1,128,1024]{2,1,0:T(8,128)(2,1)} %param.6) | copy-start | bytes 786436
  0.7 6.6 %copy-start.2 = (bf16[1,128,1024]{2,1,0:T(8,128)(2,1)S(1)}, bf16[1,128,1024]{2,1,0:T(8,128)(2,1)}, u32[]{:S(2)}) copy-start(bf16[1,128,1024]{2,1,0:T(8,128)(2,1)} %param.7) | copy-start | bytes 786436
  0.7 6.6 %copy-start.4 = (bf16[1,128,1024]{2,1,0:T(8,128)(2,1)S(1)}, bf16[1,128,1024]{2,1,0:T(8,128)(2,1)}, u32[]{:S(2)}) copy-start(bf16[1,128,1024]{2,1,0:T(8,128)(2,1)} %param.5) | copy-start | bytes 786436
  2.2 7.4 %collective-permute-start.1 = (bf16[256,256]{1,0:T(8,128)(2,1)S(1)}, bf16[256,256]{1,0:T(8,128)(2,1)S(1)}, u32[]{:S(2)}, u32[]{:S(2)}) collective-permute-start(bf16[256,256]{1,0:T(8,128)(2,1)S(1)} %get-tuple-element.48), channel_id=1, source_target_pairs={{0,2},{1,3},{2,0},{3,1},{4,6},{5,7},{6,4},{7,5},{8,10},{9,11},{10,... | collective-permute-start | bytes 393224 | tf_op jit(solution)/shard_map/ppermute | solution.py:60
  5.3 9.6 %collective-permute-start.4 = (bf16[128,1024]{1,0:T(8,128)(2,1)S(1)}, bf16[128,1024]{1,0:T(8,128)(2,1)S(1)}, u32[]{:S(2)}, u32[]{:S(2)}) collective-permute-start(bf16[128,1024]{1,0:T(8,128)(2,1)S(1)} %bitcast.16), channel_id=1, source_target_pairs={{0,2},{1,3},{2,0},{3,1},{4,6},{5,7},{6,4},{7,5},{8,10},{9,11},{10,... | collective-permute-start | bytes 786440 | tf_op jit(solution)/shard_map/ppermute | solution.py:60
  5.4 13.4 %collective-permute-start.6 = (bf16[2,512,256]{2,1,0:T(8,128)(2,1)S(1)}, bf16[2,512,256]{2,1,0:T(8,128)(2,1)S(1)}, u32[]{:S(2)}, u32[]{:S(2)}) collective-permute-start(bf16[2,512,256]{2,1,0:T(8,128)(2,1)S(1)} %get-tuple-element.50.refs_4_), channel_id=1, source_target_pairs={{0,16},{16,0},{1,17},{17,1},{2,18},{18,2},{3,19},{19,3},{4,20},{20... | collective-permute-start | bytes 1572872 | tf_op jit(solution)/shard_map/ppermute | solution.py:60
  8.6 4.6 %collective-permute-start = (bf16[1024,256]{1,0:T(8,128)(2,1)S(1)}, bf16[1024,256]{1,0:T(8,128)(2,1)S(1)}, u32[]{:S(2)}, u32[]{:S(2)}) collective-permute-start(bf16[1024,256]{1,0:T(8,128)(2,1)S(1)} %get-tuple-element.45), channel_id=1, source_target_pairs={{0,1},{1,0},{2,3},{3,2},{4,5},{5,4},{6,7},{7,6},{8,9},{9,8},{10,11... | collective-permute-start | bytes 1572872 | tf_op jit(solution)/shard_map/ppermute | solution.py:60
  9.6 1.4 %collective-permute-start.2 = (bf16[256,256]{1,0:T(8,128)(2,1)S(1)}, bf16[256,256]{1,0:T(8,128)(2,1)S(1)}, u32[]{:S(2)}, u32[]{:S(2)}) collective-permute-start(bf16[256,256]{1,0:T(8,128)(2,1)S(1)} %shard_map.94.refs_3_), channel_id=1, source_target_pairs={{0,1},{1,0},{2,3},{3,2},{4,5},{5,4},{6,7},{7,6},{8,9},{9,8},{10,11... | collective-permute-start | bytes 393224 | tf_op jit(solution)/shard_map/ppermute | solution.py:60
  11.1 4.6 %collective-permute-start.7 = (bf16[128,256]{1,0:T(8,128)(2,1)S(1)}, bf16[128,256]{1,0:T(8,128)(2,1)S(1)}, u32[]{:S(2)}, u32[]{:S(2)}) collective-permute-start(bf16[128,256]{1,0:T(8,128)(2,1)S(1)} %shard_map.95.refs_2_.refs_0_), channel_id=1, source_target_pairs={{0,4},{1,5},{2,6},{3,7},{4,0},{5,1},{6,2},{7,3},{8,12},{9,13},{10,... | collective-permute-start | bytes 196616 | tf_op jit(solution)/shard_map/ppermute | solution.py:60
  13.3 8.1 %collective-permute-start.3 = (bf16[512,256]{1,0:T(8,128)(2,1)S(1)}, bf16[512,256]{1,0:T(8,128)(2,1)S(1)}, u32[]{:S(2)}, u32[]{:S(2)}) collective-permute-start(bf16[512,256]{1,0:T(8,128)(2,1)S(1)} %shard_map.96.refs_2_), channel_id=1, source_target_pairs={{0,2},{1,3},{2,0},{3,1},{4,6},{5,7},{6,4},{7,5},{8,10},{9,11},{10,... | collective-permute-start | bytes 786440 | tf_op jit(solution)/shard_map/ppermute | solution.py:60
  14.9 3.9 %collective-permute-start.5 = (bf16[128,1024]{1,0:T(8,128)(2,1)S(1)}, bf16[128,1024]{1,0:T(8,128)(2,1)S(1)}, u32[]{:S(2)}, u32[]{:S(2)}) collective-permute-start(bf16[128,1024]{1,0:T(8,128)(2,1)S(1)} %collective-permute-done.4.refs_2_), channel_id=1, source_target_pairs={{0,1},{1,0},{2,3},{3,2},{4,5},{5,4},{6,7},{7,6},{8,9},{9,8},{10,11... | collective-permute-start | bytes 786440 | tf_op jit(solution)/shard_map/ppermute | solution.py:60
  15.7 5.6 %collective-permute-start.8 = (bf16[128,256]{1,0:T(8,128)(2,1)S(1)}, bf16[128,256]{1,0:T(8,128)(2,1)S(1)}, u32[]{:S(2)}, u32[]{:S(2)}) collective-permute-start(bf16[128,256]{1,0:T(8,128)(2,1)S(1)} %shard_map.97.refs_6_), channel_id=1, source_target_pairs={{0,8},{1,9},{2,10},{3,11},{4,12},{5,13},{6,14},{7,15},{8,0},{9,1},... | collective-permute-start | bytes 196616 | tf_op jit(solution)/shard_map/ppermute | solution.py:60
  19.3 12.2 %collective-permute-start.12 = (bf16[2,512,256]{2,1,0:T(8,128)(2,1)S(1)}, bf16[2,512,256]{2,1,0:T(8,128)(2,1)S(1)}, u32[]{:S(2)}, u32[]{:S(2)}) collective-permute-start(bf16[2,512,256]{2,1,0:T(8,128)(2,1)S(1)} %collective-permute-done.6.refs_5_.refs_9_), channel_id=1, source_target_pairs={{0,1},{1,0},{2,3},{3,2},{4,5},{5,4},{6,7},{7,6},{8,9},{9,8},{10,11... | collective-permute-start | bytes 1572872 | tf_op jit(solution)/shard_map/ppermute | solution.py:60
  23.0 8.5 %collective-permute-start.13 = (bf16[512,256]{1,0:T(8,128)(2,1)S(1)}, bf16[512,256]{1,0:T(8,128)(2,1)S(1)}, u32[]{:S(2)}, u32[]{:S(2)}) collective-permute-start(bf16[512,256]{1,0:T(8,128)(2,1)S(1)} %get-tuple-element.62.refs_2_), channel_id=1, source_target_pairs={{0,16},{16,0},{1,17},{17,1},{2,18},{18,2},{3,19},{19,3},{4,20},{20... | collective-permute-start | bytes 786440 | tf_op jit(solution)/shard_map/ppermute | solution.py:60
  24.5 4.3 %collective-permute-start.14 = (bf16[128,256]{1,0:T(8,128)(2,1)S(1)}, bf16[128,256]{1,0:T(8,128)(2,1)S(1)}, u32[]{:S(2)}, u32[]{:S(2)}) collective-permute-start(bf16[128,256]{1,0:T(8,128)(2,1)S(1)} %get-tuple-element.60.refs_2_.refs_0_), channel_id=1, source_target_pairs={{0,4},{1,5},{2,6},{3,7},{4,0},{5,1},{6,2},{7,3},{8,12},{9,13},{10,... | collective-permute-start | bytes 196616 | tf_op jit(solution)/shard_map/ppermute | solution.py:60
  25.9 8.3 %collective-permute-start.9 = (bf16[384,256]{1,0:T(8,128)(2,1)S(1)}, bf16[384,256]{1,0:T(8,128)(2,1)S(1)}, u32[]{:S(2)}, u32[]{:S(2)}) collective-permute-start(bf16[384,256]{1,0:T(8,128)(2,1)S(1)} %get-tuple-element.53), channel_id=1, source_target_pairs={{0,1},{1,0},{2,3},{3,2},{4,5},{5,4},{6,7},{7,6},{8,9},{9,8},{10,11... | collective-permute-start | bytes 589832 | tf_op jit(solution)/shard_map/ppermute | solution.py:60
  25.9 8.3 %collective-permute-start.10 = (bf16[384,256]{1,0:T(8,128)(2,1)S(1)}, bf16[384,256]{1,0:T(8,128)(2,1)S(1)}, u32[]{:S(2)}, u32[]{:S(2)}) collective-permute-start(bf16[384,256]{1,0:T(8,128)(2,1)S(1)} %get-tuple-element.54), channel_id=1, source_target_pairs={{0,2},{1,3},{2,0},{3,1},{4,6},{5,7},{6,4},{7,5},{8,10},{9,11},{10,... | collective-permute-start | bytes 589832 | tf_op jit(solution)/shard_map/ppermute | solution.py:60
  28.8 5.3 %collective-permute-start.16 = (bf16[128,256]{1,0:T(8,128)(2,1)S(1)}, bf16[128,256]{1,0:T(8,128)(2,1)S(1)}, u32[]{:S(2)}, u32[]{:S(2)}) collective-permute-start(bf16[128,256]{1,0:T(8,128)(2,1)S(1)} %shard_map.101.refs_2_), channel_id=1, source_target_pairs={{0,8},{1,9},{2,10},{3,11},{4,12},{5,13},{6,14},{7,15},{8,0},{9,1},... | collective-permute-start | bytes 196616 | tf_op jit(solution)/shard_map/ppermute | solution.py:60
  31.5 5.3 %collective-permute-start.15 = (bf16[256,256]{1,0:T(8,128)(2,1)S(1)}, bf16[256,256]{1,0:T(8,128)(2,1)S(1)}, u32[]{:S(2)}, u32[]{:S(2)}) collective-permute-start(bf16[256,256]{1,0:T(8,128)(2,1)S(1)} %get-tuple-element.64.refs_3_), channel_id=1, source_target_pairs={{0,4},{1,5},{2,6},{3,7},{4,0},{5,1},{6,2},{7,3},{8,12},{9,13},{10,... | collective-permute-start | bytes 393224 | tf_op jit(solution)/shard_map/ppermute | solution.py:60
  33.5 7.1 %collective-permute-start.11 = (bf16[384,256]{1,0:T(8,128)(2,1)S(1)}, bf16[384,256]{1,0:T(8,128)(2,1)S(1)}, u32[]{:S(2)}, u32[]{:S(2)}) collective-permute-start(bf16[384,256]{1,0:T(8,128)(2,1)S(1)} %get-tuple-element.55), channel_id=1, source_target_pairs={{0,3},{1,2},{2,1},{3,0},{4,7},{5,6},{6,5},{7,4},{8,11},{9,10},{10,... | collective-permute-start | bytes 589832 | tf_op jit(solution)/shard_map/ppermute | solution.py:60
  34.3 6.4 %copy-start = (bf16[512,1024]{1,0:T(8,128)(2,1)S(1)}, bf16[512,1024]{1,0:T(8,128)(2,1)}, u32[]{:S(2)}) copy-start(bf16[512,1024]{1,0:T(8,128)(2,1)} %refs_8_.1) | copy-start | bytes 3145732
  34.3 10.9 %collective-permute-start.17 = (bf16[256,256]{1,0:T(8,128)(2,1)S(1)}, bf16[256,256]{1,0:T(8,128)(2,1)S(1)}, u32[]{:S(2)}, u32[]{:S(2)}) collective-permute-start(bf16[256,256]{1,0:T(8,128)(2,1)S(1)} %get-tuple-element.66.refs_2_), channel_id=1, source_target_pairs={{0,2},{1,3},{2,0},{3,1},{4,6},{5,7},{6,4},{7,5},{8,10},{9,11},{10,... | collective-permute-start | bytes 393224 | tf_op jit(solution)/shard_map/ppermute | solution.py:60
  36.9 6.6 %collective-permute-start.18 = (bf16[128,256]{1,0:T(8,128)(2,1)S(1)}, bf16[128,256]{1,0:T(8,128)(2,1)S(1)}, u32[]{:S(2)}, u32[]{:S(2)}) collective-permute-start(bf16[128,256]{1,0:T(8,128)(2,1)S(1)} %get-tuple-element.67.refs_11_), channel_id=1, source_target_pairs={{0,8},{1,9},{2,10},{3,11},{4,12},{5,13},{6,14},{7,15},{8,0},{9,1},... | collective-permute-start | bytes 196616 | tf_op jit(solution)/shard_map/ppermute | solution.py:60
  43.5 4.0 %collective-permute-start.20 = (bf16[64,256]{1,0:T(8,128)(2,1)S(1)}, bf16[64,256]{1,0:T(8,128)(2,1)S(1)}, u32[]{:S(2)}, u32[]{:S(2)}) collective-permute-start(bf16[64,256]{1,0:T(8,128)(2,1)S(1)} %get-tuple-element.73.refs_2_), channel_id=1, source_target_pairs={{0,2},{1,3},{2,0},{3,1},{4,6},{5,7},{6,4},{7,5},{8,10},{9,11},{10,... | collective-permute-start | bytes 98312 | tf_op jit(solution)/shard_map/ppermute | solution.py:60
  45.2 2.3 %collective-permute-start.19 = (bf16[256,256]{1,0:T(8,128)(2,1)S(1)}, bf16[256,256]{1,0:T(8,128)(2,1)S(1)}, u32[]{:S(2)}, u32[]{:S(2)}) collective-permute-start(bf16[256,256]{1,0:T(8,128)(2,1)S(1)} %shard_map.107.refs_2_), channel_id=1, source_target_pairs={{0,1},{1,0},{2,3},{3,2},{4,5},{5,4},{6,7},{7,6},{8,9},{9,8},{10,11... | collective-permute-start | bytes 393224 | tf_op jit(solution)/shard_map/ppermute | solution.py:60
  47.5 1.2 %collective-permute-start.21 = (bf16[64,256]{1,0:T(8,128)(2,1)S(1)}, bf16[64,256]{1,0:T(8,128)(2,1)S(1)}, u32[]{:S(2)}, u32[]{:S(2)}) collective-permute-start(bf16[64,256]{1,0:T(8,128)(2,1)S(1)} %get-tuple-element.77.refs_7_.refs_2_), channel_id=1, source_target_pairs={{0,1},{1,0},{2,3},{3,2},{4,5},{5,4},{6,7},{7,6},{8,9},{9,8},{10,11... | collective-permute-start | bytes 98312 | tf_op jit(solution)/shard_map/ppermute | solution.py:60

commit v10 on v9

--- a/solution.py
+++ b/solution.py
@@ -103,7 +103,8 @@
         columns_ref[i] = w_ref[:, cut(member(2 * i), width)]
 
 
-def pack_kernel(q_ref, k_ref, v_ref, c_ref, attend_ref, own_ref, message_ref, far_ref):
+def pack_kernel(q_ref, k_ref, v_ref, c_ref, attend_ref, own_ref, message_ref, far_ref, cot_ref):
+    cot_ref[...] = c_ref[...]
     block = q_ref.shape[0]
     width = q_ref.shape[1] // SLAB
     mask = causal(block)
@@ -169,7 +170,7 @@
 
 def middle_kernel(*refs):
     own_ref, message_ref, token_far, own_state, far_state, near_state, dnormed_ref = refs[:7]
-    *before, normed_ref, back0, back1, back2, back3, u_ref, slab_ref, running = refs[7:]
+    *before, normed_ref, back_near, back_far, u_ref, slab_ref, running = refs[7:]
     _, block, width = normed_ref.shape
     heads = width // DH
     size = 2 * block
@@ -183,20 +184,19 @@
         total, running[p] = total + running[p], total
     sums = [jnp.zeros((DH, DH), F32)] * heads
     for r in range(SLAB):
-        out = (back0, back1, back2, back3)[r]
+        out = (back_near, back_far)[r // 2].at[part(r % 2, block + DH)]
         prior = running[member(r)].astype(BF16)
-        out[size:, :] = prior
+        out[block:, :] = prior
         for h in range(heads):
             q = tokens[r][:block, head(h)]
             mixed = tokens[r][block:, head(h)].astype(F32) + dot(q, prior[:, head(h)], 1, 0)
             scale = lax.rsqrt(jnp.mean(mixed * mixed, axis=-1, keepdims=True) + EPSILON)
             normed = mixed * scale
             normed_ref[r, :, head(h)] = normed.astype(BF16)
-            out[:block, head(h)] = normed.astype(BF16)
             dnormed = dnormed_ref[r, :, head(h)]
             along = jnp.mean(dnormed * normed, axis=-1, keepdims=True)
             dmixed = ((dnormed - normed * along) * scale).astype(BF16)
-            out[block:size, head(h)] = dmixed
+            out[:block, head(h)] = dmixed
             u = dot(q, dmixed, 0, 0)
             u_ref[r, :, head(h)] = u
             sums[h] = sums[h] + u
@@ -228,32 +228,37 @@
 
 
 def late_kernel(groups, *refs):
-    backs, (q_ref, k_ref, v_ref, attend_ref, own_ref) = refs[:SLAB], refs[SLAB : SLAB + 5]
-    far, (out_ref, gq_ref, gk_ref, gv_ref, normed_ref) = refs[SLAB + 5 : -5], refs[-5:]
-    block, width = q_ref.shape[0], backs[0].shape[1]
-    size = 2 * block
-    rows = own_ref.shape[0]
+    backs, (q_ref, k_ref, v_ref, attend_ref, own_ref, message_ref, far_ref) = arrived(*refs[:3]), refs[3:10]
+    weight_ref, *far, out_ref, gq_ref, gk_ref, gv_ref, normed_ref = refs[10:]
+    block, width = q_ref.shape[0], refs[0].shape[1]
+    rows = weight_ref.shape[0]
     me = lax.axis_index("dp")
     mask = causal(block)
+    withins = (own_ref.at[part(1, block)], message_ref.at[part(1, block)],
+               far_ref.at[part(1, block)], message_ref.at[part(3, block)])
     for r in range(SLAB):
         at = cut(member(r), width)
-        normed_ref[:, at] = backs[r][:block, :]
         q, k, v = q_ref[:, at], k_ref[:, at], v_ref[:, at]
-        gqs, gks, gvs = [], [], []
+        normeds, gqs, gks, gvs = [], [], [], []
         for h in range(width // DH):
-            dmixed = backs[r][block:size, head(h)]
+            dmixed, prior = backs[r][:block, head(h)], backs[r][block:, head(h)]
+            mixed = withins[r][:, head(h)].astype(F32) + dot(q[:, head(h)], prior, 1, 0)
+            scale = lax.rsqrt(jnp.mean(mixed * mixed, axis=-1, keepdims=True) + EPSILON)
+            normeds.append(mixed * scale)
             back = jnp.where(mask, dot(dmixed, v[:, head(h)], 1, 1), 0.0).astype(BF16)
-            gqs.append(dot(back, k[:, head(h)], 1, 0) + dot(dmixed, backs[r][size:, head(h)], 1, 1))
+            gqs.append(dot(back, k[:, head(h)], 1, 0) + dot(dmixed, prior, 1, 1))
             gks.append(dot(back, q[:, head(h)], 0, 0))
             gvs.append(dot(attend_ref[r, h], dmixed, 0, 0))
+        normed_ref[:, at] = jnp.concatenate(normeds, axis=1).astype(BF16)
         gq_ref[:, at] = jnp.concatenate(gqs, axis=1).astype(BF16)
         gk_ref[r] = jnp.concatenate(gks, axis=1)
         gv_ref[r] = jnp.concatenate(gvs, axis=1)
-    out_ref[:, cut(me, rows)] = dot(normed_ref[...], own_ref[...], 1, 1).astype(BF16)
+    out_ref[:, cut(me, rows)] = dot(normed_ref[...], weight_ref[...], 1, 1).astype(BF16)
     for j in range(1, groups):
         total = jnp.zeros((block, rows), F32)
         for r in range(SLAB):
-            total = total + dot(backs[r][:block, :], far[2 * (j - 1) + r % 2][r // 2], 1, 1)
+            normed = normed_ref[:, cut(member(r), width)]
+            total = total + dot(normed, far[2 * (j - 1) + r % 2][r // 2], 1, 1)
         out_ref[:, cut(jnp.bitwise_xor(me, j), rows)] = total.astype(BF16)
 
 
@@ -349,7 +354,6 @@
     def scratch(*arrays):
         return [pltpu.VMEM(x.shape, BF16) for x in arrays] + [pltpu.SemaphoreType.DMA((len(arrays),))]
 
-    cot_y = near(cot, bits=2)
     own_state, near_state, far_state, columns = call(
         front_kernel,
         [((DH, width), F32), ((DH, width), BF16), ((2 * DH, width), BF16),
@@ -358,12 +362,15 @@
     )
     far_state = near(far_state, bits=2)
     w_far = [flip(columns, "dp", dp, j) for j in range(1, dp)]
-    attend, own_tokens, message, far_tokens = call(
+    attend, own_tokens, message, far_tokens, cot_y = call(
         pack_kernel,
         [((SLAB, heads, rows, rows), BF16), ((2 * rows, width), BF16),
-         (((4 + outputs // width) * rows, width), BF16), ((2 * rows, width), BF16)],
+         (((4 + outputs // width) * rows, width), BF16), ((2 * rows, width), BF16),
+         ((rows, outputs), BF16)],
         q, k, v, cot,
     )
+    cot_y = near(cot_y, bits=2)
+    near_tokens, sent = message, (message, far_tokens)
     message = near(message, bits=1)
     (near_state,) = call(
         cross_kernel, [((2 * DH, width), BF16)], near_state, far_state, cost=5 * 10**9
@@ -380,9 +387,9 @@
         message, cot, cot_y, cot_yc, columns, *w_far,
     )
     w_all = [x for w in w_far for x in (w, near(after(w, dnormed), bits=1))]
-    normed, *backs, u, slab_u = call(
+    normed, back, back_far, u, slab_u = call(
         middle_kernel,
-        [((SLAB, rows, width), BF16)] + [((2 * rows + DH, width), BF16)] * SLAB
+        [((SLAB, rows, width), BF16)] + [((2 * rows + 2 * DH, width), BF16)] * 2
         + [((SLAB, DH, width), F32), ((DH, width), BF16)],
         own_tokens, message, far_tokens, own_state, far_state, near_state, dnormed, *before,
         cost=10**10, scratch=[pltpu.VMEM((SLAB, DH, width), F32)],
@@ -395,7 +402,7 @@
             [((outputs // dp, width), F32), ((outputs // dp, width), BF16)], cots, normed,
         )
         got = flip(send, "dp", dp, 1)
-    backs = [backs[0], *(near(backs[r], bits=r) for r in range(1, SLAB))]
+    back_far = near(back_far, bits=2)
     behind, last_u = doubling(slab_u, 10**9)
     if tuned:
         keep, send = call(
@@ -403,41 +410,42 @@
         )
         got = near(send, bits=SLAB)
     later, later_far = call(
-        later_kernel, [((2 * DH, width), BF16)] * 2, *behind, u, cost=10**9, wait=backs[1:3],
+        later_kernel, [((2 * DH, width), BF16)] * 2, *behind, u, cost=2 * 10**9,
         scratch=[pltpu.VMEM((SLAB, DH, width), F32)],
     )
     later_far = near(later_far, bits=2)
+    (send,) = call(relay_kernel, [((2 * rows + 2 * DH, width), BF16)], back, back_far)
+    back_core = near(send, bits=1)
     if tuned:
         keep, send = call(
-            split_again_kernel, [((piece, width), F32), ((piece, width), BF16)], keep, got, cost=3 * 10**8
+            split_again_kernel, [((piece, width), F32), ((piece, width), BF16)], keep, got, cost=2 * 10**9
         )
         got = near(send, bits=2 * SLAB)
     output, gq, gk_part, gv_part, own_normed = call(
         functools.partial(late_kernel, dp),
         [((rows, outputs), BF16), ((rows, features), BF16), ((SLAB, rows, width), F32),
          ((SLAB, rows, width), F32), ((rows, features), BF16)],
-        *backs, q, k, v, attend, out_weight, *w_all,
-    )
+        back, back_far, back_core, q, k, v, attend, own_tokens, *sent, out_weight, *w_all,
+    )
+    (send,) = call(relay_kernel, [((2 * DH, width), BF16)], later, later_far)
+    later_core = near(send, bits=1)
     if tuned:
         keep, share = call(
-            share_kernel, [((piece // 2, width), BF16)] * 2, keep, got,
+            share_kernel, [((piece // 2, width), BF16)] * 2, keep, got, cost=2 * 10**9,
             scratch=[pltpu.VMEM((piece, width), F32)],
         )
         got = near(share, bits=2)
-    (send,) = call(relay_kernel, [((2 * DH, width), BF16)], later, later_far)
-    later_core = near(send, bits=1)
-    if tuned:
-        keep, share = call(pass_kernel, [((piece // 2, width), BF16)] * 2, keep, got, cost=3 * 10**9)
-        got = near(share, bits=1)
     gk, gv = call(
         last_kernel, [((rows, features), BF16)] * 2,
         later, later_far, later_core, k, v, gk_part, gv_part, end=True,
     )
     if tuned:
+        keep, share = call(pass_kernel, [((piece // 2, width), BF16)] * 2, keep, got, wait=[pltpu.with_memory_space_constraint(gk, pltpu.HBM)])
+        got = near(share, bits=1)
+    if tuned:
         (grad_weight,) = call(
             functools.partial(finish_kernel, factor),
             [((piece // SLAB, features), F32)], keep, got, end=True,
-            wait=[pltpu.with_memory_space_constraint(gk, pltpu.HBM)],
         )
     else:
         partial = dot(cot, own_normed, 0, 0) * factor

time: 49.5 us -> 49.6 us (level)
  starting transfers between devices: 26.4 us -> 25.8 us
  Pallas kernels: 9.94 us -> 10.5 us
    pallas_call x19 -> x20, Pallas kernels: 9.94 us -> 10.5 us  [__call__(): pl.pallas_call(inner, out_shape=[jax.ShapeDtypeStruct(s, d) for s, d in o...]
    ppermute x22 -> x21, starting transfers between devices: 26.4 us -> 25.8 us  [flip(): return lax.ppermute(x, axis, [(i, i ^ bits) for i in range(count)])]
    ppermute x22 -> x21, waiting for transfers between devices: 12.2 us -> 12.3 us  [flip(): return lax.ppermute(x, axis, [(i, i ^ bits) for i in range(count)])]
  transfers between devices with their start and end apart: 22 -> 21, of which waited for: 11 -> 9; matrix products, arithmetic and copies ran while one was open for 0% -> 0% of each run, Pallas kernels for 16% -> 17%
where the time goes in v10:
time: 49.6 us; the launch traced here: 49.5 us
  starting transfers between devices  25.8 us (52%)
  waiting for transfers between devices  12.3 us (25%)
  Pallas kernels  10.5 us (21%)
  between operations  0.82 us (2%)
    ppermute x21, starting transfers between devices, flip(): return lax.ppermute(x, axis, [(i, i ^ bits) for i in range(count)])  25.8 us
    ppermute x21, waiting for transfers between devices, flip(): return lax.ppermute(x, axis, [(i, i ^ bits) for i in range(count)])  12.3 us
    pallas_call x20, Pallas kernels, __call__(): pl.pallas_call(inner, out_shape=[jax.ShapeDtypeStruct(s, d) for s, d in o...  10.5 us
  transfers between devices with their start and end apart: 21, of which 9 were waited for; matrix products, arithmetic and copies ran while one was open for 0% of the time, Pallas kernels for 17%

profile of v10, /device:TPU:0, one launch (start us, length us, event | category | flops | bytes accessed | tf_op | source)
XLA Modules:
  0.0 49.5 jit_solution(11881526660413832284)
XLA Ops:
  0.7 1.6 %shard_map.92 = (f32[128,256]{1,0:T(8,128)S(1)}, bf16[128,256]{1,0:T(8,128)(2,1)S(1)}, bf16[256,256]{1,0:T(8,128)(2,1)S(1)}, bf16[2,512,256]{2,1,0:T(8,128)(2,1)S(1)}) custom-call(bf16[128,1024]{1,0:T(8,128)(2,1)} %bitcast.8, bf16[128,1024]{1,0:T(8,128)(2,1)} %bitcast.12, bf16[512,1024]{1,0:T(8,128)(2,1)} %refs_10_.1), custom_call_target="tpu_custom_call" | custom-call | flops 1 | bytes 1 | tf_op jit(solution)/shard_map/pallas_call | solution.py:42
  2.2 3.0 %collective-permute-start.1 = (bf16[256,256]{1,0:T(8,128)(2,1)S(1)}, bf16[256,256]{1,0:T(8,128)(2,1)S(1)}, u32[]{:S(2)}, u32[]{:S(2)}) collective-permute-start(bf16[256,256]{1,0:T(8,128)(2,1)S(1)} %get-tuple-element.47), channel_id=1, source_target_pairs={{0,2},{1,3},{2,0},{3,1},{4,6},{5,7},{6,4},{7,5},{8,10},{9,11},{10,... | collective-permute-start | bytes 393224 | tf_op jit(solution)/shard_map/ppermute | solution.py:60
  5.3 1.5 %collective-permute-start.6 = (bf16[2,512,256]{2,1,0:T(8,128)(2,1)S(1)}, bf16[2,512,256]{2,1,0:T(8,128)(2,1)S(1)}, u32[]{:S(2)}, u32[]{:S(2)}) collective-permute-start(bf16[2,512,256]{2,1,0:T(8,128)(2,1)S(1)} %get-tuple-element.50.refs_4_), channel_id=1, source_target_pairs={{0,16},{16,0},{1,17},{17,1},{2,18},{18,2},{3,19},{19,3},{4,20},{20... | collective-permute-start | bytes 1572872 | tf_op jit(solution)/shard_map/ppermute | solution.py:60
  6.8 1.4 %shard_map.93 = (bf16[4,2,128,128]{3,2,1,0:T(8,128)(2,1)S(1)}, bf16[256,256]{1,0:T(8,128)(2,1)S(1)}, bf16[1024,256]{1,0:T(8,128)(2,1)S(1)}, bf16[256,256]{1,0:T(8,128)(2,1)S(1)}, bf16[128,1024]{1,0:T(8,128)(2,1)S(1)}) custom-call(bf16[128,1024]{1,0:T(8,128)(2,1)S(1)} %bitcast.18, bf16[128,1024]{1,0:T(8,128)(2,1)S(1)} %bitcast.9, ...), custom_call_target="tpu_custom_call" | custom-call | flops 1 | bytes 1 | tf_op jit(solution)/shard_map/pallas_call | solution.py:42
  8.1 0.6 %collective-permute-start.4 = (bf16[128,1024]{1,0:T(8,128)(2,1)S(1)}, bf16[128,1024]{1,0:T(8,128)(2,1)S(1)}, u32[]{:S(2)}, u32[]{:S(2)}) collective-permute-start(bf16[128,1024]{1,0:T(8,128)(2,1)S(1)} %get-tuple-element.48), channel_id=1, source_target_pairs={{0,2},{1,3},{2,0},{3,1},{4,6},{5,7},{6,4},{7,5},{8,10},{9,11},{10,... | collective-permute-start | bytes 786440 | tf_op jit(solution)/shard_map/ppermute | solution.py:60
  8.8 0.5 %collective-permute-start.2 = (bf16[256,256]{1,0:T(8,128)(2,1)S(1)}, bf16[256,256]{1,0:T(8,128)(2,1)S(1)}, u32[]{:S(2)}, u32[]{:S(2)}) collective-permute-start(bf16[256,256]{1,0:T(8,128)(2,1)S(1)} %shard_map.94.refs_3_), channel_id=1, source_target_pairs={{0,1},{1,0},{2,3},{3,2},{4,5},{5,4},{6,7},{7,6},{8,9},{9,8},{10,11... | collective-permute-start | bytes 393224 | tf_op jit(solution)/shard_map/ppermute | solution.py:60
  9.3 1.5 %collective-permute-done.2.refs_2_.refs_5_ = bf16[256,256]{1,0:T(8,128)(2,1)S(1)} collective-permute-done((bf16[256,256]{1,0:T(8,128)(2,1)S(1)}, bf16[256,256]{1,0:T(8,128)(2,1)S(1)}, u32[]{:S(2)}, u32[]{:S(2)}) %collective-permute-start.2) | collective-permute-done | bytes 131104 | tf_op jit(solution)/shard_map/ppermute | solution.py:60
  10.9 1.6 %collective-permute-start.7 = (bf16[128,256]{1,0:T(8,128)(2,1)S(1)}, bf16[128,256]{1,0:T(8,128)(2,1)S(1)}, u32[]{:S(2)}, u32[]{:S(2)}) collective-permute-start(bf16[128,256]{1,0:T(8,128)(2,1)S(1)} %shard_map.95.refs_2_.refs_0_), channel_id=1, source_target_pairs={{0,4},{1,5},{2,6},{3,7},{4,0},{5,1},{6,2},{7,3},{8,12},{9,13},{10,... | collective-permute-start | bytes 196616 | tf_op jit(solution)/shard_map/ppermute | solution.py:60
  12.5 1.6 %collective-permute-start.3 = (bf16[512,256]{1,0:T(8,128)(2,1)S(1)}, bf16[512,256]{1,0:T(8,128)(2,1)S(1)}, u32[]{:S(2)}, u32[]{:S(2)}) collective-permute-start(bf16[512,256]{1,0:T(8,128)(2,1)S(1)} %shard_map.96.refs_2_), channel_id=1, source_target_pairs={{0,2},{1,3},{2,0},{3,1},{4,6},{5,7},{6,4},{7,5},{8,10},{9,11},{10,... | collective-permute-start | bytes 786440 | tf_op jit(solution)/shard_map/ppermute | solution.py:60
  14.1 2.2 %collective-permute-done.4.refs_2_ = bf16[128,1024]{1,0:T(8,128)(2,1)S(1)} collective-permute-done((bf16[128,1024]{1,0:T(8,128)(2,1)S(1)}, bf16[128,1024]{1,0:T(8,128)(2,1)S(1)}, u32[]{:S(2)}, u32[]{:S(2)}) %collective-permute-start.4) | collective-permute-done | bytes 262176 | tf_op jit(solution)/shard_map/ppermute | solution.py:60
  16.3 2.6 %collective-permute-start.8 = (bf16[128,256]{1,0:T(8,128)(2,1)S(1)}, bf16[128,256]{1,0:T(8,128)(2,1)S(1)}, u32[]{:S(2)}, u32[]{:S(2)}) collective-permute-start(bf16[128,256]{1,0:T(8,128)(2,1)S(1)} %shard_map.97.refs_6_), channel_id=1, source_target_pairs={{0,8},{1,9},{2,10},{3,11},{4,12},{5,13},{6,14},{7,15},{8,0},{9,1},... | collective-permute-start | bytes 196616 | tf_op jit(solution)/shard_map/ppermute | solution.py:60
  19.0 0.5 %shard_map.98 = (f32[4,128,256]{2,1,0:T(8,128)S(1)}, bf16[4,128,1024]{2,1,0:T(8,128)(2,1)S(1)}) custom-call(bf16[1024,256]{1,0:T(8,128)(2,1)S(1)} %collective-permute-done.refs_0_.refs_1_, bf16[128,1024]{1,0:T(8,128)(2,1)S(1)} %bitcast.17, bf16[128,1024]{1,0:T(8,128)(2,1)S(1)} %collective-permute-done.4.refs_2_, ...), custom_call_target="tpu_custom_call" | custom-call | flops 1 | bytes 1 | tf_op jit(solution)/shard_map/pallas_call | solution.py:42
  19.5 0.3 collective-permute-start.13
  19.8 2.0 %collective-permute-done.8.refs_8_ = bf16[128,256]{1,0:T(8,128)(2,1)S(1)} collective-permute-done((bf16[128,256]{1,0:T(8,128)(2,1)S(1)}, bf16[128,256]{1,0:T(8,128)(2,1)S(1)}, u32[]{:S(2)}, u32[]{:S(2)}) %collective-permute-start.8) | collective-permute-done | bytes 65568 | tf_op jit(solution)/shard_map/ppermute | solution.py:60
  21.8 0.8 %shard_map.99 = (bf16[4,128,256]{2,1,0:T(8,128)(2,1)S(1)}, bf16[512,256]{1,0:T(8,128)(2,1)S(1)}, bf16[512,256]{1,0:T(8,128)(2,1)S(1)}, f32[4,128,256]{2,1,0:T(8,128)S(1)}, bf16[128,256]{1,0:T(8,128)(2,1)S(1)}) custom-call(bf16[256,256]{1,0:T(8,128)(2,1)S(1)} %get-tuple-element.43.refs_0_.refs_7_, bf16[1024,256]{1,0:T(8,128)(2,1)S(1)} %collective-permute-done.refs_0_.refs_1_, ...), custom_call_target="tpu_custom_call" | custom-call | flops 10000000000 | bytes 1 | tf_op jit(solution)/shard_map/pallas_call | solution.py:42
  22.6 0.8 %shard_map.100 = (f32[512,256]{1,0:T(8,128)S(1)}, bf16[512,256]{1,0:T(8,128)(2,1)S(1)}) custom-call(bf16[4,128,1024]{2,1,0:T(8,128)(2,1)S(1)} %get-tuple-element.55.refs_0_, bf16[4,128,256]{2,1,0:T(8,128)(2,1)S(1)} %get-tuple-element.56.refs_1_, bf16[128,256]{1,0:T(8,128)(2,1)S(1)} %get-tuple-element.54.refs_2_.refs_0_), custom_call_target="tpu_custom_call" | custom-call | flops 1 | bytes 1 | tf_op jit(solution)/shard_map/pallas_call | solution.py:42
  23.3 0.7 %collective-permute-start.12 = (bf16[512,256]{1,0:T(8,128)(2,1)S(1)}, bf16[512,256]{1,0:T(8,128)(2,1)S(1)}, u32[]{:S(2)}, u32[]{:S(2)}) collective-permute-start(bf16[512,256]{1,0:T(8,128)(2,1)S(1)} %get-tuple-element.57.refs_2_), channel_id=1, source_target_pairs={{0,16},{16,0},{1,17},{17,1},{2,18},{18,2},{3,19},{19,3},{4,20},{20... | collective-permute-start | bytes 786440 | tf_op jit(solution)/shard_map/ppermute | solution.py:60
  24.1 2.2 %collective-permute-start.10 = (bf16[128,256]{1,0:T(8,128)(2,1)S(1)}, bf16[128,256]{1,0:T(8,128)(2,1)S(1)}, u32[]{:S(2)}, u32[]{:S(2)}) collective-permute-start(bf16[128,256]{1,0:T(8,128)(2,1)S(1)} %get-tuple-element.54.refs_2_.refs_0_), channel_id=1, source_target_pairs={{0,4},{1,5},{2,6},{3,7},{4,0},{5,1},{6,2},{7,3},{8,12},{9,13},{10,... | collective-permute-start | bytes 196616 | tf_op jit(solution)/shard_map/ppermute | solution.py:60
  26.2 0.9 %collective-permute-start.9 = (bf16[512,256]{1,0:T(8,128)(2,1)S(1)}, bf16[512,256]{1,0:T(8,128)(2,1)S(1)}, u32[]{:S(2)}, u32[]{:S(2)}) collective-permute-start(bf16[512,256]{1,0:T(8,128)(2,1)S(1)} %get-tuple-element.53), channel_id=1, source_target_pairs={{0,2},{1,3},{2,0},{3,1},{4,6},{5,7},{6,4},{7,5},{8,10},{9,11},{10,... | collective-permute-start | bytes 786440 | tf_op jit(solution)/shard_map/ppermute | solution.py:60
  27.1 1.3 %collective-permute-done.10.refs_1_.refs_0_ = bf16[128,256]{1,0:T(8,128)(2,1)S(1)} collective-permute-done((bf16[128,256]{1,0:T(8,128)(2,1)S(1)}, bf16[128,256]{1,0:T(8,128)(2,1)S(1)}, u32[]{:S(2)}, u32[]{:S(2)}) %collective-permute-start.10) | collective-permute-done | bytes 65568 | tf_op jit(solution)/shard_map/ppermute | solution.py:60
  28.5 2.8 %collective-permute-start.11 = (bf16[128,256]{1,0:T(8,128)(2,1)S(1)}, bf16[128,256]{1,0:T(8,128)(2,1)S(1)}, u32[]{:S(2)}, u32[]{:S(2)}) collective-permute-start(bf16[128,256]{1,0:T(8,128)(2,1)S(1)} %shard_map.101.refs_2_), channel_id=1, source_target_pairs={{0,8},{1,9},{2,10},{3,11},{4,12},{5,13},{6,14},{7,15},{8,0},{9,1},... | collective-permute-start | bytes 196616 | tf_op jit(solution)/shard_map/ppermute | solution.py:60
  31.4 2.8 %collective-permute-start.15 = (bf16[256,256]{1,0:T(8,128)(2,1)S(1)}, bf16[256,256]{1,0:T(8,128)(2,1)S(1)}, u32[]{:S(2)}, u32[]{:S(2)}) collective-permute-start(bf16[256,256]{1,0:T(8,128)(2,1)S(1)} %get-tuple-element.61.refs_3_), channel_id=1, source_target_pairs={{0,4},{1,5},{2,6},{3,7},{4,0},{5,1},{6,2},{7,3},{8,12},{9,13},{10,... | collective-permute-start | bytes 393224 | tf_op jit(solution)/shard_map/ppermute | solution.py:60
  34.5 1.3 %collective-permute-start.16 = (bf16[256,256]{1,0:T(8,128)(2,1)S(1)}, bf16[256,256]{1,0:T(8,128)(2,1)S(1)}, u32[]{:S(2)}, u32[]{:S(2)}) collective-permute-start(bf16[256,256]{1,0:T(8,128)(2,1)S(1)} %get-tuple-element.62.refs_2_), channel_id=1, source_target_pairs={{0,2},{1,3},{2,0},{3,1},{4,6},{5,7},{6,4},{7,5},{8,10},{9,11},{10,... | collective-permute-start | bytes 393224 | tf_op jit(solution)/shard_map/ppermute | solution.py:60
  35.7 1.4 %collective-permute-done.15.refs_1_ = bf16[256,256]{1,0:T(8,128)(2,1)S(1)} collective-permute-done((bf16[256,256]{1,0:T(8,128)(2,1)S(1)}, bf16[256,256]{1,0:T(8,128)(2,1)S(1)}, u32[]{:S(2)}, u32[]{:S(2)}) %collective-permute-start.15) | collective-permute-done | bytes 131104 | tf_op jit(solution)/shard_map/ppermute | solution.py:60
  37.2 2.9 %collective-permute-start.18 = (bf16[128,256]{1,0:T(8,128)(2,1)S(1)}, bf16[128,256]{1,0:T(8,128)(2,1)S(1)}, u32[]{:S(2)}, u32[]{:S(2)}) collective-permute-start(bf16[128,256]{1,0:T(8,128)(2,1)S(1)} %get-tuple-element.65.refs_13_), channel_id=1, source_target_pairs={{0,8},{1,9},{2,10},{3,11},{4,12},{5,13},{6,14},{7,15},{8,0},{9,1},... | collective-permute-start | bytes 196616 | tf_op jit(solution)/shard_map/ppermute | solution.py:60
  40.1 3.4 %shard_map.106 = (bf16[128,1024]{1,0:T(8,128)(2,1)}, bf16[128,1024]{1,0:T(8,128)(2,1)}, f32[4,128,256]{2,1,0:T(8,128)S(1)}, f32[4,128,256]{2,1,0:T(8,128)S(1)}, bf16[128,1024]{1,0:T(8,128)(2,1)S(1)}) custom-call(bf16[512,256]{1,0:T(8,128)(2,1)S(1)} %get-tuple-element.52.refs_0_, bf16[512,256]{1,0:T(8,128)(2,1)S(1)} %collective-permute-done.9.refs_1_, ...), custom_call_target="tpu_custom_call" | custom-call | flops 1 | bytes 1 | tf_op jit(solution)/shard_map/pallas_call | solution.py:42
  43.6 0.3 collective-permute-start.19
  44.0 1.0 %collective-permute-done.17.refs_2_ = bf16[256,256]{1,0:T(8,128)(2,1)S(1)} collective-permute-done((bf16[256,256]{1,0:T(8,128)(2,1)S(1)}, bf16[256,256]{1,0:T(8,128)(2,1)S(1)}, u32[]{:S(2)}, u32[]{:S(2)}) %collective-permute-start.17) | collective-permute-done | bytes 131104 | tf_op jit(solution)/shard_map/ppermute | solution.py:60
  44.9 1.1 %shard_map.109 = (bf16[128,1024]{1,0:T(8,128)(2,1)}, bf16[128,1024]{1,0:T(8,128)(2,1)}) custom-call(bf16[256,256]{1,0:T(8,128)(2,1)S(1)} %get-tuple-element.68.refs_0_, bf16[256,256]{1,0:T(8,128)(2,1)S(1)} %collective-permute-done.16.refs_1_, bf16[256,256]{1,0:T(8,128)(2,1)S(1)} %collective-permute-done.17.refs_2_, bf16[128,1024]{1,0:T(8,128)(2,1)S(1)} %bitcast.11, ...), custom_call_target="tpu_custom_call" | custom-call | flops 1 | bytes 1 | tf_op jit(solution)/shard_map/pallas_call | solution.py:42
  46.1 1.5 %collective-permute-done.19.refs_1_ = bf16[64,256]{1,0:T(8,128)(2,1)S(1)} collective-permute-done((bf16[64,256]{1,0:T(8,128)(2,1)S(1)}, bf16[64,256]{1,0:T(8,128)(2,1)S(1)}, u32[]{:S(2)}, u32[]{:S(2)}) %collective-permute-start.19) | collective-permute-done | bytes 32800 | tf_op jit(solution)/shard_map/ppermute | solution.py:60
  47.6 1.2 %collective-permute-done.20.refs_1_ = bf16[64,256]{1,0:T(8,128)(2,1)S(1)} collective-permute-done((bf16[64,256]{1,0:T(8,128)(2,1)S(1)}, bf16[64,256]{1,0:T(8,128)(2,1)S(1)}, u32[]{:S(2)}, u32[]{:S(2)}) %collective-permute-start.20) | collective-permute-done | bytes 32800 | tf_op jit(solution)/shard_map/ppermute | solution.py:60
  48.8 0.7 %shard_map.111 = f32[32,1024]{1,0:T(8,128)} custom-call(bf16[64,256]{1,0:T(8,128)(2,1)S(1)} %get-tuple-element.77.refs_0_, bf16[64,256]{1,0:T(8,128)(2,1)S(1)} %collective-permute-done.20.refs_1_, bf16[64,256]{1,0:T(8,128)(2,1)S(1)} %get-tuple-element.78.refs_2_), custom_call_target="tpu_custom_call" | custom-call | flops 1 | bytes 1 | tf_op jit(solution)/shard_map/pallas_call | solution.py:42
  (40 shorter events, 0.7 us)
Async XLA Ops:
  0.6 6.1 %copy-start = (bf16[1,128,1024]{2,1,0:T(8,128)(2,1)S(1)}, bf16[1,128,1024]{2,1,0:T(8,128)(2,1)}, u32[]{:S(2)}) copy-start(bf16[1,128,1024]{2,1,0:T(8,128)(2,1)} %param.6) | copy-start | bytes 786436
  0.6 6.1 %copy-start.1 = (bf16[1,128,1024]{2,1,0:T(8,128)(2,1)S(1)}, bf16[1,128,1024]{2,1,0:T(8,128)(2,1)}, u32[]{:S(2)}) copy-start(bf16[1,128,1024]{2,1,0:T(8,128)(2,1)} %param.7) | copy-start | bytes 786436
  0.7 6.1 %copy-start.3 = (bf16[1,128,1024]{2,1,0:T(8,128)(2,1)S(1)}, bf16[1,128,1024]{2,1,0:T(8,128)(2,1)}, u32[]{:S(2)}) copy-start(bf16[1,128,1024]{2,1,0:T(8,128)(2,1)} %param.8) | copy-start | bytes 786436
  0.7 6.1 %copy-start.4 = (bf16[1,128,1024]{2,1,0:T(8,128)(2,1)S(1)}, bf16[1,128,1024]{2,1,0:T(8,128)(2,1)}, u32[]{:S(2)}) copy-start(bf16[1,128,1024]{2,1,0:T(8,128)(2,1)} %param.5) | copy-start | bytes 786436
  2.2 6.5 %collective-permute-start.1 = (bf16[256,256]{1,0:T(8,128)(2,1)S(1)}, bf16[256,256]{1,0:T(8,128)(2,1)S(1)}, u32[]{:S(2)}, u32[]{:S(2)}) collective-permute-start(bf16[256,256]{1,0:T(8,128)(2,1)S(1)} %get-tuple-element.47), channel_id=1, source_target_pairs={{0,2},{1,3},{2,0},{3,1},{4,6},{5,7},{6,4},{7,5},{8,10},{9,11},{10,... | collective-permute-start | bytes 393224 | tf_op jit(solution)/shard_map/ppermute | solution.py:60
  5.3 13.7 %collective-permute-start.6 = (bf16[2,512,256]{2,1,0:T(8,128)(2,1)S(1)}, bf16[2,512,256]{2,1,0:T(8,128)(2,1)S(1)}, u32[]{:S(2)}, u32[]{:S(2)}) collective-permute-start(bf16[2,512,256]{2,1,0:T(8,128)(2,1)S(1)} %get-tuple-element.50.refs_4_), channel_id=1, source_target_pairs={{0,16},{16,0},{1,17},{17,1},{2,18},{18,2},{3,19},{19,3},{4,20},{20... | collective-permute-start | bytes 1572872 | tf_op jit(solution)/shard_map/ppermute | solution.py:60
  8.1 8.1 %collective-permute-start.4 = (bf16[128,1024]{1,0:T(8,128)(2,1)S(1)}, bf16[128,1024]{1,0:T(8,128)(2,1)S(1)}, u32[]{:S(2)}, u32[]{:S(2)}) collective-permute-start(bf16[128,1024]{1,0:T(8,128)(2,1)S(1)} %get-tuple-element.48), channel_id=1, source_target_pairs={{0,2},{1,3},{2,0},{3,1},{4,6},{5,7},{6,4},{7,5},{8,10},{9,11},{10,... | collective-permute-start | bytes 786440 | tf_op jit(solution)/shard_map/ppermute | solution.py:60
  8.7 3.8 %collective-permute-start = (bf16[1024,256]{1,0:T(8,128)(2,1)S(1)}, bf16[1024,256]{1,0:T(8,128)(2,1)S(1)}, u32[]{:S(2)}, u32[]{:S(2)}) collective-permute-start(bf16[1024,256]{1,0:T(8,128)(2,1)S(1)} %get-tuple-element.44.refs_8_), channel_id=1, source_target_pairs={{0,1},{1,0},{2,3},{3,2},{4,5},{5,4},{6,7},{7,6},{8,9},{9,8},{10,11... | collective-permute-start | bytes 1572872 | tf_op jit(solution)/shard_map/ppermute | solution.py:60
  8.8 2.0 %collective-permute-start.2 = (bf16[256,256]{1,0:T(8,128)(2,1)S(1)}, bf16[256,256]{1,0:T(8,128)(2,1)S(1)}, u32[]{:S(2)}, u32[]{:S(2)}) collective-permute-start(bf16[256,256]{1,0:T(8,128)(2,1)S(1)} %shard_map.94.refs_3_), channel_id=1, source_target_pairs={{0,1},{1,0},{2,3},{3,2},{4,5},{5,4},{6,7},{7,6},{8,9},{9,8},{10,11... | collective-permute-start | bytes 393224 | tf_op jit(solution)/shard_map/ppermute | solution.py:60
  10.9 5.4 %collective-permute-start.7 = (bf16[128,256]{1,0:T(8,128)(2,1)S(1)}, bf16[128,256]{1,0:T(8,128)(2,1)S(1)}, u32[]{:S(2)}, u32[]{:S(2)}) collective-permute-start(bf16[128,256]{1,0:T(8,128)(2,1)S(1)} %shard_map.95.refs_2_.refs_0_), channel_id=1, source_target_pairs={{0,4},{1,5},{2,6},{3,7},{4,0},{5,1},{6,2},{7,3},{8,12},{9,13},{10,... | collective-permute-start | bytes 196616 | tf_op jit(solution)/shard_map/ppermute | solution.py:60
  12.5 9.3 %collective-permute-start.3 = (bf16[512,256]{1,0:T(8,128)(2,1)S(1)}, bf16[512,256]{1,0:T(8,128)(2,1)S(1)}, u32[]{:S(2)}, u32[]{:S(2)}) collective-permute-start(bf16[512,256]{1,0:T(8,128)(2,1)S(1)} %shard_map.96.refs_2_), channel_id=1, source_target_pairs={{0,2},{1,3},{2,0},{3,1},{4,6},{5,7},{6,4},{7,5},{8,10},{9,11},{10,... | collective-permute-start | bytes 786440 | tf_op jit(solution)/shard_map/ppermute | solution.py:60
  16.3 2.7 %collective-permute-start.5 = (bf16[128,1024]{1,0:T(8,128)(2,1)S(1)}, bf16[128,1024]{1,0:T(8,128)(2,1)S(1)}, u32[]{:S(2)}, u32[]{:S(2)}) collective-permute-start(bf16[128,1024]{1,0:T(8,128)(2,1)S(1)} %collective-permute-done.4.refs_2_), channel_id=1, source_target_pairs={{0,1},{1,0},{2,3},{3,2},{4,5},{5,4},{6,7},{7,6},{8,9},{9,8},{10,11... | collective-permute-start | bytes 786440 | tf_op jit(solution)/shard_map/ppermute | solution.py:60
  16.3 5.5 %collective-permute-start.8 = (bf16[128,256]{1,0:T(8,128)(2,1)S(1)}, bf16[128,256]{1,0:T(8,128)(2,1)S(1)}, u32[]{:S(2)}, u32[]{:S(2)}) collective-permute-start(bf16[128,256]{1,0:T(8,128)(2,1)S(1)} %shard_map.97.refs_6_), channel_id=1, source_target_pairs={{0,8},{1,9},{2,10},{3,11},{4,12},{5,13},{6,14},{7,15},{8,0},{9,1},... | collective-permute-start | bytes 196616 | tf_op jit(solution)/shard_map/ppermute | solution.py:60
  19.5 11.9 %collective-permute-start.13 = (bf16[2,512,256]{2,1,0:T(8,128)(2,1)S(1)}, bf16[2,512,256]{2,1,0:T(8,128)(2,1)S(1)}, u32[]{:S(2)}, u32[]{:S(2)}) collective-permute-start(bf16[2,512,256]{2,1,0:T(8,128)(2,1)S(1)} %collective-permute-done.6.refs_5_.refs_11_), channel_id=1, source_target_pairs={{0,1},{1,0},{2,3},{3,2},{4,5},{5,4},{6,7},{7,6},{8,9},{9,8},{10,11... | collective-permute-start | bytes 1572872 | tf_op jit(solution)/shard_map/ppermute | solution.py:60
  23.3 8.0 %collective-permute-start.12 = (bf16[512,256]{1,0:T(8,128)(2,1)S(1)}, bf16[512,256]{1,0:T(8,128)(2,1)S(1)}, u32[]{:S(2)}, u32[]{:S(2)}) collective-permute-start(bf16[512,256]{1,0:T(8,128)(2,1)S(1)} %get-tuple-element.57.refs_2_), channel_id=1, source_target_pairs={{0,16},{16,0},{1,17},{17,1},{2,18},{18,2},{3,19},{19,3},{4,20},{20... | collective-permute-start | bytes 786440 | tf_op jit(solution)/shard_map/ppermute | solution.py:60
  24.1 4.4 %collective-permute-start.10 = (bf16[128,256]{1,0:T(8,128)(2,1)S(1)}, bf16[128,256]{1,0:T(8,128)(2,1)S(1)}, u32[]{:S(2)}, u32[]{:S(2)}) collective-permute-start(bf16[128,256]{1,0:T(8,128)(2,1)S(1)} %get-tuple-element.54.refs_2_.refs_0_), channel_id=1, source_target_pairs={{0,4},{1,5},{2,6},{3,7},{4,0},{5,1},{6,2},{7,3},{8,12},{9,13},{10,... | collective-permute-start | bytes 196616 | tf_op jit(solution)/shard_map/ppermute | solution.py:60
  26.2 8.1 %collective-permute-start.9 = (bf16[512,256]{1,0:T(8,128)(2,1)S(1)}, bf16[512,256]{1,0:T(8,128)(2,1)S(1)}, u32[]{:S(2)}, u32[]{:S(2)}) collective-permute-start(bf16[512,256]{1,0:T(8,128)(2,1)S(1)} %get-tuple-element.53), channel_id=1, source_target_pairs={{0,2},{1,3},{2,0},{3,1},{4,6},{5,7},{6,4},{7,5},{8,10},{9,11},{10,... | collective-permute-start | bytes 786440 | tf_op jit(solution)/shard_map/ppermute | solution.py:60
  28.5 5.7 %collective-permute-start.11 = (bf16[128,256]{1,0:T(8,128)(2,1)S(1)}, bf16[128,256]{1,0:T(8,128)(2,1)S(1)}, u32[]{:S(2)}, u32[]{:S(2)}) collective-permute-start(bf16[128,256]{1,0:T(8,128)(2,1)S(1)} %shard_map.101.refs_2_), channel_id=1, source_target_pairs={{0,8},{1,9},{2,10},{3,11},{4,12},{5,13},{6,14},{7,15},{8,0},{9,1},... | collective-permute-start | bytes 196616 | tf_op jit(solution)/shard_map/ppermute | solution.py:60
  31.4 5.8 %collective-permute-start.15 = (bf16[256,256]{1,0:T(8,128)(2,1)S(1)}, bf16[256,256]{1,0:T(8,128)(2,1)S(1)}, u32[]{:S(2)}, u32[]{:S(2)}) collective-permute-start(bf16[256,256]{1,0:T(8,128)(2,1)S(1)} %get-tuple-element.61.refs_3_), channel_id=1, source_target_pairs={{0,4},{1,5},{2,6},{3,7},{4,0},{5,1},{6,2},{7,3},{8,12},{9,13},{10,... | collective-permute-start | bytes 393224 | tf_op jit(solution)/shard_map/ppermute | solution.py:60
  34.4 5.7 %collective-permute-start.14 = (bf16[512,256]{1,0:T(8,128)(2,1)S(1)}, bf16[512,256]{1,0:T(8,128)(2,1)S(1)}, u32[]{:S(2)}, u32[]{:S(2)}) collective-permute-start(bf16[512,256]{1,0:T(8,128)(2,1)S(1)} %shard_map.104.refs_2_), channel_id=1, source_target_pairs={{0,1},{1,0},{2,3},{3,2},{4,5},{5,4},{6,7},{7,6},{8,9},{9,8},{10,11... | collective-permute-start | bytes 786440 | tf_op jit(solution)/shard_map/ppermute | solution.py:60
  34.5 9.0 %collective-permute-start.16 = (bf16[256,256]{1,0:T(8,128)(2,1)S(1)}, bf16[256,256]{1,0:T(8,128)(2,1)S(1)}, u32[]{:S(2)}, u32[]{:S(2)}) collective-permute-start(bf16[256,256]{1,0:T(8,128)(2,1)S(1)} %get-tuple-element.62.refs_2_), channel_id=1, source_target_pairs={{0,2},{1,3},{2,0},{3,1},{4,6},{5,7},{6,4},{7,5},{8,10},{9,11},{10,... | collective-permute-start | bytes 393224 | tf_op jit(solution)/shard_map/ppermute | solution.py:60
  37.2 2.9 %copy-start.2 = (bf16[512,1024]{1,0:T(8,128)(2,1)S(1)}, bf16[512,1024]{1,0:T(8,128)(2,1)}, u32[]{:S(2)}) copy-start(bf16[512,1024]{1,0:T(8,128)(2,1)} %refs_10_.1) | copy-start | bytes 3145732
  37.2 6.4 %collective-permute-start.18 = (bf16[128,256]{1,0:T(8,128)(2,1)S(1)}, bf16[128,256]{1,0:T(8,128)(2,1)S(1)}, u32[]{:S(2)}, u32[]{:S(2)}) collective-permute-start(bf16[128,256]{1,0:T(8,128)(2,1)S(1)} %get-tuple-element.65.refs_13_), channel_id=1, source_target_pairs={{0,8},{1,9},{2,10},{3,11},{4,12},{5,13},{6,14},{7,15},{8,0},{9,1},... | collective-permute-start | bytes 196616 | tf_op jit(solution)/shard_map/ppermute | solution.py:60
  43.5 1.4 %collective-permute-start.17 = (bf16[256,256]{1,0:T(8,128)(2,1)S(1)}, bf16[256,256]{1,0:T(8,128)(2,1)S(1)}, u32[]{:S(2)}, u32[]{:S(2)}) collective-permute-start(bf16[256,256]{1,0:T(8,128)(2,1)S(1)} %shard_map.107.refs_2_), channel_id=1, source_target_pairs={{0,1},{1,0},{2,3},{3,2},{4,5},{5,4},{6,7},{7,6},{8,9},{9,8},{10,11... | collective-permute-start | bytes 393224 | tf_op jit(solution)/shard_map/ppermute | solution.py:60
  43.6 4.0 %collective-permute-start.19 = (bf16[64,256]{1,0:T(8,128)(2,1)S(1)}, bf16[64,256]{1,0:T(8,128)(2,1)S(1)}, u32[]{:S(2)}, u32[]{:S(2)}) collective-permute-start(bf16[64,256]{1,0:T(8,128)(2,1)S(1)} %get-tuple-element.73.refs_7_.refs_2_), channel_id=1, source_target_pairs={{0,2},{1,3},{2,0},{3,1},{4,6},{5,7},{6,4},{7,5},{8,10},{9,11},{10,... | collective-permute-start | bytes 98312 | tf_op jit(solution)/shard_map/ppermute | solution.py:60
  47.6 1.2 %collective-permute-start.20 = (bf16[64,256]{1,0:T(8,128)(2,1)S(1)}, bf16[64,256]{1,0:T(8,128)(2,1)S(1)}, u32[]{:S(2)}, u32[]{:S(2)}) collective-permute-start(bf16[64,256]{1,0:T(8,128)(2,1)S(1)} %get-tuple-element.78.refs_2_), channel_id=1, source_target_pairs={{0,1},{1,0},{2,3},{3,2},{4,5},{5,4},{6,7},{7,6},{8,9},{9,8},{10,11... | collective-permute-start | bytes 98312 | tf_op jit(solution)/shard_map/ppermute | solution.py:60

commit v11 on v10

--- a/solution.py
+++ b/solution.py
@@ -141,22 +141,27 @@
     out_ref[...] = (own_ref[...].astype(F32) + got_ref[...].astype(F32)).astype(out_ref.dtype)
 
 
-def dnormed_kernel(groups, message_ref, *refs):
-    cots, weights = refs[: SLAB - 1], refs[SLAB - 1 : SLAB - 1 + groups]
-    dnormed_ref, cot_ref = refs[SLAB - 1 + groups :]
-    block, outputs = cots[0].shape
+def dnormed_kernel(groups, members, *refs):
+    cots, weights = refs[: len(members)], refs[len(members) : len(members) + groups]
+    dnormed_ref, cot_ref = refs[len(members) + groups :]
+    _, block, outputs = cot_ref.shape
     width = dnormed_ref.shape[2]
     rows = weights[0].shape[1]
     me = lax.axis_index("dp")
-    for i in range(outputs // width):
-        cot_ref[1, :, part(i, width)] = message_ref[part(4 + i, block), :]
-    for r, ref in zip((0, 2, 3), cots):
-        cot_ref[r] = ref[...]
-    for r in range(SLAB):
-        total = dot(cot_ref[r, :, cut(me, rows)], weights[0][0], 1, 0)
+    for i, (r, ref) in enumerate(zip(members, cots)):
+        if r == 1:
+            for p in range(outputs // width):
+                cot_ref[i, :, part(p, width)] = ref[part(4 + p, block), :]
+        else:
+            cot_ref[i] = ref[...]
+        total = dot(cot_ref[i, :, cut(me, rows)], weights[0][0], 1, 0)
         for j in range(1, groups):
-            total = total + dot(cot_ref[r, :, cut(jnp.bitwise_xor(me, j), rows)], weights[j][0], 1, 0)
-        dnormed_ref[r] = total
+            total = total + dot(cot_ref[i, :, cut(jnp.bitwise_xor(me, j), rows)], weights[j][0], 1, 0)
+        dnormed_ref[i] = total
+
+
+def base_kernel(*refs):
+    refs[-1][...] = from_slabs(False, refs[:-1])
 
 
 def from_slabs(backward, refs):
@@ -169,8 +174,8 @@
 
 
 def middle_kernel(*refs):
-    own_ref, message_ref, token_far, own_state, far_state, near_state, dnormed_ref = refs[:7]
-    *before, normed_ref, back_near, back_far, u_ref, slab_ref, running = refs[7:]
+    own_ref, message_ref, token_far, own_state, far_state, near_state, base_ref, dnormed_a, dnormed_b = refs[:9]
+    normed_ref, back_near, back_far, u_ref, slab_ref, running = refs[9:]
     _, block, width = normed_ref.shape
     heads = width // DH
     size = 2 * block
@@ -179,7 +184,7 @@
     running[member(1)] = near_state[part(0, DH), :].astype(F32)
     running[member(2)] = far_state[part(0, DH), :].astype(F32)
     running[member(3)] = near_state[part(1, DH), :].astype(F32)
-    total = from_slabs(False, before)
+    total = base_ref[...]
     for p in range(SLAB):
         total, running[p] = total + running[p], total
     sums = [jnp.zeros((DH, DH), F32)] * heads
@@ -193,7 +198,7 @@
             scale = lax.rsqrt(jnp.mean(mixed * mixed, axis=-1, keepdims=True) + EPSILON)
             normed = mixed * scale
             normed_ref[r, :, head(h)] = normed.astype(BF16)
-            dnormed = dnormed_ref[r, :, head(h)]
+            dnormed = dnormed_a[r, :, head(h)] if r < 3 else dnormed_b[0, :, head(h)]
             along = jnp.mean(dnormed * normed, axis=-1, keepdims=True)
             dmixed = ((dnormed - normed * along) * scale).astype(BF16)
             out[:block, head(h)] = dmixed
@@ -277,16 +282,16 @@
         gv_ref[:, at] = jnp.concatenate(gvs, axis=1).astype(BF16)
 
 
-def product_kernel(slabs, cot_ref, normed_ref, keep_ref, send_ref):
+def product_kernel(slabs, cot_a, cot_b, normed_ref, keep_ref, send_ref):
     me = lax.axis_index("dp")
     slab = lax.div(lax.axis_index("seq"), SLAB)
     rows = keep_ref.shape[0] // slabs
     for j, out in enumerate((send_ref, keep_ref)):
         for d in range(slabs):
             at = jnp.bitwise_xor(me, 1 - j) * slabs + jnp.bitwise_xor(slab, d)
-            total = dot(cot_ref[0, :, cut(at, rows)], normed_ref[0], 0, 0)
-            for r in range(1, SLAB):
-                total = total + dot(cot_ref[r, :, cut(at, rows)], normed_ref[r], 0, 0)
+            total = dot(cot_b[0, :, cut(at, rows)], normed_ref[3], 0, 0)
+            for r in range(3):
+                total = total + dot(cot_a[r, :, cut(at, rows)], normed_ref[r], 0, 0)
             out[part(d, rows), :] = total.astype(out.dtype)
 
 
@@ -378,20 +383,25 @@
     near_state = near(near_state, bits=1)
     (slab_kv,) = call(total_kernel, [((DH, width), BF16)], own_state, far_state, near_state)
     (far_tokens,) = call(pair_kernel, [((4 * rows, width), BF16)], message, far_tokens)
-    cot_yc = near(after(cot_y, far_tokens), bits=1)
     far_tokens = near(far_tokens, bits=2)
-    before, _ = doubling(slab_kv, 22 * 10**8)
+    before, last_kv = doubling(slab_kv, 14 * 10**8)
+    cot_yc = near(after(cot_y, last_kv), bits=1)
+    weights = (columns, *w_far)
     dnormed, cots = call(
-        functools.partial(dnormed_kernel, dp),
-        [((SLAB, rows, width), F32), ((SLAB, rows, outputs), BF16)],
-        message, cot, cot_y, cot_yc, columns, *w_far,
+        functools.partial(dnormed_kernel, dp, (0, 1, 2)),
+        [((3, rows, width), F32), ((3, rows, outputs), BF16)], cot, message, cot_y, *weights,
+    )
+    (base,) = call(base_kernel, [((DH, width), F32)], *before, cost=23 * 10**8, wait=[far_tokens])
+    dnormed_b, cot_b = call(
+        functools.partial(dnormed_kernel, dp, (3,)),
+        [((1, rows, width), F32), ((1, rows, outputs), BF16)], cot_yc, *weights,
     )
     w_all = [x for w in w_far for x in (w, near(after(w, dnormed), bits=1))]
     normed, back, back_far, u, slab_u = call(
         middle_kernel,
         [((SLAB, rows, width), BF16)] + [((2 * rows + 2 * DH, width), BF16)] * 2
         + [((SLAB, DH, width), F32), ((DH, width), BF16)],
-        own_tokens, message, far_tokens, own_state, far_state, near_state, dnormed, *before,
+        own_tokens, message, far_tokens, own_state, far_state, near_state, base, dnormed, dnormed_b,
         cost=10**10, scratch=[pltpu.VMEM((SLAB, DH, width), F32)],
     )
     tuned = dp == 2 and slabs == 4 and outputs // (dp * seq) % 8 == 0
@@ -399,23 +409,23 @@
     if tuned:
         keep, send = call(
             functools.partial(product_kernel, slabs),
-            [((outputs // dp, width), F32), ((outputs // dp, width), BF16)], cots, normed,
+            [((outputs // dp, width), F32), ((outputs // dp, width), BF16)], cots, cot_b, normed,
         )
         got = flip(send, "dp", dp, 1)
     back_far = near(back_far, bits=2)
-    behind, last_u = doubling(slab_u, 10**9)
+    behind, last_u = doubling(slab_u, 15 * 10**8)
     if tuned:
         keep, send = call(
             split_kernel, [((2 * piece, width), F32), ((2 * piece, width), BF16)], keep, got, wait=w_all[1::2]
         )
         got = near(send, bits=SLAB)
+    (send,) = call(relay_kernel, [((2 * rows + 2 * DH, width), BF16)], back, back_far)
+    back_core = near(send, bits=1)
     later, later_far = call(
         later_kernel, [((2 * DH, width), BF16)] * 2, *behind, u, cost=2 * 10**9,
         scratch=[pltpu.VMEM((SLAB, DH, width), F32)],
     )
     later_far = near(later_far, bits=2)
-    (send,) = call(relay_kernel, [((2 * rows + 2 * DH, width), BF16)], back, back_far)
-    back_core = near(send, bits=1)
     if tuned:
         keep, send = call(
             split_again_kernel, [((piece, width), F32), ((piece, width), BF16)], keep, got, cost=2 * 10**9
@@ -431,7 +441,7 @@
     later_core = near(send, bits=1)
     if tuned:
         keep, share = call(
-            share_kernel, [((piece // 2, width), BF16)] * 2, keep, got, cost=2 * 10**9,
+            share_kernel, [((piece // 2, width), BF16)] * 2, keep, got, cost=3 * 10**9,
             scratch=[pltpu.VMEM((piece, width), F32)],
         )
         got = near(share, bits=2)

time: 49.6 us -> 52.3 us (1.054)
  waiting for transfers between devices: 12.3 us -> 13.7 us
  starting transfers between devices: 25.8 us -> 26.8 us
    ppermute x21, waiting for transfers between devices: 12.3 us -> 13.7 us  [flip(): return lax.ppermute(x, axis, [(i, i ^ bits) for i in range(count)])]
    ppermute x21, starting transfers between devices: 25.8 us -> 26.8 us  [flip(): return lax.ppermute(x, axis, [(i, i ^ bits) for i in range(count)])]
    pallas_call x20 -> x22, Pallas kernels: 10.5 us -> 10.7 us  [__call__(): pl.pallas_call(inner, out_shape=[jax.ShapeDtypeStruct(s, d) for s, d in o...]
  transfers between devices with their start and end apart: 21 -> 21, of which waited for: 9 -> 11; matrix products, arithmetic and copies ran while one was open for 0% -> 0% of each run, Pallas kernels for 17% -> 16%
where the time goes in v11:
time: 52.3 us; the launch traced here: 52.1 us
  starting transfers between devices  26.8 us (51%)
  waiting for transfers between devices  13.7 us (26%)
  Pallas kernels  10.7 us (20%)
  between operations  0.85 us (2%)
    ppermute x21, starting transfers between devices, flip(): return lax.ppermute(x, axis, [(i, i ^ bits) for i in range(count)])  26.8 us
    ppermute x21, waiting for transfers between devices, flip(): return lax.ppermute(x, axis, [(i, i ^ bits) for i in range(count)])  13.7 us
    pallas_call x22, Pallas kernels, __call__(): pl.pallas_call(inner, out_shape=[jax.ShapeDtypeStruct(s, d) for s, d in o...  10.7 us
  transfers between devices with their start and end apart: 21, of which 11 were waited for; matrix products, arithmetic and copies ran while one was open for 0% of the time, Pallas kernels for 16%

profile of v11, /device:TPU:0, one launch (start us, length us, event | category | flops | bytes accessed | tf_op | source)
XLA Modules:
  0.0 52.1 jit_solution(10580356773669343726)
XLA Ops:
  0.7 1.6 %shard_map.92 = (f32[128,256]{1,0:T(8,128)S(1)}, bf16[128,256]{1,0:T(8,128)(2,1)S(1)}, bf16[256,256]{1,0:T(8,128)(2,1)S(1)}, bf16[2,512,256]{2,1,0:T(8,128)(2,1)S(1)}) custom-call(bf16[128,1024]{1,0:T(8,128)(2,1)} %bitcast.8, bf16[128,1024]{1,0:T(8,128)(2,1)} %bitcast.12, bf16[512,1024]{1,0:T(8,128)(2,1)} %refs_10_.1), custom_call_target="tpu_custom_call" | custom-call | flops 1 | bytes 1 | tf_op jit(solution)/shard_map/pallas_call | solution.py:42
  2.2 3.0 %collective-permute-start.1 = (bf16[256,256]{1,0:T(8,128)(2,1)S(1)}, bf16[256,256]{1,0:T(8,128)(2,1)S(1)}, u32[]{:S(2)}, u32[]{:S(2)}) collective-permute-start(bf16[256,256]{1,0:T(8,128)(2,1)S(1)} %get-tuple-element.49), channel_id=1, source_target_pairs={{0,2},{1,3},{2,0},{3,1},{4,6},{5,7},{6,4},{7,5},{8,10},{9,11},{10,... | collective-permute-start | bytes 393224 | tf_op jit(solution)/shard_map/ppermute | solution.py:60
  5.3 1.5 %collective-permute-start.7 = (bf16[2,512,256]{2,1,0:T(8,128)(2,1)S(1)}, bf16[2,512,256]{2,1,0:T(8,128)(2,1)S(1)}, u32[]{:S(2)}, u32[]{:S(2)}) collective-permute-start(bf16[2,512,256]{2,1,0:T(8,128)(2,1)S(1)} %get-tuple-element.51.refs_3_.refs_1_), channel_id=1, source_target_pairs={{0,16},{16,0},{1,17},{17,1},{2,18},{18,2},{3,19},{19,3},{4,20},{20... | collective-permute-start | bytes 1572872 | tf_op jit(solution)/shard_map/ppermute | solution.py:60
  6.8 1.4 %shard_map.93 = (bf16[4,2,128,128]{3,2,1,0:T(8,128)(2,1)S(1)}, bf16[256,256]{1,0:T(8,128)(2,1)S(1)}, bf16[1024,256]{1,0:T(8,128)(2,1)S(1)}, bf16[256,256]{1,0:T(8,128)(2,1)S(1)}, bf16[128,1024]{1,0:T(8,128)(2,1)S(1)}) custom-call(bf16[128,1024]{1,0:T(8,128)(2,1)S(1)} %bitcast.18, bf16[128,1024]{1,0:T(8,128)(2,1)S(1)} %bitcast.9, ...), custom_call_target="tpu_custom_call" | custom-call | flops 1 | bytes 1 | tf_op jit(solution)/shard_map/pallas_call | solution.py:42
  8.2 0.5 %collective-permute-done.1.refs_1_.refs_4_ = bf16[256,256]{1,0:T(8,128)(2,1)S(1)} collective-permute-done((bf16[256,256]{1,0:T(8,128)(2,1)S(1)}, bf16[256,256]{1,0:T(8,128)(2,1)S(1)}, u32[]{:S(2)}, u32[]{:S(2)}) %collective-permute-start.1) | collective-permute-done | bytes 131104 | tf_op jit(solution)/shard_map/ppermute | solution.py:60
  8.9 1.8 %collective-permute-start.6 = (bf16[128,1024]{1,0:T(8,128)(2,1)S(1)}, bf16[128,1024]{1,0:T(8,128)(2,1)S(1)}, u32[]{:S(2)}, u32[]{:S(2)}) collective-permute-start(bf16[128,1024]{1,0:T(8,128)(2,1)S(1)} %get-tuple-element.50), channel_id=1, source_target_pairs={{0,2},{1,3},{2,0},{3,1},{4,6},{5,7},{6,4},{7,5},{8,10},{9,11},{10,... | collective-permute-start | bytes 786440 | tf_op jit(solution)/shard_map/ppermute | solution.py:60
  10.7 1.6 %collective-permute-start.4 = (bf16[128,256]{1,0:T(8,128)(2,1)S(1)}, bf16[128,256]{1,0:T(8,128)(2,1)S(1)}, u32[]{:S(2)}, u32[]{:S(2)}) collective-permute-start(bf16[128,256]{1,0:T(8,128)(2,1)S(1)} %shard_map.95.refs_2_.refs_0_), channel_id=1, source_target_pairs={{0,4},{1,5},{2,6},{3,7},{4,0},{5,1},{6,2},{7,3},{8,12},{9,13},{10,... | collective-permute-start | bytes 196616 | tf_op jit(solution)/shard_map/ppermute | solution.py:60
  12.4 1.3 %collective-permute-start.3 = (bf16[512,256]{1,0:T(8,128)(2,1)S(1)}, bf16[512,256]{1,0:T(8,128)(2,1)S(1)}, u32[]{:S(2)}, u32[]{:S(2)}) collective-permute-start(bf16[512,256]{1,0:T(8,128)(2,1)S(1)} %shard_map.96.refs_2_), channel_id=1, source_target_pairs={{0,2},{1,3},{2,0},{3,1},{4,6},{5,7},{6,4},{7,5},{8,10},{9,11},{10,... | collective-permute-start | bytes 786440 | tf_op jit(solution)/shard_map/ppermute | solution.py:60
  13.7 1.3 %collective-permute-done.4.refs_1_.refs_0_ = bf16[128,256]{1,0:T(8,128)(2,1)S(1)} collective-permute-done((bf16[128,256]{1,0:T(8,128)(2,1)S(1)}, bf16[128,256]{1,0:T(8,128)(2,1)S(1)}, u32[]{:S(2)}, u32[]{:S(2)}) %collective-permute-start.4) | collective-permute-done | bytes 65568 | tf_op jit(solution)/shard_map/ppermute | solution.py:60
  15.1 2.7 %collective-permute-start.5 = (bf16[128,256]{1,0:T(8,128)(2,1)S(1)}, bf16[128,256]{1,0:T(8,128)(2,1)S(1)}, u32[]{:S(2)}, u32[]{:S(2)}) collective-permute-start(bf16[128,256]{1,0:T(8,128)(2,1)S(1)} %shard_map.97.refs_5_), channel_id=1, source_target_pairs={{0,8},{1,9},{2,10},{3,11},{4,12},{5,13},{6,14},{7,15},{8,0},{9,1},... | collective-permute-start | bytes 196616 | tf_op jit(solution)/shard_map/ppermute | solution.py:60
  18.0 0.6 %collective-permute-done.7.refs_4_.refs_2_.refs_11_ = bf16[2,512,256]{2,1,0:T(8,128)(2,1)S(1)} collective-permute-done((bf16[2,512,256]{2,1,0:T(8,128)(2,1)S(1)}, bf16[2,512,256]{2,1,0:T(8,128)(2,1)S(1)}, u32[]{:S(2)}, u32[]{:S(2)}) %collective-permute-start.7) | collective-permute-done | bytes 524320 | tf_op jit(solution)/shard_map/ppermute | solution.py:60
  18.7 0.4 shard_map.98
  19.2 1.2 %collective-permute-done.5.refs_1_ = bf16[128,256]{1,0:T(8,128)(2,1)S(1)} collective-permute-done((bf16[128,256]{1,0:T(8,128)(2,1)S(1)}, bf16[128,256]{1,0:T(8,128)(2,1)S(1)}, u32[]{:S(2)}, u32[]{:S(2)}) %collective-permute-start.5) | collective-permute-done | bytes 65568 | tf_op jit(solution)/shard_map/ppermute | solution.py:60
  20.3 2.9 %collective-permute-done.3.refs_3_.refs_2_ = bf16[512,256]{1,0:T(8,128)(2,1)S(1)} collective-permute-done((bf16[512,256]{1,0:T(8,128)(2,1)S(1)}, bf16[512,256]{1,0:T(8,128)(2,1)S(1)}, u32[]{:S(2)}, u32[]{:S(2)}) %collective-permute-start.3) | collective-permute-done | bytes 262176 | tf_op jit(solution)/shard_map/ppermute | solution.py:60
  23.5 0.8 %shard_map.101 = (bf16[4,128,256]{2,1,0:T(8,128)(2,1)S(1)}, bf16[512,256]{1,0:T(8,128)(2,1)S(1)}, bf16[512,256]{1,0:T(8,128)(2,1)S(1)}, f32[4,128,256]{2,1,0:T(8,128)S(1)}, bf16[128,256]{1,0:T(8,128)(2,1)S(1)}) custom-call(bf16[256,256]{1,0:T(8,128)(2,1)S(1)} %get-tuple-element.45.refs_0_.refs_7_, ...), custom_call_target="tpu_custom_call" | custom-call | flops 10000000000 | bytes 1 | tf_op jit(solution)/shard_map/pallas_call | solution.py:42
  24.3 1.9 %collective-permute-start.11 = (bf16[128,256]{1,0:T(8,128)(2,1)S(1)}, bf16[128,256]{1,0:T(8,128)(2,1)S(1)}, u32[]{:S(2)}, u32[]{:S(2)}) collective-permute-start(bf16[128,256]{1,0:T(8,128)(2,1)S(1)} %get-tuple-element.60.refs_3_.refs_0_), channel_id=1, source_target_pairs={{0,4},{1,5},{2,6},{3,7},{4,0},{5,1},{6,2},{7,3},{8,12},{9,13},{10,... | collective-permute-start | bytes 196616 | tf_op jit(solution)/shard_map/ppermute | solution.py:60
  26.2 0.8 %shard_map.102 = (f32[512,256]{1,0:T(8,128)S(1)}, bf16[512,256]{1,0:T(8,128)(2,1)S(1)}) custom-call(bf16[3,128,1024]{2,1,0:T(8,128)(2,1)S(1)} %get-tuple-element.57.refs_0_, bf16[1,128,1024]{2,1,0:T(8,128)(2,1)S(1)} %get-tuple-element.58.refs_1_, bf16[4,128,256]{2,1,0:T(8,128)(2,1)S(1)} %get-tuple-element.59.refs_2_, ...), custom_call_target="tpu_custom_call" | custom-call | flops 1 | bytes 1 | tf_op jit(solution)/shard_map/pallas_call | solution.py:42
  26.9 1.5 %collective-permute-start.10 = (bf16[512,256]{1,0:T(8,128)(2,1)S(1)}, bf16[512,256]{1,0:T(8,128)(2,1)S(1)}, u32[]{:S(2)}, u32[]{:S(2)}) collective-permute-start(bf16[512,256]{1,0:T(8,128)(2,1)S(1)} %get-tuple-element.62.refs_2_), channel_id=1, source_target_pairs={{0,16},{16,0},{1,17},{17,1},{2,18},{18,2},{3,19},{19,3},{4,20},{20... | collective-permute-start | bytes 786440 | tf_op jit(solution)/shard_map/ppermute | solution.py:60
  28.5 1.5 %collective-permute-start.9 = (bf16[512,256]{1,0:T(8,128)(2,1)S(1)}, bf16[512,256]{1,0:T(8,128)(2,1)S(1)}, u32[]{:S(2)}, u32[]{:S(2)}) collective-permute-start(bf16[512,256]{1,0:T(8,128)(2,1)S(1)} %get-tuple-element.56), channel_id=1, source_target_pairs={{0,2},{1,3},{2,0},{3,1},{4,6},{5,7},{6,4},{7,5},{8,10},{9,11},{10,... | collective-permute-start | bytes 786440 | tf_op jit(solution)/shard_map/ppermute | solution.py:60
  30.0 2.7 %collective-permute-start.15 = (bf16[128,256]{1,0:T(8,128)(2,1)S(1)}, bf16[128,256]{1,0:T(8,128)(2,1)S(1)}, u32[]{:S(2)}, u32[]{:S(2)}) collective-permute-start(bf16[128,256]{1,0:T(8,128)(2,1)S(1)} %shard_map.103.refs_2_), channel_id=1, source_target_pairs={{0,8},{1,9},{2,10},{3,11},{4,12},{5,13},{6,14},{7,15},{8,0},{9,1},... | collective-permute-start | bytes 196616 | tf_op jit(solution)/shard_map/ppermute | solution.py:60
  32.7 1.9 %collective-permute-done.10.refs_1_ = bf16[512,256]{1,0:T(8,128)(2,1)S(1)} collective-permute-done((bf16[512,256]{1,0:T(8,128)(2,1)S(1)}, bf16[512,256]{1,0:T(8,128)(2,1)S(1)}, u32[]{:S(2)}, u32[]{:S(2)}) %collective-permute-start.10) | collective-permute-done | bytes 262176 | tf_op jit(solution)/shard_map/ppermute | solution.py:60
  34.6 0.4 collective-permute-start.14
  35.0 0.8 %collective-permute-done.9.refs_1_ = bf16[512,256]{1,0:T(8,128)(2,1)S(1)} collective-permute-done((bf16[512,256]{1,0:T(8,128)(2,1)S(1)}, bf16[512,256]{1,0:T(8,128)(2,1)S(1)}, u32[]{:S(2)}, u32[]{:S(2)}) %collective-permute-start.9) | collective-permute-done | bytes 262176 | tf_op jit(solution)/shard_map/ppermute | solution.py:60
  36.0 1.6 %collective-permute-start.16 = (bf16[256,256]{1,0:T(8,128)(2,1)S(1)}, bf16[256,256]{1,0:T(8,128)(2,1)S(1)}, u32[]{:S(2)}, u32[]{:S(2)}) collective-permute-start(bf16[256,256]{1,0:T(8,128)(2,1)S(1)} %get-tuple-element.68.refs_2_), channel_id=1, source_target_pairs={{0,2},{1,3},{2,0},{3,1},{4,6},{5,7},{6,4},{7,5},{8,10},{9,11},{10,... | collective-permute-start | bytes 393224 | tf_op jit(solution)/shard_map/ppermute | solution.py:60
  37.6 2.0 %collective-permute-done.14.refs_1_ = bf16[256,256]{1,0:T(8,128)(2,1)S(1)} collective-permute-done((bf16[256,256]{1,0:T(8,128)(2,1)S(1)}, bf16[256,256]{1,0:T(8,128)(2,1)S(1)}, u32[]{:S(2)}, u32[]{:S(2)}) %collective-permute-start.14) | collective-permute-done | bytes 131104 | tf_op jit(solution)/shard_map/ppermute | solution.py:60
  39.7 2.6 %collective-permute-start.18 = (bf16[128,256]{1,0:T(8,128)(2,1)S(1)}, bf16[128,256]{1,0:T(8,128)(2,1)S(1)}, u32[]{:S(2)}, u32[]{:S(2)}) collective-permute-start(bf16[128,256]{1,0:T(8,128)(2,1)S(1)} %get-tuple-element.69.refs_13_), channel_id=1, source_target_pairs={{0,8},{1,9},{2,10},{3,11},{4,12},{5,13},{6,14},{7,15},{8,0},{9,1},... | collective-permute-start | bytes 196616 | tf_op jit(solution)/shard_map/ppermute | solution.py:60
  42.4 3.4 %shard_map.108 = (bf16[128,1024]{1,0:T(8,128)(2,1)}, bf16[128,1024]{1,0:T(8,128)(2,1)}, f32[4,128,256]{2,1,0:T(8,128)S(1)}, f32[4,128,256]{2,1,0:T(8,128)S(1)}, bf16[128,1024]{1,0:T(8,128)(2,1)S(1)}) custom-call(bf16[512,256]{1,0:T(8,128)(2,1)S(1)} %get-tuple-element.55.refs_0_, bf16[512,256]{1,0:T(8,128)(2,1)S(1)} %collective-permute-done.9.refs_1_, ...), custom_call_target="tpu_custom_call" | custom-call | flops 1 | bytes 1 | tf_op jit(solution)/shard_map/pallas_call | solution.py:42
  45.9 2.3 %collective-permute-start.19 = (bf16[64,256]{1,0:T(8,128)(2,1)S(1)}, bf16[64,256]{1,0:T(8,128)(2,1)S(1)}, u32[]{:S(2)}, u32[]{:S(2)}) collective-permute-start(bf16[64,256]{1,0:T(8,128)(2,1)S(1)} %get-tuple-element.77.refs_7_.refs_2_), channel_id=1, source_target_pairs={{0,2},{1,3},{2,0},{3,1},{4,6},{5,7},{6,4},{7,5},{8,10},{9,11},{10,... | collective-permute-start | bytes 98312 | tf_op jit(solution)/shard_map/ppermute | solution.py:60
  48.2 1.1 %shard_map.111 = (bf16[128,1024]{1,0:T(8,128)(2,1)}, bf16[128,1024]{1,0:T(8,128)(2,1)}) custom-call(bf16[256,256]{1,0:T(8,128)(2,1)S(1)} %get-tuple-element.72.refs_0_, bf16[256,256]{1,0:T(8,128)(2,1)S(1)} %collective-permute-done.16.refs_1_, bf16[256,256]{1,0:T(8,128)(2,1)S(1)} %collective-permute-done.17.refs_2_, bf16[128,1024]{1,0:T(8,128)(2,1)S(1)} %bitcast.11, ...), custom_call_target="tpu_custom_call" | custom-call | flops 1 | bytes 1 | tf_op jit(solution)/shard_map/pallas_call | solution.py:42
  49.3 0.9 %collective-permute-done.19.refs_1_ = bf16[64,256]{1,0:T(8,128)(2,1)S(1)} collective-permute-done((bf16[64,256]{1,0:T(8,128)(2,1)S(1)}, bf16[64,256]{1,0:T(8,128)(2,1)S(1)}, u32[]{:S(2)}, u32[]{:S(2)}) %collective-permute-start.19) | collective-permute-done | bytes 32800 | tf_op jit(solution)/shard_map/ppermute | solution.py:60
  50.2 1.2 %collective-permute-done.20.refs_1_ = bf16[64,256]{1,0:T(8,128)(2,1)S(1)} collective-permute-done((bf16[64,256]{1,0:T(8,128)(2,1)S(1)}, bf16[64,256]{1,0:T(8,128)(2,1)S(1)}, u32[]{:S(2)}, u32[]{:S(2)}) %collective-permute-start.20) | collective-permute-done | bytes 32800 | tf_op jit(solution)/shard_map/ppermute | solution.py:60
  51.4 0.7 %shard_map.113 = f32[32,1024]{1,0:T(8,128)} custom-call(bf16[64,256]{1,0:T(8,128)(2,1)S(1)} %get-tuple-element.81.refs_0_, bf16[64,256]{1,0:T(8,128)(2,1)S(1)} %collective-permute-done.20.refs_1_, bf16[64,256]{1,0:T(8,128)(2,1)S(1)} %get-tuple-element.82.refs_2_), custom_call_target="tpu_custom_call" | custom-call | flops 1 | bytes 1 | tf_op jit(solution)/shard_map/pallas_call | solution.py:42
  (42 shorter events, 1.3 us)
Async XLA Ops:
  0.6 6.1 %copy-start = (bf16[1,128,1024]{2,1,0:T(8,128)(2,1)S(1)}, bf16[1,128,1024]{2,1,0:T(8,128)(2,1)}, u32[]{:S(2)}) copy-start(bf16[1,128,1024]{2,1,0:T(8,128)(2,1)} %param.6) | copy-start | bytes 786436
  0.6 6.1 %copy-start.1 = (bf16[1,128,1024]{2,1,0:T(8,128)(2,1)S(1)}, bf16[1,128,1024]{2,1,0:T(8,128)(2,1)}, u32[]{:S(2)}) copy-start(bf16[1,128,1024]{2,1,0:T(8,128)(2,1)} %param.7) | copy-start | bytes 786436
  0.7 6.1 %copy-start.3 = (bf16[1,128,1024]{2,1,0:T(8,128)(2,1)S(1)}, bf16[1,128,1024]{2,1,0:T(8,128)(2,1)}, u32[]{:S(2)}) copy-start(bf16[1,128,1024]{2,1,0:T(8,128)(2,1)} %param.8) | copy-start | bytes 786436
  0.7 6.1 %copy-start.4 = (bf16[1,128,1024]{2,1,0:T(8,128)(2,1)S(1)}, bf16[1,128,1024]{2,1,0:T(8,128)(2,1)}, u32[]{:S(2)}) copy-start(bf16[1,128,1024]{2,1,0:T(8,128)(2,1)} %param.5) | copy-start | bytes 786436
  2.2 6.5 %collective-permute-start.1 = (bf16[256,256]{1,0:T(8,128)(2,1)S(1)}, bf16[256,256]{1,0:T(8,128)(2,1)S(1)}, u32[]{:S(2)}, u32[]{:S(2)}) collective-permute-start(bf16[256,256]{1,0:T(8,128)(2,1)S(1)} %get-tuple-element.49), channel_id=1, source_target_pairs={{0,2},{1,3},{2,0},{3,1},{4,6},{5,7},{6,4},{7,5},{8,10},{9,11},{10,... | collective-permute-start | bytes 393224 | tf_op jit(solution)/shard_map/ppermute | solution.py:60
  5.3 13.4 %collective-permute-start.7 = (bf16[2,512,256]{2,1,0:T(8,128)(2,1)S(1)}, bf16[2,512,256]{2,1,0:T(8,128)(2,1)S(1)}, u32[]{:S(2)}, u32[]{:S(2)}) collective-permute-start(bf16[2,512,256]{2,1,0:T(8,128)(2,1)S(1)} %get-tuple-element.51.refs_3_.refs_1_), channel_id=1, source_target_pairs={{0,16},{16,0},{1,17},{17,1},{2,18},{18,2},{3,19},{19,3},{4,20},{20... | collective-permute-start | bytes 1572872 | tf_op jit(solution)/shard_map/ppermute | solution.py:60
  8.1 4.2 %collective-permute-start = (bf16[1024,256]{1,0:T(8,128)(2,1)S(1)}, bf16[1024,256]{1,0:T(8,128)(2,1)S(1)}, u32[]{:S(2)}, u32[]{:S(2)}) collective-permute-start(bf16[1024,256]{1,0:T(8,128)(2,1)S(1)} %get-tuple-element.46.refs_8_), channel_id=1, source_target_pairs={{0,1},{1,0},{2,3},{3,2},{4,5},{5,4},{6,7},{7,6},{8,9},{9,8},{10,11... | collective-permute-start | bytes 1572872 | tf_op jit(solution)/shard_map/ppermute | solution.py:60
  8.8 1.9 %collective-permute-start.2 = (bf16[256,256]{1,0:T(8,128)(2,1)S(1)}, bf16[256,256]{1,0:T(8,128)(2,1)S(1)}, u32[]{:S(2)}, u32[]{:S(2)}) collective-permute-start(bf16[256,256]{1,0:T(8,128)(2,1)S(1)} %shard_map.94.refs_3_), channel_id=1, source_target_pairs={{0,1},{1,0},{2,3},{3,2},{4,5},{5,4},{6,7},{7,6},{8,9},{9,8},{10,11... | collective-permute-start | bytes 393224 | tf_op jit(solution)/shard_map/ppermute | solution.py:60
  8.9 9.2 %collective-permute-start.6 = (bf16[128,1024]{1,0:T(8,128)(2,1)S(1)}, bf16[128,1024]{1,0:T(8,128)(2,1)S(1)}, u32[]{:S(2)}, u32[]{:S(2)}) collective-permute-start(bf16[128,1024]{1,0:T(8,128)(2,1)S(1)} %get-tuple-element.50), channel_id=1, source_target_pairs={{0,2},{1,3},{2,0},{3,1},{4,6},{5,7},{6,4},{7,5},{8,10},{9,11},{10,... | collective-permute-start | bytes 786440 | tf_op jit(solution)/shard_map/ppermute | solution.py:60
  10.7 4.3 %collective-permute-start.4 = (bf16[128,256]{1,0:T(8,128)(2,1)S(1)}, bf16[128,256]{1,0:T(8,128)(2,1)S(1)}, u32[]{:S(2)}, u32[]{:S(2)}) collective-permute-start(bf16[128,256]{1,0:T(8,128)(2,1)S(1)} %shard_map.95.refs_2_.refs_0_), channel_id=1, source_target_pairs={{0,4},{1,5},{2,6},{3,7},{4,0},{5,1},{6,2},{7,3},{8,12},{9,13},{10,... | collective-permute-start | bytes 196616 | tf_op jit(solution)/shard_map/ppermute | solution.py:60
  12.4 10.8 %collective-permute-start.3 = (bf16[512,256]{1,0:T(8,128)(2,1)S(1)}, bf16[512,256]{1,0:T(8,128)(2,1)S(1)}, u32[]{:S(2)}, u32[]{:S(2)}) collective-permute-start(bf16[512,256]{1,0:T(8,128)(2,1)S(1)} %shard_map.96.refs_2_), channel_id=1, source_target_pairs={{0,2},{1,3},{2,0},{3,1},{4,6},{5,7},{6,4},{7,5},{8,10},{9,11},{10,... | collective-permute-start | bytes 786440 | tf_op jit(solution)/shard_map/ppermute | solution.py:60
  15.1 5.3 %collective-permute-start.5 = (bf16[128,256]{1,0:T(8,128)(2,1)S(1)}, bf16[128,256]{1,0:T(8,128)(2,1)S(1)}, u32[]{:S(2)}, u32[]{:S(2)}) collective-permute-start(bf16[128,256]{1,0:T(8,128)(2,1)S(1)} %shard_map.97.refs_5_), channel_id=1, source_target_pairs={{0,8},{1,9},{2,10},{3,11},{4,12},{5,13},{6,14},{7,15},{8,0},{9,1},... | collective-permute-start | bytes 196616 | tf_op jit(solution)/shard_map/ppermute | solution.py:60
  18.0 5.2 %collective-permute-start.8 = (bf16[128,1024]{1,0:T(8,128)(2,1)S(1)}, bf16[128,1024]{1,0:T(8,128)(2,1)S(1)}, u32[]{:S(2)}, u32[]{:S(2)}) collective-permute-start(bf16[128,1024]{1,0:T(8,128)(2,1)S(1)} %collective-permute-done.6.refs_2_), channel_id=1, source_target_pairs={{0,1},{1,0},{2,3},{3,2},{4,5},{5,4},{6,7},{7,6},{8,9},{9,8},{10,11... | collective-permute-start | bytes 786440 | tf_op jit(solution)/shard_map/ppermute | solution.py:60
  19.1 15.5 %collective-permute-start.12 = (bf16[2,512,256]{2,1,0:T(8,128)(2,1)S(1)}, bf16[2,512,256]{2,1,0:T(8,128)(2,1)S(1)}, u32[]{:S(2)}, u32[]{:S(2)}) collective-permute-start(bf16[2,512,256]{2,1,0:T(8,128)(2,1)S(1)} %collective-permute-done.7.refs_4_.refs_2_.refs_11_), channel_id=1, source_target_pairs={{0,1},{1,0},{2,3},{3,2},{4,5},{5,4},{6,7},{7,6},{8,9},{9,8},{10,11... | collective-permute-start | bytes 1572872 | tf_op jit(solution)/shard_map/ppermute | solution.py:60
  24.3 5.7 %collective-permute-start.11 = (bf16[128,256]{1,0:T(8,128)(2,1)S(1)}, bf16[128,256]{1,0:T(8,128)(2,1)S(1)}, u32[]{:S(2)}, u32[]{:S(2)}) collective-permute-start(bf16[128,256]{1,0:T(8,128)(2,1)S(1)} %get-tuple-element.60.refs_3_.refs_0_), channel_id=1, source_target_pairs={{0,4},{1,5},{2,6},{3,7},{4,0},{5,1},{6,2},{7,3},{8,12},{9,13},{10,... | collective-permute-start | bytes 196616 | tf_op jit(solution)/shard_map/ppermute | solution.py:60
  26.9 7.6 %collective-permute-start.10 = (bf16[512,256]{1,0:T(8,128)(2,1)S(1)}, bf16[512,256]{1,0:T(8,128)(2,1)S(1)}, u32[]{:S(2)}, u32[]{:S(2)}) collective-permute-start(bf16[512,256]{1,0:T(8,128)(2,1)S(1)} %get-tuple-element.62.refs_2_), channel_id=1, source_target_pairs={{0,16},{16,0},{1,17},{17,1},{2,18},{18,2},{3,19},{19,3},{4,20},{20... | collective-permute-start | bytes 786440 | tf_op jit(solution)/shard_map/ppermute | solution.py:60
  28.5 7.3 %collective-permute-start.9 = (bf16[512,256]{1,0:T(8,128)(2,1)S(1)}, bf16[512,256]{1,0:T(8,128)(2,1)S(1)}, u32[]{:S(2)}, u32[]{:S(2)}) collective-permute-start(bf16[512,256]{1,0:T(8,128)(2,1)S(1)} %get-tuple-element.56), channel_id=1, source_target_pairs={{0,2},{1,3},{2,0},{3,1},{4,6},{5,7},{6,4},{7,5},{8,10},{9,11},{10,... | collective-permute-start | bytes 786440 | tf_op jit(solution)/shard_map/ppermute | solution.py:60
  30.0 5.9 %collective-permute-start.15 = (bf16[128,256]{1,0:T(8,128)(2,1)S(1)}, bf16[128,256]{1,0:T(8,128)(2,1)S(1)}, u32[]{:S(2)}, u32[]{:S(2)}) collective-permute-start(bf16[128,256]{1,0:T(8,128)(2,1)S(1)} %shard_map.103.refs_2_), channel_id=1, source_target_pairs={{0,8},{1,9},{2,10},{3,11},{4,12},{5,13},{6,14},{7,15},{8,0},{9,1},... | collective-permute-start | bytes 196616 | tf_op jit(solution)/shard_map/ppermute | solution.py:60
  34.6 5.0 %collective-permute-start.14 = (bf16[256,256]{1,0:T(8,128)(2,1)S(1)}, bf16[256,256]{1,0:T(8,128)(2,1)S(1)}, u32[]{:S(2)}, u32[]{:S(2)}) collective-permute-start(bf16[256,256]{1,0:T(8,128)(2,1)S(1)} %get-tuple-element.64.refs_2_), channel_id=1, source_target_pairs={{0,4},{1,5},{2,6},{3,7},{4,0},{5,1},{6,2},{7,3},{8,12},{9,13},{10,... | collective-permute-start | bytes 393224 | tf_op jit(solution)/shard_map/ppermute | solution.py:60
  35.8 6.5 %collective-permute-start.13 = (bf16[512,256]{1,0:T(8,128)(2,1)S(1)}, bf16[512,256]{1,0:T(8,128)(2,1)S(1)}, u32[]{:S(2)}, u32[]{:S(2)}) collective-permute-start(bf16[512,256]{1,0:T(8,128)(2,1)S(1)} %shard_map.105.refs_3_), channel_id=1, source_target_pairs={{0,1},{1,0},{2,3},{3,2},{4,5},{5,4},{6,7},{7,6},{8,9},{9,8},{10,11... | collective-permute-start | bytes 786440 | tf_op jit(solution)/shard_map/ppermute | solution.py:60
  36.0 9.7 %collective-permute-start.16 = (bf16[256,256]{1,0:T(8,128)(2,1)S(1)}, bf16[256,256]{1,0:T(8,128)(2,1)S(1)}, u32[]{:S(2)}, u32[]{:S(2)}) collective-permute-start(bf16[256,256]{1,0:T(8,128)(2,1)S(1)} %get-tuple-element.68.refs_2_), channel_id=1, source_target_pairs={{0,2},{1,3},{2,0},{3,1},{4,6},{5,7},{6,4},{7,5},{8,10},{9,11},{10,... | collective-permute-start | bytes 393224 | tf_op jit(solution)/shard_map/ppermute | solution.py:60
  39.7 2.7 %copy-start.2 = (bf16[512,1024]{1,0:T(8,128)(2,1)S(1)}, bf16[512,1024]{1,0:T(8,128)(2,1)}, u32[]{:S(2)}) copy-start(bf16[512,1024]{1,0:T(8,128)(2,1)} %refs_10_.1) | copy-start | bytes 3145732
  39.7 6.2 %collective-permute-start.18 = (bf16[128,256]{1,0:T(8,128)(2,1)S(1)}, bf16[128,256]{1,0:T(8,128)(2,1)S(1)}, u32[]{:S(2)}, u32[]{:S(2)}) collective-permute-start(bf16[128,256]{1,0:T(8,128)(2,1)S(1)} %get-tuple-element.69.refs_13_), channel_id=1, source_target_pairs={{0,8},{1,9},{2,10},{3,11},{4,12},{5,13},{6,14},{7,15},{8,0},{9,1},... | collective-permute-start | bytes 196616 | tf_op jit(solution)/shard_map/ppermute | solution.py:60
  45.8 2.4 %collective-permute-start.17 = (bf16[256,256]{1,0:T(8,128)(2,1)S(1)}, bf16[256,256]{1,0:T(8,128)(2,1)S(1)}, u32[]{:S(2)}, u32[]{:S(2)}) collective-permute-start(bf16[256,256]{1,0:T(8,128)(2,1)S(1)} %shard_map.109.refs_2_), channel_id=1, source_target_pairs={{0,1},{1,0},{2,3},{3,2},{4,5},{5,4},{6,7},{7,6},{8,9},{9,8},{10,11... | collective-permute-start | bytes 393224 | tf_op jit(solution)/shard_map/ppermute | solution.py:60
  45.9 4.3 %collective-permute-start.19 = (bf16[64,256]{1,0:T(8,128)(2,1)S(1)}, bf16[64,256]{1,0:T(8,128)(2,1)S(1)}, u32[]{:S(2)}, u32[]{:S(2)}) collective-permute-start(bf16[64,256]{1,0:T(8,128)(2,1)S(1)} %get-tuple-element.77.refs_7_.refs_2_), channel_id=1, source_target_pairs={{0,2},{1,3},{2,0},{3,1},{4,6},{5,7},{6,4},{7,5},{8,10},{9,11},{10,... | collective-permute-start | bytes 98312 | tf_op jit(solution)/shard_map/ppermute | solution.py:60
  50.2 1.2 %collective-permute-start.20 = (bf16[64,256]{1,0:T(8,128)(2,1)S(1)}, bf16[64,256]{1,0:T(8,128)(2,1)S(1)}, u32[]{:S(2)}, u32[]{:S(2)}) collective-permute-start(bf16[64,256]{1,0:T(8,128)(2,1)S(1)} %get-tuple-element.82.refs_2_), channel_id=1, source_target_pairs={{0,1},{1,0},{2,3},{3,2},{4,5},{5,4},{6,7},{7,6},{8,9},{9,8},{10,11... | collective-permute-start | bytes 98312 | tf_op jit(solution)/shard_map/ppermute | solution.py:60

commit v12 on v11

--- a/solution.py
+++ b/solution.py
@@ -103,8 +103,7 @@
         columns_ref[i] = w_ref[:, cut(member(2 * i), width)]
 
 
-def pack_kernel(q_ref, k_ref, v_ref, c_ref, attend_ref, own_ref, message_ref, far_ref, cot_ref):
-    cot_ref[...] = c_ref[...]
+def pack_kernel(q_ref, k_ref, v_ref, c_ref, attend_ref, own_ref, message_ref, far_ref):
     block = q_ref.shape[0]
     width = q_ref.shape[1] // SLAB
     mask = causal(block)
@@ -367,14 +366,13 @@
     )
     far_state = near(far_state, bits=2)
     w_far = [flip(columns, "dp", dp, j) for j in range(1, dp)]
-    attend, own_tokens, message, far_tokens, cot_y = call(
+    attend, own_tokens, message, far_tokens = call(
         pack_kernel,
         [((SLAB, heads, rows, rows), BF16), ((2 * rows, width), BF16),
-         (((4 + outputs // width) * rows, width), BF16), ((2 * rows, width), BF16),
-         ((rows, outputs), BF16)],
+         (((4 + outputs // width) * rows, width), BF16), ((2 * rows, width), BF16)],
         q, k, v, cot,
     )
-    cot_y = near(cot_y, bits=2)
+    cot_y = near(cot, bits=2)
     near_tokens, sent = message, (message, far_tokens)
     message = near(message, bits=1)
     (near_state,) = call(
@@ -383,19 +381,19 @@
     near_state = near(near_state, bits=1)
     (slab_kv,) = call(total_kernel, [((DH, width), BF16)], own_state, far_state, near_state)
     (far_tokens,) = call(pair_kernel, [((4 * rows, width), BF16)], message, far_tokens)
+    cot_yc = near(after(cot_y, far_tokens), bits=1)
     far_tokens = near(far_tokens, bits=2)
-    before, last_kv = doubling(slab_kv, 14 * 10**8)
-    cot_yc = near(after(cot_y, last_kv), bits=1)
+    before, _ = doubling(slab_kv, 22 * 10**8)
     weights = (columns, *w_far)
     dnormed, cots = call(
         functools.partial(dnormed_kernel, dp, (0, 1, 2)),
         [((3, rows, width), F32), ((3, rows, outputs), BF16)], cot, message, cot_y, *weights,
     )
-    (base,) = call(base_kernel, [((DH, width), F32)], *before, cost=23 * 10**8, wait=[far_tokens])
     dnormed_b, cot_b = call(
         functools.partial(dnormed_kernel, dp, (3,)),
         [((1, rows, width), F32), ((1, rows, outputs), BF16)], cot_yc, *weights,
     )
+    (base,) = call(base_kernel, [((DH, width), F32)], *before, cost=10**9)
     w_all = [x for w in w_far for x in (w, near(after(w, dnormed), bits=1))]
     normed, back, back_far, u, slab_u = call(
         middle_kernel,

time: 52.3 us -> 49.2 us (0.941)
  waiting for transfers between devices: 13.7 us -> 11.2 us
  starting transfers between devices: 26.8 us -> 26.2 us
    ppermute x21, waiting for transfers between devices: 13.7 us -> 11.2 us  [flip(): return lax.ppermute(x, axis, [(i, i ^ bits) for i in range(count)])]
    ppermute x21, starting transfers between devices: 26.8 us -> 26.2 us  [flip(): return lax.ppermute(x, axis, [(i, i ^ bits) for i in range(count)])]
  transfers between devices with their start and end apart: 21 -> 21, of which waited for: 11 -> 12; matrix products, arithmetic and copies ran while one was open for 0% -> 0% of each run, Pallas kernels for 16% -> 17%
where the time goes in v12:
time: 49.2 us; the launch traced here: 49 us
  starting transfers between devices  26.2 us (53%)
  waiting for transfers between devices  11.2 us (23%)
  Pallas kernels  10.7 us (22%)
  between operations  0.83 us (2%)
    ppermute x21, starting transfers between devices, flip(): return lax.ppermute(x, axis, [(i, i ^ bits) for i in range(count)])  26.2 us
    ppermute x21, waiting for transfers between devices, flip(): return lax.ppermute(x, axis, [(i, i ^ bits) for i in range(count)])  11.2 us
    pallas_call x22, Pallas kernels, __call__(): pl.pallas_call(inner, out_shape=[jax.ShapeDtypeStruct(s, d) for s, d in o...  10.7 us
  transfers between devices with their start and end apart: 21, of which 12 were waited for; matrix products, arithmetic and copies ran while one was open for 0% of the time, Pallas kernels for 17%

profile of v12, /device:TPU:0, one launch (start us, length us, event | category | flops | bytes accessed | tf_op | source)
XLA Modules:
  0.0 49.0 jit_solution(6314046002226523059)
XLA Ops:
  0.7 1.6 %shard_map.92 = (f32[128,256]{1,0:T(8,128)S(1)}, bf16[128,256]{1,0:T(8,128)(2,1)S(1)}, bf16[256,256]{1,0:T(8,128)(2,1)S(1)}, bf16[2,512,256]{2,1,0:T(8,128)(2,1)S(1)}) custom-call(bf16[128,1024]{1,0:T(8,128)(2,1)} %bitcast.8, bf16[128,1024]{1,0:T(8,128)(2,1)} %bitcast.12, bf16[512,1024]{1,0:T(8,128)(2,1)} %refs_10_.1), custom_call_target="tpu_custom_call" | custom-call | flops 1 | bytes 1 | tf_op jit(solution)/shard_map/pallas_call | solution.py:42
  2.2 3.0 %collective-permute-start.1 = (bf16[256,256]{1,0:T(8,128)(2,1)S(1)}, bf16[256,256]{1,0:T(8,128)(2,1)S(1)}, u32[]{:S(2)}, u32[]{:S(2)}) collective-permute-start(bf16[256,256]{1,0:T(8,128)(2,1)S(1)} %get-tuple-element.48), channel_id=1, source_target_pairs={{0,2},{1,3},{2,0},{3,1},{4,6},{5,7},{6,4},{7,5},{8,10},{9,11},{10,... | collective-permute-start | bytes 393224 | tf_op jit(solution)/shard_map/ppermute | solution.py:60
  5.4 1.9 %collective-permute-start.8 = (bf16[2,512,256]{2,1,0:T(8,128)(2,1)S(1)}, bf16[2,512,256]{2,1,0:T(8,128)(2,1)S(1)}, u32[]{:S(2)}, u32[]{:S(2)}) collective-permute-start(bf16[2,512,256]{2,1,0:T(8,128)(2,1)S(1)} %get-tuple-element.50.refs_3_.refs_1_), channel_id=1, source_target_pairs={{0,16},{16,0},{1,17},{17,1},{2,18},{18,2},{3,19},{19,3},{4,20},{20... | collective-permute-start | bytes 1572872 | tf_op jit(solution)/shard_map/ppermute | solution.py:60
  7.3 1.4 %shard_map.93 = (bf16[4,2,128,128]{3,2,1,0:T(8,128)(2,1)S(1)}, bf16[256,256]{1,0:T(8,128)(2,1)S(1)}, bf16[1024,256]{1,0:T(8,128)(2,1)S(1)}, bf16[256,256]{1,0:T(8,128)(2,1)S(1)}) custom-call(bf16[128,1024]{1,0:T(8,128)(2,1)S(1)} %bitcast.19, bf16[128,1024]{1,0:T(8,128)(2,1)S(1)} %bitcast.9, bf16[128,1024]{1,0:T(8,128)(2,1)S(1)} %bitcast.13, ...), custom_call_target="tpu_custom_call" | custom-call | flops 1 | bytes 1 | tf_op jit(solution)/shard_map/pallas_call | solution.py:42
  8.7 0.9 %collective-permute-done.1.refs_1_.refs_4_ = bf16[256,256]{1,0:T(8,128)(2,1)S(1)} collective-permute-done((bf16[256,256]{1,0:T(8,128)(2,1)S(1)}, bf16[256,256]{1,0:T(8,128)(2,1)S(1)}, u32[]{:S(2)}, u32[]{:S(2)}) %collective-permute-start.1) | collective-permute-done | bytes 131104 | tf_op jit(solution)/shard_map/ppermute | solution.py:60
  9.7 1.3 %collective-permute-done.2.refs_2_.refs_5_ = bf16[256,256]{1,0:T(8,128)(2,1)S(1)} collective-permute-done((bf16[256,256]{1,0:T(8,128)(2,1)S(1)}, bf16[256,256]{1,0:T(8,128)(2,1)S(1)}, u32[]{:S(2)}, u32[]{:S(2)}) %collective-permute-start.2) | collective-permute-done | bytes 131104 | tf_op jit(solution)/shard_map/ppermute | solution.py:60
  11.1 2.2 %collective-permute-start.4 = (bf16[128,256]{1,0:T(8,128)(2,1)S(1)}, bf16[128,256]{1,0:T(8,128)(2,1)S(1)}, u32[]{:S(2)}, u32[]{:S(2)}) collective-permute-start(bf16[128,256]{1,0:T(8,128)(2,1)S(1)} %shard_map.95.refs_2_.refs_0_), channel_id=1, source_target_pairs={{0,4},{1,5},{2,6},{3,7},{4,0},{5,1},{6,2},{7,3},{8,12},{9,13},{10,... | collective-permute-start | bytes 196616 | tf_op jit(solution)/shard_map/ppermute | solution.py:60
  13.3 1.6 %collective-permute-start.3 = (bf16[512,256]{1,0:T(8,128)(2,1)S(1)}, bf16[512,256]{1,0:T(8,128)(2,1)S(1)}, u32[]{:S(2)}, u32[]{:S(2)}) collective-permute-start(bf16[512,256]{1,0:T(8,128)(2,1)S(1)} %shard_map.96.refs_2_), channel_id=1, source_target_pairs={{0,2},{1,3},{2,0},{3,1},{4,6},{5,7},{6,4},{7,5},{8,10},{9,11},{10,... | collective-permute-start | bytes 786440 | tf_op jit(solution)/shard_map/ppermute | solution.py:60
  14.9 0.8 %collective-permute-done.4.refs_1_.refs_0_ = bf16[128,256]{1,0:T(8,128)(2,1)S(1)} collective-permute-done((bf16[128,256]{1,0:T(8,128)(2,1)S(1)}, bf16[128,256]{1,0:T(8,128)(2,1)S(1)}, u32[]{:S(2)}, u32[]{:S(2)}) %collective-permute-start.4) | collective-permute-done | bytes 65568 | tf_op jit(solution)/shard_map/ppermute | solution.py:60
  15.7 2.9 %collective-permute-start.5 = (bf16[128,256]{1,0:T(8,128)(2,1)S(1)}, bf16[128,256]{1,0:T(8,128)(2,1)S(1)}, u32[]{:S(2)}, u32[]{:S(2)}) collective-permute-start(bf16[128,256]{1,0:T(8,128)(2,1)S(1)} %shard_map.97.refs_5_), channel_id=1, source_target_pairs={{0,8},{1,9},{2,10},{3,11},{4,12},{5,13},{6,14},{7,15},{8,0},{9,1},... | collective-permute-start | bytes 196616 | tf_op jit(solution)/shard_map/ppermute | solution.py:60
  18.7 0.4 shard_map.98
  19.3 0.2 shard_map.99
  19.5 1.7 %collective-permute-done.5.refs_1_ = bf16[128,256]{1,0:T(8,128)(2,1)S(1)} collective-permute-done((bf16[128,256]{1,0:T(8,128)(2,1)S(1)}, bf16[128,256]{1,0:T(8,128)(2,1)S(1)}, u32[]{:S(2)}, u32[]{:S(2)}) %collective-permute-start.5) | collective-permute-done | bytes 65568 | tf_op jit(solution)/shard_map/ppermute | solution.py:60
  21.4 0.8 %shard_map.101 = (bf16[4,128,256]{2,1,0:T(8,128)(2,1)S(1)}, bf16[512,256]{1,0:T(8,128)(2,1)S(1)}, bf16[512,256]{1,0:T(8,128)(2,1)S(1)}, f32[4,128,256]{2,1,0:T(8,128)S(1)}, bf16[128,256]{1,0:T(8,128)(2,1)S(1)}) custom-call(bf16[256,256]{1,0:T(8,128)(2,1)S(1)} %get-tuple-element.44.refs_0_.refs_7_, ...), custom_call_target="tpu_custom_call" | custom-call | flops 10000000000 | bytes 1 | tf_op jit(solution)/shard_map/pallas_call | solution.py:42
  22.2 1.5 %collective-permute-start.11 = (bf16[128,256]{1,0:T(8,128)(2,1)S(1)}, bf16[128,256]{1,0:T(8,128)(2,1)S(1)}, u32[]{:S(2)}, u32[]{:S(2)}) collective-permute-start(bf16[128,256]{1,0:T(8,128)(2,1)S(1)} %get-tuple-element.58.refs_3_.refs_0_), channel_id=1, source_target_pairs={{0,4},{1,5},{2,6},{3,7},{4,0},{5,1},{6,2},{7,3},{8,12},{9,13},{10,... | collective-permute-start | bytes 196616 | tf_op jit(solution)/shard_map/ppermute | solution.py:60
  23.7 0.8 %shard_map.102 = (f32[512,256]{1,0:T(8,128)S(1)}, bf16[512,256]{1,0:T(8,128)(2,1)S(1)}) custom-call(bf16[3,128,1024]{2,1,0:T(8,128)(2,1)S(1)} %get-tuple-element.55.refs_0_, bf16[1,128,1024]{2,1,0:T(8,128)(2,1)S(1)} %get-tuple-element.56.refs_1_, bf16[4,128,256]{2,1,0:T(8,128)(2,1)S(1)} %get-tuple-element.57.refs_2_, ...), custom_call_target="tpu_custom_call" | custom-call | flops 1 | bytes 1 | tf_op jit(solution)/shard_map/pallas_call | solution.py:42
  24.4 1.5 %collective-permute-start.10 = (bf16[512,256]{1,0:T(8,128)(2,1)S(1)}, bf16[512,256]{1,0:T(8,128)(2,1)S(1)}, u32[]{:S(2)}, u32[]{:S(2)}) collective-permute-start(bf16[512,256]{1,0:T(8,128)(2,1)S(1)} %get-tuple-element.60.refs_2_), channel_id=1, source_target_pairs={{0,16},{16,0},{1,17},{17,1},{2,18},{18,2},{3,19},{19,3},{4,20},{20... | collective-permute-start | bytes 786440 | tf_op jit(solution)/shard_map/ppermute | solution.py:60
  26.0 1.5 %collective-permute-start.9 = (bf16[512,256]{1,0:T(8,128)(2,1)S(1)}, bf16[512,256]{1,0:T(8,128)(2,1)S(1)}, u32[]{:S(2)}, u32[]{:S(2)}) collective-permute-start(bf16[512,256]{1,0:T(8,128)(2,1)S(1)} %get-tuple-element.54), channel_id=1, source_target_pairs={{0,2},{1,3},{2,0},{3,1},{4,6},{5,7},{6,4},{7,5},{8,10},{9,11},{10,... | collective-permute-start | bytes 786440 | tf_op jit(solution)/shard_map/ppermute | solution.py:60
  27.5 3.2 %collective-permute-start.15 = (bf16[128,256]{1,0:T(8,128)(2,1)S(1)}, bf16[128,256]{1,0:T(8,128)(2,1)S(1)}, u32[]{:S(2)}, u32[]{:S(2)}) collective-permute-start(bf16[128,256]{1,0:T(8,128)(2,1)S(1)} %shard_map.103.refs_2_), channel_id=1, source_target_pairs={{0,8},{1,9},{2,10},{3,11},{4,12},{5,13},{6,14},{7,15},{8,0},{9,1},... | collective-permute-start | bytes 196616 | tf_op jit(solution)/shard_map/ppermute | solution.py:60
  30.8 0.6 %collective-permute-done.10.refs_1_ = bf16[512,256]{1,0:T(8,128)(2,1)S(1)} collective-permute-done((bf16[512,256]{1,0:T(8,128)(2,1)S(1)}, bf16[512,256]{1,0:T(8,128)(2,1)S(1)}, u32[]{:S(2)}, u32[]{:S(2)}) %collective-permute-start.10) | collective-permute-done | bytes 262176 | tf_op jit(solution)/shard_map/ppermute | solution.py:60
  31.5 0.7 %collective-permute-start.14 = (bf16[256,256]{1,0:T(8,128)(2,1)S(1)}, bf16[256,256]{1,0:T(8,128)(2,1)S(1)}, u32[]{:S(2)}, u32[]{:S(2)}) collective-permute-start(bf16[256,256]{1,0:T(8,128)(2,1)S(1)} %get-tuple-element.62.refs_2_), channel_id=1, source_target_pairs={{0,4},{1,5},{2,6},{3,7},{4,0},{5,1},{6,2},{7,3},{8,12},{9,13},{10,... | collective-permute-start | bytes 393224 | tf_op jit(solution)/shard_map/ppermute | solution.py:60
  32.2 0.4 collective-permute-done.9.refs_1_
  32.7 1.0 %collective-permute-done.15.refs_1_ = bf16[128,256]{1,0:T(8,128)(2,1)S(1)} collective-permute-done((bf16[128,256]{1,0:T(8,128)(2,1)S(1)}, bf16[128,256]{1,0:T(8,128)(2,1)S(1)}, u32[]{:S(2)}, u32[]{:S(2)}) %collective-permute-start.15) | collective-permute-done | bytes 65568 | tf_op jit(solution)/shard_map/ppermute | solution.py:60
  33.8 0.6 %collective-permute-start.16 = (bf16[256,256]{1,0:T(8,128)(2,1)S(1)}, bf16[256,256]{1,0:T(8,128)(2,1)S(1)}, u32[]{:S(2)}, u32[]{:S(2)}) collective-permute-start(bf16[256,256]{1,0:T(8,128)(2,1)S(1)} %get-tuple-element.66.refs_2_), channel_id=1, source_target_pairs={{0,2},{1,3},{2,0},{3,1},{4,6},{5,7},{6,4},{7,5},{8,10},{9,11},{10,... | collective-permute-start | bytes 393224 | tf_op jit(solution)/shard_map/ppermute | solution.py:60
  34.4 2.1 %collective-permute-done.14.refs_1_ = bf16[256,256]{1,0:T(8,128)(2,1)S(1)} collective-permute-done((bf16[256,256]{1,0:T(8,128)(2,1)S(1)}, bf16[256,256]{1,0:T(8,128)(2,1)S(1)}, u32[]{:S(2)}, u32[]{:S(2)}) %collective-permute-start.14) | collective-permute-done | bytes 131104 | tf_op jit(solution)/shard_map/ppermute | solution.py:60
  36.5 2.7 %collective-permute-start.18 = (bf16[128,256]{1,0:T(8,128)(2,1)S(1)}, bf16[128,256]{1,0:T(8,128)(2,1)S(1)}, u32[]{:S(2)}, u32[]{:S(2)}) collective-permute-start(bf16[128,256]{1,0:T(8,128)(2,1)S(1)} %get-tuple-element.67.refs_13_), channel_id=1, source_target_pairs={{0,8},{1,9},{2,10},{3,11},{4,12},{5,13},{6,14},{7,15},{8,0},{9,1},... | collective-permute-start | bytes 196616 | tf_op jit(solution)/shard_map/ppermute | solution.py:60
  39.2 3.4 %shard_map.108 = (bf16[128,1024]{1,0:T(8,128)(2,1)}, bf16[128,1024]{1,0:T(8,128)(2,1)}, f32[4,128,256]{2,1,0:T(8,128)S(1)}, f32[4,128,256]{2,1,0:T(8,128)S(1)}, bf16[128,1024]{1,0:T(8,128)(2,1)S(1)}) custom-call(bf16[512,256]{1,0:T(8,128)(2,1)S(1)} %get-tuple-element.53.refs_0_, bf16[512,256]{1,0:T(8,128)(2,1)S(1)} %collective-permute-done.9.refs_1_, ...), custom_call_target="tpu_custom_call" | custom-call | flops 1 | bytes 1 | tf_op jit(solution)/shard_map/pallas_call | solution.py:42
  42.8 2.3 %collective-permute-start.19 = (bf16[64,256]{1,0:T(8,128)(2,1)S(1)}, bf16[64,256]{1,0:T(8,128)(2,1)S(1)}, u32[]{:S(2)}, u32[]{:S(2)}) collective-permute-start(bf16[64,256]{1,0:T(8,128)(2,1)S(1)} %get-tuple-element.75.refs_7_.refs_2_), channel_id=1, source_target_pairs={{0,2},{1,3},{2,0},{3,1},{4,6},{5,7},{6,4},{7,5},{8,10},{9,11},{10,... | collective-permute-start | bytes 98312 | tf_op jit(solution)/shard_map/ppermute | solution.py:60
  45.1 1.1 %shard_map.111 = (bf16[128,1024]{1,0:T(8,128)(2,1)}, bf16[128,1024]{1,0:T(8,128)(2,1)}) custom-call(bf16[256,256]{1,0:T(8,128)(2,1)S(1)} %get-tuple-element.70.refs_0_, bf16[256,256]{1,0:T(8,128)(2,1)S(1)} %collective-permute-done.16.refs_1_, bf16[256,256]{1,0:T(8,128)(2,1)S(1)} %collective-permute-done.17.refs_2_, bf16[128,1024]{1,0:T(8,128)(2,1)S(1)} %bitcast.11, ...), custom_call_target="tpu_custom_call" | custom-call | flops 1 | bytes 1 | tf_op jit(solution)/shard_map/pallas_call | solution.py:42
  46.2 0.9 %collective-permute-done.19.refs_1_ = bf16[64,256]{1,0:T(8,128)(2,1)S(1)} collective-permute-done((bf16[64,256]{1,0:T(8,128)(2,1)S(1)}, bf16[64,256]{1,0:T(8,128)(2,1)S(1)}, u32[]{:S(2)}, u32[]{:S(2)}) %collective-permute-start.19) | collective-permute-done | bytes 32800 | tf_op jit(solution)/shard_map/ppermute | solution.py:60
  47.1 1.2 %collective-permute-done.20.refs_1_ = bf16[64,256]{1,0:T(8,128)(2,1)S(1)} collective-permute-done((bf16[64,256]{1,0:T(8,128)(2,1)S(1)}, bf16[64,256]{1,0:T(8,128)(2,1)S(1)}, u32[]{:S(2)}, u32[]{:S(2)}) %collective-permute-start.20) | collective-permute-done | bytes 32800 | tf_op jit(solution)/shard_map/ppermute | solution.py:60
  48.3 0.7 %shard_map.113 = f32[32,1024]{1,0:T(8,128)} custom-call(bf16[64,256]{1,0:T(8,128)(2,1)S(1)} %get-tuple-element.79.refs_0_, bf16[64,256]{1,0:T(8,128)(2,1)S(1)} %collective-permute-done.20.refs_1_, bf16[64,256]{1,0:T(8,128)(2,1)S(1)} %get-tuple-element.80.refs_2_), custom_call_target="tpu_custom_call" | custom-call | flops 1 | bytes 1 | tf_op jit(solution)/shard_map/pallas_call | solution.py:42
  (42 shorter events, 1.2 us)
Async XLA Ops:
  0.6 4.6 %copy-start.3 = (bf16[1,128,1024]{2,1,0:T(8,128)(2,1)S(1)}, bf16[1,128,1024]{2,1,0:T(8,128)(2,1)}, u32[]{:S(2)}) copy-start(bf16[1,128,1024]{2,1,0:T(8,128)(2,1)} %param.8) | copy-start | bytes 786436
  0.6 6.6 %copy-start = (bf16[1,128,1024]{2,1,0:T(8,128)(2,1)S(1)}, bf16[1,128,1024]{2,1,0:T(8,128)(2,1)}, u32[]{:S(2)}) copy-start(bf16[1,128,1024]{2,1,0:T(8,128)(2,1)} %param.6) | copy-start | bytes 786436
  0.7 6.6 %copy-start.1 = (bf16[1,128,1024]{2,1,0:T(8,128)(2,1)S(1)}, bf16[1,128,1024]{2,1,0:T(8,128)(2,1)}, u32[]{:S(2)}) copy-start(bf16[1,128,1024]{2,1,0:T(8,128)(2,1)} %param.7) | copy-start | bytes 786436
  0.7 6.6 %copy-start.4 = (bf16[1,128,1024]{2,1,0:T(8,128)(2,1)S(1)}, bf16[1,128,1024]{2,1,0:T(8,128)(2,1)}, u32[]{:S(2)}) copy-start(bf16[1,128,1024]{2,1,0:T(8,128)(2,1)} %param.5) | copy-start | bytes 786436
  2.2 7.4 %collective-permute-start.1 = (bf16[256,256]{1,0:T(8,128)(2,1)S(1)}, bf16[256,256]{1,0:T(8,128)(2,1)S(1)}, u32[]{:S(2)}, u32[]{:S(2)}) collective-permute-start(bf16[256,256]{1,0:T(8,128)(2,1)S(1)} %get-tuple-element.48), channel_id=1, source_target_pairs={{0,2},{1,3},{2,0},{3,1},{4,6},{5,7},{6,4},{7,5},{8,10},{9,11},{10,... | collective-permute-start | bytes 393224 | tf_op jit(solution)/shard_map/ppermute | solution.py:60
  5.3 9.6 %collective-permute-start.6 = (bf16[128,1024]{1,0:T(8,128)(2,1)S(1)}, bf16[128,1024]{1,0:T(8,128)(2,1)S(1)}, u32[]{:S(2)}, u32[]{:S(2)}) collective-permute-start(bf16[128,1024]{1,0:T(8,128)(2,1)S(1)} %bitcast.16), channel_id=1, source_target_pairs={{0,2},{1,3},{2,0},{3,1},{4,6},{5,7},{6,4},{7,5},{8,10},{9,11},{10,... | collective-permute-start | bytes 786440 | tf_op jit(solution)/shard_map/ppermute | solution.py:60
  5.4 13.4 %collective-permute-start.8 = (bf16[2,512,256]{2,1,0:T(8,128)(2,1)S(1)}, bf16[2,512,256]{2,1,0:T(8,128)(2,1)S(1)}, u32[]{:S(2)}, u32[]{:S(2)}) collective-permute-start(bf16[2,512,256]{2,1,0:T(8,128)(2,1)S(1)} %get-tuple-element.50.refs_3_.refs_1_), channel_id=1, source_target_pairs={{0,16},{16,0},{1,17},{17,1},{2,18},{18,2},{3,19},{19,3},{4,20},{20... | collective-permute-start | bytes 1572872 | tf_op jit(solution)/shard_map/ppermute | solution.py:60
  8.6 4.6 %collective-permute-start = (bf16[1024,256]{1,0:T(8,128)(2,1)S(1)}, bf16[1024,256]{1,0:T(8,128)(2,1)S(1)}, u32[]{:S(2)}, u32[]{:S(2)}) collective-permute-start(bf16[1024,256]{1,0:T(8,128)(2,1)S(1)} %get-tuple-element.45.refs_8_), channel_id=1, source_target_pairs={{0,1},{1,0},{2,3},{3,2},{4,5},{5,4},{6,7},{7,6},{8,9},{9,8},{10,11... | collective-permute-start | bytes 1572872 | tf_op jit(solution)/shard_map/ppermute | solution.py:60
  9.6 1.4 %collective-permute-start.2 = (bf16[256,256]{1,0:T(8,128)(2,1)S(1)}, bf16[256,256]{1,0:T(8,128)(2,1)S(1)}, u32[]{:S(2)}, u32[]{:S(2)}) collective-permute-start(bf16[256,256]{1,0:T(8,128)(2,1)S(1)} %shard_map.94.refs_3_), channel_id=1, source_target_pairs={{0,1},{1,0},{2,3},{3,2},{4,5},{5,4},{6,7},{7,6},{8,9},{9,8},{10,11... | collective-permute-start | bytes 393224 | tf_op jit(solution)/shard_map/ppermute | solution.py:60
  11.1 4.6 %collective-permute-start.4 = (bf16[128,256]{1,0:T(8,128)(2,1)S(1)}, bf16[128,256]{1,0:T(8,128)(2,1)S(1)}, u32[]{:S(2)}, u32[]{:S(2)}) collective-permute-start(bf16[128,256]{1,0:T(8,128)(2,1)S(1)} %shard_map.95.refs_2_.refs_0_), channel_id=1, source_target_pairs={{0,4},{1,5},{2,6},{3,7},{4,0},{5,1},{6,2},{7,3},{8,12},{9,13},{10,... | collective-permute-start | bytes 196616 | tf_op jit(solution)/shard_map/ppermute | solution.py:60
  13.3 8.1 %collective-permute-start.3 = (bf16[512,256]{1,0:T(8,128)(2,1)S(1)}, bf16[512,256]{1,0:T(8,128)(2,1)S(1)}, u32[]{:S(2)}, u32[]{:S(2)}) collective-permute-start(bf16[512,256]{1,0:T(8,128)(2,1)S(1)} %shard_map.96.refs_2_), channel_id=1, source_target_pairs={{0,2},{1,3},{2,0},{3,1},{4,6},{5,7},{6,4},{7,5},{8,10},{9,11},{10,... | collective-permute-start | bytes 786440 | tf_op jit(solution)/shard_map/ppermute | solution.py:60
  14.9 4.4 %collective-permute-start.7 = (bf16[128,1024]{1,0:T(8,128)(2,1)S(1)}, bf16[128,1024]{1,0:T(8,128)(2,1)S(1)}, u32[]{:S(2)}, u32[]{:S(2)}) collective-permute-start(bf16[128,1024]{1,0:T(8,128)(2,1)S(1)} %collective-permute-done.6.refs_2_), channel_id=1, source_target_pairs={{0,1},{1,0},{2,3},{3,2},{4,5},{5,4},{6,7},{7,6},{8,9},{9,8},{10,11... | collective-permute-start | bytes 786440 | tf_op jit(solution)/shard_map/ppermute | solution.py:60
  15.7 5.6 %collective-permute-start.5 = (bf16[128,256]{1,0:T(8,128)(2,1)S(1)}, bf16[128,256]{1,0:T(8,128)(2,1)S(1)}, u32[]{:S(2)}, u32[]{:S(2)}) collective-permute-start(bf16[128,256]{1,0:T(8,128)(2,1)S(1)} %shard_map.97.refs_5_), channel_id=1, source_target_pairs={{0,8},{1,9},{2,10},{3,11},{4,12},{5,13},{6,14},{7,15},{8,0},{9,1},... | collective-permute-start | bytes 196616 | tf_op jit(solution)/shard_map/ppermute | solution.py:60
  19.2 12.3 %collective-permute-start.12 = (bf16[2,512,256]{2,1,0:T(8,128)(2,1)S(1)}, bf16[2,512,256]{2,1,0:T(8,128)(2,1)S(1)}, u32[]{:S(2)}, u32[]{:S(2)}) collective-permute-start(bf16[2,512,256]{2,1,0:T(8,128)(2,1)S(1)} %collective-permute-done.8.refs_4_.refs_2_.refs_11_), channel_id=1, source_target_pairs={{0,1},{1,0},{2,3},{3,2},{4,5},{5,4},{6,7},{7,6},{8,9},{9,8},{10,11... | collective-permute-start | bytes 1572872 | tf_op jit(solution)/shard_map/ppermute | solution.py:60
  22.2 5.3 %collective-permute-start.11 = (bf16[128,256]{1,0:T(8,128)(2,1)S(1)}, bf16[128,256]{1,0:T(8,128)(2,1)S(1)}, u32[]{:S(2)}, u32[]{:S(2)}) collective-permute-start(bf16[128,256]{1,0:T(8,128)(2,1)S(1)} %get-tuple-element.58.refs_3_.refs_0_), channel_id=1, source_target_pairs={{0,4},{1,5},{2,6},{3,7},{4,0},{5,1},{6,2},{7,3},{8,12},{9,13},{10,... | collective-permute-start | bytes 196616 | tf_op jit(solution)/shard_map/ppermute | solution.py:60
  24.4 7.0 %collective-permute-start.10 = (bf16[512,256]{1,0:T(8,128)(2,1)S(1)}, bf16[512,256]{1,0:T(8,128)(2,1)S(1)}, u32[]{:S(2)}, u32[]{:S(2)}) collective-permute-start(bf16[512,256]{1,0:T(8,128)(2,1)S(1)} %get-tuple-element.60.refs_2_), channel_id=1, source_target_pairs={{0,16},{16,0},{1,17},{17,1},{2,18},{18,2},{3,19},{19,3},{4,20},{20... | collective-permute-start | bytes 786440 | tf_op jit(solution)/shard_map/ppermute | solution.py:60
  26.0 6.6 %collective-permute-start.9 = (bf16[512,256]{1,0:T(8,128)(2,1)S(1)}, bf16[512,256]{1,0:T(8,128)(2,1)S(1)}, u32[]{:S(2)}, u32[]{:S(2)}) collective-permute-start(bf16[512,256]{1,0:T(8,128)(2,1)S(1)} %get-tuple-element.54), channel_id=1, source_target_pairs={{0,2},{1,3},{2,0},{3,1},{4,6},{5,7},{6,4},{7,5},{8,10},{9,11},{10,... | collective-permute-start | bytes 786440 | tf_op jit(solution)/shard_map/ppermute | solution.py:60
  27.5 6.2 %collective-permute-start.15 = (bf16[128,256]{1,0:T(8,128)(2,1)S(1)}, bf16[128,256]{1,0:T(8,128)(2,1)S(1)}, u32[]{:S(2)}, u32[]{:S(2)}) collective-permute-start(bf16[128,256]{1,0:T(8,128)(2,1)S(1)} %shard_map.103.refs_2_), channel_id=1, source_target_pairs={{0,8},{1,9},{2,10},{3,11},{4,12},{5,13},{6,14},{7,15},{8,0},{9,1},... | collective-permute-start | bytes 196616 | tf_op jit(solution)/shard_map/ppermute | solution.py:60
  31.5 5.0 %collective-permute-start.14 = (bf16[256,256]{1,0:T(8,128)(2,1)S(1)}, bf16[256,256]{1,0:T(8,128)(2,1)S(1)}, u32[]{:S(2)}, u32[]{:S(2)}) collective-permute-start(bf16[256,256]{1,0:T(8,128)(2,1)S(1)} %get-tuple-element.62.refs_2_), channel_id=1, source_target_pairs={{0,4},{1,5},{2,6},{3,7},{4,0},{5,1},{6,2},{7,3},{8,12},{9,13},{10,... | collective-permute-start | bytes 393224 | tf_op jit(solution)/shard_map/ppermute | solution.py:60
  32.6 6.6 %collective-permute-start.13 = (bf16[512,256]{1,0:T(8,128)(2,1)S(1)}, bf16[512,256]{1,0:T(8,128)(2,1)S(1)}, u32[]{:S(2)}, u32[]{:S(2)}) collective-permute-start(bf16[512,256]{1,0:T(8,128)(2,1)S(1)} %shard_map.105.refs_3_), channel_id=1, source_target_pairs={{0,1},{1,0},{2,3},{3,2},{4,5},{5,4},{6,7},{7,6},{8,9},{9,8},{10,11... | collective-permute-start | bytes 786440 | tf_op jit(solution)/shard_map/ppermute | solution.py:60
  33.8 8.8 %collective-permute-start.16 = (bf16[256,256]{1,0:T(8,128)(2,1)S(1)}, bf16[256,256]{1,0:T(8,128)(2,1)S(1)}, u32[]{:S(2)}, u32[]{:S(2)}) collective-permute-start(bf16[256,256]{1,0:T(8,128)(2,1)S(1)} %get-tuple-element.66.refs_2_), channel_id=1, source_target_pairs={{0,2},{1,3},{2,0},{3,1},{4,6},{5,7},{6,4},{7,5},{8,10},{9,11},{10,... | collective-permute-start | bytes 393224 | tf_op jit(solution)/shard_map/ppermute | solution.py:60
  36.5 2.7 %copy-start.2 = (bf16[512,1024]{1,0:T(8,128)(2,1)S(1)}, bf16[512,1024]{1,0:T(8,128)(2,1)}, u32[]{:S(2)}) copy-start(bf16[512,1024]{1,0:T(8,128)(2,1)} %refs_10_.1) | copy-start | bytes 3145732
  36.5 6.2 %collective-permute-start.18 = (bf16[128,256]{1,0:T(8,128)(2,1)S(1)}, bf16[128,256]{1,0:T(8,128)(2,1)S(1)}, u32[]{:S(2)}, u32[]{:S(2)}) collective-permute-start(bf16[128,256]{1,0:T(8,128)(2,1)S(1)} %get-tuple-element.67.refs_13_), channel_id=1, source_target_pairs={{0,8},{1,9},{2,10},{3,11},{4,12},{5,13},{6,14},{7,15},{8,0},{9,1},... | collective-permute-start | bytes 196616 | tf_op jit(solution)/shard_map/ppermute | solution.py:60
  42.7 2.4 %collective-permute-start.17 = (bf16[256,256]{1,0:T(8,128)(2,1)S(1)}, bf16[256,256]{1,0:T(8,128)(2,1)S(1)}, u32[]{:S(2)}, u32[]{:S(2)}) collective-permute-start(bf16[256,256]{1,0:T(8,128)(2,1)S(1)} %shard_map.109.refs_2_), channel_id=1, source_target_pairs={{0,1},{1,0},{2,3},{3,2},{4,5},{5,4},{6,7},{7,6},{8,9},{9,8},{10,11... | collective-permute-start | bytes 393224 | tf_op jit(solution)/shard_map/ppermute | solution.py:60
  42.8 4.3 %collective-permute-start.19 = (bf16[64,256]{1,0:T(8,128)(2,1)S(1)}, bf16[64,256]{1,0:T(8,128)(2,1)S(1)}, u32[]{:S(2)}, u32[]{:S(2)}) collective-permute-start(bf16[64,256]{1,0:T(8,128)(2,1)S(1)} %get-tuple-element.75.refs_7_.refs_2_), channel_id=1, source_target_pairs={{0,2},{1,3},{2,0},{3,1},{4,6},{5,7},{6,4},{7,5},{8,10},{9,11},{10,... | collective-permute-start | bytes 98312 | tf_op jit(solution)/shard_map/ppermute | solution.py:60
  47.1 1.2 %collective-permute-start.20 = (bf16[64,256]{1,0:T(8,128)(2,1)S(1)}, bf16[64,256]{1,0:T(8,128)(2,1)S(1)}, u32[]{:S(2)}, u32[]{:S(2)}) collective-permute-start(bf16[64,256]{1,0:T(8,128)(2,1)S(1)} %get-tuple-element.80.refs_2_), channel_id=1, source_target_pairs={{0,1},{1,0},{2,3},{3,2},{4,5},{5,4},{6,7},{7,6},{8,9},{9,8},{10,11... | collective-permute-start | bytes 98312 | tf_op jit(solution)/shard_map/ppermute | solution.py:60

commit v13 on v12

--- a/solution.py
+++ b/solution.py
@@ -231,12 +231,10 @@
     return near_ref.at[first], core_ref.at[first], far_ref.at[first], core_ref.at[second]
 
 
-def late_kernel(groups, *refs):
+def late_kernel(*refs):
     backs, (q_ref, k_ref, v_ref, attend_ref, own_ref, message_ref, far_ref) = arrived(*refs[:3]), refs[3:10]
-    weight_ref, *far, out_ref, gq_ref, gk_ref, gv_ref, normed_ref = refs[10:]
+    gq_ref, gk_ref, gv_ref, normed_ref = refs[10:]
     block, width = q_ref.shape[0], refs[0].shape[1]
-    rows = weight_ref.shape[0]
-    me = lax.axis_index("dp")
     mask = causal(block)
     withins = (own_ref.at[part(1, block)], message_ref.at[part(1, block)],
                far_ref.at[part(1, block)], message_ref.at[part(3, block)])
@@ -257,9 +255,16 @@
         gq_ref[:, at] = jnp.concatenate(gqs, axis=1).astype(BF16)
         gk_ref[r] = jnp.concatenate(gks, axis=1)
         gv_ref[r] = jnp.concatenate(gvs, axis=1)
+
+
+def output_kernel(normed_ref, weight_ref, *refs):
+    *far, out_ref = refs
+    width = normed_ref.shape[1] // SLAB
+    rows = weight_ref.shape[0]
+    me = lax.axis_index("dp")
     out_ref[:, cut(me, rows)] = dot(normed_ref[...], weight_ref[...], 1, 1).astype(BF16)
-    for j in range(1, groups):
-        total = jnp.zeros((block, rows), F32)
+    for j in range(1, len(far) // 2 + 1):
+        total = jnp.zeros((normed_ref.shape[0], rows), F32)
         for r in range(SLAB):
             normed = normed_ref[:, cut(member(r), width)]
             total = total + dot(normed, far[2 * (j - 1) + r % 2][r // 2], 1, 1)
@@ -429,11 +434,10 @@
             split_again_kernel, [((piece, width), F32), ((piece, width), BF16)], keep, got, cost=2 * 10**9
         )
         got = near(send, bits=2 * SLAB)
-    output, gq, gk_part, gv_part, own_normed = call(
-        functools.partial(late_kernel, dp),
-        [((rows, outputs), BF16), ((rows, features), BF16), ((SLAB, rows, width), F32),
-         ((SLAB, rows, width), F32), ((rows, features), BF16)],
-        back, back_far, back_core, q, k, v, attend, own_tokens, *sent, out_weight, *w_all,
+    gq, gk_part, gv_part, own_normed = call(
+        late_kernel,
+        [((rows, features), BF16), ((SLAB, rows, width), F32), ((SLAB, rows, width), F32), ((rows, features), BF16)],
+        back, back_far, back_core, q, k, v, attend, own_tokens, *sent,
     )
     (send,) = call(relay_kernel, [((2 * DH, width), BF16)], later, later_far)
     later_core = near(send, bits=1)
@@ -447,8 +451,14 @@
         last_kernel, [((rows, features), BF16)] * 2,
         later, later_far, later_core, k, v, gk_part, gv_part, end=True,
     )
-    if tuned:
-        keep, share = call(pass_kernel, [((piece // 2, width), BF16)] * 2, keep, got, wait=[pltpu.with_memory_space_constraint(gk, pltpu.HBM)])
+    (output,) = call(
+        output_kernel, [((rows, outputs), BF16)], own_normed, out_weight, *w_all, end=True,
+    )
+    if tuned:
+        keep, share = call(
+            pass_kernel, [((piece // 2, width), BF16)] * 2, keep, got,
+            wait=[pltpu.with_memory_space_constraint(x, pltpu.HBM) for x in (gk, output)],
+        )
         got = near(share, bits=1)
     if tuned:
         (grad_weight,) = call(

time: 49.2 us -> 49.1 us (level)
  Pallas kernels: 10.7 us -> 11.5 us
  waiting for transfers between devices: 11.2 us -> 10.6 us
    pallas_call x22 -> x23, Pallas kernels: 10.7 us -> 11.5 us  [__call__(): pl.pallas_call(inner, out_shape=[jax.ShapeDtypeStruct(s, d) for s, d in o...]
    ppermute x21, waiting for transfers between devices: 11.2 us -> 10.6 us  [flip(): return lax.ppermute(x, axis, [(i, i ^ bits) for i in range(count)])]
  transfers between devices with their start and end apart: 21 -> 21, of which waited for: 12 -> 12; matrix products, arithmetic and copies ran while one was open for 0% -> 0% of each run, Pallas kernels for 17% -> 19%
where the time goes in v13:
time: 49.1 us; the launch traced here: 48.9 us
  starting transfers between devices  26 us (53%)
  Pallas kernels  11.5 us (23%)
  waiting for transfers between devices  10.6 us (22%)
  between operations  0.82 us (2%)
    ppermute x21, starting transfers between devices, flip(): return lax.ppermute(x, axis, [(i, i ^ bits) for i in range(count)])  26 us
    pallas_call x23, Pallas kernels, __call__(): pl.pallas_call(inner, out_shape=[jax.ShapeDtypeStruct(s, d) for s, d in o...  11.5 us
    ppermute x21, waiting for transfers between devices, flip(): return lax.ppermute(x, axis, [(i, i ^ bits) for i in range(count)])  10.6 us
  transfers between devices with their start and end apart: 21, of which 12 were waited for; matrix products, arithmetic and copies ran while one was open for 0% of the time, Pallas kernels for 19%

profile of v13, /device:TPU:0, one launch (start us, length us, event | category | flops | bytes accessed | tf_op | source)
XLA Modules:
  0.0 48.9 jit_solution(6890072019524556152)
XLA Ops:
  0.7 1.6 %shard_map.92 = (f32[128,256]{1,0:T(8,128)S(1)}, bf16[128,256]{1,0:T(8,128)(2,1)S(1)}, bf16[256,256]{1,0:T(8,128)(2,1)S(1)}, bf16[2,512,256]{2,1,0:T(8,128)(2,1)S(1)}) custom-call(bf16[128,1024]{1,0:T(8,128)(2,1)} %bitcast.8, bf16[128,1024]{1,0:T(8,128)(2,1)} %bitcast.12, bf16[512,1024]{1,0:T(8,128)(2,1)} %refs_1_.1), custom_call_target="tpu_custom_call" | custom-call | flops 1 | bytes 1 | tf_op jit(solution)/shard_map/pallas_call | solution.py:42
  2.2 3.0 %collective-permute-start.1 = (bf16[256,256]{1,0:T(8,128)(2,1)S(1)}, bf16[256,256]{1,0:T(8,128)(2,1)S(1)}, u32[]{:S(2)}, u32[]{:S(2)}) collective-permute-start(bf16[256,256]{1,0:T(8,128)(2,1)S(1)} %get-tuple-element.47), channel_id=1, source_target_pairs={{0,2},{1,3},{2,0},{3,1},{4,6},{5,7},{6,4},{7,5},{8,10},{9,11},{10,... | collective-permute-start | bytes 393224 | tf_op jit(solution)/shard_map/ppermute | solution.py:60
  5.4 1.9 %collective-permute-start.8 = (bf16[2,512,256]{2,1,0:T(8,128)(2,1)S(1)}, bf16[2,512,256]{2,1,0:T(8,128)(2,1)S(1)}, u32[]{:S(2)}, u32[]{:S(2)}) collective-permute-start(bf16[2,512,256]{2,1,0:T(8,128)(2,1)S(1)} %get-tuple-element.49.refs_3_.refs_1_), channel_id=1, source_target_pairs={{0,16},{16,0},{1,17},{17,1},{2,18},{18,2},{3,19},{19,3},{4,20},{20... | collective-permute-start | bytes 1572872 | tf_op jit(solution)/shard_map/ppermute | solution.py:60
  7.3 1.4 %shard_map.93 = (bf16[4,2,128,128]{3,2,1,0:T(8,128)(2,1)S(1)}, bf16[256,256]{1,0:T(8,128)(2,1)S(1)}, bf16[1024,256]{1,0:T(8,128)(2,1)S(1)}, bf16[256,256]{1,0:T(8,128)(2,1)S(1)}) custom-call(bf16[128,1024]{1,0:T(8,128)(2,1)S(1)} %bitcast.19, bf16[128,1024]{1,0:T(8,128)(2,1)S(1)} %bitcast.9, bf16[128,1024]{1,0:T(8,128)(2,1)S(1)} %bitcast.13, ...), custom_call_target="tpu_custom_call" | custom-call | flops 1 | bytes 1 | tf_op jit(solution)/shard_map/pallas_call | solution.py:42
  8.7 0.9 %collective-permute-done.1.refs_1_.refs_4_ = bf16[256,256]{1,0:T(8,128)(2,1)S(1)} collective-permute-done((bf16[256,256]{1,0:T(8,128)(2,1)S(1)}, bf16[256,256]{1,0:T(8,128)(2,1)S(1)}, u32[]{:S(2)}, u32[]{:S(2)}) %collective-permute-start.1) | collective-permute-done | bytes 131104 | tf_op jit(solution)/shard_map/ppermute | solution.py:60
  9.7 1.3 %collective-permute-done.2.refs_2_.refs_5_ = bf16[256,256]{1,0:T(8,128)(2,1)S(1)} collective-permute-done((bf16[256,256]{1,0:T(8,128)(2,1)S(1)}, bf16[256,256]{1,0:T(8,128)(2,1)S(1)}, u32[]{:S(2)}, u32[]{:S(2)}) %collective-permute-start.2) | collective-permute-done | bytes 131104 | tf_op jit(solution)/shard_map/ppermute | solution.py:60
  11.1 2.2 %collective-permute-start.4 = (bf16[128,256]{1,0:T(8,128)(2,1)S(1)}, bf16[128,256]{1,0:T(8,128)(2,1)S(1)}, u32[]{:S(2)}, u32[]{:S(2)}) collective-permute-start(bf16[128,256]{1,0:T(8,128)(2,1)S(1)} %shard_map.95.refs_2_.refs_0_), channel_id=1, source_target_pairs={{0,4},{1,5},{2,6},{3,7},{4,0},{5,1},{6,2},{7,3},{8,12},{9,13},{10,... | collective-permute-start | bytes 196616 | tf_op jit(solution)/shard_map/ppermute | solution.py:60
  13.3 1.6 %collective-permute-start.3 = (bf16[512,256]{1,0:T(8,128)(2,1)S(1)}, bf16[512,256]{1,0:T(8,128)(2,1)S(1)}, u32[]{:S(2)}, u32[]{:S(2)}) collective-permute-start(bf16[512,256]{1,0:T(8,128)(2,1)S(1)} %shard_map.96.refs_2_), channel_id=1, source_target_pairs={{0,2},{1,3},{2,0},{3,1},{4,6},{5,7},{6,4},{7,5},{8,10},{9,11},{10,... | collective-permute-start | bytes 786440 | tf_op jit(solution)/shard_map/ppermute | solution.py:60
  14.9 0.8 %collective-permute-done.4.refs_1_.refs_0_ = bf16[128,256]{1,0:T(8,128)(2,1)S(1)} collective-permute-done((bf16[128,256]{1,0:T(8,128)(2,1)S(1)}, bf16[128,256]{1,0:T(8,128)(2,1)S(1)}, u32[]{:S(2)}, u32[]{:S(2)}) %collective-permute-start.4) | collective-permute-done | bytes 65568 | tf_op jit(solution)/shard_map/ppermute | solution.py:60
  15.7 2.9 %collective-permute-start.5 = (bf16[128,256]{1,0:T(8,128)(2,1)S(1)}, bf16[128,256]{1,0:T(8,128)(2,1)S(1)}, u32[]{:S(2)}, u32[]{:S(2)}) collective-permute-start(bf16[128,256]{1,0:T(8,128)(2,1)S(1)} %shard_map.97.refs_5_), channel_id=1, source_target_pairs={{0,8},{1,9},{2,10},{3,11},{4,12},{5,13},{6,14},{7,15},{8,0},{9,1},... | collective-permute-start | bytes 196616 | tf_op jit(solution)/shard_map/ppermute | solution.py:60
  18.7 0.4 shard_map.98
  19.5 1.7 %collective-permute-done.5.refs_1_ = bf16[128,256]{1,0:T(8,128)(2,1)S(1)} collective-permute-done((bf16[128,256]{1,0:T(8,128)(2,1)S(1)}, bf16[128,256]{1,0:T(8,128)(2,1)S(1)}, u32[]{:S(2)}, u32[]{:S(2)}) %collective-permute-start.5) | collective-permute-done | bytes 65568 | tf_op jit(solution)/shard_map/ppermute | solution.py:60
  21.4 0.8 %shard_map.101 = (bf16[4,128,256]{2,1,0:T(8,128)(2,1)S(1)}, bf16[512,256]{1,0:T(8,128)(2,1)S(1)}, bf16[512,256]{1,0:T(8,128)(2,1)S(1)}, f32[4,128,256]{2,1,0:T(8,128)S(1)}, bf16[128,256]{1,0:T(8,128)(2,1)S(1)}) custom-call(bf16[256,256]{1,0:T(8,128)(2,1)S(1)} %get-tuple-element.43.refs_0_.refs_7_, ...), custom_call_target="tpu_custom_call" | custom-call | flops 10000000000 | bytes 1 | tf_op jit(solution)/shard_map/pallas_call | solution.py:42
  22.2 1.5 %collective-permute-start.11 = (bf16[128,256]{1,0:T(8,128)(2,1)S(1)}, bf16[128,256]{1,0:T(8,128)(2,1)S(1)}, u32[]{:S(2)}, u32[]{:S(2)}) collective-permute-start(bf16[128,256]{1,0:T(8,128)(2,1)S(1)} %get-tuple-element.57.refs_3_.refs_0_), channel_id=1, source_target_pairs={{0,4},{1,5},{2,6},{3,7},{4,0},{5,1},{6,2},{7,3},{8,12},{9,13},{10,... | collective-permute-start | bytes 196616 | tf_op jit(solution)/shard_map/ppermute | solution.py:60
  23.7 0.8 %shard_map.102 = (f32[512,256]{1,0:T(8,128)S(1)}, bf16[512,256]{1,0:T(8,128)(2,1)S(1)}) custom-call(bf16[3,128,1024]{2,1,0:T(8,128)(2,1)S(1)} %get-tuple-element.54.refs_0_, bf16[1,128,1024]{2,1,0:T(8,128)(2,1)S(1)} %get-tuple-element.55.refs_1_, bf16[4,128,256]{2,1,0:T(8,128)(2,1)S(1)} %get-tuple-element.56.refs_2_, ...), custom_call_target="tpu_custom_call" | custom-call | flops 1 | bytes 1 | tf_op jit(solution)/shard_map/pallas_call | solution.py:42
  24.4 1.5 %collective-permute-start.10 = (bf16[512,256]{1,0:T(8,128)(2,1)S(1)}, bf16[512,256]{1,0:T(8,128)(2,1)S(1)}, u32[]{:S(2)}, u32[]{:S(2)}) collective-permute-start(bf16[512,256]{1,0:T(8,128)(2,1)S(1)} %get-tuple-element.59.refs_2_), channel_id=1, source_target_pairs={{0,16},{16,0},{1,17},{17,1},{2,18},{18,2},{3,19},{19,3},{4,20},{20... | collective-permute-start | bytes 786440 | tf_op jit(solution)/shard_map/ppermute | solution.py:60
  26.0 1.5 %collective-permute-start.9 = (bf16[512,256]{1,0:T(8,128)(2,1)S(1)}, bf16[512,256]{1,0:T(8,128)(2,1)S(1)}, u32[]{:S(2)}, u32[]{:S(2)}) collective-permute-start(bf16[512,256]{1,0:T(8,128)(2,1)S(1)} %get-tuple-element.53), channel_id=1, source_target_pairs={{0,2},{1,3},{2,0},{3,1},{4,6},{5,7},{6,4},{7,5},{8,10},{9,11},{10,... | collective-permute-start | bytes 786440 | tf_op jit(solution)/shard_map/ppermute | solution.py:60
  27.5 3.2 %collective-permute-start.15 = (bf16[128,256]{1,0:T(8,128)(2,1)S(1)}, bf16[128,256]{1,0:T(8,128)(2,1)S(1)}, u32[]{:S(2)}, u32[]{:S(2)}) collective-permute-start(bf16[128,256]{1,0:T(8,128)(2,1)S(1)} %shard_map.103.refs_2_), channel_id=1, source_target_pairs={{0,8},{1,9},{2,10},{3,11},{4,12},{5,13},{6,14},{7,15},{8,0},{9,1},... | collective-permute-start | bytes 196616 | tf_op jit(solution)/shard_map/ppermute | solution.py:60
  30.8 0.6 %collective-permute-done.10.refs_1_ = bf16[512,256]{1,0:T(8,128)(2,1)S(1)} collective-permute-done((bf16[512,256]{1,0:T(8,128)(2,1)S(1)}, bf16[512,256]{1,0:T(8,128)(2,1)S(1)}, u32[]{:S(2)}, u32[]{:S(2)}) %collective-permute-start.10) | collective-permute-done | bytes 262176 | tf_op jit(solution)/shard_map/ppermute | solution.py:60
  31.5 0.7 %collective-permute-start.14 = (bf16[256,256]{1,0:T(8,128)(2,1)S(1)}, bf16[256,256]{1,0:T(8,128)(2,1)S(1)}, u32[]{:S(2)}, u32[]{:S(2)}) collective-permute-start(bf16[256,256]{1,0:T(8,128)(2,1)S(1)} %get-tuple-element.61.refs_2_), channel_id=1, source_target_pairs={{0,4},{1,5},{2,6},{3,7},{4,0},{5,1},{6,2},{7,3},{8,12},{9,13},{10,... | collective-permute-start | bytes 393224 | tf_op jit(solution)/shard_map/ppermute | solution.py:60
  32.2 0.4 collective-permute-done.9.refs_1_
  32.7 1.0 %collective-permute-done.15.refs_1_ = bf16[128,256]{1,0:T(8,128)(2,1)S(1)} collective-permute-done((bf16[128,256]{1,0:T(8,128)(2,1)S(1)}, bf16[128,256]{1,0:T(8,128)(2,1)S(1)}, u32[]{:S(2)}, u32[]{:S(2)}) %collective-permute-start.15) | collective-permute-done | bytes 65568 | tf_op jit(solution)/shard_map/ppermute | solution.py:60
  33.8 0.6 %collective-permute-start.17 = (bf16[256,256]{1,0:T(8,128)(2,1)S(1)}, bf16[256,256]{1,0:T(8,128)(2,1)S(1)}, u32[]{:S(2)}, u32[]{:S(2)}) collective-permute-start(bf16[256,256]{1,0:T(8,128)(2,1)S(1)} %get-tuple-element.65.refs_2_), channel_id=1, source_target_pairs={{0,2},{1,3},{2,0},{3,1},{4,6},{5,7},{6,4},{7,5},{8,10},{9,11},{10,... | collective-permute-start | bytes 393224 | tf_op jit(solution)/shard_map/ppermute | solution.py:60
  34.4 2.1 %collective-permute-done.14.refs_1_ = bf16[256,256]{1,0:T(8,128)(2,1)S(1)} collective-permute-done((bf16[256,256]{1,0:T(8,128)(2,1)S(1)}, bf16[256,256]{1,0:T(8,128)(2,1)S(1)}, u32[]{:S(2)}, u32[]{:S(2)}) %collective-permute-start.14) | collective-permute-done | bytes 131104 | tf_op jit(solution)/shard_map/ppermute | solution.py:60
  36.5 2.7 %collective-permute-start.16 = (bf16[128,256]{1,0:T(8,128)(2,1)S(1)}, bf16[128,256]{1,0:T(8,128)(2,1)S(1)}, u32[]{:S(2)}, u32[]{:S(2)}) collective-permute-start(bf16[128,256]{1,0:T(8,128)(2,1)S(1)} %get-tuple-element.66.refs_10_), channel_id=1, source_target_pairs={{0,8},{1,9},{2,10},{3,11},{4,12},{5,13},{6,14},{7,15},{8,0},{9,1},... | collective-permute-start | bytes 196616 | tf_op jit(solution)/shard_map/ppermute | solution.py:60
  39.2 2.6 %shard_map.108 = (bf16[128,1024]{1,0:T(8,128)(2,1)}, f32[4,128,256]{2,1,0:T(8,128)S(1)}, f32[4,128,256]{2,1,0:T(8,128)S(1)}, bf16[128,1024]{1,0:T(8,128)(2,1)S(1)}) custom-call(bf16[512,256]{1,0:T(8,128)(2,1)S(1)} %get-tuple-element.52.refs_0_, bf16[512,256]{1,0:T(8,128)(2,1)S(1)} %collective-permute-done.9.refs_1_, ...), custom_call_target="tpu_custom_call" | custom-call | flops 1 | bytes 1 | tf_op jit(solution)/shard_map/pallas_call | solution.py:42
  42.0 0.5 %collective-permute-done.16.refs_1_ = bf16[128,256]{1,0:T(8,128)(2,1)S(1)} collective-permute-done((bf16[128,256]{1,0:T(8,128)(2,1)S(1)}, bf16[128,256]{1,0:T(8,128)(2,1)S(1)}, u32[]{:S(2)}, u32[]{:S(2)}) %collective-permute-start.16) | collective-permute-done | bytes 65568 | tf_op jit(solution)/shard_map/ppermute | solution.py:60
  42.5 1.8 %collective-permute-start.19 = (bf16[64,256]{1,0:T(8,128)(2,1)S(1)}, bf16[64,256]{1,0:T(8,128)(2,1)S(1)}, u32[]{:S(2)}, u32[]{:S(2)}) collective-permute-start(bf16[64,256]{1,0:T(8,128)(2,1)S(1)} %get-tuple-element.70.refs_4_.refs_7_.refs_2_), channel_id=1, source_target_pairs={{0,2},{1,3},{2,0},{3,1},{4,6},{5,7},{6,4},{7,5},{8,10},{9,11},{10,... | collective-permute-start | bytes 98312 | tf_op jit(solution)/shard_map/ppermute | solution.py:60
  44.3 1.5 %shard_map.111.refs_4_ = bf16[128,1024]{1,0:T(8,128)(2,1)} custom-call(bf16[128,1024]{1,0:T(8,128)(2,1)S(1)} %get-tuple-element.67.refs_2_.refs_0_, bf16[512,1024]{1,0:T(8,128)(2,1)S(1)} %copy-done, bf16[2,512,256]{2,1,0:T(8,128)(2,1)S(1)} %collective-permute-done.8.refs_4_.refs_2_, bf16[2,512,256]{2,1,0:T(8,128)(2,1)S(1)} %collective-permute-done.12.refs_3_, ...), custom_call_target="tpu_custom_call" | custom-call | flops 1 | bytes 1 | tf_op jit(solution)/shard_map/pallas_call | solution.py:42
  45.8 1.1 %shard_map.112 = (bf16[128,1024]{1,0:T(8,128)(2,1)}, bf16[128,1024]{1,0:T(8,128)(2,1)}) custom-call(bf16[256,256]{1,0:T(8,128)(2,1)S(1)} %get-tuple-element.69.refs_0_, bf16[256,256]{1,0:T(8,128)(2,1)S(1)} %collective-permute-done.17.refs_1_, bf16[256,256]{1,0:T(8,128)(2,1)S(1)} %collective-permute-done.18.refs_2_, bf16[128,1024]{1,0:T(8,128)(2,1)S(1)} %bitcast.11, ...), custom_call_target="tpu_custom_call" | custom-call | flops 1 | bytes 1 | tf_op jit(solution)/shard_map/pallas_call | solution.py:42
  47.3 1.0 %collective-permute-done.20.refs_1_ = bf16[64,256]{1,0:T(8,128)(2,1)S(1)} collective-permute-done((bf16[64,256]{1,0:T(8,128)(2,1)S(1)}, bf16[64,256]{1,0:T(8,128)(2,1)S(1)}, u32[]{:S(2)}, u32[]{:S(2)}) %collective-permute-start.20) | collective-permute-done | bytes 32800 | tf_op jit(solution)/shard_map/ppermute | solution.py:60
  48.3 0.7 %shard_map.114 = f32[32,1024]{1,0:T(8,128)} custom-call(bf16[64,256]{1,0:T(8,128)(2,1)S(1)} %get-tuple-element.77.refs_0_, bf16[64,256]{1,0:T(8,128)(2,1)S(1)} %collective-permute-done.20.refs_1_, bf16[64,256]{1,0:T(8,128)(2,1)S(1)} %get-tuple-element.78.refs_2_), custom_call_target="tpu_custom_call" | custom-call | flops 1 | bytes 1 | tf_op jit(solution)/shard_map/pallas_call | solution.py:42
  (43 shorter events, 1.7 us)
Async XLA Ops:
  0.6 4.6 %copy-start.3 = (bf16[1,128,1024]{2,1,0:T(8,128)(2,1)S(1)}, bf16[1,128,1024]{2,1,0:T(8,128)(2,1)}, u32[]{:S(2)}) copy-start(bf16[1,128,1024]{2,1,0:T(8,128)(2,1)} %param.8) | copy-start | bytes 786436
  0.6 6.6 %copy-start.1 = (bf16[1,128,1024]{2,1,0:T(8,128)(2,1)S(1)}, bf16[1,128,1024]{2,1,0:T(8,128)(2,1)}, u32[]{:S(2)}) copy-start(bf16[1,128,1024]{2,1,0:T(8,128)(2,1)} %param.6) | copy-start | bytes 786436
  0.7 6.6 %copy-start.2 = (bf16[1,128,1024]{2,1,0:T(8,128)(2,1)S(1)}, bf16[1,128,1024]{2,1,0:T(8,128)(2,1)}, u32[]{:S(2)}) copy-start(bf16[1,128,1024]{2,1,0:T(8,128)(2,1)} %param.7) | copy-start | bytes 786436
  0.7 6.6 %copy-start.4 = (bf16[1,128,1024]{2,1,0:T(8,128)(2,1)S(1)}, bf16[1,128,1024]{2,1,0:T(8,128)(2,1)}, u32[]{:S(2)}) copy-start(bf16[1,128,1024]{2,1,0:T(8,128)(2,1)} %param.5) | copy-start | bytes 786436
  2.2 7.4 %collective-permute-start.1 = (bf16[256,256]{1,0:T(8,128)(2,1)S(1)}, bf16[256,256]{1,0:T(8,128)(2,1)S(1)}, u32[]{:S(2)}, u32[]{:S(2)}) collective-permute-start(bf16[256,256]{1,0:T(8,128)(2,1)S(1)} %get-tuple-element.47), channel_id=1, source_target_pairs={{0,2},{1,3},{2,0},{3,1},{4,6},{5,7},{6,4},{7,5},{8,10},{9,11},{10,... | collective-permute-start | bytes 393224 | tf_op jit(solution)/shard_map/ppermute | solution.py:60
  5.3 9.6 %collective-permute-start.6 = (bf16[128,1024]{1,0:T(8,128)(2,1)S(1)}, bf16[128,1024]{1,0:T(8,128)(2,1)S(1)}, u32[]{:S(2)}, u32[]{:S(2)}) collective-permute-start(bf16[128,1024]{1,0:T(8,128)(2,1)S(1)} %bitcast.16), channel_id=1, source_target_pairs={{0,2},{1,3},{2,0},{3,1},{4,6},{5,7},{6,4},{7,5},{8,10},{9,11},{10,... | collective-permute-start | bytes 786440 | tf_op jit(solution)/shard_map/ppermute | solution.py:60
  5.4 13.4 %collective-permute-start.8 = (bf16[2,512,256]{2,1,0:T(8,128)(2,1)S(1)}, bf16[2,512,256]{2,1,0:T(8,128)(2,1)S(1)}, u32[]{:S(2)}, u32[]{:S(2)}) collective-permute-start(bf16[2,512,256]{2,1,0:T(8,128)(2,1)S(1)} %get-tuple-element.49.refs_3_.refs_1_), channel_id=1, source_target_pairs={{0,16},{16,0},{1,17},{17,1},{2,18},{18,2},{3,19},{19,3},{4,20},{20... | collective-permute-start | bytes 1572872 | tf_op jit(solution)/shard_map/ppermute | solution.py:60
  8.6 4.6 %collective-permute-start = (bf16[1024,256]{1,0:T(8,128)(2,1)S(1)}, bf16[1024,256]{1,0:T(8,128)(2,1)S(1)}, u32[]{:S(2)}, u32[]{:S(2)}) collective-permute-start(bf16[1024,256]{1,0:T(8,128)(2,1)S(1)} %get-tuple-element.44.refs_8_), channel_id=1, source_target_pairs={{0,1},{1,0},{2,3},{3,2},{4,5},{5,4},{6,7},{7,6},{8,9},{9,8},{10,11... | collective-permute-start | bytes 1572872 | tf_op jit(solution)/shard_map/ppermute | solution.py:60
  9.6 1.4 %collective-permute-start.2 = (bf16[256,256]{1,0:T(8,128)(2,1)S(1)}, bf16[256,256]{1,0:T(8,128)(2,1)S(1)}, u32[]{:S(2)}, u32[]{:S(2)}) collective-permute-start(bf16[256,256]{1,0:T(8,128)(2,1)S(1)} %shard_map.94.refs_3_), channel_id=1, source_target_pairs={{0,1},{1,0},{2,3},{3,2},{4,5},{5,4},{6,7},{7,6},{8,9},{9,8},{10,11... | collective-permute-start | bytes 393224 | tf_op jit(solution)/shard_map/ppermute | solution.py:60
  11.1 4.6 %collective-permute-start.4 = (bf16[128,256]{1,0:T(8,128)(2,1)S(1)}, bf16[128,256]{1,0:T(8,128)(2,1)S(1)}, u32[]{:S(2)}, u32[]{:S(2)}) collective-permute-start(bf16[128,256]{1,0:T(8,128)(2,1)S(1)} %shard_map.95.refs_2_.refs_0_), channel_id=1, source_target_pairs={{0,4},{1,5},{2,6},{3,7},{4,0},{5,1},{6,2},{7,3},{8,12},{9,13},{10,... | collective-permute-start | bytes 196616 | tf_op jit(solution)/shard_map/ppermute | solution.py:60
  13.3 8.1 %collective-permute-start.3 = (bf16[512,256]{1,0:T(8,128)(2,1)S(1)}, bf16[512,256]{1,0:T(8,128)(2,1)S(1)}, u32[]{:S(2)}, u32[]{:S(2)}) collective-permute-start(bf16[512,256]{1,0:T(8,128)(2,1)S(1)} %shard_map.96.refs_2_), channel_id=1, source_target_pairs={{0,2},{1,3},{2,0},{3,1},{4,6},{5,7},{6,4},{7,5},{8,10},{9,11},{10,... | collective-permute-start | bytes 786440 | tf_op jit(solution)/shard_map/ppermute | solution.py:60
  14.9 4.4 %collective-permute-start.7 = (bf16[128,1024]{1,0:T(8,128)(2,1)S(1)}, bf16[128,1024]{1,0:T(8,128)(2,1)S(1)}, u32[]{:S(2)}, u32[]{:S(2)}) collective-permute-start(bf16[128,1024]{1,0:T(8,128)(2,1)S(1)} %collective-permute-done.6.refs_2_), channel_id=1, source_target_pairs={{0,1},{1,0},{2,3},{3,2},{4,5},{5,4},{6,7},{7,6},{8,9},{9,8},{10,11... | collective-permute-start | bytes 786440 | tf_op jit(solution)/shard_map/ppermute | solution.py:60
  15.7 5.6 %collective-permute-start.5 = (bf16[128,256]{1,0:T(8,128)(2,1)S(1)}, bf16[128,256]{1,0:T(8,128)(2,1)S(1)}, u32[]{:S(2)}, u32[]{:S(2)}) collective-permute-start(bf16[128,256]{1,0:T(8,128)(2,1)S(1)} %shard_map.97.refs_5_), channel_id=1, source_target_pairs={{0,8},{1,9},{2,10},{3,11},{4,12},{5,13},{6,14},{7,15},{8,0},{9,1},... | collective-permute-start | bytes 196616 | tf_op jit(solution)/shard_map/ppermute | solution.py:60
  19.2 12.3 %collective-permute-start.12 = (bf16[2,512,256]{2,1,0:T(8,128)(2,1)S(1)}, bf16[2,512,256]{2,1,0:T(8,128)(2,1)S(1)}, u32[]{:S(2)}, u32[]{:S(2)}) collective-permute-start(bf16[2,512,256]{2,1,0:T(8,128)(2,1)S(1)} %collective-permute-done.8.refs_4_.refs_2_), channel_id=1, source_target_pairs={{0,1},{1,0},{2,3},{3,2},{4,5},{5,4},{6,7},{7,6},{8,9},{9,8},{10,11... | collective-permute-start | bytes 1572872 | tf_op jit(solution)/shard_map/ppermute | solution.py:60
  22.2 5.3 %collective-permute-start.11 = (bf16[128,256]{1,0:T(8,128)(2,1)S(1)}, bf16[128,256]{1,0:T(8,128)(2,1)S(1)}, u32[]{:S(2)}, u32[]{:S(2)}) collective-permute-start(bf16[128,256]{1,0:T(8,128)(2,1)S(1)} %get-tuple-element.57.refs_3_.refs_0_), channel_id=1, source_target_pairs={{0,4},{1,5},{2,6},{3,7},{4,0},{5,1},{6,2},{7,3},{8,12},{9,13},{10,... | collective-permute-start | bytes 196616 | tf_op jit(solution)/shard_map/ppermute | solution.py:60
  24.4 7.0 %collective-permute-start.10 = (bf16[512,256]{1,0:T(8,128)(2,1)S(1)}, bf16[512,256]{1,0:T(8,128)(2,1)S(1)}, u32[]{:S(2)}, u32[]{:S(2)}) collective-permute-start(bf16[512,256]{1,0:T(8,128)(2,1)S(1)} %get-tuple-element.59.refs_2_), channel_id=1, source_target_pairs={{0,16},{16,0},{1,17},{17,1},{2,18},{18,2},{3,19},{19,3},{4,20},{20... | collective-permute-start | bytes 786440 | tf_op jit(solution)/shard_map/ppermute | solution.py:60
  26.0 6.6 %collective-permute-start.9 = (bf16[512,256]{1,0:T(8,128)(2,1)S(1)}, bf16[512,256]{1,0:T(8,128)(2,1)S(1)}, u32[]{:S(2)}, u32[]{:S(2)}) collective-permute-start(bf16[512,256]{1,0:T(8,128)(2,1)S(1)} %get-tuple-element.53), channel_id=1, source_target_pairs={{0,2},{1,3},{2,0},{3,1},{4,6},{5,7},{6,4},{7,5},{8,10},{9,11},{10,... | collective-permute-start | bytes 786440 | tf_op jit(solution)/shard_map/ppermute | solution.py:60
  27.5 6.2 %collective-permute-start.15 = (bf16[128,256]{1,0:T(8,128)(2,1)S(1)}, bf16[128,256]{1,0:T(8,128)(2,1)S(1)}, u32[]{:S(2)}, u32[]{:S(2)}) collective-permute-start(bf16[128,256]{1,0:T(8,128)(2,1)S(1)} %shard_map.103.refs_2_), channel_id=1, source_target_pairs={{0,8},{1,9},{2,10},{3,11},{4,12},{5,13},{6,14},{7,15},{8,0},{9,1},... | collective-permute-start | bytes 196616 | tf_op jit(solution)/shard_map/ppermute | solution.py:60
  31.5 5.0 %collective-permute-start.14 = (bf16[256,256]{1,0:T(8,128)(2,1)S(1)}, bf16[256,256]{1,0:T(8,128)(2,1)S(1)}, u32[]{:S(2)}, u32[]{:S(2)}) collective-permute-start(bf16[256,256]{1,0:T(8,128)(2,1)S(1)} %get-tuple-element.61.refs_2_), channel_id=1, source_target_pairs={{0,4},{1,5},{2,6},{3,7},{4,0},{5,1},{6,2},{7,3},{8,12},{9,13},{10,... | collective-permute-start | bytes 393224 | tf_op jit(solution)/shard_map/ppermute | solution.py:60
  32.6 6.6 %collective-permute-start.13 = (bf16[512,256]{1,0:T(8,128)(2,1)S(1)}, bf16[512,256]{1,0:T(8,128)(2,1)S(1)}, u32[]{:S(2)}, u32[]{:S(2)}) collective-permute-start(bf16[512,256]{1,0:T(8,128)(2,1)S(1)} %shard_map.105.refs_3_), channel_id=1, source_target_pairs={{0,1},{1,0},{2,3},{3,2},{4,5},{5,4},{6,7},{7,6},{8,9},{9,8},{10,11... | collective-permute-start | bytes 786440 | tf_op jit(solution)/shard_map/ppermute | solution.py:60
  33.8 8.0 %collective-permute-start.17 = (bf16[256,256]{1,0:T(8,128)(2,1)S(1)}, bf16[256,256]{1,0:T(8,128)(2,1)S(1)}, u32[]{:S(2)}, u32[]{:S(2)}) collective-permute-start(bf16[256,256]{1,0:T(8,128)(2,1)S(1)} %get-tuple-element.65.refs_2_), channel_id=1, source_target_pairs={{0,2},{1,3},{2,0},{3,1},{4,6},{5,7},{6,4},{7,5},{8,10},{9,11},{10,... | collective-permute-start | bytes 393224 | tf_op jit(solution)/shard_map/ppermute | solution.py:60
  36.5 5.9 %collective-permute-start.16 = (bf16[128,256]{1,0:T(8,128)(2,1)S(1)}, bf16[128,256]{1,0:T(8,128)(2,1)S(1)}, u32[]{:S(2)}, u32[]{:S(2)}) collective-permute-start(bf16[128,256]{1,0:T(8,128)(2,1)S(1)} %get-tuple-element.66.refs_10_), channel_id=1, source_target_pairs={{0,8},{1,9},{2,10},{3,11},{4,12},{5,13},{6,14},{7,15},{8,0},{9,1},... | collective-permute-start | bytes 196616 | tf_op jit(solution)/shard_map/ppermute | solution.py:60
  41.9 4.0 %collective-permute-start.18 = (bf16[256,256]{1,0:T(8,128)(2,1)S(1)}, bf16[256,256]{1,0:T(8,128)(2,1)S(1)}, u32[]{:S(2)}, u32[]{:S(2)}) collective-permute-start(bf16[256,256]{1,0:T(8,128)(2,1)S(1)} %shard_map.109.refs_2_), channel_id=1, source_target_pairs={{0,1},{1,0},{2,3},{3,2},{4,5},{5,4},{6,7},{7,6},{8,9},{9,8},{10,11... | collective-permute-start | bytes 393224 | tf_op jit(solution)/shard_map/ppermute | solution.py:60
  42.5 1.8 %copy-start = (bf16[512,1024]{1,0:T(8,128)(2,1)S(1)}, bf16[512,1024]{1,0:T(8,128)(2,1)}, u32[]{:S(2)}) copy-start(bf16[512,1024]{1,0:T(8,128)(2,1)} %refs_1_.1) | copy-start | bytes 3145732
  42.5 4.5 %collective-permute-start.19 = (bf16[64,256]{1,0:T(8,128)(2,1)S(1)}, bf16[64,256]{1,0:T(8,128)(2,1)S(1)}, u32[]{:S(2)}, u32[]{:S(2)}) collective-permute-start(bf16[64,256]{1,0:T(8,128)(2,1)S(1)} %get-tuple-element.70.refs_4_.refs_7_.refs_2_), channel_id=1, source_target_pairs={{0,2},{1,3},{2,0},{3,1},{4,6},{5,7},{6,4},{7,5},{8,10},{9,11},{10,... | collective-permute-start | bytes 98312 | tf_op jit(solution)/shard_map/ppermute | solution.py:60
  47.0 1.3 %collective-permute-start.20 = (bf16[64,256]{1,0:T(8,128)(2,1)S(1)}, bf16[64,256]{1,0:T(8,128)(2,1)S(1)}, u32[]{:S(2)}, u32[]{:S(2)}) collective-permute-start(bf16[64,256]{1,0:T(8,128)(2,1)S(1)} %get-tuple-element.78.refs_2_), channel_id=1, source_target_pairs={{0,1},{1,0},{2,3},{3,2},{4,5},{5,4},{6,7},{7,6},{8,9},{9,8},{10,11... | collective-permute-start | bytes 98312 | tf_op jit(solution)/shard_map/ppermute | solution.py:60

commit v14 on v13

--- a/solution.py
+++ b/solution.py
@@ -447,23 +447,24 @@
             scratch=[pltpu.VMEM((piece, width), F32)],
         )
         got = near(share, bits=2)
+    (output,) = call(
+        output_kernel, [((rows, outputs), BF16)], own_normed, out_weight, *w_all, end=True,
+    )
+    if tuned:
+        keep, share = call(
+            pass_kernel, [((piece // 2, width), BF16)] * 2, keep, got,
+            wait=[pltpu.with_memory_space_constraint(x, pltpu.HBM) for x in (output,)],
+        )
+        got = near(share, bits=1)
     gk, gv = call(
         last_kernel, [((rows, features), BF16)] * 2,
         later, later_far, later_core, k, v, gk_part, gv_part, end=True,
     )
-    (output,) = call(
-        output_kernel, [((rows, outputs), BF16)], own_normed, out_weight, *w_all, end=True,
-    )
-    if tuned:
-        keep, share = call(
-            pass_kernel, [((piece // 2, width), BF16)] * 2, keep, got,
-            wait=[pltpu.with_memory_space_constraint(x, pltpu.HBM) for x in (gk, output)],
-        )
-        got = near(share, bits=1)
     if tuned:
         (grad_weight,) = call(
             functools.partial(finish_kernel, factor),
             [((piece // SLAB, features), F32)], keep, got, end=True,
+            wait=[pltpu.with_memory_space_constraint(gk, pltpu.HBM)],
         )
     else:
         partial = dot(cot, own_normed, 0, 0) * factor

time: 49.1 us -> 48.5 us (0.988)
  no operation moved by 1% of the time
where the time goes in v14:
time: 48.5 us; the launch traced here: 48.4 us
  starting transfers between devices  25.7 us (53%)
  Pallas kernels  11.5 us (24%)
  waiting for transfers between devices  10.3 us (21%)
  between operations  0.83 us (2%)
    ppermute x21, starting transfers between devices, flip(): return lax.ppermute(x, axis, [(i, i ^ bits) for i in range(count)])  25.7 us
    pallas_call x23, Pallas kernels, __call__(): pl.pallas_call(inner, out_shape=[jax.ShapeDtypeStruct(s, d) for s, d in o...  11.5 us
    ppermute x21, waiting for transfers between devices, flip(): return lax.ppermute(x, axis, [(i, i ^ bits) for i in range(count)])  10.3 us
  transfers between devices with their start and end apart: 21, of which 12 were waited for; matrix products, arithmetic and copies ran while one was open for 0% of the time, Pallas kernels for 19%

profile of v14, /device:TPU:0, one launch (start us, length us, event | category | flops | bytes accessed | tf_op | source)
XLA Modules:
  0.0 48.4 jit_solution(6468652932834305426)
XLA Ops:
  0.7 1.6 %shard_map.92 = (f32[128,256]{1,0:T(8,128)S(1)}, bf16[128,256]{1,0:T(8,128)(2,1)S(1)}, bf16[256,256]{1,0:T(8,128)(2,1)S(1)}, bf16[2,512,256]{2,1,0:T(8,128)(2,1)S(1)}) custom-call(bf16[128,1024]{1,0:T(8,128)(2,1)} %bitcast.8, bf16[128,1024]{1,0:T(8,128)(2,1)} %bitcast.12, bf16[512,1024]{1,0:T(8,128)(2,1)} %refs_1_.1), custom_call_target="tpu_custom_call" | custom-call | flops 1 | bytes 1 | tf_op jit(solution)/shard_map/pallas_call | solution.py:42
  2.2 3.0 %collective-permute-start.1 = (bf16[256,256]{1,0:T(8,128)(2,1)S(1)}, bf16[256,256]{1,0:T(8,128)(2,1)S(1)}, u32[]{:S(2)}, u32[]{:S(2)}) collective-permute-start(bf16[256,256]{1,0:T(8,128)(2,1)S(1)} %get-tuple-element.47), channel_id=1, source_target_pairs={{0,2},{1,3},{2,0},{3,1},{4,6},{5,7},{6,4},{7,5},{8,10},{9,11},{10,... | collective-permute-start | bytes 393224 | tf_op jit(solution)/shard_map/ppermute | solution.py:60
  5.4 1.9 %collective-permute-start.8 = (bf16[2,512,256]{2,1,0:T(8,128)(2,1)S(1)}, bf16[2,512,256]{2,1,0:T(8,128)(2,1)S(1)}, u32[]{:S(2)}, u32[]{:S(2)}) collective-permute-start(bf16[2,512,256]{2,1,0:T(8,128)(2,1)S(1)} %get-tuple-element.49.refs_3_.refs_1_), channel_id=1, source_target_pairs={{0,16},{16,0},{1,17},{17,1},{2,18},{18,2},{3,19},{19,3},{4,20},{20... | collective-permute-start | bytes 1572872 | tf_op jit(solution)/shard_map/ppermute | solution.py:60
  7.3 1.4 %shard_map.93 = (bf16[4,2,128,128]{3,2,1,0:T(8,128)(2,1)S(1)}, bf16[256,256]{1,0:T(8,128)(2,1)S(1)}, bf16[1024,256]{1,0:T(8,128)(2,1)S(1)}, bf16[256,256]{1,0:T(8,128)(2,1)S(1)}) custom-call(bf16[128,1024]{1,0:T(8,128)(2,1)S(1)} %bitcast.19, bf16[128,1024]{1,0:T(8,128)(2,1)S(1)} %bitcast.9, bf16[128,1024]{1,0:T(8,128)(2,1)S(1)} %bitcast.13, ...), custom_call_target="tpu_custom_call" | custom-call | flops 1 | bytes 1 | tf_op jit(solution)/shard_map/pallas_call | solution.py:42
  8.7 0.9 %collective-permute-done.1.refs_1_.refs_4_ = bf16[256,256]{1,0:T(8,128)(2,1)S(1)} collective-permute-done((bf16[256,256]{1,0:T(8,128)(2,1)S(1)}, bf16[256,256]{1,0:T(8,128)(2,1)S(1)}, u32[]{:S(2)}, u32[]{:S(2)}) %collective-permute-start.1) | collective-permute-done | bytes 131104 | tf_op jit(solution)/shard_map/ppermute | solution.py:60
  9.7 1.3 %collective-permute-done.2.refs_2_.refs_5_ = bf16[256,256]{1,0:T(8,128)(2,1)S(1)} collective-permute-done((bf16[256,256]{1,0:T(8,128)(2,1)S(1)}, bf16[256,256]{1,0:T(8,128)(2,1)S(1)}, u32[]{:S(2)}, u32[]{:S(2)}) %collective-permute-start.2) | collective-permute-done | bytes 131104 | tf_op jit(solution)/shard_map/ppermute | solution.py:60
  11.1 2.2 %collective-permute-start.4 = (bf16[128,256]{1,0:T(8,128)(2,1)S(1)}, bf16[128,256]{1,0:T(8,128)(2,1)S(1)}, u32[]{:S(2)}, u32[]{:S(2)}) collective-permute-start(bf16[128,256]{1,0:T(8,128)(2,1)S(1)} %shard_map.95.refs_2_.refs_0_), channel_id=1, source_target_pairs={{0,4},{1,5},{2,6},{3,7},{4,0},{5,1},{6,2},{7,3},{8,12},{9,13},{10,... | collective-permute-start | bytes 196616 | tf_op jit(solution)/shard_map/ppermute | solution.py:60
  13.3 1.6 %collective-permute-start.3 = (bf16[512,256]{1,0:T(8,128)(2,1)S(1)}, bf16[512,256]{1,0:T(8,128)(2,1)S(1)}, u32[]{:S(2)}, u32[]{:S(2)}) collective-permute-start(bf16[512,256]{1,0:T(8,128)(2,1)S(1)} %shard_map.96.refs_2_), channel_id=1, source_target_pairs={{0,2},{1,3},{2,0},{3,1},{4,6},{5,7},{6,4},{7,5},{8,10},{9,11},{10,... | collective-permute-start | bytes 786440 | tf_op jit(solution)/shard_map/ppermute | solution.py:60
  14.9 0.8 %collective-permute-done.4.refs_1_.refs_0_ = bf16[128,256]{1,0:T(8,128)(2,1)S(1)} collective-permute-done((bf16[128,256]{1,0:T(8,128)(2,1)S(1)}, bf16[128,256]{1,0:T(8,128)(2,1)S(1)}, u32[]{:S(2)}, u32[]{:S(2)}) %collective-permute-start.4) | collective-permute-done | bytes 65568 | tf_op jit(solution)/shard_map/ppermute | solution.py:60
  15.7 2.9 %collective-permute-start.5 = (bf16[128,256]{1,0:T(8,128)(2,1)S(1)}, bf16[128,256]{1,0:T(8,128)(2,1)S(1)}, u32[]{:S(2)}, u32[]{:S(2)}) collective-permute-start(bf16[128,256]{1,0:T(8,128)(2,1)S(1)} %shard_map.97.refs_5_), channel_id=1, source_target_pairs={{0,8},{1,9},{2,10},{3,11},{4,12},{5,13},{6,14},{7,15},{8,0},{9,1},... | collective-permute-start | bytes 196616 | tf_op jit(solution)/shard_map/ppermute | solution.py:60
  18.7 0.4 shard_map.98
  19.5 1.7 %collective-permute-done.5.refs_1_ = bf16[128,256]{1,0:T(8,128)(2,1)S(1)} collective-permute-done((bf16[128,256]{1,0:T(8,128)(2,1)S(1)}, bf16[128,256]{1,0:T(8,128)(2,1)S(1)}, u32[]{:S(2)}, u32[]{:S(2)}) %collective-permute-start.5) | collective-permute-done | bytes 65568 | tf_op jit(solution)/shard_map/ppermute | solution.py:60
  21.4 0.8 %shard_map.101 = (bf16[4,128,256]{2,1,0:T(8,128)(2,1)S(1)}, bf16[512,256]{1,0:T(8,128)(2,1)S(1)}, bf16[512,256]{1,0:T(8,128)(2,1)S(1)}, f32[4,128,256]{2,1,0:T(8,128)S(1)}, bf16[128,256]{1,0:T(8,128)(2,1)S(1)}) custom-call(bf16[256,256]{1,0:T(8,128)(2,1)S(1)} %get-tuple-element.43.refs_0_.refs_7_, ...), custom_call_target="tpu_custom_call" | custom-call | flops 10000000000 | bytes 1 | tf_op jit(solution)/shard_map/pallas_call | solution.py:42
  22.2 1.5 %collective-permute-start.11 = (bf16[128,256]{1,0:T(8,128)(2,1)S(1)}, bf16[128,256]{1,0:T(8,128)(2,1)S(1)}, u32[]{:S(2)}, u32[]{:S(2)}) collective-permute-start(bf16[128,256]{1,0:T(8,128)(2,1)S(1)} %get-tuple-element.57.refs_3_.refs_0_), channel_id=1, source_target_pairs={{0,4},{1,5},{2,6},{3,7},{4,0},{5,1},{6,2},{7,3},{8,12},{9,13},{10,... | collective-permute-start | bytes 196616 | tf_op jit(solution)/shard_map/ppermute | solution.py:60
  23.7 0.8 %shard_map.102 = (f32[512,256]{1,0:T(8,128)S(1)}, bf16[512,256]{1,0:T(8,128)(2,1)S(1)}) custom-call(bf16[3,128,1024]{2,1,0:T(8,128)(2,1)S(1)} %get-tuple-element.54.refs_0_, bf16[1,128,1024]{2,1,0:T(8,128)(2,1)S(1)} %get-tuple-element.55.refs_1_, bf16[4,128,256]{2,1,0:T(8,128)(2,1)S(1)} %get-tuple-element.56.refs_2_, ...), custom_call_target="tpu_custom_call" | custom-call | flops 1 | bytes 1 | tf_op jit(solution)/shard_map/pallas_call | solution.py:42
  24.4 1.5 %collective-permute-start.10 = (bf16[512,256]{1,0:T(8,128)(2,1)S(1)}, bf16[512,256]{1,0:T(8,128)(2,1)S(1)}, u32[]{:S(2)}, u32[]{:S(2)}) collective-permute-start(bf16[512,256]{1,0:T(8,128)(2,1)S(1)} %get-tuple-element.59.refs_2_), channel_id=1, source_target_pairs={{0,16},{16,0},{1,17},{17,1},{2,18},{18,2},{3,19},{19,3},{4,20},{20... | collective-permute-start | bytes 786440 | tf_op jit(solution)/shard_map/ppermute | solution.py:60
  26.0 1.5 %collective-permute-start.9 = (bf16[512,256]{1,0:T(8,128)(2,1)S(1)}, bf16[512,256]{1,0:T(8,128)(2,1)S(1)}, u32[]{:S(2)}, u32[]{:S(2)}) collective-permute-start(bf16[512,256]{1,0:T(8,128)(2,1)S(1)} %get-tuple-element.53), channel_id=1, source_target_pairs={{0,2},{1,3},{2,0},{3,1},{4,6},{5,7},{6,4},{7,5},{8,10},{9,11},{10,... | collective-permute-start | bytes 786440 | tf_op jit(solution)/shard_map/ppermute | solution.py:60
  27.5 3.2 %collective-permute-start.15 = (bf16[128,256]{1,0:T(8,128)(2,1)S(1)}, bf16[128,256]{1,0:T(8,128)(2,1)S(1)}, u32[]{:S(2)}, u32[]{:S(2)}) collective-permute-start(bf16[128,256]{1,0:T(8,128)(2,1)S(1)} %shard_map.103.refs_2_), channel_id=1, source_target_pairs={{0,8},{1,9},{2,10},{3,11},{4,12},{5,13},{6,14},{7,15},{8,0},{9,1},... | collective-permute-start | bytes 196616 | tf_op jit(solution)/shard_map/ppermute | solution.py:60
  30.8 0.6 %collective-permute-done.10.refs_1_ = bf16[512,256]{1,0:T(8,128)(2,1)S(1)} collective-permute-done((bf16[512,256]{1,0:T(8,128)(2,1)S(1)}, bf16[512,256]{1,0:T(8,128)(2,1)S(1)}, u32[]{:S(2)}, u32[]{:S(2)}) %collective-permute-start.10) | collective-permute-done | bytes 262176 | tf_op jit(solution)/shard_map/ppermute | solution.py:60
  31.5 0.7 %collective-permute-start.14 = (bf16[256,256]{1,0:T(8,128)(2,1)S(1)}, bf16[256,256]{1,0:T(8,128)(2,1)S(1)}, u32[]{:S(2)}, u32[]{:S(2)}) collective-permute-start(bf16[256,256]{1,0:T(8,128)(2,1)S(1)} %get-tuple-element.61.refs_2_), channel_id=1, source_target_pairs={{0,4},{1,5},{2,6},{3,7},{4,0},{5,1},{6,2},{7,3},{8,12},{9,13},{10,... | collective-permute-start | bytes 393224 | tf_op jit(solution)/shard_map/ppermute | solution.py:60
  32.2 0.4 collective-permute-done.9.refs_1_
  32.7 1.0 %collective-permute-done.15.refs_1_ = bf16[128,256]{1,0:T(8,128)(2,1)S(1)} collective-permute-done((bf16[128,256]{1,0:T(8,128)(2,1)S(1)}, bf16[128,256]{1,0:T(8,128)(2,1)S(1)}, u32[]{:S(2)}, u32[]{:S(2)}) %collective-permute-start.15) | collective-permute-done | bytes 65568 | tf_op jit(solution)/shard_map/ppermute | solution.py:60
  33.8 0.6 %collective-permute-start.17 = (bf16[256,256]{1,0:T(8,128)(2,1)S(1)}, bf16[256,256]{1,0:T(8,128)(2,1)S(1)}, u32[]{:S(2)}, u32[]{:S(2)}) collective-permute-start(bf16[256,256]{1,0:T(8,128)(2,1)S(1)} %get-tuple-element.65.refs_2_), channel_id=1, source_target_pairs={{0,2},{1,3},{2,0},{3,1},{4,6},{5,7},{6,4},{7,5},{8,10},{9,11},{10,... | collective-permute-start | bytes 393224 | tf_op jit(solution)/shard_map/ppermute | solution.py:60
  34.4 2.1 %collective-permute-done.14.refs_1_ = bf16[256,256]{1,0:T(8,128)(2,1)S(1)} collective-permute-done((bf16[256,256]{1,0:T(8,128)(2,1)S(1)}, bf16[256,256]{1,0:T(8,128)(2,1)S(1)}, u32[]{:S(2)}, u32[]{:S(2)}) %collective-permute-start.14) | collective-permute-done | bytes 131104 | tf_op jit(solution)/shard_map/ppermute | solution.py:60
  36.5 2.7 %collective-permute-start.16 = (bf16[128,256]{1,0:T(8,128)(2,1)S(1)}, bf16[128,256]{1,0:T(8,128)(2,1)S(1)}, u32[]{:S(2)}, u32[]{:S(2)}) collective-permute-start(bf16[128,256]{1,0:T(8,128)(2,1)S(1)} %get-tuple-element.66.refs_10_), channel_id=1, source_target_pairs={{0,8},{1,9},{2,10},{3,11},{4,12},{5,13},{6,14},{7,15},{8,0},{9,1},... | collective-permute-start | bytes 196616 | tf_op jit(solution)/shard_map/ppermute | solution.py:60
  39.2 2.6 %shard_map.108 = (bf16[128,1024]{1,0:T(8,128)(2,1)}, f32[4,128,256]{2,1,0:T(8,128)S(1)}, f32[4,128,256]{2,1,0:T(8,128)S(1)}, bf16[128,1024]{1,0:T(8,128)(2,1)S(1)}) custom-call(bf16[512,256]{1,0:T(8,128)(2,1)S(1)} %get-tuple-element.52.refs_0_, bf16[512,256]{1,0:T(8,128)(2,1)S(1)} %collective-permute-done.9.refs_1_, ...), custom_call_target="tpu_custom_call" | custom-call | flops 1 | bytes 1 | tf_op jit(solution)/shard_map/pallas_call | solution.py:42
  42.0 0.5 %collective-permute-done.16.refs_1_ = bf16[128,256]{1,0:T(8,128)(2,1)S(1)} collective-permute-done((bf16[128,256]{1,0:T(8,128)(2,1)S(1)}, bf16[128,256]{1,0:T(8,128)(2,1)S(1)}, u32[]{:S(2)}, u32[]{:S(2)}) %collective-permute-start.16) | collective-permute-done | bytes 65568 | tf_op jit(solution)/shard_map/ppermute | solution.py:60
  42.5 1.8 %collective-permute-start.19 = (bf16[64,256]{1,0:T(8,128)(2,1)S(1)}, bf16[64,256]{1,0:T(8,128)(2,1)S(1)}, u32[]{:S(2)}, u32[]{:S(2)}) collective-permute-start(bf16[64,256]{1,0:T(8,128)(2,1)S(1)} %get-tuple-element.70.refs_4_.refs_2_), channel_id=1, source_target_pairs={{0,2},{1,3},{2,0},{3,1},{4,6},{5,7},{6,4},{7,5},{8,10},{9,11},{10,... | collective-permute-start | bytes 98312 | tf_op jit(solution)/shard_map/ppermute | solution.py:60
  44.3 1.5 %shard_map.111.refs_3_ = bf16[128,1024]{1,0:T(8,128)(2,1)} custom-call(bf16[128,1024]{1,0:T(8,128)(2,1)S(1)} %get-tuple-element.67.refs_2_.refs_0_, bf16[512,1024]{1,0:T(8,128)(2,1)S(1)} %copy-done, bf16[2,512,256]{2,1,0:T(8,128)(2,1)S(1)} %collective-permute-done.8.refs_4_.refs_2_, bf16[2,512,256]{2,1,0:T(8,128)(2,1)S(1)} %collective-permute-done.12.refs_3_, ...), custom_call_target="tpu_custom_call" | custom-call | flops 1 | bytes 1 | tf_op jit(solution)/shard_map/pallas_call | solution.py:42
  45.8 0.6 %collective-permute-done.19.refs_1_ = bf16[64,256]{1,0:T(8,128)(2,1)S(1)} collective-permute-done((bf16[64,256]{1,0:T(8,128)(2,1)S(1)}, bf16[64,256]{1,0:T(8,128)(2,1)S(1)}, u32[]{:S(2)}, u32[]{:S(2)}) %collective-permute-start.19) | collective-permute-done | bytes 32800 | tf_op jit(solution)/shard_map/ppermute | solution.py:60
  46.5 1.2 %shard_map.113 = (bf16[128,1024]{1,0:T(8,128)(2,1)}, bf16[128,1024]{1,0:T(8,128)(2,1)}) custom-call(bf16[256,256]{1,0:T(8,128)(2,1)S(1)} %get-tuple-element.69.refs_0_, bf16[256,256]{1,0:T(8,128)(2,1)S(1)} %collective-permute-done.17.refs_1_, bf16[256,256]{1,0:T(8,128)(2,1)S(1)} %collective-permute-done.18.refs_2_, bf16[128,1024]{1,0:T(8,128)(2,1)S(1)} %bitcast.11, ...), custom_call_target="tpu_custom_call" | custom-call | flops 1 | bytes 1 | tf_op jit(solution)/shard_map/pallas_call | solution.py:42
  47.7 0.7 %shard_map.114 = f32[32,1024]{1,0:T(8,128)} custom-call(bf16[64,256]{1,0:T(8,128)(2,1)S(1)} %get-tuple-element.78.refs_0_, bf16[64,256]{1,0:T(8,128)(2,1)S(1)} %collective-permute-done.20.refs_1_, bf16[64,256]{1,0:T(8,128)(2,1)S(1)} %get-tuple-element.75.refs_7_.refs_2_, bf16[128,1024]{1,0:T(8,128)(2,1)} %get-tuple-element.76.refs_3_), custom_call_target="tpu_custom_call" | custom-call | flops 1 | bytes 1 | tf_op jit(solution)/shard_map/pallas_call | solution.py:42
  (43 shorter events, 1.4 us)
Async XLA Ops:
  0.6 4.6 %copy-start.3 = (bf16[1,128,1024]{2,1,0:T(8,128)(2,1)S(1)}, bf16[1,128,1024]{2,1,0:T(8,128)(2,1)}, u32[]{:S(2)}) copy-start(bf16[1,128,1024]{2,1,0:T(8,128)(2,1)} %param.8) | copy-start | bytes 786436
  0.6 6.6 %copy-start.1 = (bf16[1,128,1024]{2,1,0:T(8,128)(2,1)S(1)}, bf16[1,128,1024]{2,1,0:T(8,128)(2,1)}, u32[]{:S(2)}) copy-start(bf16[1,128,1024]{2,1,0:T(8,128)(2,1)} %param.6) | copy-start | bytes 786436
  0.7 6.6 %copy-start.2 = (bf16[1,128,1024]{2,1,0:T(8,128)(2,1)S(1)}, bf16[1,128,1024]{2,1,0:T(8,128)(2,1)}, u32[]{:S(2)}) copy-start(bf16[1,128,1024]{2,1,0:T(8,128)(2,1)} %param.7) | copy-start | bytes 786436
  0.7 6.6 %copy-start.4 = (bf16[1,128,1024]{2,1,0:T(8,128)(2,1)S(1)}, bf16[1,128,1024]{2,1,0:T(8,128)(2,1)}, u32[]{:S(2)}) copy-start(bf16[1,128,1024]{2,1,0:T(8,128)(2,1)} %param.5) | copy-start | bytes 786436
  2.2 7.4 %collective-permute-start.1 = (bf16[256,256]{1,0:T(8,128)(2,1)S(1)}, bf16[256,256]{1,0:T(8,128)(2,1)S(1)}, u32[]{:S(2)}, u32[]{:S(2)}) collective-permute-start(bf16[256,256]{1,0:T(8,128)(2,1)S(1)} %get-tuple-element.47), channel_id=1, source_target_pairs={{0,2},{1,3},{2,0},{3,1},{4,6},{5,7},{6,4},{7,5},{8,10},{9,11},{10,... | collective-permute-start | bytes 393224 | tf_op jit(solution)/shard_map/ppermute | solution.py:60
  5.3 9.6 %collective-permute-start.6 = (bf16[128,1024]{1,0:T(8,128)(2,1)S(1)}, bf16[128,1024]{1,0:T(8,128)(2,1)S(1)}, u32[]{:S(2)}, u32[]{:S(2)}) collective-permute-start(bf16[128,1024]{1,0:T(8,128)(2,1)S(1)} %bitcast.16), channel_id=1, source_target_pairs={{0,2},{1,3},{2,0},{3,1},{4,6},{5,7},{6,4},{7,5},{8,10},{9,11},{10,... | collective-permute-start | bytes 786440 | tf_op jit(solution)/shard_map/ppermute | solution.py:60
  5.4 13.4 %collective-permute-start.8 = (bf16[2,512,256]{2,1,0:T(8,128)(2,1)S(1)}, bf16[2,512,256]{2,1,0:T(8,128)(2,1)S(1)}, u32[]{:S(2)}, u32[]{:S(2)}) collective-permute-start(bf16[2,512,256]{2,1,0:T(8,128)(2,1)S(1)} %get-tuple-element.49.refs_3_.refs_1_), channel_id=1, source_target_pairs={{0,16},{16,0},{1,17},{17,1},{2,18},{18,2},{3,19},{19,3},{4,20},{20... | collective-permute-start | bytes 1572872 | tf_op jit(solution)/shard_map/ppermute | solution.py:60
  8.6 4.6 %collective-permute-start = (bf16[1024,256]{1,0:T(8,128)(2,1)S(1)}, bf16[1024,256]{1,0:T(8,128)(2,1)S(1)}, u32[]{:S(2)}, u32[]{:S(2)}) collective-permute-start(bf16[1024,256]{1,0:T(8,128)(2,1)S(1)} %get-tuple-element.44.refs_8_), channel_id=1, source_target_pairs={{0,1},{1,0},{2,3},{3,2},{4,5},{5,4},{6,7},{7,6},{8,9},{9,8},{10,11... | collective-permute-start | bytes 1572872 | tf_op jit(solution)/shard_map/ppermute | solution.py:60
  9.6 1.4 %collective-permute-start.2 = (bf16[256,256]{1,0:T(8,128)(2,1)S(1)}, bf16[256,256]{1,0:T(8,128)(2,1)S(1)}, u32[]{:S(2)}, u32[]{:S(2)}) collective-permute-start(bf16[256,256]{1,0:T(8,128)(2,1)S(1)} %shard_map.94.refs_3_), channel_id=1, source_target_pairs={{0,1},{1,0},{2,3},{3,2},{4,5},{5,4},{6,7},{7,6},{8,9},{9,8},{10,11... | collective-permute-start | bytes 393224 | tf_op jit(solution)/shard_map/ppermute | solution.py:60
  11.1 4.6 %collective-permute-start.4 = (bf16[128,256]{1,0:T(8,128)(2,1)S(1)}, bf16[128,256]{1,0:T(8,128)(2,1)S(1)}, u32[]{:S(2)}, u32[]{:S(2)}) collective-permute-start(bf16[128,256]{1,0:T(8,128)(2,1)S(1)} %shard_map.95.refs_2_.refs_0_), channel_id=1, source_target_pairs={{0,4},{1,5},{2,6},{3,7},{4,0},{5,1},{6,2},{7,3},{8,12},{9,13},{10,... | collective-permute-start | bytes 196616 | tf_op jit(solution)/shard_map/ppermute | solution.py:60
  13.3 8.1 %collective-permute-start.3 = (bf16[512,256]{1,0:T(8,128)(2,1)S(1)}, bf16[512,256]{1,0:T(8,128)(2,1)S(1)}, u32[]{:S(2)}, u32[]{:S(2)}) collective-permute-start(bf16[512,256]{1,0:T(8,128)(2,1)S(1)} %shard_map.96.refs_2_), channel_id=1, source_target_pairs={{0,2},{1,3},{2,0},{3,1},{4,6},{5,7},{6,4},{7,5},{8,10},{9,11},{10,... | collective-permute-start | bytes 786440 | tf_op jit(solution)/shard_map/ppermute | solution.py:60
  14.9 4.4 %collective-permute-start.7 = (bf16[128,1024]{1,0:T(8,128)(2,1)S(1)}, bf16[128,1024]{1,0:T(8,128)(2,1)S(1)}, u32[]{:S(2)}, u32[]{:S(2)}) collective-permute-start(bf16[128,1024]{1,0:T(8,128)(2,1)S(1)} %collective-permute-done.6.refs_2_), channel_id=1, source_target_pairs={{0,1},{1,0},{2,3},{3,2},{4,5},{5,4},{6,7},{7,6},{8,9},{9,8},{10,11... | collective-permute-start | bytes 786440 | tf_op jit(solution)/shard_map/ppermute | solution.py:60
  15.7 5.6 %collective-permute-start.5 = (bf16[128,256]{1,0:T(8,128)(2,1)S(1)}, bf16[128,256]{1,0:T(8,128)(2,1)S(1)}, u32[]{:S(2)}, u32[]{:S(2)}) collective-permute-start(bf16[128,256]{1,0:T(8,128)(2,1)S(1)} %shard_map.97.refs_5_), channel_id=1, source_target_pairs={{0,8},{1,9},{2,10},{3,11},{4,12},{5,13},{6,14},{7,15},{8,0},{9,1},... | collective-permute-start | bytes 196616 | tf_op jit(solution)/shard_map/ppermute | solution.py:60
  19.2 12.3 %collective-permute-start.12 = (bf16[2,512,256]{2,1,0:T(8,128)(2,1)S(1)}, bf16[2,512,256]{2,1,0:T(8,128)(2,1)S(1)}, u32[]{:S(2)}, u32[]{:S(2)}) collective-permute-start(bf16[2,512,256]{2,1,0:T(8,128)(2,1)S(1)} %collective-permute-done.8.refs_4_.refs_2_), channel_id=1, source_target_pairs={{0,1},{1,0},{2,3},{3,2},{4,5},{5,4},{6,7},{7,6},{8,9},{9,8},{10,11... | collective-permute-start | bytes 1572872 | tf_op jit(solution)/shard_map/ppermute | solution.py:60
  22.2 5.3 %collective-permute-start.11 = (bf16[128,256]{1,0:T(8,128)(2,1)S(1)}, bf16[128,256]{1,0:T(8,128)(2,1)S(1)}, u32[]{:S(2)}, u32[]{:S(2)}) collective-permute-start(bf16[128,256]{1,0:T(8,128)(2,1)S(1)} %get-tuple-element.57.refs_3_.refs_0_), channel_id=1, source_target_pairs={{0,4},{1,5},{2,6},{3,7},{4,0},{5,1},{6,2},{7,3},{8,12},{9,13},{10,... | collective-permute-start | bytes 196616 | tf_op jit(solution)/shard_map/ppermute | solution.py:60
  24.4 7.0 %collective-permute-start.10 = (bf16[512,256]{1,0:T(8,128)(2,1)S(1)}, bf16[512,256]{1,0:T(8,128)(2,1)S(1)}, u32[]{:S(2)}, u32[]{:S(2)}) collective-permute-start(bf16[512,256]{1,0:T(8,128)(2,1)S(1)} %get-tuple-element.59.refs_2_), channel_id=1, source_target_pairs={{0,16},{16,0},{1,17},{17,1},{2,18},{18,2},{3,19},{19,3},{4,20},{20... | collective-permute-start | bytes 786440 | tf_op jit(solution)/shard_map/ppermute | solution.py:60
  26.0 6.6 %collective-permute-start.9 = (bf16[512,256]{1,0:T(8,128)(2,1)S(1)}, bf16[512,256]{1,0:T(8,128)(2,1)S(1)}, u32[]{:S(2)}, u32[]{:S(2)}) collective-permute-start(bf16[512,256]{1,0:T(8,128)(2,1)S(1)} %get-tuple-element.53), channel_id=1, source_target_pairs={{0,2},{1,3},{2,0},{3,1},{4,6},{5,7},{6,4},{7,5},{8,10},{9,11},{10,... | collective-permute-start | bytes 786440 | tf_op jit(solution)/shard_map/ppermute | solution.py:60
  27.5 6.2 %collective-permute-start.15 = (bf16[128,256]{1,0:T(8,128)(2,1)S(1)}, bf16[128,256]{1,0:T(8,128)(2,1)S(1)}, u32[]{:S(2)}, u32[]{:S(2)}) collective-permute-start(bf16[128,256]{1,0:T(8,128)(2,1)S(1)} %shard_map.103.refs_2_), channel_id=1, source_target_pairs={{0,8},{1,9},{2,10},{3,11},{4,12},{5,13},{6,14},{7,15},{8,0},{9,1},... | collective-permute-start | bytes 196616 | tf_op jit(solution)/shard_map/ppermute | solution.py:60
  31.5 5.0 %collective-permute-start.14 = (bf16[256,256]{1,0:T(8,128)(2,1)S(1)}, bf16[256,256]{1,0:T(8,128)(2,1)S(1)}, u32[]{:S(2)}, u32[]{:S(2)}) collective-permute-start(bf16[256,256]{1,0:T(8,128)(2,1)S(1)} %get-tuple-element.61.refs_2_), channel_id=1, source_target_pairs={{0,4},{1,5},{2,6},{3,7},{4,0},{5,1},{6,2},{7,3},{8,12},{9,13},{10,... | collective-permute-start | bytes 393224 | tf_op jit(solution)/shard_map/ppermute | solution.py:60
  32.6 6.6 %collective-permute-start.13 = (bf16[512,256]{1,0:T(8,128)(2,1)S(1)}, bf16[512,256]{1,0:T(8,128)(2,1)S(1)}, u32[]{:S(2)}, u32[]{:S(2)}) collective-permute-start(bf16[512,256]{1,0:T(8,128)(2,1)S(1)} %shard_map.105.refs_3_), channel_id=1, source_target_pairs={{0,1},{1,0},{2,3},{3,2},{4,5},{5,4},{6,7},{7,6},{8,9},{9,8},{10,11... | collective-permute-start | bytes 786440 | tf_op jit(solution)/shard_map/ppermute | solution.py:60
  33.8 8.0 %collective-permute-start.17 = (bf16[256,256]{1,0:T(8,128)(2,1)S(1)}, bf16[256,256]{1,0:T(8,128)(2,1)S(1)}, u32[]{:S(2)}, u32[]{:S(2)}) collective-permute-start(bf16[256,256]{1,0:T(8,128)(2,1)S(1)} %get-tuple-element.65.refs_2_), channel_id=1, source_target_pairs={{0,2},{1,3},{2,0},{3,1},{4,6},{5,7},{6,4},{7,5},{8,10},{9,11},{10,... | collective-permute-start | bytes 393224 | tf_op jit(solution)/shard_map/ppermute | solution.py:60
  36.5 5.9 %collective-permute-start.16 = (bf16[128,256]{1,0:T(8,128)(2,1)S(1)}, bf16[128,256]{1,0:T(8,128)(2,1)S(1)}, u32[]{:S(2)}, u32[]{:S(2)}) collective-permute-start(bf16[128,256]{1,0:T(8,128)(2,1)S(1)} %get-tuple-element.66.refs_10_), channel_id=1, source_target_pairs={{0,8},{1,9},{2,10},{3,11},{4,12},{5,13},{6,14},{7,15},{8,0},{9,1},... | collective-permute-start | bytes 196616 | tf_op jit(solution)/shard_map/ppermute | solution.py:60
  41.9 4.6 %collective-permute-start.18 = (bf16[256,256]{1,0:T(8,128)(2,1)S(1)}, bf16[256,256]{1,0:T(8,128)(2,1)S(1)}, u32[]{:S(2)}, u32[]{:S(2)}) collective-permute-start(bf16[256,256]{1,0:T(8,128)(2,1)S(1)} %shard_map.109.refs_2_), channel_id=1, source_target_pairs={{0,1},{1,0},{2,3},{3,2},{4,5},{5,4},{6,7},{7,6},{8,9},{9,8},{10,11... | collective-permute-start | bytes 393224 | tf_op jit(solution)/shard_map/ppermute | solution.py:60
  42.5 1.8 %copy-start = (bf16[512,1024]{1,0:T(8,128)(2,1)S(1)}, bf16[512,1024]{1,0:T(8,128)(2,1)}, u32[]{:S(2)}) copy-start(bf16[512,1024]{1,0:T(8,128)(2,1)} %refs_1_.1) | copy-start | bytes 3145732
  42.5 4.0 %collective-permute-start.19 = (bf16[64,256]{1,0:T(8,128)(2,1)S(1)}, bf16[64,256]{1,0:T(8,128)(2,1)S(1)}, u32[]{:S(2)}, u32[]{:S(2)}) collective-permute-start(bf16[64,256]{1,0:T(8,128)(2,1)S(1)} %get-tuple-element.70.refs_4_.refs_2_), channel_id=1, source_target_pairs={{0,2},{1,3},{2,0},{3,1},{4,6},{5,7},{6,4},{7,5},{8,10},{9,11},{10,... | collective-permute-start | bytes 98312 | tf_op jit(solution)/shard_map/ppermute | solution.py:60
  46.5 1.2 %collective-permute-start.20 = (bf16[64,256]{1,0:T(8,128)(2,1)S(1)}, bf16[64,256]{1,0:T(8,128)(2,1)S(1)}, u32[]{:S(2)}, u32[]{:S(2)}) collective-permute-start(bf16[64,256]{1,0:T(8,128)(2,1)S(1)} %get-tuple-element.75.refs_7_.refs_2_), channel_id=1, source_target_pairs={{0,1},{1,0},{2,3},{3,2},{4,5},{5,4},{6,7},{7,6},{8,9},{9,8},{10,11... | collective-permute-start | bytes 98312 | tf_op jit(solution)/shard_map/ppermute | solution.py:60

commit v15 on v14

--- a/solution.py
+++ b/solution.py
@@ -286,32 +286,36 @@
         gv_ref[:, at] = jnp.concatenate(gvs, axis=1).astype(BF16)
 
 
-def product_kernel(slabs, cot_a, cot_b, normed_ref, keep_ref, send_ref):
+def product_kernel(slabs, cot_a, cot_b, normed_ref, keep_a, send_a, keep_b, send_b):
     me = lax.axis_index("dp")
     slab = lax.div(lax.axis_index("seq"), SLAB)
-    rows = keep_ref.shape[0] // slabs
-    for j, out in enumerate((send_ref, keep_ref)):
-        for d in range(slabs):
-            at = jnp.bitwise_xor(me, 1 - j) * slabs + jnp.bitwise_xor(slab, d)
-            total = dot(cot_b[0, :, cut(at, rows)], normed_ref[3], 0, 0)
-            for r in range(3):
-                total = total + dot(cot_a[r, :, cut(at, rows)], normed_ref[r], 0, 0)
-            out[part(d, rows), :] = total.astype(out.dtype)
-
-
-def split_kernel(own_ref, got_ref, keep_ref, send_ref):
-    rows = keep_ref.shape[0] // 2
-    for i in range(4):
-        total = own_ref[part(i, rows), :] + got_ref[part(i, rows), :].astype(F32)
-        out = (keep_ref, send_ref)[i % 2]
-        out[part(i // 2, rows), :] = total.astype(out.dtype)
-
-
-def split_again_kernel(own_ref, got_ref, keep_ref, send_ref):
-    rows = keep_ref.shape[0]
-    for i, out in enumerate((keep_ref, send_ref)):
-        total = own_ref[part(i, rows), :] + got_ref[part(i, rows), :].astype(F32)
-        out[...] = total.astype(out.dtype)
+    rows, width = keep_a.shape[0] // 4, keep_a.shape[1]
+    for j in range(2):
+        for l in range(2):
+            for h in range(2):
+                at = jnp.bitwise_xor(me, j) * slabs + jnp.bitwise_xor(slab, l + 2 * h)
+                total = dot(cot_b[0, :, cut(at, rows)], normed_ref[3], 0, 0)
+                for r in range(3):
+                    total = total + dot(cot_a[r, :, cut(at, rows)], normed_ref[r], 0, 0)
+                out = (keep_a, send_a)[j]
+                out[part(2 * l + h, rows), :] = total[:, :width].astype(out.dtype)
+                out = (keep_b, send_b)[l]
+                out[part(2 * j + h, rows), :] = total[:, width:].astype(out.dtype)
+
+
+def split_kernel(own_a, got_a, own_b, got_b, keep_a, send_a, keep_b, send_b):
+    size = keep_a.shape[0]
+    for own, got, keep, send in ((own_a, got_a, keep_a, send_a), (own_b, got_b, keep_b, send_b)):
+        keep[...] = own[:size, :] + got[:size, :].astype(F32)
+        send[...] = (own[size:, :] + got[size:, :].astype(F32)).astype(BF16)
+
+
+def split_again_kernel(own_a, got_a, own_b, got_b, keep_ref, send_ref):
+    rows, width = keep_ref.shape[0], own_a.shape[1]
+    for i, (own, got) in enumerate(((own_a, got_a), (own_b, got_b))):
+        total = own[...] + got[...].astype(F32)
+        keep_ref[:, part(i, width)] = total[:rows, :]
+        send_ref[:, part(i, width)] = total[rows:, :].astype(BF16)
 
 
 def share_kernel(own_ref, got_ref, keep_ref, send_ref, total_ref):
@@ -410,49 +414,51 @@
     tuned = dp == 2 and slabs == 4 and outputs // (dp * seq) % 8 == 0
     piece = outputs // (dp * slabs)
     if tuned:
-        keep, send = call(
+        keep_a, send_a, keep_b, send_b = call(
             functools.partial(product_kernel, slabs),
-            [((outputs // dp, width), F32), ((outputs // dp, width), BF16)], cots, cot_b, normed,
-        )
-        got = flip(send, "dp", dp, 1)
+            [((4 * piece, width // 2), F32), ((4 * piece, width // 2), BF16)] * 2, cots, cot_b, normed,
+        )
+        got_a, got_b = flip(send_a, "dp", dp, 1), near(send_b, bits=SLAB)
     back_far = near(back_far, bits=2)
-    behind, last_u = doubling(slab_u, 15 * 10**8)
-    if tuned:
-        keep, send = call(
-            split_kernel, [((2 * piece, width), F32), ((2 * piece, width), BF16)], keep, got, wait=w_all[1::2]
-        )
-        got = near(send, bits=SLAB)
+    if tuned:
+        keep_a, send_a, keep_b, send_b = call(
+            split_kernel, [((2 * piece, width // 2), F32), ((2 * piece, width // 2), BF16)] * 2,
+            keep_a, got_a, keep_b, got_b, wait=w_all[1::2],
+        )
+        got_a, got_b = near(send_a, bits=SLAB), flip(send_b, "dp", dp, 1)
+    behind, last_u = doubling(slab_u)
     (send,) = call(relay_kernel, [((2 * rows + 2 * DH, width), BF16)], back, back_far)
     back_core = near(send, bits=1)
+    if tuned:
+        keep, send = call(
+            split_again_kernel, [((piece, width), F32), ((piece, width), BF16)],
+            keep_a, got_a, keep_b, got_b, cost=3 * 10**9,
+        )
+        got = near(send, bits=2 * SLAB)
     later, later_far = call(
-        later_kernel, [((2 * DH, width), BF16)] * 2, *behind, u, cost=2 * 10**9,
+        later_kernel, [((2 * DH, width), BF16)] * 2, *behind, u,
         scratch=[pltpu.VMEM((SLAB, DH, width), F32)],
     )
     later_far = near(later_far, bits=2)
-    if tuned:
-        keep, send = call(
-            split_again_kernel, [((piece, width), F32), ((piece, width), BF16)], keep, got, cost=2 * 10**9
-        )
-        got = near(send, bits=2 * SLAB)
     gq, gk_part, gv_part, own_normed = call(
         late_kernel,
         [((rows, features), BF16), ((SLAB, rows, width), F32), ((SLAB, rows, width), F32), ((rows, features), BF16)],
         back, back_far, back_core, q, k, v, attend, own_tokens, *sent,
     )
-    (send,) = call(relay_kernel, [((2 * DH, width), BF16)], later, later_far)
-    later_core = near(send, bits=1)
     if tuned:
         keep, share = call(
             share_kernel, [((piece // 2, width), BF16)] * 2, keep, got, cost=3 * 10**9,
             scratch=[pltpu.VMEM((piece, width), F32)],
         )
         got = near(share, bits=2)
+    (send,) = call(relay_kernel, [((2 * DH, width), BF16)], later, later_far)
+    later_core = near(send, bits=1)
     (output,) = call(
         output_kernel, [((rows, outputs), BF16)], own_normed, out_weight, *w_all, end=True,
     )
     if tuned:
         keep, share = call(
-            pass_kernel, [((piece // 2, width), BF16)] * 2, keep, got,
+            pass_kernel, [((piece // 2, width), BF16)] * 2, keep, got, cost=3 * 10**9,
             wait=[pltpu.with_memory_space_constraint(x, pltpu.HBM) for x in (output,)],
         )
         got = near(share, bits=1)

time: 48.5 us -> 49.9 us (1.029)
  starting transfers between devices: 25.7 us -> 28.5 us
  waiting for transfers between devices: 10.3 us -> 8.87 us
    ppermute x21 -> x23, starting transfers between devices: 25.7 us -> 28.5 us  [flip(): return lax.ppermute(x, axis, [(i, i ^ bits) for i in range(count)])]
    ppermute x21 -> x23, waiting for transfers between devices: 10.3 us -> 8.87 us  [flip(): return lax.ppermute(x, axis, [(i, i ^ bits) for i in range(count)])]
  transfers between devices with their start and end apart: 21 -> 23, of which waited for: 12 -> 10; matrix products, arithmetic and copies ran while one was open for 0% -> 0% of each run, Pallas kernels for 19% -> 19%
where the time goes in v15:
time: 49.9 us; the launch traced here: 49.7 us
  starting transfers between devices  28.5 us (57%)
  Pallas kernels  11.5 us (23%)
  waiting for transfers between devices  8.87 us (18%)
  between operations  0.85 us (2%)
    ppermute x23, starting transfers between devices, flip(): return lax.ppermute(x, axis, [(i, i ^ bits) for i in range(count)])  28.5 us
    pallas_call x23, Pallas kernels, __call__(): pl.pallas_call(inner, out_shape=[jax.ShapeDtypeStruct(s, d) for s, d in o...  11.5 us
    ppermute x23, waiting for transfers between devices, flip(): return lax.ppermute(x, axis, [(i, i ^ bits) for i in range(count)])  8.87 us
  transfers between devices with their start and end apart: 23, of which 10 were waited for; matrix products, arithmetic and copies ran while one was open for 0% of the time, Pallas kernels for 19%

profile of v15, /device:TPU:0, one launch (start us, length us, event | category | flops | bytes accessed | tf_op | source)
XLA Modules:
  0.0 49.7 jit_solution(13331789820201307545)
XLA Ops:
  0.7 1.6 %shard_map.92 = (f32[128,256]{1,0:T(8,128)S(1)}, bf16[128,256]{1,0:T(8,128)(2,1)S(1)}, bf16[256,256]{1,0:T(8,128)(2,1)S(1)}, bf16[2,512,256]{2,1,0:T(8,128)(2,1)S(1)}) custom-call(bf16[128,1024]{1,0:T(8,128)(2,1)} %bitcast.8, bf16[128,1024]{1,0:T(8,128)(2,1)} %bitcast.12, bf16[512,1024]{1,0:T(8,128)(2,1)} %refs_1_.1), custom_call_target="tpu_custom_call" | custom-call | flops 1 | bytes 1 | tf_op jit(solution)/shard_map/pallas_call | solution.py:42
  2.2 3.0 %collective-permute-start.1 = (bf16[256,256]{1,0:T(8,128)(2,1)S(1)}, bf16[256,256]{1,0:T(8,128)(2,1)S(1)}, u32[]{:S(2)}, u32[]{:S(2)}) collective-permute-start(bf16[256,256]{1,0:T(8,128)(2,1)S(1)} %get-tuple-element.51), channel_id=1, source_target_pairs={{0,2},{1,3},{2,0},{3,1},{4,6},{5,7},{6,4},{7,5},{8,10},{9,11},{10,... | collective-permute-start | bytes 393224 | tf_op jit(solution)/shard_map/ppermute | solution.py:60
  5.4 1.9 %collective-permute-start.8 = (bf16[2,512,256]{2,1,0:T(8,128)(2,1)S(1)}, bf16[2,512,256]{2,1,0:T(8,128)(2,1)S(1)}, u32[]{:S(2)}, u32[]{:S(2)}) collective-permute-start(bf16[2,512,256]{2,1,0:T(8,128)(2,1)S(1)} %get-tuple-element.53.refs_3_.refs_1_), channel_id=1, source_target_pairs={{0,16},{16,0},{1,17},{17,1},{2,18},{18,2},{3,19},{19,3},{4,20},{20... | collective-permute-start | bytes 1572872 | tf_op jit(solution)/shard_map/ppermute | solution.py:60
  7.3 1.4 %shard_map.93 = (bf16[4,2,128,128]{3,2,1,0:T(8,128)(2,1)S(1)}, bf16[256,256]{1,0:T(8,128)(2,1)S(1)}, bf16[1024,256]{1,0:T(8,128)(2,1)S(1)}, bf16[256,256]{1,0:T(8,128)(2,1)S(1)}) custom-call(bf16[128,1024]{1,0:T(8,128)(2,1)S(1)} %bitcast.19, bf16[128,1024]{1,0:T(8,128)(2,1)S(1)} %bitcast.9, bf16[128,1024]{1,0:T(8,128)(2,1)S(1)} %bitcast.13, ...), custom_call_target="tpu_custom_call" | custom-call | flops 1 | bytes 1 | tf_op jit(solution)/shard_map/pallas_call | solution.py:42
  8.7 0.9 %collective-permute-done.1.refs_1_.refs_4_ = bf16[256,256]{1,0:T(8,128)(2,1)S(1)} collective-permute-done((bf16[256,256]{1,0:T(8,128)(2,1)S(1)}, bf16[256,256]{1,0:T(8,128)(2,1)S(1)}, u32[]{:S(2)}, u32[]{:S(2)}) %collective-permute-start.1) | collective-permute-done | bytes 131104 | tf_op jit(solution)/shard_map/ppermute | solution.py:60
  9.7 1.3 %collective-permute-done.2.refs_2_.refs_5_ = bf16[256,256]{1,0:T(8,128)(2,1)S(1)} collective-permute-done((bf16[256,256]{1,0:T(8,128)(2,1)S(1)}, bf16[256,256]{1,0:T(8,128)(2,1)S(1)}, u32[]{:S(2)}, u32[]{:S(2)}) %collective-permute-start.2) | collective-permute-done | bytes 131104 | tf_op jit(solution)/shard_map/ppermute | solution.py:60
  11.1 2.2 %collective-permute-start.4 = (bf16[128,256]{1,0:T(8,128)(2,1)S(1)}, bf16[128,256]{1,0:T(8,128)(2,1)S(1)}, u32[]{:S(2)}, u32[]{:S(2)}) collective-permute-start(bf16[128,256]{1,0:T(8,128)(2,1)S(1)} %shard_map.95.refs_2_.refs_0_), channel_id=1, source_target_pairs={{0,4},{1,5},{2,6},{3,7},{4,0},{5,1},{6,2},{7,3},{8,12},{9,13},{10,... | collective-permute-start | bytes 196616 | tf_op jit(solution)/shard_map/ppermute | solution.py:60
  13.3 1.6 %collective-permute-start.3 = (bf16[512,256]{1,0:T(8,128)(2,1)S(1)}, bf16[512,256]{1,0:T(8,128)(2,1)S(1)}, u32[]{:S(2)}, u32[]{:S(2)}) collective-permute-start(bf16[512,256]{1,0:T(8,128)(2,1)S(1)} %shard_map.96.refs_2_), channel_id=1, source_target_pairs={{0,2},{1,3},{2,0},{3,1},{4,6},{5,7},{6,4},{7,5},{8,10},{9,11},{10,... | collective-permute-start | bytes 786440 | tf_op jit(solution)/shard_map/ppermute | solution.py:60
  14.9 0.8 %collective-permute-done.4.refs_1_.refs_0_ = bf16[128,256]{1,0:T(8,128)(2,1)S(1)} collective-permute-done((bf16[128,256]{1,0:T(8,128)(2,1)S(1)}, bf16[128,256]{1,0:T(8,128)(2,1)S(1)}, u32[]{:S(2)}, u32[]{:S(2)}) %collective-permute-start.4) | collective-permute-done | bytes 65568 | tf_op jit(solution)/shard_map/ppermute | solution.py:60
  15.7 2.9 %collective-permute-start.5 = (bf16[128,256]{1,0:T(8,128)(2,1)S(1)}, bf16[128,256]{1,0:T(8,128)(2,1)S(1)}, u32[]{:S(2)}, u32[]{:S(2)}) collective-permute-start(bf16[128,256]{1,0:T(8,128)(2,1)S(1)} %shard_map.97.refs_5_), channel_id=1, source_target_pairs={{0,8},{1,9},{2,10},{3,11},{4,12},{5,13},{6,14},{7,15},{8,0},{9,1},... | collective-permute-start | bytes 196616 | tf_op jit(solution)/shard_map/ppermute | solution.py:60
  18.7 0.4 shard_map.98
  19.3 0.2 shard_map.99
  19.5 1.7 %collective-permute-done.5.refs_1_ = bf16[128,256]{1,0:T(8,128)(2,1)S(1)} collective-permute-done((bf16[128,256]{1,0:T(8,128)(2,1)S(1)}, bf16[128,256]{1,0:T(8,128)(2,1)S(1)}, u32[]{:S(2)}, u32[]{:S(2)}) %collective-permute-start.5) | collective-permute-done | bytes 65568 | tf_op jit(solution)/shard_map/ppermute | solution.py:60
  21.4 0.8 %shard_map.101 = (bf16[4,128,256]{2,1,0:T(8,128)(2,1)S(1)}, bf16[512,256]{1,0:T(8,128)(2,1)S(1)}, bf16[512,256]{1,0:T(8,128)(2,1)S(1)}, f32[4,128,256]{2,1,0:T(8,128)S(1)}, bf16[128,256]{1,0:T(8,128)(2,1)S(1)}) custom-call(bf16[256,256]{1,0:T(8,128)(2,1)S(1)} %get-tuple-element.47.refs_0_.refs_7_, ...), custom_call_target="tpu_custom_call" | custom-call | flops 10000000000 | bytes 1 | tf_op jit(solution)/shard_map/pallas_call | solution.py:42
  22.2 1.6 %collective-permute-start.9 = (bf16[512,256]{1,0:T(8,128)(2,1)S(1)}, bf16[512,256]{1,0:T(8,128)(2,1)S(1)}, u32[]{:S(2)}, u32[]{:S(2)}) collective-permute-start(bf16[512,256]{1,0:T(8,128)(2,1)S(1)} %get-tuple-element.57), channel_id=1, source_target_pairs={{0,2},{1,3},{2,0},{3,1},{4,6},{5,7},{6,4},{7,5},{8,10},{9,11},{10,... | collective-permute-start | bytes 786440 | tf_op jit(solution)/shard_map/ppermute | solution.py:60
  23.8 0.8 %shard_map.102 = (f32[512,128]{1,0:T(8,128)S(1)}, bf16[512,128]{1,0:T(8,128)(2,1)S(1)}, f32[512,128]{1,0:T(8,128)S(1)}, bf16[512,128]{1,0:T(8,128)(2,1)S(1)}) custom-call(bf16[3,128,1024]{2,1,0:T(8,128)(2,1)S(1)} %get-tuple-element.59.refs_0_, bf16[1,128,1024]{2,1,0:T(8,128)(2,1)S(1)} %get-tuple-element.60.refs_1_, ...), custom_call_target="tpu_custom_call" | custom-call | flops 1 | bytes 1 | tf_op jit(solution)/shard_map/pallas_call | solution.py:42
  24.6 1.5 %collective-permute-start.11 = (bf16[512,128]{1,0:T(8,128)(2,1)S(1)}, bf16[512,128]{1,0:T(8,128)(2,1)S(1)}, u32[]{:S(2)}, u32[]{:S(2)}) collective-permute-start(bf16[512,128]{1,0:T(8,128)(2,1)S(1)} %get-tuple-element.63), channel_id=1, source_target_pairs={{0,16},{16,0},{1,17},{17,1},{2,18},{18,2},{3,19},{19,3},{4,20},{20... | collective-permute-start | bytes 393224 | tf_op jit(solution)/shard_map/ppermute | solution.py:60
  26.1 1.4 %collective-permute-start.12 = (bf16[512,128]{1,0:T(8,128)(2,1)S(1)}, bf16[512,128]{1,0:T(8,128)(2,1)S(1)}, u32[]{:S(2)}, u32[]{:S(2)}) collective-permute-start(bf16[512,128]{1,0:T(8,128)(2,1)S(1)} %get-tuple-element.65.refs_4_), channel_id=1, source_target_pairs={{0,4},{1,5},{2,6},{3,7},{4,0},{5,1},{6,2},{7,3},{8,12},{9,13},{10,... | collective-permute-start | bytes 393224 | tf_op jit(solution)/shard_map/ppermute | solution.py:60
  27.5 0.6 %collective-permute-start.10 = (bf16[128,256]{1,0:T(8,128)(2,1)S(1)}, bf16[128,256]{1,0:T(8,128)(2,1)S(1)}, u32[]{:S(2)}, u32[]{:S(2)}) collective-permute-start(bf16[128,256]{1,0:T(8,128)(2,1)S(1)} %get-tuple-element.58.refs_3_.refs_0_), channel_id=1, source_target_pairs={{0,4},{1,5},{2,6},{3,7},{4,0},{5,1},{6,2},{7,3},{8,12},{9,13},{10,... | collective-permute-start | bytes 196616 | tf_op jit(solution)/shard_map/ppermute | solution.py:60
  28.1 1.5 %collective-permute-done.11.refs_1_ = bf16[512,128]{1,0:T(8,128)(2,1)S(1)} collective-permute-done((bf16[512,128]{1,0:T(8,128)(2,1)S(1)}, bf16[512,128]{1,0:T(8,128)(2,1)S(1)}, u32[]{:S(2)}, u32[]{:S(2)}) %collective-permute-start.11) | collective-permute-done | bytes 131104 | tf_op jit(solution)/shard_map/ppermute | solution.py:60
  29.6 1.5 %collective-permute-done.12.refs_3_ = bf16[512,128]{1,0:T(8,128)(2,1)S(1)} collective-permute-done((bf16[512,128]{1,0:T(8,128)(2,1)S(1)}, bf16[512,128]{1,0:T(8,128)(2,1)S(1)}, u32[]{:S(2)}, u32[]{:S(2)}) %collective-permute-start.12) | collective-permute-done | bytes 131104 | tf_op jit(solution)/shard_map/ppermute | solution.py:60
  31.1 1.5 %collective-permute-start.16 = (bf16[256,128]{1,0:T(8,128)(2,1)S(1)}, bf16[256,128]{1,0:T(8,128)(2,1)S(1)}, u32[]{:S(2)}, u32[]{:S(2)}) collective-permute-start(bf16[256,128]{1,0:T(8,128)(2,1)S(1)} %get-tuple-element.71), channel_id=1, source_target_pairs={{0,4},{1,5},{2,6},{3,7},{4,0},{5,1},{6,2},{7,3},{8,12},{9,13},{10,... | collective-permute-start | bytes 196616 | tf_op jit(solution)/shard_map/ppermute | solution.py:60
  32.6 0.5 %collective-permute-start.17 = (bf16[256,128]{1,0:T(8,128)(2,1)S(1)}, bf16[256,128]{1,0:T(8,128)(2,1)S(1)}, u32[]{:S(2)}, u32[]{:S(2)}) collective-permute-start(bf16[256,128]{1,0:T(8,128)(2,1)S(1)} %get-tuple-element.67.refs_2_), channel_id=1, source_target_pairs={{0,16},{16,0},{1,17},{17,1},{2,18},{18,2},{3,19},{19,3},{4,20},{20... | collective-permute-start | bytes 196616 | tf_op jit(solution)/shard_map/ppermute | solution.py:60
  33.2 3.5 %collective-permute-start.15 = (bf16[128,256]{1,0:T(8,128)(2,1)S(1)}, bf16[128,256]{1,0:T(8,128)(2,1)S(1)}, u32[]{:S(2)}, u32[]{:S(2)}) collective-permute-start(bf16[128,256]{1,0:T(8,128)(2,1)S(1)} %shard_map.104.refs_2_), channel_id=1, source_target_pairs={{0,8},{1,9},{2,10},{3,11},{4,12},{5,13},{6,14},{7,15},{8,0},{9,1},... | collective-permute-start | bytes 196616 | tf_op jit(solution)/shard_map/ppermute | solution.py:60
  36.9 3.5 %collective-permute-start.19 = (bf16[128,256]{1,0:T(8,128)(2,1)S(1)}, bf16[128,256]{1,0:T(8,128)(2,1)S(1)}, u32[]{:S(2)}, u32[]{:S(2)}) collective-permute-start(bf16[128,256]{1,0:T(8,128)(2,1)S(1)} %get-tuple-element.73.refs_3_), channel_id=1, source_target_pairs={{0,8},{1,9},{2,10},{3,11},{4,12},{5,13},{6,14},{7,15},{8,0},{9,1},... | collective-permute-start | bytes 196616 | tf_op jit(solution)/shard_map/ppermute | solution.py:60
  40.6 0.6 %collective-permute-start.18 = (bf16[256,256]{1,0:T(8,128)(2,1)S(1)}, bf16[256,256]{1,0:T(8,128)(2,1)S(1)}, u32[]{:S(2)}, u32[]{:S(2)}) collective-permute-start(bf16[256,256]{1,0:T(8,128)(2,1)S(1)} %get-tuple-element.74.refs_10_), channel_id=1, source_target_pairs={{0,2},{1,3},{2,0},{3,1},{4,6},{5,7},{6,4},{7,5},{8,10},{9,11},{10,... | collective-permute-start | bytes 393224 | tf_op jit(solution)/shard_map/ppermute | solution.py:60
  41.2 2.6 %shard_map.108 = (bf16[128,1024]{1,0:T(8,128)(2,1)}, f32[4,128,256]{2,1,0:T(8,128)S(1)}, f32[4,128,256]{2,1,0:T(8,128)S(1)}, bf16[128,1024]{1,0:T(8,128)(2,1)S(1)}) custom-call(bf16[512,256]{1,0:T(8,128)(2,1)S(1)} %get-tuple-element.56.refs_0_, bf16[512,256]{1,0:T(8,128)(2,1)S(1)} %collective-permute-done.9.refs_1_, ...), custom_call_target="tpu_custom_call" | custom-call | flops 1 | bytes 1 | tf_op jit(solution)/shard_map/pallas_call | solution.py:42
  43.8 1.6 %collective-permute-start.21 = (bf16[64,256]{1,0:T(8,128)(2,1)S(1)}, bf16[64,256]{1,0:T(8,128)(2,1)S(1)}, u32[]{:S(2)}, u32[]{:S(2)}) collective-permute-start(bf16[64,256]{1,0:T(8,128)(2,1)S(1)} %get-tuple-element.78.refs_2_), channel_id=1, source_target_pairs={{0,2},{1,3},{2,0},{3,1},{4,6},{5,7},{6,4},{7,5},{8,10},{9,11},{10,... | collective-permute-start | bytes 98312 | tf_op jit(solution)/shard_map/ppermute | solution.py:60
  45.7 1.5 %shard_map.111.refs_3_ = bf16[128,1024]{1,0:T(8,128)(2,1)} custom-call(bf16[128,1024]{1,0:T(8,128)(2,1)S(1)} %get-tuple-element.75.refs_2_.refs_0_, bf16[512,1024]{1,0:T(8,128)(2,1)S(1)} %copy-done, bf16[2,512,256]{2,1,0:T(8,128)(2,1)S(1)} %collective-permute-done.8.refs_4_.refs_2_, bf16[2,512,256]{2,1,0:T(8,128)(2,1)S(1)} %collective-permute-done.13.refs_5_.refs_3_, ...), custom_call_target="tpu_custom_call" | custom-call | flops 1 | bytes 1 | tf_op jit(solution)/shard_map/pallas_call | solution.py:42
  47.2 0.6 %collective-permute-done.21.refs_1_ = bf16[64,256]{1,0:T(8,128)(2,1)S(1)} collective-permute-done((bf16[64,256]{1,0:T(8,128)(2,1)S(1)}, bf16[64,256]{1,0:T(8,128)(2,1)S(1)}, u32[]{:S(2)}, u32[]{:S(2)}) %collective-permute-start.21) | collective-permute-done | bytes 32800 | tf_op jit(solution)/shard_map/ppermute | solution.py:60
  47.8 1.2 %shard_map.113 = (bf16[128,1024]{1,0:T(8,128)(2,1)}, bf16[128,1024]{1,0:T(8,128)(2,1)}) custom-call(bf16[256,256]{1,0:T(8,128)(2,1)S(1)} %get-tuple-element.76.refs_0_, bf16[256,256]{1,0:T(8,128)(2,1)S(1)} %collective-permute-done.18.refs_1_, bf16[256,256]{1,0:T(8,128)(2,1)S(1)} %collective-permute-done.20.refs_2_, bf16[128,1024]{1,0:T(8,128)(2,1)S(1)} %bitcast.11, ...), custom_call_target="tpu_custom_call" | custom-call | flops 1 | bytes 1 | tf_op jit(solution)/shard_map/pallas_call | solution.py:42
  49.0 0.7 %shard_map.114 = f32[32,1024]{1,0:T(8,128)} custom-call(bf16[64,256]{1,0:T(8,128)(2,1)S(1)} %get-tuple-element.86.refs_0_, bf16[64,256]{1,0:T(8,128)(2,1)S(1)} %collective-permute-done.22.refs_1_, bf16[64,256]{1,0:T(8,128)(2,1)S(1)} %get-tuple-element.83.refs_7_.refs_2_, bf16[128,1024]{1,0:T(8,128)(2,1)} %get-tuple-element.84.refs_3_), custom_call_target="tpu_custom_call" | custom-call | flops 1 | bytes 1 | tf_op jit(solution)/shard_map/pallas_call | solution.py:42
  (47 shorter events, 1.5 us)
Async XLA Ops:
  0.6 4.6 %copy-start.3 = (bf16[1,128,1024]{2,1,0:T(8,128)(2,1)S(1)}, bf16[1,128,1024]{2,1,0:T(8,128)(2,1)}, u32[]{:S(2)}) copy-start(bf16[1,128,1024]{2,1,0:T(8,128)(2,1)} %param.8) | copy-start | bytes 786436
  0.6 6.6 %copy-start.1 = (bf16[1,128,1024]{2,1,0:T(8,128)(2,1)S(1)}, bf16[1,128,1024]{2,1,0:T(8,128)(2,1)}, u32[]{:S(2)}) copy-start(bf16[1,128,1024]{2,1,0:T(8,128)(2,1)} %param.6) | copy-start | bytes 786436
  0.7 6.6 %copy-start.2 = (bf16[1,128,1024]{2,1,0:T(8,128)(2,1)S(1)}, bf16[1,128,1024]{2,1,0:T(8,128)(2,1)}, u32[]{:S(2)}) copy-start(bf16[1,128,1024]{2,1,0:T(8,128)(2,1)} %param.7) | copy-start | bytes 786436
  0.7 6.6 %copy-start.4 = (bf16[1,128,1024]{2,1,0:T(8,128)(2,1)S(1)}, bf16[1,128,1024]{2,1,0:T(8,128)(2,1)}, u32[]{:S(2)}) copy-start(bf16[1,128,1024]{2,1,0:T(8,128)(2,1)} %param.5) | copy-start | bytes 786436
  2.2 7.4 %collective-permute-start.1 = (bf16[256,256]{1,0:T(8,128)(2,1)S(1)}, bf16[256,256]{1,0:T(8,128)(2,1)S(1)}, u32[]{:S(2)}, u32[]{:S(2)}) collective-permute-start(bf16[256,256]{1,0:T(8,128)(2,1)S(1)} %get-tuple-element.51), channel_id=1, source_target_pairs={{0,2},{1,3},{2,0},{3,1},{4,6},{5,7},{6,4},{7,5},{8,10},{9,11},{10,... | collective-permute-start | bytes 393224 | tf_op jit(solution)/shard_map/ppermute | solution.py:60
  5.3 9.6 %collective-permute-start.6 = (bf16[128,1024]{1,0:T(8,128)(2,1)S(1)}, bf16[128,1024]{1,0:T(8,128)(2,1)S(1)}, u32[]{:S(2)}, u32[]{:S(2)}) collective-permute-start(bf16[128,1024]{1,0:T(8,128)(2,1)S(1)} %bitcast.16), channel_id=1, source_target_pairs={{0,2},{1,3},{2,0},{3,1},{4,6},{5,7},{6,4},{7,5},{8,10},{9,11},{10,... | collective-permute-start | bytes 786440 | tf_op jit(solution)/shard_map/ppermute | solution.py:60
  5.4 13.4 %collective-permute-start.8 = (bf16[2,512,256]{2,1,0:T(8,128)(2,1)S(1)}, bf16[2,512,256]{2,1,0:T(8,128)(2,1)S(1)}, u32[]{:S(2)}, u32[]{:S(2)}) collective-permute-start(bf16[2,512,256]{2,1,0:T(8,128)(2,1)S(1)} %get-tuple-element.53.refs_3_.refs_1_), channel_id=1, source_target_pairs={{0,16},{16,0},{1,17},{17,1},{2,18},{18,2},{3,19},{19,3},{4,20},{20... | collective-permute-start | bytes 1572872 | tf_op jit(solution)/shard_map/ppermute | solution.py:60
  8.6 4.6 %collective-permute-start = (bf16[1024,256]{1,0:T(8,128)(2,1)S(1)}, bf16[1024,256]{1,0:T(8,128)(2,1)S(1)}, u32[]{:S(2)}, u32[]{:S(2)}) collective-permute-start(bf16[1024,256]{1,0:T(8,128)(2,1)S(1)} %get-tuple-element.48.refs_8_), channel_id=1, source_target_pairs={{0,1},{1,0},{2,3},{3,2},{4,5},{5,4},{6,7},{7,6},{8,9},{9,8},{10,11... | collective-permute-start | bytes 1572872 | tf_op jit(solution)/shard_map/ppermute | solution.py:60
  9.6 1.4 %collective-permute-start.2 = (bf16[256,256]{1,0:T(8,128)(2,1)S(1)}, bf16[256,256]{1,0:T(8,128)(2,1)S(1)}, u32[]{:S(2)}, u32[]{:S(2)}) collective-permute-start(bf16[256,256]{1,0:T(8,128)(2,1)S(1)} %shard_map.94.refs_3_), channel_id=1, source_target_pairs={{0,1},{1,0},{2,3},{3,2},{4,5},{5,4},{6,7},{7,6},{8,9},{9,8},{10,11... | collective-permute-start | bytes 393224 | tf_op jit(solution)/shard_map/ppermute | solution.py:60
  11.1 4.6 %collective-permute-start.4 = (bf16[128,256]{1,0:T(8,128)(2,1)S(1)}, bf16[128,256]{1,0:T(8,128)(2,1)S(1)}, u32[]{:S(2)}, u32[]{:S(2)}) collective-permute-start(bf16[128,256]{1,0:T(8,128)(2,1)S(1)} %shard_map.95.refs_2_.refs_0_), channel_id=1, source_target_pairs={{0,4},{1,5},{2,6},{3,7},{4,0},{5,1},{6,2},{7,3},{8,12},{9,13},{10,... | collective-permute-start | bytes 196616 | tf_op jit(solution)/shard_map/ppermute | solution.py:60
  13.3 8.1 %collective-permute-start.3 = (bf16[512,256]{1,0:T(8,128)(2,1)S(1)}, bf16[512,256]{1,0:T(8,128)(2,1)S(1)}, u32[]{:S(2)}, u32[]{:S(2)}) collective-permute-start(bf16[512,256]{1,0:T(8,128)(2,1)S(1)} %shard_map.96.refs_2_), channel_id=1, source_target_pairs={{0,2},{1,3},{2,0},{3,1},{4,6},{5,7},{6,4},{7,5},{8,10},{9,11},{10,... | collective-permute-start | bytes 786440 | tf_op jit(solution)/shard_map/ppermute | solution.py:60
  14.9 4.4 %collective-permute-start.7 = (bf16[128,1024]{1,0:T(8,128)(2,1)S(1)}, bf16[128,1024]{1,0:T(8,128)(2,1)S(1)}, u32[]{:S(2)}, u32[]{:S(2)}) collective-permute-start(bf16[128,1024]{1,0:T(8,128)(2,1)S(1)} %collective-permute-done.6.refs_2_), channel_id=1, source_target_pairs={{0,1},{1,0},{2,3},{3,2},{4,5},{5,4},{6,7},{7,6},{8,9},{9,8},{10,11... | collective-permute-start | bytes 786440 | tf_op jit(solution)/shard_map/ppermute | solution.py:60
  15.7 5.6 %collective-permute-start.5 = (bf16[128,256]{1,0:T(8,128)(2,1)S(1)}, bf16[128,256]{1,0:T(8,128)(2,1)S(1)}, u32[]{:S(2)}, u32[]{:S(2)}) collective-permute-start(bf16[128,256]{1,0:T(8,128)(2,1)S(1)} %shard_map.97.refs_5_), channel_id=1, source_target_pairs={{0,8},{1,9},{2,10},{3,11},{4,12},{5,13},{6,14},{7,15},{8,0},{9,1},... | collective-permute-start | bytes 196616 | tf_op jit(solution)/shard_map/ppermute | solution.py:60
  19.2 11.9 %collective-permute-start.13 = (bf16[2,512,256]{2,1,0:T(8,128)(2,1)S(1)}, bf16[2,512,256]{2,1,0:T(8,128)(2,1)S(1)}, u32[]{:S(2)}, u32[]{:S(2)}) collective-permute-start(bf16[2,512,256]{2,1,0:T(8,128)(2,1)S(1)} %collective-permute-done.8.refs_4_.refs_2_), channel_id=1, source_target_pairs={{0,1},{1,0},{2,3},{3,2},{4,5},{5,4},{6,7},{7,6},{8,9},{9,8},{10,11... | collective-permute-start | bytes 1572872 | tf_op jit(solution)/shard_map/ppermute | solution.py:60
  22.2 14.5 %collective-permute-start.9 = (bf16[512,256]{1,0:T(8,128)(2,1)S(1)}, bf16[512,256]{1,0:T(8,128)(2,1)S(1)}, u32[]{:S(2)}, u32[]{:S(2)}) collective-permute-start(bf16[512,256]{1,0:T(8,128)(2,1)S(1)} %get-tuple-element.57), channel_id=1, source_target_pairs={{0,2},{1,3},{2,0},{3,1},{4,6},{5,7},{6,4},{7,5},{8,10},{9,11},{10,... | collective-permute-start | bytes 786440 | tf_op jit(solution)/shard_map/ppermute | solution.py:60
  24.6 5.0 %collective-permute-start.11 = (bf16[512,128]{1,0:T(8,128)(2,1)S(1)}, bf16[512,128]{1,0:T(8,128)(2,1)S(1)}, u32[]{:S(2)}, u32[]{:S(2)}) collective-permute-start(bf16[512,128]{1,0:T(8,128)(2,1)S(1)} %get-tuple-element.63), channel_id=1, source_target_pairs={{0,16},{16,0},{1,17},{17,1},{2,18},{18,2},{3,19},{19,3},{4,20},{20... | collective-permute-start | bytes 393224 | tf_op jit(solution)/shard_map/ppermute | solution.py:60
  26.1 5.0 %collective-permute-start.12 = (bf16[512,128]{1,0:T(8,128)(2,1)S(1)}, bf16[512,128]{1,0:T(8,128)(2,1)S(1)}, u32[]{:S(2)}, u32[]{:S(2)}) collective-permute-start(bf16[512,128]{1,0:T(8,128)(2,1)S(1)} %get-tuple-element.65.refs_4_), channel_id=1, source_target_pairs={{0,4},{1,5},{2,6},{3,7},{4,0},{5,1},{6,2},{7,3},{8,12},{9,13},{10,... | collective-permute-start | bytes 393224 | tf_op jit(solution)/shard_map/ppermute | solution.py:60
  27.5 5.6 %collective-permute-start.10 = (bf16[128,256]{1,0:T(8,128)(2,1)S(1)}, bf16[128,256]{1,0:T(8,128)(2,1)S(1)}, u32[]{:S(2)}, u32[]{:S(2)}) collective-permute-start(bf16[128,256]{1,0:T(8,128)(2,1)S(1)} %get-tuple-element.58.refs_3_.refs_0_), channel_id=1, source_target_pairs={{0,4},{1,5},{2,6},{3,7},{4,0},{5,1},{6,2},{7,3},{8,12},{9,13},{10,... | collective-permute-start | bytes 196616 | tf_op jit(solution)/shard_map/ppermute | solution.py:60
  31.1 5.7 %collective-permute-start.16 = (bf16[256,128]{1,0:T(8,128)(2,1)S(1)}, bf16[256,128]{1,0:T(8,128)(2,1)S(1)}, u32[]{:S(2)}, u32[]{:S(2)}) collective-permute-start(bf16[256,128]{1,0:T(8,128)(2,1)S(1)} %get-tuple-element.71), channel_id=1, source_target_pairs={{0,4},{1,5},{2,6},{3,7},{4,0},{5,1},{6,2},{7,3},{8,12},{9,13},{10,... | collective-permute-start | bytes 196616 | tf_op jit(solution)/shard_map/ppermute | solution.py:60
  32.6 4.3 %collective-permute-start.17 = (bf16[256,128]{1,0:T(8,128)(2,1)S(1)}, bf16[256,128]{1,0:T(8,128)(2,1)S(1)}, u32[]{:S(2)}, u32[]{:S(2)}) collective-permute-start(bf16[256,128]{1,0:T(8,128)(2,1)S(1)} %get-tuple-element.67.refs_2_), channel_id=1, source_target_pairs={{0,16},{16,0},{1,17},{17,1},{2,18},{18,2},{3,19},{19,3},{4,20},{20... | collective-permute-start | bytes 196616 | tf_op jit(solution)/shard_map/ppermute | solution.py:60
  33.2 7.3 %collective-permute-start.15 = (bf16[128,256]{1,0:T(8,128)(2,1)S(1)}, bf16[128,256]{1,0:T(8,128)(2,1)S(1)}, u32[]{:S(2)}, u32[]{:S(2)}) collective-permute-start(bf16[128,256]{1,0:T(8,128)(2,1)S(1)} %shard_map.104.refs_2_), channel_id=1, source_target_pairs={{0,8},{1,9},{2,10},{3,11},{4,12},{5,13},{6,14},{7,15},{8,0},{9,1},... | collective-permute-start | bytes 196616 | tf_op jit(solution)/shard_map/ppermute | solution.py:60
  36.7 4.4 %collective-permute-start.14 = (bf16[512,256]{1,0:T(8,128)(2,1)S(1)}, bf16[512,256]{1,0:T(8,128)(2,1)S(1)}, u32[]{:S(2)}, u32[]{:S(2)}) collective-permute-start(bf16[512,256]{1,0:T(8,128)(2,1)S(1)} %shard_map.105.refs_4_), channel_id=1, source_target_pairs={{0,1},{1,0},{2,3},{3,2},{4,5},{5,4},{6,7},{7,6},{8,9},{9,8},{10,11... | collective-permute-start | bytes 786440 | tf_op jit(solution)/shard_map/ppermute | solution.py:60
  36.9 6.9 %collective-permute-start.19 = (bf16[128,256]{1,0:T(8,128)(2,1)S(1)}, bf16[128,256]{1,0:T(8,128)(2,1)S(1)}, u32[]{:S(2)}, u32[]{:S(2)}) collective-permute-start(bf16[128,256]{1,0:T(8,128)(2,1)S(1)} %get-tuple-element.73.refs_3_), channel_id=1, source_target_pairs={{0,8},{1,9},{2,10},{3,11},{4,12},{5,13},{6,14},{7,15},{8,0},{9,1},... | collective-permute-start | bytes 196616 | tf_op jit(solution)/shard_map/ppermute | solution.py:60
  40.6 5.0 %collective-permute-start.18 = (bf16[256,256]{1,0:T(8,128)(2,1)S(1)}, bf16[256,256]{1,0:T(8,128)(2,1)S(1)}, u32[]{:S(2)}, u32[]{:S(2)}) collective-permute-start(bf16[256,256]{1,0:T(8,128)(2,1)S(1)} %get-tuple-element.74.refs_10_), channel_id=1, source_target_pairs={{0,2},{1,3},{2,0},{3,1},{4,6},{5,7},{6,4},{7,5},{8,10},{9,11},{10,... | collective-permute-start | bytes 393224 | tf_op jit(solution)/shard_map/ppermute | solution.py:60
  43.8 1.9 %copy-start = (bf16[512,1024]{1,0:T(8,128)(2,1)S(1)}, bf16[512,1024]{1,0:T(8,128)(2,1)}, u32[]{:S(2)}) copy-start(bf16[512,1024]{1,0:T(8,128)(2,1)} %refs_1_.1) | copy-start | bytes 3145732
  43.8 4.0 %collective-permute-start.21 = (bf16[64,256]{1,0:T(8,128)(2,1)S(1)}, bf16[64,256]{1,0:T(8,128)(2,1)S(1)}, u32[]{:S(2)}, u32[]{:S(2)}) collective-permute-start(bf16[64,256]{1,0:T(8,128)(2,1)S(1)} %get-tuple-element.78.refs_2_), channel_id=1, source_target_pairs={{0,2},{1,3},{2,0},{3,1},{4,6},{5,7},{6,4},{7,5},{8,10},{9,11},{10,... | collective-permute-start | bytes 98312 | tf_op jit(solution)/shard_map/ppermute | solution.py:60
  45.6 2.2 %collective-permute-start.20 = (bf16[256,256]{1,0:T(8,128)(2,1)S(1)}, bf16[256,256]{1,0:T(8,128)(2,1)S(1)}, u32[]{:S(2)}, u32[]{:S(2)}) collective-permute-start(bf16[256,256]{1,0:T(8,128)(2,1)S(1)} %shard_map.110.refs_4_.refs_2_), channel_id=1, source_target_pairs={{0,1},{1,0},{2,3},{3,2},{4,5},{5,4},{6,7},{7,6},{8,9},{9,8},{10,11... | collective-permute-start | bytes 393224 | tf_op jit(solution)/shard_map/ppermute | solution.py:60
  47.8 1.2 %collective-permute-start.22 = (bf16[64,256]{1,0:T(8,128)(2,1)S(1)}, bf16[64,256]{1,0:T(8,128)(2,1)S(1)}, u32[]{:S(2)}, u32[]{:S(2)}) collective-permute-start(bf16[64,256]{1,0:T(8,128)(2,1)S(1)} %get-tuple-element.83.refs_7_.refs_2_), channel_id=1, source_target_pairs={{0,1},{1,0},{2,3},{3,2},{4,5},{5,4},{6,7},{7,6},{8,9},{9,8},{10,11... | collective-permute-start | bytes 98312 | tf_op jit(solution)/shard_map/ppermute | solution.py:60

commit v16 on v14

--- a/solution.py
+++ b/solution.py
@@ -231,43 +231,48 @@
     return near_ref.at[first], core_ref.at[first], far_ref.at[first], core_ref.at[second]
 
 
-def late_kernel(*refs):
-    backs, (q_ref, k_ref, v_ref, attend_ref, own_ref, message_ref, far_ref) = arrived(*refs[:3]), refs[3:10]
-    gq_ref, gk_ref, gv_ref, normed_ref = refs[10:]
-    block, width = q_ref.shape[0], refs[0].shape[1]
+def late_kernel(near_ref, far_ref, core_ref, q_ref, k_ref, v_ref, attend_ref, gq_ref, gk_ref, gv_ref):
+    backs = arrived(near_ref, far_ref, core_ref)
+    block, width = q_ref.shape[0], near_ref.shape[1]
     mask = causal(block)
-    withins = (own_ref.at[part(1, block)], message_ref.at[part(1, block)],
-               far_ref.at[part(1, block)], message_ref.at[part(3, block)])
     for r in range(SLAB):
         at = cut(member(r), width)
         q, k, v = q_ref[:, at], k_ref[:, at], v_ref[:, at]
-        normeds, gqs, gks, gvs = [], [], [], []
+        gqs, gks, gvs = [], [], []
         for h in range(width // DH):
             dmixed, prior = backs[r][:block, head(h)], backs[r][block:, head(h)]
-            mixed = withins[r][:, head(h)].astype(F32) + dot(q[:, head(h)], prior, 1, 0)
-            scale = lax.rsqrt(jnp.mean(mixed * mixed, axis=-1, keepdims=True) + EPSILON)
-            normeds.append(mixed * scale)
             back = jnp.where(mask, dot(dmixed, v[:, head(h)], 1, 1), 0.0).astype(BF16)
             gqs.append(dot(back, k[:, head(h)], 1, 0) + dot(dmixed, prior, 1, 1))
             gks.append(dot(back, q[:, head(h)], 0, 0))
             gvs.append(dot(attend_ref[r, h], dmixed, 0, 0))
-        normed_ref[:, at] = jnp.concatenate(normeds, axis=1).astype(BF16)
         gq_ref[:, at] = jnp.concatenate(gqs, axis=1).astype(BF16)
         gk_ref[r] = jnp.concatenate(gks, axis=1)
         gv_ref[r] = jnp.concatenate(gvs, axis=1)
 
 
-def output_kernel(normed_ref, weight_ref, *refs):
-    *far, out_ref = refs
-    width = normed_ref.shape[1] // SLAB
+def output_kernel(near_ref, back_far, core_ref, q_ref, own_ref, message_ref, far_ref, weight_ref, *refs):
+    *far, out_ref, normed_ref = refs
+    backs = arrived(near_ref, back_far, core_ref)
+    block, width = q_ref.shape[0], near_ref.shape[1]
     rows = weight_ref.shape[0]
     me = lax.axis_index("dp")
+    withins = (own_ref.at[part(1, block)], message_ref.at[part(1, block)],
+               far_ref.at[part(1, block)], message_ref.at[part(3, block)])
+    totals = [jnp.zeros((block, rows), F32)] * (len(far) // 2)
+    for r in range(SLAB):
+        at = cut(member(r), width)
+        q = q_ref[:, at]
+        normeds = []
+        for h in range(width // DH):
+            mixed = withins[r][:, head(h)].astype(F32) + dot(q[:, head(h)], backs[r][block:, head(h)], 1, 0)
+            scale = lax.rsqrt(jnp.mean(mixed * mixed, axis=-1, keepdims=True) + EPSILON)
+            normeds.append(mixed * scale)
+        normed = jnp.concatenate(normeds, axis=1).astype(BF16)
+        normed_ref[:, at] = normed
+        for j in range(len(totals)):
+            totals[j] = totals[j] + dot(normed, far[2 * j + r % 2][r // 2], 1, 1)
     out_ref[:, cut(me, rows)] = dot(normed_ref[...], weight_ref[...], 1, 1).astype(BF16)
-    for j in range(1, len(far) // 2 + 1):
-        total = jnp.zeros((normed_ref.shape[0], rows), F32)
-        for r in range(SLAB):
-            normed = normed_ref[:, cut(member(r), width)]
-            total = total + dot(normed, far[2 * (j - 1) + r % 2][r // 2], 1, 1)
+    for j, total in enumerate(totals, 1):
         out_ref[:, cut(jnp.bitwise_xor(me, j), rows)] = total.astype(BF16)
 
 
@@ -416,43 +421,44 @@
         )
         got = flip(send, "dp", dp, 1)
     back_far = near(back_far, bits=2)
-    behind, last_u = doubling(slab_u, 15 * 10**8)
     if tuned:
         keep, send = call(
             split_kernel, [((2 * piece, width), F32), ((2 * piece, width), BF16)], keep, got, wait=w_all[1::2]
         )
         got = near(send, bits=SLAB)
+    behind, last_u = doubling(slab_u, 10**9)
     (send,) = call(relay_kernel, [((2 * rows + 2 * DH, width), BF16)], back, back_far)
     back_core = near(send, bits=1)
+    if tuned:
+        keep, send = call(
+            split_again_kernel, [((piece, width), F32), ((piece, width), BF16)], keep, got, cost=3 * 10**9
+        )
+        got = near(send, bits=2 * SLAB)
     later, later_far = call(
-        later_kernel, [((2 * DH, width), BF16)] * 2, *behind, u, cost=2 * 10**9,
+        later_kernel, [((2 * DH, width), BF16)] * 2, *behind, u,
         scratch=[pltpu.VMEM((SLAB, DH, width), F32)],
     )
     later_far = near(later_far, bits=2)
-    if tuned:
-        keep, send = call(
-            split_again_kernel, [((piece, width), F32), ((piece, width), BF16)], keep, got, cost=2 * 10**9
-        )
-        got = near(send, bits=2 * SLAB)
-    gq, gk_part, gv_part, own_normed = call(
+    gq, gk_part, gv_part = call(
         late_kernel,
-        [((rows, features), BF16), ((SLAB, rows, width), F32), ((SLAB, rows, width), F32), ((rows, features), BF16)],
-        back, back_far, back_core, q, k, v, attend, own_tokens, *sent,
-    )
-    (send,) = call(relay_kernel, [((2 * DH, width), BF16)], later, later_far)
-    later_core = near(send, bits=1)
+        [((rows, features), BF16), ((SLAB, rows, width), F32), ((SLAB, rows, width), F32)],
+        back, back_far, back_core, q, k, v, attend,
+    )
     if tuned:
         keep, share = call(
             share_kernel, [((piece // 2, width), BF16)] * 2, keep, got, cost=3 * 10**9,
             scratch=[pltpu.VMEM((piece, width), F32)],
         )
         got = near(share, bits=2)
-    (output,) = call(
-        output_kernel, [((rows, outputs), BF16)], own_normed, out_weight, *w_all, end=True,
+    (send,) = call(relay_kernel, [((2 * DH, width), BF16)], later, later_far)
+    later_core = near(send, bits=1)
+    output, own_normed = call(
+        output_kernel, [((rows, outputs), BF16), ((rows, features), BF16)],
+        back, back_far, back_core, q, own_tokens, *sent, out_weight, *w_all, end=True,
     )
     if tuned:
         keep, share = call(
-            pass_kernel, [((piece // 2, width), BF16)] * 2, keep, got,
+            pass_kernel, [((piece // 2, width), BF16)] * 2, keep, got, cost=3 * 10**9,
             wait=[pltpu.with_memory_space_constraint(x, pltpu.HBM) for x in (output,)],
         )
         got = near(share, bits=1)

time: 48.5 us -> 48.2 us (level)
  transfers between devices with their start and end apart: 21 -> 21, of which waited for: 12 -> 10; matrix products, arithmetic and copies ran while one was open for 0% -> 0% of each run, Pallas kernels for 19% -> 19%
where the time goes in v16:
time: 48.2 us; the launch traced here: 48 us
  starting transfers between devices  25.8 us (54%)
  Pallas kernels  11.5 us (24%)
  waiting for transfers between devices  9.89 us (21%)
  between operations  0.83 us (2%)
    ppermute x21, starting transfers between devices, flip(): return lax.ppermute(x, axis, [(i, i ^ bits) for i in range(count)])  25.8 us
    pallas_call x23, Pallas kernels, __call__(): pl.pallas_call(inner, out_shape=[jax.ShapeDtypeStruct(s, d) for s, d in o...  11.5 us
    ppermute x21, waiting for transfers between devices, flip(): return lax.ppermute(x, axis, [(i, i ^ bits) for i in range(count)])  9.89 us
  transfers between devices with their start and end apart: 21, of which 10 were waited for; matrix products, arithmetic and copies ran while one was open for 0% of the time, Pallas kernels for 19%

profile of v16, /device:TPU:0, one launch (start us, length us, event | category | flops | bytes accessed | tf_op | source)
XLA Modules:
  0.0 48.0 jit_solution(8595493114931159726)
XLA Ops:
  0.7 1.6 %shard_map.92 = (f32[128,256]{1,0:T(8,128)S(1)}, bf16[128,256]{1,0:T(8,128)(2,1)S(1)}, bf16[256,256]{1,0:T(8,128)(2,1)S(1)}, bf16[2,512,256]{2,1,0:T(8,128)(2,1)S(1)}) custom-call(bf16[128,1024]{1,0:T(8,128)(2,1)} %bitcast.8, bf16[128,1024]{1,0:T(8,128)(2,1)} %bitcast.12, bf16[512,1024]{1,0:T(8,128)(2,1)} %refs_7_.1), custom_call_target="tpu_custom_call" | custom-call | flops 1 | bytes 1 | tf_op jit(solution)/shard_map/pallas_call | solution.py:42
  2.2 3.0 %collective-permute-start.1 = (bf16[256,256]{1,0:T(8,128)(2,1)S(1)}, bf16[256,256]{1,0:T(8,128)(2,1)S(1)}, u32[]{:S(2)}, u32[]{:S(2)}) collective-permute-start(bf16[256,256]{1,0:T(8,128)(2,1)S(1)} %get-tuple-element.47), channel_id=1, source_target_pairs={{0,2},{1,3},{2,0},{3,1},{4,6},{5,7},{6,4},{7,5},{8,10},{9,11},{10,... | collective-permute-start | bytes 393224 | tf_op jit(solution)/shard_map/ppermute | solution.py:60
  5.4 1.9 %collective-permute-start.8 = (bf16[2,512,256]{2,1,0:T(8,128)(2,1)S(1)}, bf16[2,512,256]{2,1,0:T(8,128)(2,1)S(1)}, u32[]{:S(2)}, u32[]{:S(2)}) collective-permute-start(bf16[2,512,256]{2,1,0:T(8,128)(2,1)S(1)} %get-tuple-element.49.refs_3_.refs_1_), channel_id=1, source_target_pairs={{0,16},{16,0},{1,17},{17,1},{2,18},{18,2},{3,19},{19,3},{4,20},{20... | collective-permute-start | bytes 1572872 | tf_op jit(solution)/shard_map/ppermute | solution.py:60
  7.3 1.4 %shard_map.93 = (bf16[4,2,128,128]{3,2,1,0:T(8,128)(2,1)S(1)}, bf16[256,256]{1,0:T(8,128)(2,1)S(1)}, bf16[1024,256]{1,0:T(8,128)(2,1)S(1)}, bf16[256,256]{1,0:T(8,128)(2,1)S(1)}) custom-call(bf16[128,1024]{1,0:T(8,128)(2,1)S(1)} %bitcast.16, bf16[128,1024]{1,0:T(8,128)(2,1)S(1)} %bitcast.9, bf16[128,1024]{1,0:T(8,128)(2,1)S(1)} %bitcast.13, ...), custom_call_target="tpu_custom_call" | custom-call | flops 1 | bytes 1 | tf_op jit(solution)/shard_map/pallas_call | solution.py:42
  8.7 0.9 %collective-permute-done.1.refs_1_.refs_4_ = bf16[256,256]{1,0:T(8,128)(2,1)S(1)} collective-permute-done((bf16[256,256]{1,0:T(8,128)(2,1)S(1)}, bf16[256,256]{1,0:T(8,128)(2,1)S(1)}, u32[]{:S(2)}, u32[]{:S(2)}) %collective-permute-start.1) | collective-permute-done | bytes 131104 | tf_op jit(solution)/shard_map/ppermute | solution.py:60
  9.7 1.3 %collective-permute-done.2.refs_2_.refs_5_ = bf16[256,256]{1,0:T(8,128)(2,1)S(1)} collective-permute-done((bf16[256,256]{1,0:T(8,128)(2,1)S(1)}, bf16[256,256]{1,0:T(8,128)(2,1)S(1)}, u32[]{:S(2)}, u32[]{:S(2)}) %collective-permute-start.2) | collective-permute-done | bytes 131104 | tf_op jit(solution)/shard_map/ppermute | solution.py:60
  11.1 2.2 %collective-permute-start.4 = (bf16[128,256]{1,0:T(8,128)(2,1)S(1)}, bf16[128,256]{1,0:T(8,128)(2,1)S(1)}, u32[]{:S(2)}, u32[]{:S(2)}) collective-permute-start(bf16[128,256]{1,0:T(8,128)(2,1)S(1)} %shard_map.95.refs_2_.refs_0_), channel_id=1, source_target_pairs={{0,4},{1,5},{2,6},{3,7},{4,0},{5,1},{6,2},{7,3},{8,12},{9,13},{10,... | collective-permute-start | bytes 196616 | tf_op jit(solution)/shard_map/ppermute | solution.py:60
  13.3 1.6 %collective-permute-start.3 = (bf16[512,256]{1,0:T(8,128)(2,1)S(1)}, bf16[512,256]{1,0:T(8,128)(2,1)S(1)}, u32[]{:S(2)}, u32[]{:S(2)}) collective-permute-start(bf16[512,256]{1,0:T(8,128)(2,1)S(1)} %shard_map.96.refs_2_), channel_id=1, source_target_pairs={{0,2},{1,3},{2,0},{3,1},{4,6},{5,7},{6,4},{7,5},{8,10},{9,11},{10,... | collective-permute-start | bytes 786440 | tf_op jit(solution)/shard_map/ppermute | solution.py:60
  14.9 0.8 %collective-permute-done.4.refs_1_.refs_0_ = bf16[128,256]{1,0:T(8,128)(2,1)S(1)} collective-permute-done((bf16[128,256]{1,0:T(8,128)(2,1)S(1)}, bf16[128,256]{1,0:T(8,128)(2,1)S(1)}, u32[]{:S(2)}, u32[]{:S(2)}) %collective-permute-start.4) | collective-permute-done | bytes 65568 | tf_op jit(solution)/shard_map/ppermute | solution.py:60
  15.7 2.9 %collective-permute-start.5 = (bf16[128,256]{1,0:T(8,128)(2,1)S(1)}, bf16[128,256]{1,0:T(8,128)(2,1)S(1)}, u32[]{:S(2)}, u32[]{:S(2)}) collective-permute-start(bf16[128,256]{1,0:T(8,128)(2,1)S(1)} %shard_map.97.refs_5_), channel_id=1, source_target_pairs={{0,8},{1,9},{2,10},{3,11},{4,12},{5,13},{6,14},{7,15},{8,0},{9,1},... | collective-permute-start | bytes 196616 | tf_op jit(solution)/shard_map/ppermute | solution.py:60
  18.7 0.4 shard_map.98
  19.3 0.2 shard_map.99
  19.5 1.7 %collective-permute-done.5.refs_1_ = bf16[128,256]{1,0:T(8,128)(2,1)S(1)} collective-permute-done((bf16[128,256]{1,0:T(8,128)(2,1)S(1)}, bf16[128,256]{1,0:T(8,128)(2,1)S(1)}, u32[]{:S(2)}, u32[]{:S(2)}) %collective-permute-start.5) | collective-permute-done | bytes 65568 | tf_op jit(solution)/shard_map/ppermute | solution.py:60
  21.4 0.8 %shard_map.101 = (bf16[4,128,256]{2,1,0:T(8,128)(2,1)S(1)}, bf16[512,256]{1,0:T(8,128)(2,1)S(1)}, bf16[512,256]{1,0:T(8,128)(2,1)S(1)}, f32[4,128,256]{2,1,0:T(8,128)S(1)}, bf16[128,256]{1,0:T(8,128)(2,1)S(1)}) custom-call(bf16[256,256]{1,0:T(8,128)(2,1)S(1)} %get-tuple-element.43.refs_0_.refs_4_, ...), custom_call_target="tpu_custom_call" | custom-call | flops 10000000000 | bytes 1 | tf_op jit(solution)/shard_map/pallas_call | solution.py:42
  22.2 0.8 %shard_map.102 = (f32[512,256]{1,0:T(8,128)S(1)}, bf16[512,256]{1,0:T(8,128)(2,1)S(1)}) custom-call(bf16[3,128,1024]{2,1,0:T(8,128)(2,1)S(1)} %get-tuple-element.55.refs_0_, bf16[1,128,1024]{2,1,0:T(8,128)(2,1)S(1)} %get-tuple-element.56.refs_1_, bf16[4,128,256]{2,1,0:T(8,128)(2,1)S(1)} %get-tuple-element.57.refs_2_, ...), custom_call_target="tpu_custom_call" | custom-call | flops 1 | bytes 1 | tf_op jit(solution)/shard_map/pallas_call | solution.py:42
  23.0 1.6 %collective-permute-start.11 = (bf16[512,256]{1,0:T(8,128)(2,1)S(1)}, bf16[512,256]{1,0:T(8,128)(2,1)S(1)}, u32[]{:S(2)}, u32[]{:S(2)}) collective-permute-start(bf16[512,256]{1,0:T(8,128)(2,1)S(1)} %get-tuple-element.59.refs_2_), channel_id=1, source_target_pairs={{0,16},{16,0},{1,17},{17,1},{2,18},{18,2},{3,19},{19,3},{4,20},{20... | collective-permute-start | bytes 786440 | tf_op jit(solution)/shard_map/ppermute | solution.py:60
  24.5 1.5 %collective-permute-start.9 = (bf16[512,256]{1,0:T(8,128)(2,1)S(1)}, bf16[512,256]{1,0:T(8,128)(2,1)S(1)}, u32[]{:S(2)}, u32[]{:S(2)}) collective-permute-start(bf16[512,256]{1,0:T(8,128)(2,1)S(1)} %get-tuple-element.53), channel_id=1, source_target_pairs={{0,2},{1,3},{2,0},{3,1},{4,6},{5,7},{6,4},{7,5},{8,10},{9,11},{10,... | collective-permute-start | bytes 786440 | tf_op jit(solution)/shard_map/ppermute | solution.py:60
  26.1 1.4 %collective-permute-start.10 = (bf16[128,256]{1,0:T(8,128)(2,1)S(1)}, bf16[128,256]{1,0:T(8,128)(2,1)S(1)}, u32[]{:S(2)}, u32[]{:S(2)}) collective-permute-start(bf16[128,256]{1,0:T(8,128)(2,1)S(1)} %get-tuple-element.54.refs_3_.refs_0_), channel_id=1, source_target_pairs={{0,4},{1,5},{2,6},{3,7},{4,0},{5,1},{6,2},{7,3},{8,12},{9,13},{10,... | collective-permute-start | bytes 196616 | tf_op jit(solution)/shard_map/ppermute | solution.py:60
  27.5 2.8 %collective-permute-done.11.refs_1_ = bf16[512,256]{1,0:T(8,128)(2,1)S(1)} collective-permute-done((bf16[512,256]{1,0:T(8,128)(2,1)S(1)}, bf16[512,256]{1,0:T(8,128)(2,1)S(1)}, u32[]{:S(2)}, u32[]{:S(2)}) %collective-permute-start.11) | collective-permute-done | bytes 262176 | tf_op jit(solution)/shard_map/ppermute | solution.py:60
  30.3 1.4 %collective-permute-start.15 = (bf16[256,256]{1,0:T(8,128)(2,1)S(1)}, bf16[256,256]{1,0:T(8,128)(2,1)S(1)}, u32[]{:S(2)}, u32[]{:S(2)}) collective-permute-start(bf16[256,256]{1,0:T(8,128)(2,1)S(1)} %get-tuple-element.61.refs_2_), channel_id=1, source_target_pairs={{0,4},{1,5},{2,6},{3,7},{4,0},{5,1},{6,2},{7,3},{8,12},{9,13},{10,... | collective-permute-start | bytes 393224 | tf_op jit(solution)/shard_map/ppermute | solution.py:60
  31.8 2.7 %collective-permute-start.14 = (bf16[128,256]{1,0:T(8,128)(2,1)S(1)}, bf16[128,256]{1,0:T(8,128)(2,1)S(1)}, u32[]{:S(2)}, u32[]{:S(2)}) collective-permute-start(bf16[128,256]{1,0:T(8,128)(2,1)S(1)} %shard_map.104.refs_2_), channel_id=1, source_target_pairs={{0,8},{1,9},{2,10},{3,11},{4,12},{5,13},{6,14},{7,15},{8,0},{9,1},... | collective-permute-start | bytes 196616 | tf_op jit(solution)/shard_map/ppermute | solution.py:60
  34.5 0.8 %collective-permute-done.15.refs_1_ = bf16[256,256]{1,0:T(8,128)(2,1)S(1)} collective-permute-done((bf16[256,256]{1,0:T(8,128)(2,1)S(1)}, bf16[256,256]{1,0:T(8,128)(2,1)S(1)}, u32[]{:S(2)}, u32[]{:S(2)}) %collective-permute-start.15) | collective-permute-done | bytes 131104 | tf_op jit(solution)/shard_map/ppermute | solution.py:60
  35.4 2.7 %collective-permute-start.17 = (bf16[128,256]{1,0:T(8,128)(2,1)S(1)}, bf16[128,256]{1,0:T(8,128)(2,1)S(1)}, u32[]{:S(2)}, u32[]{:S(2)}) collective-permute-start(bf16[128,256]{1,0:T(8,128)(2,1)S(1)} %get-tuple-element.64.refs_3_), channel_id=1, source_target_pairs={{0,8},{1,9},{2,10},{3,11},{4,12},{5,13},{6,14},{7,15},{8,0},{9,1},... | collective-permute-start | bytes 196616 | tf_op jit(solution)/shard_map/ppermute | solution.py:60
  38.2 1.6 %collective-permute-start.16 = (bf16[256,256]{1,0:T(8,128)(2,1)S(1)}, bf16[256,256]{1,0:T(8,128)(2,1)S(1)}, u32[]{:S(2)}, u32[]{:S(2)}) collective-permute-start(bf16[256,256]{1,0:T(8,128)(2,1)S(1)} %get-tuple-element.66.refs_7_), channel_id=1, source_target_pairs={{0,2},{1,3},{2,0},{3,1},{4,6},{5,7},{6,4},{7,5},{8,10},{9,11},{10,... | collective-permute-start | bytes 393224 | tf_op jit(solution)/shard_map/ppermute | solution.py:60
  39.7 2.1 %shard_map.108 = (bf16[128,1024]{1,0:T(8,128)(2,1)}, f32[4,128,256]{2,1,0:T(8,128)S(1)}, f32[4,128,256]{2,1,0:T(8,128)S(1)}) custom-call(bf16[512,256]{1,0:T(8,128)(2,1)S(1)} %get-tuple-element.52.refs_0_, bf16[512,256]{1,0:T(8,128)(2,1)S(1)} %collective-permute-done.9.refs_1_, bf16[512,256]{1,0:T(8,128)(2,1)S(1)} %collective-permute-done.13.refs_2_, ...), custom_call_target="tpu_custom_call" | custom-call | flops 1 | bytes 1 | tf_op jit(solution)/shard_map/pallas_call | solution.py:42
  41.9 0.6 %collective-permute-start.19 = (bf16[64,256]{1,0:T(8,128)(2,1)S(1)}, bf16[64,256]{1,0:T(8,128)(2,1)S(1)}, u32[]{:S(2)}, u32[]{:S(2)}) collective-permute-start(bf16[64,256]{1,0:T(8,128)(2,1)S(1)} %get-tuple-element.70.refs_2_), channel_id=1, source_target_pairs={{0,2},{1,3},{2,0},{3,1},{4,6},{5,7},{6,4},{7,5},{8,10},{9,11},{10,... | collective-permute-start | bytes 98312 | tf_op jit(solution)/shard_map/ppermute | solution.py:60
  42.4 1.0 %collective-permute-done.16.refs_1_ = bf16[256,256]{1,0:T(8,128)(2,1)S(1)} collective-permute-done((bf16[256,256]{1,0:T(8,128)(2,1)S(1)}, bf16[256,256]{1,0:T(8,128)(2,1)S(1)}, u32[]{:S(2)}, u32[]{:S(2)}) %collective-permute-start.16) | collective-permute-done | bytes 131104 | tf_op jit(solution)/shard_map/ppermute | solution.py:60
  43.6 2.1 %shard_map.111 = (bf16[128,1024]{1,0:T(8,128)(2,1)}, bf16[128,1024]{1,0:T(8,128)(2,1)}) custom-call(bf16[512,256]{1,0:T(8,128)(2,1)S(1)} %get-tuple-element.52.refs_0_, bf16[512,256]{1,0:T(8,128)(2,1)S(1)} %collective-permute-done.9.refs_1_, bf16[512,256]{1,0:T(8,128)(2,1)S(1)} %collective-permute-done.13.refs_2_, bf16[128,1024]{1,0:T(8,128)(2,1)S(1)} %bitcast.18, ...), custom_call_target="tpu_custom_call" | custom-call | flops 1 | bytes 1 | tf_op jit(solution)/shard_map/pallas_call | solution.py:42
  45.6 0.2 collective-permute-done.19.refs_1_
  45.8 0.4 collective-permute-start.20
  46.2 1.1 %shard_map.113 = (bf16[128,1024]{1,0:T(8,128)(2,1)}, bf16[128,1024]{1,0:T(8,128)(2,1)}) custom-call(bf16[256,256]{1,0:T(8,128)(2,1)S(1)} %get-tuple-element.65.refs_0_, bf16[256,256]{1,0:T(8,128)(2,1)S(1)} %collective-permute-done.16.refs_1_, bf16[256,256]{1,0:T(8,128)(2,1)S(1)} %collective-permute-done.18.refs_2_, bf16[128,1024]{1,0:T(8,128)(2,1)S(1)} %bitcast.11, ...), custom_call_target="tpu_custom_call" | custom-call | flops 1 | bytes 1 | tf_op jit(solution)/shard_map/pallas_call | solution.py:42
  47.4 0.7 %shard_map.114 = f32[32,1024]{1,0:T(8,128)} custom-call(bf16[64,256]{1,0:T(8,128)(2,1)S(1)} %get-tuple-element.78.refs_0_, bf16[64,256]{1,0:T(8,128)(2,1)S(1)} %collective-permute-done.20.refs_1_, bf16[64,256]{1,0:T(8,128)(2,1)S(1)} %get-tuple-element.75.refs_7_.refs_2_, bf16[128,1024]{1,0:T(8,128)(2,1)} %get-tuple-element.76.refs_3_), custom_call_target="tpu_custom_call" | custom-call | flops 1 | bytes 1 | tf_op jit(solution)/shard_map/pallas_call | solution.py:42
  (43 shorter events, 1.2 us)
Async XLA Ops:
  0.6 4.6 %copy-start.4 = (bf16[1,128,1024]{2,1,0:T(8,128)(2,1)S(1)}, bf16[1,128,1024]{2,1,0:T(8,128)(2,1)}, u32[]{:S(2)}) copy-start(bf16[1,128,1024]{2,1,0:T(8,128)(2,1)} %param.8) | copy-start | bytes 786436
  0.6 6.6 %copy-start = (bf16[1,128,1024]{2,1,0:T(8,128)(2,1)S(1)}, bf16[1,128,1024]{2,1,0:T(8,128)(2,1)}, u32[]{:S(2)}) copy-start(bf16[1,128,1024]{2,1,0:T(8,128)(2,1)} %param.6) | copy-start | bytes 786436
  0.7 6.6 %copy-start.1 = (bf16[1,128,1024]{2,1,0:T(8,128)(2,1)S(1)}, bf16[1,128,1024]{2,1,0:T(8,128)(2,1)}, u32[]{:S(2)}) copy-start(bf16[1,128,1024]{2,1,0:T(8,128)(2,1)} %param.7) | copy-start | bytes 786436
  0.7 6.6 %copy-start.3 = (bf16[1,128,1024]{2,1,0:T(8,128)(2,1)S(1)}, bf16[1,128,1024]{2,1,0:T(8,128)(2,1)}, u32[]{:S(2)}) copy-start(bf16[1,128,1024]{2,1,0:T(8,128)(2,1)} %param.5) | copy-start | bytes 786436
  2.2 7.4 %collective-permute-start.1 = (bf16[256,256]{1,0:T(8,128)(2,1)S(1)}, bf16[256,256]{1,0:T(8,128)(2,1)S(1)}, u32[]{:S(2)}, u32[]{:S(2)}) collective-permute-start(bf16[256,256]{1,0:T(8,128)(2,1)S(1)} %get-tuple-element.47), channel_id=1, source_target_pairs={{0,2},{1,3},{2,0},{3,1},{4,6},{5,7},{6,4},{7,5},{8,10},{9,11},{10,... | collective-permute-start | bytes 393224 | tf_op jit(solution)/shard_map/ppermute | solution.py:60
  5.3 9.6 %collective-permute-start.6 = (bf16[128,1024]{1,0:T(8,128)(2,1)S(1)}, bf16[128,1024]{1,0:T(8,128)(2,1)S(1)}, u32[]{:S(2)}, u32[]{:S(2)}) collective-permute-start(bf16[128,1024]{1,0:T(8,128)(2,1)S(1)} %bitcast.19), channel_id=1, source_target_pairs={{0,2},{1,3},{2,0},{3,1},{4,6},{5,7},{6,4},{7,5},{8,10},{9,11},{10,... | collective-permute-start | bytes 786440 | tf_op jit(solution)/shard_map/ppermute | solution.py:60
  5.4 13.4 %collective-permute-start.8 = (bf16[2,512,256]{2,1,0:T(8,128)(2,1)S(1)}, bf16[2,512,256]{2,1,0:T(8,128)(2,1)S(1)}, u32[]{:S(2)}, u32[]{:S(2)}) collective-permute-start(bf16[2,512,256]{2,1,0:T(8,128)(2,1)S(1)} %get-tuple-element.49.refs_3_.refs_1_), channel_id=1, source_target_pairs={{0,16},{16,0},{1,17},{17,1},{2,18},{18,2},{3,19},{19,3},{4,20},{20... | collective-permute-start | bytes 1572872 | tf_op jit(solution)/shard_map/ppermute | solution.py:60
  8.6 4.6 %collective-permute-start = (bf16[1024,256]{1,0:T(8,128)(2,1)S(1)}, bf16[1024,256]{1,0:T(8,128)(2,1)S(1)}, u32[]{:S(2)}, u32[]{:S(2)}) collective-permute-start(bf16[1024,256]{1,0:T(8,128)(2,1)S(1)} %get-tuple-element.44.refs_5_), channel_id=1, source_target_pairs={{0,1},{1,0},{2,3},{3,2},{4,5},{5,4},{6,7},{7,6},{8,9},{9,8},{10,11... | collective-permute-start | bytes 1572872 | tf_op jit(solution)/shard_map/ppermute | solution.py:60
  9.6 1.4 %collective-permute-start.2 = (bf16[256,256]{1,0:T(8,128)(2,1)S(1)}, bf16[256,256]{1,0:T(8,128)(2,1)S(1)}, u32[]{:S(2)}, u32[]{:S(2)}) collective-permute-start(bf16[256,256]{1,0:T(8,128)(2,1)S(1)} %shard_map.94.refs_3_), channel_id=1, source_target_pairs={{0,1},{1,0},{2,3},{3,2},{4,5},{5,4},{6,7},{7,6},{8,9},{9,8},{10,11... | collective-permute-start | bytes 393224 | tf_op jit(solution)/shard_map/ppermute | solution.py:60
  11.1 4.6 %collective-permute-start.4 = (bf16[128,256]{1,0:T(8,128)(2,1)S(1)}, bf16[128,256]{1,0:T(8,128)(2,1)S(1)}, u32[]{:S(2)}, u32[]{:S(2)}) collective-permute-start(bf16[128,256]{1,0:T(8,128)(2,1)S(1)} %shard_map.95.refs_2_.refs_0_), channel_id=1, source_target_pairs={{0,4},{1,5},{2,6},{3,7},{4,0},{5,1},{6,2},{7,3},{8,12},{9,13},{10,... | collective-permute-start | bytes 196616 | tf_op jit(solution)/shard_map/ppermute | solution.py:60
  13.3 8.1 %collective-permute-start.3 = (bf16[512,256]{1,0:T(8,128)(2,1)S(1)}, bf16[512,256]{1,0:T(8,128)(2,1)S(1)}, u32[]{:S(2)}, u32[]{:S(2)}) collective-permute-start(bf16[512,256]{1,0:T(8,128)(2,1)S(1)} %shard_map.96.refs_2_), channel_id=1, source_target_pairs={{0,2},{1,3},{2,0},{3,1},{4,6},{5,7},{6,4},{7,5},{8,10},{9,11},{10,... | collective-permute-start | bytes 786440 | tf_op jit(solution)/shard_map/ppermute | solution.py:60
  14.9 4.4 %collective-permute-start.7 = (bf16[128,1024]{1,0:T(8,128)(2,1)S(1)}, bf16[128,1024]{1,0:T(8,128)(2,1)S(1)}, u32[]{:S(2)}, u32[]{:S(2)}) collective-permute-start(bf16[128,1024]{1,0:T(8,128)(2,1)S(1)} %collective-permute-done.6.refs_2_), channel_id=1, source_target_pairs={{0,1},{1,0},{2,3},{3,2},{4,5},{5,4},{6,7},{7,6},{8,9},{9,8},{10,11... | collective-permute-start | bytes 786440 | tf_op jit(solution)/shard_map/ppermute | solution.py:60
  15.7 5.6 %collective-permute-start.5 = (bf16[128,256]{1,0:T(8,128)(2,1)S(1)}, bf16[128,256]{1,0:T(8,128)(2,1)S(1)}, u32[]{:S(2)}, u32[]{:S(2)}) collective-permute-start(bf16[128,256]{1,0:T(8,128)(2,1)S(1)} %shard_map.97.refs_5_), channel_id=1, source_target_pairs={{0,8},{1,9},{2,10},{3,11},{4,12},{5,13},{6,14},{7,15},{8,0},{9,1},... | collective-permute-start | bytes 196616 | tf_op jit(solution)/shard_map/ppermute | solution.py:60
  19.2 11.1 %collective-permute-start.12 = (bf16[2,512,256]{2,1,0:T(8,128)(2,1)S(1)}, bf16[2,512,256]{2,1,0:T(8,128)(2,1)S(1)}, u32[]{:S(2)}, u32[]{:S(2)}) collective-permute-start(bf16[2,512,256]{2,1,0:T(8,128)(2,1)S(1)} %collective-permute-done.8.refs_4_.refs_2_.refs_8_), channel_id=1, source_target_pairs={{0,1},{1,0},{2,3},{3,2},{4,5},{5,4},{6,7},{7,6},{8,9},{9,8},{10,11... | collective-permute-start | bytes 1572872 | tf_op jit(solution)/shard_map/ppermute | solution.py:60
  23.0 7.3 %collective-permute-start.11 = (bf16[512,256]{1,0:T(8,128)(2,1)S(1)}, bf16[512,256]{1,0:T(8,128)(2,1)S(1)}, u32[]{:S(2)}, u32[]{:S(2)}) collective-permute-start(bf16[512,256]{1,0:T(8,128)(2,1)S(1)} %get-tuple-element.59.refs_2_), channel_id=1, source_target_pairs={{0,16},{16,0},{1,17},{17,1},{2,18},{18,2},{3,19},{19,3},{4,20},{20... | collective-permute-start | bytes 786440 | tf_op jit(solution)/shard_map/ppermute | solution.py:60
  24.5 9.9 %collective-permute-start.9 = (bf16[512,256]{1,0:T(8,128)(2,1)S(1)}, bf16[512,256]{1,0:T(8,128)(2,1)S(1)}, u32[]{:S(2)}, u32[]{:S(2)}) collective-permute-start(bf16[512,256]{1,0:T(8,128)(2,1)S(1)} %get-tuple-element.53), channel_id=1, source_target_pairs={{0,2},{1,3},{2,0},{3,1},{4,6},{5,7},{6,4},{7,5},{8,10},{9,11},{10,... | collective-permute-start | bytes 786440 | tf_op jit(solution)/shard_map/ppermute | solution.py:60
  26.1 5.7 %collective-permute-start.10 = (bf16[128,256]{1,0:T(8,128)(2,1)S(1)}, bf16[128,256]{1,0:T(8,128)(2,1)S(1)}, u32[]{:S(2)}, u32[]{:S(2)}) collective-permute-start(bf16[128,256]{1,0:T(8,128)(2,1)S(1)} %get-tuple-element.54.refs_3_.refs_0_), channel_id=1, source_target_pairs={{0,4},{1,5},{2,6},{3,7},{4,0},{5,1},{6,2},{7,3},{8,12},{9,13},{10,... | collective-permute-start | bytes 196616 | tf_op jit(solution)/shard_map/ppermute | solution.py:60
  30.3 5.0 %collective-permute-start.15 = (bf16[256,256]{1,0:T(8,128)(2,1)S(1)}, bf16[256,256]{1,0:T(8,128)(2,1)S(1)}, u32[]{:S(2)}, u32[]{:S(2)}) collective-permute-start(bf16[256,256]{1,0:T(8,128)(2,1)S(1)} %get-tuple-element.61.refs_2_), channel_id=1, source_target_pairs={{0,4},{1,5},{2,6},{3,7},{4,0},{5,1},{6,2},{7,3},{8,12},{9,13},{10,... | collective-permute-start | bytes 393224 | tf_op jit(solution)/shard_map/ppermute | solution.py:60
  31.8 6.3 %collective-permute-start.14 = (bf16[128,256]{1,0:T(8,128)(2,1)S(1)}, bf16[128,256]{1,0:T(8,128)(2,1)S(1)}, u32[]{:S(2)}, u32[]{:S(2)}) collective-permute-start(bf16[128,256]{1,0:T(8,128)(2,1)S(1)} %shard_map.104.refs_2_), channel_id=1, source_target_pairs={{0,8},{1,9},{2,10},{3,11},{4,12},{5,13},{6,14},{7,15},{8,0},{9,1},... | collective-permute-start | bytes 196616 | tf_op jit(solution)/shard_map/ppermute | solution.py:60
  34.5 5.3 %collective-permute-start.13 = (bf16[512,256]{1,0:T(8,128)(2,1)S(1)}, bf16[512,256]{1,0:T(8,128)(2,1)S(1)}, u32[]{:S(2)}, u32[]{:S(2)}) collective-permute-start(bf16[512,256]{1,0:T(8,128)(2,1)S(1)} %shard_map.105.refs_2_), channel_id=1, source_target_pairs={{0,1},{1,0},{2,3},{3,2},{4,5},{5,4},{6,7},{7,6},{8,9},{9,8},{10,11... | collective-permute-start | bytes 786440 | tf_op jit(solution)/shard_map/ppermute | solution.py:60
  35.4 6.4 %collective-permute-start.17 = (bf16[128,256]{1,0:T(8,128)(2,1)S(1)}, bf16[128,256]{1,0:T(8,128)(2,1)S(1)}, u32[]{:S(2)}, u32[]{:S(2)}) collective-permute-start(bf16[128,256]{1,0:T(8,128)(2,1)S(1)} %get-tuple-element.64.refs_3_), channel_id=1, source_target_pairs={{0,8},{1,9},{2,10},{3,11},{4,12},{5,13},{6,14},{7,15},{8,0},{9,1},... | collective-permute-start | bytes 196616 | tf_op jit(solution)/shard_map/ppermute | solution.py:60
  38.2 5.3 %collective-permute-start.16 = (bf16[256,256]{1,0:T(8,128)(2,1)S(1)}, bf16[256,256]{1,0:T(8,128)(2,1)S(1)}, u32[]{:S(2)}, u32[]{:S(2)}) collective-permute-start(bf16[256,256]{1,0:T(8,128)(2,1)S(1)} %get-tuple-element.66.refs_7_), channel_id=1, source_target_pairs={{0,2},{1,3},{2,0},{3,1},{4,6},{5,7},{6,4},{7,5},{8,10},{9,11},{10,... | collective-permute-start | bytes 393224 | tf_op jit(solution)/shard_map/ppermute | solution.py:60
  41.8 1.7 %copy-start.2 = (bf16[512,1024]{1,0:T(8,128)(2,1)S(1)}, bf16[512,1024]{1,0:T(8,128)(2,1)}, u32[]{:S(2)}) copy-start(bf16[512,1024]{1,0:T(8,128)(2,1)} %refs_7_.1) | copy-start | bytes 3145732
  41.9 4.0 %collective-permute-start.19 = (bf16[64,256]{1,0:T(8,128)(2,1)S(1)}, bf16[64,256]{1,0:T(8,128)(2,1)S(1)}, u32[]{:S(2)}, u32[]{:S(2)}) collective-permute-start(bf16[64,256]{1,0:T(8,128)(2,1)S(1)} %get-tuple-element.70.refs_2_), channel_id=1, source_target_pairs={{0,2},{1,3},{2,0},{3,1},{4,6},{5,7},{6,4},{7,5},{8,10},{9,11},{10,... | collective-permute-start | bytes 98312 | tf_op jit(solution)/shard_map/ppermute | solution.py:60
  43.5 2.7 %collective-permute-start.18 = (bf16[256,256]{1,0:T(8,128)(2,1)S(1)}, bf16[256,256]{1,0:T(8,128)(2,1)S(1)}, u32[]{:S(2)}, u32[]{:S(2)}) collective-permute-start(bf16[256,256]{1,0:T(8,128)(2,1)S(1)} %shard_map.110.refs_10_.refs_2_), channel_id=1, source_target_pairs={{0,1},{1,0},{2,3},{3,2},{4,5},{5,4},{6,7},{7,6},{8,9},{9,8},{10,11... | collective-permute-start | bytes 393224 | tf_op jit(solution)/shard_map/ppermute | solution.py:60
  45.8 1.5 %collective-permute-start.20 = (bf16[64,256]{1,0:T(8,128)(2,1)S(1)}, bf16[64,256]{1,0:T(8,128)(2,1)S(1)}, u32[]{:S(2)}, u32[]{:S(2)}) collective-permute-start(bf16[64,256]{1,0:T(8,128)(2,1)S(1)} %get-tuple-element.75.refs_7_.refs_2_), channel_id=1, source_target_pairs={{0,1},{1,0},{2,3},{3,2},{4,5},{5,4},{6,7},{7,6},{8,9},{9,8},{10,11... | collective-permute-start | bytes 98312 | tf_op jit(solution)/shard_map/ppermute | solution.py:60

commit v17 on v16

--- a/solution.py
+++ b/solution.py
@@ -231,49 +231,56 @@
     return near_ref.at[first], core_ref.at[first], far_ref.at[first], core_ref.at[second]
 
 
-def late_kernel(near_ref, far_ref, core_ref, q_ref, k_ref, v_ref, attend_ref, gq_ref, gk_ref, gv_ref):
+def late_kernel(near_ref, far_ref, core_ref, q_ref, k_ref, v_ref, gq_ref, gk_ref):
     backs = arrived(near_ref, far_ref, core_ref)
     block, width = q_ref.shape[0], near_ref.shape[1]
     mask = causal(block)
     for r in range(SLAB):
         at = cut(member(r), width)
         q, k, v = q_ref[:, at], k_ref[:, at], v_ref[:, at]
-        gqs, gks, gvs = [], [], []
+        gqs, gks = [], []
         for h in range(width // DH):
             dmixed, prior = backs[r][:block, head(h)], backs[r][block:, head(h)]
             back = jnp.where(mask, dot(dmixed, v[:, head(h)], 1, 1), 0.0).astype(BF16)
             gqs.append(dot(back, k[:, head(h)], 1, 0) + dot(dmixed, prior, 1, 1))
             gks.append(dot(back, q[:, head(h)], 0, 0))
-            gvs.append(dot(attend_ref[r, h], dmixed, 0, 0))
         gq_ref[:, at] = jnp.concatenate(gqs, axis=1).astype(BF16)
         gk_ref[r] = jnp.concatenate(gks, axis=1)
-        gv_ref[r] = jnp.concatenate(gvs, axis=1)
-
-
-def output_kernel(near_ref, back_far, core_ref, q_ref, own_ref, message_ref, far_ref, weight_ref, *refs):
-    *far, out_ref, normed_ref = refs
+
+
+def turn_kernel(weight_ref, *refs):
+    *far, out_ref = refs
+    rows = weight_ref.shape[0]
+    width = weight_ref.shape[1] // SLAB
+    me = lax.axis_index("dp")
+    for p in range(SLAB):
+        out_ref[part(p, width), cut(me, rows)] = weight_ref[:, part(p, width)].T
+    for j in range(1, len(far) // 2 + 1):
+        for r in range(SLAB):
+            place = (cut(member(r), width), cut(jnp.bitwise_xor(me, j), rows))
+            out_ref[place] = far[2 * (j - 1) + r % 2][r // 2].T
+
+
+def output_kernel(
+    near_ref, back_far, core_ref, q_ref, own_ref, message_ref, far_ref, attend_ref, turned_ref,
+    out_ref, gv_ref, normed_ref,
+):
     backs = arrived(near_ref, back_far, core_ref)
     block, width = q_ref.shape[0], near_ref.shape[1]
-    rows = weight_ref.shape[0]
-    me = lax.axis_index("dp")
     withins = (own_ref.at[part(1, block)], message_ref.at[part(1, block)],
                far_ref.at[part(1, block)], message_ref.at[part(3, block)])
-    totals = [jnp.zeros((block, rows), F32)] * (len(far) // 2)
     for r in range(SLAB):
         at = cut(member(r), width)
         q = q_ref[:, at]
-        normeds = []
+        normeds, gvs = [], []
         for h in range(width // DH):
             mixed = withins[r][:, head(h)].astype(F32) + dot(q[:, head(h)], backs[r][block:, head(h)], 1, 0)
             scale = lax.rsqrt(jnp.mean(mixed * mixed, axis=-1, keepdims=True) + EPSILON)
             normeds.append(mixed * scale)
-        normed = jnp.concatenate(normeds, axis=1).astype(BF16)
-        normed_ref[:, at] = normed
-        for j in range(len(totals)):
-            totals[j] = totals[j] + dot(normed, far[2 * j + r % 2][r // 2], 1, 1)
-    out_ref[:, cut(me, rows)] = dot(normed_ref[...], weight_ref[...], 1, 1).astype(BF16)
-    for j, total in enumerate(totals, 1):
-        out_ref[:, cut(jnp.bitwise_xor(me, j), rows)] = total.astype(BF16)
+            gvs.append(dot(attend_ref[r, h], backs[r][:block, head(h)], 0, 0))
+        normed_ref[:, at] = jnp.concatenate(normeds, axis=1).astype(BF16)
+        gv_ref[r] = jnp.concatenate(gvs, axis=1)
+    out_ref[...] = dot(normed_ref[...], turned_ref[...], 1, 0).astype(BF16)
 
 
 def last_kernel(near_ref, far_ref, core_ref, k_ref, v_ref, gk_part, gv_part, gk_ref, gv_ref):
@@ -421,9 +428,10 @@
         )
         got = flip(send, "dp", dp, 1)
     back_far = near(back_far, bits=2)
+    (turned,) = call(turn_kernel, [((features, outputs), BF16)], out_weight, *w_all)
     if tuned:
         keep, send = call(
-            split_kernel, [((2 * piece, width), F32), ((2 * piece, width), BF16)], keep, got, wait=w_all[1::2]
+            split_kernel, [((2 * piece, width), F32), ((2 * piece, width), BF16)], keep, got, cost=1
         )
         got = near(send, bits=SLAB)
     behind, last_u = doubling(slab_u, 10**9)
@@ -439,10 +447,9 @@
         scratch=[pltpu.VMEM((SLAB, DH, width), F32)],
     )
     later_far = near(later_far, bits=2)
-    gq, gk_part, gv_part = call(
-        late_kernel,
-        [((rows, features), BF16), ((SLAB, rows, width), F32), ((SLAB, rows, width), F32)],
-        back, back_far, back_core, q, k, v, attend,
+    gq, gk_part = call(
+        late_kernel, [((rows, features), BF16), ((SLAB, rows, width), F32)],
+        back, back_far, back_core, q, k, v,
     )
     if tuned:
         keep, share = call(
@@ -452,9 +459,9 @@
         got = near(share, bits=2)
     (send,) = call(relay_kernel, [((2 * DH, width), BF16)], later, later_far)
     later_core = near(send, bits=1)
-    output, own_normed = call(
-        output_kernel, [((rows, outputs), BF16), ((rows, features), BF16)],
-        back, back_far, back_core, q, own_tokens, *sent, out_weight, *w_all, end=True,
+    output, gv_part, own_normed = call(
+        output_kernel, [((rows, outputs), BF16), ((SLAB, rows, width), F32), ((rows, features), BF16)],
+        back, back_far, back_core, q, own_tokens, *sent, attend, turned, end=True,
     )
     if tuned:
         keep, share = call(

time: 48.2 us -> 55.4 us (1.15)
  local copies, waits for them, and re-layouts: 0.02 us -> 3.82 us
  waiting for transfers between devices: 9.89 us -> 12.6 us
    unnamed x10 -> x18, local copies, waits for them, and re-layouts: 0.02 us -> 3.82 us
    ppermute x21, waiting for transfers between devices: 9.89 us -> 12.6 us  [flip(): return lax.ppermute(x, axis, [(i, i ^ bits) for i in range(count)])]
    pallas_call x23 -> x24, Pallas kernels: 11.5 us -> 11.9 us  [__call__(): pl.pallas_call(inner, out_shape=[jax.ShapeDtypeStruct(s, d) for s, d in o...]
  transfers between devices with their start and end apart: 21 -> 21, of which waited for: 10 -> 7; matrix products, arithmetic and copies ran while one was open for 0% -> 0% of each run, Pallas kernels for 19% -> 18%
where the time goes in v17:
time: 55.4 us; the launch traced here: 55.1 us
  starting transfers between devices  25.9 us (47%)
  waiting for transfers between devices  12.6 us (23%)
  Pallas kernels  11.9 us (21%)
  local copies, waits for them, and re-layouts  3.82 us (7%)
  between operations  0.85 us (2%)
    ppermute x21, starting transfers between devices, flip(): return lax.ppermute(x, axis, [(i, i ^ bits) for i in range(count)])  25.9 us
    ppermute x21, waiting for transfers between devices, flip(): return lax.ppermute(x, axis, [(i, i ^ bits) for i in range(count)])  12.6 us
    pallas_call x24, Pallas kernels, __call__(): pl.pallas_call(inner, out_shape=[jax.ShapeDtypeStruct(s, d) for s, d in o...  11.9 us
    unnamed x18, local copies, waits for them, and re-layouts  3.82 us
  transfers between devices with their start and end apart: 21, of which 7 were waited for; matrix products, arithmetic and copies ran while one was open for 0% of the time, Pallas kernels for 18%

profile of v17, /device:TPU:0, one launch (start us, length us, event | category | flops | bytes accessed | tf_op | source)
XLA Modules:
  0.0 55.1 jit_solution(7806235186628355899)
XLA Ops:
  0.6 1.5 %shard_map.92 = (f32[128,256]{1,0:T(8,128)S(1)}, bf16[128,256]{1,0:T(8,128)(2,1)S(1)}, bf16[256,256]{1,0:T(8,128)(2,1)S(1)}, bf16[2,512,256]{2,1,0:T(8,128)(2,1)S(1)}) custom-call(bf16[128,1024]{1,0:T(8,128)(2,1)} %bitcast.8, bf16[128,1024]{1,0:T(8,128)(2,1)} %bitcast.12, bf16[512,1024]{1,0:T(8,128)(2,1)} %refs_0_.1), custom_call_target="tpu_custom_call" | custom-call | flops 1 | bytes 1 | tf_op jit(solution)/shard_map/pallas_call | solution.py:42
  2.1 3.0 %collective-permute-start.1 = (bf16[256,256]{1,0:T(8,128)(2,1)S(1)}, bf16[256,256]{1,0:T(8,128)(2,1)S(1)}, u32[]{:S(2)}, u32[]{:S(2)}) collective-permute-start(bf16[256,256]{1,0:T(8,128)(2,1)S(1)} %get-tuple-element.47), channel_id=1, source_target_pairs={{0,2},{1,3},{2,0},{3,1},{4,6},{5,7},{6,4},{7,5},{8,10},{9,11},{10,... | collective-permute-start | bytes 393224 | tf_op jit(solution)/shard_map/ppermute | solution.py:60
  5.2 0.9 %copy-done.1 = bf16[1,128,1024]{2,1,0:T(8,128)(2,1)S(1)} copy-done((bf16[1,128,1024]{2,1,0:T(8,128)(2,1)S(1)}, bf16[1,128,1024]{2,1,0:T(8,128)(2,1)}, u32[]{:S(2)}) %copy-start.1) | copy-done | bytes 262168
  6.2 0.9 %copy-done.3 = bf16[1,128,1024]{2,1,0:T(8,128)(2,1)S(1)} copy-done((bf16[1,128,1024]{2,1,0:T(8,128)(2,1)S(1)}, bf16[1,128,1024]{2,1,0:T(8,128)(2,1)}, u32[]{:S(2)}) %copy-start.3) | copy-done | bytes 262168
  7.1 0.9 %copy-done.5 = bf16[1,128,1024]{2,1,0:T(8,128)(2,1)S(1)} copy-done((bf16[1,128,1024]{2,1,0:T(8,128)(2,1)S(1)}, bf16[1,128,1024]{2,1,0:T(8,128)(2,1)}, u32[]{:S(2)}) %copy-start.5) | copy-done | bytes 262168
  8.1 0.9 %copy-done.7 = bf16[1,128,1024]{2,1,0:T(8,128)(2,1)S(1)} copy-done((bf16[1,128,1024]{2,1,0:T(8,128)(2,1)S(1)}, bf16[1,128,1024]{2,1,0:T(8,128)(2,1)}, u32[]{:S(2)}) %copy-start.7) | copy-done | bytes 262168
  9.0 1.3 %shard_map.93 = (bf16[4,2,128,128]{3,2,1,0:T(8,128)(2,1)S(1)}, bf16[256,256]{1,0:T(8,128)(2,1)S(1)}, bf16[1024,256]{1,0:T(8,128)(2,1)S(1)}, bf16[256,256]{1,0:T(8,128)(2,1)S(1)}) custom-call(bf16[128,1024]{1,0:T(8,128)(2,1)S(1)} %bitcast.16, bf16[128,1024]{1,0:T(8,128)(2,1)S(1)} %bitcast.9, bf16[128,1024]{1,0:T(8,128)(2,1)S(1)} %bitcast.13, ...), custom_call_target="tpu_custom_call" | custom-call | flops 1 | bytes 1 | tf_op jit(solution)/shard_map/pallas_call | solution.py:42
  10.5 2.0 %collective-permute-start.8 = (bf16[2,512,256]{2,1,0:T(8,128)(2,1)S(1)}, bf16[2,512,256]{2,1,0:T(8,128)(2,1)S(1)}, u32[]{:S(2)}, u32[]{:S(2)}) collective-permute-start(bf16[2,512,256]{2,1,0:T(8,128)(2,1)S(1)} %get-tuple-element.49.refs_3_.refs_1_), channel_id=1, source_target_pairs={{0,16},{16,0},{1,17},{17,1},{2,18},{18,2},{3,19},{19,3},{4,20},{20... | collective-permute-start | bytes 1572872 | tf_op jit(solution)/shard_map/ppermute | solution.py:60
  12.7 1.2 %collective-permute-done.2.refs_2_.refs_5_ = bf16[256,256]{1,0:T(8,128)(2,1)S(1)} collective-permute-done((bf16[256,256]{1,0:T(8,128)(2,1)S(1)}, bf16[256,256]{1,0:T(8,128)(2,1)S(1)}, u32[]{:S(2)}, u32[]{:S(2)}) %collective-permute-start.2) | collective-permute-done | bytes 131104 | tf_op jit(solution)/shard_map/ppermute | solution.py:60
  13.9 1.6 %collective-permute-start.4 = (bf16[128,256]{1,0:T(8,128)(2,1)S(1)}, bf16[128,256]{1,0:T(8,128)(2,1)S(1)}, u32[]{:S(2)}, u32[]{:S(2)}) collective-permute-start(bf16[128,256]{1,0:T(8,128)(2,1)S(1)} %shard_map.95.refs_2_.refs_0_), channel_id=1, source_target_pairs={{0,4},{1,5},{2,6},{3,7},{4,0},{5,1},{6,2},{7,3},{8,12},{9,13},{10,... | collective-permute-start | bytes 196616 | tf_op jit(solution)/shard_map/ppermute | solution.py:60
  15.6 1.6 %collective-permute-start.3 = (bf16[512,256]{1,0:T(8,128)(2,1)S(1)}, bf16[512,256]{1,0:T(8,128)(2,1)S(1)}, u32[]{:S(2)}, u32[]{:S(2)}) collective-permute-start(bf16[512,256]{1,0:T(8,128)(2,1)S(1)} %shard_map.96.refs_2_), channel_id=1, source_target_pairs={{0,2},{1,3},{2,0},{3,1},{4,6},{5,7},{6,4},{7,5},{8,10},{9,11},{10,... | collective-permute-start | bytes 786440 | tf_op jit(solution)/shard_map/ppermute | solution.py:60
  17.2 1.1 %collective-permute-done.4.refs_1_.refs_0_ = bf16[128,256]{1,0:T(8,128)(2,1)S(1)} collective-permute-done((bf16[128,256]{1,0:T(8,128)(2,1)S(1)}, bf16[128,256]{1,0:T(8,128)(2,1)S(1)}, u32[]{:S(2)}, u32[]{:S(2)}) %collective-permute-start.4) | collective-permute-done | bytes 65568 | tf_op jit(solution)/shard_map/ppermute | solution.py:60
  18.3 2.7 %collective-permute-start.5 = (bf16[128,256]{1,0:T(8,128)(2,1)S(1)}, bf16[128,256]{1,0:T(8,128)(2,1)S(1)}, u32[]{:S(2)}, u32[]{:S(2)}) collective-permute-start(bf16[128,256]{1,0:T(8,128)(2,1)S(1)} %shard_map.97.refs_5_), channel_id=1, source_target_pairs={{0,8},{1,9},{2,10},{3,11},{4,12},{5,13},{6,14},{7,15},{8,0},{9,1},... | collective-permute-start | bytes 196616 | tf_op jit(solution)/shard_map/ppermute | solution.py:60
  20.9 4.0 %collective-permute-done.8.refs_4_.refs_2_.refs_1_ = bf16[2,512,256]{2,1,0:T(8,128)(2,1)S(1)} collective-permute-done((bf16[2,512,256]{2,1,0:T(8,128)(2,1)S(1)}, bf16[2,512,256]{2,1,0:T(8,128)(2,1)S(1)}, u32[]{:S(2)}, u32[]{:S(2)}) %collective-permute-start.8) | collective-permute-done | bytes 524320 | tf_op jit(solution)/shard_map/ppermute | solution.py:60
  25.8 0.8 %shard_map.101 = (bf16[4,128,256]{2,1,0:T(8,128)(2,1)S(1)}, bf16[512,256]{1,0:T(8,128)(2,1)S(1)}, bf16[512,256]{1,0:T(8,128)(2,1)S(1)}, f32[4,128,256]{2,1,0:T(8,128)S(1)}, bf16[128,256]{1,0:T(8,128)(2,1)S(1)}) custom-call(bf16[256,256]{1,0:T(8,128)(2,1)S(1)} %get-tuple-element.43.refs_0_.refs_4_, ...), custom_call_target="tpu_custom_call" | custom-call | flops 10000000000 | bytes 1 | tf_op jit(solution)/shard_map/pallas_call | solution.py:42
  26.6 0.8 %shard_map.102 = (f32[512,256]{1,0:T(8,128)S(1)}, bf16[512,256]{1,0:T(8,128)(2,1)S(1)}) custom-call(bf16[3,128,1024]{2,1,0:T(8,128)(2,1)S(1)} %get-tuple-element.55.refs_0_, bf16[1,128,1024]{2,1,0:T(8,128)(2,1)S(1)} %get-tuple-element.56.refs_1_, bf16[4,128,256]{2,1,0:T(8,128)(2,1)S(1)} %get-tuple-element.57.refs_2_, ...), custom_call_target="tpu_custom_call" | custom-call | flops 1 | bytes 1 | tf_op jit(solution)/shard_map/pallas_call | solution.py:42
  27.4 1.8 %collective-permute-start.11 = (bf16[512,256]{1,0:T(8,128)(2,1)S(1)}, bf16[512,256]{1,0:T(8,128)(2,1)S(1)}, u32[]{:S(2)}, u32[]{:S(2)}) collective-permute-start(bf16[512,256]{1,0:T(8,128)(2,1)S(1)} %get-tuple-element.59.refs_3_), channel_id=1, source_target_pairs={{0,16},{16,0},{1,17},{17,1},{2,18},{18,2},{3,19},{19,3},{4,20},{20... | collective-permute-start | bytes 786440 | tf_op jit(solution)/shard_map/ppermute | solution.py:60
  29.2 1.5 %collective-permute-start.9 = (bf16[512,256]{1,0:T(8,128)(2,1)S(1)}, bf16[512,256]{1,0:T(8,128)(2,1)S(1)}, u32[]{:S(2)}, u32[]{:S(2)}) collective-permute-start(bf16[512,256]{1,0:T(8,128)(2,1)S(1)} %get-tuple-element.53), channel_id=1, source_target_pairs={{0,2},{1,3},{2,0},{3,1},{4,6},{5,7},{6,4},{7,5},{8,10},{9,11},{10,... | collective-permute-start | bytes 786440 | tf_op jit(solution)/shard_map/ppermute | solution.py:60
  30.7 1.6 %collective-permute-start.10 = (bf16[128,256]{1,0:T(8,128)(2,1)S(1)}, bf16[128,256]{1,0:T(8,128)(2,1)S(1)}, u32[]{:S(2)}, u32[]{:S(2)}) collective-permute-start(bf16[128,256]{1,0:T(8,128)(2,1)S(1)} %get-tuple-element.54.refs_3_.refs_0_), channel_id=1, source_target_pairs={{0,4},{1,5},{2,6},{3,7},{4,0},{5,1},{6,2},{7,3},{8,12},{9,13},{10,... | collective-permute-start | bytes 196616 | tf_op jit(solution)/shard_map/ppermute | solution.py:60
  32.3 0.6 %shard_map.103.refs_2_.refs_8_ = bf16[1024,1024]{1,0:T(8,128)(2,1)S(1)} custom-call(bf16[512,1024]{1,0:T(8,128)(2,1)S(1)} %copy-done, bf16[2,512,256]{2,1,0:T(8,128)(2,1)S(1)} %collective-permute-done.8.refs_4_.refs_2_.refs_1_, bf16[2,512,256]{2,1,0:T(8,128)(2,1)S(1)} %collective-permute-done.12.refs_2_, bf16[512,256]{1,0:T(8,128)(2,1)S(1)} %get-tuple-element.59.refs_3_), custom_call_target="tpu_custom_call" | custom-call | flops 1 | bytes 1 | tf_op jit(solution)/shard_map/pallas_call | solution.py:42
  33.0 3.2 %collective-permute-done.11.refs_1_ = bf16[512,256]{1,0:T(8,128)(2,1)S(1)} collective-permute-done((bf16[512,256]{1,0:T(8,128)(2,1)S(1)}, bf16[512,256]{1,0:T(8,128)(2,1)S(1)}, u32[]{:S(2)}, u32[]{:S(2)}) %collective-permute-start.11) | collective-permute-done | bytes 262176 | tf_op jit(solution)/shard_map/ppermute | solution.py:60
  36.2 1.9 %collective-permute-start.15 = (bf16[256,256]{1,0:T(8,128)(2,1)S(1)}, bf16[256,256]{1,0:T(8,128)(2,1)S(1)}, u32[]{:S(2)}, u32[]{:S(2)}) collective-permute-start(bf16[256,256]{1,0:T(8,128)(2,1)S(1)} %get-tuple-element.61.refs_2_), channel_id=1, source_target_pairs={{0,4},{1,5},{2,6},{3,7},{4,0},{5,1},{6,2},{7,3},{8,12},{9,13},{10,... | collective-permute-start | bytes 393224 | tf_op jit(solution)/shard_map/ppermute | solution.py:60
  38.1 2.6 %collective-permute-start.14 = (bf16[128,256]{1,0:T(8,128)(2,1)S(1)}, bf16[128,256]{1,0:T(8,128)(2,1)S(1)}, u32[]{:S(2)}, u32[]{:S(2)}) collective-permute-start(bf16[128,256]{1,0:T(8,128)(2,1)S(1)} %shard_map.105.refs_2_), channel_id=1, source_target_pairs={{0,8},{1,9},{2,10},{3,11},{4,12},{5,13},{6,14},{7,15},{8,0},{9,1},... | collective-permute-start | bytes 196616 | tf_op jit(solution)/shard_map/ppermute | solution.py:60
  40.9 1.3 %collective-permute-done.15.refs_1_ = bf16[256,256]{1,0:T(8,128)(2,1)S(1)} collective-permute-done((bf16[256,256]{1,0:T(8,128)(2,1)S(1)}, bf16[256,256]{1,0:T(8,128)(2,1)S(1)}, u32[]{:S(2)}, u32[]{:S(2)}) %collective-permute-start.15) | collective-permute-done | bytes 131104 | tf_op jit(solution)/shard_map/ppermute | solution.py:60
  42.2 2.8 %collective-permute-start.17 = (bf16[128,256]{1,0:T(8,128)(2,1)S(1)}, bf16[128,256]{1,0:T(8,128)(2,1)S(1)}, u32[]{:S(2)}, u32[]{:S(2)}) collective-permute-start(bf16[128,256]{1,0:T(8,128)(2,1)S(1)} %get-tuple-element.65.refs_3_), channel_id=1, source_target_pairs={{0,8},{1,9},{2,10},{3,11},{4,12},{5,13},{6,14},{7,15},{8,0},{9,1},... | collective-permute-start | bytes 196616 | tf_op jit(solution)/shard_map/ppermute | solution.py:60
  45.2 1.6 %collective-permute-start.16 = (bf16[256,256]{1,0:T(8,128)(2,1)S(1)}, bf16[256,256]{1,0:T(8,128)(2,1)S(1)}, u32[]{:S(2)}, u32[]{:S(2)}) collective-permute-start(bf16[256,256]{1,0:T(8,128)(2,1)S(1)} %get-tuple-element.67.refs_6_), channel_id=1, source_target_pairs={{0,2},{1,3},{2,0},{3,1},{4,6},{5,7},{6,4},{7,5},{8,10},{9,11},{10,... | collective-permute-start | bytes 393224 | tf_op jit(solution)/shard_map/ppermute | solution.py:60
  46.8 2.5 %shard_map.109 = (bf16[128,1024]{1,0:T(8,128)(2,1)}, f32[4,128,256]{2,1,0:T(8,128)S(1)}) custom-call(bf16[512,256]{1,0:T(8,128)(2,1)S(1)} %get-tuple-element.52.refs_0_, bf16[512,256]{1,0:T(8,128)(2,1)S(1)} %collective-permute-done.9.refs_1_, bf16[512,256]{1,0:T(8,128)(2,1)S(1)} %collective-permute-done.13.refs_2_, bf16[128,1024]{1,0:T(8,128)(2,1)S(1)} %bitcast.17, ...), custom_call_target="tpu_custom_call" | custom-call | flops 1 | bytes 1 | tf_op jit(solution)/shard_map/pallas_call | solution.py:42
  49.9 0.7 %collective-permute-done.16.refs_1_ = bf16[256,256]{1,0:T(8,128)(2,1)S(1)} collective-permute-done((bf16[256,256]{1,0:T(8,128)(2,1)S(1)}, bf16[256,256]{1,0:T(8,128)(2,1)S(1)}, u32[]{:S(2)}, u32[]{:S(2)}) %collective-permute-start.16) | collective-permute-done | bytes 131104 | tf_op jit(solution)/shard_map/ppermute | solution.py:60
  50.7 1.5 %shard_map.112 = (bf16[128,1024]{1,0:T(8,128)(2,1)}, f32[4,128,256]{2,1,0:T(8,128)S(1)}, bf16[128,1024]{1,0:T(8,128)(2,1)}) custom-call(bf16[512,256]{1,0:T(8,128)(2,1)S(1)} %get-tuple-element.52.refs_0_, bf16[512,256]{1,0:T(8,128)(2,1)S(1)} %collective-permute-done.9.refs_1_, bf16[512,256]{1,0:T(8,128)(2,1)S(1)} %collective-permute-done.13.refs_2_, ...), custom_call_target="tpu_custom_call" | custom-call | flops 1 | bytes 1 | tf_op jit(solution)/shard_map/pallas_call | solution.py:42
  52.2 1.1 %collective-permute-done.19.refs_1_ = bf16[64,256]{1,0:T(8,128)(2,1)S(1)} collective-permute-done((bf16[64,256]{1,0:T(8,128)(2,1)S(1)}, bf16[64,256]{1,0:T(8,128)(2,1)S(1)}, u32[]{:S(2)}, u32[]{:S(2)}) %collective-permute-start.19) | collective-permute-done | bytes 32800 | tf_op jit(solution)/shard_map/ppermute | solution.py:60
  53.3 1.2 %shard_map.114 = (bf16[128,1024]{1,0:T(8,128)(2,1)}, bf16[128,1024]{1,0:T(8,128)(2,1)}) custom-call(bf16[256,256]{1,0:T(8,128)(2,1)S(1)} %get-tuple-element.66.refs_0_, bf16[256,256]{1,0:T(8,128)(2,1)S(1)} %collective-permute-done.16.refs_1_, bf16[256,256]{1,0:T(8,128)(2,1)S(1)} %collective-permute-done.18.refs_2_, bf16[128,1024]{1,0:T(8,128)(2,1)S(1)} %bitcast.11, ...), custom_call_target="tpu_custom_call" | custom-call | flops 1 | bytes 1 | tf_op jit(solution)/shard_map/pallas_call | solution.py:42
  54.5 0.7 %shard_map.115 = f32[32,1024]{1,0:T(8,128)} custom-call(bf16[64,256]{1,0:T(8,128)(2,1)S(1)} %get-tuple-element.78.refs_0_, bf16[64,256]{1,0:T(8,128)(2,1)S(1)} %collective-permute-done.20.refs_1_, bf16[64,256]{1,0:T(8,128)(2,1)S(1)} %get-tuple-element.75.refs_7_.refs_2_, bf16[128,1024]{1,0:T(8,128)(2,1)} %get-tuple-element.76.refs_3_), custom_call_target="tpu_custom_call" | custom-call | flops 1 | bytes 1 | tf_op jit(solution)/shard_map/pallas_call | solution.py:42
  (52 shorter events, 2.3 us)
Async XLA Ops:
  2.1 10.3 %collective-permute-start.1 = (bf16[256,256]{1,0:T(8,128)(2,1)S(1)}, bf16[256,256]{1,0:T(8,128)(2,1)S(1)}, u32[]{:S(2)}, u32[]{:S(2)}) collective-permute-start(bf16[256,256]{1,0:T(8,128)(2,1)S(1)} %get-tuple-element.47), channel_id=1, source_target_pairs={{0,2},{1,3},{2,0},{3,1},{4,6},{5,7},{6,4},{7,5},{8,10},{9,11},{10,... | collective-permute-start | bytes 393224 | tf_op jit(solution)/shard_map/ppermute | solution.py:60
  5.2 12.0 %collective-permute-start.6 = (bf16[128,1024]{1,0:T(8,128)(2,1)}, bf16[128,1024]{1,0:T(8,128)(2,1)S(1)}, u32[]{:S(2)}, u32[]{:S(2)}) collective-permute-start(bf16[128,1024]{1,0:T(8,128)(2,1)} %bitcast.19), channel_id=1, source_target_pairs={{0,2},{1,3},{2,0},{3,1},{4,6},{5,7},{6,4},{7,5},{8,10},{9,11},{10,... | collective-permute-start | bytes 786440 | tf_op jit(solution)/shard_map/ppermute | solution.py:60
  5.2 0.9 %copy-start.1 = (bf16[1,128,1024]{2,1,0:T(8,128)(2,1)S(1)}, bf16[1,128,1024]{2,1,0:T(8,128)(2,1)}, u32[]{:S(2)}) copy-start(bf16[1,128,1024]{2,1,0:T(8,128)(2,1)} %param.6) | copy-start | bytes 786436
  6.2 0.9 %copy-start.3 = (bf16[1,128,1024]{2,1,0:T(8,128)(2,1)S(1)}, bf16[1,128,1024]{2,1,0:T(8,128)(2,1)}, u32[]{:S(2)}) copy-start(bf16[1,128,1024]{2,1,0:T(8,128)(2,1)} %param.7) | copy-start | bytes 786436
  7.1 0.9 %copy-start.5 = (bf16[1,128,1024]{2,1,0:T(8,128)(2,1)S(1)}, bf16[1,128,1024]{2,1,0:T(8,128)(2,1)}, u32[]{:S(2)}) copy-start(bf16[1,128,1024]{2,1,0:T(8,128)(2,1)} %param.5) | copy-start | bytes 786436
  8.1 0.9 %copy-start.7 = (bf16[1,128,1024]{2,1,0:T(8,128)(2,1)S(1)}, bf16[1,128,1024]{2,1,0:T(8,128)(2,1)}, u32[]{:S(2)}) copy-start(bf16[1,128,1024]{2,1,0:T(8,128)(2,1)} %param.8) | copy-start | bytes 786436
  10.4 5.2 %collective-permute-start = (bf16[1024,256]{1,0:T(8,128)(2,1)S(1)}, bf16[1024,256]{1,0:T(8,128)(2,1)S(1)}, u32[]{:S(2)}, u32[]{:S(2)}) collective-permute-start(bf16[1024,256]{1,0:T(8,128)(2,1)S(1)} %get-tuple-element.44.refs_5_), channel_id=1, source_target_pairs={{0,1},{1,0},{2,3},{3,2},{4,5},{5,4},{6,7},{7,6},{8,9},{9,8},{10,11... | collective-permute-start | bytes 1572872 | tf_op jit(solution)/shard_map/ppermute | solution.py:60
  10.5 14.5 %collective-permute-start.8 = (bf16[2,512,256]{2,1,0:T(8,128)(2,1)S(1)}, bf16[2,512,256]{2,1,0:T(8,128)(2,1)S(1)}, u32[]{:S(2)}, u32[]{:S(2)}) collective-permute-start(bf16[2,512,256]{2,1,0:T(8,128)(2,1)S(1)} %get-tuple-element.49.refs_3_.refs_1_), channel_id=1, source_target_pairs={{0,16},{16,0},{1,17},{17,1},{2,18},{18,2},{3,19},{19,3},{4,20},{20... | collective-permute-start | bytes 1572872 | tf_op jit(solution)/shard_map/ppermute | solution.py:60
  12.5 1.4 %collective-permute-start.2 = (bf16[256,256]{1,0:T(8,128)(2,1)S(1)}, bf16[256,256]{1,0:T(8,128)(2,1)S(1)}, u32[]{:S(2)}, u32[]{:S(2)}) collective-permute-start(bf16[256,256]{1,0:T(8,128)(2,1)S(1)} %shard_map.94.refs_3_), channel_id=1, source_target_pairs={{0,1},{1,0},{2,3},{3,2},{4,5},{5,4},{6,7},{7,6},{8,9},{9,8},{10,11... | collective-permute-start | bytes 393224 | tf_op jit(solution)/shard_map/ppermute | solution.py:60
  13.9 4.3 %collective-permute-start.4 = (bf16[128,256]{1,0:T(8,128)(2,1)S(1)}, bf16[128,256]{1,0:T(8,128)(2,1)S(1)}, u32[]{:S(2)}, u32[]{:S(2)}) collective-permute-start(bf16[128,256]{1,0:T(8,128)(2,1)S(1)} %shard_map.95.refs_2_.refs_0_), channel_id=1, source_target_pairs={{0,4},{1,5},{2,6},{3,7},{4,0},{5,1},{6,2},{7,3},{8,12},{9,13},{10,... | collective-permute-start | bytes 196616 | tf_op jit(solution)/shard_map/ppermute | solution.py:60
  15.6 9.4 %copy-start.8 = (bf16[1,128,1024]{2,1,0:T(8,128)(2,1)S(1)}, bf16[1,128,1024]{2,1,0:T(8,128)(2,1)}, u32[]{:S(2)}) copy-start(bf16[1,128,1024]{2,1,0:T(8,128)(2,1)} %param.8) | copy-start | bytes 786436
  15.6 10.2 %collective-permute-start.3 = (bf16[512,256]{1,0:T(8,128)(2,1)S(1)}, bf16[512,256]{1,0:T(8,128)(2,1)S(1)}, u32[]{:S(2)}, u32[]{:S(2)}) collective-permute-start(bf16[512,256]{1,0:T(8,128)(2,1)S(1)} %shard_map.96.refs_2_), channel_id=1, source_target_pairs={{0,2},{1,3},{2,0},{3,1},{4,6},{5,7},{6,4},{7,5},{8,10},{9,11},{10,... | collective-permute-start | bytes 786440 | tf_op jit(solution)/shard_map/ppermute | solution.py:60
  17.2 8.3 %collective-permute-start.7 = (bf16[128,1024]{1,0:T(8,128)(2,1)S(1)}, bf16[128,1024]{1,0:T(8,128)(2,1)S(1)}, u32[]{:S(2)}, u32[]{:S(2)}) collective-permute-start(bf16[128,1024]{1,0:T(8,128)(2,1)S(1)} %collective-permute-done.6.refs_2_), channel_id=1, source_target_pairs={{0,1},{1,0},{2,3},{3,2},{4,5},{5,4},{6,7},{7,6},{8,9},{9,8},{10,11... | collective-permute-start | bytes 786440 | tf_op jit(solution)/shard_map/ppermute | solution.py:60
  18.3 7.5 %collective-permute-start.5 = (bf16[128,256]{1,0:T(8,128)(2,1)S(1)}, bf16[128,256]{1,0:T(8,128)(2,1)S(1)}, u32[]{:S(2)}, u32[]{:S(2)}) collective-permute-start(bf16[128,256]{1,0:T(8,128)(2,1)S(1)} %shard_map.97.refs_5_), channel_id=1, source_target_pairs={{0,8},{1,9},{2,10},{3,11},{4,12},{5,13},{6,14},{7,15},{8,0},{9,1},... | collective-permute-start | bytes 196616 | tf_op jit(solution)/shard_map/ppermute | solution.py:60
  25.4 6.9 %collective-permute-start.12 = (bf16[2,512,256]{2,1,0:T(8,128)(2,1)S(1)}, bf16[2,512,256]{2,1,0:T(8,128)(2,1)S(1)}, u32[]{:S(2)}, u32[]{:S(2)}) collective-permute-start(bf16[2,512,256]{2,1,0:T(8,128)(2,1)S(1)} %collective-permute-done.8.refs_4_.refs_2_.refs_1_), channel_id=1, source_target_pairs={{0,1},{1,0},{2,3},{3,2},{4,5},{5,4},{6,7},{7,6},{8,9},{9,8},{10,11... | collective-permute-start | bytes 1572872 | tf_op jit(solution)/shard_map/ppermute | solution.py:60
  26.6 5.7 %copy-start = (bf16[512,1024]{1,0:T(8,128)(2,1)S(1)}, bf16[512,1024]{1,0:T(8,128)(2,1)}, u32[]{:S(2)}) copy-start(bf16[512,1024]{1,0:T(8,128)(2,1)} %refs_0_.1) | copy-start | bytes 3145732
  27.4 8.8 %collective-permute-start.11 = (bf16[512,256]{1,0:T(8,128)(2,1)S(1)}, bf16[512,256]{1,0:T(8,128)(2,1)S(1)}, u32[]{:S(2)}, u32[]{:S(2)}) collective-permute-start(bf16[512,256]{1,0:T(8,128)(2,1)S(1)} %get-tuple-element.59.refs_3_), channel_id=1, source_target_pairs={{0,16},{16,0},{1,17},{17,1},{2,18},{18,2},{3,19},{19,3},{4,20},{20... | collective-permute-start | bytes 786440 | tf_op jit(solution)/shard_map/ppermute | solution.py:60
  29.2 11.6 %collective-permute-start.9 = (bf16[512,256]{1,0:T(8,128)(2,1)S(1)}, bf16[512,256]{1,0:T(8,128)(2,1)S(1)}, u32[]{:S(2)}, u32[]{:S(2)}) collective-permute-start(bf16[512,256]{1,0:T(8,128)(2,1)S(1)} %get-tuple-element.53), channel_id=1, source_target_pairs={{0,2},{1,3},{2,0},{3,1},{4,6},{5,7},{6,4},{7,5},{8,10},{9,11},{10,... | collective-permute-start | bytes 786440 | tf_op jit(solution)/shard_map/ppermute | solution.py:60
  30.7 7.4 %collective-permute-start.10 = (bf16[128,256]{1,0:T(8,128)(2,1)S(1)}, bf16[128,256]{1,0:T(8,128)(2,1)S(1)}, u32[]{:S(2)}, u32[]{:S(2)}) collective-permute-start(bf16[128,256]{1,0:T(8,128)(2,1)S(1)} %get-tuple-element.54.refs_3_.refs_0_), channel_id=1, source_target_pairs={{0,4},{1,5},{2,6},{3,7},{4,0},{5,1},{6,2},{7,3},{8,12},{9,13},{10,... | collective-permute-start | bytes 196616 | tf_op jit(solution)/shard_map/ppermute | solution.py:60
  36.2 6.0 %collective-permute-start.15 = (bf16[256,256]{1,0:T(8,128)(2,1)S(1)}, bf16[256,256]{1,0:T(8,128)(2,1)S(1)}, u32[]{:S(2)}, u32[]{:S(2)}) collective-permute-start(bf16[256,256]{1,0:T(8,128)(2,1)S(1)} %get-tuple-element.61.refs_2_), channel_id=1, source_target_pairs={{0,4},{1,5},{2,6},{3,7},{4,0},{5,1},{6,2},{7,3},{8,12},{9,13},{10,... | collective-permute-start | bytes 393224 | tf_op jit(solution)/shard_map/ppermute | solution.py:60
  38.1 6.9 %collective-permute-start.14 = (bf16[128,256]{1,0:T(8,128)(2,1)S(1)}, bf16[128,256]{1,0:T(8,128)(2,1)S(1)}, u32[]{:S(2)}, u32[]{:S(2)}) collective-permute-start(bf16[128,256]{1,0:T(8,128)(2,1)S(1)} %shard_map.105.refs_2_), channel_id=1, source_target_pairs={{0,8},{1,9},{2,10},{3,11},{4,12},{5,13},{6,14},{7,15},{8,0},{9,1},... | collective-permute-start | bytes 196616 | tf_op jit(solution)/shard_map/ppermute | solution.py:60
  40.8 5.9 %collective-permute-start.13 = (bf16[512,256]{1,0:T(8,128)(2,1)S(1)}, bf16[512,256]{1,0:T(8,128)(2,1)S(1)}, u32[]{:S(2)}, u32[]{:S(2)}) collective-permute-start(bf16[512,256]{1,0:T(8,128)(2,1)S(1)} %shard_map.106.refs_2_), channel_id=1, source_target_pairs={{0,1},{1,0},{2,3},{3,2},{4,5},{5,4},{6,7},{7,6},{8,9},{9,8},{10,11... | collective-permute-start | bytes 786440 | tf_op jit(solution)/shard_map/ppermute | solution.py:60
  42.2 4.6 %copy-start.2 = (bf16[1,128,1024]{2,1,0:T(8,128)(2,1)S(1)}, bf16[1,128,1024]{2,1,0:T(8,128)(2,1)}, u32[]{:S(2)}) copy-start(bf16[1,128,1024]{2,1,0:T(8,128)(2,1)} %param.6) | copy-start | bytes 786436
  42.2 4.6 %copy-start.4 = (bf16[1,128,1024]{2,1,0:T(8,128)(2,1)S(1)}, bf16[1,128,1024]{2,1,0:T(8,128)(2,1)}, u32[]{:S(2)}) copy-start(bf16[1,128,1024]{2,1,0:T(8,128)(2,1)} %param.7) | copy-start | bytes 786436
  42.2 4.6 %copy-start.6 = (bf16[1,128,1024]{2,1,0:T(8,128)(2,1)S(1)}, bf16[1,128,1024]{2,1,0:T(8,128)(2,1)}, u32[]{:S(2)}) copy-start(bf16[1,128,1024]{2,1,0:T(8,128)(2,1)} %param.5) | copy-start | bytes 786436
  42.2 7.0 %collective-permute-start.17 = (bf16[128,256]{1,0:T(8,128)(2,1)S(1)}, bf16[128,256]{1,0:T(8,128)(2,1)S(1)}, u32[]{:S(2)}, u32[]{:S(2)}) collective-permute-start(bf16[128,256]{1,0:T(8,128)(2,1)S(1)} %get-tuple-element.65.refs_3_), channel_id=1, source_target_pairs={{0,8},{1,9},{2,10},{3,11},{4,12},{5,13},{6,14},{7,15},{8,0},{9,1},... | collective-permute-start | bytes 196616 | tf_op jit(solution)/shard_map/ppermute | solution.py:60
  45.2 5.4 %collective-permute-start.16 = (bf16[256,256]{1,0:T(8,128)(2,1)S(1)}, bf16[256,256]{1,0:T(8,128)(2,1)S(1)}, u32[]{:S(2)}, u32[]{:S(2)}) collective-permute-start(bf16[256,256]{1,0:T(8,128)(2,1)S(1)} %get-tuple-element.67.refs_6_), channel_id=1, source_target_pairs={{0,2},{1,3},{2,0},{3,1},{4,6},{5,7},{6,4},{7,5},{8,10},{9,11},{10,... | collective-permute-start | bytes 393224 | tf_op jit(solution)/shard_map/ppermute | solution.py:60
  49.3 4.0 %collective-permute-start.19 = (bf16[64,256]{1,0:T(8,128)(2,1)S(1)}, bf16[64,256]{1,0:T(8,128)(2,1)S(1)}, u32[]{:S(2)}, u32[]{:S(2)}) collective-permute-start(bf16[64,256]{1,0:T(8,128)(2,1)S(1)} %get-tuple-element.70.refs_2_), channel_id=1, source_target_pairs={{0,2},{1,3},{2,0},{3,1},{4,6},{5,7},{6,4},{7,5},{8,10},{9,11},{10,... | collective-permute-start | bytes 98312 | tf_op jit(solution)/shard_map/ppermute | solution.py:60
  50.6 2.7 %collective-permute-start.18 = (bf16[256,256]{1,0:T(8,128)(2,1)S(1)}, bf16[256,256]{1,0:T(8,128)(2,1)S(1)}, u32[]{:S(2)}, u32[]{:S(2)}) collective-permute-start(bf16[256,256]{1,0:T(8,128)(2,1)S(1)} %shard_map.111.refs_9_.refs_2_), channel_id=1, source_target_pairs={{0,1},{1,0},{2,3},{3,2},{4,5},{5,4},{6,7},{7,6},{8,9},{9,8},{10,11... | collective-permute-start | bytes 393224 | tf_op jit(solution)/shard_map/ppermute | solution.py:60
  53.3 1.2 %collective-permute-start.20 = (bf16[64,256]{1,0:T(8,128)(2,1)S(1)}, bf16[64,256]{1,0:T(8,128)(2,1)S(1)}, u32[]{:S(2)}, u32[]{:S(2)}) collective-permute-start(bf16[64,256]{1,0:T(8,128)(2,1)S(1)} %get-tuple-element.75.refs_7_.refs_2_), channel_id=1, source_target_pairs={{0,1},{1,0},{2,3},{3,2},{4,5},{5,4},{6,7},{7,6},{8,9},{9,8},{10,11... | collective-permute-start | bytes 98312 | tf_op jit(solution)/shard_map/ppermute | solution.py:60

commit v18 on v16

--- a/solution.py
+++ b/solution.py
@@ -291,17 +291,16 @@
         gv_ref[:, at] = jnp.concatenate(gvs, axis=1).astype(BF16)
 
 
-def product_kernel(slabs, cot_a, cot_b, normed_ref, keep_ref, send_ref):
+def product_kernel(slabs, j, cot_a, cot_b, normed_ref, out_ref):
     me = lax.axis_index("dp")
     slab = lax.div(lax.axis_index("seq"), SLAB)
-    rows = keep_ref.shape[0] // slabs
-    for j, out in enumerate((send_ref, keep_ref)):
-        for d in range(slabs):
-            at = jnp.bitwise_xor(me, 1 - j) * slabs + jnp.bitwise_xor(slab, d)
-            total = dot(cot_b[0, :, cut(at, rows)], normed_ref[3], 0, 0)
-            for r in range(3):
-                total = total + dot(cot_a[r, :, cut(at, rows)], normed_ref[r], 0, 0)
-            out[part(d, rows), :] = total.astype(out.dtype)
+    rows = out_ref.shape[0] // slabs
+    for d in range(slabs):
+        at = jnp.bitwise_xor(me, j) * slabs + jnp.bitwise_xor(slab, d)
+        total = dot(cot_b[0, :, cut(at, rows)], normed_ref[3], 0, 0)
+        for r in range(3):
+            total = total + dot(cot_a[r, :, cut(at, rows)], normed_ref[r], 0, 0)
+        out_ref[part(d, rows), :] = total.astype(out_ref.dtype)
 
 
 def split_kernel(own_ref, got_ref, keep_ref, send_ref):
@@ -415,11 +414,13 @@
     tuned = dp == 2 and slabs == 4 and outputs // (dp * seq) % 8 == 0
     piece = outputs // (dp * slabs)
     if tuned:
-        keep, send = call(
-            functools.partial(product_kernel, slabs),
-            [((outputs // dp, width), F32), ((outputs // dp, width), BF16)], cots, cot_b, normed,
+        (send,) = call(
+            functools.partial(product_kernel, slabs, 1), [((outputs // dp, width), BF16)], cots, cot_b, normed
         )
         got = flip(send, "dp", dp, 1)
+        (keep,) = call(
+            functools.partial(product_kernel, slabs, 0), [((outputs // dp, width), F32)], cots, cot_b, normed
+        )
     back_far = near(back_far, bits=2)
     if tuned:
         keep, send = call(

time: 48.2 us -> 47.9 us (level)
    pallas_call x23 -> x24, Pallas kernels: 11.5 us -> 11.7 us  [__call__(): pl.pallas_call(inner, out_shape=[jax.ShapeDtypeStruct(s, d) for s, d in o...]
  transfers between devices with their start and end apart: 21 -> 21, of which waited for: 10 -> 10; matrix products, arithmetic and copies ran while one was open for 0% -> 0% of each run, Pallas kernels for 19% -> 20%
where the time goes in v18:
time: 47.9 us; the launch traced here: 47.8 us
  starting transfers between devices  25.8 us (54%)
  Pallas kernels  11.7 us (24%)
  waiting for transfers between devices  9.42 us (20%)
  between operations  0.83 us (2%)
    ppermute x21, starting transfers between devices, flip(): return lax.ppermute(x, axis, [(i, i ^ bits) for i in range(count)])  25.8 us
    pallas_call x24, Pallas kernels, __call__(): pl.pallas_call(inner, out_shape=[jax.ShapeDtypeStruct(s, d) for s, d in o...  11.7 us
    ppermute x21, waiting for transfers between devices, flip(): return lax.ppermute(x, axis, [(i, i ^ bits) for i in range(count)])  9.42 us
  transfers between devices with their start and end apart: 21, of which 10 were waited for; matrix products, arithmetic and copies ran while one was open for 0% of the time, Pallas kernels for 20%

profile of v18, /device:TPU:0, one launch (start us, length us, event | category | flops | bytes accessed | tf_op | source)
XLA Modules:
  0.0 47.8 jit_solution(11397254541885644550)
XLA Ops:
  0.7 1.6 %shard_map.92 = (f32[128,256]{1,0:T(8,128)S(1)}, bf16[128,256]{1,0:T(8,128)(2,1)S(1)}, bf16[256,256]{1,0:T(8,128)(2,1)S(1)}, bf16[2,512,256]{2,1,0:T(8,128)(2,1)S(1)}) custom-call(bf16[128,1024]{1,0:T(8,128)(2,1)} %bitcast.8, bf16[128,1024]{1,0:T(8,128)(2,1)} %bitcast.12, bf16[512,1024]{1,0:T(8,128)(2,1)} %refs_7_.1), custom_call_target="tpu_custom_call" | custom-call | flops 1 | bytes 1 | tf_op jit(solution)/shard_map/pallas_call | solution.py:42
  2.2 3.0 %collective-permute-start.1 = (bf16[256,256]{1,0:T(8,128)(2,1)S(1)}, bf16[256,256]{1,0:T(8,128)(2,1)S(1)}, u32[]{:S(2)}, u32[]{:S(2)}) collective-permute-start(bf16[256,256]{1,0:T(8,128)(2,1)S(1)} %get-tuple-element.45), channel_id=1, source_target_pairs={{0,2},{1,3},{2,0},{3,1},{4,6},{5,7},{6,4},{7,5},{8,10},{9,11},{10,... | collective-permute-start | bytes 393224 | tf_op jit(solution)/shard_map/ppermute | solution.py:60
  5.4 1.9 %collective-permute-start.8 = (bf16[2,512,256]{2,1,0:T(8,128)(2,1)S(1)}, bf16[2,512,256]{2,1,0:T(8,128)(2,1)S(1)}, u32[]{:S(2)}, u32[]{:S(2)}) collective-permute-start(bf16[2,512,256]{2,1,0:T(8,128)(2,1)S(1)} %get-tuple-element.47.refs_3_.refs_1_), channel_id=1, source_target_pairs={{0,16},{16,0},{1,17},{17,1},{2,18},{18,2},{3,19},{19,3},{4,20},{20... | collective-permute-start | bytes 1572872 | tf_op jit(solution)/shard_map/ppermute | solution.py:60
  7.3 1.4 %shard_map.93 = (bf16[4,2,128,128]{3,2,1,0:T(8,128)(2,1)S(1)}, bf16[256,256]{1,0:T(8,128)(2,1)S(1)}, bf16[1024,256]{1,0:T(8,128)(2,1)S(1)}, bf16[256,256]{1,0:T(8,128)(2,1)S(1)}) custom-call(bf16[128,1024]{1,0:T(8,128)(2,1)S(1)} %bitcast.16, bf16[128,1024]{1,0:T(8,128)(2,1)S(1)} %bitcast.9, bf16[128,1024]{1,0:T(8,128)(2,1)S(1)} %bitcast.13, ...), custom_call_target="tpu_custom_call" | custom-call | flops 1 | bytes 1 | tf_op jit(solution)/shard_map/pallas_call | solution.py:42
  8.7 0.9 %collective-permute-done.1.refs_1_.refs_4_ = bf16[256,256]{1,0:T(8,128)(2,1)S(1)} collective-permute-done((bf16[256,256]{1,0:T(8,128)(2,1)S(1)}, bf16[256,256]{1,0:T(8,128)(2,1)S(1)}, u32[]{:S(2)}, u32[]{:S(2)}) %collective-permute-start.1) | collective-permute-done | bytes 131104 | tf_op jit(solution)/shard_map/ppermute | solution.py:60
  9.7 1.3 %collective-permute-done.2.refs_2_.refs_5_ = bf16[256,256]{1,0:T(8,128)(2,1)S(1)} collective-permute-done((bf16[256,256]{1,0:T(8,128)(2,1)S(1)}, bf16[256,256]{1,0:T(8,128)(2,1)S(1)}, u32[]{:S(2)}, u32[]{:S(2)}) %collective-permute-start.2) | collective-permute-done | bytes 131104 | tf_op jit(solution)/shard_map/ppermute | solution.py:60
  11.1 2.2 %collective-permute-start.4 = (bf16[128,256]{1,0:T(8,128)(2,1)S(1)}, bf16[128,256]{1,0:T(8,128)(2,1)S(1)}, u32[]{:S(2)}, u32[]{:S(2)}) collective-permute-start(bf16[128,256]{1,0:T(8,128)(2,1)S(1)} %shard_map.95.refs_2_.refs_0_), channel_id=1, source_target_pairs={{0,4},{1,5},{2,6},{3,7},{4,0},{5,1},{6,2},{7,3},{8,12},{9,13},{10,... | collective-permute-start | bytes 196616 | tf_op jit(solution)/shard_map/ppermute | solution.py:60
  13.3 1.6 %collective-permute-start.3 = (bf16[512,256]{1,0:T(8,128)(2,1)S(1)}, bf16[512,256]{1,0:T(8,128)(2,1)S(1)}, u32[]{:S(2)}, u32[]{:S(2)}) collective-permute-start(bf16[512,256]{1,0:T(8,128)(2,1)S(1)} %shard_map.96.refs_2_), channel_id=1, source_target_pairs={{0,2},{1,3},{2,0},{3,1},{4,6},{5,7},{6,4},{7,5},{8,10},{9,11},{10,... | collective-permute-start | bytes 786440 | tf_op jit(solution)/shard_map/ppermute | solution.py:60
  14.9 0.8 %collective-permute-done.4.refs_1_.refs_0_ = bf16[128,256]{1,0:T(8,128)(2,1)S(1)} collective-permute-done((bf16[128,256]{1,0:T(8,128)(2,1)S(1)}, bf16[128,256]{1,0:T(8,128)(2,1)S(1)}, u32[]{:S(2)}, u32[]{:S(2)}) %collective-permute-start.4) | collective-permute-done | bytes 65568 | tf_op jit(solution)/shard_map/ppermute | solution.py:60
  15.7 2.9 %collective-permute-start.5 = (bf16[128,256]{1,0:T(8,128)(2,1)S(1)}, bf16[128,256]{1,0:T(8,128)(2,1)S(1)}, u32[]{:S(2)}, u32[]{:S(2)}) collective-permute-start(bf16[128,256]{1,0:T(8,128)(2,1)S(1)} %shard_map.97.refs_5_), channel_id=1, source_target_pairs={{0,8},{1,9},{2,10},{3,11},{4,12},{5,13},{6,14},{7,15},{8,0},{9,1},... | collective-permute-start | bytes 196616 | tf_op jit(solution)/shard_map/ppermute | solution.py:60
  18.7 0.4 shard_map.98
  19.3 0.2 shard_map.99
  19.5 1.7 %collective-permute-done.5.refs_1_ = bf16[128,256]{1,0:T(8,128)(2,1)S(1)} collective-permute-done((bf16[128,256]{1,0:T(8,128)(2,1)S(1)}, bf16[128,256]{1,0:T(8,128)(2,1)S(1)}, u32[]{:S(2)}, u32[]{:S(2)}) %collective-permute-start.5) | collective-permute-done | bytes 65568 | tf_op jit(solution)/shard_map/ppermute | solution.py:60
  21.4 0.8 %shard_map.101 = (bf16[4,128,256]{2,1,0:T(8,128)(2,1)S(1)}, bf16[512,256]{1,0:T(8,128)(2,1)S(1)}, bf16[512,256]{1,0:T(8,128)(2,1)S(1)}, f32[4,128,256]{2,1,0:T(8,128)S(1)}, bf16[128,256]{1,0:T(8,128)(2,1)S(1)}) custom-call(bf16[256,256]{1,0:T(8,128)(2,1)S(1)} %get-tuple-element.41.refs_0_.refs_4_, ...), custom_call_target="tpu_custom_call" | custom-call | flops 10000000000 | bytes 1 | tf_op jit(solution)/shard_map/pallas_call | solution.py:42
  22.2 0.5 %shard_map.102.refs_3_ = bf16[512,256]{1,0:T(8,128)(2,1)S(1)} custom-call(bf16[3,128,1024]{2,1,0:T(8,128)(2,1)S(1)} %get-tuple-element.53.refs_0_, bf16[1,128,1024]{2,1,0:T(8,128)(2,1)S(1)} %get-tuple-element.54.refs_1_, bf16[4,128,256]{2,1,0:T(8,128)(2,1)S(1)} %get-tuple-element.55.refs_2_, bf16[128,256]{1,0:T(8,128)(2,1)S(1)} %get-tuple-element.52.refs_3_.refs_0_), custom_call_target="tpu_custom_call" | custom-call | flops 1 | bytes 1 | tf_op jit(solution)/shard_map/pallas_call | solution.py:42
  22.7 1.5 %collective-permute-start.11 = (bf16[512,256]{1,0:T(8,128)(2,1)S(1)}, bf16[512,256]{1,0:T(8,128)(2,1)S(1)}, u32[]{:S(2)}, u32[]{:S(2)}) collective-permute-start(bf16[512,256]{1,0:T(8,128)(2,1)S(1)} %shard_map.102.refs_3_), channel_id=1, source_target_pairs={{0,16},{16,0},{1,17},{17,1},{2,18},{18,2},{3,19},{19,3},{4,20},{20... | collective-permute-start | bytes 786440 | tf_op jit(solution)/shard_map/ppermute | solution.py:60
  24.3 1.5 %collective-permute-start.9 = (bf16[512,256]{1,0:T(8,128)(2,1)S(1)}, bf16[512,256]{1,0:T(8,128)(2,1)S(1)}, u32[]{:S(2)}, u32[]{:S(2)}) collective-permute-start(bf16[512,256]{1,0:T(8,128)(2,1)S(1)} %get-tuple-element.51), channel_id=1, source_target_pairs={{0,2},{1,3},{2,0},{3,1},{4,6},{5,7},{6,4},{7,5},{8,10},{9,11},{10,... | collective-permute-start | bytes 786440 | tf_op jit(solution)/shard_map/ppermute | solution.py:60
  25.8 1.4 %collective-permute-start.10 = (bf16[128,256]{1,0:T(8,128)(2,1)S(1)}, bf16[128,256]{1,0:T(8,128)(2,1)S(1)}, u32[]{:S(2)}, u32[]{:S(2)}) collective-permute-start(bf16[128,256]{1,0:T(8,128)(2,1)S(1)} %get-tuple-element.52.refs_3_.refs_0_), channel_id=1, source_target_pairs={{0,4},{1,5},{2,6},{3,7},{4,0},{5,1},{6,2},{7,3},{8,12},{9,13},{10,... | collective-permute-start | bytes 196616 | tf_op jit(solution)/shard_map/ppermute | solution.py:60
  27.2 0.5 %shard_map.103.refs_0_.refs_2_ = f32[512,256]{1,0:T(8,128)S(1)} custom-call(bf16[3,128,1024]{2,1,0:T(8,128)(2,1)S(1)} %get-tuple-element.53.refs_0_, bf16[1,128,1024]{2,1,0:T(8,128)(2,1)S(1)} %get-tuple-element.54.refs_1_, bf16[4,128,256]{2,1,0:T(8,128)(2,1)S(1)} %get-tuple-element.55.refs_2_, bf16[512,256]{1,0:T(8,128)(2,1)S(1)} %shard_map.102.refs_3_), custom_call_target="tpu_custom_call" | custom-call | flops 1 | bytes 1 | tf_op jit(solution)/shard_map/pallas_call | solution.py:42
  27.7 2.3 %collective-permute-done.11.refs_1_ = bf16[512,256]{1,0:T(8,128)(2,1)S(1)} collective-permute-done((bf16[512,256]{1,0:T(8,128)(2,1)S(1)}, bf16[512,256]{1,0:T(8,128)(2,1)S(1)}, u32[]{:S(2)}, u32[]{:S(2)}) %collective-permute-start.11) | collective-permute-done | bytes 262176 | tf_op jit(solution)/shard_map/ppermute | solution.py:60
  30.0 1.4 %collective-permute-start.15 = (bf16[256,256]{1,0:T(8,128)(2,1)S(1)}, bf16[256,256]{1,0:T(8,128)(2,1)S(1)}, u32[]{:S(2)}, u32[]{:S(2)}) collective-permute-start(bf16[256,256]{1,0:T(8,128)(2,1)S(1)} %get-tuple-element.57.refs_2_), channel_id=1, source_target_pairs={{0,4},{1,5},{2,6},{3,7},{4,0},{5,1},{6,2},{7,3},{8,12},{9,13},{10,... | collective-permute-start | bytes 393224 | tf_op jit(solution)/shard_map/ppermute | solution.py:60
  31.5 2.7 %collective-permute-start.14 = (bf16[128,256]{1,0:T(8,128)(2,1)S(1)}, bf16[128,256]{1,0:T(8,128)(2,1)S(1)}, u32[]{:S(2)}, u32[]{:S(2)}) collective-permute-start(bf16[128,256]{1,0:T(8,128)(2,1)S(1)} %shard_map.105.refs_2_), channel_id=1, source_target_pairs={{0,8},{1,9},{2,10},{3,11},{4,12},{5,13},{6,14},{7,15},{8,0},{9,1},... | collective-permute-start | bytes 196616 | tf_op jit(solution)/shard_map/ppermute | solution.py:60
  34.3 0.8 %collective-permute-done.15.refs_1_ = bf16[256,256]{1,0:T(8,128)(2,1)S(1)} collective-permute-done((bf16[256,256]{1,0:T(8,128)(2,1)S(1)}, bf16[256,256]{1,0:T(8,128)(2,1)S(1)}, u32[]{:S(2)}, u32[]{:S(2)}) %collective-permute-start.15) | collective-permute-done | bytes 131104 | tf_op jit(solution)/shard_map/ppermute | solution.py:60
  35.1 2.7 %collective-permute-start.17 = (bf16[128,256]{1,0:T(8,128)(2,1)S(1)}, bf16[128,256]{1,0:T(8,128)(2,1)S(1)}, u32[]{:S(2)}, u32[]{:S(2)}) collective-permute-start(bf16[128,256]{1,0:T(8,128)(2,1)S(1)} %get-tuple-element.60.refs_3_), channel_id=1, source_target_pairs={{0,8},{1,9},{2,10},{3,11},{4,12},{5,13},{6,14},{7,15},{8,0},{9,1},... | collective-permute-start | bytes 196616 | tf_op jit(solution)/shard_map/ppermute | solution.py:60
  37.9 1.6 %collective-permute-start.16 = (bf16[256,256]{1,0:T(8,128)(2,1)S(1)}, bf16[256,256]{1,0:T(8,128)(2,1)S(1)}, u32[]{:S(2)}, u32[]{:S(2)}) collective-permute-start(bf16[256,256]{1,0:T(8,128)(2,1)S(1)} %get-tuple-element.62.refs_7_), channel_id=1, source_target_pairs={{0,2},{1,3},{2,0},{3,1},{4,6},{5,7},{6,4},{7,5},{8,10},{9,11},{10,... | collective-permute-start | bytes 393224 | tf_op jit(solution)/shard_map/ppermute | solution.py:60
  39.5 2.1 %shard_map.109 = (bf16[128,1024]{1,0:T(8,128)(2,1)}, f32[4,128,256]{2,1,0:T(8,128)S(1)}, f32[4,128,256]{2,1,0:T(8,128)S(1)}) custom-call(bf16[512,256]{1,0:T(8,128)(2,1)S(1)} %get-tuple-element.50.refs_0_, bf16[512,256]{1,0:T(8,128)(2,1)S(1)} %collective-permute-done.9.refs_1_, bf16[512,256]{1,0:T(8,128)(2,1)S(1)} %collective-permute-done.13.refs_2_, ...), custom_call_target="tpu_custom_call" | custom-call | flops 1 | bytes 1 | tf_op jit(solution)/shard_map/pallas_call | solution.py:42
  41.6 0.6 %collective-permute-start.19 = (bf16[64,256]{1,0:T(8,128)(2,1)S(1)}, bf16[64,256]{1,0:T(8,128)(2,1)S(1)}, u32[]{:S(2)}, u32[]{:S(2)}) collective-permute-start(bf16[64,256]{1,0:T(8,128)(2,1)S(1)} %get-tuple-element.66.refs_2_), channel_id=1, source_target_pairs={{0,2},{1,3},{2,0},{3,1},{4,6},{5,7},{6,4},{7,5},{8,10},{9,11},{10,... | collective-permute-start | bytes 98312 | tf_op jit(solution)/shard_map/ppermute | solution.py:60
  42.2 1.1 %collective-permute-done.16.refs_1_ = bf16[256,256]{1,0:T(8,128)(2,1)S(1)} collective-permute-done((bf16[256,256]{1,0:T(8,128)(2,1)S(1)}, bf16[256,256]{1,0:T(8,128)(2,1)S(1)}, u32[]{:S(2)}, u32[]{:S(2)}) %collective-permute-start.16) | collective-permute-done | bytes 131104 | tf_op jit(solution)/shard_map/ppermute | solution.py:60
  43.3 2.1 %shard_map.112 = (bf16[128,1024]{1,0:T(8,128)(2,1)}, bf16[128,1024]{1,0:T(8,128)(2,1)}) custom-call(bf16[512,256]{1,0:T(8,128)(2,1)S(1)} %get-tuple-element.50.refs_0_, bf16[512,256]{1,0:T(8,128)(2,1)S(1)} %collective-permute-done.9.refs_1_, bf16[512,256]{1,0:T(8,128)(2,1)S(1)} %collective-permute-done.13.refs_2_, bf16[128,1024]{1,0:T(8,128)(2,1)S(1)} %bitcast.18, ...), custom_call_target="tpu_custom_call" | custom-call | flops 1 | bytes 1 | tf_op jit(solution)/shard_map/pallas_call | solution.py:42
  45.6 0.4 collective-permute-start.20
  46.0 1.1 %shard_map.114 = (bf16[128,1024]{1,0:T(8,128)(2,1)}, bf16[128,1024]{1,0:T(8,128)(2,1)}) custom-call(bf16[256,256]{1,0:T(8,128)(2,1)S(1)} %get-tuple-element.61.refs_0_, bf16[256,256]{1,0:T(8,128)(2,1)S(1)} %collective-permute-done.16.refs_1_, bf16[256,256]{1,0:T(8,128)(2,1)S(1)} %collective-permute-done.18.refs_2_, bf16[128,1024]{1,0:T(8,128)(2,1)S(1)} %bitcast.11, ...), custom_call_target="tpu_custom_call" | custom-call | flops 1 | bytes 1 | tf_op jit(solution)/shard_map/pallas_call | solution.py:42
  47.1 0.7 %shard_map.115 = f32[32,1024]{1,0:T(8,128)} custom-call(bf16[64,256]{1,0:T(8,128)(2,1)S(1)} %get-tuple-element.74.refs_0_, bf16[64,256]{1,0:T(8,128)(2,1)S(1)} %collective-permute-done.20.refs_1_, bf16[64,256]{1,0:T(8,128)(2,1)S(1)} %get-tuple-element.71.refs_7_.refs_2_, bf16[128,1024]{1,0:T(8,128)(2,1)} %get-tuple-element.72.refs_3_), custom_call_target="tpu_custom_call" | custom-call | flops 1 | bytes 1 | tf_op jit(solution)/shard_map/pallas_call | solution.py:42
  (44 shorter events, 1.3 us)
Async XLA Ops:
  0.6 4.6 %copy-start.4 = (bf16[1,128,1024]{2,1,0:T(8,128)(2,1)S(1)}, bf16[1,128,1024]{2,1,0:T(8,128)(2,1)}, u32[]{:S(2)}) copy-start(bf16[1,128,1024]{2,1,0:T(8,128)(2,1)} %param.8) | copy-start | bytes 786436
  0.6 6.6 %copy-start = (bf16[1,128,1024]{2,1,0:T(8,128)(2,1)S(1)}, bf16[1,128,1024]{2,1,0:T(8,128)(2,1)}, u32[]{:S(2)}) copy-start(bf16[1,128,1024]{2,1,0:T(8,128)(2,1)} %param.6) | copy-start | bytes 786436
  0.7 6.6 %copy-start.1 = (bf16[1,128,1024]{2,1,0:T(8,128)(2,1)S(1)}, bf16[1,128,1024]{2,1,0:T(8,128)(2,1)}, u32[]{:S(2)}) copy-start(bf16[1,128,1024]{2,1,0:T(8,128)(2,1)} %param.7) | copy-start | bytes 786436
  0.7 6.6 %copy-start.3 = (bf16[1,128,1024]{2,1,0:T(8,128)(2,1)S(1)}, bf16[1,128,1024]{2,1,0:T(8,128)(2,1)}, u32[]{:S(2)}) copy-start(bf16[1,128,1024]{2,1,0:T(8,128)(2,1)} %param.5) | copy-start | bytes 786436
  2.2 7.4 %collective-permute-start.1 = (bf16[256,256]{1,0:T(8,128)(2,1)S(1)}, bf16[256,256]{1,0:T(8,128)(2,1)S(1)}, u32[]{:S(2)}, u32[]{:S(2)}) collective-permute-start(bf16[256,256]{1,0:T(8,128)(2,1)S(1)} %get-tuple-element.45), channel_id=1, source_target_pairs={{0,2},{1,3},{2,0},{3,1},{4,6},{5,7},{6,4},{7,5},{8,10},{9,11},{10,... | collective-permute-start | bytes 393224 | tf_op jit(solution)/shard_map/ppermute | solution.py:60
  5.3 9.6 %collective-permute-start.6 = (bf16[128,1024]{1,0:T(8,128)(2,1)S(1)}, bf16[128,1024]{1,0:T(8,128)(2,1)S(1)}, u32[]{:S(2)}, u32[]{:S(2)}) collective-permute-start(bf16[128,1024]{1,0:T(8,128)(2,1)S(1)} %bitcast.19), channel_id=1, source_target_pairs={{0,2},{1,3},{2,0},{3,1},{4,6},{5,7},{6,4},{7,5},{8,10},{9,11},{10,... | collective-permute-start | bytes 786440 | tf_op jit(solution)/shard_map/ppermute | solution.py:60
  5.4 13.4 %collective-permute-start.8 = (bf16[2,512,256]{2,1,0:T(8,128)(2,1)S(1)}, bf16[2,512,256]{2,1,0:T(8,128)(2,1)S(1)}, u32[]{:S(2)}, u32[]{:S(2)}) collective-permute-start(bf16[2,512,256]{2,1,0:T(8,128)(2,1)S(1)} %get-tuple-element.47.refs_3_.refs_1_), channel_id=1, source_target_pairs={{0,16},{16,0},{1,17},{17,1},{2,18},{18,2},{3,19},{19,3},{4,20},{20... | collective-permute-start | bytes 1572872 | tf_op jit(solution)/shard_map/ppermute | solution.py:60
  8.6 4.6 %collective-permute-start = (bf16[1024,256]{1,0:T(8,128)(2,1)S(1)}, bf16[1024,256]{1,0:T(8,128)(2,1)S(1)}, u32[]{:S(2)}, u32[]{:S(2)}) collective-permute-start(bf16[1024,256]{1,0:T(8,128)(2,1)S(1)} %get-tuple-element.42.refs_5_), channel_id=1, source_target_pairs={{0,1},{1,0},{2,3},{3,2},{4,5},{5,4},{6,7},{7,6},{8,9},{9,8},{10,11... | collective-permute-start | bytes 1572872 | tf_op jit(solution)/shard_map/ppermute | solution.py:60
  9.6 1.4 %collective-permute-start.2 = (bf16[256,256]{1,0:T(8,128)(2,1)S(1)}, bf16[256,256]{1,0:T(8,128)(2,1)S(1)}, u32[]{:S(2)}, u32[]{:S(2)}) collective-permute-start(bf16[256,256]{1,0:T(8,128)(2,1)S(1)} %shard_map.94.refs_3_), channel_id=1, source_target_pairs={{0,1},{1,0},{2,3},{3,2},{4,5},{5,4},{6,7},{7,6},{8,9},{9,8},{10,11... | collective-permute-start | bytes 393224 | tf_op jit(solution)/shard_map/ppermute | solution.py:60
  11.1 4.6 %collective-permute-start.4 = (bf16[128,256]{1,0:T(8,128)(2,1)S(1)}, bf16[128,256]{1,0:T(8,128)(2,1)S(1)}, u32[]{:S(2)}, u32[]{:S(2)}) collective-permute-start(bf16[128,256]{1,0:T(8,128)(2,1)S(1)} %shard_map.95.refs_2_.refs_0_), channel_id=1, source_target_pairs={{0,4},{1,5},{2,6},{3,7},{4,0},{5,1},{6,2},{7,3},{8,12},{9,13},{10,... | collective-permute-start | bytes 196616 | tf_op jit(solution)/shard_map/ppermute | solution.py:60
  13.3 8.1 %collective-permute-start.3 = (bf16[512,256]{1,0:T(8,128)(2,1)S(1)}, bf16[512,256]{1,0:T(8,128)(2,1)S(1)}, u32[]{:S(2)}, u32[]{:S(2)}) collective-permute-start(bf16[512,256]{1,0:T(8,128)(2,1)S(1)} %shard_map.96.refs_2_), channel_id=1, source_target_pairs={{0,2},{1,3},{2,0},{3,1},{4,6},{5,7},{6,4},{7,5},{8,10},{9,11},{10,... | collective-permute-start | bytes 786440 | tf_op jit(solution)/shard_map/ppermute | solution.py:60
  14.9 4.4 %collective-permute-start.7 = (bf16[128,1024]{1,0:T(8,128)(2,1)S(1)}, bf16[128,1024]{1,0:T(8,128)(2,1)S(1)}, u32[]{:S(2)}, u32[]{:S(2)}) collective-permute-start(bf16[128,1024]{1,0:T(8,128)(2,1)S(1)} %collective-permute-done.6.refs_2_), channel_id=1, source_target_pairs={{0,1},{1,0},{2,3},{3,2},{4,5},{5,4},{6,7},{7,6},{8,9},{9,8},{10,11... | collective-permute-start | bytes 786440 | tf_op jit(solution)/shard_map/ppermute | solution.py:60
  15.7 5.6 %collective-permute-start.5 = (bf16[128,256]{1,0:T(8,128)(2,1)S(1)}, bf16[128,256]{1,0:T(8,128)(2,1)S(1)}, u32[]{:S(2)}, u32[]{:S(2)}) collective-permute-start(bf16[128,256]{1,0:T(8,128)(2,1)S(1)} %shard_map.97.refs_5_), channel_id=1, source_target_pairs={{0,8},{1,9},{2,10},{3,11},{4,12},{5,13},{6,14},{7,15},{8,0},{9,1},... | collective-permute-start | bytes 196616 | tf_op jit(solution)/shard_map/ppermute | solution.py:60
  19.2 10.8 %collective-permute-start.12 = (bf16[2,512,256]{2,1,0:T(8,128)(2,1)S(1)}, bf16[2,512,256]{2,1,0:T(8,128)(2,1)S(1)}, u32[]{:S(2)}, u32[]{:S(2)}) collective-permute-start(bf16[2,512,256]{2,1,0:T(8,128)(2,1)S(1)} %collective-permute-done.8.refs_4_.refs_2_.refs_8_), channel_id=1, source_target_pairs={{0,1},{1,0},{2,3},{3,2},{4,5},{5,4},{6,7},{7,6},{8,9},{9,8},{10,11... | collective-permute-start | bytes 1572872 | tf_op jit(solution)/shard_map/ppermute | solution.py:60
  22.7 7.3 %collective-permute-start.11 = (bf16[512,256]{1,0:T(8,128)(2,1)S(1)}, bf16[512,256]{1,0:T(8,128)(2,1)S(1)}, u32[]{:S(2)}, u32[]{:S(2)}) collective-permute-start(bf16[512,256]{1,0:T(8,128)(2,1)S(1)} %shard_map.102.refs_3_), channel_id=1, source_target_pairs={{0,16},{16,0},{1,17},{17,1},{2,18},{18,2},{3,19},{19,3},{4,20},{20... | collective-permute-start | bytes 786440 | tf_op jit(solution)/shard_map/ppermute | solution.py:60
  24.3 9.9 %collective-permute-start.9 = (bf16[512,256]{1,0:T(8,128)(2,1)S(1)}, bf16[512,256]{1,0:T(8,128)(2,1)S(1)}, u32[]{:S(2)}, u32[]{:S(2)}) collective-permute-start(bf16[512,256]{1,0:T(8,128)(2,1)S(1)} %get-tuple-element.51), channel_id=1, source_target_pairs={{0,2},{1,3},{2,0},{3,1},{4,6},{5,7},{6,4},{7,5},{8,10},{9,11},{10,... | collective-permute-start | bytes 786440 | tf_op jit(solution)/shard_map/ppermute | solution.py:60
  25.8 5.7 %collective-permute-start.10 = (bf16[128,256]{1,0:T(8,128)(2,1)S(1)}, bf16[128,256]{1,0:T(8,128)(2,1)S(1)}, u32[]{:S(2)}, u32[]{:S(2)}) collective-permute-start(bf16[128,256]{1,0:T(8,128)(2,1)S(1)} %get-tuple-element.52.refs_3_.refs_0_), channel_id=1, source_target_pairs={{0,4},{1,5},{2,6},{3,7},{4,0},{5,1},{6,2},{7,3},{8,12},{9,13},{10,... | collective-permute-start | bytes 196616 | tf_op jit(solution)/shard_map/ppermute | solution.py:60
  30.0 5.0 %collective-permute-start.15 = (bf16[256,256]{1,0:T(8,128)(2,1)S(1)}, bf16[256,256]{1,0:T(8,128)(2,1)S(1)}, u32[]{:S(2)}, u32[]{:S(2)}) collective-permute-start(bf16[256,256]{1,0:T(8,128)(2,1)S(1)} %get-tuple-element.57.refs_2_), channel_id=1, source_target_pairs={{0,4},{1,5},{2,6},{3,7},{4,0},{5,1},{6,2},{7,3},{8,12},{9,13},{10,... | collective-permute-start | bytes 393224 | tf_op jit(solution)/shard_map/ppermute | solution.py:60
  31.5 6.3 %collective-permute-start.14 = (bf16[128,256]{1,0:T(8,128)(2,1)S(1)}, bf16[128,256]{1,0:T(8,128)(2,1)S(1)}, u32[]{:S(2)}, u32[]{:S(2)}) collective-permute-start(bf16[128,256]{1,0:T(8,128)(2,1)S(1)} %shard_map.105.refs_2_), channel_id=1, source_target_pairs={{0,8},{1,9},{2,10},{3,11},{4,12},{5,13},{6,14},{7,15},{8,0},{9,1},... | collective-permute-start | bytes 196616 | tf_op jit(solution)/shard_map/ppermute | solution.py:60
  34.2 5.3 %collective-permute-start.13 = (bf16[512,256]{1,0:T(8,128)(2,1)S(1)}, bf16[512,256]{1,0:T(8,128)(2,1)S(1)}, u32[]{:S(2)}, u32[]{:S(2)}) collective-permute-start(bf16[512,256]{1,0:T(8,128)(2,1)S(1)} %shard_map.106.refs_2_), channel_id=1, source_target_pairs={{0,1},{1,0},{2,3},{3,2},{4,5},{5,4},{6,7},{7,6},{8,9},{9,8},{10,11... | collective-permute-start | bytes 786440 | tf_op jit(solution)/shard_map/ppermute | solution.py:60
  35.1 6.5 %collective-permute-start.17 = (bf16[128,256]{1,0:T(8,128)(2,1)S(1)}, bf16[128,256]{1,0:T(8,128)(2,1)S(1)}, u32[]{:S(2)}, u32[]{:S(2)}) collective-permute-start(bf16[128,256]{1,0:T(8,128)(2,1)S(1)} %get-tuple-element.60.refs_3_), channel_id=1, source_target_pairs={{0,8},{1,9},{2,10},{3,11},{4,12},{5,13},{6,14},{7,15},{8,0},{9,1},... | collective-permute-start | bytes 196616 | tf_op jit(solution)/shard_map/ppermute | solution.py:60
  37.9 5.3 %collective-permute-start.16 = (bf16[256,256]{1,0:T(8,128)(2,1)S(1)}, bf16[256,256]{1,0:T(8,128)(2,1)S(1)}, u32[]{:S(2)}, u32[]{:S(2)}) collective-permute-start(bf16[256,256]{1,0:T(8,128)(2,1)S(1)} %get-tuple-element.62.refs_7_), channel_id=1, source_target_pairs={{0,2},{1,3},{2,0},{3,1},{4,6},{5,7},{6,4},{7,5},{8,10},{9,11},{10,... | collective-permute-start | bytes 393224 | tf_op jit(solution)/shard_map/ppermute | solution.py:60
  41.6 1.8 %copy-start.2 = (bf16[512,1024]{1,0:T(8,128)(2,1)S(1)}, bf16[512,1024]{1,0:T(8,128)(2,1)}, u32[]{:S(2)}) copy-start(bf16[512,1024]{1,0:T(8,128)(2,1)} %refs_7_.1) | copy-start | bytes 3145732
  41.6 4.0 %collective-permute-start.19 = (bf16[64,256]{1,0:T(8,128)(2,1)S(1)}, bf16[64,256]{1,0:T(8,128)(2,1)S(1)}, u32[]{:S(2)}, u32[]{:S(2)}) collective-permute-start(bf16[64,256]{1,0:T(8,128)(2,1)S(1)} %get-tuple-element.66.refs_2_), channel_id=1, source_target_pairs={{0,2},{1,3},{2,0},{3,1},{4,6},{5,7},{6,4},{7,5},{8,10},{9,11},{10,... | collective-permute-start | bytes 98312 | tf_op jit(solution)/shard_map/ppermute | solution.py:60
  43.2 2.7 %collective-permute-start.18 = (bf16[256,256]{1,0:T(8,128)(2,1)S(1)}, bf16[256,256]{1,0:T(8,128)(2,1)S(1)}, u32[]{:S(2)}, u32[]{:S(2)}) collective-permute-start(bf16[256,256]{1,0:T(8,128)(2,1)S(1)} %shard_map.111.refs_10_.refs_2_), channel_id=1, source_target_pairs={{0,1},{1,0},{2,3},{3,2},{4,5},{5,4},{6,7},{7,6},{8,9},{9,8},{10,11... | collective-permute-start | bytes 393224 | tf_op jit(solution)/shard_map/ppermute | solution.py:60
  45.6 1.5 %collective-permute-start.20 = (bf16[64,256]{1,0:T(8,128)(2,1)S(1)}, bf16[64,256]{1,0:T(8,128)(2,1)S(1)}, u32[]{:S(2)}, u32[]{:S(2)}) collective-permute-start(bf16[64,256]{1,0:T(8,128)(2,1)S(1)} %get-tuple-element.71.refs_7_.refs_2_), channel_id=1, source_target_pairs={{0,1},{1,0},{2,3},{3,2},{4,5},{5,4},{6,7},{7,6},{8,9},{9,8},{10,11... | collective-permute-start | bytes 98312 | tf_op jit(solution)/shard_map/ppermute | solution.py:60

commit v19 on v18

--- a/solution.py
+++ b/solution.py
@@ -172,11 +172,11 @@
     return total
 
 
-def middle_kernel(*refs):
-    own_ref, message_ref, token_far, own_state, far_state, near_state, base_ref, dnormed_a, dnormed_b = refs[:9]
-    normed_ref, back_near, back_far, u_ref, slab_ref, running = refs[9:]
+def mixed_kernel(
+    own_ref, message_ref, token_far, own_state, far_state, near_state, base_ref,
+    normed_ref, mixed_ref, prior_ref, running,
+):
     _, block, width = normed_ref.shape
-    heads = width // DH
     size = 2 * block
     tokens = (own_ref, message_ref.at[:size], token_far.at[:size], token_far.at[size:])
     running[member(0)] = own_state[...]
@@ -186,25 +186,40 @@
     total = base_ref[...]
     for p in range(SLAB):
         total, running[p] = total + running[p], total
-    sums = [jnp.zeros((DH, DH), F32)] * heads
-    for r in range(SLAB):
-        out = (back_near, back_far)[r // 2].at[part(r % 2, block + DH)]
+    for r in range(SLAB):
         prior = running[member(r)].astype(BF16)
-        out[block:, :] = prior
-        for h in range(heads):
+        prior_ref[r] = prior
+        for h in range(width // DH):
             q = tokens[r][:block, head(h)]
             mixed = tokens[r][block:, head(h)].astype(F32) + dot(q, prior[:, head(h)], 1, 0)
             scale = lax.rsqrt(jnp.mean(mixed * mixed, axis=-1, keepdims=True) + EPSILON)
+            mixed_ref[r, :, head(h)] = mixed
+            normed_ref[r, :, head(h)] = (mixed * scale).astype(BF16)
+
+
+def middle_kernel(
+    own_ref, message_ref, token_far, mixed_ref, prior_ref, dnormed_a, dnormed_b,
+    near_ref, far_ref, u_ref, slab_ref,
+):
+    _, block, width = mixed_ref.shape
+    size = 2 * block
+    tokens = (own_ref, message_ref.at[:size], token_far.at[:size], token_far.at[size:])
+    sums = [jnp.zeros((DH, DH), F32)] * (width // DH)
+    for r in range(SLAB):
+        out = (near_ref, far_ref)[r // 2].at[part(r % 2, block + DH)]
+        out[block:, :] = prior_ref[r]
+        for h in range(width // DH):
+            mixed = mixed_ref[r, :, head(h)]
+            scale = lax.rsqrt(jnp.mean(mixed * mixed, axis=-1, keepdims=True) + EPSILON)
             normed = mixed * scale
-            normed_ref[r, :, head(h)] = normed.astype(BF16)
             dnormed = dnormed_a[r, :, head(h)] if r < 3 else dnormed_b[0, :, head(h)]
             along = jnp.mean(dnormed * normed, axis=-1, keepdims=True)
             dmixed = ((dnormed - normed * along) * scale).astype(BF16)
             out[:block, head(h)] = dmixed
-            u = dot(q, dmixed, 0, 0)
+            u = dot(tokens[r][:block, head(h)], dmixed, 0, 0)
             u_ref[r, :, head(h)] = u
             sums[h] = sums[h] + u
-    for h in range(heads):
+    for h in range(width // DH):
         slab_ref[:, head(h)] = sums[h].astype(BF16)
 
 
@@ -404,12 +419,12 @@
     )
     (base,) = call(base_kernel, [((DH, width), F32)], *before, cost=10**9)
     w_all = [x for w in w_far for x in (w, near(after(w, dnormed), bits=1))]
-    normed, back, back_far, u, slab_u = call(
-        middle_kernel,
-        [((SLAB, rows, width), BF16)] + [((2 * rows + 2 * DH, width), BF16)] * 2
-        + [((SLAB, DH, width), F32), ((DH, width), BF16)],
-        own_tokens, message, far_tokens, own_state, far_state, near_state, base, dnormed, dnormed_b,
-        cost=10**10, scratch=[pltpu.VMEM((SLAB, DH, width), F32)],
+    tokens = (own_tokens, message, far_tokens)
+    normed, mixed, prior = call(
+        mixed_kernel,
+        [((SLAB, rows, width), BF16), ((SLAB, rows, width), F32), ((SLAB, DH, width), BF16)],
+        *tokens, own_state, far_state, near_state, base, cost=10**10,
+        scratch=[pltpu.VMEM((SLAB, DH, width), F32)],
     )
     tuned = dp == 2 and slabs == 4 and outputs // (dp * seq) % 8 == 0
     piece = outputs // (dp * slabs)
@@ -418,6 +433,12 @@
             functools.partial(product_kernel, slabs, 1), [((outputs // dp, width), BF16)], cots, cot_b, normed
         )
         got = flip(send, "dp", dp, 1)
+    back, back_far, u, slab_u = call(
+        middle_kernel,
+        [((2 * rows + 2 * DH, width), BF16)] * 2 + [((SLAB, DH, width), F32), ((DH, width), BF16)],
+        *tokens, mixed, prior, dnormed, dnormed_b,
+    )
+    if tuned:
         (keep,) = call(
             functools.partial(product_kernel, slabs, 0), [((outputs // dp, width), F32)], cots, cot_b, normed
         )

time: 47.9 us -> 47.7 us (level)
    pallas_call x24 -> x25, Pallas kernels: 11.7 us -> 12 us  [__call__(): pl.pallas_call(inner, out_shape=[jax.ShapeDtypeStruct(s, d) for s, d in o...]
  transfers between devices with their start and end apart: 21 -> 21, of which waited for: 10 -> 11; matrix products, arithmetic and copies ran while one was open for 0% -> 0% of each run, Pallas kernels for 20% -> 21%
where the time goes in v19:
time: 47.7 us; the launch traced here: 47.5 us
  starting transfers between devices  25.6 us (54%)
  Pallas kernels  12 us (25%)
  waiting for transfers between devices  9 us (19%)
  between operations  0.84 us (2%)
    ppermute x21, starting transfers between devices, flip(): return lax.ppermute(x, axis, [(i, i ^ bits) for i in range(count)])  25.6 us
    pallas_call x25, Pallas kernels, __call__(): pl.pallas_call(inner, out_shape=[jax.ShapeDtypeStruct(s, d) for s, d in o...  12 us
    ppermute x21, waiting for transfers between devices, flip(): return lax.ppermute(x, axis, [(i, i ^ bits) for i in range(count)])  9 us
  transfers between devices with their start and end apart: 21, of which 11 were waited for; matrix products, arithmetic and copies ran while one was open for 0% of the time, Pallas kernels for 21%

profile of v19, /device:TPU:0, one launch (start us, length us, event | category | flops | bytes accessed | tf_op | source)
XLA Modules:
  0.0 47.5 jit_solution(7010914999864358214)
XLA Ops:
  0.7 1.6 %shard_map.92 = (f32[128,256]{1,0:T(8,128)S(1)}, bf16[128,256]{1,0:T(8,128)(2,1)S(1)}, bf16[256,256]{1,0:T(8,128)(2,1)S(1)}, bf16[2,512,256]{2,1,0:T(8,128)(2,1)S(1)}) custom-call(bf16[128,1024]{1,0:T(8,128)(2,1)} %bitcast.8, bf16[128,1024]{1,0:T(8,128)(2,1)} %bitcast.12, bf16[512,1024]{1,0:T(8,128)(2,1)} %refs_7_.1), custom_call_target="tpu_custom_call" | custom-call | flops 1 | bytes 1 | tf_op jit(solution)/shard_map/pallas_call | solution.py:42
  2.2 3.0 %collective-permute-start.1 = (bf16[256,256]{1,0:T(8,128)(2,1)S(1)}, bf16[256,256]{1,0:T(8,128)(2,1)S(1)}, u32[]{:S(2)}, u32[]{:S(2)}) collective-permute-start(bf16[256,256]{1,0:T(8,128)(2,1)S(1)} %get-tuple-element.47), channel_id=1, source_target_pairs={{0,2},{1,3},{2,0},{3,1},{4,6},{5,7},{6,4},{7,5},{8,10},{9,11},{10,... | collective-permute-start | bytes 393224 | tf_op jit(solution)/shard_map/ppermute | solution.py:60
  5.4 1.9 %collective-permute-start.8 = (bf16[2,512,256]{2,1,0:T(8,128)(2,1)S(1)}, bf16[2,512,256]{2,1,0:T(8,128)(2,1)S(1)}, u32[]{:S(2)}, u32[]{:S(2)}) collective-permute-start(bf16[2,512,256]{2,1,0:T(8,128)(2,1)S(1)} %get-tuple-element.49.refs_3_.refs_1_), channel_id=1, source_target_pairs={{0,16},{16,0},{1,17},{17,1},{2,18},{18,2},{3,19},{19,3},{4,20},{20... | collective-permute-start | bytes 1572872 | tf_op jit(solution)/shard_map/ppermute | solution.py:60
  7.3 1.4 %shard_map.93 = (bf16[4,2,128,128]{3,2,1,0:T(8,128)(2,1)S(1)}, bf16[256,256]{1,0:T(8,128)(2,1)S(1)}, bf16[1024,256]{1,0:T(8,128)(2,1)S(1)}, bf16[256,256]{1,0:T(8,128)(2,1)S(1)}) custom-call(bf16[128,1024]{1,0:T(8,128)(2,1)S(1)} %bitcast.16, bf16[128,1024]{1,0:T(8,128)(2,1)S(1)} %bitcast.9, bf16[128,1024]{1,0:T(8,128)(2,1)S(1)} %bitcast.13, ...), custom_call_target="tpu_custom_call" | custom-call | flops 1 | bytes 1 | tf_op jit(solution)/shard_map/pallas_call | solution.py:42
  8.7 0.9 %collective-permute-done.1.refs_1_.refs_4_ = bf16[256,256]{1,0:T(8,128)(2,1)S(1)} collective-permute-done((bf16[256,256]{1,0:T(8,128)(2,1)S(1)}, bf16[256,256]{1,0:T(8,128)(2,1)S(1)}, u32[]{:S(2)}, u32[]{:S(2)}) %collective-permute-start.1) | collective-permute-done | bytes 131104 | tf_op jit(solution)/shard_map/ppermute | solution.py:60
  9.7 1.3 %collective-permute-done.2.refs_2_.refs_5_ = bf16[256,256]{1,0:T(8,128)(2,1)S(1)} collective-permute-done((bf16[256,256]{1,0:T(8,128)(2,1)S(1)}, bf16[256,256]{1,0:T(8,128)(2,1)S(1)}, u32[]{:S(2)}, u32[]{:S(2)}) %collective-permute-start.2) | collective-permute-done | bytes 131104 | tf_op jit(solution)/shard_map/ppermute | solution.py:60
  11.1 2.2 %collective-permute-start.4 = (bf16[128,256]{1,0:T(8,128)(2,1)S(1)}, bf16[128,256]{1,0:T(8,128)(2,1)S(1)}, u32[]{:S(2)}, u32[]{:S(2)}) collective-permute-start(bf16[128,256]{1,0:T(8,128)(2,1)S(1)} %shard_map.95.refs_2_.refs_0_), channel_id=1, source_target_pairs={{0,4},{1,5},{2,6},{3,7},{4,0},{5,1},{6,2},{7,3},{8,12},{9,13},{10,... | collective-permute-start | bytes 196616 | tf_op jit(solution)/shard_map/ppermute | solution.py:60
  13.3 1.6 %collective-permute-start.3 = (bf16[512,256]{1,0:T(8,128)(2,1)S(1)}, bf16[512,256]{1,0:T(8,128)(2,1)S(1)}, u32[]{:S(2)}, u32[]{:S(2)}) collective-permute-start(bf16[512,256]{1,0:T(8,128)(2,1)S(1)} %shard_map.96.refs_2_), channel_id=1, source_target_pairs={{0,2},{1,3},{2,0},{3,1},{4,6},{5,7},{6,4},{7,5},{8,10},{9,11},{10,... | collective-permute-start | bytes 786440 | tf_op jit(solution)/shard_map/ppermute | solution.py:60
  14.9 0.8 %collective-permute-done.4.refs_1_.refs_0_ = bf16[128,256]{1,0:T(8,128)(2,1)S(1)} collective-permute-done((bf16[128,256]{1,0:T(8,128)(2,1)S(1)}, bf16[128,256]{1,0:T(8,128)(2,1)S(1)}, u32[]{:S(2)}, u32[]{:S(2)}) %collective-permute-start.4) | collective-permute-done | bytes 65568 | tf_op jit(solution)/shard_map/ppermute | solution.py:60
  15.7 2.9 %collective-permute-start.5 = (bf16[128,256]{1,0:T(8,128)(2,1)S(1)}, bf16[128,256]{1,0:T(8,128)(2,1)S(1)}, u32[]{:S(2)}, u32[]{:S(2)}) collective-permute-start(bf16[128,256]{1,0:T(8,128)(2,1)S(1)} %shard_map.97.refs_5_), channel_id=1, source_target_pairs={{0,8},{1,9},{2,10},{3,11},{4,12},{5,13},{6,14},{7,15},{8,0},{9,1},... | collective-permute-start | bytes 196616 | tf_op jit(solution)/shard_map/ppermute | solution.py:60
  18.7 0.4 shard_map.98
  19.5 1.7 %collective-permute-done.5.refs_1_ = bf16[128,256]{1,0:T(8,128)(2,1)S(1)} collective-permute-done((bf16[128,256]{1,0:T(8,128)(2,1)S(1)}, bf16[128,256]{1,0:T(8,128)(2,1)S(1)}, u32[]{:S(2)}, u32[]{:S(2)}) %collective-permute-start.5) | collective-permute-done | bytes 65568 | tf_op jit(solution)/shard_map/ppermute | solution.py:60
  21.4 0.5 shard_map.101
  21.9 0.5 %shard_map.102.refs_7_ = bf16[512,256]{1,0:T(8,128)(2,1)S(1)} custom-call(bf16[3,128,1024]{2,1,0:T(8,128)(2,1)S(1)} %get-tuple-element.54.refs_0_, bf16[1,128,1024]{2,1,0:T(8,128)(2,1)S(1)} %get-tuple-element.55.refs_1_, bf16[4,128,256]{2,1,0:T(8,128)(2,1)S(1)} %get-tuple-element.56.refs_2_, bf16[4,128,256]{2,1,0:T(8,128)(2,1)S(1)} %get-tuple-element.53.refs_3_.refs_4_), custom_call_target="tpu_custom_call" | custom-call | flops 1 | bytes 1 | tf_op jit(solution)/shard_map/pallas_call | solution.py:42
  22.4 1.5 %collective-permute-start.11 = (bf16[512,256]{1,0:T(8,128)(2,1)S(1)}, bf16[512,256]{1,0:T(8,128)(2,1)S(1)}, u32[]{:S(2)}, u32[]{:S(2)}) collective-permute-start(bf16[512,256]{1,0:T(8,128)(2,1)S(1)} %shard_map.102.refs_7_), channel_id=1, source_target_pairs={{0,16},{16,0},{1,17},{17,1},{2,18},{18,2},{3,19},{19,3},{4,20},{20... | collective-permute-start | bytes 786440 | tf_op jit(solution)/shard_map/ppermute | solution.py:60
  23.9 0.7 %shard_map.103 = (bf16[512,256]{1,0:T(8,128)(2,1)S(1)}, bf16[512,256]{1,0:T(8,128)(2,1)S(1)}, f32[4,128,256]{2,1,0:T(8,128)S(1)}, bf16[128,256]{1,0:T(8,128)(2,1)S(1)}) custom-call(bf16[256,256]{1,0:T(8,128)(2,1)S(1)} %get-tuple-element.43.refs_0_.refs_4_, bf16[1024,256]{1,0:T(8,128)(2,1)S(1)} %collective-permute-done.refs_0_.refs_1_, ...), custom_call_target="tpu_custom_call" | custom-call | flops 1 | bytes 1 | tf_op jit(solution)/shard_map/pallas_call | solution.py:42
  24.6 1.6 %collective-permute-start.9 = (bf16[512,256]{1,0:T(8,128)(2,1)S(1)}, bf16[512,256]{1,0:T(8,128)(2,1)S(1)}, u32[]{:S(2)}, u32[]{:S(2)}) collective-permute-start(bf16[512,256]{1,0:T(8,128)(2,1)S(1)} %get-tuple-element.58), channel_id=1, source_target_pairs={{0,2},{1,3},{2,0},{3,1},{4,6},{5,7},{6,4},{7,5},{8,10},{9,11},{10,... | collective-permute-start | bytes 786440 | tf_op jit(solution)/shard_map/ppermute | solution.py:60
  26.2 1.4 %collective-permute-start.10 = (bf16[128,256]{1,0:T(8,128)(2,1)S(1)}, bf16[128,256]{1,0:T(8,128)(2,1)S(1)}, u32[]{:S(2)}, u32[]{:S(2)}) collective-permute-start(bf16[128,256]{1,0:T(8,128)(2,1)S(1)} %get-tuple-element.59.refs_3_.refs_0_), channel_id=1, source_target_pairs={{0,4},{1,5},{2,6},{3,7},{4,0},{5,1},{6,2},{7,3},{8,12},{9,13},{10,... | collective-permute-start | bytes 196616 | tf_op jit(solution)/shard_map/ppermute | solution.py:60
  27.6 0.5 %shard_map.104.refs_0_.refs_2_ = f32[512,256]{1,0:T(8,128)S(1)} custom-call(bf16[3,128,1024]{2,1,0:T(8,128)(2,1)S(1)} %get-tuple-element.54.refs_0_, bf16[1,128,1024]{2,1,0:T(8,128)(2,1)S(1)} %get-tuple-element.55.refs_1_, bf16[4,128,256]{2,1,0:T(8,128)(2,1)S(1)} %get-tuple-element.56.refs_2_, bf16[128,256]{1,0:T(8,128)(2,1)S(1)} %get-tuple-element.59.refs_3_.refs_0_), custom_call_target="tpu_custom_call" | custom-call | flops 1 | bytes 1 | tf_op jit(solution)/shard_map/pallas_call | solution.py:42
  28.1 1.6 %collective-permute-done.11.refs_1_ = bf16[512,256]{1,0:T(8,128)(2,1)S(1)} collective-permute-done((bf16[512,256]{1,0:T(8,128)(2,1)S(1)}, bf16[512,256]{1,0:T(8,128)(2,1)S(1)}, u32[]{:S(2)}, u32[]{:S(2)}) %collective-permute-start.11) | collective-permute-done | bytes 262176 | tf_op jit(solution)/shard_map/ppermute | solution.py:60
  29.7 1.4 %collective-permute-start.15 = (bf16[256,256]{1,0:T(8,128)(2,1)S(1)}, bf16[256,256]{1,0:T(8,128)(2,1)S(1)}, u32[]{:S(2)}, u32[]{:S(2)}) collective-permute-start(bf16[256,256]{1,0:T(8,128)(2,1)S(1)} %get-tuple-element.61.refs_2_), channel_id=1, source_target_pairs={{0,4},{1,5},{2,6},{3,7},{4,0},{5,1},{6,2},{7,3},{8,12},{9,13},{10,... | collective-permute-start | bytes 393224 | tf_op jit(solution)/shard_map/ppermute | solution.py:60
  31.2 2.7 %collective-permute-start.14 = (bf16[128,256]{1,0:T(8,128)(2,1)S(1)}, bf16[128,256]{1,0:T(8,128)(2,1)S(1)}, u32[]{:S(2)}, u32[]{:S(2)}) collective-permute-start(bf16[128,256]{1,0:T(8,128)(2,1)S(1)} %shard_map.106.refs_2_), channel_id=1, source_target_pairs={{0,8},{1,9},{2,10},{3,11},{4,12},{5,13},{6,14},{7,15},{8,0},{9,1},... | collective-permute-start | bytes 196616 | tf_op jit(solution)/shard_map/ppermute | solution.py:60
  33.9 0.8 %collective-permute-done.15.refs_1_ = bf16[256,256]{1,0:T(8,128)(2,1)S(1)} collective-permute-done((bf16[256,256]{1,0:T(8,128)(2,1)S(1)}, bf16[256,256]{1,0:T(8,128)(2,1)S(1)}, u32[]{:S(2)}, u32[]{:S(2)}) %collective-permute-start.15) | collective-permute-done | bytes 131104 | tf_op jit(solution)/shard_map/ppermute | solution.py:60
  34.8 2.7 %collective-permute-start.17 = (bf16[128,256]{1,0:T(8,128)(2,1)S(1)}, bf16[128,256]{1,0:T(8,128)(2,1)S(1)}, u32[]{:S(2)}, u32[]{:S(2)}) collective-permute-start(bf16[128,256]{1,0:T(8,128)(2,1)S(1)} %get-tuple-element.64.refs_3_), channel_id=1, source_target_pairs={{0,8},{1,9},{2,10},{3,11},{4,12},{5,13},{6,14},{7,15},{8,0},{9,1},... | collective-permute-start | bytes 196616 | tf_op jit(solution)/shard_map/ppermute | solution.py:60
  37.6 1.6 %collective-permute-start.16 = (bf16[256,256]{1,0:T(8,128)(2,1)S(1)}, bf16[256,256]{1,0:T(8,128)(2,1)S(1)}, u32[]{:S(2)}, u32[]{:S(2)}) collective-permute-start(bf16[256,256]{1,0:T(8,128)(2,1)S(1)} %get-tuple-element.66.refs_7_), channel_id=1, source_target_pairs={{0,2},{1,3},{2,0},{3,1},{4,6},{5,7},{6,4},{7,5},{8,10},{9,11},{10,... | collective-permute-start | bytes 393224 | tf_op jit(solution)/shard_map/ppermute | solution.py:60
  39.2 2.1 %shard_map.110 = (bf16[128,1024]{1,0:T(8,128)(2,1)}, f32[4,128,256]{2,1,0:T(8,128)S(1)}, f32[4,128,256]{2,1,0:T(8,128)S(1)}) custom-call(bf16[512,256]{1,0:T(8,128)(2,1)S(1)} %get-tuple-element.57.refs_0_, bf16[512,256]{1,0:T(8,128)(2,1)S(1)} %collective-permute-done.9.refs_1_, bf16[512,256]{1,0:T(8,128)(2,1)S(1)} %collective-permute-done.13.refs_2_, ...), custom_call_target="tpu_custom_call" | custom-call | flops 1 | bytes 1 | tf_op jit(solution)/shard_map/pallas_call | solution.py:42
  41.4 0.4 collective-permute-start.19
  41.8 1.1 %collective-permute-done.16.refs_1_ = bf16[256,256]{1,0:T(8,128)(2,1)S(1)} collective-permute-done((bf16[256,256]{1,0:T(8,128)(2,1)S(1)}, bf16[256,256]{1,0:T(8,128)(2,1)S(1)}, u32[]{:S(2)}, u32[]{:S(2)}) %collective-permute-start.16) | collective-permute-done | bytes 131104 | tf_op jit(solution)/shard_map/ppermute | solution.py:60
  43.1 2.1 %shard_map.113 = (bf16[128,1024]{1,0:T(8,128)(2,1)}, bf16[128,1024]{1,0:T(8,128)(2,1)}) custom-call(bf16[512,256]{1,0:T(8,128)(2,1)S(1)} %get-tuple-element.57.refs_0_, bf16[512,256]{1,0:T(8,128)(2,1)S(1)} %collective-permute-done.9.refs_1_, bf16[512,256]{1,0:T(8,128)(2,1)S(1)} %collective-permute-done.13.refs_2_, bf16[128,1024]{1,0:T(8,128)(2,1)S(1)} %bitcast.18, ...), custom_call_target="tpu_custom_call" | custom-call | flops 1 | bytes 1 | tf_op jit(solution)/shard_map/pallas_call | solution.py:42
  45.1 0.3 collective-permute-done.19.refs_1_
  45.7 1.1 %shard_map.115 = (bf16[128,1024]{1,0:T(8,128)(2,1)}, bf16[128,1024]{1,0:T(8,128)(2,1)}) custom-call(bf16[256,256]{1,0:T(8,128)(2,1)S(1)} %get-tuple-element.65.refs_0_, bf16[256,256]{1,0:T(8,128)(2,1)S(1)} %collective-permute-done.16.refs_1_, bf16[256,256]{1,0:T(8,128)(2,1)S(1)} %collective-permute-done.18.refs_2_, bf16[128,1024]{1,0:T(8,128)(2,1)S(1)} %bitcast.11, ...), custom_call_target="tpu_custom_call" | custom-call | flops 1 | bytes 1 | tf_op jit(solution)/shard_map/pallas_call | solution.py:42
  46.8 0.7 %shard_map.116 = f32[32,1024]{1,0:T(8,128)} custom-call(bf16[64,256]{1,0:T(8,128)(2,1)S(1)} %get-tuple-element.78.refs_0_, bf16[64,256]{1,0:T(8,128)(2,1)S(1)} %collective-permute-done.20.refs_1_, bf16[64,256]{1,0:T(8,128)(2,1)S(1)} %get-tuple-element.75.refs_7_.refs_2_, bf16[128,1024]{1,0:T(8,128)(2,1)} %get-tuple-element.76.refs_3_), custom_call_target="tpu_custom_call" | custom-call | flops 1 | bytes 1 | tf_op jit(solution)/shard_map/pallas_call | solution.py:42
  (45 shorter events, 1.8 us)
Async XLA Ops:
  0.6 4.6 %copy-start.4 = (bf16[1,128,1024]{2,1,0:T(8,128)(2,1)S(1)}, bf16[1,128,1024]{2,1,0:T(8,128)(2,1)}, u32[]{:S(2)}) copy-start(bf16[1,128,1024]{2,1,0:T(8,128)(2,1)} %param.8) | copy-start | bytes 786436
  0.6 6.6 %copy-start = (bf16[1,128,1024]{2,1,0:T(8,128)(2,1)S(1)}, bf16[1,128,1024]{2,1,0:T(8,128)(2,1)}, u32[]{:S(2)}) copy-start(bf16[1,128,1024]{2,1,0:T(8,128)(2,1)} %param.6) | copy-start | bytes 786436
  0.7 6.6 %copy-start.1 = (bf16[1,128,1024]{2,1,0:T(8,128)(2,1)S(1)}, bf16[1,128,1024]{2,1,0:T(8,128)(2,1)}, u32[]{:S(2)}) copy-start(bf16[1,128,1024]{2,1,0:T(8,128)(2,1)} %param.7) | copy-start | bytes 786436
  0.7 6.6 %copy-start.3 = (bf16[1,128,1024]{2,1,0:T(8,128)(2,1)S(1)}, bf16[1,128,1024]{2,1,0:T(8,128)(2,1)}, u32[]{:S(2)}) copy-start(bf16[1,128,1024]{2,1,0:T(8,128)(2,1)} %param.5) | copy-start | bytes 786436
  2.2 7.4 %collective-permute-start.1 = (bf16[256,256]{1,0:T(8,128)(2,1)S(1)}, bf16[256,256]{1,0:T(8,128)(2,1)S(1)}, u32[]{:S(2)}, u32[]{:S(2)}) collective-permute-start(bf16[256,256]{1,0:T(8,128)(2,1)S(1)} %get-tuple-element.47), channel_id=1, source_target_pairs={{0,2},{1,3},{2,0},{3,1},{4,6},{5,7},{6,4},{7,5},{8,10},{9,11},{10,... | collective-permute-start | bytes 393224 | tf_op jit(solution)/shard_map/ppermute | solution.py:60
  5.3 9.6 %collective-permute-start.6 = (bf16[128,1024]{1,0:T(8,128)(2,1)S(1)}, bf16[128,1024]{1,0:T(8,128)(2,1)S(1)}, u32[]{:S(2)}, u32[]{:S(2)}) collective-permute-start(bf16[128,1024]{1,0:T(8,128)(2,1)S(1)} %bitcast.19), channel_id=1, source_target_pairs={{0,2},{1,3},{2,0},{3,1},{4,6},{5,7},{6,4},{7,5},{8,10},{9,11},{10,... | collective-permute-start | bytes 786440 | tf_op jit(solution)/shard_map/ppermute | solution.py:60
  5.4 13.4 %collective-permute-start.8 = (bf16[2,512,256]{2,1,0:T(8,128)(2,1)S(1)}, bf16[2,512,256]{2,1,0:T(8,128)(2,1)S(1)}, u32[]{:S(2)}, u32[]{:S(2)}) collective-permute-start(bf16[2,512,256]{2,1,0:T(8,128)(2,1)S(1)} %get-tuple-element.49.refs_3_.refs_1_), channel_id=1, source_target_pairs={{0,16},{16,0},{1,17},{17,1},{2,18},{18,2},{3,19},{19,3},{4,20},{20... | collective-permute-start | bytes 1572872 | tf_op jit(solution)/shard_map/ppermute | solution.py:60
  8.6 4.6 %collective-permute-start = (bf16[1024,256]{1,0:T(8,128)(2,1)S(1)}, bf16[1024,256]{1,0:T(8,128)(2,1)S(1)}, u32[]{:S(2)}, u32[]{:S(2)}) collective-permute-start(bf16[1024,256]{1,0:T(8,128)(2,1)S(1)} %get-tuple-element.44.refs_5_), channel_id=1, source_target_pairs={{0,1},{1,0},{2,3},{3,2},{4,5},{5,4},{6,7},{7,6},{8,9},{9,8},{10,11... | collective-permute-start | bytes 1572872 | tf_op jit(solution)/shard_map/ppermute | solution.py:60
  9.6 1.4 %collective-permute-start.2 = (bf16[256,256]{1,0:T(8,128)(2,1)S(1)}, bf16[256,256]{1,0:T(8,128)(2,1)S(1)}, u32[]{:S(2)}, u32[]{:S(2)}) collective-permute-start(bf16[256,256]{1,0:T(8,128)(2,1)S(1)} %shard_map.94.refs_3_), channel_id=1, source_target_pairs={{0,1},{1,0},{2,3},{3,2},{4,5},{5,4},{6,7},{7,6},{8,9},{9,8},{10,11... | collective-permute-start | bytes 393224 | tf_op jit(solution)/shard_map/ppermute | solution.py:60
  11.1 4.6 %collective-permute-start.4 = (bf16[128,256]{1,0:T(8,128)(2,1)S(1)}, bf16[128,256]{1,0:T(8,128)(2,1)S(1)}, u32[]{:S(2)}, u32[]{:S(2)}) collective-permute-start(bf16[128,256]{1,0:T(8,128)(2,1)S(1)} %shard_map.95.refs_2_.refs_0_), channel_id=1, source_target_pairs={{0,4},{1,5},{2,6},{3,7},{4,0},{5,1},{6,2},{7,3},{8,12},{9,13},{10,... | collective-permute-start | bytes 196616 | tf_op jit(solution)/shard_map/ppermute | solution.py:60
  13.3 8.1 %collective-permute-start.3 = (bf16[512,256]{1,0:T(8,128)(2,1)S(1)}, bf16[512,256]{1,0:T(8,128)(2,1)S(1)}, u32[]{:S(2)}, u32[]{:S(2)}) collective-permute-start(bf16[512,256]{1,0:T(8,128)(2,1)S(1)} %shard_map.96.refs_2_), channel_id=1, source_target_pairs={{0,2},{1,3},{2,0},{3,1},{4,6},{5,7},{6,4},{7,5},{8,10},{9,11},{10,... | collective-permute-start | bytes 786440 | tf_op jit(solution)/shard_map/ppermute | solution.py:60
  14.9 4.4 %collective-permute-start.7 = (bf16[128,1024]{1,0:T(8,128)(2,1)S(1)}, bf16[128,1024]{1,0:T(8,128)(2,1)S(1)}, u32[]{:S(2)}, u32[]{:S(2)}) collective-permute-start(bf16[128,1024]{1,0:T(8,128)(2,1)S(1)} %collective-permute-done.6.refs_2_), channel_id=1, source_target_pairs={{0,1},{1,0},{2,3},{3,2},{4,5},{5,4},{6,7},{7,6},{8,9},{9,8},{10,11... | collective-permute-start | bytes 786440 | tf_op jit(solution)/shard_map/ppermute | solution.py:60
  15.7 5.6 %collective-permute-start.5 = (bf16[128,256]{1,0:T(8,128)(2,1)S(1)}, bf16[128,256]{1,0:T(8,128)(2,1)S(1)}, u32[]{:S(2)}, u32[]{:S(2)}) collective-permute-start(bf16[128,256]{1,0:T(8,128)(2,1)S(1)} %shard_map.97.refs_5_), channel_id=1, source_target_pairs={{0,8},{1,9},{2,10},{3,11},{4,12},{5,13},{6,14},{7,15},{8,0},{9,1},... | collective-permute-start | bytes 196616 | tf_op jit(solution)/shard_map/ppermute | solution.py:60
  19.2 10.5 %collective-permute-start.12 = (bf16[2,512,256]{2,1,0:T(8,128)(2,1)S(1)}, bf16[2,512,256]{2,1,0:T(8,128)(2,1)S(1)}, u32[]{:S(2)}, u32[]{:S(2)}) collective-permute-start(bf16[2,512,256]{2,1,0:T(8,128)(2,1)S(1)} %collective-permute-done.8.refs_4_.refs_2_.refs_8_), channel_id=1, source_target_pairs={{0,1},{1,0},{2,3},{3,2},{4,5},{5,4},{6,7},{7,6},{8,9},{9,8},{10,11... | collective-permute-start | bytes 1572872 | tf_op jit(solution)/shard_map/ppermute | solution.py:60
  22.4 7.3 %collective-permute-start.11 = (bf16[512,256]{1,0:T(8,128)(2,1)S(1)}, bf16[512,256]{1,0:T(8,128)(2,1)S(1)}, u32[]{:S(2)}, u32[]{:S(2)}) collective-permute-start(bf16[512,256]{1,0:T(8,128)(2,1)S(1)} %shard_map.102.refs_7_), channel_id=1, source_target_pairs={{0,16},{16,0},{1,17},{17,1},{2,18},{18,2},{3,19},{19,3},{4,20},{20... | collective-permute-start | bytes 786440 | tf_op jit(solution)/shard_map/ppermute | solution.py:60
  24.6 9.2 %collective-permute-start.9 = (bf16[512,256]{1,0:T(8,128)(2,1)S(1)}, bf16[512,256]{1,0:T(8,128)(2,1)S(1)}, u32[]{:S(2)}, u32[]{:S(2)}) collective-permute-start(bf16[512,256]{1,0:T(8,128)(2,1)S(1)} %get-tuple-element.58), channel_id=1, source_target_pairs={{0,2},{1,3},{2,0},{3,1},{4,6},{5,7},{6,4},{7,5},{8,10},{9,11},{10,... | collective-permute-start | bytes 786440 | tf_op jit(solution)/shard_map/ppermute | solution.py:60
  26.2 4.9 %collective-permute-start.10 = (bf16[128,256]{1,0:T(8,128)(2,1)S(1)}, bf16[128,256]{1,0:T(8,128)(2,1)S(1)}, u32[]{:S(2)}, u32[]{:S(2)}) collective-permute-start(bf16[128,256]{1,0:T(8,128)(2,1)S(1)} %get-tuple-element.59.refs_3_.refs_0_), channel_id=1, source_target_pairs={{0,4},{1,5},{2,6},{3,7},{4,0},{5,1},{6,2},{7,3},{8,12},{9,13},{10,... | collective-permute-start | bytes 196616 | tf_op jit(solution)/shard_map/ppermute | solution.py:60
  29.7 5.0 %collective-permute-start.15 = (bf16[256,256]{1,0:T(8,128)(2,1)S(1)}, bf16[256,256]{1,0:T(8,128)(2,1)S(1)}, u32[]{:S(2)}, u32[]{:S(2)}) collective-permute-start(bf16[256,256]{1,0:T(8,128)(2,1)S(1)} %get-tuple-element.61.refs_2_), channel_id=1, source_target_pairs={{0,4},{1,5},{2,6},{3,7},{4,0},{5,1},{6,2},{7,3},{8,12},{9,13},{10,... | collective-permute-start | bytes 393224 | tf_op jit(solution)/shard_map/ppermute | solution.py:60
  31.2 6.3 %collective-permute-start.14 = (bf16[128,256]{1,0:T(8,128)(2,1)S(1)}, bf16[128,256]{1,0:T(8,128)(2,1)S(1)}, u32[]{:S(2)}, u32[]{:S(2)}) collective-permute-start(bf16[128,256]{1,0:T(8,128)(2,1)S(1)} %shard_map.106.refs_2_), channel_id=1, source_target_pairs={{0,8},{1,9},{2,10},{3,11},{4,12},{5,13},{6,14},{7,15},{8,0},{9,1},... | collective-permute-start | bytes 196616 | tf_op jit(solution)/shard_map/ppermute | solution.py:60
  33.8 5.3 %collective-permute-start.13 = (bf16[512,256]{1,0:T(8,128)(2,1)S(1)}, bf16[512,256]{1,0:T(8,128)(2,1)S(1)}, u32[]{:S(2)}, u32[]{:S(2)}) collective-permute-start(bf16[512,256]{1,0:T(8,128)(2,1)S(1)} %shard_map.107.refs_2_), channel_id=1, source_target_pairs={{0,1},{1,0},{2,3},{3,2},{4,5},{5,4},{6,7},{7,6},{8,9},{9,8},{10,11... | collective-permute-start | bytes 786440 | tf_op jit(solution)/shard_map/ppermute | solution.py:60
  34.8 6.6 %collective-permute-start.17 = (bf16[128,256]{1,0:T(8,128)(2,1)S(1)}, bf16[128,256]{1,0:T(8,128)(2,1)S(1)}, u32[]{:S(2)}, u32[]{:S(2)}) collective-permute-start(bf16[128,256]{1,0:T(8,128)(2,1)S(1)} %get-tuple-element.64.refs_3_), channel_id=1, source_target_pairs={{0,8},{1,9},{2,10},{3,11},{4,12},{5,13},{6,14},{7,15},{8,0},{9,1},... | collective-permute-start | bytes 196616 | tf_op jit(solution)/shard_map/ppermute | solution.py:60
  37.6 5.4 %collective-permute-start.16 = (bf16[256,256]{1,0:T(8,128)(2,1)S(1)}, bf16[256,256]{1,0:T(8,128)(2,1)S(1)}, u32[]{:S(2)}, u32[]{:S(2)}) collective-permute-start(bf16[256,256]{1,0:T(8,128)(2,1)S(1)} %get-tuple-element.66.refs_7_), channel_id=1, source_target_pairs={{0,2},{1,3},{2,0},{3,1},{4,6},{5,7},{6,4},{7,5},{8,10},{9,11},{10,... | collective-permute-start | bytes 393224 | tf_op jit(solution)/shard_map/ppermute | solution.py:60
  41.4 1.6 %copy-start.2 = (bf16[512,1024]{1,0:T(8,128)(2,1)S(1)}, bf16[512,1024]{1,0:T(8,128)(2,1)}, u32[]{:S(2)}) copy-start(bf16[512,1024]{1,0:T(8,128)(2,1)} %refs_7_.1) | copy-start | bytes 3145732
  41.4 4.0 %collective-permute-start.19 = (bf16[64,256]{1,0:T(8,128)(2,1)S(1)}, bf16[64,256]{1,0:T(8,128)(2,1)S(1)}, u32[]{:S(2)}, u32[]{:S(2)}) collective-permute-start(bf16[64,256]{1,0:T(8,128)(2,1)S(1)} %get-tuple-element.70.refs_2_), channel_id=1, source_target_pairs={{0,2},{1,3},{2,0},{3,1},{4,6},{5,7},{6,4},{7,5},{8,10},{9,11},{10,... | collective-permute-start | bytes 98312 | tf_op jit(solution)/shard_map/ppermute | solution.py:60
  43.0 2.7 %collective-permute-start.18 = (bf16[256,256]{1,0:T(8,128)(2,1)S(1)}, bf16[256,256]{1,0:T(8,128)(2,1)S(1)}, u32[]{:S(2)}, u32[]{:S(2)}) collective-permute-start(bf16[256,256]{1,0:T(8,128)(2,1)S(1)} %shard_map.112.refs_10_.refs_2_), channel_id=1, source_target_pairs={{0,1},{1,0},{2,3},{3,2},{4,5},{5,4},{6,7},{7,6},{8,9},{9,8},{10,11... | collective-permute-start | bytes 393224 | tf_op jit(solution)/shard_map/ppermute | solution.py:60
  45.4 1.4 %collective-permute-start.20 = (bf16[64,256]{1,0:T(8,128)(2,1)S(1)}, bf16[64,256]{1,0:T(8,128)(2,1)S(1)}, u32[]{:S(2)}, u32[]{:S(2)}) collective-permute-start(bf16[64,256]{1,0:T(8,128)(2,1)S(1)} %get-tuple-element.75.refs_7_.refs_2_), channel_id=1, source_target_pairs={{0,1},{1,0},{2,3},{3,2},{4,5},{5,4},{6,7},{7,6},{8,9},{9,8},{10,11... | collective-permute-start | bytes 98312 | tf_op jit(solution)/shard_map/ppermute | solution.py:60

commit v20 on v19

--- a/solution.py
+++ b/solution.py
@@ -369,13 +369,15 @@
     factor = 1.0 / math.sqrt(rows * dp * seq)
     near = functools.partial(flip, axis="seq", count=seq)
 
-    def doubling(total, cost=1):
+    def doubling(total, backward, price=1):
         found = []
         bits = SLAB
         while bits < seq:
             if found:
-                (total,) = call(add_kernel, [(total.shape, BF16)], total, found[-1], cost=cost)
-            found.append(near(total, bits=bits))
+                (total,) = call(add_kernel, [(total.shape, BF16)], total, found[-1], cost=price)
+            last = 2 * bits >= seq
+            pairs = [(i, i ^ bits) for i in range(seq) if not last or bool(i & bits) == backward]
+            found.append(lax.ppermute(total, "seq", pairs))
             bits *= 2
         return found, total
 
@@ -407,7 +409,7 @@
     (far_tokens,) = call(pair_kernel, [((4 * rows, width), BF16)], message, far_tokens)
     cot_yc = near(after(cot_y, far_tokens), bits=1)
     far_tokens = near(far_tokens, bits=2)
-    before, _ = doubling(slab_kv, 22 * 10**8)
+    before, _ = doubling(slab_kv, False, 22 * 10**8)
     weights = (columns, *w_far)
     dnormed, cots = call(
         functools.partial(dnormed_kernel, dp, (0, 1, 2)),
@@ -448,7 +450,7 @@
             split_kernel, [((2 * piece, width), F32), ((2 * piece, width), BF16)], keep, got, wait=w_all[1::2]
         )
         got = near(send, bits=SLAB)
-    behind, last_u = doubling(slab_u, 10**9)
+    behind, last_u = doubling(slab_u, True, 10**9)
     (send,) = call(relay_kernel, [((2 * rows + 2 * DH, width), BF16)], back, back_far)
     back_core = near(send, bits=1)
     if tuned:

time: 47.7 us -> 52.5 us (1.10)
  waiting for transfers between devices: 9 us -> 12.6 us
  starting transfers between devices: 25.6 us -> 26.7 us
    ppermute x0 -> x4, starting transfers between devices: none -> 10.3 us  [doubling(): found.append(lax.ppermute(total, 'seq', pairs))]
    ppermute x21 -> x17, starting transfers between devices: 25.6 us -> 16.4 us  [flip(): return lax.ppermute(x, axis, [(i, i ^ bits) for i in range(count)])]
    ppermute x0 -> x4, waiting for transfers between devices: none -> 5.48 us  [doubling(): found.append(lax.ppermute(total, 'seq', pairs))]
    ppermute x21 -> x17, waiting for transfers between devices: 9 us -> 7.16 us  [flip(): return lax.ppermute(x, axis, [(i, i ^ bits) for i in range(count)])]
  transfers between devices with their start and end apart: 21 -> 21, of which waited for: 11 -> 9; matrix products, arithmetic and copies ran while one was open for 0% -> 0% of each run, Pallas kernels for 21% -> 19%
where the time goes in v20:
time: 52.5 us; the launch traced here: 52.3 us
  starting transfers between devices  26.7 us (51%)
  waiting for transfers between devices  12.6 us (24%)
  Pallas kernels  12 us (23%)
  between operations  0.88 us (2%)
    ppermute x17, starting transfers between devices, flip(): return lax.ppermute(x, axis, [(i, i ^ bits) for i in range(count)])  16.4 us
    pallas_call x25, Pallas kernels, __call__(): pl.pallas_call(inner, out_shape=[jax.ShapeDtypeStruct(s, d) for s, d in o...  12 us
    ppermute x4, starting transfers between devices, doubling(): found.append(lax.ppermute(total, 'seq', pairs))  10.3 us
    ppermute x17, waiting for transfers between devices, flip(): return lax.ppermute(x, axis, [(i, i ^ bits) for i in range(count)])  7.16 us
    ppermute x4, waiting for transfers between devices, doubling(): found.append(lax.ppermute(total, 'seq', pairs))  5.48 us
  transfers between devices with their start and end apart: 21, of which 9 were waited for; matrix products, arithmetic and copies ran while one was open for 0% of the time, Pallas kernels for 19%

profile of v20, /device:TPU:0, one launch (start us, length us, event | category | flops | bytes accessed | tf_op | source)
XLA Modules:
  0.0 52.3 jit_solution(3011776076364654392)
XLA Ops:
  0.7 1.6 %shard_map.92 = (f32[128,256]{1,0:T(8,128)S(1)}, bf16[128,256]{1,0:T(8,128)(2,1)S(1)}, bf16[256,256]{1,0:T(8,128)(2,1)S(1)}, bf16[2,512,256]{2,1,0:T(8,128)(2,1)S(1)}) custom-call(bf16[128,1024]{1,0:T(8,128)(2,1)} %bitcast.8, bf16[128,1024]{1,0:T(8,128)(2,1)} %bitcast.12, bf16[512,1024]{1,0:T(8,128)(2,1)} %refs_7_.1), custom_call_target="tpu_custom_call" | custom-call | flops 1 | bytes 1 | tf_op jit(solution)/shard_map/pallas_call | solution.py:42
  2.2 3.0 %collective-permute-start.1 = (bf16[256,256]{1,0:T(8,128)(2,1)S(1)}, bf16[256,256]{1,0:T(8,128)(2,1)S(1)}, u32[]{:S(2)}, u32[]{:S(2)}) collective-permute-start(bf16[256,256]{1,0:T(8,128)(2,1)S(1)} %get-tuple-element.47), channel_id=1, source_target_pairs={{0,2},{1,3},{2,0},{3,1},{4,6},{5,7},{6,4},{7,5},{8,10},{9,11},{10,... | collective-permute-start | bytes 393224 | tf_op jit(solution)/shard_map/ppermute | solution.py:60
  5.4 1.9 %collective-permute-start.8 = (bf16[2,512,256]{2,1,0:T(8,128)(2,1)S(1)}, bf16[2,512,256]{2,1,0:T(8,128)(2,1)S(1)}, u32[]{:S(2)}, u32[]{:S(2)}) collective-permute-start(bf16[2,512,256]{2,1,0:T(8,128)(2,1)S(1)} %get-tuple-element.49.refs_3_.refs_1_), channel_id=1, source_target_pairs={{0,16},{16,0},{1,17},{17,1},{2,18},{18,2},{3,19},{19,3},{4,20},{20... | collective-permute-start | bytes 1572872 | tf_op jit(solution)/shard_map/ppermute | solution.py:60
  7.3 1.4 %shard_map.93 = (bf16[4,2,128,128]{3,2,1,0:T(8,128)(2,1)S(1)}, bf16[256,256]{1,0:T(8,128)(2,1)S(1)}, bf16[1024,256]{1,0:T(8,128)(2,1)S(1)}, bf16[256,256]{1,0:T(8,128)(2,1)S(1)}) custom-call(bf16[128,1024]{1,0:T(8,128)(2,1)S(1)} %bitcast.16, bf16[128,1024]{1,0:T(8,128)(2,1)S(1)} %bitcast.9, bf16[128,1024]{1,0:T(8,128)(2,1)S(1)} %bitcast.13, ...), custom_call_target="tpu_custom_call" | custom-call | flops 1 | bytes 1 | tf_op jit(solution)/shard_map/pallas_call | solution.py:42
  8.7 0.9 %collective-permute-done.1.refs_1_.refs_4_ = bf16[256,256]{1,0:T(8,128)(2,1)S(1)} collective-permute-done((bf16[256,256]{1,0:T(8,128)(2,1)S(1)}, bf16[256,256]{1,0:T(8,128)(2,1)S(1)}, u32[]{:S(2)}, u32[]{:S(2)}) %collective-permute-start.1) | collective-permute-done | bytes 131104 | tf_op jit(solution)/shard_map/ppermute | solution.py:60
  9.7 1.3 %collective-permute-done.2.refs_2_.refs_5_ = bf16[256,256]{1,0:T(8,128)(2,1)S(1)} collective-permute-done((bf16[256,256]{1,0:T(8,128)(2,1)S(1)}, bf16[256,256]{1,0:T(8,128)(2,1)S(1)}, u32[]{:S(2)}, u32[]{:S(2)}) %collective-permute-start.2) | collective-permute-done | bytes 131104 | tf_op jit(solution)/shard_map/ppermute | solution.py:60
  11.1 2.2 %collective-permute-start.4 = (bf16[128,256]{1,0:T(8,128)(2,1)S(1)}, bf16[128,256]{1,0:T(8,128)(2,1)S(1)}, u32[]{:S(2)}, u32[]{:S(2)}) collective-permute-start(bf16[128,256]{1,0:T(8,128)(2,1)S(1)} %shard_map.95.refs_2_.refs_0_), channel_id=1, source_target_pairs={{0,4},{1,5},{2,6},{3,7},{4,0},{5,1},{6,2},{7,3},{8,12},{9,13},{10,... | collective-permute-start | bytes 196616 | tf_op jit(solution)/shard_map/ppermute | solution.py:380
  13.3 1.6 %collective-permute-start.3 = (bf16[512,256]{1,0:T(8,128)(2,1)S(1)}, bf16[512,256]{1,0:T(8,128)(2,1)S(1)}, u32[]{:S(2)}, u32[]{:S(2)}) collective-permute-start(bf16[512,256]{1,0:T(8,128)(2,1)S(1)} %shard_map.96.refs_2_), channel_id=1, source_target_pairs={{0,2},{1,3},{2,0},{3,1},{4,6},{5,7},{6,4},{7,5},{8,10},{9,11},{10,... | collective-permute-start | bytes 786440 | tf_op jit(solution)/shard_map/ppermute | solution.py:60
  14.9 0.8 %collective-permute-done.4.refs_1_.refs_0_ = bf16[128,256]{1,0:T(8,128)(2,1)S(1)} collective-permute-done((bf16[128,256]{1,0:T(8,128)(2,1)S(1)}, bf16[128,256]{1,0:T(8,128)(2,1)S(1)}, u32[]{:S(2)}, u32[]{:S(2)}) %collective-permute-start.4) | collective-permute-done | bytes 65568 | tf_op jit(solution)/shard_map/ppermute | solution.py:380
  15.7 4.8 %collective-permute-start.5 = (bf16[128,256]{1,0:T(8,128)(2,1)S(1)}, bf16[128,256]{1,0:T(8,128)(2,1)S(1)}, u32[]{:S(2)}, u32[]{:S(2)}) collective-permute-start(bf16[128,256]{1,0:T(8,128)(2,1)S(1)} %shard_map.97.refs_5_), channel_id=1, source_target_pairs={{0,8},{1,9},{2,10},{3,11},{4,12},{5,13},{6,14},{7,15},{16,24},{17,... | collective-permute-start | bytes 196616 | tf_op jit(solution)/shard_map/ppermute | solution.py:380
  20.5 0.4 shard_map.98
  21.2 1.1 %collective-permute-done.5.refs_1_ = bf16[128,256]{1,0:T(8,128)(2,1)S(1)} collective-permute-done((bf16[128,256]{1,0:T(8,128)(2,1)S(1)}, bf16[128,256]{1,0:T(8,128)(2,1)S(1)}, u32[]{:S(2)}, u32[]{:S(2)}) %collective-permute-start.5) | collective-permute-done | bytes 65568 | tf_op jit(solution)/shard_map/ppermute | solution.py:380
  22.4 0.5 shard_map.101
  22.9 0.5 shard_map.102.refs_7_
  23.4 1.5 %collective-permute-start.11 = (bf16[512,256]{1,0:T(8,128)(2,1)S(1)}, bf16[512,256]{1,0:T(8,128)(2,1)S(1)}, u32[]{:S(2)}, u32[]{:S(2)}) collective-permute-start(bf16[512,256]{1,0:T(8,128)(2,1)S(1)} %shard_map.102.refs_7_), channel_id=1, source_target_pairs={{0,16},{16,0},{1,17},{17,1},{2,18},{18,2},{3,19},{19,3},{4,20},{20... | collective-permute-start | bytes 786440 | tf_op jit(solution)/shard_map/ppermute | solution.py:60
  24.9 0.7 %shard_map.103 = (bf16[512,256]{1,0:T(8,128)(2,1)S(1)}, bf16[512,256]{1,0:T(8,128)(2,1)S(1)}, f32[4,128,256]{2,1,0:T(8,128)S(1)}, bf16[128,256]{1,0:T(8,128)(2,1)S(1)}) custom-call(bf16[256,256]{1,0:T(8,128)(2,1)S(1)} %get-tuple-element.43.refs_0_.refs_4_, bf16[1024,256]{1,0:T(8,128)(2,1)S(1)} %collective-permute-done.refs_0_.refs_1_, ...), custom_call_target="tpu_custom_call" | custom-call | flops 1 | bytes 1 | tf_op jit(solution)/shard_map/pallas_call | solution.py:42
  25.6 1.6 %collective-permute-start.9 = (bf16[512,256]{1,0:T(8,128)(2,1)S(1)}, bf16[512,256]{1,0:T(8,128)(2,1)S(1)}, u32[]{:S(2)}, u32[]{:S(2)}) collective-permute-start(bf16[512,256]{1,0:T(8,128)(2,1)S(1)} %get-tuple-element.58), channel_id=1, source_target_pairs={{0,2},{1,3},{2,0},{3,1},{4,6},{5,7},{6,4},{7,5},{8,10},{9,11},{10,... | collective-permute-start | bytes 786440 | tf_op jit(solution)/shard_map/ppermute | solution.py:60
  27.2 2.0 %collective-permute-start.10 = (bf16[128,256]{1,0:T(8,128)(2,1)S(1)}, bf16[128,256]{1,0:T(8,128)(2,1)S(1)}, u32[]{:S(2)}, u32[]{:S(2)}) collective-permute-start(bf16[128,256]{1,0:T(8,128)(2,1)S(1)} %get-tuple-element.59.refs_3_.refs_0_), channel_id=1, source_target_pairs={{0,4},{1,5},{2,6},{3,7},{4,0},{5,1},{6,2},{7,3},{8,12},{9,13},{10,... | collective-permute-start | bytes 196616 | tf_op jit(solution)/shard_map/ppermute | solution.py:380
  29.2 0.5 shard_map.104.refs_0_.refs_2_
  29.7 1.3 %collective-permute-done.11.refs_1_ = bf16[512,256]{1,0:T(8,128)(2,1)S(1)} collective-permute-done((bf16[512,256]{1,0:T(8,128)(2,1)S(1)}, bf16[512,256]{1,0:T(8,128)(2,1)S(1)}, u32[]{:S(2)}, u32[]{:S(2)}) %collective-permute-start.11) | collective-permute-done | bytes 262176 | tf_op jit(solution)/shard_map/ppermute | solution.py:60
  31.1 1.6 %collective-permute-start.15 = (bf16[256,256]{1,0:T(8,128)(2,1)S(1)}, bf16[256,256]{1,0:T(8,128)(2,1)S(1)}, u32[]{:S(2)}, u32[]{:S(2)}) collective-permute-start(bf16[256,256]{1,0:T(8,128)(2,1)S(1)} %get-tuple-element.61.refs_2_), channel_id=1, source_target_pairs={{0,4},{1,5},{2,6},{3,7},{4,0},{5,1},{6,2},{7,3},{8,12},{9,13},{10,... | collective-permute-start | bytes 393224 | tf_op jit(solution)/shard_map/ppermute | solution.py:60
  32.7 1.3 %collective-permute-start.14 = (bf16[128,256]{1,0:T(8,128)(2,1)S(1)}, bf16[128,256]{1,0:T(8,128)(2,1)S(1)}, u32[]{:S(2)}, u32[]{:S(2)}) collective-permute-start(bf16[128,256]{1,0:T(8,128)(2,1)S(1)} %shard_map.106.refs_2_), channel_id=1, source_target_pairs={{8,0},{9,1},{10,2},{11,3},{12,4},{13,5},{14,6},{15,7},{24,16},{25,... | collective-permute-start | bytes 196616 | tf_op jit(solution)/shard_map/ppermute | solution.py:380
  34.2 2.4 %collective-permute-done.15.refs_1_ = bf16[256,256]{1,0:T(8,128)(2,1)S(1)} collective-permute-done((bf16[256,256]{1,0:T(8,128)(2,1)S(1)}, bf16[256,256]{1,0:T(8,128)(2,1)S(1)}, u32[]{:S(2)}, u32[]{:S(2)}) %collective-permute-start.15) | collective-permute-done | bytes 131104 | tf_op jit(solution)/shard_map/ppermute | solution.py:60
  36.6 2.4 %collective-permute-start.17 = (bf16[128,256]{1,0:T(8,128)(2,1)S(1)}, bf16[128,256]{1,0:T(8,128)(2,1)S(1)}, u32[]{:S(2)}, u32[]{:S(2)}) collective-permute-start(bf16[128,256]{1,0:T(8,128)(2,1)S(1)} %get-tuple-element.64.refs_3_), channel_id=1, source_target_pairs={{0,8},{1,9},{2,10},{3,11},{4,12},{5,13},{6,14},{7,15},{8,0},{9,1},... | collective-permute-start | bytes 196616 | tf_op jit(solution)/shard_map/ppermute | solution.py:60
  39.0 3.6 %collective-permute-done.14.refs_1_ = bf16[128,256]{1,0:T(8,128)(2,1)S(1)} collective-permute-done((bf16[128,256]{1,0:T(8,128)(2,1)S(1)}, bf16[128,256]{1,0:T(8,128)(2,1)S(1)}, u32[]{:S(2)}, u32[]{:S(2)}) %collective-permute-start.14) | collective-permute-done | bytes 65568 | tf_op jit(solution)/shard_map/ppermute | solution.py:380
  42.7 1.5 %collective-permute-start.16 = (bf16[256,256]{1,0:T(8,128)(2,1)S(1)}, bf16[256,256]{1,0:T(8,128)(2,1)S(1)}, u32[]{:S(2)}, u32[]{:S(2)}) collective-permute-start(bf16[256,256]{1,0:T(8,128)(2,1)S(1)} %get-tuple-element.66.refs_7_), channel_id=1, source_target_pairs={{0,2},{1,3},{2,0},{3,1},{4,6},{5,7},{6,4},{7,5},{8,10},{9,11},{10,... | collective-permute-start | bytes 393224 | tf_op jit(solution)/shard_map/ppermute | solution.py:60
  44.2 2.1 %shard_map.110 = (bf16[128,1024]{1,0:T(8,128)(2,1)}, f32[4,128,256]{2,1,0:T(8,128)S(1)}, f32[4,128,256]{2,1,0:T(8,128)S(1)}) custom-call(bf16[512,256]{1,0:T(8,128)(2,1)S(1)} %get-tuple-element.57.refs_0_, bf16[512,256]{1,0:T(8,128)(2,1)S(1)} %collective-permute-done.9.refs_1_, bf16[512,256]{1,0:T(8,128)(2,1)S(1)} %collective-permute-done.13.refs_2_, ...), custom_call_target="tpu_custom_call" | custom-call | flops 1 | bytes 1 | tf_op jit(solution)/shard_map/pallas_call | solution.py:42
  46.3 0.6 %collective-permute-start.19 = (bf16[64,256]{1,0:T(8,128)(2,1)S(1)}, bf16[64,256]{1,0:T(8,128)(2,1)S(1)}, u32[]{:S(2)}, u32[]{:S(2)}) collective-permute-start(bf16[64,256]{1,0:T(8,128)(2,1)S(1)} %get-tuple-element.70.refs_2_), channel_id=1, source_target_pairs={{0,2},{1,3},{2,0},{3,1},{4,6},{5,7},{6,4},{7,5},{8,10},{9,11},{10,... | collective-permute-start | bytes 98312 | tf_op jit(solution)/shard_map/ppermute | solution.py:60
  47.0 0.8 %collective-permute-done.16.refs_1_ = bf16[256,256]{1,0:T(8,128)(2,1)S(1)} collective-permute-done((bf16[256,256]{1,0:T(8,128)(2,1)S(1)}, bf16[256,256]{1,0:T(8,128)(2,1)S(1)}, u32[]{:S(2)}, u32[]{:S(2)}) %collective-permute-start.16) | collective-permute-done | bytes 131104 | tf_op jit(solution)/shard_map/ppermute | solution.py:60
  47.8 2.1 %shard_map.113 = (bf16[128,1024]{1,0:T(8,128)(2,1)}, bf16[128,1024]{1,0:T(8,128)(2,1)}) custom-call(bf16[512,256]{1,0:T(8,128)(2,1)S(1)} %get-tuple-element.57.refs_0_, bf16[512,256]{1,0:T(8,128)(2,1)S(1)} %collective-permute-done.9.refs_1_, bf16[512,256]{1,0:T(8,128)(2,1)S(1)} %collective-permute-done.13.refs_2_, bf16[128,1024]{1,0:T(8,128)(2,1)S(1)} %bitcast.18, ...), custom_call_target="tpu_custom_call" | custom-call | flops 1 | bytes 1 | tf_op jit(solution)/shard_map/pallas_call | solution.py:42
  50.5 1.1 %shard_map.115 = (bf16[128,1024]{1,0:T(8,128)(2,1)}, bf16[128,1024]{1,0:T(8,128)(2,1)}) custom-call(bf16[256,256]{1,0:T(8,128)(2,1)S(1)} %get-tuple-element.65.refs_0_, bf16[256,256]{1,0:T(8,128)(2,1)S(1)} %collective-permute-done.16.refs_1_, bf16[256,256]{1,0:T(8,128)(2,1)S(1)} %collective-permute-done.18.refs_2_, bf16[128,1024]{1,0:T(8,128)(2,1)S(1)} %bitcast.11, ...), custom_call_target="tpu_custom_call" | custom-call | flops 1 | bytes 1 | tf_op jit(solution)/shard_map/pallas_call | solution.py:42
  51.6 0.7 %shard_map.116 = f32[32,1024]{1,0:T(8,128)} custom-call(bf16[64,256]{1,0:T(8,128)(2,1)S(1)} %get-tuple-element.78.refs_0_, bf16[64,256]{1,0:T(8,128)(2,1)S(1)} %collective-permute-done.20.refs_1_, bf16[64,256]{1,0:T(8,128)(2,1)S(1)} %get-tuple-element.75.refs_7_.refs_2_, bf16[128,1024]{1,0:T(8,128)(2,1)} %get-tuple-element.76.refs_3_), custom_call_target="tpu_custom_call" | custom-call | flops 1 | bytes 1 | tf_op jit(solution)/shard_map/pallas_call | solution.py:42
  (45 shorter events, 1.7 us)
Async XLA Ops:
  0.6 4.6 %copy-start.4 = (bf16[1,128,1024]{2,1,0:T(8,128)(2,1)S(1)}, bf16[1,128,1024]{2,1,0:T(8,128)(2,1)}, u32[]{:S(2)}) copy-start(bf16[1,128,1024]{2,1,0:T(8,128)(2,1)} %param.8) | copy-start | bytes 786436
  0.6 6.6 %copy-start = (bf16[1,128,1024]{2,1,0:T(8,128)(2,1)S(1)}, bf16[1,128,1024]{2,1,0:T(8,128)(2,1)}, u32[]{:S(2)}) copy-start(bf16[1,128,1024]{2,1,0:T(8,128)(2,1)} %param.6) | copy-start | bytes 786436
  0.7 6.6 %copy-start.1 = (bf16[1,128,1024]{2,1,0:T(8,128)(2,1)S(1)}, bf16[1,128,1024]{2,1,0:T(8,128)(2,1)}, u32[]{:S(2)}) copy-start(bf16[1,128,1024]{2,1,0:T(8,128)(2,1)} %param.7) | copy-start | bytes 786436
  0.7 6.6 %copy-start.3 = (bf16[1,128,1024]{2,1,0:T(8,128)(2,1)S(1)}, bf16[1,128,1024]{2,1,0:T(8,128)(2,1)}, u32[]{:S(2)}) copy-start(bf16[1,128,1024]{2,1,0:T(8,128)(2,1)} %param.5) | copy-start | bytes 786436
  2.2 7.4 %collective-permute-start.1 = (bf16[256,256]{1,0:T(8,128)(2,1)S(1)}, bf16[256,256]{1,0:T(8,128)(2,1)S(1)}, u32[]{:S(2)}, u32[]{:S(2)}) collective-permute-start(bf16[256,256]{1,0:T(8,128)(2,1)S(1)} %get-tuple-element.47), channel_id=1, source_target_pairs={{0,2},{1,3},{2,0},{3,1},{4,6},{5,7},{6,4},{7,5},{8,10},{9,11},{10,... | collective-permute-start | bytes 393224 | tf_op jit(solution)/shard_map/ppermute | solution.py:60
  5.3 9.6 %collective-permute-start.6 = (bf16[128,1024]{1,0:T(8,128)(2,1)S(1)}, bf16[128,1024]{1,0:T(8,128)(2,1)S(1)}, u32[]{:S(2)}, u32[]{:S(2)}) collective-permute-start(bf16[128,1024]{1,0:T(8,128)(2,1)S(1)} %bitcast.19), channel_id=1, source_target_pairs={{0,2},{1,3},{2,0},{3,1},{4,6},{5,7},{6,4},{7,5},{8,10},{9,11},{10,... | collective-permute-start | bytes 786440 | tf_op jit(solution)/shard_map/ppermute | solution.py:60
  5.4 15.1 %collective-permute-start.8 = (bf16[2,512,256]{2,1,0:T(8,128)(2,1)S(1)}, bf16[2,512,256]{2,1,0:T(8,128)(2,1)S(1)}, u32[]{:S(2)}, u32[]{:S(2)}) collective-permute-start(bf16[2,512,256]{2,1,0:T(8,128)(2,1)S(1)} %get-tuple-element.49.refs_3_.refs_1_), channel_id=1, source_target_pairs={{0,16},{16,0},{1,17},{17,1},{2,18},{18,2},{3,19},{19,3},{4,20},{20... | collective-permute-start | bytes 1572872 | tf_op jit(solution)/shard_map/ppermute | solution.py:60
  8.6 4.6 %collective-permute-start = (bf16[1024,256]{1,0:T(8,128)(2,1)S(1)}, bf16[1024,256]{1,0:T(8,128)(2,1)S(1)}, u32[]{:S(2)}, u32[]{:S(2)}) collective-permute-start(bf16[1024,256]{1,0:T(8,128)(2,1)S(1)} %get-tuple-element.44.refs_5_), channel_id=1, source_target_pairs={{0,1},{1,0},{2,3},{3,2},{4,5},{5,4},{6,7},{7,6},{8,9},{9,8},{10,11... | collective-permute-start | bytes 1572872 | tf_op jit(solution)/shard_map/ppermute | solution.py:60
  9.6 1.4 %collective-permute-start.2 = (bf16[256,256]{1,0:T(8,128)(2,1)S(1)}, bf16[256,256]{1,0:T(8,128)(2,1)S(1)}, u32[]{:S(2)}, u32[]{:S(2)}) collective-permute-start(bf16[256,256]{1,0:T(8,128)(2,1)S(1)} %shard_map.94.refs_3_), channel_id=1, source_target_pairs={{0,1},{1,0},{2,3},{3,2},{4,5},{5,4},{6,7},{7,6},{8,9},{9,8},{10,11... | collective-permute-start | bytes 393224 | tf_op jit(solution)/shard_map/ppermute | solution.py:60
  11.1 4.6 %collective-permute-start.4 = (bf16[128,256]{1,0:T(8,128)(2,1)S(1)}, bf16[128,256]{1,0:T(8,128)(2,1)S(1)}, u32[]{:S(2)}, u32[]{:S(2)}) collective-permute-start(bf16[128,256]{1,0:T(8,128)(2,1)S(1)} %shard_map.95.refs_2_.refs_0_), channel_id=1, source_target_pairs={{0,4},{1,5},{2,6},{3,7},{4,0},{5,1},{6,2},{7,3},{8,12},{9,13},{10,... | collective-permute-start | bytes 196616 | tf_op jit(solution)/shard_map/ppermute | solution.py:380
  13.3 9.1 %collective-permute-start.3 = (bf16[512,256]{1,0:T(8,128)(2,1)S(1)}, bf16[512,256]{1,0:T(8,128)(2,1)S(1)}, u32[]{:S(2)}, u32[]{:S(2)}) collective-permute-start(bf16[512,256]{1,0:T(8,128)(2,1)S(1)} %shard_map.96.refs_2_), channel_id=1, source_target_pairs={{0,2},{1,3},{2,0},{3,1},{4,6},{5,7},{6,4},{7,5},{8,10},{9,11},{10,... | collective-permute-start | bytes 786440 | tf_op jit(solution)/shard_map/ppermute | solution.py:60
  14.9 6.1 %collective-permute-start.7 = (bf16[128,1024]{1,0:T(8,128)(2,1)S(1)}, bf16[128,1024]{1,0:T(8,128)(2,1)S(1)}, u32[]{:S(2)}, u32[]{:S(2)}) collective-permute-start(bf16[128,1024]{1,0:T(8,128)(2,1)S(1)} %collective-permute-done.6.refs_2_), channel_id=1, source_target_pairs={{0,1},{1,0},{2,3},{3,2},{4,5},{5,4},{6,7},{7,6},{8,9},{9,8},{10,11... | collective-permute-start | bytes 786440 | tf_op jit(solution)/shard_map/ppermute | solution.py:60
  15.7 6.7 %collective-permute-start.5 = (bf16[128,256]{1,0:T(8,128)(2,1)S(1)}, bf16[128,256]{1,0:T(8,128)(2,1)S(1)}, u32[]{:S(2)}, u32[]{:S(2)}) collective-permute-start(bf16[128,256]{1,0:T(8,128)(2,1)S(1)} %shard_map.97.refs_5_), channel_id=1, source_target_pairs={{0,8},{1,9},{2,10},{3,11},{4,12},{5,13},{6,14},{7,15},{16,24},{17,... | collective-permute-start | bytes 196616 | tf_op jit(solution)/shard_map/ppermute | solution.py:380
  20.9 10.2 %collective-permute-start.12 = (bf16[2,512,256]{2,1,0:T(8,128)(2,1)S(1)}, bf16[2,512,256]{2,1,0:T(8,128)(2,1)S(1)}, u32[]{:S(2)}, u32[]{:S(2)}) collective-permute-start(bf16[2,512,256]{2,1,0:T(8,128)(2,1)S(1)} %collective-permute-done.8.refs_4_.refs_2_.refs_8_), channel_id=1, source_target_pairs={{0,1},{1,0},{2,3},{3,2},{4,5},{5,4},{6,7},{7,6},{8,9},{9,8},{10,11... | collective-permute-start | bytes 1572872 | tf_op jit(solution)/shard_map/ppermute | solution.py:60
  23.4 7.7 %collective-permute-start.11 = (bf16[512,256]{1,0:T(8,128)(2,1)S(1)}, bf16[512,256]{1,0:T(8,128)(2,1)S(1)}, u32[]{:S(2)}, u32[]{:S(2)}) collective-permute-start(bf16[512,256]{1,0:T(8,128)(2,1)S(1)} %shard_map.102.refs_7_), channel_id=1, source_target_pairs={{0,16},{16,0},{1,17},{17,1},{2,18},{18,2},{3,19},{19,3},{4,20},{20... | collective-permute-start | bytes 786440 | tf_op jit(solution)/shard_map/ppermute | solution.py:60
  25.6 8.5 %collective-permute-start.9 = (bf16[512,256]{1,0:T(8,128)(2,1)S(1)}, bf16[512,256]{1,0:T(8,128)(2,1)S(1)}, u32[]{:S(2)}, u32[]{:S(2)}) collective-permute-start(bf16[512,256]{1,0:T(8,128)(2,1)S(1)} %get-tuple-element.58), channel_id=1, source_target_pairs={{0,2},{1,3},{2,0},{3,1},{4,6},{5,7},{6,4},{7,5},{8,10},{9,11},{10,... | collective-permute-start | bytes 786440 | tf_op jit(solution)/shard_map/ppermute | solution.py:60
  27.2 5.5 %collective-permute-start.10 = (bf16[128,256]{1,0:T(8,128)(2,1)S(1)}, bf16[128,256]{1,0:T(8,128)(2,1)S(1)}, u32[]{:S(2)}, u32[]{:S(2)}) collective-permute-start(bf16[128,256]{1,0:T(8,128)(2,1)S(1)} %get-tuple-element.59.refs_3_.refs_0_), channel_id=1, source_target_pairs={{0,4},{1,5},{2,6},{3,7},{4,0},{5,1},{6,2},{7,3},{8,12},{9,13},{10,... | collective-permute-start | bytes 196616 | tf_op jit(solution)/shard_map/ppermute | solution.py:380
  31.1 5.5 %collective-permute-start.15 = (bf16[256,256]{1,0:T(8,128)(2,1)S(1)}, bf16[256,256]{1,0:T(8,128)(2,1)S(1)}, u32[]{:S(2)}, u32[]{:S(2)}) collective-permute-start(bf16[256,256]{1,0:T(8,128)(2,1)S(1)} %get-tuple-element.61.refs_2_), channel_id=1, source_target_pairs={{0,4},{1,5},{2,6},{3,7},{4,0},{5,1},{6,2},{7,3},{8,12},{9,13},{10,... | collective-permute-start | bytes 393224 | tf_op jit(solution)/shard_map/ppermute | solution.py:60
  32.7 9.8 %collective-permute-start.14 = (bf16[128,256]{1,0:T(8,128)(2,1)S(1)}, bf16[128,256]{1,0:T(8,128)(2,1)S(1)}, u32[]{:S(2)}, u32[]{:S(2)}) collective-permute-start(bf16[128,256]{1,0:T(8,128)(2,1)S(1)} %shard_map.106.refs_2_), channel_id=1, source_target_pairs={{8,0},{9,1},{10,2},{11,3},{12,4},{13,5},{14,6},{15,7},{24,16},{25,... | collective-permute-start | bytes 196616 | tf_op jit(solution)/shard_map/ppermute | solution.py:380
  34.1 10.1 %collective-permute-start.13 = (bf16[512,256]{1,0:T(8,128)(2,1)S(1)}, bf16[512,256]{1,0:T(8,128)(2,1)S(1)}, u32[]{:S(2)}, u32[]{:S(2)}) collective-permute-start(bf16[512,256]{1,0:T(8,128)(2,1)S(1)} %shard_map.107.refs_2_), channel_id=1, source_target_pairs={{0,1},{1,0},{2,3},{3,2},{4,5},{5,4},{6,7},{7,6},{8,9},{9,8},{10,11... | collective-permute-start | bytes 786440 | tf_op jit(solution)/shard_map/ppermute | solution.py:60
  36.6 9.7 %collective-permute-start.17 = (bf16[128,256]{1,0:T(8,128)(2,1)S(1)}, bf16[128,256]{1,0:T(8,128)(2,1)S(1)}, u32[]{:S(2)}, u32[]{:S(2)}) collective-permute-start(bf16[128,256]{1,0:T(8,128)(2,1)S(1)} %get-tuple-element.64.refs_3_), channel_id=1, source_target_pairs={{0,8},{1,9},{2,10},{3,11},{4,12},{5,13},{6,14},{7,15},{8,0},{9,1},... | collective-permute-start | bytes 196616 | tf_op jit(solution)/shard_map/ppermute | solution.py:60
  42.7 5.0 %collective-permute-start.16 = (bf16[256,256]{1,0:T(8,128)(2,1)S(1)}, bf16[256,256]{1,0:T(8,128)(2,1)S(1)}, u32[]{:S(2)}, u32[]{:S(2)}) collective-permute-start(bf16[256,256]{1,0:T(8,128)(2,1)S(1)} %get-tuple-element.66.refs_7_), channel_id=1, source_target_pairs={{0,2},{1,3},{2,0},{3,1},{4,6},{5,7},{6,4},{7,5},{8,10},{9,11},{10,... | collective-permute-start | bytes 393224 | tf_op jit(solution)/shard_map/ppermute | solution.py:60
  46.3 1.5 %copy-start.2 = (bf16[512,1024]{1,0:T(8,128)(2,1)S(1)}, bf16[512,1024]{1,0:T(8,128)(2,1)}, u32[]{:S(2)}) copy-start(bf16[512,1024]{1,0:T(8,128)(2,1)} %refs_7_.1) | copy-start | bytes 3145732
  46.3 4.0 %collective-permute-start.19 = (bf16[64,256]{1,0:T(8,128)(2,1)S(1)}, bf16[64,256]{1,0:T(8,128)(2,1)S(1)}, u32[]{:S(2)}, u32[]{:S(2)}) collective-permute-start(bf16[64,256]{1,0:T(8,128)(2,1)S(1)} %get-tuple-element.70.refs_2_), channel_id=1, source_target_pairs={{0,2},{1,3},{2,0},{3,1},{4,6},{5,7},{6,4},{7,5},{8,10},{9,11},{10,... | collective-permute-start | bytes 98312 | tf_op jit(solution)/shard_map/ppermute | solution.py:60
  47.7 2.7 %collective-permute-start.18 = (bf16[256,256]{1,0:T(8,128)(2,1)S(1)}, bf16[256,256]{1,0:T(8,128)(2,1)S(1)}, u32[]{:S(2)}, u32[]{:S(2)}) collective-permute-start(bf16[256,256]{1,0:T(8,128)(2,1)S(1)} %shard_map.112.refs_10_.refs_2_), channel_id=1, source_target_pairs={{0,1},{1,0},{2,3},{3,2},{4,5},{5,4},{6,7},{7,6},{8,9},{9,8},{10,11... | collective-permute-start | bytes 393224 | tf_op jit(solution)/shard_map/ppermute | solution.py:60
  50.3 1.3 %collective-permute-start.20 = (bf16[64,256]{1,0:T(8,128)(2,1)S(1)}, bf16[64,256]{1,0:T(8,128)(2,1)S(1)}, u32[]{:S(2)}, u32[]{:S(2)}) collective-permute-start(bf16[64,256]{1,0:T(8,128)(2,1)S(1)} %get-tuple-element.75.refs_7_.refs_2_), channel_id=1, source_target_pairs={{0,1},{1,0},{2,3},{3,2},{4,5},{5,4},{6,7},{7,6},{8,9},{9,8},{10,11... | collective-permute-start | bytes 98312 | tf_op jit(solution)/shard_map/ppermute | solution.py:60

commit v21 on v19

--- a/solution.py
+++ b/solution.py
@@ -88,9 +88,10 @@
     return copies
 
 
-def front_kernel(k_hbm, v_hbm, w_hbm, own_ref, near_ref, far_ref, columns_ref, k_ref, v_ref, w_ref, sems):
-    copies = fetch([(k_hbm, k_ref), (v_hbm, v_ref), (w_hbm, w_ref)], sems)
+def front_kernel(k_hbm, v_hbm, w_hbm, own_ref, near_ref, far_ref, columns_ref, k_ref, v_ref, sems):
     width = k_ref.shape[1] // SLAB
+    blocks = [(w_hbm.at[:, cut(member(2 * i), width)], columns_ref.at[i]) for i in range(2)]
+    copies = fetch([(k_hbm, k_ref), (v_hbm, v_ref), *blocks], sems)
     copies[0].wait()
     copies[1].wait()
     places = (own_ref, near_ref, far_ref.at[part(0, DH)], far_ref.at[part(1, DH)])
@@ -99,8 +100,7 @@
         for h in range(width // DH):
             out[:, head(h)] = dot(k[:, head(h)], v[:, head(h)], 0, 0).astype(out.dtype)
     copies[2].wait()
-    for i in range(2):
-        columns_ref[i] = w_ref[:, cut(member(2 * i), width)]
+    copies[3].wait()
 
 
 def pack_kernel(q_ref, k_ref, v_ref, c_ref, attend_ref, own_ref, message_ref, far_ref):
@@ -386,7 +386,7 @@
         front_kernel,
         [((DH, width), F32), ((DH, width), BF16), ((2 * DH, width), BF16),
          ((2, out_weight.shape[0], width), BF16)],
-        k, v, out_weight, far=True, scratch=scratch(k, v, out_weight),
+        k, v, out_weight, far=True, scratch=scratch(k, v)[:2] + [pltpu.SemaphoreType.DMA((4,))],
     )
     far_state = near(far_state, bits=2)
     w_far = [flip(columns, "dp", dp, j) for j in range(1, dp)]

time: 47.7 us -> 47.5 us (level)
  no operation moved by 1% of the time
where the time goes in v21:
time: 47.5 us; the launch traced here: 47.4 us
  starting transfers between devices  25.5 us (54%)
  Pallas kernels  11.9 us (25%)
  waiting for transfers between devices  9.06 us (19%)
  between operations  0.84 us (2%)
    ppermute x21, starting transfers between devices, flip(): return lax.ppermute(x, axis, [(i, i ^ bits) for i in range(count)])  25.5 us
    pallas_call x25, Pallas kernels, __call__(): pl.pallas_call(inner, out_shape=[jax.ShapeDtypeStruct(s, d) for s, d in o...  11.9 us
    ppermute x21, waiting for transfers between devices, flip(): return lax.ppermute(x, axis, [(i, i ^ bits) for i in range(count)])  9.06 us
  transfers between devices with their start and end apart: 21, of which 11 were waited for; matrix products, arithmetic and copies ran while one was open for 0% of the time, Pallas kernels for 21%

profile of v21, /device:TPU:0, one launch (start us, length us, event | category | flops | bytes accessed | tf_op | source)
XLA Modules:
  0.0 47.4 jit_solution(16878108207920950587)
XLA Ops:
  0.7 1.4 %shard_map.92 = (f32[128,256]{1,0:T(8,128)S(1)}, bf16[128,256]{1,0:T(8,128)(2,1)S(1)}, bf16[256,256]{1,0:T(8,128)(2,1)S(1)}, bf16[2,512,256]{2,1,0:T(8,128)(2,1)S(1)}) custom-call(bf16[128,1024]{1,0:T(8,128)(2,1)} %bitcast.8, bf16[128,1024]{1,0:T(8,128)(2,1)} %bitcast.12, bf16[512,1024]{1,0:T(8,128)(2,1)} %refs_7_.1), custom_call_target="tpu_custom_call" | custom-call | flops 1 | bytes 1 | tf_op jit(solution)/shard_map/pallas_call | solution.py:42
  2.1 3.0 %collective-permute-start.1 = (bf16[256,256]{1,0:T(8,128)(2,1)S(1)}, bf16[256,256]{1,0:T(8,128)(2,1)S(1)}, u32[]{:S(2)}, u32[]{:S(2)}) collective-permute-start(bf16[256,256]{1,0:T(8,128)(2,1)S(1)} %get-tuple-element.47), channel_id=1, source_target_pairs={{0,2},{1,3},{2,0},{3,1},{4,6},{5,7},{6,4},{7,5},{8,10},{9,11},{10,... | collective-permute-start | bytes 393224 | tf_op jit(solution)/shard_map/ppermute | solution.py:60
  5.2 1.9 %collective-permute-start.8 = (bf16[2,512,256]{2,1,0:T(8,128)(2,1)S(1)}, bf16[2,512,256]{2,1,0:T(8,128)(2,1)S(1)}, u32[]{:S(2)}, u32[]{:S(2)}) collective-permute-start(bf16[2,512,256]{2,1,0:T(8,128)(2,1)S(1)} %get-tuple-element.49.refs_3_.refs_1_), channel_id=1, source_target_pairs={{0,16},{16,0},{1,17},{17,1},{2,18},{18,2},{3,19},{19,3},{4,20},{20... | collective-permute-start | bytes 1572872 | tf_op jit(solution)/shard_map/ppermute | solution.py:60
  7.1 1.4 %shard_map.93 = (bf16[4,2,128,128]{3,2,1,0:T(8,128)(2,1)S(1)}, bf16[256,256]{1,0:T(8,128)(2,1)S(1)}, bf16[1024,256]{1,0:T(8,128)(2,1)S(1)}, bf16[256,256]{1,0:T(8,128)(2,1)S(1)}) custom-call(bf16[128,1024]{1,0:T(8,128)(2,1)S(1)} %bitcast.16, bf16[128,1024]{1,0:T(8,128)(2,1)S(1)} %bitcast.9, bf16[128,1024]{1,0:T(8,128)(2,1)S(1)} %bitcast.13, ...), custom_call_target="tpu_custom_call" | custom-call | flops 1 | bytes 1 | tf_op jit(solution)/shard_map/pallas_call | solution.py:42
  8.6 0.9 %collective-permute-done.1.refs_1_.refs_4_ = bf16[256,256]{1,0:T(8,128)(2,1)S(1)} collective-permute-done((bf16[256,256]{1,0:T(8,128)(2,1)S(1)}, bf16[256,256]{1,0:T(8,128)(2,1)S(1)}, u32[]{:S(2)}, u32[]{:S(2)}) %collective-permute-start.1) | collective-permute-done | bytes 131104 | tf_op jit(solution)/shard_map/ppermute | solution.py:60
  9.5 1.3 %collective-permute-done.2.refs_2_.refs_5_ = bf16[256,256]{1,0:T(8,128)(2,1)S(1)} collective-permute-done((bf16[256,256]{1,0:T(8,128)(2,1)S(1)}, bf16[256,256]{1,0:T(8,128)(2,1)S(1)}, u32[]{:S(2)}, u32[]{:S(2)}) %collective-permute-start.2) | collective-permute-done | bytes 131104 | tf_op jit(solution)/shard_map/ppermute | solution.py:60
  10.9 2.2 %collective-permute-start.4 = (bf16[128,256]{1,0:T(8,128)(2,1)S(1)}, bf16[128,256]{1,0:T(8,128)(2,1)S(1)}, u32[]{:S(2)}, u32[]{:S(2)}) collective-permute-start(bf16[128,256]{1,0:T(8,128)(2,1)S(1)} %shard_map.95.refs_2_.refs_0_), channel_id=1, source_target_pairs={{0,4},{1,5},{2,6},{3,7},{4,0},{5,1},{6,2},{7,3},{8,12},{9,13},{10,... | collective-permute-start | bytes 196616 | tf_op jit(solution)/shard_map/ppermute | solution.py:60
  13.1 1.6 %collective-permute-start.3 = (bf16[512,256]{1,0:T(8,128)(2,1)S(1)}, bf16[512,256]{1,0:T(8,128)(2,1)S(1)}, u32[]{:S(2)}, u32[]{:S(2)}) collective-permute-start(bf16[512,256]{1,0:T(8,128)(2,1)S(1)} %shard_map.96.refs_2_), channel_id=1, source_target_pairs={{0,2},{1,3},{2,0},{3,1},{4,6},{5,7},{6,4},{7,5},{8,10},{9,11},{10,... | collective-permute-start | bytes 786440 | tf_op jit(solution)/shard_map/ppermute | solution.py:60
  14.7 0.8 %collective-permute-done.4.refs_1_.refs_0_ = bf16[128,256]{1,0:T(8,128)(2,1)S(1)} collective-permute-done((bf16[128,256]{1,0:T(8,128)(2,1)S(1)}, bf16[128,256]{1,0:T(8,128)(2,1)S(1)}, u32[]{:S(2)}, u32[]{:S(2)}) %collective-permute-start.4) | collective-permute-done | bytes 65568 | tf_op jit(solution)/shard_map/ppermute | solution.py:60
  15.5 2.9 %collective-permute-start.5 = (bf16[128,256]{1,0:T(8,128)(2,1)S(1)}, bf16[128,256]{1,0:T(8,128)(2,1)S(1)}, u32[]{:S(2)}, u32[]{:S(2)}) collective-permute-start(bf16[128,256]{1,0:T(8,128)(2,1)S(1)} %shard_map.97.refs_5_), channel_id=1, source_target_pairs={{0,8},{1,9},{2,10},{3,11},{4,12},{5,13},{6,14},{7,15},{8,0},{9,1},... | collective-permute-start | bytes 196616 | tf_op jit(solution)/shard_map/ppermute | solution.py:60
  18.6 0.4 shard_map.98
  19.4 1.7 %collective-permute-done.5.refs_1_ = bf16[128,256]{1,0:T(8,128)(2,1)S(1)} collective-permute-done((bf16[128,256]{1,0:T(8,128)(2,1)S(1)}, bf16[128,256]{1,0:T(8,128)(2,1)S(1)}, u32[]{:S(2)}, u32[]{:S(2)}) %collective-permute-start.5) | collective-permute-done | bytes 65568 | tf_op jit(solution)/shard_map/ppermute | solution.py:60
  21.3 0.5 shard_map.101
  21.7 0.5 %shard_map.102.refs_7_ = bf16[512,256]{1,0:T(8,128)(2,1)S(1)} custom-call(bf16[3,128,1024]{2,1,0:T(8,128)(2,1)S(1)} %get-tuple-element.54.refs_0_, bf16[1,128,1024]{2,1,0:T(8,128)(2,1)S(1)} %get-tuple-element.55.refs_1_, bf16[4,128,256]{2,1,0:T(8,128)(2,1)S(1)} %get-tuple-element.56.refs_2_, bf16[4,128,256]{2,1,0:T(8,128)(2,1)S(1)} %get-tuple-element.53.refs_3_.refs_4_), custom_call_target="tpu_custom_call" | custom-call | flops 1 | bytes 1 | tf_op jit(solution)/shard_map/pallas_call | solution.py:42
  22.2 1.5 %collective-permute-start.11 = (bf16[512,256]{1,0:T(8,128)(2,1)S(1)}, bf16[512,256]{1,0:T(8,128)(2,1)S(1)}, u32[]{:S(2)}, u32[]{:S(2)}) collective-permute-start(bf16[512,256]{1,0:T(8,128)(2,1)S(1)} %shard_map.102.refs_7_), channel_id=1, source_target_pairs={{0,16},{16,0},{1,17},{17,1},{2,18},{18,2},{3,19},{19,3},{4,20},{20... | collective-permute-start | bytes 786440 | tf_op jit(solution)/shard_map/ppermute | solution.py:60
  23.8 0.7 %shard_map.103 = (bf16[512,256]{1,0:T(8,128)(2,1)S(1)}, bf16[512,256]{1,0:T(8,128)(2,1)S(1)}, f32[4,128,256]{2,1,0:T(8,128)S(1)}, bf16[128,256]{1,0:T(8,128)(2,1)S(1)}) custom-call(bf16[256,256]{1,0:T(8,128)(2,1)S(1)} %get-tuple-element.43.refs_0_.refs_4_, bf16[1024,256]{1,0:T(8,128)(2,1)S(1)} %collective-permute-done.refs_0_.refs_1_, ...), custom_call_target="tpu_custom_call" | custom-call | flops 1 | bytes 1 | tf_op jit(solution)/shard_map/pallas_call | solution.py:42
  24.5 1.6 %collective-permute-start.9 = (bf16[512,256]{1,0:T(8,128)(2,1)S(1)}, bf16[512,256]{1,0:T(8,128)(2,1)S(1)}, u32[]{:S(2)}, u32[]{:S(2)}) collective-permute-start(bf16[512,256]{1,0:T(8,128)(2,1)S(1)} %get-tuple-element.58), channel_id=1, source_target_pairs={{0,2},{1,3},{2,0},{3,1},{4,6},{5,7},{6,4},{7,5},{8,10},{9,11},{10,... | collective-permute-start | bytes 786440 | tf_op jit(solution)/shard_map/ppermute | solution.py:60
  26.1 1.4 %collective-permute-start.10 = (bf16[128,256]{1,0:T(8,128)(2,1)S(1)}, bf16[128,256]{1,0:T(8,128)(2,1)S(1)}, u32[]{:S(2)}, u32[]{:S(2)}) collective-permute-start(bf16[128,256]{1,0:T(8,128)(2,1)S(1)} %get-tuple-element.59.refs_3_.refs_0_), channel_id=1, source_target_pairs={{0,4},{1,5},{2,6},{3,7},{4,0},{5,1},{6,2},{7,3},{8,12},{9,13},{10,... | collective-permute-start | bytes 196616 | tf_op jit(solution)/shard_map/ppermute | solution.py:60
  27.5 0.5 %shard_map.104.refs_0_.refs_2_ = f32[512,256]{1,0:T(8,128)S(1)} custom-call(bf16[3,128,1024]{2,1,0:T(8,128)(2,1)S(1)} %get-tuple-element.54.refs_0_, bf16[1,128,1024]{2,1,0:T(8,128)(2,1)S(1)} %get-tuple-element.55.refs_1_, bf16[4,128,256]{2,1,0:T(8,128)(2,1)S(1)} %get-tuple-element.56.refs_2_, bf16[128,256]{1,0:T(8,128)(2,1)S(1)} %get-tuple-element.59.refs_3_.refs_0_), custom_call_target="tpu_custom_call" | custom-call | flops 1 | bytes 1 | tf_op jit(solution)/shard_map/pallas_call | solution.py:42
  28.0 1.6 %collective-permute-done.11.refs_1_ = bf16[512,256]{1,0:T(8,128)(2,1)S(1)} collective-permute-done((bf16[512,256]{1,0:T(8,128)(2,1)S(1)}, bf16[512,256]{1,0:T(8,128)(2,1)S(1)}, u32[]{:S(2)}, u32[]{:S(2)}) %collective-permute-start.11) | collective-permute-done | bytes 262176 | tf_op jit(solution)/shard_map/ppermute | solution.py:60
  29.6 1.4 %collective-permute-start.15 = (bf16[256,256]{1,0:T(8,128)(2,1)S(1)}, bf16[256,256]{1,0:T(8,128)(2,1)S(1)}, u32[]{:S(2)}, u32[]{:S(2)}) collective-permute-start(bf16[256,256]{1,0:T(8,128)(2,1)S(1)} %get-tuple-element.61.refs_2_), channel_id=1, source_target_pairs={{0,4},{1,5},{2,6},{3,7},{4,0},{5,1},{6,2},{7,3},{8,12},{9,13},{10,... | collective-permute-start | bytes 393224 | tf_op jit(solution)/shard_map/ppermute | solution.py:60
  31.0 2.6 %collective-permute-start.14 = (bf16[128,256]{1,0:T(8,128)(2,1)S(1)}, bf16[128,256]{1,0:T(8,128)(2,1)S(1)}, u32[]{:S(2)}, u32[]{:S(2)}) collective-permute-start(bf16[128,256]{1,0:T(8,128)(2,1)S(1)} %shard_map.106.refs_2_), channel_id=1, source_target_pairs={{0,8},{1,9},{2,10},{3,11},{4,12},{5,13},{6,14},{7,15},{8,0},{9,1},... | collective-permute-start | bytes 196616 | tf_op jit(solution)/shard_map/ppermute | solution.py:60
  33.8 0.8 %collective-permute-done.15.refs_1_ = bf16[256,256]{1,0:T(8,128)(2,1)S(1)} collective-permute-done((bf16[256,256]{1,0:T(8,128)(2,1)S(1)}, bf16[256,256]{1,0:T(8,128)(2,1)S(1)}, u32[]{:S(2)}, u32[]{:S(2)}) %collective-permute-start.15) | collective-permute-done | bytes 131104 | tf_op jit(solution)/shard_map/ppermute | solution.py:60
  34.6 2.6 %collective-permute-start.17 = (bf16[128,256]{1,0:T(8,128)(2,1)S(1)}, bf16[128,256]{1,0:T(8,128)(2,1)S(1)}, u32[]{:S(2)}, u32[]{:S(2)}) collective-permute-start(bf16[128,256]{1,0:T(8,128)(2,1)S(1)} %get-tuple-element.64.refs_3_), channel_id=1, source_target_pairs={{0,8},{1,9},{2,10},{3,11},{4,12},{5,13},{6,14},{7,15},{8,0},{9,1},... | collective-permute-start | bytes 196616 | tf_op jit(solution)/shard_map/ppermute | solution.py:60
  37.4 1.6 %collective-permute-start.16 = (bf16[256,256]{1,0:T(8,128)(2,1)S(1)}, bf16[256,256]{1,0:T(8,128)(2,1)S(1)}, u32[]{:S(2)}, u32[]{:S(2)}) collective-permute-start(bf16[256,256]{1,0:T(8,128)(2,1)S(1)} %get-tuple-element.66.refs_7_), channel_id=1, source_target_pairs={{0,2},{1,3},{2,0},{3,1},{4,6},{5,7},{6,4},{7,5},{8,10},{9,11},{10,... | collective-permute-start | bytes 393224 | tf_op jit(solution)/shard_map/ppermute | solution.py:60
  39.0 2.1 %shard_map.110 = (bf16[128,1024]{1,0:T(8,128)(2,1)}, f32[4,128,256]{2,1,0:T(8,128)S(1)}, f32[4,128,256]{2,1,0:T(8,128)S(1)}) custom-call(bf16[512,256]{1,0:T(8,128)(2,1)S(1)} %get-tuple-element.57.refs_0_, bf16[512,256]{1,0:T(8,128)(2,1)S(1)} %collective-permute-done.9.refs_1_, bf16[512,256]{1,0:T(8,128)(2,1)S(1)} %collective-permute-done.13.refs_2_, ...), custom_call_target="tpu_custom_call" | custom-call | flops 1 | bytes 1 | tf_op jit(solution)/shard_map/pallas_call | solution.py:42
  41.3 0.4 collective-permute-start.19
  41.7 1.1 %collective-permute-done.16.refs_1_ = bf16[256,256]{1,0:T(8,128)(2,1)S(1)} collective-permute-done((bf16[256,256]{1,0:T(8,128)(2,1)S(1)}, bf16[256,256]{1,0:T(8,128)(2,1)S(1)}, u32[]{:S(2)}, u32[]{:S(2)}) %collective-permute-start.16) | collective-permute-done | bytes 131104 | tf_op jit(solution)/shard_map/ppermute | solution.py:60
  42.9 2.1 %shard_map.113 = (bf16[128,1024]{1,0:T(8,128)(2,1)}, bf16[128,1024]{1,0:T(8,128)(2,1)}) custom-call(bf16[512,256]{1,0:T(8,128)(2,1)S(1)} %get-tuple-element.57.refs_0_, bf16[512,256]{1,0:T(8,128)(2,1)S(1)} %collective-permute-done.9.refs_1_, bf16[512,256]{1,0:T(8,128)(2,1)S(1)} %collective-permute-done.13.refs_2_, bf16[128,1024]{1,0:T(8,128)(2,1)S(1)} %bitcast.18, ...), custom_call_target="tpu_custom_call" | custom-call | flops 1 | bytes 1 | tf_op jit(solution)/shard_map/pallas_call | solution.py:42
  45.0 0.3 collective-permute-done.19.refs_1_
  45.5 1.1 %shard_map.115 = (bf16[128,1024]{1,0:T(8,128)(2,1)}, bf16[128,1024]{1,0:T(8,128)(2,1)}) custom-call(bf16[256,256]{1,0:T(8,128)(2,1)S(1)} %get-tuple-element.65.refs_0_, bf16[256,256]{1,0:T(8,128)(2,1)S(1)} %collective-permute-done.16.refs_1_, bf16[256,256]{1,0:T(8,128)(2,1)S(1)} %collective-permute-done.18.refs_2_, bf16[128,1024]{1,0:T(8,128)(2,1)S(1)} %bitcast.11, ...), custom_call_target="tpu_custom_call" | custom-call | flops 1 | bytes 1 | tf_op jit(solution)/shard_map/pallas_call | solution.py:42
  46.7 0.7 %shard_map.116 = f32[32,1024]{1,0:T(8,128)} custom-call(bf16[64,256]{1,0:T(8,128)(2,1)S(1)} %get-tuple-element.78.refs_0_, bf16[64,256]{1,0:T(8,128)(2,1)S(1)} %collective-permute-done.20.refs_1_, bf16[64,256]{1,0:T(8,128)(2,1)S(1)} %get-tuple-element.75.refs_7_.refs_2_, bf16[128,1024]{1,0:T(8,128)(2,1)} %get-tuple-element.76.refs_3_), custom_call_target="tpu_custom_call" | custom-call | flops 1 | bytes 1 | tf_op jit(solution)/shard_map/pallas_call | solution.py:42
  (45 shorter events, 1.8 us)
Async XLA Ops:
  0.6 4.5 %copy-start.4 = (bf16[1,128,1024]{2,1,0:T(8,128)(2,1)S(1)}, bf16[1,128,1024]{2,1,0:T(8,128)(2,1)}, u32[]{:S(2)}) copy-start(bf16[1,128,1024]{2,1,0:T(8,128)(2,1)} %param.8) | copy-start | bytes 786436
  0.6 6.5 %copy-start = (bf16[1,128,1024]{2,1,0:T(8,128)(2,1)S(1)}, bf16[1,128,1024]{2,1,0:T(8,128)(2,1)}, u32[]{:S(2)}) copy-start(bf16[1,128,1024]{2,1,0:T(8,128)(2,1)} %param.6) | copy-start | bytes 786436
  0.7 6.5 %copy-start.1 = (bf16[1,128,1024]{2,1,0:T(8,128)(2,1)S(1)}, bf16[1,128,1024]{2,1,0:T(8,128)(2,1)}, u32[]{:S(2)}) copy-start(bf16[1,128,1024]{2,1,0:T(8,128)(2,1)} %param.7) | copy-start | bytes 786436
  0.7 6.5 %copy-start.3 = (bf16[1,128,1024]{2,1,0:T(8,128)(2,1)S(1)}, bf16[1,128,1024]{2,1,0:T(8,128)(2,1)}, u32[]{:S(2)}) copy-start(bf16[1,128,1024]{2,1,0:T(8,128)(2,1)} %param.5) | copy-start | bytes 786436
  2.1 7.4 %collective-permute-start.1 = (bf16[256,256]{1,0:T(8,128)(2,1)S(1)}, bf16[256,256]{1,0:T(8,128)(2,1)S(1)}, u32[]{:S(2)}, u32[]{:S(2)}) collective-permute-start(bf16[256,256]{1,0:T(8,128)(2,1)S(1)} %get-tuple-element.47), channel_id=1, source_target_pairs={{0,2},{1,3},{2,0},{3,1},{4,6},{5,7},{6,4},{7,5},{8,10},{9,11},{10,... | collective-permute-start | bytes 393224 | tf_op jit(solution)/shard_map/ppermute | solution.py:60
  5.1 9.6 %collective-permute-start.6 = (bf16[128,1024]{1,0:T(8,128)(2,1)S(1)}, bf16[128,1024]{1,0:T(8,128)(2,1)S(1)}, u32[]{:S(2)}, u32[]{:S(2)}) collective-permute-start(bf16[128,1024]{1,0:T(8,128)(2,1)S(1)} %bitcast.19), channel_id=1, source_target_pairs={{0,2},{1,3},{2,0},{3,1},{4,6},{5,7},{6,4},{7,5},{8,10},{9,11},{10,... | collective-permute-start | bytes 786440 | tf_op jit(solution)/shard_map/ppermute | solution.py:60
  5.2 13.4 %collective-permute-start.8 = (bf16[2,512,256]{2,1,0:T(8,128)(2,1)S(1)}, bf16[2,512,256]{2,1,0:T(8,128)(2,1)S(1)}, u32[]{:S(2)}, u32[]{:S(2)}) collective-permute-start(bf16[2,512,256]{2,1,0:T(8,128)(2,1)S(1)} %get-tuple-element.49.refs_3_.refs_1_), channel_id=1, source_target_pairs={{0,16},{16,0},{1,17},{17,1},{2,18},{18,2},{3,19},{19,3},{4,20},{20... | collective-permute-start | bytes 1572872 | tf_op jit(solution)/shard_map/ppermute | solution.py:60
  8.5 4.6 %collective-permute-start = (bf16[1024,256]{1,0:T(8,128)(2,1)S(1)}, bf16[1024,256]{1,0:T(8,128)(2,1)S(1)}, u32[]{:S(2)}, u32[]{:S(2)}) collective-permute-start(bf16[1024,256]{1,0:T(8,128)(2,1)S(1)} %get-tuple-element.44.refs_5_), channel_id=1, source_target_pairs={{0,1},{1,0},{2,3},{3,2},{4,5},{5,4},{6,7},{7,6},{8,9},{9,8},{10,11... | collective-permute-start | bytes 1572872 | tf_op jit(solution)/shard_map/ppermute | solution.py:60
  9.5 1.4 %collective-permute-start.2 = (bf16[256,256]{1,0:T(8,128)(2,1)S(1)}, bf16[256,256]{1,0:T(8,128)(2,1)S(1)}, u32[]{:S(2)}, u32[]{:S(2)}) collective-permute-start(bf16[256,256]{1,0:T(8,128)(2,1)S(1)} %shard_map.94.refs_3_), channel_id=1, source_target_pairs={{0,1},{1,0},{2,3},{3,2},{4,5},{5,4},{6,7},{7,6},{8,9},{9,8},{10,11... | collective-permute-start | bytes 393224 | tf_op jit(solution)/shard_map/ppermute | solution.py:60
  10.9 4.6 %collective-permute-start.4 = (bf16[128,256]{1,0:T(8,128)(2,1)S(1)}, bf16[128,256]{1,0:T(8,128)(2,1)S(1)}, u32[]{:S(2)}, u32[]{:S(2)}) collective-permute-start(bf16[128,256]{1,0:T(8,128)(2,1)S(1)} %shard_map.95.refs_2_.refs_0_), channel_id=1, source_target_pairs={{0,4},{1,5},{2,6},{3,7},{4,0},{5,1},{6,2},{7,3},{8,12},{9,13},{10,... | collective-permute-start | bytes 196616 | tf_op jit(solution)/shard_map/ppermute | solution.py:60
  13.1 8.1 %collective-permute-start.3 = (bf16[512,256]{1,0:T(8,128)(2,1)S(1)}, bf16[512,256]{1,0:T(8,128)(2,1)S(1)}, u32[]{:S(2)}, u32[]{:S(2)}) collective-permute-start(bf16[512,256]{1,0:T(8,128)(2,1)S(1)} %shard_map.96.refs_2_), channel_id=1, source_target_pairs={{0,2},{1,3},{2,0},{3,1},{4,6},{5,7},{6,4},{7,5},{8,10},{9,11},{10,... | collective-permute-start | bytes 786440 | tf_op jit(solution)/shard_map/ppermute | solution.py:60
  14.7 4.4 %collective-permute-start.7 = (bf16[128,1024]{1,0:T(8,128)(2,1)S(1)}, bf16[128,1024]{1,0:T(8,128)(2,1)S(1)}, u32[]{:S(2)}, u32[]{:S(2)}) collective-permute-start(bf16[128,1024]{1,0:T(8,128)(2,1)S(1)} %collective-permute-done.6.refs_2_), channel_id=1, source_target_pairs={{0,1},{1,0},{2,3},{3,2},{4,5},{5,4},{6,7},{7,6},{8,9},{9,8},{10,11... | collective-permute-start | bytes 786440 | tf_op jit(solution)/shard_map/ppermute | solution.py:60
  15.5 5.6 %collective-permute-start.5 = (bf16[128,256]{1,0:T(8,128)(2,1)S(1)}, bf16[128,256]{1,0:T(8,128)(2,1)S(1)}, u32[]{:S(2)}, u32[]{:S(2)}) collective-permute-start(bf16[128,256]{1,0:T(8,128)(2,1)S(1)} %shard_map.97.refs_5_), channel_id=1, source_target_pairs={{0,8},{1,9},{2,10},{3,11},{4,12},{5,13},{6,14},{7,15},{8,0},{9,1},... | collective-permute-start | bytes 196616 | tf_op jit(solution)/shard_map/ppermute | solution.py:60
  19.0 10.5 %collective-permute-start.12 = (bf16[2,512,256]{2,1,0:T(8,128)(2,1)S(1)}, bf16[2,512,256]{2,1,0:T(8,128)(2,1)S(1)}, u32[]{:S(2)}, u32[]{:S(2)}) collective-permute-start(bf16[2,512,256]{2,1,0:T(8,128)(2,1)S(1)} %collective-permute-done.8.refs_4_.refs_2_.refs_8_), channel_id=1, source_target_pairs={{0,1},{1,0},{2,3},{3,2},{4,5},{5,4},{6,7},{7,6},{8,9},{9,8},{10,11... | collective-permute-start | bytes 1572872 | tf_op jit(solution)/shard_map/ppermute | solution.py:60
  22.2 7.3 %collective-permute-start.11 = (bf16[512,256]{1,0:T(8,128)(2,1)S(1)}, bf16[512,256]{1,0:T(8,128)(2,1)S(1)}, u32[]{:S(2)}, u32[]{:S(2)}) collective-permute-start(bf16[512,256]{1,0:T(8,128)(2,1)S(1)} %shard_map.102.refs_7_), channel_id=1, source_target_pairs={{0,16},{16,0},{1,17},{17,1},{2,18},{18,2},{3,19},{19,3},{4,20},{20... | collective-permute-start | bytes 786440 | tf_op jit(solution)/shard_map/ppermute | solution.py:60
  24.5 9.2 %collective-permute-start.9 = (bf16[512,256]{1,0:T(8,128)(2,1)S(1)}, bf16[512,256]{1,0:T(8,128)(2,1)S(1)}, u32[]{:S(2)}, u32[]{:S(2)}) collective-permute-start(bf16[512,256]{1,0:T(8,128)(2,1)S(1)} %get-tuple-element.58), channel_id=1, source_target_pairs={{0,2},{1,3},{2,0},{3,1},{4,6},{5,7},{6,4},{7,5},{8,10},{9,11},{10,... | collective-permute-start | bytes 786440 | tf_op jit(solution)/shard_map/ppermute | solution.py:60
  26.1 4.9 %collective-permute-start.10 = (bf16[128,256]{1,0:T(8,128)(2,1)S(1)}, bf16[128,256]{1,0:T(8,128)(2,1)S(1)}, u32[]{:S(2)}, u32[]{:S(2)}) collective-permute-start(bf16[128,256]{1,0:T(8,128)(2,1)S(1)} %get-tuple-element.59.refs_3_.refs_0_), channel_id=1, source_target_pairs={{0,4},{1,5},{2,6},{3,7},{4,0},{5,1},{6,2},{7,3},{8,12},{9,13},{10,... | collective-permute-start | bytes 196616 | tf_op jit(solution)/shard_map/ppermute | solution.py:60
  29.6 5.0 %collective-permute-start.15 = (bf16[256,256]{1,0:T(8,128)(2,1)S(1)}, bf16[256,256]{1,0:T(8,128)(2,1)S(1)}, u32[]{:S(2)}, u32[]{:S(2)}) collective-permute-start(bf16[256,256]{1,0:T(8,128)(2,1)S(1)} %get-tuple-element.61.refs_2_), channel_id=1, source_target_pairs={{0,4},{1,5},{2,6},{3,7},{4,0},{5,1},{6,2},{7,3},{8,12},{9,13},{10,... | collective-permute-start | bytes 393224 | tf_op jit(solution)/shard_map/ppermute | solution.py:60
  31.0 6.3 %collective-permute-start.14 = (bf16[128,256]{1,0:T(8,128)(2,1)S(1)}, bf16[128,256]{1,0:T(8,128)(2,1)S(1)}, u32[]{:S(2)}, u32[]{:S(2)}) collective-permute-start(bf16[128,256]{1,0:T(8,128)(2,1)S(1)} %shard_map.106.refs_2_), channel_id=1, source_target_pairs={{0,8},{1,9},{2,10},{3,11},{4,12},{5,13},{6,14},{7,15},{8,0},{9,1},... | collective-permute-start | bytes 196616 | tf_op jit(solution)/shard_map/ppermute | solution.py:60
  33.7 5.3 %collective-permute-start.13 = (bf16[512,256]{1,0:T(8,128)(2,1)S(1)}, bf16[512,256]{1,0:T(8,128)(2,1)S(1)}, u32[]{:S(2)}, u32[]{:S(2)}) collective-permute-start(bf16[512,256]{1,0:T(8,128)(2,1)S(1)} %shard_map.107.refs_2_), channel_id=1, source_target_pairs={{0,1},{1,0},{2,3},{3,2},{4,5},{5,4},{6,7},{7,6},{8,9},{9,8},{10,11... | collective-permute-start | bytes 786440 | tf_op jit(solution)/shard_map/ppermute | solution.py:60
  34.6 6.6 %collective-permute-start.17 = (bf16[128,256]{1,0:T(8,128)(2,1)S(1)}, bf16[128,256]{1,0:T(8,128)(2,1)S(1)}, u32[]{:S(2)}, u32[]{:S(2)}) collective-permute-start(bf16[128,256]{1,0:T(8,128)(2,1)S(1)} %get-tuple-element.64.refs_3_), channel_id=1, source_target_pairs={{0,8},{1,9},{2,10},{3,11},{4,12},{5,13},{6,14},{7,15},{8,0},{9,1},... | collective-permute-start | bytes 196616 | tf_op jit(solution)/shard_map/ppermute | solution.py:60
  37.4 5.4 %collective-permute-start.16 = (bf16[256,256]{1,0:T(8,128)(2,1)S(1)}, bf16[256,256]{1,0:T(8,128)(2,1)S(1)}, u32[]{:S(2)}, u32[]{:S(2)}) collective-permute-start(bf16[256,256]{1,0:T(8,128)(2,1)S(1)} %get-tuple-element.66.refs_7_), channel_id=1, source_target_pairs={{0,2},{1,3},{2,0},{3,1},{4,6},{5,7},{6,4},{7,5},{8,10},{9,11},{10,... | collective-permute-start | bytes 393224 | tf_op jit(solution)/shard_map/ppermute | solution.py:60
  41.3 1.6 %copy-start.2 = (bf16[512,1024]{1,0:T(8,128)(2,1)S(1)}, bf16[512,1024]{1,0:T(8,128)(2,1)}, u32[]{:S(2)}) copy-start(bf16[512,1024]{1,0:T(8,128)(2,1)} %refs_7_.1) | copy-start | bytes 3145732
  41.3 4.0 %collective-permute-start.19 = (bf16[64,256]{1,0:T(8,128)(2,1)S(1)}, bf16[64,256]{1,0:T(8,128)(2,1)S(1)}, u32[]{:S(2)}, u32[]{:S(2)}) collective-permute-start(bf16[64,256]{1,0:T(8,128)(2,1)S(1)} %get-tuple-element.70.refs_2_), channel_id=1, source_target_pairs={{0,2},{1,3},{2,0},{3,1},{4,6},{5,7},{6,4},{7,5},{8,10},{9,11},{10,... | collective-permute-start | bytes 98312 | tf_op jit(solution)/shard_map/ppermute | solution.py:60
  42.8 2.7 %collective-permute-start.18 = (bf16[256,256]{1,0:T(8,128)(2,1)S(1)}, bf16[256,256]{1,0:T(8,128)(2,1)S(1)}, u32[]{:S(2)}, u32[]{:S(2)}) collective-permute-start(bf16[256,256]{1,0:T(8,128)(2,1)S(1)} %shard_map.112.refs_10_.refs_2_), channel_id=1, source_target_pairs={{0,1},{1,0},{2,3},{3,2},{4,5},{5,4},{6,7},{7,6},{8,9},{9,8},{10,11... | collective-permute-start | bytes 393224 | tf_op jit(solution)/shard_map/ppermute | solution.py:60
  45.3 1.4 %collective-permute-start.20 = (bf16[64,256]{1,0:T(8,128)(2,1)S(1)}, bf16[64,256]{1,0:T(8,128)(2,1)S(1)}, u32[]{:S(2)}, u32[]{:S(2)}) collective-permute-start(bf16[64,256]{1,0:T(8,128)(2,1)S(1)} %get-tuple-element.75.refs_7_.refs_2_), channel_id=1, source_target_pairs={{0,1},{1,0},{2,3},{3,2},{4,5},{5,4},{6,7},{7,6},{8,9},{9,8},{10,11... | collective-permute-start | bytes 98312 | tf_op jit(solution)/shard_map/ppermute | solution.py:60

commit v22 on v21

--- a/solution.py
+++ b/solution.py
@@ -472,12 +472,15 @@
             scratch=[pltpu.VMEM((piece, width), F32)],
         )
         got = near(share, bits=2)
-    (send,) = call(relay_kernel, [((2 * DH, width), BF16)], later, later_far)
-    later_core = near(send, bits=1)
     output, own_normed = call(
         output_kernel, [((rows, outputs), BF16), ((rows, features), BF16)],
         back, back_far, back_core, q, own_tokens, *sent, out_weight, *w_all, end=True,
     )
+    (send,) = call(
+        relay_kernel, [((2 * DH, width), BF16)], later, later_far,
+        wait=[pltpu.with_memory_space_constraint(output, pltpu.HBM)],
+    )
+    later_core = near(send, bits=1)
     if tuned:
         keep, share = call(
             pass_kernel, [((piece // 2, width), BF16)] * 2, keep, got, cost=3 * 10**9,

time: 47.5 us -> 48 us (1.011)
  local copies, waits for them, and re-layouts: 0.02 us -> 0.83 us
    unnamed x10, local copies, waits for them, and re-layouts: 0.02 us -> 0.83 us
  transfers between devices with their start and end apart: 21 -> 21, of which waited for: 11 -> 11; matrix products, arithmetic and copies ran while one was open for 0% -> 0% of each run, Pallas kernels for 21% -> 20%
where the time goes in v22:
time: 48 us; the launch traced here: 47.8 us
  starting transfers between devices  25.3 us (53%)
  Pallas kernels  11.9 us (25%)
  waiting for transfers between devices  8.96 us (19%)
  between operations  0.84 us (2%)
  local copies, waits for them, and re-layouts  0.83 us (2%)
    ppermute x21, starting transfers between devices, flip(): return lax.ppermute(x, axis, [(i, i ^ bits) for i in range(count)])  25.3 us
    pallas_call x25, Pallas kernels, __call__(): pl.pallas_call(inner, out_shape=[jax.ShapeDtypeStruct(s, d) for s, d in o...  11.9 us
    ppermute x21, waiting for transfers between devices, flip(): return lax.ppermute(x, axis, [(i, i ^ bits) for i in range(count)])  8.96 us
  transfers between devices with their start and end apart: 21, of which 11 were waited for; matrix products, arithmetic and copies ran while one was open for 0% of the time, Pallas kernels for 20%

profile of v22, /device:TPU:0, one launch (start us, length us, event | category | flops | bytes accessed | tf_op | source)
XLA Modules:
  0.0 47.8 jit_solution(11644681275735252691)
XLA Ops:
  0.7 1.4 %shard_map.92 = (f32[128,256]{1,0:T(8,128)S(1)}, bf16[128,256]{1,0:T(8,128)(2,1)S(1)}, bf16[256,256]{1,0:T(8,128)(2,1)S(1)}, bf16[2,512,256]{2,1,0:T(8,128)(2,1)S(1)}) custom-call(bf16[128,1024]{1,0:T(8,128)(2,1)} %bitcast.8, bf16[128,1024]{1,0:T(8,128)(2,1)} %bitcast.12, bf16[512,1024]{1,0:T(8,128)(2,1)} %refs_7_.1), custom_call_target="tpu_custom_call" | custom-call | flops 1 | bytes 1 | tf_op jit(solution)/shard_map/pallas_call | solution.py:42
  2.1 3.0 %collective-permute-start.1 = (bf16[256,256]{1,0:T(8,128)(2,1)S(1)}, bf16[256,256]{1,0:T(8,128)(2,1)S(1)}, u32[]{:S(2)}, u32[]{:S(2)}) collective-permute-start(bf16[256,256]{1,0:T(8,128)(2,1)S(1)} %get-tuple-element.47), channel_id=1, source_target_pairs={{0,2},{1,3},{2,0},{3,1},{4,6},{5,7},{6,4},{7,5},{8,10},{9,11},{10,... | collective-permute-start | bytes 393224 | tf_op jit(solution)/shard_map/ppermute | solution.py:60
  5.2 1.9 %collective-permute-start.8 = (bf16[2,512,256]{2,1,0:T(8,128)(2,1)S(1)}, bf16[2,512,256]{2,1,0:T(8,128)(2,1)S(1)}, u32[]{:S(2)}, u32[]{:S(2)}) collective-permute-start(bf16[2,512,256]{2,1,0:T(8,128)(2,1)S(1)} %get-tuple-element.49.refs_3_.refs_1_), channel_id=1, source_target_pairs={{0,16},{16,0},{1,17},{17,1},{2,18},{18,2},{3,19},{19,3},{4,20},{20... | collective-permute-start | bytes 1572872 | tf_op jit(solution)/shard_map/ppermute | solution.py:60
  7.1 1.4 %shard_map.93 = (bf16[4,2,128,128]{3,2,1,0:T(8,128)(2,1)S(1)}, bf16[256,256]{1,0:T(8,128)(2,1)S(1)}, bf16[1024,256]{1,0:T(8,128)(2,1)S(1)}, bf16[256,256]{1,0:T(8,128)(2,1)S(1)}) custom-call(bf16[128,1024]{1,0:T(8,128)(2,1)S(1)} %bitcast.16, bf16[128,1024]{1,0:T(8,128)(2,1)S(1)} %bitcast.9, bf16[128,1024]{1,0:T(8,128)(2,1)S(1)} %bitcast.13, ...), custom_call_target="tpu_custom_call" | custom-call | flops 1 | bytes 1 | tf_op jit(solution)/shard_map/pallas_call | solution.py:42
  8.6 0.9 %collective-permute-done.1.refs_1_.refs_4_ = bf16[256,256]{1,0:T(8,128)(2,1)S(1)} collective-permute-done((bf16[256,256]{1,0:T(8,128)(2,1)S(1)}, bf16[256,256]{1,0:T(8,128)(2,1)S(1)}, u32[]{:S(2)}, u32[]{:S(2)}) %collective-permute-start.1) | collective-permute-done | bytes 131104 | tf_op jit(solution)/shard_map/ppermute | solution.py:60
  9.5 1.3 %collective-permute-done.2.refs_2_.refs_5_ = bf16[256,256]{1,0:T(8,128)(2,1)S(1)} collective-permute-done((bf16[256,256]{1,0:T(8,128)(2,1)S(1)}, bf16[256,256]{1,0:T(8,128)(2,1)S(1)}, u32[]{:S(2)}, u32[]{:S(2)}) %collective-permute-start.2) | collective-permute-done | bytes 131104 | tf_op jit(solution)/shard_map/ppermute | solution.py:60
  10.9 2.2 %collective-permute-start.4 = (bf16[128,256]{1,0:T(8,128)(2,1)S(1)}, bf16[128,256]{1,0:T(8,128)(2,1)S(1)}, u32[]{:S(2)}, u32[]{:S(2)}) collective-permute-start(bf16[128,256]{1,0:T(8,128)(2,1)S(1)} %shard_map.95.refs_2_.refs_0_), channel_id=1, source_target_pairs={{0,4},{1,5},{2,6},{3,7},{4,0},{5,1},{6,2},{7,3},{8,12},{9,13},{10,... | collective-permute-start | bytes 196616 | tf_op jit(solution)/shard_map/ppermute | solution.py:60
  13.1 1.6 %collective-permute-start.3 = (bf16[512,256]{1,0:T(8,128)(2,1)S(1)}, bf16[512,256]{1,0:T(8,128)(2,1)S(1)}, u32[]{:S(2)}, u32[]{:S(2)}) collective-permute-start(bf16[512,256]{1,0:T(8,128)(2,1)S(1)} %shard_map.96.refs_2_), channel_id=1, source_target_pairs={{0,2},{1,3},{2,0},{3,1},{4,6},{5,7},{6,4},{7,5},{8,10},{9,11},{10,... | collective-permute-start | bytes 786440 | tf_op jit(solution)/shard_map/ppermute | solution.py:60
  14.7 0.8 %collective-permute-done.4.refs_1_.refs_0_ = bf16[128,256]{1,0:T(8,128)(2,1)S(1)} collective-permute-done((bf16[128,256]{1,0:T(8,128)(2,1)S(1)}, bf16[128,256]{1,0:T(8,128)(2,1)S(1)}, u32[]{:S(2)}, u32[]{:S(2)}) %collective-permute-start.4) | collective-permute-done | bytes 65568 | tf_op jit(solution)/shard_map/ppermute | solution.py:60
  15.5 2.9 %collective-permute-start.5 = (bf16[128,256]{1,0:T(8,128)(2,1)S(1)}, bf16[128,256]{1,0:T(8,128)(2,1)S(1)}, u32[]{:S(2)}, u32[]{:S(2)}) collective-permute-start(bf16[128,256]{1,0:T(8,128)(2,1)S(1)} %shard_map.97.refs_5_), channel_id=1, source_target_pairs={{0,8},{1,9},{2,10},{3,11},{4,12},{5,13},{6,14},{7,15},{8,0},{9,1},... | collective-permute-start | bytes 196616 | tf_op jit(solution)/shard_map/ppermute | solution.py:60
  18.6 0.4 shard_map.98
  19.4 1.7 %collective-permute-done.5.refs_1_ = bf16[128,256]{1,0:T(8,128)(2,1)S(1)} collective-permute-done((bf16[128,256]{1,0:T(8,128)(2,1)S(1)}, bf16[128,256]{1,0:T(8,128)(2,1)S(1)}, u32[]{:S(2)}, u32[]{:S(2)}) %collective-permute-start.5) | collective-permute-done | bytes 65568 | tf_op jit(solution)/shard_map/ppermute | solution.py:60
  21.3 0.5 shard_map.101
  21.7 0.5 %shard_map.102.refs_7_ = bf16[512,256]{1,0:T(8,128)(2,1)S(1)} custom-call(bf16[3,128,1024]{2,1,0:T(8,128)(2,1)S(1)} %get-tuple-element.54.refs_0_, bf16[1,128,1024]{2,1,0:T(8,128)(2,1)S(1)} %get-tuple-element.55.refs_1_, bf16[4,128,256]{2,1,0:T(8,128)(2,1)S(1)} %get-tuple-element.56.refs_2_, bf16[4,128,256]{2,1,0:T(8,128)(2,1)S(1)} %get-tuple-element.53.refs_3_.refs_4_), custom_call_target="tpu_custom_call" | custom-call | flops 1 | bytes 1 | tf_op jit(solution)/shard_map/pallas_call | solution.py:42
  22.2 1.5 %collective-permute-start.11 = (bf16[512,256]{1,0:T(8,128)(2,1)S(1)}, bf16[512,256]{1,0:T(8,128)(2,1)S(1)}, u32[]{:S(2)}, u32[]{:S(2)}) collective-permute-start(bf16[512,256]{1,0:T(8,128)(2,1)S(1)} %shard_map.102.refs_7_), channel_id=1, source_target_pairs={{0,16},{16,0},{1,17},{17,1},{2,18},{18,2},{3,19},{19,3},{4,20},{20... | collective-permute-start | bytes 786440 | tf_op jit(solution)/shard_map/ppermute | solution.py:60
  23.8 0.7 %shard_map.103 = (bf16[512,256]{1,0:T(8,128)(2,1)S(1)}, bf16[512,256]{1,0:T(8,128)(2,1)S(1)}, f32[4,128,256]{2,1,0:T(8,128)S(1)}, bf16[128,256]{1,0:T(8,128)(2,1)S(1)}) custom-call(bf16[256,256]{1,0:T(8,128)(2,1)S(1)} %get-tuple-element.43.refs_0_.refs_4_, bf16[1024,256]{1,0:T(8,128)(2,1)S(1)} %collective-permute-done.refs_0_.refs_1_, ...), custom_call_target="tpu_custom_call" | custom-call | flops 1 | bytes 1 | tf_op jit(solution)/shard_map/pallas_call | solution.py:42
  24.5 1.6 %collective-permute-start.9 = (bf16[512,256]{1,0:T(8,128)(2,1)S(1)}, bf16[512,256]{1,0:T(8,128)(2,1)S(1)}, u32[]{:S(2)}, u32[]{:S(2)}) collective-permute-start(bf16[512,256]{1,0:T(8,128)(2,1)S(1)} %get-tuple-element.58), channel_id=1, source_target_pairs={{0,2},{1,3},{2,0},{3,1},{4,6},{5,7},{6,4},{7,5},{8,10},{9,11},{10,... | collective-permute-start | bytes 786440 | tf_op jit(solution)/shard_map/ppermute | solution.py:60
  26.1 1.4 %collective-permute-start.10 = (bf16[128,256]{1,0:T(8,128)(2,1)S(1)}, bf16[128,256]{1,0:T(8,128)(2,1)S(1)}, u32[]{:S(2)}, u32[]{:S(2)}) collective-permute-start(bf16[128,256]{1,0:T(8,128)(2,1)S(1)} %get-tuple-element.59.refs_3_.refs_0_), channel_id=1, source_target_pairs={{0,4},{1,5},{2,6},{3,7},{4,0},{5,1},{6,2},{7,3},{8,12},{9,13},{10,... | collective-permute-start | bytes 196616 | tf_op jit(solution)/shard_map/ppermute | solution.py:60
  27.5 0.5 shard_map.104.refs_0_.refs_2_
  28.0 1.6 %collective-permute-done.11.refs_1_ = bf16[512,256]{1,0:T(8,128)(2,1)S(1)} collective-permute-done((bf16[512,256]{1,0:T(8,128)(2,1)S(1)}, bf16[512,256]{1,0:T(8,128)(2,1)S(1)}, u32[]{:S(2)}, u32[]{:S(2)}) %collective-permute-start.11) | collective-permute-done | bytes 262176 | tf_op jit(solution)/shard_map/ppermute | solution.py:60
  29.6 1.4 %collective-permute-start.14 = (bf16[256,256]{1,0:T(8,128)(2,1)S(1)}, bf16[256,256]{1,0:T(8,128)(2,1)S(1)}, u32[]{:S(2)}, u32[]{:S(2)}) collective-permute-start(bf16[256,256]{1,0:T(8,128)(2,1)S(1)} %get-tuple-element.61.refs_2_), channel_id=1, source_target_pairs={{0,4},{1,5},{2,6},{3,7},{4,0},{5,1},{6,2},{7,3},{8,12},{9,13},{10,... | collective-permute-start | bytes 393224 | tf_op jit(solution)/shard_map/ppermute | solution.py:60
  31.0 2.6 %collective-permute-start.16 = (bf16[128,256]{1,0:T(8,128)(2,1)S(1)}, bf16[128,256]{1,0:T(8,128)(2,1)S(1)}, u32[]{:S(2)}, u32[]{:S(2)}) collective-permute-start(bf16[128,256]{1,0:T(8,128)(2,1)S(1)} %shard_map.106.refs_2_), channel_id=1, source_target_pairs={{0,8},{1,9},{2,10},{3,11},{4,12},{5,13},{6,14},{7,15},{8,0},{9,1},... | collective-permute-start | bytes 196616 | tf_op jit(solution)/shard_map/ppermute | solution.py:60
  33.8 0.8 %collective-permute-done.14.refs_1_ = bf16[256,256]{1,0:T(8,128)(2,1)S(1)} collective-permute-done((bf16[256,256]{1,0:T(8,128)(2,1)S(1)}, bf16[256,256]{1,0:T(8,128)(2,1)S(1)}, u32[]{:S(2)}, u32[]{:S(2)}) %collective-permute-start.14) | collective-permute-done | bytes 131104 | tf_op jit(solution)/shard_map/ppermute | solution.py:60
  34.6 2.6 %collective-permute-start.15 = (bf16[128,256]{1,0:T(8,128)(2,1)S(1)}, bf16[128,256]{1,0:T(8,128)(2,1)S(1)}, u32[]{:S(2)}, u32[]{:S(2)}) collective-permute-start(bf16[128,256]{1,0:T(8,128)(2,1)S(1)} %get-tuple-element.64.refs_3_), channel_id=1, source_target_pairs={{0,8},{1,9},{2,10},{3,11},{4,12},{5,13},{6,14},{7,15},{8,0},{9,1},... | collective-permute-start | bytes 196616 | tf_op jit(solution)/shard_map/ppermute | solution.py:60
  37.4 1.6 %collective-permute-start.17 = (bf16[256,256]{1,0:T(8,128)(2,1)S(1)}, bf16[256,256]{1,0:T(8,128)(2,1)S(1)}, u32[]{:S(2)}, u32[]{:S(2)}) collective-permute-start(bf16[256,256]{1,0:T(8,128)(2,1)S(1)} %get-tuple-element.67.refs_7_), channel_id=1, source_target_pairs={{0,2},{1,3},{2,0},{3,1},{4,6},{5,7},{6,4},{7,5},{8,10},{9,11},{10,... | collective-permute-start | bytes 393224 | tf_op jit(solution)/shard_map/ppermute | solution.py:60
  39.0 2.1 %shard_map.110 = (bf16[128,1024]{1,0:T(8,128)(2,1)}, f32[4,128,256]{2,1,0:T(8,128)S(1)}, f32[4,128,256]{2,1,0:T(8,128)S(1)}) custom-call(bf16[512,256]{1,0:T(8,128)(2,1)S(1)} %get-tuple-element.57.refs_0_, bf16[512,256]{1,0:T(8,128)(2,1)S(1)} %collective-permute-done.9.refs_1_, bf16[512,256]{1,0:T(8,128)(2,1)S(1)} %collective-permute-done.13.refs_2_, ...), custom_call_target="tpu_custom_call" | custom-call | flops 1 | bytes 1 | tf_op jit(solution)/shard_map/pallas_call | solution.py:42
  41.7 0.8 %copy-done.2 = bf16[512,1024]{1,0:T(8,128)(2,1)S(1)} copy-done((bf16[512,1024]{1,0:T(8,128)(2,1)S(1)}, bf16[512,1024]{1,0:T(8,128)(2,1)}, u32[]{:S(2)}) %copy-start.2) | copy-done | bytes 1048600
  42.5 2.1 %shard_map.112 = (bf16[128,1024]{1,0:T(8,128)(2,1)}, bf16[128,1024]{1,0:T(8,128)(2,1)}) custom-call(bf16[512,256]{1,0:T(8,128)(2,1)S(1)} %get-tuple-element.57.refs_0_, bf16[512,256]{1,0:T(8,128)(2,1)S(1)} %collective-permute-done.9.refs_1_, bf16[512,256]{1,0:T(8,128)(2,1)S(1)} %collective-permute-done.13.refs_2_, bf16[128,1024]{1,0:T(8,128)(2,1)S(1)} %bitcast.18, ...), custom_call_target="tpu_custom_call" | custom-call | flops 1 | bytes 1 | tf_op jit(solution)/shard_map/pallas_call | solution.py:42
  44.7 0.6 %collective-permute-done.19.refs_1_ = bf16[64,256]{1,0:T(8,128)(2,1)S(1)} collective-permute-done((bf16[64,256]{1,0:T(8,128)(2,1)S(1)}, bf16[64,256]{1,0:T(8,128)(2,1)S(1)}, u32[]{:S(2)}, u32[]{:S(2)}) %collective-permute-start.19) | collective-permute-done | bytes 32800 | tf_op jit(solution)/shard_map/ppermute | solution.py:60
  45.3 0.7 %collective-permute-done.18.refs_2_ = bf16[256,256]{1,0:T(8,128)(2,1)S(1)} collective-permute-done((bf16[256,256]{1,0:T(8,128)(2,1)S(1)}, bf16[256,256]{1,0:T(8,128)(2,1)S(1)}, u32[]{:S(2)}, u32[]{:S(2)}) %collective-permute-start.18) | collective-permute-done | bytes 131104 | tf_op jit(solution)/shard_map/ppermute | solution.py:60
  46.0 1.1 %shard_map.115 = (bf16[128,1024]{1,0:T(8,128)(2,1)}, bf16[128,1024]{1,0:T(8,128)(2,1)}) custom-call(bf16[256,256]{1,0:T(8,128)(2,1)S(1)} %get-tuple-element.72.refs_0_, bf16[256,256]{1,0:T(8,128)(2,1)S(1)} %collective-permute-done.17.refs_1_, bf16[256,256]{1,0:T(8,128)(2,1)S(1)} %collective-permute-done.18.refs_2_, bf16[128,1024]{1,0:T(8,128)(2,1)S(1)} %bitcast.11, ...), custom_call_target="tpu_custom_call" | custom-call | flops 1 | bytes 1 | tf_op jit(solution)/shard_map/pallas_call | solution.py:42
  47.1 0.7 %shard_map.116 = f32[32,1024]{1,0:T(8,128)} custom-call(bf16[64,256]{1,0:T(8,128)(2,1)S(1)} %get-tuple-element.78.refs_0_, bf16[64,256]{1,0:T(8,128)(2,1)S(1)} %collective-permute-done.20.refs_1_, bf16[64,256]{1,0:T(8,128)(2,1)S(1)} %get-tuple-element.75.refs_7_.refs_2_, bf16[128,1024]{1,0:T(8,128)(2,1)} %get-tuple-element.76.refs_3_), custom_call_target="tpu_custom_call" | custom-call | flops 1 | bytes 1 | tf_op jit(solution)/shard_map/pallas_call | solution.py:42
  (45 shorter events, 2.0 us)
Async XLA Ops:
  0.6 4.5 %copy-start.4 = (bf16[1,128,1024]{2,1,0:T(8,128)(2,1)S(1)}, bf16[1,128,1024]{2,1,0:T(8,128)(2,1)}, u32[]{:S(2)}) copy-start(bf16[1,128,1024]{2,1,0:T(8,128)(2,1)} %param.8) | copy-start | bytes 786436
  0.6 6.5 %copy-start = (bf16[1,128,1024]{2,1,0:T(8,128)(2,1)S(1)}, bf16[1,128,1024]{2,1,0:T(8,128)(2,1)}, u32[]{:S(2)}) copy-start(bf16[1,128,1024]{2,1,0:T(8,128)(2,1)} %param.6) | copy-start | bytes 786436
  0.7 6.5 %copy-start.1 = (bf16[1,128,1024]{2,1,0:T(8,128)(2,1)S(1)}, bf16[1,128,1024]{2,1,0:T(8,128)(2,1)}, u32[]{:S(2)}) copy-start(bf16[1,128,1024]{2,1,0:T(8,128)(2,1)} %param.7) | copy-start | bytes 786436
  0.7 6.5 %copy-start.3 = (bf16[1,128,1024]{2,1,0:T(8,128)(2,1)S(1)}, bf16[1,128,1024]{2,1,0:T(8,128)(2,1)}, u32[]{:S(2)}) copy-start(bf16[1,128,1024]{2,1,0:T(8,128)(2,1)} %param.5) | copy-start | bytes 786436
  2.1 7.4 %collective-permute-start.1 = (bf16[256,256]{1,0:T(8,128)(2,1)S(1)}, bf16[256,256]{1,0:T(8,128)(2,1)S(1)}, u32[]{:S(2)}, u32[]{:S(2)}) collective-permute-start(bf16[256,256]{1,0:T(8,128)(2,1)S(1)} %get-tuple-element.47), channel_id=1, source_target_pairs={{0,2},{1,3},{2,0},{3,1},{4,6},{5,7},{6,4},{7,5},{8,10},{9,11},{10,... | collective-permute-start | bytes 393224 | tf_op jit(solution)/shard_map/ppermute | solution.py:60
  5.1 9.6 %collective-permute-start.6 = (bf16[128,1024]{1,0:T(8,128)(2,1)S(1)}, bf16[128,1024]{1,0:T(8,128)(2,1)S(1)}, u32[]{:S(2)}, u32[]{:S(2)}) collective-permute-start(bf16[128,1024]{1,0:T(8,128)(2,1)S(1)} %bitcast.19), channel_id=1, source_target_pairs={{0,2},{1,3},{2,0},{3,1},{4,6},{5,7},{6,4},{7,5},{8,10},{9,11},{10,... | collective-permute-start | bytes 786440 | tf_op jit(solution)/shard_map/ppermute | solution.py:60
  5.2 13.4 %collective-permute-start.8 = (bf16[2,512,256]{2,1,0:T(8,128)(2,1)S(1)}, bf16[2,512,256]{2,1,0:T(8,128)(2,1)S(1)}, u32[]{:S(2)}, u32[]{:S(2)}) collective-permute-start(bf16[2,512,256]{2,1,0:T(8,128)(2,1)S(1)} %get-tuple-element.49.refs_3_.refs_1_), channel_id=1, source_target_pairs={{0,16},{16,0},{1,17},{17,1},{2,18},{18,2},{3,19},{19,3},{4,20},{20... | collective-permute-start | bytes 1572872 | tf_op jit(solution)/shard_map/ppermute | solution.py:60
  8.5 4.6 %collective-permute-start = (bf16[1024,256]{1,0:T(8,128)(2,1)S(1)}, bf16[1024,256]{1,0:T(8,128)(2,1)S(1)}, u32[]{:S(2)}, u32[]{:S(2)}) collective-permute-start(bf16[1024,256]{1,0:T(8,128)(2,1)S(1)} %get-tuple-element.44.refs_5_), channel_id=1, source_target_pairs={{0,1},{1,0},{2,3},{3,2},{4,5},{5,4},{6,7},{7,6},{8,9},{9,8},{10,11... | collective-permute-start | bytes 1572872 | tf_op jit(solution)/shard_map/ppermute | solution.py:60
  9.5 1.4 %collective-permute-start.2 = (bf16[256,256]{1,0:T(8,128)(2,1)S(1)}, bf16[256,256]{1,0:T(8,128)(2,1)S(1)}, u32[]{:S(2)}, u32[]{:S(2)}) collective-permute-start(bf16[256,256]{1,0:T(8,128)(2,1)S(1)} %shard_map.94.refs_3_), channel_id=1, source_target_pairs={{0,1},{1,0},{2,3},{3,2},{4,5},{5,4},{6,7},{7,6},{8,9},{9,8},{10,11... | collective-permute-start | bytes 393224 | tf_op jit(solution)/shard_map/ppermute | solution.py:60
  10.9 4.6 %collective-permute-start.4 = (bf16[128,256]{1,0:T(8,128)(2,1)S(1)}, bf16[128,256]{1,0:T(8,128)(2,1)S(1)}, u32[]{:S(2)}, u32[]{:S(2)}) collective-permute-start(bf16[128,256]{1,0:T(8,128)(2,1)S(1)} %shard_map.95.refs_2_.refs_0_), channel_id=1, source_target_pairs={{0,4},{1,5},{2,6},{3,7},{4,0},{5,1},{6,2},{7,3},{8,12},{9,13},{10,... | collective-permute-start | bytes 196616 | tf_op jit(solution)/shard_map/ppermute | solution.py:60
  13.1 8.1 %collective-permute-start.3 = (bf16[512,256]{1,0:T(8,128)(2,1)S(1)}, bf16[512,256]{1,0:T(8,128)(2,1)S(1)}, u32[]{:S(2)}, u32[]{:S(2)}) collective-permute-start(bf16[512,256]{1,0:T(8,128)(2,1)S(1)} %shard_map.96.refs_2_), channel_id=1, source_target_pairs={{0,2},{1,3},{2,0},{3,1},{4,6},{5,7},{6,4},{7,5},{8,10},{9,11},{10,... | collective-permute-start | bytes 786440 | tf_op jit(solution)/shard_map/ppermute | solution.py:60
  14.7 4.4 %collective-permute-start.7 = (bf16[128,1024]{1,0:T(8,128)(2,1)S(1)}, bf16[128,1024]{1,0:T(8,128)(2,1)S(1)}, u32[]{:S(2)}, u32[]{:S(2)}) collective-permute-start(bf16[128,1024]{1,0:T(8,128)(2,1)S(1)} %collective-permute-done.6.refs_2_), channel_id=1, source_target_pairs={{0,1},{1,0},{2,3},{3,2},{4,5},{5,4},{6,7},{7,6},{8,9},{9,8},{10,11... | collective-permute-start | bytes 786440 | tf_op jit(solution)/shard_map/ppermute | solution.py:60
  15.5 5.6 %collective-permute-start.5 = (bf16[128,256]{1,0:T(8,128)(2,1)S(1)}, bf16[128,256]{1,0:T(8,128)(2,1)S(1)}, u32[]{:S(2)}, u32[]{:S(2)}) collective-permute-start(bf16[128,256]{1,0:T(8,128)(2,1)S(1)} %shard_map.97.refs_5_), channel_id=1, source_target_pairs={{0,8},{1,9},{2,10},{3,11},{4,12},{5,13},{6,14},{7,15},{8,0},{9,1},... | collective-permute-start | bytes 196616 | tf_op jit(solution)/shard_map/ppermute | solution.py:60
  19.0 10.5 %collective-permute-start.12 = (bf16[2,512,256]{2,1,0:T(8,128)(2,1)S(1)}, bf16[2,512,256]{2,1,0:T(8,128)(2,1)S(1)}, u32[]{:S(2)}, u32[]{:S(2)}) collective-permute-start(bf16[2,512,256]{2,1,0:T(8,128)(2,1)S(1)} %collective-permute-done.8.refs_4_.refs_2_.refs_8_), channel_id=1, source_target_pairs={{0,1},{1,0},{2,3},{3,2},{4,5},{5,4},{6,7},{7,6},{8,9},{9,8},{10,11... | collective-permute-start | bytes 1572872 | tf_op jit(solution)/shard_map/ppermute | solution.py:60
  22.2 7.3 %collective-permute-start.11 = (bf16[512,256]{1,0:T(8,128)(2,1)S(1)}, bf16[512,256]{1,0:T(8,128)(2,1)S(1)}, u32[]{:S(2)}, u32[]{:S(2)}) collective-permute-start(bf16[512,256]{1,0:T(8,128)(2,1)S(1)} %shard_map.102.refs_7_), channel_id=1, source_target_pairs={{0,16},{16,0},{1,17},{17,1},{2,18},{18,2},{3,19},{19,3},{4,20},{20... | collective-permute-start | bytes 786440 | tf_op jit(solution)/shard_map/ppermute | solution.py:60
  24.5 9.2 %collective-permute-start.9 = (bf16[512,256]{1,0:T(8,128)(2,1)S(1)}, bf16[512,256]{1,0:T(8,128)(2,1)S(1)}, u32[]{:S(2)}, u32[]{:S(2)}) collective-permute-start(bf16[512,256]{1,0:T(8,128)(2,1)S(1)} %get-tuple-element.58), channel_id=1, source_target_pairs={{0,2},{1,3},{2,0},{3,1},{4,6},{5,7},{6,4},{7,5},{8,10},{9,11},{10,... | collective-permute-start | bytes 786440 | tf_op jit(solution)/shard_map/ppermute | solution.py:60
  26.1 4.9 %collective-permute-start.10 = (bf16[128,256]{1,0:T(8,128)(2,1)S(1)}, bf16[128,256]{1,0:T(8,128)(2,1)S(1)}, u32[]{:S(2)}, u32[]{:S(2)}) collective-permute-start(bf16[128,256]{1,0:T(8,128)(2,1)S(1)} %get-tuple-element.59.refs_3_.refs_0_), channel_id=1, source_target_pairs={{0,4},{1,5},{2,6},{3,7},{4,0},{5,1},{6,2},{7,3},{8,12},{9,13},{10,... | collective-permute-start | bytes 196616 | tf_op jit(solution)/shard_map/ppermute | solution.py:60
  29.6 5.0 %collective-permute-start.14 = (bf16[256,256]{1,0:T(8,128)(2,1)S(1)}, bf16[256,256]{1,0:T(8,128)(2,1)S(1)}, u32[]{:S(2)}, u32[]{:S(2)}) collective-permute-start(bf16[256,256]{1,0:T(8,128)(2,1)S(1)} %get-tuple-element.61.refs_2_), channel_id=1, source_target_pairs={{0,4},{1,5},{2,6},{3,7},{4,0},{5,1},{6,2},{7,3},{8,12},{9,13},{10,... | collective-permute-start | bytes 393224 | tf_op jit(solution)/shard_map/ppermute | solution.py:60
  31.0 6.3 %collective-permute-start.16 = (bf16[128,256]{1,0:T(8,128)(2,1)S(1)}, bf16[128,256]{1,0:T(8,128)(2,1)S(1)}, u32[]{:S(2)}, u32[]{:S(2)}) collective-permute-start(bf16[128,256]{1,0:T(8,128)(2,1)S(1)} %shard_map.106.refs_2_), channel_id=1, source_target_pairs={{0,8},{1,9},{2,10},{3,11},{4,12},{5,13},{6,14},{7,15},{8,0},{9,1},... | collective-permute-start | bytes 196616 | tf_op jit(solution)/shard_map/ppermute | solution.py:60
  33.7 5.3 %collective-permute-start.13 = (bf16[512,256]{1,0:T(8,128)(2,1)S(1)}, bf16[512,256]{1,0:T(8,128)(2,1)S(1)}, u32[]{:S(2)}, u32[]{:S(2)}) collective-permute-start(bf16[512,256]{1,0:T(8,128)(2,1)S(1)} %shard_map.107.refs_2_), channel_id=1, source_target_pairs={{0,1},{1,0},{2,3},{3,2},{4,5},{5,4},{6,7},{7,6},{8,9},{9,8},{10,11... | collective-permute-start | bytes 786440 | tf_op jit(solution)/shard_map/ppermute | solution.py:60
  34.6 6.6 %collective-permute-start.15 = (bf16[128,256]{1,0:T(8,128)(2,1)S(1)}, bf16[128,256]{1,0:T(8,128)(2,1)S(1)}, u32[]{:S(2)}, u32[]{:S(2)}) collective-permute-start(bf16[128,256]{1,0:T(8,128)(2,1)S(1)} %get-tuple-element.64.refs_3_), channel_id=1, source_target_pairs={{0,8},{1,9},{2,10},{3,11},{4,12},{5,13},{6,14},{7,15},{8,0},{9,1},... | collective-permute-start | bytes 196616 | tf_op jit(solution)/shard_map/ppermute | solution.py:60
  37.4 7.1 %collective-permute-start.17 = (bf16[256,256]{1,0:T(8,128)(2,1)S(1)}, bf16[256,256]{1,0:T(8,128)(2,1)S(1)}, u32[]{:S(2)}, u32[]{:S(2)}) collective-permute-start(bf16[256,256]{1,0:T(8,128)(2,1)S(1)} %get-tuple-element.67.refs_7_), channel_id=1, source_target_pairs={{0,2},{1,3},{2,0},{3,1},{4,6},{5,7},{6,4},{7,5},{8,10},{9,11},{10,... | collective-permute-start | bytes 393224 | tf_op jit(solution)/shard_map/ppermute | solution.py:60
  41.3 1.2 %copy-start.2 = (bf16[512,1024]{1,0:T(8,128)(2,1)S(1)}, bf16[512,1024]{1,0:T(8,128)(2,1)}, u32[]{:S(2)}) copy-start(bf16[512,1024]{1,0:T(8,128)(2,1)} %refs_7_.1) | copy-start | bytes 3145732
  41.3 4.0 %collective-permute-start.19 = (bf16[64,256]{1,0:T(8,128)(2,1)S(1)}, bf16[64,256]{1,0:T(8,128)(2,1)S(1)}, u32[]{:S(2)}, u32[]{:S(2)}) collective-permute-start(bf16[64,256]{1,0:T(8,128)(2,1)S(1)} %get-tuple-element.69.refs_10_.refs_2_), channel_id=1, source_target_pairs={{0,2},{1,3},{2,0},{3,1},{4,6},{5,7},{6,4},{7,5},{8,10},{9,11},{10,... | collective-permute-start | bytes 98312 | tf_op jit(solution)/shard_map/ppermute | solution.py:60
  44.6 1.4 %collective-permute-start.18 = (bf16[256,256]{1,0:T(8,128)(2,1)S(1)}, bf16[256,256]{1,0:T(8,128)(2,1)S(1)}, u32[]{:S(2)}, u32[]{:S(2)}) collective-permute-start(bf16[256,256]{1,0:T(8,128)(2,1)S(1)} %shard_map.113.refs_2_), channel_id=1, source_target_pairs={{0,1},{1,0},{2,3},{3,2},{4,5},{5,4},{6,7},{7,6},{8,9},{9,8},{10,11... | collective-permute-start | bytes 393224 | tf_op jit(solution)/shard_map/ppermute | solution.py:60
  45.3 1.9 %collective-permute-start.20 = (bf16[64,256]{1,0:T(8,128)(2,1)S(1)}, bf16[64,256]{1,0:T(8,128)(2,1)S(1)}, u32[]{:S(2)}, u32[]{:S(2)}) collective-permute-start(bf16[64,256]{1,0:T(8,128)(2,1)S(1)} %get-tuple-element.75.refs_7_.refs_2_), channel_id=1, source_target_pairs={{0,1},{1,0},{2,3},{3,2},{4,5},{5,4},{6,7},{7,6},{8,9},{9,8},{10,11... | collective-permute-start | bytes 98312 | tf_op jit(solution)/shard_map/ppermute | solution.py:60
